TPU v7x, 32 devices: a whole 2x2x4 slice. The times are simulated.
32 devices in a mesh: parts: 2 (over y), frame: 4 (over z), head: 4 (over x, core).
Axes of the slice: x: 2, y: 2, z: 4, core: 2. Of those that a mesh axis runs over, the one named last changes fastest.
Arguments:
- queries: bfloat16 [4096, 2560], P(('parts', 'frame', 'head')), parts along dimension 0, may hold values from -108 to 108
- keys: bfloat16 [4096, 2560], P(('parts', 'frame', 'head')), parts along dimension 0, may hold values from -4 to 4
- values: bfloat16 [4096, 2560], P(('parts', 'frame', 'head')), parts along dimension 0, may hold values from -6 to 6
- pair_mask: int32 [8, 4], P(('parts', 'frame')), parts along dimension 0, may hold values 0 or 1
- tile_offset: int32 [8], P(('parts', 'frame')), parts along dimension 0, may hold values from 0 to 1
Outputs:
- attended: bfloat16 [4096, 2560], P(('parts', 'frame', 'head')), parts along dimension 0
There are 2 independent parts, one for each index of `parts`. A program takes and returns all parts, laid end to end along the dimension named above; each array names one. Nothing has to cross between parts.
All inputs are finite; a program needn't handle non-finite values. No bound on the sum of `pair_mask` on one device may be relied on, other than what follows from the above.
Results may differ from a plain program's by a relative error of at most 0.003.
Values may be sent and summed in bfloat16 or wider, within the bound.
No kernel may reach another device: no remote copies, remote signals or barrier semaphores. Data moves between devices by JAX's collectives and lax.ppermute only.
A program may use at most 128 MiB of HBM per device.

v0:
```python
import jax
import jax.numpy as jnp
from jax import lax
from jax.sharding import PartitionSpec as P

HEAD_DIM = 128


def padded(x, sides, width):
    for axis, dim in sides:
        peers, length = (lax.axis_size(axis), x.shape[dim])
        up = [(i, (i + 1) % peers) for i in range(peers - 1)]
        down = [(j, i) for i, j in up]
        last = lax.slice_in_dim(x, length - width, length, axis=dim)
        leading = lax.slice_in_dim(x, 0, width, axis=dim)
        before = lax.ppermute(last, axis, up)
        after = lax.ppermute(leading, axis, down)
        x = jnp.concatenate([before, x, after], axis=dim)
    return x


def shortened(x):

    def short(part):
        return part.astype(jnp.bfloat16) if part.dtype == jnp.float32 else part

    return jax.tree.map(short, x)


def from_partner(x, axis, bit):
    return lax.ppermute(x, axis, [(i, i ^ 1 << bit) for i in range(lax.axis_size(axis))])


def subsample(frame_rows, offset, level, tiles, tile):
    step = 2**level
    width = frame_rows.shape[-1]
    grouped = frame_rows.reshape(tiles // step, step, tile, width)
    picked = lax.dynamic_index_in_dim(grouped, offset % step, 1, keepdims=False)
    return picked.reshape(-1, width)


def attend(query_rows, key_rows, value_rows, valid):
    count = query_rows.shape[0]
    heads = query_rows.shape[1] // HEAD_DIM
    q_three = query_rows.reshape(count, heads, HEAD_DIM).transpose(1, 0, 2)
    k_three = key_rows.reshape(-1, heads, HEAD_DIM).transpose(1, 0, 2)
    v_three = value_rows.reshape(-1, heads, HEAD_DIM).transpose(1, 0, 2)
    scale = 1.0 / HEAD_DIM**0.5

    def one_head(operands):
        q_head, k_head, v_head = operands
        scores = jnp.dot(q_head, k_head.T, preferred_element_type=jnp.float32) * scale
        scores = jnp.where(valid[None, :] > 0, scores, -1e30)
        top = jnp.max(scores, axis=1, keepdims=True)
        weights = jnp.exp(scores - top) * valid[None, :]
        total = jnp.sum(weights, axis=1, keepdims=True)
        mixed = jnp.dot(weights.astype(jnp.bfloat16), v_head, preferred_element_type=jnp.float32)
        return mixed / total

    outcome = lax.map(one_head, (q_three, k_three, v_three))
    return outcome.transpose(1, 0, 2).reshape(count, heads * HEAD_DIM).astype(jnp.bfloat16)


def ordered(mine, theirs, upper):
    return jnp.where(upper == 1, jnp.concatenate([theirs, mine]), jnp.concatenate([mine, theirs]))


def per_device(queries, keys, values, pair_mask, tile_offset):
    frames_n = lax.axis_size("frame")
    current = lax.axis_index("frame")
    q_rows, k_rows, v_rows = (
        lax.all_to_all(queries, "head", split_axis=1, concat_axis=0, tiled=True),
        lax.all_to_all(keys, "head", split_axis=1, concat_axis=0, tiled=True),
        lax.all_to_all(values, "head", split_axis=1, concat_axis=0, tiled=True),
    )
    count = q_rows.shape[0]
    width = q_rows.shape[1]
    tiles = frames_n // 2
    tile = count // tiles
    depth = frames_n.bit_length() - 1
    stacked = jnp.stack([k_rows, v_rows])
    near = padded(stacked, (("frame", 1),), count)
    near_index = current - 1 + jnp.arange(3, dtype=jnp.int32)
    near_good = ((near_index >= 0) & (near_index < frames_n)).astype(jnp.float32)
    key_parts = [near[0]]
    value_parts = [near[1]]
    valid_parts = [jnp.repeat(near_good, count)]
    mask_row = pair_mask[0]
    offset = tile_offset[0]
    k_tiles = k_rows.reshape(tiles, tile, width)
    v_tiles = v_rows.reshape(tiles, tile, width)
    own = {}
    for level in range(1, depth):
        own[level] = (
            subsample(k_tiles, offset, level, tiles, tile)[None],
            subsample(v_tiles, offset, level, tiles, tile)[None],
        )
    sibling = {}
    cut = max(1, depth - 2)
    upper_levels = [level for level in range(1, depth) if level >= cut]
    k_pack = jnp.concatenate([own[level][0].reshape(-1, width) for level in upper_levels])
    v_pack = jnp.concatenate([own[level][1].reshape(-1, width) for level in upper_levels])
    k_every, v_every = (
        lax.all_gather(k_pack, "frame", axis=0, tiled=True),
        lax.all_gather(v_pack, "frame", axis=0, tiled=True),
    )
    k_every = k_every.reshape(frames_n, -1, width)
    v_every = v_every.reshape(frames_n, -1, width)
    position = 0
    for level in upper_levels:
        step = 2**level
        rows = count // step
        start = jnp.bitwise_xor(current // step, 1) * step
        block_k = lax.dynamic_slice_in_dim(k_every[:, position : position + rows], start, step, 0)
        block_v = lax.dynamic_slice_in_dim(v_every[:, position : position + rows], start, step, 0)
        sibling[level] = (block_k, block_v)
        position = position + rows
    swap_levels = [level for level in range(1, depth) if level < cut]
    growing = {level: own[level] for level in swap_levels}
    sections = cut if swap_levels else 0
    for bit in range(sections):
        active = [level for level in swap_levels if level >= bit]
        k_pack = jnp.concatenate([growing[level][0].reshape(-1, width) for level in active])
        v_pack = jnp.concatenate([growing[level][1].reshape(-1, width) for level in active])
        k_in, v_in = (
            from_partner(shortened(k_pack), "frame", bit).astype(k_pack.dtype),
            from_partner(shortened(v_pack), "frame", bit).astype(v_pack.dtype),
        )
        upper = current // 2**bit % 2
        position = 0
        for level in active:
            shape = growing[level][0].shape
            size = shape[0] * shape[1]
            theirs_k = k_in[position : position + size].reshape(shape)
            theirs_v = v_in[position : position + size].reshape(shape)
            position = position + size
            if level == bit:
                sibling[level] = (theirs_k, theirs_v)
            else:
                growing[level] = (
                    ordered(growing[level][0], theirs_k, upper),
                    ordered(growing[level][1], theirs_v, upper),
                )
    for level in range(1, depth):
        step = 2**level
        start = jnp.bitwise_xor(current // step, 1) * step
        frame_ids = start + jnp.arange(step, dtype=jnp.int32)
        allowed = lax.dynamic_slice_in_dim(mask_row, start, step, 0)
        good = ((jnp.abs(frame_ids - current) >= 2) & (allowed == 1)).astype(jnp.float32)
        block_k, block_v = sibling[level]
        key_parts.append(block_k.reshape(-1, width))
        value_parts.append(block_v.reshape(-1, width))
        valid_parts.append(jnp.repeat(good, block_k.shape[1]))
    result = attend(
        q_rows,
        jnp.concatenate(key_parts),
        jnp.concatenate(value_parts),
        jnp.concatenate(valid_parts),
    )
    return lax.all_to_all(result, "head", split_axis=0, concat_axis=1, tiled=True)


def solution(mesh):
    return jax.shard_map(
        per_device,
        mesh=mesh,
        in_specs=(
            P(("parts", "frame", "head"), None),
            P(("parts", "frame", "head"), None),
            P(("parts", "frame", "head"), None),
            P(("parts", "frame"), None),
            P(("parts", "frame")),
        ),
        out_specs=P(("parts", "frame", "head"), None),
        check_vma=False,
    )
```

profile of v0, /device:TPU:0, one launch (start us, length us, event | category | flops | bytes accessed | tf_op | source)
XLA Modules:
  0.0 171.4 jit_solution(8684390858961733421)
XLA Ops:
  6.5 2.2 %copy.34 = bf16[128,2560]{0,1:T(8,128)(2,1)} copy(bf16[128,2560]{1,0:T(8,128)(2,1)} %param.8) | data formatting | bytes 1310720 | tf_op args[1]
  8.8 4.2 %all-to-all-start.1 = ((bf16[128,4,640]{0,2,1:T(8,128)(2,1)}), bf16[128,4,640]{0,2,1:T(8,128)(2,1)S(1)}, u32[]{:S(2)}, u32[]{:S(2)}) async-start(bf16[128,4,640]{0,2,1:T(8,128)(2,1)} %bitcast.8), calls=%async_computation.1 | async-start | bytes 1310720 | tf_op jit(solution)/shard_map/all_to_all | solution.py:73
  13.6 9.6 %all-to-all-done.1 = bf16[128,4,640]{0,2,1:T(8,128)(2,1)S(1)} async-done(((bf16[128,4,640]{0,2,1:T(8,128)(2,1)}), bf16[128,4,640]{0,2,1:T(8,128)(2,1)S(1)}, u32[]{:S(2)}, u32[]{:S(2)}) %all-to-all-start.1) | async-done | bytes 655392 | tf_op jit(solution)/shard_map/all_to_all | solution.py:73
  23.2 0.3 copy.35
  23.5 0.7 constant_dynamic-slice_fusion.3
  24.4 0.3 copy.36
  24.7 12.7 %all_to_all.64 = bf16[128,4,640]{0,2,1:T(8,128)(2,1)S(1)} all-to-all(bf16[128,4,640]{0,2,1:T(8,128)(2,1)S(1)} %bitcast.85), channel_id=1, replica_groups=mesh['parts'=2,'frame'=4,'head'=4] {'head'}, dimensions={1} | all-to-all | bytes 1310720 | tf_op jit(solution)/shard_map/all_to_all | solution.py:74
  37.6 1.2 pad_maximum_fusion.1
  38.9 5.2 %collective-permute-start = (bf16[2,512,640]{2,1,0:T(8,128)(2,1)}, bf16[2,512,640]{2,1,0:T(8,128)(2,1)}, u32[]{:S(2)}, u32[]{:S(2)}) collective-permute-start(bf16[2,512,640]{2,1,0:T(8,128)(2,1)} %pad_maximum_fusion.1), channel_id=1, source_target_pairs={{0,4},{4,8},{8,12},{1,5},{5,9},{9,13},{2,6},{6,10},{10,14},{3,7},{... | collective-permute-start | bytes 3932168 | tf_op jit(solution)/shard_map/ppermute | solution.py:16
  44.1 1.3 collective-permute-start.1
  45.4 0.8 constant_dynamic-slice_fusion.1
  46.2 1.1 copy.32
  47.3 3.5 %all-to-all-start = ((bf16[128,4,640]{0,2,1:T(8,128)(2,1)}), bf16[128,4,640]{0,2,1:T(8,128)(2,1)S(1)}, u32[]{:S(2)}, u32[]{:S(2)}) async-start(bf16[128,4,640]{0,2,1:T(8,128)(2,1)} %bitcast.5), calls=%async_computation | async-start | bytes 1310720 | tf_op jit(solution)/shard_map/all_to_all | solution.py:72
  51.0 9.9 %all-to-all-done = bf16[128,4,640]{0,2,1:T(8,128)(2,1)S(1)} async-done(((bf16[128,4,640]{0,2,1:T(8,128)(2,1)}), bf16[128,4,640]{0,2,1:T(8,128)(2,1)S(1)}, u32[]{:S(2)}, u32[]{:S(2)}) %all-to-all-start) | async-done | bytes 655392 | tf_op jit(solution)/shard_map/all_to_all | solution.py:72
  61.0 0.5 copy.33
  61.7 26.5 %collective-permute-done = bf16[2,512,640]{2,1,0:T(8,128)(2,1)} collective-permute-done((bf16[2,512,640]{2,1,0:T(8,128)(2,1)}, bf16[2,512,640]{2,1,0:T(8,128)(2,1)}, u32[]{:S(2)}, u32[]{:S(2)}) %collective-permute-start) | collective-permute-done | bytes 1310752 | tf_op jit(solution)/shard_map/ppermute | solution.py:16
  88.3 7.3 %collective-permute-done.1 = bf16[2,512,640]{2,1,0:T(8,128)(2,1)} collective-permute-done((bf16[2,512,640]{2,1,0:T(8,128)(2,1)}, bf16[2,512,640]{2,1,0:T(8,128)(2,1)}, u32[]{:S(2)}, u32[]{:S(2)}) %collective-permute-start.1) | collective-permute-done | bytes 1310752 | tf_op jit(solution)/shard_map/ppermute | solution.py:17
  95.5 5.5 %pad_maximum_fusion = bf16[2,1536,640]{2,1,0:T(8,128)(2,1)S(1)} fusion(bf16[2,512,640]{2,1,0:T(8,128)(2,1)} %collective-permute-done.1, bf16[1,512,640]{2,1,0:T(8,128)(2,1)S(1)} %bitcast.77, bf16[1,512,640]{2,1,0:T(8,128)(2,1)S(1)} %bitcast.74, bf16[2,512,640]{2,1,0:T(8,128)(2,1)} %collective-permute-done), kind=kLoop, calls=%fused_computation.22 | loop fusion | flops 15728640 | bytes 7864320 | tf_op jit(solution)/shard_map/concatenate | solution.py:18
  101.0 2.2 %fusion.27 = (bf16[1,1536,640]{2,1,0:T(8,128)(2,1)}, bf16[1,1536,640]{2,1,0:T(8,128)(2,1)}) fusion(bf16[2,1536,640]{2,1,0:T(8,128)(2,1)S(1)} %pad_maximum_fusion), kind=kLoop, calls=%fused_computation.37 | loop fusion | bytes 7864320 | tf_op jit(solution)/shard_map/slice | solution.py:86
  103.3 2.7 %copy.41 = bf16[1,1536,640]{1,2,0:T(8,128)(2,1)S(1)} copy(bf16[1,1536,640]{2,1,0:T(8,128)(2,1)} %get-tuple-element.70) | data formatting | bytes 3932160 | tf_op jit(solution)/shard_map/slice | solution.py:86
  105.9 4.0 %copy.38 = bf16[1,1536,640]{1,2,0:T(8,128)(2,1)} copy(bf16[1,1536,640]{2,1,0:T(8,128)(2,1)} %get-tuple-element.71) | data formatting | bytes 3932160 | tf_op jit(solution)/shard_map/slice | solution.py:85
  110.0 2.2 %constant_dynamic-slice_fusion = (bf16[2,256,640]{2,1,0:T(8,128)(2,1)S(1)}, bf16[2,256,640]{2,1,0:T(8,128)(2,1)}) fusion(bf16[4,256,640]{2,1,0:T(8,128)(2,1)} %bitcast.87, s32[]{:T(128)S(6)} %select_n.29, bf16[4,256,640]{2,1,0:T(8,128)(2,1)} %bitcast.86), kind=kLoop, calls=%fused_computation.31 | loop fusion | bytes 2621444 | tf_op jit(solution)/shard_map/dynamic_slice | solution.py:115
  112.2 1.8 %copy.54 = bf16[2,256,640]{1,0,2:T(2,128)(2,1)} copy(bf16[2,256,640]{2,1,0:T(8,128)(2,1)S(1)} %get-tuple-element.72) | data formatting | bytes 1310720
  114.0 2.2 %concatenate.28 = bf16[512,5,128]{0,2,1:T(8,128)(2,1)S(1)} reshape(bf16[2,256,640]{1,0,2:T(2,128)(2,1)} %copy.54) | data formatting | bytes 1310720 | tf_op jit(solution)/shard_map/concatenate | solution.py:157
  116.2 2.9 %copy.53 = bf16[2,256,640]{1,0,2:T(2,128)(2,1)} copy(bf16[2,256,640]{2,1,0:T(8,128)(2,1)} %get-tuple-element.73) | data formatting | bytes 1310720
  119.2 2.9 %concatenate.25 = bf16[512,5,128]{0,2,1:T(8,128)(2,1)} reshape(bf16[2,256,640]{1,0,2:T(2,128)(2,1)} %copy.53) | data formatting | bytes 1310720 | tf_op jit(solution)/shard_map/concatenate | solution.py:156
  122.0 1.9 %maximum_bitcast_fusion.1 = bf16[5,2048,128]{1,2,0:T(8,128)(2,1)} fusion(bf16[512,5,128]{0,2,1:T(8,128)(2,1)S(1)} %concatenate.28, bf16[1536,5,128]{0,2,1:T(8,128)(2,1)S(1)} %bitcast.78), kind=kLoop, calls=%fused_computation.24 | loop fusion | flops 5242880 | bytes 5242880 | tf_op jit(solution)/shard_map/transpose | solution.py:47
  124.0 0.6 copy-done.1
  124.6 0.3 maximum_bitcast_fusion
  124.9 24.3 %while.10 = (s32[]{:T(128)}, bf16[5,512,128]{2,1,0:T(8,128)(2,1)}, f32[2048]{0:T(1024)S(1)}, bf16[5,512,128]{1,2,0:T(8,128)(2,1)S(1)}, bf16[5,2048,128]{1,2,0:T(...) while((s32[]{:T(128)}, bf16[5,512,128]{2,1,0:T(8,128)(2,1)}, f32[2048]{0:T(1024)S(1)}, ...), condition=%wide.region_3.4_spmd, body=%wide.region_0.3_spmd.sunk | while | flops 550568960 | bytes 14069837 | solution.py:60
  125.0 0.9 fusion.35
  125.9 1.1 fusion.36
  127.0 2.8 %fusion.37 = bf16[5,512,128]{2,1,0:T(8,128)(2,1)} fusion(bf16[5,512,128]{2,1,0:T(8,128)(2,1)} %get-tuple-element.123, s32[]{:T(128)} %get-tuple-element.122, f32[512,2048]{1,0:T(8,128)S(1)} %get-tuple-element.113, f32[2048]{0:T(1024)S(1)} %get-tuple-element.131, f32[512]{0:T(512)S(1)} %get-tuple-element.114, ...), kind=kOutput, calls=%fused_computation.9.clone.1 | convolution fusion | flops 273743872 | bytes 4996096 | tf_op jit(solution)/shard_map/while/body/eval_jaxpr/dot_general | solution.py:57
  129.8 0.9 fusion.35
  130.7 1.1 fusion.36
  131.8 2.8 %fusion.37 = bf16[5,512,128]{2,1,0:T(8,128)(2,1)} fusion(bf16[5,512,128]{2,1,0:T(8,128)(2,1)} %get-tuple-element.123, s32[]{:T(128)} %get-tuple-element.122, f32[512,2048]{1,0:T(8,128)S(1)} %get-tuple-element.113, f32[2048]{0:T(1024)S(1)} %get-tuple-element.131, f32[512]{0:T(512)S(1)} %get-tuple-element.114, ...), kind=kOutput, calls=%fused_computation.9.clone.1 | convolution fusion | flops 273743872 | bytes 4996096 | tf_op jit(solution)/shard_map/while/body/eval_jaxpr/dot_general | solution.py:57
  134.7 0.9 fusion.35
  135.6 1.1 fusion.36
  136.7 2.8 %fusion.37 = bf16[5,512,128]{2,1,0:T(8,128)(2,1)} fusion(bf16[5,512,128]{2,1,0:T(8,128)(2,1)} %get-tuple-element.123, s32[]{:T(128)} %get-tuple-element.122, f32[512,2048]{1,0:T(8,128)S(1)} %get-tuple-element.113, f32[2048]{0:T(1024)S(1)} %get-tuple-element.131, f32[512]{0:T(512)S(1)} %get-tuple-element.114, ...), kind=kOutput, calls=%fused_computation.9.clone.1 | convolution fusion | flops 273743872 | bytes 4996096 | tf_op jit(solution)/shard_map/while/body/eval_jaxpr/dot_general | solution.py:57
  139.5 0.9 fusion.35
  140.4 1.1 fusion.36
  141.5 2.8 %fusion.37 = bf16[5,512,128]{2,1,0:T(8,128)(2,1)} fusion(bf16[5,512,128]{2,1,0:T(8,128)(2,1)} %get-tuple-element.123, s32[]{:T(128)} %get-tuple-element.122, f32[512,2048]{1,0:T(8,128)S(1)} %get-tuple-element.113, f32[2048]{0:T(1024)S(1)} %get-tuple-element.131, f32[512]{0:T(512)S(1)} %get-tuple-element.114, ...), kind=kOutput, calls=%fused_computation.9.clone.1 | convolution fusion | flops 273743872 | bytes 4996096 | tf_op jit(solution)/shard_map/while/body/eval_jaxpr/dot_general | solution.py:57
  144.4 0.9 fusion.35
  145.3 1.1 fusion.36
  146.4 2.8 %fusion.37 = bf16[5,512,128]{2,1,0:T(8,128)(2,1)} fusion(bf16[5,512,128]{2,1,0:T(8,128)(2,1)} %get-tuple-element.123, s32[]{:T(128)} %get-tuple-element.122, f32[512,2048]{1,0:T(8,128)S(1)} %get-tuple-element.113, f32[2048]{0:T(1024)S(1)} %get-tuple-element.131, f32[512]{0:T(512)S(1)} %get-tuple-element.114, ...), kind=kOutput, calls=%fused_computation.9.clone.1 | convolution fusion | flops 273743872 | bytes 4996096 | tf_op jit(solution)/shard_map/while/body/eval_jaxpr/dot_general | solution.py:57
  149.2 1.3 copy.47
  150.8 12.7 %all_to_all.65 = bf16[4,128,640]{1,2,0:T(8,128)(2,1)S(1)} all-to-all(bf16[4,128,640]{1,2,0:T(8,128)(2,1)S(1)} %copy.48), channel_id=1, replica_groups=mesh['parts'=2,'frame'=4,'head'=4] {'head'}, dimensions={0} | all-to-all | bytes 1310720 | tf_op jit(solution)/shard_map/all_to_all | solution.py:160
  163.4 1.1 copy.49
  (32 shorter events, 1.2 us)
Async XLA Ops:
  6.5 17.8 %copy-start.2 = (bf16[128,2560]{1,0:T(8,128)(2,1)S(1)}, bf16[128,2560]{1,0:T(8,128)(2,1)}, u32[]{:S(2)}) copy-start(bf16[128,2560]{1,0:T(8,128)(2,1)} %param.9) | copy-start | bytes 1966084
  8.8 14.5 %all-to-all-start.1 = ((bf16[128,4,640]{0,2,1:T(8,128)(2,1)}), bf16[128,4,640]{0,2,1:T(8,128)(2,1)S(1)}, u32[]{:S(2)}, u32[]{:S(2)}) async-start(bf16[128,4,640]{0,2,1:T(8,128)(2,1)} %bitcast.8), calls=%async_computation.1 | async-start | bytes 1310720 | tf_op jit(solution)/shard_map/all_to_all | solution.py:73
  13.0 97.0 %all-gather.5.cloned.1.call-start = ((), (), s32[]{:S(2)}) async-start(), calls=%async_computation.4 | async-start | bytes 1638400 | tf_op jit(solution)/shard_map/all_gather | solution.py:104
  24.3 21.9 %copy-start.3 = (bf16[128,2560]{1,0:T(8,128)(2,1)S(1)}, bf16[128,2560]{1,0:T(8,128)(2,1)}, u32[]{:S(2)}) copy-start(bf16[128,2560]{1,0:T(8,128)(2,1)} %param.7) | copy-start | bytes 1966084
  24.3 85.7 %all-gather.7.cloned.1.call-start = ((), (), s32[]{:S(2)}) async-start(), calls=%async_computation.5 | async-start | bytes 1638400 | tf_op jit(solution)/shard_map/all_gather | solution.py:105
  37.3 13.4 %copy-start.4 = (s32[1,4]{1,0:T(1,128)S(1)}, s32[1,4]{1,0:T(1,128)}, u32[]{:S(2)}) copy-start(s32[1,4]{1,0:T(1,128)} %param.10) | copy-start | bytes 52
  38.9 49.4 %collective-permute-start = (bf16[2,512,640]{2,1,0:T(8,128)(2,1)}, bf16[2,512,640]{2,1,0:T(8,128)(2,1)}, u32[]{:S(2)}, u32[]{:S(2)}) collective-permute-start(bf16[2,512,640]{2,1,0:T(8,128)(2,1)} %pad_maximum_fusion.1), channel_id=1, source_target_pairs={{0,4},{4,8},{8,12},{1,5},{5,9},{9,13},{2,6},{6,10},{10,14},{3,7},{... | collective-permute-start | bytes 3932168 | tf_op jit(solution)/shard_map/ppermute | solution.py:16
  44.1 51.4 %collective-permute-start.1 = (bf16[2,512,640]{2,1,0:T(8,128)(2,1)}, bf16[2,512,640]{2,1,0:T(8,128)(2,1)}, u32[]{:S(2)}, u32[]{:S(2)}) collective-permute-start(bf16[2,512,640]{2,1,0:T(8,128)(2,1)} %pad_maximum_fusion.1), channel_id=1, source_target_pairs={{4,0},{8,4},{12,8},{5,1},{9,5},{13,9},{6,2},{10,6},{14,10},{7,3},{... | collective-permute-start | bytes 3932168 | tf_op jit(solution)/shard_map/ppermute | solution.py:17
  47.3 13.7 %all-to-all-start = ((bf16[128,4,640]{0,2,1:T(8,128)(2,1)}), bf16[128,4,640]{0,2,1:T(8,128)(2,1)S(1)}, u32[]{:S(2)}, u32[]{:S(2)}) async-start(bf16[128,4,640]{0,2,1:T(8,128)(2,1)} %bitcast.5), calls=%async_computation | async-start | bytes 1310720 | tf_op jit(solution)/shard_map/all_to_all | solution.py:72
  122.0 2.0 %copy-start = (bf16[1,1536,640]{1,2,0:T(8,128)(2,1)S(1)}, bf16[1,1536,640]{1,2,0:T(8,128)(2,1)}, u32[]{:S(2)}) copy-start(bf16[1,1536,640]{1,2,0:T(8,128)(2,1)} %copy.38) | copy-start | bytes 5898244
  122.0 2.6 %copy-start.1 = (bf16[512,5,128]{0,2,1:T(8,128)(2,1)S(1)}, bf16[512,5,128]{0,2,1:T(8,128)(2,1)}, u32[]{:S(2)}) copy-start(bf16[512,5,128]{0,2,1:T(8,128)(2,1)} %concatenate.25) | copy-start | bytes 1966084
Sparse Core Ops, SparseCore 0:
  24.4 41.4 all-gather.4
  67.4 39.9 all-gather.6
where the time goes:
time: 172 us; the launch traced here: 171 us
  waiting for transfers between devices  53.3 us (31%)
  local copies, waits for them, and re-layouts  31 us (18%)
  blocking collectives  25.3 us (15%)
  matrix products  18.7 us (11%)
  other arithmetic  14.5 us (8%)
  starting transfers between devices  14.2 us (8%)
  between operations  14.2 us (8%)
    ppermute x1, waiting for transfers between devices, padded(): before = lax.ppermute(last, axis, up)  26.5 us
    dot_general x5, matrix products, one_head(): jnp.dot(weights.astype(jnp.bfloat16), v_head, preferred_element_type=jnp....  14.2 us
    all_to_all x1, blocking collectives, per_device(): lax.all_to_all(values, 'head', split_axis=1, concat_axis=0, tiled=True)  12.7 us
    all_to_all x1, blocking collectives, per_device(): lax.all_to_all(result, 'head', split_axis=0, concat_axis=1, tiled=True)  12.7 us
    all_to_all x1, waiting for transfers between devices, per_device(): lax.all_to_all(queries, 'head', split_axis=1, concat_axis=0, tiled=True)  9.93 us
    all_to_all x1, waiting for transfers between devices, per_device(): lax.all_to_all(keys, 'head', split_axis=1, concat_axis=0, tiled=True)  9.58 us
    unnamed x17, local copies, waits for them, and re-layouts  9.13 us
    ppermute x1, waiting for transfers between devices, padded(): after = lax.ppermute(leading, axis, down)  7.26 us
  transfers between devices with their start and end apart: 6, of which 4 were waited for; matrix products, arithmetic and copies ran while one was open for 11% of the time, Pallas kernels for 0%

commit v1 on v0

--- a/solution.py
+++ b/solution.py
@@ -1,9 +1,15 @@
+import math
+
 import jax
 import jax.numpy as jnp
 from jax import lax
+from jax.experimental import pallas as pl
+from jax.experimental.pallas import tpu as pltpu
 from jax.sharding import PartitionSpec as P
 
 HEAD_DIM = 128
+SCALE = 1.0 / HEAD_DIM**0.5
+LOG2E = math.log2(math.e)
 
 
 def padded(x, sides, width):
@@ -19,14 +25,6 @@
     return x
 
 
-def shortened(x):
-
-    def short(part):
-        return part.astype(jnp.bfloat16) if part.dtype == jnp.float32 else part
-
-    return jax.tree.map(short, x)
-
-
 def from_partner(x, axis, bit):
     return lax.ppermute(x, axis, [(i, i ^ 1 << bit) for i in range(lax.axis_size(axis))])
 
@@ -45,11 +43,10 @@
     q_three = query_rows.reshape(count, heads, HEAD_DIM).transpose(1, 0, 2)
     k_three = key_rows.reshape(-1, heads, HEAD_DIM).transpose(1, 0, 2)
     v_three = value_rows.reshape(-1, heads, HEAD_DIM).transpose(1, 0, 2)
-    scale = 1.0 / HEAD_DIM**0.5
 
     def one_head(operands):
         q_head, k_head, v_head = operands
-        scores = jnp.dot(q_head, k_head.T, preferred_element_type=jnp.float32) * scale
+        scores = jnp.dot(q_head, k_head.T, preferred_element_type=jnp.float32) * SCALE
         scores = jnp.where(valid[None, :] > 0, scores, -1e30)
         top = jnp.max(scores, axis=1, keepdims=True)
         weights = jnp.exp(scores - top) * valid[None, :]
@@ -65,7 +62,7 @@
     return jnp.where(upper == 1, jnp.concatenate([theirs, mine]), jnp.concatenate([mine, theirs]))
 
 
-def per_device(queries, keys, values, pair_mask, tile_offset):
+def general(queries, keys, values, pair_mask, tile_offset):
     frames_n = lax.axis_size("frame")
     current = lax.axis_index("frame")
     q_rows, k_rows, v_rows = (
@@ -122,10 +119,7 @@
         active = [level for level in swap_levels if level >= bit]
         k_pack = jnp.concatenate([growing[level][0].reshape(-1, width) for level in active])
         v_pack = jnp.concatenate([growing[level][1].reshape(-1, width) for level in active])
-        k_in, v_in = (
-            from_partner(shortened(k_pack), "frame", bit).astype(k_pack.dtype),
-            from_partner(shortened(v_pack), "frame", bit).astype(v_pack.dtype),
-        )
+        k_in, v_in = (from_partner(k_pack, "frame", bit), from_partner(v_pack, "frame", bit))
         upper = current // 2**bit % 2
         position = 0
         for level in active:
@@ -160,7 +154,119 @@
     return lax.all_to_all(result, "head", split_axis=0, concat_axis=1, tiled=True)
 
 
+def attention_kernel(info, q0, q1, q2, q3, own_s, own_u, n1_s, n1_u, n2_s, n2_u, r1, r2, r3, o0, o1, o2, o3, held):
+    tile = own_s.shape[1]
+    rows = q0.shape[0]
+    factor = SCALE * LOG2E
+
+    def body(slots):
+        for pair in ((q0, q1, o0, o1), (q2, q3, o2, o3)):
+            q = jnp.concatenate([pair[0][...], pair[1][...]], axis=0)
+            top = None
+            for at, (ref, valid) in enumerate(slots):
+                s = lax.dot_general(q, ref[0], (((1,), (1,)), ((), ())), preferred_element_type=jnp.float32)
+                held[:, at * tile : (at + 1) * tile] = s
+                best = jnp.max(s, axis=1, keepdims=True)
+                if valid is not None:
+                    best = jnp.where(valid == 1, best, -1e30)
+                top = best if top is None else jnp.maximum(top, best)
+            total, mixed = None, None
+            for at, (ref, valid) in enumerate(slots):
+                level = top if valid is None else jnp.where(valid == 1, top, 1e30)
+                w = jnp.exp2((held[:, at * tile : (at + 1) * tile] - level) * factor)
+                part = jnp.sum(w, axis=1, keepdims=True)
+                mix = jnp.dot(w.astype(jnp.bfloat16), ref[1], preferred_element_type=jnp.float32)
+                total = part if total is None else total + part
+                mixed = mix if mixed is None else mixed + mix
+            result = (mixed / total).astype(jnp.bfloat16)
+            pair[2][...] = result[:rows]
+            pair[3][...] = result[rows:]
+
+    always = [(own_s, None), (own_u, None), (n1_s, None), (n1_u, None)]
+
+    @pl.when(info[1] == 1)
+    def _():
+        body(always + [(n2_s, None), (n2_u, None), (r1, info[2])])
+
+    @pl.when(info[1] == 0)
+    def _():
+        body(always + [(r2, info[2]), (r3, info[3])])
+
+
+def attention(info, q_own, q_in, slots, heads):
+    rows = q_in[0].shape[0]
+    tile = slots[0].shape[1]
+    q_own_spec = pl.BlockSpec((rows, HEAD_DIM), lambda i, info: (0, info[0] * heads + i))
+    q_spec = pl.BlockSpec((rows, HEAD_DIM), lambda i, info: (0, i))
+    kv_spec = pl.BlockSpec((2, tile, HEAD_DIM), lambda i, info: (0, 0, i))
+    flops = heads * 4 * rows * 7 * tile * HEAD_DIM * 4
+    return pl.pallas_call(
+        attention_kernel,
+        grid_spec=pltpu.PrefetchScalarGridSpec(
+            num_scalar_prefetch=1,
+            grid=(heads,),
+            in_specs=[q_own_spec] + [q_spec] * 3 + [kv_spec] * len(slots),
+            out_specs=[q_spec] * 4,
+            scratch_shapes=[pltpu.VMEM((2 * rows, 7 * tile), jnp.float32)],
+        ),
+        out_shape=[jax.ShapeDtypeStruct((rows, heads * HEAD_DIM), jnp.bfloat16)] * 4,
+        compiler_params=pltpu.CompilerParams(vmem_limit_bytes=32 * 1024 * 1024),
+        cost_estimate=pl.CostEstimate(
+            flops=flops, bytes_accessed=heads * HEAD_DIM * 2 * (8 * rows + 18 * tile), transcendentals=heads * 28 * rows * tile
+        ),
+    )(info, q_own, *q_in, *slots)
+
+
+def four_frames(queries, keys, values, pair_mask, tile_offset):
+    z = lax.axis_index("frame")
+    h = lax.axis_index("head")
+    rows, features = queries.shape
+    width = features // 4
+    heads = width // HEAD_DIM
+
+    def columns(x, j):
+        return lax.dynamic_slice_in_dim(x, j * width, width, axis=1)
+
+    def to_head(x, d):
+        return lax.ppermute(x, "head", [(i, i ^ d) for i in range(4)])
+
+    def along(x, pairs):
+        return lax.ppermute(x, "frame", pairs)
+
+    kv = [jnp.stack([columns(keys, h ^ d), columns(values, h ^ d)]) for d in range(4)]
+    kv = [kv[0]] + [to_head(kv[d], d) for d in (1, 2, 3)]
+    mine = jnp.concatenate(kv[:2], axis=1)
+    other = jnp.concatenate(kv[2:], axis=1)
+    here = h // 2 == tile_offset[0]
+    own_s = jnp.where(here, mine, other)
+    own_u = jnp.where(here, other, mine)
+
+    outer = [(0, 1), (1, 0), (2, 3), (3, 2)]
+    inner = [(1, 2), (2, 1)]
+    outward = [(1, 0), (2, 3)]
+    n1_s = along(own_s, outer)
+    n2_s = along(own_s, inner)
+    r1 = along(n1_s, inner)
+    r2 = along(n2_s, outward)
+    n1_u = along(own_u, outer)
+    n2_u = along(own_u, inner)
+    r3 = along(r1, outward)
+
+    q_in = [to_head(columns(queries, h ^ d), d) for d in (1, 2, 3)]
+
+    mask_row = pair_mask[0]
+    info = jnp.stack([h, ((z == 1) | (z == 2)).astype(jnp.int32), mask_row[z ^ 2], mask_row[z ^ 3]]).astype(jnp.int32)
+    out = attention(info, queries, q_in, [own_s, own_u, n1_s, n1_u, n2_s, n2_u, r1, r2, r3], heads)
+    out = [out[0]] + [to_head(out[d], d) for d in (1, 2, 3)]
+    result = jnp.zeros((rows, features), jnp.bfloat16)
+    for d in range(4):
+        result = lax.dynamic_update_slice_in_dim(result, out[d], (h ^ d) * width, axis=1)
+    return result
+
+
 def solution(mesh):
+    sizes = dict(mesh.shape)
+    per_device = four_frames if sizes["frame"] == 4 and sizes["head"] == 4 else general
     return jax.shard_map(
         per_device,
         mesh=mesh,

time: 172 us -> 106 us (0.62)
  local copies, waits for them, and re-layouts: 31 us -> 5.35 us
  blocking collectives: 25.3 us -> 0 us
  matrix products: 18.7 us -> 0 us
  waiting for transfers between devices: 53.3 us -> 68.9 us
  between operations: 14.2 us -> 0.83 us
  other arithmetic: 14.5 us -> 1.69 us
  Pallas kernels: 0 us -> 9.83 us
  starting transfers between devices: 14.2 us -> 18.9 us
    ppermute x2 -> x16, waiting for transfers between devices: 33.8 us -> 68.9 us  [the longest x7 37.8 us: along(): return lax.ppermute(x, 'frame', pairs)]
    all_to_all x2 -> x0, blocking collectives: 25.3 us -> none  [the longest x1 12.7 us: per_device(): lax.all_to_all(values, 'head', split_axis=1, concat_axis=0, tiled=True)]
    all_to_all x2 -> x0, waiting for transfers between devices: 19.5 us -> none  [the longest x1 9.93 us: per_device(): lax.all_to_all(queries, 'head', split_axis=1, concat_axis=0, tiled=True)]
    dot_general x10 -> x0, matrix products: 18.7 us -> none  [the longest x5 14.2 us: one_head(): jnp.dot(weights.astype(jnp.bfloat16), v_head, preferred_element_type=jnp....]
    ppermute x2 -> x16, starting transfers between devices: 6.51 us -> 18.9 us  [the longest x7 11.7 us: along(): return lax.ppermute(x, 'frame', pairs)]
    pallas_call x0 -> x1, Pallas kernels: none -> 9.83 us  [attention(): pl.pallas_call(attention_kernel, grid_spec=pltpu.PrefetchScalarGridSpec(n...]
    slice x3 -> x0, local copies, waits for them, and re-layouts: 8.96 us -> none  [the longest x2 4.92 us: per_device(): value_parts = [near[1]]]
    all_to_all x2 -> x0, starting transfers between devices: 7.69 us -> none  [the longest x1 4.21 us: per_device(): lax.all_to_all(keys, 'head', split_axis=1, concat_axis=0, tiled=True)]
  transfers between devices with their start and end apart: 6 -> 16, of which waited for: 4 -> 10; matrix products, arithmetic and copies ran while one was open for 11% -> 3% of each run, Pallas kernels for 0% -> 0%
where the time goes in v1:
time: 106 us; the launch traced here: 105 us
  waiting for transfers between devices  68.9 us (65%)
  starting transfers between devices  18.9 us (18%)
  Pallas kernels  9.83 us (9%)
  local copies, waits for them, and re-layouts  5.35 us (5%)
  other arithmetic  1.69 us (2%)
    ppermute x7, waiting for transfers between devices, along(): return lax.ppermute(x, 'frame', pairs)  37.8 us
    ppermute x9, waiting for transfers between devices, to_head(): return lax.ppermute(x, 'head', [(i, i ^ d) for i in range(4)])  31.1 us
    ppermute x7, starting transfers between devices, along(): return lax.ppermute(x, 'frame', pairs)  11.7 us
    pallas_call x1, Pallas kernels, attention(): pl.pallas_call(attention_kernel, grid_spec=pltpu.PrefetchScalarGridSpec(n...  9.83 us
    ppermute x9, starting transfers between devices, to_head(): return lax.ppermute(x, 'head', [(i, i ^ d) for i in range(4)])  7.17 us
  transfers between devices with their start and end apart: 16, of which 10 were waited for; matrix products, arithmetic and copies ran while one was open for 3% of the time, Pallas kernels for 0%

profile of v1, /device:TPU:0, one launch (start us, length us, event | category | flops | bytes accessed | tf_op | source)
XLA Modules:
  0.0 105.5 jit_solution(15947098774293024752)
XLA Ops:
  0.0 1.5 %dynamic-slice_bitcast_fusion.6 = (bf16[1,128,640]{2,1,0:T(8,128)(2,1)S(1)}, bf16[1,128,640]{2,1,0:T(8,128)(2,1)S(1)}, bf16[1,128,640]{2,1,0:T(8,128)(2,1)S(1)},...) fusion(bf16[128,2560]{1,0:T(8,128)(2,1)} %param.7, ...), kind=kLoop, calls=%fused_computation.12 | loop fusion | bytes 2621456 | tf_op jit(solution)/shard_map/stack | solution.py:236
  1.6 3.0 %collective-permute-start.4 = (bf16[2,128,640]{2,1,0:T(8,128)(2,1)S(1)}, bf16[2,128,640]{2,1,0:T(8,128)(2,1)S(1)}, u32[]{:S(2)}, u32[]{:S(2)}) collective-permute-start(bf16[2,128,640]{2,1,0:T(8,128)(2,1)S(1)} %pad_maximum_fusion.2), channel_id=1, source_target_pairs={{0,2},{1,3},{2,0},{3,1},{4,6},{5,7},{6,4},{7,5},{8,10},{9,11},{10,... | collective-permute-start | bytes 983048 | tf_op jit(solution)/shard_map/ppermute | solution.py:231
  4.6 0.1 collective-permute-start.5
  4.7 0.2 collective-permute-start.3
  5.6 7.5 %collective-permute-done.4 = bf16[2,128,640]{2,1,0:T(8,128)(2,1)S(1)} collective-permute-done((bf16[2,128,640]{2,1,0:T(8,128)(2,1)S(1)}, bf16[2,128,640]{2,1,0:T(8,128)(2,1)S(1)}, u32[]{:S(2)}, u32[]{:S(2)}) %collective-permute-start.4) | collective-permute-done | bytes 327712 | tf_op jit(solution)/shard_map/ppermute | solution.py:231
  13.1 5.4 %collective-permute-done.5 = bf16[2,128,640]{2,1,0:T(8,128)(2,1)S(1)} collective-permute-done((bf16[2,128,640]{2,1,0:T(8,128)(2,1)S(1)}, bf16[2,128,640]{2,1,0:T(8,128)(2,1)S(1)}, u32[]{:S(2)}, u32[]{:S(2)}) %collective-permute-start.5) | collective-permute-done | bytes 327712 | tf_op jit(solution)/shard_map/ppermute | solution.py:231
  18.6 0.0 collective-permute-done.3
  18.6 0.0 copy-start
  18.6 0.2 broadcast_select_fusion
  18.9 0.0 copy-start.4
  18.9 1.6 %collective-permute-start.6 = (bf16[2,256,640]{2,1,0:T(8,128)(2,1)S(1)}, bf16[2,256,640]{2,1,0:T(8,128)(2,1)S(1)}, u32[]{:S(2)}, u32[]{:S(2)}) collective-permute-start(bf16[2,256,640]{2,1,0:T(8,128)(2,1)S(1)} %get-tuple-element.14.own_s), channel_id=1, source_target_pairs={{0,4},{4,0},{8,12},{12,8},{1,5},{5,1},{9,13},{13,9},{2,6},{6,2},{1... | collective-permute-start | bytes 1966088 | tf_op jit(solution)/shard_map/ppermute | solution.py:234
  20.5 0.7 collective-permute-start.8
  21.2 15.0 %collective-permute-done.6.n1_s = bf16[2,256,640]{2,1,0:T(8,128)(2,1)S(1)} collective-permute-done((bf16[2,256,640]{2,1,0:T(8,128)(2,1)S(1)}, bf16[2,256,640]{2,1,0:T(8,128)(2,1)S(1)}, u32[]{:S(2)}, u32[]{:S(2)}) %collective-permute-start.6) | collective-permute-done | bytes 655392 | tf_op jit(solution)/shard_map/ppermute | solution.py:234
  36.2 1.5 %collective-permute-start.10 = (bf16[2,256,640]{2,1,0:T(8,128)(2,1)S(1)}, bf16[2,256,640]{2,1,0:T(8,128)(2,1)}, u32[]{:S(2)}, u32[]{:S(2)}) collective-permute-start(bf16[2,256,640]{2,1,0:T(8,128)(2,1)S(1)} %collective-permute-done.6.n1_s), channel_id=1, source_target_pairs={{4,8},{8,4},{5,9},{9,5},{6,10},{10,6},{7,11},{11,7},{20,24},{24,20... | collective-permute-start | bytes 1966088 | tf_op jit(solution)/shard_map/ppermute | solution.py:234
  37.8 3.8 %collective-permute-start.7 = (bf16[2,256,640]{2,1,0:T(8,128)(2,1)S(1)}, bf16[2,256,640]{2,1,0:T(8,128)(2,1)}, u32[]{:S(2)}, u32[]{:S(2)}) collective-permute-start(bf16[2,256,640]{2,1,0:T(8,128)(2,1)S(1)} %get-tuple-element.13.own_u), channel_id=1, source_target_pairs={{0,4},{4,0},{8,12},{12,8},{1,5},{5,1},{9,13},{13,9},{2,6},{6,2},{1... | collective-permute-start | bytes 1966088 | tf_op jit(solution)/shard_map/ppermute | solution.py:234
  41.5 1.5 %collective-permute-start.9 = (bf16[2,256,640]{2,1,0:T(8,128)(2,1)S(1)}, bf16[2,256,640]{2,1,0:T(8,128)(2,1)}, u32[]{:S(2)}, u32[]{:S(2)}) collective-permute-start(bf16[2,256,640]{2,1,0:T(8,128)(2,1)S(1)} %get-tuple-element.13.own_u), channel_id=1, source_target_pairs={{4,8},{8,4},{5,9},{9,5},{6,10},{10,6},{7,11},{11,7},{20,24},{24,20... | collective-permute-start | bytes 1966088 | tf_op jit(solution)/shard_map/ppermute | solution.py:234
  43.0 0.0 collective-permute-done.8.n2_s
  43.0 1.3 %collective-permute-start.11 = (bf16[2,256,640]{2,1,0:T(8,128)(2,1)S(1)}, bf16[2,256,640]{2,1,0:T(8,128)(2,1)}, u32[]{:S(2)}, u32[]{:S(2)}) collective-permute-start(bf16[2,256,640]{2,1,0:T(8,128)(2,1)S(1)} %collective-permute-done.8.n2_s), channel_id=1, source_target_pairs={{4,0},{8,12},{5,1},{9,13},{6,2},{10,14},{7,3},{11,15},{20,16},{24,... | collective-permute-start | bytes 1966088 | tf_op jit(solution)/shard_map/ppermute | solution.py:234
  44.3 0.0 collective-permute-done.10.r1
  44.3 1.3 %collective-permute-start.12 = (bf16[2,256,640]{2,1,0:T(8,128)(2,1)}, bf16[2,256,640]{2,1,0:T(8,128)(2,1)}, u32[]{:S(2)}, u32[]{:S(2)}) collective-permute-start(bf16[2,256,640]{2,1,0:T(8,128)(2,1)} %collective-permute-done.10.r1), channel_id=1, source_target_pairs={{4,0},{8,12},{5,1},{9,13},{6,2},{10,14},{7,3},{11,15},{20,16},{24,... | collective-permute-start | bytes 1966088 | tf_op jit(solution)/shard_map/ppermute | solution.py:234
  45.6 0.0 copy-done
  45.7 0.7 constant_dynamic-slice_fusion
  46.4 0.0 collective-permute-start
  46.4 1.4 %collective-permute-done.q1 = bf16[128,640]{1,0:T(8,128)(2,1)S(1)} collective-permute-done((bf16[128,640]{1,0:T(8,128)(2,1)S(1)}, bf16[128,640]{1,0:T(8,128)(2,1)S(1)}, u32[]{:S(2)}, u32[]{:S(2)}) %collective-permute-start) | collective-permute-done | bytes 163872 | tf_op jit(solution)/shard_map/ppermute | solution.py:231
  47.8 1.5 %collective-permute-start.1 = (bf16[128,640]{1,0:T(8,128)(2,1)S(1)}, bf16[128,640]{1,0:T(8,128)(2,1)S(1)}, u32[]{:S(2)}, u32[]{:S(2)}) collective-permute-start(bf16[128,640]{1,0:T(8,128)(2,1)S(1)} %get-tuple-element.24), channel_id=1, source_target_pairs={{0,2},{1,3},{2,0},{3,1},{4,6},{5,7},{6,4},{7,5},{8,10},{9,11},{10,... | collective-permute-start | bytes 491528 | tf_op jit(solution)/shard_map/ppermute | solution.py:231
  49.3 4.8 %collective-permute-done.1.q2 = bf16[128,640]{1,0:T(8,128)(2,1)S(1)} collective-permute-done((bf16[128,640]{1,0:T(8,128)(2,1)S(1)}, bf16[128,640]{1,0:T(8,128)(2,1)S(1)}, u32[]{:S(2)}, u32[]{:S(2)}) %collective-permute-start.1) | collective-permute-done | bytes 163872 | tf_op jit(solution)/shard_map/ppermute | solution.py:231
  54.0 0.0 copy-start.1
  54.0 0.7 copy-done.1
  54.7 0.5 collective-permute-start.2
  55.2 0.0 copy-done.4
  55.2 0.6 constant_dynamic-slice_fusion.4
  55.8 1.3 %pad_add_fusion.info = s32[4]{0:T(128)S(1)} fusion(s32[1]{0:T(128)} %bitcast.3, s32[1]{0:T(128)} %bitcast.2, s32[1]{0:T(128)} %bitcast.1, s32[1]{0:T(128)} %bitcast), kind=kLoop, calls=%fused_computation.25 | loop fusion | flops 12 | bytes 32 | tf_op jit(solution)/shard_map/stack | solution.py:258
  57.2 4.3 %collective-permute-done.2.q3 = bf16[128,640]{1,0:T(8,128)(2,1)} collective-permute-done((bf16[128,640]{1,0:T(8,128)(2,1)}, bf16[128,640]{1,0:T(8,128)(2,1)}, u32[]{:S(2)}, u32[]{:S(2)}) %collective-permute-start.2) | collective-permute-done | bytes 163872 | tf_op jit(solution)/shard_map/ppermute | solution.py:231
  61.5 0.0 collective-permute-done.7.n1_u
  61.5 0.0 collective-permute-done.9.n2_u
  61.5 9.8 %collective-permute-done.11.r2 = bf16[2,256,640]{2,1,0:T(8,128)(2,1)} collective-permute-done((bf16[2,256,640]{2,1,0:T(8,128)(2,1)S(1)}, bf16[2,256,640]{2,1,0:T(8,128)(2,1)}, u32[]{:S(2)}, u32[]{:S(2)}) %collective-permute-start.11) | collective-permute-done | bytes 655392 | tf_op jit(solution)/shard_map/ppermute | solution.py:234
  71.3 13.0 %collective-permute-done.12.r3 = bf16[2,256,640]{2,1,0:T(8,128)(2,1)} collective-permute-done((bf16[2,256,640]{2,1,0:T(8,128)(2,1)}, bf16[2,256,640]{2,1,0:T(8,128)(2,1)}, u32[]{:S(2)}, u32[]{:S(2)}) %collective-permute-start.12) | collective-permute-done | bytes 655392 | tf_op jit(solution)/shard_map/ppermute | solution.py:234
  84.3 0.9 copy-done.2
  85.2 9.8 %shard_map.55 = (bf16[128,640]{1,0:T(8,128)(2,1)S(1)}, bf16[128,640]{1,0:T(8,128)(2,1)S(1)}, bf16[128,640]{1,0:T(8,128)(2,1)S(1)}, bf16[128,640]{1,0:T(8,128)(2,1)S(1)}) custom-call(s32[4]{0:T(128)S(1)} %pad_add_fusion.info, bf16[128,2560]{1,0:T(8,128)(2,1)S(1)} %copy-done, bf16[128,640]{1,0:T(8,128)(2,1)S(1)} %collective-permute-done.q1, ...), custom_call_target="tpu_custom_call" | custom-call | flops 2348810240 | bytes 7208960 | tf_op jit(solution)/shard_map/pallas_call | solution.py:203
  95.0 0.1 collective-permute-start.13
  95.1 1.7 %collective-permute-start.14 = (bf16[128,640]{1,0:T(8,128)(2,1)S(1)}, bf16[128,640]{1,0:T(8,128)(2,1)S(1)}, u32[]{:S(2)}, u32[]{:S(2)}) collective-permute-start(bf16[128,640]{1,0:T(8,128)(2,1)S(1)} %get-tuple-element.11), channel_id=1, source_target_pairs={{0,2},{1,3},{2,0},{3,1},{4,6},{5,7},{6,4},{7,5},{8,10},{9,11},{10,... | collective-permute-start | bytes 491528 | tf_op jit(solution)/shard_map/ppermute | solution.py:231
  96.8 0.1 collective-permute-start.15
  97.1 0.0 collective-permute-done.13
  97.1 5.1 %collective-permute-done.14 = bf16[128,640]{1,0:T(8,128)(2,1)S(1)} collective-permute-done((bf16[128,640]{1,0:T(8,128)(2,1)S(1)}, bf16[128,640]{1,0:T(8,128)(2,1)S(1)}, u32[]{:S(2)}, u32[]{:S(2)}) %collective-permute-start.14) | collective-permute-done | bytes 163872 | tf_op jit(solution)/shard_map/ppermute | solution.py:231
  102.2 0.0 copy-start.3
  102.2 2.6 %collective-permute-done.15 = bf16[128,640]{1,0:T(8,128)(2,1)S(1)} collective-permute-done((bf16[128,640]{1,0:T(8,128)(2,1)S(1)}, bf16[128,640]{1,0:T(8,128)(2,1)S(1)}, u32[]{:S(2)}, u32[]{:S(2)}) %collective-permute-start.15) | collective-permute-done | bytes 163872 | tf_op jit(solution)/shard_map/ppermute | solution.py:231
  104.8 0.0 copy-done.3
  104.8 0.7 constant_dynamic-update-slice_fusion.2
  (10 shorter events, 0.3 us)
Async XLA Ops:
  1.6 11.5 %collective-permute-start.4 = (bf16[2,128,640]{2,1,0:T(8,128)(2,1)S(1)}, bf16[2,128,640]{2,1,0:T(8,128)(2,1)S(1)}, u32[]{:S(2)}, u32[]{:S(2)}) collective-permute-start(bf16[2,128,640]{2,1,0:T(8,128)(2,1)S(1)} %pad_maximum_fusion.2), channel_id=1, source_target_pairs={{0,2},{1,3},{2,0},{3,1},{4,6},{5,7},{6,4},{7,5},{8,10},{9,11},{10,... | collective-permute-start | bytes 983048 | tf_op jit(solution)/shard_map/ppermute | solution.py:231
  4.6 14.0 %collective-permute-start.5 = (bf16[2,128,640]{2,1,0:T(8,128)(2,1)S(1)}, bf16[2,128,640]{2,1,0:T(8,128)(2,1)S(1)}, u32[]{:S(2)}, u32[]{:S(2)}) collective-permute-start(bf16[2,128,640]{2,1,0:T(8,128)(2,1)S(1)} %pad_maximum_fusion.3), channel_id=1, source_target_pairs={{0,3},{1,2},{2,1},{3,0},{4,7},{5,6},{6,5},{7,4},{8,11},{9,10},{10,... | collective-permute-start | bytes 983048 | tf_op jit(solution)/shard_map/ppermute | solution.py:231
  4.7 13.9 %collective-permute-start.3 = (bf16[2,128,640]{2,1,0:T(8,128)(2,1)S(1)}, bf16[2,128,640]{2,1,0:T(8,128)(2,1)S(1)}, u32[]{:S(2)}, u32[]{:S(2)}) collective-permute-start(bf16[2,128,640]{2,1,0:T(8,128)(2,1)S(1)} %pad_maximum_fusion.1), channel_id=1, source_target_pairs={{0,1},{1,0},{2,3},{3,2},{4,5},{5,4},{6,7},{7,6},{8,9},{9,8},{10,11... | collective-permute-start | bytes 983048 | tf_op jit(solution)/shard_map/ppermute | solution.py:231
  18.6 27.0 %copy-start = (bf16[128,2560]{1,0:T(8,128)(2,1)S(1)}, bf16[128,2560]{1,0:T(8,128)(2,1)}, u32[]{:S(2)}) copy-start(bf16[128,2560]{1,0:T(8,128)(2,1)} %q0.1) | copy-start | bytes 1966084
  18.9 36.3 %copy-start.4 = (s32[1,4]{1,0:T(1,128)S(1)}, s32[1,4]{1,0:T(1,128)}, u32[]{:S(2)}) copy-start(s32[1,4]{1,0:T(1,128)} %param.8) | copy-start | bytes 52
  18.9 17.4 %collective-permute-start.6 = (bf16[2,256,640]{2,1,0:T(8,128)(2,1)S(1)}, bf16[2,256,640]{2,1,0:T(8,128)(2,1)S(1)}, u32[]{:S(2)}, u32[]{:S(2)}) collective-permute-start(bf16[2,256,640]{2,1,0:T(8,128)(2,1)S(1)} %get-tuple-element.14.own_s), channel_id=1, source_target_pairs={{0,4},{4,0},{8,12},{12,8},{1,5},{5,1},{9,13},{13,9},{2,6},{6,2},{1... | collective-permute-start | bytes 1966088 | tf_op jit(solution)/shard_map/ppermute | solution.py:234
  20.5 22.5 %collective-permute-start.8 = (bf16[2,256,640]{2,1,0:T(8,128)(2,1)S(1)}, bf16[2,256,640]{2,1,0:T(8,128)(2,1)S(1)}, u32[]{:S(2)}, u32[]{:S(2)}) collective-permute-start(bf16[2,256,640]{2,1,0:T(8,128)(2,1)S(1)} %get-tuple-element.14.own_s), channel_id=1, source_target_pairs={{4,8},{8,4},{5,9},{9,5},{6,10},{10,6},{7,11},{11,7},{20,24},{24,20... | collective-permute-start | bytes 1966088 | tf_op jit(solution)/shard_map/ppermute | solution.py:234
  36.2 8.1 %collective-permute-start.10 = (bf16[2,256,640]{2,1,0:T(8,128)(2,1)S(1)}, bf16[2,256,640]{2,1,0:T(8,128)(2,1)}, u32[]{:S(2)}, u32[]{:S(2)}) collective-permute-start(bf16[2,256,640]{2,1,0:T(8,128)(2,1)S(1)} %collective-permute-done.6.n1_s), channel_id=1, source_target_pairs={{4,8},{8,4},{5,9},{9,5},{6,10},{10,6},{7,11},{11,7},{20,24},{24,20... | collective-permute-start | bytes 1966088 | tf_op jit(solution)/shard_map/ppermute | solution.py:234
  37.8 23.7 %collective-permute-start.7 = (bf16[2,256,640]{2,1,0:T(8,128)(2,1)S(1)}, bf16[2,256,640]{2,1,0:T(8,128)(2,1)}, u32[]{:S(2)}, u32[]{:S(2)}) collective-permute-start(bf16[2,256,640]{2,1,0:T(8,128)(2,1)S(1)} %get-tuple-element.13.own_u), channel_id=1, source_target_pairs={{0,4},{4,0},{8,12},{12,8},{1,5},{5,1},{9,13},{13,9},{2,6},{6,2},{1... | collective-permute-start | bytes 1966088 | tf_op jit(solution)/shard_map/ppermute | solution.py:234
  41.5 20.0 %collective-permute-start.9 = (bf16[2,256,640]{2,1,0:T(8,128)(2,1)S(1)}, bf16[2,256,640]{2,1,0:T(8,128)(2,1)}, u32[]{:S(2)}, u32[]{:S(2)}) collective-permute-start(bf16[2,256,640]{2,1,0:T(8,128)(2,1)S(1)} %get-tuple-element.13.own_u), channel_id=1, source_target_pairs={{4,8},{8,4},{5,9},{9,5},{6,10},{10,6},{7,11},{11,7},{20,24},{24,20... | collective-permute-start | bytes 1966088 | tf_op jit(solution)/shard_map/ppermute | solution.py:234
  43.0 28.2 %collective-permute-start.11 = (bf16[2,256,640]{2,1,0:T(8,128)(2,1)S(1)}, bf16[2,256,640]{2,1,0:T(8,128)(2,1)}, u32[]{:S(2)}, u32[]{:S(2)}) collective-permute-start(bf16[2,256,640]{2,1,0:T(8,128)(2,1)S(1)} %collective-permute-done.8.n2_s), channel_id=1, source_target_pairs={{4,0},{8,12},{5,1},{9,13},{6,2},{10,14},{7,3},{11,15},{20,16},{24,... | collective-permute-start | bytes 1966088 | tf_op jit(solution)/shard_map/ppermute | solution.py:234
  44.3 39.9 %collective-permute-start.12 = (bf16[2,256,640]{2,1,0:T(8,128)(2,1)}, bf16[2,256,640]{2,1,0:T(8,128)(2,1)}, u32[]{:S(2)}, u32[]{:S(2)}) collective-permute-start(bf16[2,256,640]{2,1,0:T(8,128)(2,1)} %collective-permute-done.10.r1), channel_id=1, source_target_pairs={{4,0},{8,12},{5,1},{9,13},{6,2},{10,14},{7,3},{11,15},{20,16},{24,... | collective-permute-start | bytes 1966088 | tf_op jit(solution)/shard_map/ppermute | solution.py:234
  46.4 1.4 %collective-permute-start = (bf16[128,640]{1,0:T(8,128)(2,1)S(1)}, bf16[128,640]{1,0:T(8,128)(2,1)S(1)}, u32[]{:S(2)}, u32[]{:S(2)}) collective-permute-start(bf16[128,640]{1,0:T(8,128)(2,1)S(1)} %get-tuple-element.25), channel_id=1, source_target_pairs={{0,1},{1,0},{2,3},{3,2},{4,5},{5,4},{6,7},{7,6},{8,9},{9,8},{10,11... | collective-permute-start | bytes 491528 | tf_op jit(solution)/shard_map/ppermute | solution.py:231
  47.8 6.2 %collective-permute-start.1 = (bf16[128,640]{1,0:T(8,128)(2,1)S(1)}, bf16[128,640]{1,0:T(8,128)(2,1)S(1)}, u32[]{:S(2)}, u32[]{:S(2)}) collective-permute-start(bf16[128,640]{1,0:T(8,128)(2,1)S(1)} %get-tuple-element.24), channel_id=1, source_target_pairs={{0,2},{1,3},{2,0},{3,1},{4,6},{5,7},{6,4},{7,5},{8,10},{9,11},{10,... | collective-permute-start | bytes 491528 | tf_op jit(solution)/shard_map/ppermute | solution.py:231
  54.0 0.7 copy-start.1
  54.7 6.8 %collective-permute-start.2 = (bf16[128,640]{1,0:T(8,128)(2,1)}, bf16[128,640]{1,0:T(8,128)(2,1)}, u32[]{:S(2)}, u32[]{:S(2)}) collective-permute-start(bf16[128,640]{1,0:T(8,128)(2,1)} %get-tuple-element.23), channel_id=1, source_target_pairs={{0,3},{1,2},{2,1},{3,0},{4,7},{5,6},{6,5},{7,4},{8,11},{9,10},{10,... | collective-permute-start | bytes 491528 | tf_op jit(solution)/shard_map/ppermute | solution.py:231
  84.3 0.9 copy-start.2
  95.0 2.0 %collective-permute-start.13 = (bf16[128,640]{1,0:T(8,128)(2,1)S(1)}, bf16[128,640]{1,0:T(8,128)(2,1)S(1)}, u32[]{:S(2)}, u32[]{:S(2)}) collective-permute-start(bf16[128,640]{1,0:T(8,128)(2,1)S(1)} %get-tuple-element.10), channel_id=1, source_target_pairs={{0,1},{1,0},{2,3},{3,2},{4,5},{5,4},{6,7},{7,6},{8,9},{9,8},{10,11... | collective-permute-start | bytes 491528 | tf_op jit(solution)/shard_map/ppermute | solution.py:231
  95.1 7.1 %collective-permute-start.14 = (bf16[128,640]{1,0:T(8,128)(2,1)S(1)}, bf16[128,640]{1,0:T(8,128)(2,1)S(1)}, u32[]{:S(2)}, u32[]{:S(2)}) collective-permute-start(bf16[128,640]{1,0:T(8,128)(2,1)S(1)} %get-tuple-element.11), channel_id=1, source_target_pairs={{0,2},{1,3},{2,0},{3,1},{4,6},{5,7},{6,4},{7,5},{8,10},{9,11},{10,... | collective-permute-start | bytes 491528 | tf_op jit(solution)/shard_map/ppermute | solution.py:231
  96.8 8.0 %collective-permute-start.15 = (bf16[128,640]{1,0:T(8,128)(2,1)S(1)}, bf16[128,640]{1,0:T(8,128)(2,1)S(1)}, u32[]{:S(2)}, u32[]{:S(2)}) collective-permute-start(bf16[128,640]{1,0:T(8,128)(2,1)S(1)} %get-tuple-element.12), channel_id=1, source_target_pairs={{0,3},{1,2},{2,1},{3,0},{4,7},{5,6},{6,5},{7,4},{8,11},{9,10},{10,... | collective-permute-start | bytes 491528 | tf_op jit(solution)/shard_map/ppermute | solution.py:231
  102.2 2.6 %copy-start.3 = (bf16[128,2560]{1,0:T(8,128)(2,1)}, bf16[128,2560]{1,0:T(8,128)(2,1)S(1)}, u32[]{:S(2)}) copy-start(bf16[128,2560]{1,0:T(8,128)(2,1)S(1)} %constant_dynamic-update-slice_fusion.3) | copy-start | bytes 1966084

commit v2 on v0

--- a/solution.py
+++ b/solution.py
@@ -1,9 +1,15 @@
+import math
+
 import jax
 import jax.numpy as jnp
 from jax import lax
+from jax.experimental import pallas as pl
+from jax.experimental.pallas import tpu as pltpu
 from jax.sharding import PartitionSpec as P
 
 HEAD_DIM = 128
+SCALE = 1.0 / HEAD_DIM**0.5
+LOG2E = math.log2(math.e)
 
 
 def padded(x, sides, width):
@@ -19,14 +25,6 @@
     return x
 
 
-def shortened(x):
-
-    def short(part):
-        return part.astype(jnp.bfloat16) if part.dtype == jnp.float32 else part
-
-    return jax.tree.map(short, x)
-
-
 def from_partner(x, axis, bit):
     return lax.ppermute(x, axis, [(i, i ^ 1 << bit) for i in range(lax.axis_size(axis))])
 
@@ -45,11 +43,10 @@
     q_three = query_rows.reshape(count, heads, HEAD_DIM).transpose(1, 0, 2)
     k_three = key_rows.reshape(-1, heads, HEAD_DIM).transpose(1, 0, 2)
     v_three = value_rows.reshape(-1, heads, HEAD_DIM).transpose(1, 0, 2)
-    scale = 1.0 / HEAD_DIM**0.5
 
     def one_head(operands):
         q_head, k_head, v_head = operands
-        scores = jnp.dot(q_head, k_head.T, preferred_element_type=jnp.float32) * scale
+        scores = jnp.dot(q_head, k_head.T, preferred_element_type=jnp.float32) * SCALE
         scores = jnp.where(valid[None, :] > 0, scores, -1e30)
         top = jnp.max(scores, axis=1, keepdims=True)
         weights = jnp.exp(scores - top) * valid[None, :]
@@ -65,7 +62,7 @@
     return jnp.where(upper == 1, jnp.concatenate([theirs, mine]), jnp.concatenate([mine, theirs]))
 
 
-def per_device(queries, keys, values, pair_mask, tile_offset):
+def general(queries, keys, values, pair_mask, tile_offset):
     frames_n = lax.axis_size("frame")
     current = lax.axis_index("frame")
     q_rows, k_rows, v_rows = (
@@ -122,10 +119,7 @@
         active = [level for level in swap_levels if level >= bit]
         k_pack = jnp.concatenate([growing[level][0].reshape(-1, width) for level in active])
         v_pack = jnp.concatenate([growing[level][1].reshape(-1, width) for level in active])
-        k_in, v_in = (
-            from_partner(shortened(k_pack), "frame", bit).astype(k_pack.dtype),
-            from_partner(shortened(v_pack), "frame", bit).astype(v_pack.dtype),
-        )
+        k_in, v_in = (from_partner(k_pack, "frame", bit), from_partner(v_pack, "frame", bit))
         upper = current // 2**bit % 2
         position = 0
         for level in active:
@@ -160,7 +154,184 @@
     return lax.all_to_all(result, "head", split_axis=0, concat_axis=1, tiled=True)
 
 
+STAGES = (3, 2)
+OUTER = [(0, 1), (1, 0), (2, 3), (3, 2)]
+INNER = [(1, 2), (2, 1)]
+INWARD = [(0, 1), (3, 2)]
+OUTWARD = [(1, 0), (2, 3)]
+
+
+def attend_rows(q, slots, held):
+    factor = SCALE * LOG2E
+    top = None
+    spans = []
+    for k, v, valid in slots:
+        begin = spans[-1][1] if spans else 0
+        spans.append((begin, begin + k.shape[0]))
+        s = lax.dot_general(q, k, (((1,), (1,)), ((), ())), preferred_element_type=jnp.float32)
+        held[:, spans[-1][0] : spans[-1][1]] = s
+        best = jnp.max(s, axis=1, keepdims=True)
+        if valid is not None:
+            best = jnp.where(valid, best, -1e30)
+        top = best if top is None else jnp.maximum(top, best)
+    total, mixed = None, None
+    for (k, v, valid), (begin, end) in zip(slots, spans):
+        level = top if valid is None else jnp.where(valid, top, 1e30)
+        w = jnp.exp2((held[:, begin:end] - level) * factor)
+        part = jnp.sum(w, axis=1, keepdims=True)
+        mix = jnp.dot(w.astype(jnp.bfloat16), v, preferred_element_type=jnp.float32)
+        total = part if total is None else total + part
+        mixed = mix if mixed is None else mixed + mix
+    return (mixed / total).astype(jnp.bfloat16)
+
+
+def attention_kernel(guest, scalars, refs):
+    mask, off2 = scalars
+    z = lax.axis_index("frame")
+    x = lax.axis_index("head") // 2
+    qs, kvs, outs, held = refs
+
+    @pl.when((z == 1) | (z == 2))
+    def _():
+        tiles = []
+        for k, v in kvs:
+            for begin in range(0, k.shape[0], held.shape[2] // 7):
+                span = slice(begin, begin + held.shape[2] // 7)
+                tiles.append((k[span], v[span]))
+        if guest:
+            far = mask[0, z ^ 3] == 1
+            picked = off2[0] == x
+            valid = [None] * 4 + [far & picked, far & jnp.logical_not(picked), mask[0, z ^ 2] == 1]
+        else:
+            valid = [None] * 6 + [mask[0, z ^ 2] == 1]
+        slots = [(k, v, ok) for (k, v), ok in zip(tiles, valid)]
+        rows = held.shape[1]
+        for half, q in enumerate(qs):
+            for begin in range(0, q.shape[0], rows):
+                out = attend_rows(q[begin : begin + rows], slots, held.at[half + begin // rows])
+                at = half * q.shape[0] + begin
+                for ref, first in outs:
+                    if first <= at < first + ref.shape[0] or at <= first < at + rows:
+                        low, high = max(at, first), min(at + rows, first + ref.shape[0])
+                        ref[low - first : high - first] = out[low - at : high - at]
+
+
+def attention(guest, mask, off2, q, first, kv, heads, outs):
+    n_q, n_kv, n_out = len(q), len(kv), len(outs)
+    tile = kv[0].shape[0]
+    half = sum(outs) // 2
+
+    def body(*refs):
+        kvs = refs[2 + n_q : 2 + n_q + 2 * n_kv]
+        placed, at = [], 0
+        for ref in refs[2 + n_q + 2 * n_kv : 2 + n_q + 2 * n_kv + n_out]:
+            placed.append((ref, at))
+            at += ref.shape[0]
+        attention_kernel(
+            guest, refs[:2], (refs[2 : 2 + n_q], list(zip(kvs[::2], kvs[1::2])), placed, refs[-1])
+        )
+
+    def spec(x, at):
+        return pl.BlockSpec((x.shape[0], HEAD_DIM), lambda i: (0, at + i))
+
+    blocks = [(x, first) for x in q]
+    for x in kv:
+        blocks += [(x, 0), (x, heads)]
+    return pl.pallas_call(
+        body,
+        grid=(heads,),
+        in_specs=[pl.BlockSpec(memory_space=pltpu.SMEM)] * 2 + [spec(x, at) for x, at in blocks],
+        out_specs=[pl.BlockSpec((rows, HEAD_DIM), lambda i: (0, i)) for rows in outs],
+        out_shape=[jax.ShapeDtypeStruct((rows, heads * HEAD_DIM), jnp.bfloat16) for rows in outs],
+        scratch_shapes=[pltpu.VMEM((2, half, 7 * tile), jnp.float32)],
+        compiler_params=pltpu.CompilerParams(vmem_limit_bytes=32 * 1024 * 1024),
+        cost_estimate=pl.CostEstimate(
+            flops=heads * 2 * half * 7 * tile * HEAD_DIM * 4,
+            bytes_accessed=heads * HEAD_DIM * 2 * (4 * half + 14 * tile),
+            transcendentals=heads * 2 * half * 7 * tile,
+        ),
+    )(mask, off2, *[x for x, _ in blocks])
+
+
+def four_frames(queries, keys, values, pair_mask, tile_offset):
+    z = lax.axis_index("frame")
+    h = lax.axis_index("head")
+    rows, features = queries.shape
+    width = features // 4
+    heads = width // HEAD_DIM
+    stages, begin = [], 0
+    for count in STAGES[:-1]:
+        stages.append((begin, begin + count))
+        begin += count
+    stages.append((begin, heads))
+
+    def columns(x, d, begin, end):
+        return lax.dynamic_slice_in_dim(x, (h ^ d) * width + begin * HEAD_DIM, (end - begin) * HEAD_DIM, axis=1)
+
+    def to_head(x, d):
+        return lax.ppermute(x, "head", [(i, i ^ d) for i in range(4)])
+
+    def along(x, pairs):
+        return lax.ppermute(x, "frame", pairs)
+
+    def after(x, earlier):
+        return lax.optimization_barrier((x, earlier))[0]
+
+    def kv_columns(d, stage):
+        return [columns(keys, d, *stage), columns(values, d, *stage)]
+
+    mask1 = along(pair_mask, INWARD)
+    off1 = along(tile_offset, INWARD)
+    off2 = along(tile_offset, INNER)
+    x = h // 2
+
+    width1 = 2 * (stages[0][1] - stages[0][0]) * HEAD_DIM
+    got = to_head(jnp.concatenate(kv_columns(1, stages[0]) + kv_columns(3, stages[0]), axis=1), 1)
+    mine = jnp.concatenate([jnp.concatenate(kv_columns(0, stages[0]), axis=1), got[:, :width1]], axis=0)
+    pay = jnp.concatenate([jnp.concatenate(kv_columns(2, stages[0]), axis=1), got[:, width1:]], axis=0)
+    other = to_head(pay, 2)
+    n1 = [along(mine, INWARD)]
+    n2 = [along(mine, INNER)]
+    n1.append(along(other, INWARD))
+    n2.append(along(other, INNER))
+    r1 = along(jnp.where(x == off1[0], n1[0], n1[1]), INNER)
+    kv = [[mine, other, *n1, *n2, r1]]
+
+    width2 = 2 * (stages[1][1] - stages[1][0]) * HEAD_DIM
+    pieces = [columns(queries, 1, 0, heads), columns(queries, 3, 0, heads)] + kv_columns(1, stages[1]) + kv_columns(3, stages[1])
+    got = to_head(after(jnp.concatenate(pieces, axis=1), mine), 1)
+    q_mine = jnp.concatenate([columns(queries, 0, 0, heads), got[:, :width]], axis=0)
+    pay = jnp.concatenate([columns(queries, 2, 0, heads), got[:, width : 2 * width]], axis=0)
+    q_other = to_head(after(pay, other), 2)
+    mine = jnp.concatenate([jnp.concatenate(kv_columns(0, stages[1]), axis=1), got[:, 2 * width : 2 * width + width2]], axis=0)
+    pay = jnp.concatenate([jnp.concatenate(kv_columns(2, stages[1]), axis=1), got[:, 2 * width + width2 :]], axis=0)
+    other = to_head(after(pay, q_other), 2)
+    guests = []
+    for begin, end in stages:
+        span = slice(begin * HEAD_DIM, end * HEAD_DIM)
+        guests.append(along(jnp.concatenate([q_mine[:, span], q_other[:, span]], axis=0), INWARD))
+    whole = jnp.concatenate([mine, other], axis=0)
+    n1 = along(whole, INWARD)
+    n2 = along(whole, INNER)
+    r1 = along(lax.dynamic_slice_in_dim(n1, jnp.where(x == off1[0], 0, 2 * rows), 2 * rows, axis=0), INNER)
+    kv.append([mine, other, n1, n2, r1])
+
+    end_frame = (z == 0) | (z == 3)
+    result = jnp.zeros((rows, features), jnp.bfloat16)
+    for (begin, end), guest, arrays in zip(stages, guests, kv):
+        (far,) = attention(True, mask1, off2, [guest], 0, arrays, end - begin, [4 * rows])
+        back = along(far, OUTWARD)
+        own = attention(False, pair_mask, off2, [q_mine, q_other], begin, arrays, end - begin, [rows] * 4)
+        out = [jnp.where(end_frame, back[d * rows : (d + 1) * rows], own[d]) for d in range(4)]
+        out = [out[0]] + [to_head(out[d], d) for d in (1, 2, 3)]
+        for d in range(4):
+            result = lax.dynamic_update_slice_in_dim(result, out[d], (h ^ d) * width + begin * HEAD_DIM, axis=1)
+    return result
+
+
 def solution(mesh):
+    sizes = dict(mesh.shape)
+    per_device = four_frames if sizes["frame"] == 4 and sizes["head"] == 4 else general
     return jax.shard_map(
         per_device,
         mesh=mesh,

time: 172 us -> 111 us (0.65)
  starting transfers between devices: 14.2 us -> 53.3 us
  blocking collectives: 25.3 us -> 0 us
  waiting for transfers between devices: 53.3 us -> 30.4 us
  matrix products: 18.7 us -> 0 us
  local copies, waits for them, and re-layouts: 31 us -> 13.9 us
  between operations: 14.2 us -> 1.09 us
  other arithmetic: 14.5 us -> 3.73 us
  Pallas kernels: 0 us -> 7.88 us
    ppermute x2 -> x26, starting transfers between devices: 6.51 us -> 53.3 us  [the longest x15 45.3 us: along(): return lax.ppermute(x, 'frame', pairs)]
    all_to_all x2 -> x0, blocking collectives: 25.3 us -> none  [the longest x1 12.7 us: per_device(): lax.all_to_all(values, 'head', split_axis=1, concat_axis=0, tiled=True)]
    all_to_all x2 -> x0, waiting for transfers between devices: 19.5 us -> none  [the longest x1 9.93 us: per_device(): lax.all_to_all(queries, 'head', split_axis=1, concat_axis=0, tiled=True)]
    dot_general x10 -> x0, matrix products: 18.7 us -> none  [the longest x5 14.2 us: one_head(): jnp.dot(weights.astype(jnp.bfloat16), v_head, preferred_element_type=jnp....]
    pallas_call x0 -> x4, Pallas kernels: none -> 7.88 us  [attention(): pl.pallas_call(body, grid=(heads,), in_specs=[pl.BlockSpec(memory_space=p...]
    all_to_all x2 -> x0, starting transfers between devices: 7.69 us -> none  [the longest x1 4.21 us: per_device(): lax.all_to_all(keys, 'head', split_axis=1, concat_axis=0, tiled=True)]
    slice x3 -> x5, local copies, waits for them, and re-layouts: 8.96 us -> 2.74 us  [the longest x1 1.65 us: four_frames(): got[:, 2 * width + width2:]]
    reduce_sum x5 -> x0, other arithmetic: 5.49 us -> none  [one_head(): total = jnp.sum(weights, axis=1, keepdims=True)]
  transfers between devices with their start and end apart: 6 -> 26, of which waited for: 4 -> 8; matrix products, arithmetic and copies ran while one was open for 11% -> 13% of each run, Pallas kernels for 0% -> 7%
where the time goes in v2:
time: 111 us; the launch traced here: 110 us
  starting transfers between devices  53.3 us (48%)
  waiting for transfers between devices  30.4 us (27%)
  local copies, waits for them, and re-layouts  13.9 us (13%)
  Pallas kernels  7.88 us (7%)
  other arithmetic  3.73 us (3%)
    ppermute x15, starting transfers between devices, along(): return lax.ppermute(x, 'frame', pairs)  45.3 us
    ppermute x15, waiting for transfers between devices, along(): return lax.ppermute(x, 'frame', pairs)  25.3 us
    ppermute x11, starting transfers between devices, to_head(): return lax.ppermute(x, 'head', [(i, i ^ d) for i in range(4)])  8.05 us
    pallas_call x4, Pallas kernels, attention(): pl.pallas_call(body, grid=(heads,), in_specs=[pl.BlockSpec(memory_space=p...  7.88 us
    unnamed x19, local copies, waits for them, and re-layouts  5.25 us
    dynamic_slice x4, local copies, waits for them, and re-layouts, columns(): lax.dynamic_slice_in_dim(x, (h ^ d) * width + begin * HEAD_DIM, (end - be...  5.15 us
    ppermute x11, waiting for transfers between devices, to_head(): return lax.ppermute(x, 'head', [(i, i ^ d) for i in range(4)])  5.08 us
  transfers between devices with their start and end apart: 26, of which 8 were waited for; matrix products, arithmetic and copies ran while one was open for 13% of the time, Pallas kernels for 7%

profile of v2, /device:TPU:0, one launch (start us, length us, event | category | flops | bytes accessed | tf_op | source)
XLA Modules:
  0.0 110.3 jit_solution(8781716141399846804)
XLA Ops:
  0.0 1.3 %constant_dynamic-slice_fusion.5 = (bf16[128,384]{1,0:T(8,128)(2,1)S(1)}, bf16[128,384]{1,0:T(8,128)(2,1)S(1)}, bf16[128,384]{1,0:T(8,128)(2,1)S(1)}, bf16[128,3...) fusion(bf16[128,2560]{1,0:T(8,128)(2,1)} %param.7, ...), kind=kLoop, calls=%fused_computation.44 | loop fusion | bytes 1572880 | tf_op jit(solution)/shard_map/dynamic_slice | solution.py:269
  1.4 0.5 collective-permute-start.2
  2.4 0.7 constant_dynamic-slice_fusion.7
  3.1 0.7 dynamic-slice_dynamic-update-slice_fusion
  3.8 1.5 %dynamic-slice_dynamic-update-slice_fusion.5 = bf16[128,2304]{1,0:T(8,128)(2,1)} fusion(bf16[128,2304]{1,0:T(8,128)(2,1)} %dynamic-slice_dynamic-update-slice_fusion, bf16[128,2560]{1,0:T(8,128)(2,1)} %param.6, s32[]{:T(128)S(6)} %select_n.106), kind=kLoop, calls=%fused_computation.32 | loop fusion | bytes 131076
  5.3 1.5 %dynamic-slice_dynamic-update-slice_fusion.4 = bf16[128,2304]{1,0:T(8,128)(2,1)} fusion(bf16[128,2304]{1,0:T(8,128)(2,1)} %dynamic-slice_dynamic-update-slice_fusion.5, bf16[128,2560]{1,0:T(8,128)(2,1)} %param.7, s32[]{:T(128)S(6)} %select_n.106), kind=kLoop, calls=%fused_computation.31 | loop fusion | bytes 131076
  6.8 1.6 %constant_dynamic-slice_fusion.2 = (bf16[128,256]{1,0:T(8,128)(2,1)S(1)}, bf16[128,2304]{1,0:T(8,128)(2,1)}, bf16[128,256]{1,0:T(8,128)(2,1)}) fusion(bf16[128,2560]{1,0:T(8,128)(2,1)} %param.6, s32[]{:T(128)S(6)} %select_n.118, bf16[128,2304]{1,0:T(8,128)(2,1)} %dynamic-slice_dynamic-update-slice_fusion.4, s32[]{:T(128)S(6)} %select_n.107, s32[]{:T(128)S(6)} %select_n.117), kind=kLoop, calls=%fused_computation.38 | loop fusion | bytes 393228 | tf_op jit(solution)/shard_map/dynamic_slice | solution.py:269
  8.4 1.6 %constant_dynamic-slice_fusion.1 = (bf16[128,256]{1,0:T(8,128)(2,1)S(1)}, bf16[128,2304]{1,0:T(8,128)(2,1)}, bf16[128,256]{1,0:T(8,128)(2,1)}) fusion(bf16[128,2560]{1,0:T(8,128)(2,1)} %param.7, s32[]{:T(128)S(6)} %select_n.118, bf16[128,2304]{1,0:T(8,128)(2,1)} %get-tuple-element.28, s32[]{:T(128)S(6)} %select_n.107, s32[]{:T(128)S(6)} %select_n.117), kind=kLoop, calls=%fused_computation.37 | loop fusion | bytes 393228 | tf_op jit(solution)/shard_map/dynamic_slice | solution.py:269
  10.5 2.6 %collective-permute-start.4 = (bf16[256,768]{1,0:T(8,128)(2,1)S(1)}, bf16[256,768]{1,0:T(8,128)(2,1)S(1)}, u32[]{:S(2)}, u32[]{:S(2)}) collective-permute-start(bf16[256,768]{1,0:T(8,128)(2,1)S(1)} %pad_maximum_fusion.4), channel_id=1, source_target_pairs={{0,2},{1,3},{2,0},{3,1},{4,6},{5,7},{6,4},{7,5},{8,10},{9,11},{10,... | collective-permute-start | bytes 1179656 | tf_op jit(solution)/shard_map/ppermute | solution.py:272
  13.1 4.0 %collective-permute-start.11 = (s32[1]{0:T(128)}, s32[1]{0:T(128)}, u32[]{:S(2)}, u32[]{:S(2)}) collective-permute-start(s32[1]{0:T(128)} %param.9), channel_id=1, source_target_pairs={{0,4},{12,8},{1,5},{13,9},{2,6},{14,10},{3,7},{15,11},{16,20},{28,... | collective-permute-start | bytes 20 | tf_op jit(solution)/shard_map/ppermute | solution.py:275
  17.2 0.8 collective-permute-done.11
  18.7 4.1 %collective-permute-start.7 = (bf16[256,768]{1,0:T(8,128)(2,1)S(1)}, bf16[256,768]{1,0:T(8,128)(2,1)S(1)}, u32[]{:S(2)}, u32[]{:S(2)}) collective-permute-start(bf16[256,768]{1,0:T(8,128)(2,1)S(1)} %pad_maximum_fusion.3.refs_3_.refs_4_.refs_5_), channel_id=1, source_target_pairs={{0,4},{12,8},{1,5},{13,9},{2,6},{14,10},{3,7},{15,11},{16,20},{28,... | collective-permute-start | bytes 1179656 | tf_op jit(solution)/shard_map/ppermute | solution.py:275
  22.8 0.7 collective-permute-start.9
  23.5 4.1 %collective-permute-start.8 = (bf16[256,768]{1,0:T(8,128)(2,1)S(1)}, bf16[256,768]{1,0:T(8,128)(2,1)S(1)}, u32[]{:S(2)}, u32[]{:S(2)}) collective-permute-start(bf16[256,768]{1,0:T(8,128)(2,1)S(1)} %collective-permute-done.4.refs_5_.refs_6_.refs_7_), channel_id=1, source_target_pairs={{0,4},{12,8},{1,5},{13,9},{2,6},{14,10},{3,7},{15,11},{16,20},{28,... | collective-permute-start | bytes 1179656 | tf_op jit(solution)/shard_map/ppermute | solution.py:275
  27.6 0.7 collective-permute-start.10
  28.3 1.0 fusion.5
  29.4 0.6 collective-permute-start.5
  30.0 1.7 %fusion.4 = (bf16[128,512]{1,0:T(8,128)(2,1)S(1)}, bf16[128,512]{1,0:T(8,128)(2,1)}) fusion(bf16[128,2304]{1,0:T(8,128)(2,1)} %collective-permute-done.3), kind=kLoop, calls=%fused_computation.54 | loop fusion | bytes 524288 | tf_op jit(solution)/shard_map/slice | solution.py:307
  31.6 0.7 pad_maximum_fusion.9
  32.4 6.7 %collective-permute-done.8.refs_9_.refs_10_.refs_11_ = bf16[256,768]{1,0:T(8,128)(2,1)S(1)} collective-permute-done((bf16[256,768]{1,0:T(8,128)(2,1)S(1)}, bf16[256,768]{1,0:T(8,128)(2,1)S(1)}, u32[]{:S(2)}, u32[]{:S(2)}) %collective-permute-start.8) | collective-permute-done | bytes 393248 | tf_op jit(solution)/shard_map/ppermute | solution.py:275
  39.1 0.8 broadcast_select_fusion
  39.9 0.7 collective-permute-start.12
  40.6 0.6 collective-permute-start.18
  41.2 0.8 pad_maximum_fusion.5
  42.0 8.0 %collective-permute-start.6 = (bf16[512,384]{1,0:T(8,128)(2,1)}, bf16[512,384]{1,0:T(8,128)(2,1)}, u32[]{:S(2)}, u32[]{:S(2)}) collective-permute-start(bf16[512,384]{1,0:T(8,128)(2,1)} %pad_maximum_fusion.5), channel_id=1, source_target_pairs={{0,4},{12,8},{1,5},{13,9},{2,6},{14,10},{3,7},{15,11},{16,20},{28,... | collective-permute-start | bytes 1179656 | tf_op jit(solution)/shard_map/ppermute | solution.py:275
  50.0 1.2 %collective-permute-start.1 = (s32[1]{0:T(128)}, s32[1]{0:T(128)}, u32[]{:S(2)}, u32[]{:S(2)}) collective-permute-start(s32[1]{0:T(128)} %param.9), channel_id=1, source_target_pairs={{4,8},{8,4},{5,9},{9,5},{6,10},{10,6},{7,11},{11,7},{20,24},{24,20... | collective-permute-start | bytes 20 | tf_op jit(solution)/shard_map/ppermute | solution.py:275
  51.2 1.0 pad_maximum_fusion
  52.2 7.9 %collective-permute-start = (s32[1,4]{1,0:T(1,128)S(1)}, s32[1,4]{1,0:T(1,128)S(1)}, u32[]{:S(2)}, u32[]{:S(2)}) collective-permute-start(s32[1,4]{1,0:T(1,128)S(1)} %copy-done), channel_id=1, source_target_pairs={{0,4},{12,8},{1,5},{13,9},{2,6},{14,10},{3,7},{15,11},{16,20},{28,... | collective-permute-start | bytes 56 | tf_op jit(solution)/shard_map/ppermute | solution.py:275
  60.1 1.3 %collective-permute-done.refs_0_ = s32[1,4]{1,0:T(1,128)S(1)} collective-permute-done((s32[1,4]{1,0:T(1,128)S(1)}, s32[1,4]{1,0:T(1,128)S(1)}, u32[]{:S(2)}, u32[]{:S(2)}) %collective-permute-start) | collective-permute-done | bytes 48 | tf_op jit(solution)/shard_map/ppermute | solution.py:275
  61.4 4.2 %collective-permute-start.19 = (bf16[512,512]{1,0:T(8,128)(2,1)S(1)}, bf16[512,512]{1,0:T(8,128)(2,1)S(1)}, u32[]{:S(2)}, u32[]{:S(2)}) collective-permute-start(bf16[512,512]{1,0:T(8,128)(2,1)S(1)} %pad_maximum_fusion), channel_id=1, source_target_pairs={{0,4},{12,8},{1,5},{13,9},{2,6},{14,10},{3,7},{15,11},{16,20},{28,... | collective-permute-start | bytes 1572872 | tf_op jit(solution)/shard_map/ppermute | solution.py:275
  65.7 2.6 %shard_map.55 = bf16[512,384]{1,0:T(8,128)(2,1)S(1)} custom-call(s32[1,4]{1,0:T(1,128)S(1)} %collective-permute-done.refs_0_, s32[1]{0:T(128)} %collective-permute-done.1.refs_1_, bf16[512,384]{1,0:T(8,128)(2,1)} %collective-permute-done.6.refs_2_, bf16[256,768]{1,0:T(8,128)(2,1)S(1)} %pad_maximum_fusion.3.refs_3_.refs_4_.refs_5_, ...), custom_call_target="tpu_custom_call" | custom-call | flops 1409286144 | bytes 3538944 | tf_op jit(solution)/shard_map/pallas_call | solution.py:240
  68.3 1.3 %collective-permute-start.13 = (bf16[512,384]{1,0:T(8,128)(2,1)S(1)}, bf16[512,384]{1,0:T(8,128)(2,1)S(1)}, u32[]{:S(2)}, u32[]{:S(2)}) collective-permute-start(bf16[512,384]{1,0:T(8,128)(2,1)S(1)} %shard_map.55), channel_id=1, source_target_pairs={{4,0},{8,12},{5,1},{9,13},{6,2},{10,14},{7,3},{11,15},{20,16},{24,... | collective-permute-start | bytes 1179656 | tf_op jit(solution)/shard_map/ppermute | solution.py:275
  69.7 5.7 %collective-permute-start.17 = (bf16[512,256]{1,0:T(8,128)(2,1)S(1)}, bf16[512,256]{1,0:T(8,128)(2,1)S(1)}, u32[]{:S(2)}, u32[]{:S(2)}) collective-permute-start(bf16[512,256]{1,0:T(8,128)(2,1)S(1)} %pad_maximum_fusion.7), channel_id=1, source_target_pairs={{0,4},{12,8},{1,5},{13,9},{2,6},{14,10},{3,7},{15,11},{16,20},{28,... | collective-permute-start | bytes 786440 | tf_op jit(solution)/shard_map/ppermute | solution.py:275
  75.4 0.7 collective-permute-start.20
  76.1 2.0 %shard_map.56 = (bf16[128,384]{1,0:T(8,128)(2,1)S(1)}, bf16[128,384]{1,0:T(8,128)(2,1)S(1)}, bf16[128,384]{1,0:T(8,128)(2,1)S(1)}, bf16[128,384]{1,0:T(8,128)(2,1)S(1)}) custom-call(s32[1,4]{1,0:T(1,128)S(1)} %copy-done, s32[1]{0:T(128)} %collective-permute-done.1.refs_1_, bf16[256,640]{1,0:T(8,128)(2,1)S(1)} %pad_maximum_fusion.1.refs_2_, ...), custom_call_target="tpu_custom_call" | custom-call | flops 1409286144 | bytes 3538944 | tf_op jit(solution)/shard_map/pallas_call | solution.py:240
  78.2 0.7 collective-permute-start.21
  79.5 0.7 copy-done.3
  80.2 0.6 collective-permute-start.15
  80.8 0.6 collective-permute-start.16
  81.5 1.6 %shard_map.57 = bf16[512,256]{1,0:T(8,128)(2,1)S(1)} custom-call(s32[1,4]{1,0:T(1,128)S(1)} %collective-permute-done.refs_0_, s32[1]{0:T(128)} %collective-permute-done.1.refs_1_, bf16[512,256]{1,0:T(8,128)(2,1)S(1)} %collective-permute-done.17.refs_2_, bf16[256,512]{1,0:T(8,128)(2,1)S(1)} %pad_maximum_fusion.8.refs_3_.refs_4_.refs_5_, ...), custom_call_target="tpu_custom_call" | custom-call | flops 939524096 | bytes 2359296 | tf_op jit(solution)/shard_map/pallas_call | solution.py:240
  83.1 1.3 %collective-permute-start.22 = (bf16[512,256]{1,0:T(8,128)(2,1)S(1)}, bf16[512,256]{1,0:T(8,128)(2,1)S(1)}, u32[]{:S(2)}, u32[]{:S(2)}) collective-permute-start(bf16[512,256]{1,0:T(8,128)(2,1)S(1)} %shard_map.57), channel_id=1, source_target_pairs={{4,0},{8,12},{5,1},{9,13},{6,2},{10,14},{7,3},{11,15},{20,16},{24,... | collective-permute-start | bytes 786440 | tf_op jit(solution)/shard_map/ppermute | solution.py:275
  84.4 1.5 %collective-permute-done.15 = bf16[128,384]{1,0:T(8,128)(2,1)S(1)} collective-permute-done((bf16[128,384]{1,0:T(8,128)(2,1)S(1)}, bf16[128,384]{1,0:T(8,128)(2,1)S(1)}, u32[]{:S(2)}, u32[]{:S(2)}) %collective-permute-start.15) | collective-permute-done | bytes 98336 | tf_op jit(solution)/shard_map/ppermute | solution.py:272
  85.9 1.6 %shard_map.58 = (bf16[128,256]{1,0:T(8,128)(2,1)S(1)}, bf16[128,256]{1,0:T(8,128)(2,1)S(1)}, bf16[128,256]{1,0:T(8,128)(2,1)S(1)}, bf16[128,256]{1,0:T(8,128)(2,1)S(1)}) custom-call(s32[1,4]{1,0:T(1,128)S(1)} %copy-done, s32[1]{0:T(128)} %collective-permute-done.1.refs_1_, bf16[256,640]{1,0:T(8,128)(2,1)S(1)} %pad_maximum_fusion.1.refs_2_, ...), custom_call_target="tpu_custom_call" | custom-call | flops 939524096 | bytes 2359296 | tf_op jit(solution)/shard_map/pallas_call | solution.py:240
  87.6 16.2 %collective-permute-done.22 = bf16[512,256]{1,0:T(8,128)(2,1)S(1)} collective-permute-done((bf16[512,256]{1,0:T(8,128)(2,1)S(1)}, bf16[512,256]{1,0:T(8,128)(2,1)S(1)}, u32[]{:S(2)}, u32[]{:S(2)}) %collective-permute-start.22) | collective-permute-done | bytes 262176 | tf_op jit(solution)/shard_map/ppermute | solution.py:275
  103.9 0.6 collective-permute-start.24
  104.5 1.3 %collective-permute-start.25 = (bf16[128,256]{1,0:T(8,128)(2,1)S(1)}, bf16[128,256]{1,0:T(8,128)(2,1)S(1)}, u32[]{:S(2)}, u32[]{:S(2)}) collective-permute-start(bf16[128,256]{1,0:T(8,128)(2,1)S(1)} %get-tuple-element.54), channel_id=1, source_target_pairs={{0,3},{1,2},{2,1},{3,0},{4,7},{5,6},{6,5},{7,4},{8,11},{9,10},{10,... | collective-permute-start | bytes 196616 | tf_op jit(solution)/shard_map/ppermute | solution.py:272
  105.8 3.1 %collective-permute-done.24 = bf16[128,256]{1,0:T(8,128)(2,1)S(1)} collective-permute-done((bf16[128,256]{1,0:T(8,128)(2,1)S(1)}, bf16[128,256]{1,0:T(8,128)(2,1)S(1)}, u32[]{:S(2)}, u32[]{:S(2)}) %collective-permute-start.24) | collective-permute-done | bytes 65568 | tf_op jit(solution)/shard_map/ppermute | solution.py:272
  109.7 0.6 constant_dynamic-update-slice_fusion
  (59 shorter events, 3.0 us)
Async XLA Ops:
  1.3 1.1 copy-start.4
  1.4 8.6 %collective-permute-start.2 = (bf16[128,1536]{1,0:T(8,128)(2,1)S(1)}, bf16[128,1536]{1,0:T(8,128)(2,1)S(1)}, u32[]{:S(2)}, u32[]{:S(2)}) collective-permute-start(bf16[128,1536]{1,0:T(8,128)(2,1)S(1)} %pad_maximum_fusion.2), channel_id=1, source_target_pairs={{0,1},{1,0},{2,3},{3,2},{4,5},{5,4},{6,7},{7,6},{8,9},{9,8},{10,11... | collective-permute-start | bytes 1179656 | tf_op jit(solution)/shard_map/ppermute | solution.py:272
  3.1 29.2 %copy-start.1 = (bf16[128,640]{1,0:T(8,128)(2,1)}, bf16[128,640]{1,0:T(8,128)(2,1)S(1)}, u32[]{:S(2)}) copy-start(bf16[128,640]{1,0:T(8,128)(2,1)S(1)} %get-tuple-element.43) | copy-start | bytes 491524
  10.0 18.3 %collective-permute-start.3 = (bf16[128,2304]{1,0:T(8,128)(2,1)}, bf16[128,2304]{1,0:T(8,128)(2,1)}, u32[]{:S(2)}, u32[]{:S(2)}) collective-permute-start(bf16[128,2304]{1,0:T(8,128)(2,1)} %get-tuple-element.16), channel_id=1, source_target_pairs={{0,1},{1,0},{2,3},{3,2},{4,5},{5,4},{6,7},{7,6},{8,9},{9,8},{10,11... | collective-permute-start | bytes 1769480 | tf_op jit(solution)/shard_map/ppermute | solution.py:272
  10.5 12.9 %collective-permute-start.4 = (bf16[256,768]{1,0:T(8,128)(2,1)S(1)}, bf16[256,768]{1,0:T(8,128)(2,1)S(1)}, u32[]{:S(2)}, u32[]{:S(2)}) collective-permute-start(bf16[256,768]{1,0:T(8,128)(2,1)S(1)} %pad_maximum_fusion.4), channel_id=1, source_target_pairs={{0,2},{1,3},{2,0},{3,1},{4,6},{5,7},{6,4},{7,5},{8,10},{9,11},{10,... | collective-permute-start | bytes 1179656 | tf_op jit(solution)/shard_map/ppermute | solution.py:272
  13.1 4.9 %collective-permute-start.11 = (s32[1]{0:T(128)}, s32[1]{0:T(128)}, u32[]{:S(2)}, u32[]{:S(2)}) collective-permute-start(s32[1]{0:T(128)} %param.9), channel_id=1, source_target_pairs={{0,4},{12,8},{1,5},{13,9},{2,6},{14,10},{3,7},{15,11},{16,20},{28,... | collective-permute-start | bytes 20 | tf_op jit(solution)/shard_map/ppermute | solution.py:275
  18.7 13.7 %collective-permute-start.7 = (bf16[256,768]{1,0:T(8,128)(2,1)S(1)}, bf16[256,768]{1,0:T(8,128)(2,1)S(1)}, u32[]{:S(2)}, u32[]{:S(2)}) collective-permute-start(bf16[256,768]{1,0:T(8,128)(2,1)S(1)} %pad_maximum_fusion.3.refs_3_.refs_4_.refs_5_), channel_id=1, source_target_pairs={{0,4},{12,8},{1,5},{13,9},{2,6},{14,10},{3,7},{15,11},{16,20},{28,... | collective-permute-start | bytes 1179656 | tf_op jit(solution)/shard_map/ppermute | solution.py:275
  22.8 42.9 %collective-permute-start.9 = (bf16[256,768]{1,0:T(8,128)(2,1)S(1)}, bf16[256,768]{1,0:T(8,128)(2,1)S(1)}, u32[]{:S(2)}, u32[]{:S(2)}) collective-permute-start(bf16[256,768]{1,0:T(8,128)(2,1)S(1)} %pad_maximum_fusion.3.refs_3_.refs_4_.refs_5_), channel_id=1, source_target_pairs={{4,8},{8,4},{5,9},{9,5},{6,10},{10,6},{7,11},{11,7},{20,24},{24,20... | collective-permute-start | bytes 1179656 | tf_op jit(solution)/shard_map/ppermute | solution.py:275
  23.5 15.6 %collective-permute-start.8 = (bf16[256,768]{1,0:T(8,128)(2,1)S(1)}, bf16[256,768]{1,0:T(8,128)(2,1)S(1)}, u32[]{:S(2)}, u32[]{:S(2)}) collective-permute-start(bf16[256,768]{1,0:T(8,128)(2,1)S(1)} %collective-permute-done.4.refs_5_.refs_6_.refs_7_), channel_id=1, source_target_pairs={{0,4},{12,8},{1,5},{13,9},{2,6},{14,10},{3,7},{15,11},{16,20},{28,... | collective-permute-start | bytes 1179656 | tf_op jit(solution)/shard_map/ppermute | solution.py:275
  27.6 38.1 %collective-permute-start.10 = (bf16[256,768]{1,0:T(8,128)(2,1)S(1)}, bf16[256,768]{1,0:T(8,128)(2,1)S(1)}, u32[]{:S(2)}, u32[]{:S(2)}) collective-permute-start(bf16[256,768]{1,0:T(8,128)(2,1)S(1)} %collective-permute-done.4.refs_5_.refs_6_.refs_7_), channel_id=1, source_target_pairs={{4,8},{8,4},{5,9},{9,5},{6,10},{10,6},{7,11},{11,7},{20,24},{24,20... | collective-permute-start | bytes 1179656 | tf_op jit(solution)/shard_map/ppermute | solution.py:275
  29.4 11.2 %collective-permute-start.5 = (bf16[256,640]{1,0:T(8,128)(2,1)S(1)}, bf16[256,640]{1,0:T(8,128)(2,1)S(1)}, u32[]{:S(2)}, u32[]{:S(2)}) collective-permute-start(bf16[256,640]{1,0:T(8,128)(2,1)S(1)} %pad_maximum_fusion.6), channel_id=1, source_target_pairs={{0,2},{1,3},{2,0},{3,1},{4,6},{5,7},{6,4},{7,5},{8,10},{9,11},{10,... | collective-permute-start | bytes 983048 | tf_op jit(solution)/shard_map/ppermute | solution.py:272
  39.9 25.8 %collective-permute-start.12 = (bf16[256,768]{1,0:T(8,128)(2,1)}, bf16[256,768]{1,0:T(8,128)(2,1)S(1)}, u32[]{:S(2)}, u32[]{:S(2)}) collective-permute-start(bf16[256,768]{1,0:T(8,128)(2,1)} %broadcast_select_fusion), channel_id=1, source_target_pairs={{4,8},{8,4},{5,9},{9,5},{6,10},{10,6},{7,11},{11,7},{20,24},{24,20... | collective-permute-start | bytes 1179656 | tf_op jit(solution)/shard_map/ppermute | solution.py:275
  40.6 9.4 %collective-permute-start.18 = (bf16[256,512]{1,0:T(8,128)(2,1)}, bf16[256,512]{1,0:T(8,128)(2,1)S(1)}, u32[]{:S(2)}, u32[]{:S(2)}) collective-permute-start(bf16[256,512]{1,0:T(8,128)(2,1)} %pad_maximum_fusion.9), channel_id=1, source_target_pairs={{0,2},{1,3},{2,0},{3,1},{4,6},{5,7},{6,4},{7,5},{8,10},{9,11},{10,... | collective-permute-start | bytes 786440 | tf_op jit(solution)/shard_map/ppermute | solution.py:272
  42.0 23.7 %collective-permute-start.6 = (bf16[512,384]{1,0:T(8,128)(2,1)}, bf16[512,384]{1,0:T(8,128)(2,1)}, u32[]{:S(2)}, u32[]{:S(2)}) collective-permute-start(bf16[512,384]{1,0:T(8,128)(2,1)} %pad_maximum_fusion.5), channel_id=1, source_target_pairs={{0,4},{12,8},{1,5},{13,9},{2,6},{14,10},{3,7},{15,11},{16,20},{28,... | collective-permute-start | bytes 1179656 | tf_op jit(solution)/shard_map/ppermute | solution.py:275
  50.0 2.2 %collective-permute-start.1 = (s32[1]{0:T(128)}, s32[1]{0:T(128)}, u32[]{:S(2)}, u32[]{:S(2)}) collective-permute-start(s32[1]{0:T(128)} %param.9), channel_id=1, source_target_pairs={{4,8},{8,4},{5,9},{9,5},{6,10},{10,6},{7,11},{11,7},{20,24},{24,20... | collective-permute-start | bytes 20 | tf_op jit(solution)/shard_map/ppermute | solution.py:275
  51.1 1.0 copy-start
  51.1 14.4 %copy-start.2 = (bf16[128,640]{1,0:T(8,128)(2,1)S(1)}, bf16[128,640]{1,0:T(8,128)(2,1)}, u32[]{:S(2)}) copy-start(bf16[128,640]{1,0:T(8,128)(2,1)} %copy-done.1) | copy-start | bytes 491524
  52.2 9.2 %collective-permute-start = (s32[1,4]{1,0:T(1,128)S(1)}, s32[1,4]{1,0:T(1,128)S(1)}, u32[]{:S(2)}, u32[]{:S(2)}) collective-permute-start(s32[1,4]{1,0:T(1,128)S(1)} %copy-done), channel_id=1, source_target_pairs={{0,4},{12,8},{1,5},{13,9},{2,6},{14,10},{3,7},{15,11},{16,20},{28,... | collective-permute-start | bytes 56 | tf_op jit(solution)/shard_map/ppermute | solution.py:275
  61.4 16.7 %collective-permute-start.19 = (bf16[512,512]{1,0:T(8,128)(2,1)S(1)}, bf16[512,512]{1,0:T(8,128)(2,1)S(1)}, u32[]{:S(2)}, u32[]{:S(2)}) collective-permute-start(bf16[512,512]{1,0:T(8,128)(2,1)S(1)} %pad_maximum_fusion), channel_id=1, source_target_pairs={{0,4},{12,8},{1,5},{13,9},{2,6},{14,10},{3,7},{15,11},{16,20},{28,... | collective-permute-start | bytes 1572872 | tf_op jit(solution)/shard_map/ppermute | solution.py:275
  68.3 10.8 %collective-permute-start.13 = (bf16[512,384]{1,0:T(8,128)(2,1)S(1)}, bf16[512,384]{1,0:T(8,128)(2,1)S(1)}, u32[]{:S(2)}, u32[]{:S(2)}) collective-permute-start(bf16[512,384]{1,0:T(8,128)(2,1)S(1)} %shard_map.55), channel_id=1, source_target_pairs={{4,0},{8,12},{5,1},{9,13},{6,2},{10,14},{7,3},{11,15},{20,16},{24,... | collective-permute-start | bytes 1179656 | tf_op jit(solution)/shard_map/ppermute | solution.py:275
  69.7 11.7 %collective-permute-start.17 = (bf16[512,256]{1,0:T(8,128)(2,1)S(1)}, bf16[512,256]{1,0:T(8,128)(2,1)S(1)}, u32[]{:S(2)}, u32[]{:S(2)}) collective-permute-start(bf16[512,256]{1,0:T(8,128)(2,1)S(1)} %pad_maximum_fusion.7), channel_id=1, source_target_pairs={{0,4},{12,8},{1,5},{13,9},{2,6},{14,10},{3,7},{15,11},{16,20},{28,... | collective-permute-start | bytes 786440 | tf_op jit(solution)/shard_map/ppermute | solution.py:275
  75.4 6.0 %collective-permute-start.20 = (bf16[512,512]{1,0:T(8,128)(2,1)S(1)}, bf16[512,512]{1,0:T(8,128)(2,1)S(1)}, u32[]{:S(2)}, u32[]{:S(2)}) collective-permute-start(bf16[512,512]{1,0:T(8,128)(2,1)S(1)} %pad_maximum_fusion), channel_id=1, source_target_pairs={{4,8},{8,4},{5,9},{9,5},{6,10},{10,6},{7,11},{11,7},{20,24},{24,20... | collective-permute-start | bytes 1572872 | tf_op jit(solution)/shard_map/ppermute | solution.py:275
  78.2 3.2 %collective-permute-start.21 = (bf16[256,512]{1,0:T(8,128)(2,1)S(1)}, bf16[256,512]{1,0:T(8,128)(2,1)S(1)}, u32[]{:S(2)}, u32[]{:S(2)}) collective-permute-start(bf16[256,512]{1,0:T(8,128)(2,1)S(1)} %constant_dynamic-slice_fusion), channel_id=1, source_target_pairs={{4,8},{8,4},{5,9},{9,5},{6,10},{10,6},{7,11},{11,7},{20,24},{24,20... | collective-permute-start | bytes 786440 | tf_op jit(solution)/shard_map/ppermute | solution.py:275
  79.2 0.9 copy-start.3
  79.2 0.9 copy-start.6
  79.2 0.9 copy-start.7
  79.4 1.4 %collective-permute-start.14 = (bf16[128,384]{1,0:T(8,128)(2,1)S(1)}, bf16[128,384]{1,0:T(8,128)(2,1)S(1)}, u32[]{:S(2)}, u32[]{:S(2)}) collective-permute-start(bf16[128,384]{1,0:T(8,128)(2,1)S(1)} %get-tuple-element.50), channel_id=1, source_target_pairs={{0,1},{1,0},{2,3},{3,2},{4,5},{5,4},{6,7},{7,6},{8,9},{9,8},{10,11... | collective-permute-start | bytes 294920 | tf_op jit(solution)/shard_map/ppermute | solution.py:272
  80.2 5.7 %collective-permute-start.15 = (bf16[128,384]{1,0:T(8,128)(2,1)S(1)}, bf16[128,384]{1,0:T(8,128)(2,1)S(1)}, u32[]{:S(2)}, u32[]{:S(2)}) collective-permute-start(bf16[128,384]{1,0:T(8,128)(2,1)S(1)} %get-tuple-element.49), channel_id=1, source_target_pairs={{0,2},{1,3},{2,0},{3,1},{4,6},{5,7},{6,4},{7,5},{8,10},{9,11},{10,... | collective-permute-start | bytes 294920 | tf_op jit(solution)/shard_map/ppermute | solution.py:272
  80.8 5.1 %collective-permute-start.16 = (bf16[128,384]{1,0:T(8,128)(2,1)S(1)}, bf16[128,384]{1,0:T(8,128)(2,1)S(1)}, u32[]{:S(2)}, u32[]{:S(2)}) collective-permute-start(bf16[128,384]{1,0:T(8,128)(2,1)S(1)} %get-tuple-element.48), channel_id=1, source_target_pairs={{0,3},{1,2},{2,1},{3,0},{4,7},{5,6},{6,5},{7,4},{8,11},{9,10},{10,... | collective-permute-start | bytes 294920 | tf_op jit(solution)/shard_map/ppermute | solution.py:272
  83.1 20.7 %collective-permute-start.22 = (bf16[512,256]{1,0:T(8,128)(2,1)S(1)}, bf16[512,256]{1,0:T(8,128)(2,1)S(1)}, u32[]{:S(2)}, u32[]{:S(2)}) collective-permute-start(bf16[512,256]{1,0:T(8,128)(2,1)S(1)} %shard_map.57), channel_id=1, source_target_pairs={{4,0},{8,12},{5,1},{9,13},{6,2},{10,14},{7,3},{11,15},{20,16},{24,... | collective-permute-start | bytes 786440 | tf_op jit(solution)/shard_map/ppermute | solution.py:275
  103.8 1.9 %collective-permute-start.23 = (bf16[128,256]{1,0:T(8,128)(2,1)S(1)}, bf16[128,256]{1,0:T(8,128)(2,1)S(1)}, u32[]{:S(2)}, u32[]{:S(2)}) collective-permute-start(bf16[128,256]{1,0:T(8,128)(2,1)S(1)} %get-tuple-element.56), channel_id=1, source_target_pairs={{0,1},{1,0},{2,3},{3,2},{4,5},{5,4},{6,7},{7,6},{8,9},{9,8},{10,11... | collective-permute-start | bytes 196616 | tf_op jit(solution)/shard_map/ppermute | solution.py:272
  103.9 5.0 %collective-permute-start.24 = (bf16[128,256]{1,0:T(8,128)(2,1)S(1)}, bf16[128,256]{1,0:T(8,128)(2,1)S(1)}, u32[]{:S(2)}, u32[]{:S(2)}) collective-permute-start(bf16[128,256]{1,0:T(8,128)(2,1)S(1)} %get-tuple-element.55), channel_id=1, source_target_pairs={{0,2},{1,3},{2,0},{3,1},{4,6},{5,7},{6,4},{7,5},{8,10},{9,11},{10,... | collective-permute-start | bytes 196616 | tf_op jit(solution)/shard_map/ppermute | solution.py:272
  104.5 4.9 %collective-permute-start.25 = (bf16[128,256]{1,0:T(8,128)(2,1)S(1)}, bf16[128,256]{1,0:T(8,128)(2,1)S(1)}, u32[]{:S(2)}, u32[]{:S(2)}) collective-permute-start(bf16[128,256]{1,0:T(8,128)(2,1)S(1)} %get-tuple-element.54), channel_id=1, source_target_pairs={{0,3},{1,2},{2,1},{3,0},{4,7},{5,6},{6,5},{7,4},{8,11},{9,10},{10,... | collective-permute-start | bytes 196616 | tf_op jit(solution)/shard_map/ppermute | solution.py:272
  108.9 0.8 copy-start.5

commit v3 on v0

--- a/solution.py
+++ b/solution.py
@@ -1,9 +1,15 @@
+import math
+
 import jax
 import jax.numpy as jnp
 from jax import lax
+from jax.experimental import pallas as pl
+from jax.experimental.pallas import tpu as pltpu
 from jax.sharding import PartitionSpec as P
 
 HEAD_DIM = 128
+SCALE = 1.0 / HEAD_DIM**0.5
+LOG2E = math.log2(math.e)
 
 
 def padded(x, sides, width):
@@ -19,14 +25,6 @@
     return x
 
 
-def shortened(x):
-
-    def short(part):
-        return part.astype(jnp.bfloat16) if part.dtype == jnp.float32 else part
-
-    return jax.tree.map(short, x)
-
-
 def from_partner(x, axis, bit):
     return lax.ppermute(x, axis, [(i, i ^ 1 << bit) for i in range(lax.axis_size(axis))])
 
@@ -45,11 +43,10 @@
     q_three = query_rows.reshape(count, heads, HEAD_DIM).transpose(1, 0, 2)
     k_three = key_rows.reshape(-1, heads, HEAD_DIM).transpose(1, 0, 2)
     v_three = value_rows.reshape(-1, heads, HEAD_DIM).transpose(1, 0, 2)
-    scale = 1.0 / HEAD_DIM**0.5
 
     def one_head(operands):
         q_head, k_head, v_head = operands
-        scores = jnp.dot(q_head, k_head.T, preferred_element_type=jnp.float32) * scale
+        scores = jnp.dot(q_head, k_head.T, preferred_element_type=jnp.float32) * SCALE
         scores = jnp.where(valid[None, :] > 0, scores, -1e30)
         top = jnp.max(scores, axis=1, keepdims=True)
         weights = jnp.exp(scores - top) * valid[None, :]
@@ -65,7 +62,7 @@
     return jnp.where(upper == 1, jnp.concatenate([theirs, mine]), jnp.concatenate([mine, theirs]))
 
 
-def per_device(queries, keys, values, pair_mask, tile_offset):
+def general(queries, keys, values, pair_mask, tile_offset):
     frames_n = lax.axis_size("frame")
     current = lax.axis_index("frame")
     q_rows, k_rows, v_rows = (
@@ -122,10 +119,7 @@
         active = [level for level in swap_levels if level >= bit]
         k_pack = jnp.concatenate([growing[level][0].reshape(-1, width) for level in active])
         v_pack = jnp.concatenate([growing[level][1].reshape(-1, width) for level in active])
-        k_in, v_in = (
-            from_partner(shortened(k_pack), "frame", bit).astype(k_pack.dtype),
-            from_partner(shortened(v_pack), "frame", bit).astype(v_pack.dtype),
-        )
+        k_in, v_in = (from_partner(k_pack, "frame", bit), from_partner(v_pack, "frame", bit))
         upper = current // 2**bit % 2
         position = 0
         for level in active:
@@ -160,7 +154,269 @@
     return lax.all_to_all(result, "head", split_axis=0, concat_axis=1, tiled=True)
 
 
+FIRST = 3
+INFO_ROWS = 16
+OUTER = [(0, 1), (1, 0), (2, 3), (3, 2)]
+INNER = [(0, 0), (1, 2), (2, 1), (3, 3)]
+OUTWARD = [(1, 0), (2, 3)]
+
+
+def fold(x):
+    parts = [x[:, at : at + 128] for at in range(0, x.shape[1], 128)]
+    best = parts[0]
+    for part in parts[1:]:
+        best = jnp.maximum(best, part)
+    return best
+
+
+def scores_of(q, slots, held):
+    free, top = None, None
+    for at, (k, _, valid) in enumerate(slots):
+        s = lax.dot_general(q, k(), (((1,), (1,)), ((), ())), preferred_element_type=jnp.float32)
+        held[:, at * s.shape[1] : (at + 1) * s.shape[1]] = s
+        best = fold(s)
+        if valid is None:
+            free = best if free is None else jnp.maximum(free, best)
+        else:
+            best = jnp.where(valid, jnp.max(best, axis=1, keepdims=True), -1e30)
+            top = best if top is None else jnp.maximum(top, best)
+    free = jnp.max(free, axis=1, keepdims=True)
+    return free if top is None else jnp.maximum(free, top)
+
+
+def mixed_of(top, slots, held):
+    factor = SCALE * LOG2E
+    total, mixed = None, None
+    for at, (_, v, valid) in enumerate(slots):
+        values = v()
+        tile = values.shape[0]
+        level = top if valid is None else jnp.where(valid, top, 1e30)
+        w = jnp.exp2((held[:, at * tile : (at + 1) * tile] - level) * factor)
+        mix = jnp.dot(w.astype(jnp.bfloat16), values, preferred_element_type=jnp.float32)
+        mixed = mix if mixed is None else mixed + mix
+        for begin in range(0, tile, 128):
+            part = w[:, begin : begin + 128]
+            total = part if total is None else total + part
+    return (mixed * (1.0 / jnp.sum(total, axis=1, keepdims=True))).astype(jnp.bfloat16)
+
+
+def tiles_of(ref, i, tile):
+    half = ref.shape[1] // 2
+
+    def load(begin, at):
+        return lambda: ref[begin : begin + tile, pl.ds(pl.multiple_of(at + i * HEAD_DIM, HEAD_DIM), HEAD_DIM)]
+
+    return [(load(begin, 0), load(begin, half)) for begin in range(0, ref.shape[0] - tile + 1, tile)]
+
+
+def with_valid(pairs, valid):
+    return [(k, v, ok) for (k, v), ok in zip(pairs, valid)]
+
+
+def run_chunks(chunks):
+    tops = []
+    for q, slots, held, _ in chunks:
+        tops.append(scores_of(q(), slots, held))
+    for top, (_, slots, held, store) in zip(tops, chunks):
+        store(mixed_of(top, slots, held))
+
+
+def first_kernel(mask, q_mine, q_other, q_guest, mine, other, n1_mine, n1_other, n2_mine, n2_other, r1, *rest):
+    outs, guest_out, held = rest[:4], rest[4], rest[5:]
+    z = lax.axis_index("frame")
+    x = (lax.axis_index("head") // 2).astype(jnp.float32)
+    tile = r1.shape[0]
+    rows = tile // 2
+    heads = r1.shape[1] // (2 * HEAD_DIM)
+
+    @pl.when((z == 1) | (z == 2))
+    def _():
+        def told(ref, group):
+            return ref[tile : tile + 1, group * 128 : (group + 1) * 128][:, :1].astype(jnp.float32)
+
+        near2 = jnp.where(z == 1, told(n1_mine, 2), told(n1_mine, 1)) > 0.5
+        near1 = jnp.where(z == 1, told(n1_mine, 3), told(n1_mine, 0)) > 0.5
+        picked = told(n2_mine, 4) == x
+        own_valid = [None] * 6 + [mask[0, z ^ 2] == 1]
+        guest_valid = [None] * 4 + [near2 & picked, near2 & jnp.logical_not(picked), near1]
+
+        def one_head(i, carry):
+            lanes = pl.ds(pl.multiple_of(i * HEAD_DIM, HEAD_DIM), HEAD_DIM)
+            pairs = []
+            for ref in (mine, other, n1_mine, n1_other, n2_mine, n2_other, r1):
+                pairs += tiles_of(ref, i, tile)
+            own, guest = with_valid(pairs, own_valid), with_valid(pairs, guest_valid)
+
+            def keep_own(half):
+                def store(value):
+                    outs[2 * half][:, lanes] = value[:rows]
+                    outs[2 * half + 1][:, lanes] = value[rows:]
+
+                return store
+
+            def keep_guest(half):
+                def store(value):
+                    guest_out[half * tile : (half + 1) * tile, lanes] = value
+
+                return store
+
+            chunks = [
+                (lambda: q_guest[:tile, lanes], guest, held[0], keep_guest(0)),
+                (lambda: q_guest[tile:, lanes], guest, held[1], keep_guest(1)),
+                (lambda: q_mine[:, lanes], own, held[2], keep_own(0)),
+                (lambda: q_other[:, lanes], own, held[3], keep_own(1)),
+            ]
+            run_chunks(chunks)
+            return carry
+
+        lax.fori_loop(0, heads, one_head, 0)
+
+
+def second_kernel(mask, q_mine, q_other, whole, n1, n2, r1, r2, r3, *rest):
+    outs, held = rest[:4], rest[4:]
+    z = lax.axis_index("frame")
+    tile = r1.shape[0]
+    rows = tile // 2
+    heads = r1.shape[1] // (2 * HEAD_DIM)
+    skip = q_mine.shape[1] - heads * HEAD_DIM
+
+    def body(refs, valid):
+        def one_head(i, carry):
+            lanes = pl.ds(pl.multiple_of(i * HEAD_DIM, HEAD_DIM), HEAD_DIM)
+            q_lanes = pl.ds(pl.multiple_of(skip + i * HEAD_DIM, HEAD_DIM), HEAD_DIM)
+            pairs = []
+            for ref in refs:
+                pairs += tiles_of(ref, i, tile)
+            slots = with_valid(pairs, valid)
+
+            def keep(half):
+                def store(value):
+                    outs[2 * half][:, lanes] = value[:rows]
+                    outs[2 * half + 1][:, lanes] = value[rows:]
+
+                return store
+
+            run_chunks(
+                [
+                    (lambda: q_mine[:, q_lanes], slots, held[0], keep(0)),
+                    (lambda: q_other[:, q_lanes], slots, held[1], keep(1)),
+                ]
+            )
+            return carry
+
+        lax.fori_loop(0, heads, one_head, 0)
+
+    inner = (z == 1) | (z == 2)
+
+    @pl.when(inner)
+    def _():
+        body([whole, n1, n2, r1], [None] * 6 + [mask[0, z ^ 2] == 1])
+
+    @pl.when(jnp.logical_not(inner))
+    def _():
+        body([whole, n1, r2, r3], [None] * 4 + [mask[0, z ^ 2] == 1, mask[0, z ^ 3] == 1])
+
+
+def run_kernel(kernel, mask, arrays, outs, chunks, tile, heads):
+    return pl.pallas_call(
+        kernel,
+        in_specs=[pl.BlockSpec(memory_space=pltpu.SMEM)] + [pl.BlockSpec(memory_space=pltpu.VMEM)] * len(arrays),
+        out_specs=[pl.BlockSpec(memory_space=pltpu.VMEM)] * len(outs),
+        out_shape=[jax.ShapeDtypeStruct((rows, heads * HEAD_DIM), jnp.bfloat16) for rows in outs],
+        scratch_shapes=[pltpu.VMEM((tile, 7 * tile), jnp.float32) for _ in range(chunks)],
+        compiler_params=pltpu.CompilerParams(vmem_limit_bytes=20 * 1024 * 1024),
+        cost_estimate=pl.CostEstimate(
+            flops=heads * chunks * tile * 7 * tile * HEAD_DIM * 4,
+            bytes_accessed=sum(x.size * 2 for x in arrays),
+            transcendentals=heads * chunks * tile * 7 * tile,
+        ),
+    )(mask, *arrays)
+
+
+def four_frames(queries, keys, values, pair_mask, tile_offset):
+    z = lax.axis_index("frame")
+    h = lax.axis_index("head")
+    x = h // 2
+    rows, features = queries.shape
+    tile = 2 * rows
+    width = features // 4
+    heads = width // HEAD_DIM
+    cut = FIRST * HEAD_DIM
+
+    def columns(array, d, begin, end):
+        return lax.dynamic_slice_in_dim(array, (h ^ d) * width + begin, end - begin, axis=1)
+
+    def to_head(array, d):
+        return lax.ppermute(array, "head", [(i, i ^ d) for i in range(4)])
+
+    def along(array, pairs):
+        return lax.ppermute(array, "frame", pairs)
+
+    def after(array, earlier):
+        return lax.optimization_barrier((array, earlier))[0]
+
+    def beside(*arrays):
+        return jnp.concatenate(arrays, axis=1)
+
+    def below(*arrays):
+        return jnp.concatenate(arrays, axis=0)
+
+    k = [columns(keys, d, 0, cut) for d in range(4)]
+    v = [columns(values, d, 0, cut) for d in range(4)]
+    k, v = lax.optimization_barrier((k, v))
+    got = to_head(beside(k[1], v[1], k[3], v[3]), 1)
+    told = [pair_mask[0, g] for g in range(4)] + [tile_offset[0]] + [0] * (2 * FIRST - 5)
+    told = beside(*[jnp.broadcast_to(jnp.asarray(t).astype(jnp.bfloat16), (INFO_ROWS, 128)) for t in told])
+    mine = below(beside(k[0], v[0]), got[:, : 2 * cut], told)
+    other = to_head(below(beside(k[2], v[2]), got[:, 2 * cut :]), 2)
+    n1_mine = along(mine, OUTER)
+    n2_mine = along(mine, INNER)
+    n1_other = along(other, OUTER)
+    n2_other = along(other, INNER)
+    picked = n1_mine[tile, 4 * 128] == x.astype(jnp.bfloat16)
+    r1 = along(jnp.where(picked, n1_mine[:tile], n1_other), INNER)
+    first = [mine, other, n1_mine, n1_other, n2_mine, n2_other, r1]
+
+    q = [columns(queries, d, 0, width) for d in range(4)]
+    k = [columns(keys, d, cut, width) for d in range(4)]
+    v = [columns(values, d, cut, width) for d in range(4)]
+    q, k, v = lax.optimization_barrier((q, k, v))
+    got = to_head(after(beside(q[1], q[3], k[1], v[1], k[3], v[3]), mine), 1)
+    q_mine = below(q[0], got[:, :width])
+    q_other = to_head(after(below(q[2], got[:, width : 2 * width]), other), 2)
+    split = 2 * width + 2 * (width - cut)
+    mine2 = below(beside(k[0], v[0]), got[:, 2 * width : split])
+    other2 = to_head(after(below(beside(k[2], v[2]), got[:, split:]), q_other), 2)
+    q_guest = along(below(q_mine[:, :cut], q_other[:, :cut]), OUTER)
+    whole = jnp.where(x == tile_offset[0], below(mine2, other2), below(other2, mine2))
+    n1 = along(whole, OUTER)
+    n2 = along(whole, INNER)
+    r1 = along(n1[:tile], INNER)
+    r2 = along(n2[:tile], OUTER)
+    r3 = along(r1, OUTER)
+
+    *own, guest = run_kernel(
+        first_kernel, pair_mask, [q_mine, q_other, q_guest, *first], [rows] * 4 + [2 * tile], 4, tile, FIRST
+    )
+    back = along(guest, OUTWARD)
+    end_frame = (z == 0) | (z == 3)
+    out = [jnp.where(end_frame, back[d * rows : (d + 1) * rows], own[d]) for d in range(4)]
+    out = [out[0]] + [to_head(out[d], d) for d in (1, 2, 3)]
+    late = run_kernel(
+        second_kernel, pair_mask, [q_mine, q_other, whole, n1, n2, r1, r2, r3], [rows] * 4, 2, tile, heads - FIRST
+    )
+    late = [late[0]] + [to_head(late[d], d) for d in (1, 2, 3)]
+    result = jnp.zeros((rows, features), jnp.bfloat16)
+    for d in range(4):
+        result = lax.dynamic_update_slice_in_dim(result, out[d], (h ^ d) * width, axis=1)
+    for d in range(4):
+        result = lax.dynamic_update_slice_in_dim(result, late[d], (h ^ d) * width + cut, axis=1)
+    return result
+
+
 def solution(mesh):
+    sizes = dict(mesh.shape)
+    per_device = four_frames if sizes["frame"] == 4 and sizes["head"] == 4 else general
     return jax.shard_map(
         per_device,
         mesh=mesh,

time: 172 us -> 103 us (0.60)
  blocking collectives: 25.3 us -> 0 us
  matrix products: 18.7 us -> 0 us
  starting transfers between devices: 14.2 us -> 32.6 us
  local copies, waits for them, and re-layouts: 31 us -> 14.2 us
  between operations: 14.2 us -> 1.69 us
  other arithmetic: 14.5 us -> 3.1 us
  waiting for transfers between devices: 53.3 us -> 45.4 us
  Pallas kernels: 0 us -> 5.42 us
    ppermute x2 -> x23, starting transfers between devices: 6.51 us -> 32.6 us  [the longest x12 24.6 us: along(): return lax.ppermute(array, 'frame', pairs)]
    all_to_all x2 -> x0, blocking collectives: 25.3 us -> none  [the longest x1 12.7 us: per_device(): lax.all_to_all(values, 'head', split_axis=1, concat_axis=0, tiled=True)]
    all_to_all x2 -> x0, waiting for transfers between devices: 19.5 us -> none  [the longest x1 9.93 us: per_device(): lax.all_to_all(queries, 'head', split_axis=1, concat_axis=0, tiled=True)]
    dot_general x10 -> x0, matrix products: 18.7 us -> none  [the longest x5 14.2 us: one_head(): jnp.dot(weights.astype(jnp.bfloat16), v_head, preferred_element_type=jnp....]
    ppermute x2 -> x23, waiting for transfers between devices: 33.8 us -> 45.4 us  [the longest x12 26.5 us: along(): return lax.ppermute(array, 'frame', pairs)]
    all_to_all x2 -> x0, starting transfers between devices: 7.69 us -> none  [the longest x1 4.21 us: per_device(): lax.all_to_all(keys, 'head', split_axis=1, concat_axis=0, tiled=True)]
    slice x3 -> x8, local copies, waits for them, and re-layouts: 8.96 us -> 1.36 us  [the longest x1 0.65 us: four_frames(): pair_mask[0, g]]
    reduce_sum x5 -> x0, other arithmetic: 5.49 us -> none  [one_head(): total = jnp.sum(weights, axis=1, keepdims=True)]
  transfers between devices with their start and end apart: 6 -> 23, of which waited for: 4 -> 10; matrix products, arithmetic and copies ran while one was open for 11% -> 13% of each run, Pallas kernels for 0% -> 2%
where the time goes in v3:
time: 103 us; the launch traced here: 102 us
  waiting for transfers between devices  45.4 us (44%)
  starting transfers between devices  32.6 us (32%)
  local copies, waits for them, and re-layouts  14.2 us (14%)
  Pallas kernels  5.42 us (5%)
  other arithmetic  3.1 us (3%)
  between operations  1.69 us (2%)
    ppermute x12, waiting for transfers between devices, along(): return lax.ppermute(array, 'frame', pairs)  26.5 us
    ppermute x12, starting transfers between devices, along(): return lax.ppermute(array, 'frame', pairs)  24.6 us
    ppermute x11, waiting for transfers between devices, to_head(): return lax.ppermute(array, 'head', [(i, i ^ d) for i in range(4)])  18.9 us
    unnamed x27, local copies, waits for them, and re-layouts  8.22 us
    ppermute x11, starting transfers between devices, to_head(): return lax.ppermute(array, 'head', [(i, i ^ d) for i in range(4)])  7.96 us
    pallas_call x2, Pallas kernels, run_kernel(): pl.pallas_call(kernel, in_specs=[pl.BlockSpec(memory_space=pltpu.SMEM)] +...  5.42 us
    dynamic_slice x3, local copies, waits for them, and re-layouts, columns(): lax.dynamic_slice_in_dim(array, (h ^ d) * width + begin, end - begin, axi...  3.17 us
  transfers between devices with their start and end apart: 23, of which 10 were waited for; matrix products, arithmetic and copies ran while one was open for 13% of the time, Pallas kernels for 2%

profile of v3, /device:TPU:0, one launch (start us, length us, event | category | flops | bytes accessed | tf_op | source)
XLA Modules:
  0.0 102.4 jit_solution(15314329360888453169)
XLA Ops:
  0.0 1.3 %constant_dynamic-slice_fusion = (bf16[128,384]{1,0:T(8,128)(2,1)S(1)}, bf16[128,384]{1,0:T(8,128)(2,1)S(1)}, bf16[128,384]{1,0:T(8,128)(2,1)S(1)}, bf16[128,384...) fusion(bf16[128,2560]{1,0:T(8,128)(2,1)} %param.7, ...), kind=kLoop, calls=%fused_computation.38 | loop fusion | bytes 1572880 | tf_op jit(solution)/shard_map/dynamic_slice | solution.py:347
  1.9 0.7 copy-done.2
  2.5 0.7 fusion.5
  3.2 0.6 constant_dynamic-update-slice_fusion.11
  4.6 1.8 %constant_dynamic-slice_fusion.8 = (bf16[128,256]{1,0:T(8,128)(2,1)S(1)}, bf16[128,256]{1,0:T(8,128)(2,1)}, bf16[128,256]{1,0:T(8,128)(2,1)S(1)}, bf16[128,256]{...) fusion(bf16[128,2560]{1,0:T(8,128)(2,1)} %param.7, ...), kind=kLoop, calls=%fused_computation.46 | loop fusion | bytes 1048592 | tf_op jit(solution)/shard_map/dynamic_slice | solution.py:347
  6.4 0.7 constant_dynamic-update-slice_fusion.5
  7.1 0.6 constant_dynamic-update-slice_fusion.10
  7.7 0.6 constant_dynamic-update-slice_fusion.9
  8.3 0.6 constant_dynamic-update-slice_fusion.8
  9.0 0.7 constant_dynamic-update-slice_fusion.4
  9.7 0.6 constant_dynamic-update-slice_fusion.3
  10.3 0.6 constant_dynamic-update-slice_fusion.2
  11.0 0.6 constant_dynamic-update-slice_fusion.1
  11.6 0.6 constant_dynamic-update-slice_fusion
  12.5 3.0 %collective-permute-start.5 = (bf16[272,768]{1,0:T(8,128)(2,1)S(1)}, bf16[272,768]{1,0:T(8,128)(2,1)S(1)}, u32[]{:S(2)}, u32[]{:S(2)}) collective-permute-start(bf16[272,768]{1,0:T(8,128)(2,1)S(1)} %pad_maximum_fusion.mine), channel_id=1, source_target_pairs={{0,4},{4,0},{8,12},{12,8},{1,5},{5,1},{9,13},{13,9},{2,6},{6,2},{1... | collective-permute-start | bytes 1253384 | tf_op jit(solution)/shard_map/ppermute | solution.py:353
  15.5 1.6 %collective-permute-start.2 = (bf16[256,768]{1,0:T(8,128)(2,1)S(1)}, bf16[256,768]{1,0:T(8,128)(2,1)}, u32[]{:S(2)}, u32[]{:S(2)}) collective-permute-start(bf16[256,768]{1,0:T(8,128)(2,1)S(1)} %pad_maximum_fusion.2), channel_id=1, source_target_pairs={{0,2},{1,3},{2,0},{3,1},{4,6},{5,7},{6,4},{7,5},{8,10},{9,11},{10,... | collective-permute-start | bytes 1179656 | tf_op jit(solution)/shard_map/ppermute | solution.py:350
  17.0 0.7 collective-permute-start.7
  17.7 8.8 %collective-permute-done.2.other = bf16[256,768]{1,0:T(8,128)(2,1)} collective-permute-done((bf16[256,768]{1,0:T(8,128)(2,1)S(1)}, bf16[256,768]{1,0:T(8,128)(2,1)}, u32[]{:S(2)}, u32[]{:S(2)}) %collective-permute-start.2) | collective-permute-done | bytes 393248 | tf_op jit(solution)/shard_map/ppermute | solution.py:350
  26.8 4.5 %collective-permute-start.8 = (bf16[256,768]{1,0:T(8,128)(2,1)}, bf16[256,768]{1,0:T(8,128)(2,1)}, u32[]{:S(2)}, u32[]{:S(2)}) collective-permute-start(bf16[256,768]{1,0:T(8,128)(2,1)} %collective-permute-done.2.other), channel_id=1, source_target_pairs={{0,0},{4,8},{8,4},{12,12},{1,1},{5,9},{9,5},{13,13},{2,2},{6,10},{... | collective-permute-start | bytes 1179656 | tf_op jit(solution)/shard_map/ppermute | solution.py:353
  31.3 0.6 slice.91
  32.6 1.7 %collective-permute-start.3 = (bf16[256,640]{1,0:T(8,128)(2,1)S(1)}, bf16[256,640]{1,0:T(8,128)(2,1)S(1)}, u32[]{:S(2)}, u32[]{:S(2)}) collective-permute-start(bf16[256,640]{1,0:T(8,128)(2,1)S(1)} %pad_maximum_fusion.5), channel_id=1, source_target_pairs={{0,2},{1,3},{2,0},{3,1},{4,6},{5,7},{6,4},{7,5},{8,10},{9,11},{10,... | collective-permute-start | bytes 983048 | tf_op jit(solution)/shard_map/ppermute | solution.py:350
  34.4 2.2 %collective-permute-done.6.n1_other = bf16[256,768]{1,0:T(8,128)(2,1)S(1)} collective-permute-done((bf16[256,768]{1,0:T(8,128)(2,1)}, bf16[256,768]{1,0:T(8,128)(2,1)S(1)}, u32[]{:S(2)}, u32[]{:S(2)}) %collective-permute-start.6) | collective-permute-done | bytes 393248 | tf_op jit(solution)/shard_map/ppermute | solution.py:353
  36.6 0.8 slice_select_fusion
  37.4 4.5 %collective-permute-start.9 = (bf16[256,768]{1,0:T(8,128)(2,1)}, bf16[256,768]{1,0:T(8,128)(2,1)}, u32[]{:S(2)}, u32[]{:S(2)}) collective-permute-start(bf16[256,768]{1,0:T(8,128)(2,1)} %slice_select_fusion), channel_id=1, source_target_pairs={{0,0},{4,8},{8,4},{12,12},{1,1},{5,9},{9,5},{13,13},{2,2},{6,10},{... | collective-permute-start | bytes 1179656 | tf_op jit(solution)/shard_map/ppermute | solution.py:353
  41.9 1.5 %collective-permute-start.14 = (bf16[256,512]{1,0:T(8,128)(2,1)S(1)}, bf16[256,512]{1,0:T(8,128)(2,1)}, u32[]{:S(2)}, u32[]{:S(2)}) collective-permute-start(bf16[256,512]{1,0:T(8,128)(2,1)S(1)} %pad_maximum_fusion.6), channel_id=1, source_target_pairs={{0,2},{1,3},{2,0},{3,1},{4,6},{5,7},{6,4},{7,5},{8,10},{9,11},{10,... | collective-permute-start | bytes 786440 | tf_op jit(solution)/shard_map/ppermute | solution.py:350
  43.4 0.8 pad_maximum_fusion.3
  44.2 0.7 collective-permute-start.4
  44.9 3.4 %collective-permute-done.14 = bf16[256,512]{1,0:T(8,128)(2,1)} collective-permute-done((bf16[256,512]{1,0:T(8,128)(2,1)S(1)}, bf16[256,512]{1,0:T(8,128)(2,1)}, u32[]{:S(2)}, u32[]{:S(2)}) %collective-permute-start.14) | collective-permute-done | bytes 262176 | tf_op jit(solution)/shard_map/ppermute | solution.py:350
  48.4 1.2 %maximum_select_fusion.whole = bf16[512,512]{1,0:T(8,128)(2,1)S(1)} fusion(bf16[256,512]{1,0:T(8,128)(2,1)} %collective-permute-done.14, bf16[128,512]{1,0:T(8,128)(2,1)S(1)} %get-tuple-element.89, bf16[128,512]{1,0:T(8,128)(2,1)S(1)} %constant_dynamic-update-slice_fusion.12, pred[]{:T(512)S(6)} %eq.15), kind=kLoop, calls=%fused_computation | loop fusion | flops 3407872 | bytes 1048577 | tf_op jit(solution)/shard_map/jit(_where)/select_n | solution.py:391
  49.6 0.7 collective-permute-start.15
  50.3 0.8 copy-done
  51.0 5.5 %collective-permute-done.4.q_guest = bf16[512,384]{1,0:T(8,128)(2,1)} collective-permute-done((bf16[512,384]{1,0:T(8,128)(2,1)}, bf16[512,384]{1,0:T(8,128)(2,1)}, u32[]{:S(2)}, u32[]{:S(2)}) %collective-permute-start.4) | collective-permute-done | bytes 393248 | tf_op jit(solution)/shard_map/ppermute | solution.py:353
  56.6 1.0 copy-done.1
  57.6 2.1 %shard_map.55 = (bf16[128,384]{1,0:T(8,128)(2,1)S(1)}, bf16[128,384]{1,0:T(8,128)(2,1)S(1)}, bf16[128,384]{1,0:T(8,128)(2,1)S(1)}, bf16[128,384]{1,0:T(8,128)(2,1)S(1)}, bf16[512,384]{1,0:T(8,128)(2,1)}) custom-call(s32[1,4]{1,0:T(1,128)S(1)} %copy-done.2, bf16[256,640]{1,0:T(8,128)(2,1)S(1)} %pad_maximum_fusion.4.q_mine, ...), custom_call_target="tpu_custom_call" | custom-call | flops 2818572288 | bytes 3874816 | tf_op jit(solution)/shard_map/pallas_call | solution.py:321
  59.7 1.3 %collective-permute-start.10 = (bf16[512,384]{1,0:T(8,128)(2,1)}, bf16[512,384]{1,0:T(8,128)(2,1)S(1)}, u32[]{:S(2)}, u32[]{:S(2)}) collective-permute-start(bf16[512,384]{1,0:T(8,128)(2,1)} %get-tuple-element.55), channel_id=1, source_target_pairs={{4,0},{8,12},{5,1},{9,13},{6,2},{10,14},{7,3},{11,15},{20,16},{24,... | collective-permute-start | bytes 1179656 | tf_op jit(solution)/shard_map/ppermute | solution.py:353
  61.0 0.7 collective-permute-start.16
  61.7 2.7 %collective-permute-done.15.n1 = bf16[512,512]{1,0:T(8,128)(2,1)S(1)} collective-permute-done((bf16[512,512]{1,0:T(8,128)(2,1)S(1)}, bf16[512,512]{1,0:T(8,128)(2,1)S(1)}, u32[]{:S(2)}, u32[]{:S(2)}) %collective-permute-start.15) | collective-permute-done | bytes 524320 | tf_op jit(solution)/shard_map/ppermute | solution.py:353
  64.4 0.7 collective-permute-start.17
  65.1 12.3 %collective-permute-done.10 = bf16[512,384]{1,0:T(8,128)(2,1)S(1)} collective-permute-done((bf16[512,384]{1,0:T(8,128)(2,1)}, bf16[512,384]{1,0:T(8,128)(2,1)S(1)}, u32[]{:S(2)}, u32[]{:S(2)}) %collective-permute-start.10) | collective-permute-done | bytes 393248 | tf_op jit(solution)/shard_map/ppermute | solution.py:353
  77.7 5.5 %collective-permute-start.18 = (bf16[256,512]{1,0:T(8,128)(2,1)S(1)}, bf16[256,512]{1,0:T(8,128)(2,1)S(1)}, u32[]{:S(2)}, u32[]{:S(2)}) collective-permute-start(bf16[256,512]{1,0:T(8,128)(2,1)S(1)} %slice.100), channel_id=1, source_target_pairs={{0,4},{4,0},{8,12},{12,8},{1,5},{5,1},{9,13},{13,9},{2,6},{6,2},{1... | collective-permute-start | bytes 786440 | tf_op jit(solution)/shard_map/ppermute | solution.py:353
  83.7 2.2 %collective-permute-start.19 = (bf16[256,512]{1,0:T(8,128)(2,1)S(1)}, bf16[256,512]{1,0:T(8,128)(2,1)S(1)}, u32[]{:S(2)}, u32[]{:S(2)}) collective-permute-start(bf16[256,512]{1,0:T(8,128)(2,1)S(1)} %collective-permute-done.17.r1), channel_id=1, source_target_pairs={{0,4},{4,0},{8,12},{12,8},{1,5},{5,1},{9,13},{13,9},{2,6},{6,2},{1... | collective-permute-start | bytes 786440 | tf_op jit(solution)/shard_map/ppermute | solution.py:353
  85.9 2.9 %collective-permute-done.12 = bf16[128,384]{1,0:T(8,128)(2,1)S(1)} collective-permute-done((bf16[128,384]{1,0:T(8,128)(2,1)S(1)}, bf16[128,384]{1,0:T(8,128)(2,1)S(1)}, u32[]{:S(2)}, u32[]{:S(2)}) %collective-permute-start.12) | collective-permute-done | bytes 98336 | tf_op jit(solution)/shard_map/ppermute | solution.py:350
  88.9 3.8 %collective-permute-done.19.r3 = bf16[256,512]{1,0:T(8,128)(2,1)S(1)} collective-permute-done((bf16[256,512]{1,0:T(8,128)(2,1)S(1)}, bf16[256,512]{1,0:T(8,128)(2,1)S(1)}, u32[]{:S(2)}, u32[]{:S(2)}) %collective-permute-start.19) | collective-permute-done | bytes 262176 | tf_op jit(solution)/shard_map/ppermute | solution.py:353
  92.7 3.3 %shard_map.56 = (bf16[128,256]{1,0:T(8,128)(2,1)S(1)}, bf16[128,256]{1,0:T(8,128)(2,1)S(1)}, bf16[128,256]{1,0:T(8,128)(2,1)S(1)}, bf16[128,256]{1,0:T(8,128)(2,1)S(1)}) custom-call(s32[1,4]{1,0:T(1,128)S(1)} %copy-done.2, bf16[256,640]{1,0:T(8,128)(2,1)S(1)} %pad_maximum_fusion.4.q_mine, bf16[256,640]{1,0:T(8,128)(2,1)S(1)} %collective-permute-done.3.q_other, ...), custom_call_target="tpu_custom_call" | custom-call | flops 939524096 | bytes 3014656 | tf_op jit(solution)/shard_map/pallas_call | solution.py:321
  96.3 1.2 %collective-permute-start.21 = (bf16[128,256]{1,0:T(8,128)(2,1)S(1)}, bf16[128,256]{1,0:T(8,128)(2,1)S(1)}, u32[]{:S(2)}, u32[]{:S(2)}) collective-permute-start(bf16[128,256]{1,0:T(8,128)(2,1)S(1)} %get-tuple-element.67), channel_id=1, source_target_pairs={{0,2},{1,3},{2,0},{3,1},{4,6},{5,7},{6,4},{7,5},{8,10},{9,11},{10,... | collective-permute-start | bytes 196616 | tf_op jit(solution)/shard_map/ppermute | solution.py:350
  98.0 2.8 %collective-permute-done.21 = bf16[128,256]{1,0:T(8,128)(2,1)S(1)} collective-permute-done((bf16[128,256]{1,0:T(8,128)(2,1)S(1)}, bf16[128,256]{1,0:T(8,128)(2,1)S(1)}, u32[]{:S(2)}, u32[]{:S(2)}) %collective-permute-start.21) | collective-permute-done | bytes 65568 | tf_op jit(solution)/shard_map/ppermute | solution.py:350
  100.8 1.0 collective-permute-done.22
  101.8 0.6 constant_dynamic-update-slice_fusion.14
  (61 shorter events, 3.1 us)
Async XLA Ops:
  1.3 3.2 %copy-start.3 = (bf16[128,2560]{1,0:T(8,128)(2,1)S(1)}, bf16[128,2560]{1,0:T(8,128)(2,1)}, u32[]{:S(2)}) copy-start(bf16[128,2560]{1,0:T(8,128)(2,1)} %param.5) | copy-start | bytes 1966084
  1.4 10.9 %collective-permute-start = (bf16[128,1536]{1,0:T(8,128)(2,1)S(1)}, bf16[128,1536]{1,0:T(8,128)(2,1)S(1)}, u32[]{:S(2)}, u32[]{:S(2)}) collective-permute-start(bf16[128,1536]{1,0:T(8,128)(2,1)S(1)} %pad_maximum_fusion.1), channel_id=1, source_target_pairs={{0,1},{1,0},{2,3},{3,2},{4,5},{5,4},{6,7},{7,6},{8,9},{9,8},{10,11... | collective-permute-start | bytes 1179656 | tf_op jit(solution)/shard_map/ppermute | solution.py:350
  1.9 0.7 copy-start.2
  12.3 20.2 %collective-permute-start.1 = (bf16[128,2304]{1,0:T(8,128)(2,1)}, bf16[128,2304]{1,0:T(8,128)(2,1)S(1)}, u32[]{:S(2)}, u32[]{:S(2)}) collective-permute-start(bf16[128,2304]{1,0:T(8,128)(2,1)} %constant_dynamic-update-slice_fusion), channel_id=1, source_target_pairs={{0,1},{1,0},{2,3},{3,2},{4,5},{5,4},{6,7},{7,6},{8,9},{9,8},{10,11... | collective-permute-start | bytes 1769480 | tf_op jit(solution)/shard_map/ppermute | solution.py:350
  12.5 18.8 %collective-permute-start.5 = (bf16[272,768]{1,0:T(8,128)(2,1)S(1)}, bf16[272,768]{1,0:T(8,128)(2,1)S(1)}, u32[]{:S(2)}, u32[]{:S(2)}) collective-permute-start(bf16[272,768]{1,0:T(8,128)(2,1)S(1)} %pad_maximum_fusion.mine), channel_id=1, source_target_pairs={{0,4},{4,0},{8,12},{12,8},{1,5},{5,1},{9,13},{13,9},{2,6},{6,2},{1... | collective-permute-start | bytes 1253384 | tf_op jit(solution)/shard_map/ppermute | solution.py:353
  15.5 11.0 %collective-permute-start.2 = (bf16[256,768]{1,0:T(8,128)(2,1)S(1)}, bf16[256,768]{1,0:T(8,128)(2,1)}, u32[]{:S(2)}, u32[]{:S(2)}) collective-permute-start(bf16[256,768]{1,0:T(8,128)(2,1)S(1)} %pad_maximum_fusion.2), channel_id=1, source_target_pairs={{0,2},{1,3},{2,0},{3,1},{4,6},{5,7},{6,4},{7,5},{8,10},{9,11},{10,... | collective-permute-start | bytes 1179656 | tf_op jit(solution)/shard_map/ppermute | solution.py:350
  17.0 33.2 %collective-permute-start.7 = (bf16[272,768]{1,0:T(8,128)(2,1)S(1)}, bf16[272,768]{1,0:T(8,128)(2,1)S(1)}, u32[]{:S(2)}, u32[]{:S(2)}) collective-permute-start(bf16[272,768]{1,0:T(8,128)(2,1)S(1)} %pad_maximum_fusion.mine), channel_id=1, source_target_pairs={{0,0},{4,8},{8,4},{12,12},{1,1},{5,9},{9,5},{13,13},{2,2},{6,10},{... | collective-permute-start | bytes 1253384 | tf_op jit(solution)/shard_map/ppermute | solution.py:353
  26.5 10.2 %collective-permute-start.6 = (bf16[256,768]{1,0:T(8,128)(2,1)}, bf16[256,768]{1,0:T(8,128)(2,1)S(1)}, u32[]{:S(2)}, u32[]{:S(2)}) collective-permute-start(bf16[256,768]{1,0:T(8,128)(2,1)} %collective-permute-done.2.other), channel_id=1, source_target_pairs={{0,4},{4,0},{8,12},{12,8},{1,5},{5,1},{9,13},{13,9},{2,6},{6,2},{1... | collective-permute-start | bytes 1179656 | tf_op jit(solution)/shard_map/ppermute | solution.py:353
  26.8 24.3 %collective-permute-start.8 = (bf16[256,768]{1,0:T(8,128)(2,1)}, bf16[256,768]{1,0:T(8,128)(2,1)}, u32[]{:S(2)}, u32[]{:S(2)}) collective-permute-start(bf16[256,768]{1,0:T(8,128)(2,1)} %collective-permute-done.2.other), channel_id=1, source_target_pairs={{0,0},{4,8},{8,4},{12,12},{1,1},{5,9},{9,5},{13,13},{2,2},{6,10},{... | collective-permute-start | bytes 1179656 | tf_op jit(solution)/shard_map/ppermute | solution.py:353
  32.6 1.8 %copy-start.6 = (bf16[128,256]{1,0:T(8,128)(2,1)S(1)}, bf16[128,256]{1,0:T(8,128)(2,1)}, u32[]{:S(2)}) copy-start(bf16[128,256]{1,0:T(8,128)(2,1)} %get-tuple-element.63) | copy-start | bytes 196612
  32.6 1.8 %copy-start.7 = (bf16[128,256]{1,0:T(8,128)(2,1)S(1)}, bf16[128,256]{1,0:T(8,128)(2,1)}, u32[]{:S(2)}) copy-start(bf16[128,256]{1,0:T(8,128)(2,1)} %get-tuple-element.62) | copy-start | bytes 196612
  32.6 9.3 %collective-permute-start.3 = (bf16[256,640]{1,0:T(8,128)(2,1)S(1)}, bf16[256,640]{1,0:T(8,128)(2,1)S(1)}, u32[]{:S(2)}, u32[]{:S(2)}) collective-permute-start(bf16[256,640]{1,0:T(8,128)(2,1)S(1)} %pad_maximum_fusion.5), channel_id=1, source_target_pairs={{0,2},{1,3},{2,0},{3,1},{4,6},{5,7},{6,4},{7,5},{8,10},{9,11},{10,... | collective-permute-start | bytes 983048 | tf_op jit(solution)/shard_map/ppermute | solution.py:350
  37.4 13.6 %collective-permute-start.9 = (bf16[256,768]{1,0:T(8,128)(2,1)}, bf16[256,768]{1,0:T(8,128)(2,1)}, u32[]{:S(2)}, u32[]{:S(2)}) collective-permute-start(bf16[256,768]{1,0:T(8,128)(2,1)} %slice_select_fusion), channel_id=1, source_target_pairs={{0,0},{4,8},{8,4},{12,12},{1,1},{5,9},{9,5},{13,13},{2,2},{6,10},{... | collective-permute-start | bytes 1179656 | tf_op jit(solution)/shard_map/ppermute | solution.py:353
  41.9 6.5 %collective-permute-start.14 = (bf16[256,512]{1,0:T(8,128)(2,1)S(1)}, bf16[256,512]{1,0:T(8,128)(2,1)}, u32[]{:S(2)}, u32[]{:S(2)}) collective-permute-start(bf16[256,512]{1,0:T(8,128)(2,1)S(1)} %pad_maximum_fusion.6), channel_id=1, source_target_pairs={{0,2},{1,3},{2,0},{3,1},{4,6},{5,7},{6,4},{7,5},{8,10},{9,11},{10,... | collective-permute-start | bytes 786440 | tf_op jit(solution)/shard_map/ppermute | solution.py:350
  43.4 1.5 %copy-start.5 = (bf16[128,256]{1,0:T(8,128)(2,1)S(1)}, bf16[128,256]{1,0:T(8,128)(2,1)}, u32[]{:S(2)}) copy-start(bf16[128,256]{1,0:T(8,128)(2,1)} %get-tuple-element.60) | copy-start | bytes 196612
  44.2 12.4 %collective-permute-start.4 = (bf16[512,384]{1,0:T(8,128)(2,1)}, bf16[512,384]{1,0:T(8,128)(2,1)}, u32[]{:S(2)}, u32[]{:S(2)}) collective-permute-start(bf16[512,384]{1,0:T(8,128)(2,1)} %pad_maximum_fusion.3), channel_id=1, source_target_pairs={{0,4},{4,0},{8,12},{12,8},{1,5},{5,1},{9,13},{13,9},{2,6},{6,2},{1... | collective-permute-start | bytes 1179656 | tf_op jit(solution)/shard_map/ppermute | solution.py:353
  49.6 14.8 %collective-permute-start.15 = (bf16[512,512]{1,0:T(8,128)(2,1)S(1)}, bf16[512,512]{1,0:T(8,128)(2,1)S(1)}, u32[]{:S(2)}, u32[]{:S(2)}) collective-permute-start(bf16[512,512]{1,0:T(8,128)(2,1)S(1)} %maximum_select_fusion.whole), channel_id=1, source_target_pairs={{0,4},{4,0},{8,12},{12,8},{1,5},{5,1},{9,13},{13,9},{2,6},{6,2},{1... | collective-permute-start | bytes 1572872 | tf_op jit(solution)/shard_map/ppermute | solution.py:353
  50.3 0.8 copy-start
  56.6 1.0 copy-start.1
  59.7 17.6 %collective-permute-start.10 = (bf16[512,384]{1,0:T(8,128)(2,1)}, bf16[512,384]{1,0:T(8,128)(2,1)S(1)}, u32[]{:S(2)}, u32[]{:S(2)}) collective-permute-start(bf16[512,384]{1,0:T(8,128)(2,1)} %get-tuple-element.55), channel_id=1, source_target_pairs={{4,0},{8,12},{5,1},{9,13},{6,2},{10,14},{7,3},{11,15},{20,16},{24,... | collective-permute-start | bytes 1179656 | tf_op jit(solution)/shard_map/ppermute | solution.py:353
  61.0 16.6 %collective-permute-start.16 = (bf16[512,512]{1,0:T(8,128)(2,1)S(1)}, bf16[512,512]{1,0:T(8,128)(2,1)S(1)}, u32[]{:S(2)}, u32[]{:S(2)}) collective-permute-start(bf16[512,512]{1,0:T(8,128)(2,1)S(1)} %maximum_select_fusion.whole), channel_id=1, source_target_pairs={{0,0},{4,8},{8,4},{12,12},{1,1},{5,9},{9,5},{13,13},{2,2},{6,10},{... | collective-permute-start | bytes 1572872 | tf_op jit(solution)/shard_map/ppermute | solution.py:353
  64.4 19.3 %collective-permute-start.17 = (bf16[256,512]{1,0:T(8,128)(2,1)S(1)}, bf16[256,512]{1,0:T(8,128)(2,1)S(1)}, u32[]{:S(2)}, u32[]{:S(2)}) collective-permute-start(bf16[256,512]{1,0:T(8,128)(2,1)S(1)} %slice.99), channel_id=1, source_target_pairs={{0,0},{4,8},{8,4},{12,12},{1,1},{5,9},{9,5},{13,13},{2,2},{6,10},{... | collective-permute-start | bytes 786440 | tf_op jit(solution)/shard_map/ppermute | solution.py:353
  77.5 8.4 %collective-permute-start.11 = (bf16[128,384]{1,0:T(8,128)(2,1)S(1)}, bf16[128,384]{1,0:T(8,128)(2,1)S(1)}, u32[]{:S(2)}, u32[]{:S(2)}) collective-permute-start(bf16[128,384]{1,0:T(8,128)(2,1)S(1)} %get-tuple-element.95), channel_id=1, source_target_pairs={{0,1},{1,0},{2,3},{3,2},{4,5},{5,4},{6,7},{7,6},{8,9},{9,8},{10,11... | collective-permute-start | bytes 294920 | tf_op jit(solution)/shard_map/ppermute | solution.py:350
  77.7 11.2 %collective-permute-start.18 = (bf16[256,512]{1,0:T(8,128)(2,1)S(1)}, bf16[256,512]{1,0:T(8,128)(2,1)S(1)}, u32[]{:S(2)}, u32[]{:S(2)}) collective-permute-start(bf16[256,512]{1,0:T(8,128)(2,1)S(1)} %slice.100), channel_id=1, source_target_pairs={{0,4},{4,0},{8,12},{12,8},{1,5},{5,1},{9,13},{13,9},{2,6},{6,2},{1... | collective-permute-start | bytes 786440 | tf_op jit(solution)/shard_map/ppermute | solution.py:353
  83.2 5.6 %collective-permute-start.12 = (bf16[128,384]{1,0:T(8,128)(2,1)S(1)}, bf16[128,384]{1,0:T(8,128)(2,1)S(1)}, u32[]{:S(2)}, u32[]{:S(2)}) collective-permute-start(bf16[128,384]{1,0:T(8,128)(2,1)S(1)} %get-tuple-element.94), channel_id=1, source_target_pairs={{0,2},{1,3},{2,0},{3,1},{4,6},{5,7},{6,4},{7,5},{8,10},{9,11},{10,... | collective-permute-start | bytes 294920 | tf_op jit(solution)/shard_map/ppermute | solution.py:350
  83.7 5.1 %collective-permute-start.13 = (bf16[128,384]{1,0:T(8,128)(2,1)S(1)}, bf16[128,384]{1,0:T(8,128)(2,1)S(1)}, u32[]{:S(2)}, u32[]{:S(2)}) collective-permute-start(bf16[128,384]{1,0:T(8,128)(2,1)S(1)} %get-tuple-element.93), channel_id=1, source_target_pairs={{0,3},{1,2},{2,1},{3,0},{4,7},{5,6},{6,5},{7,4},{8,11},{9,10},{10,... | collective-permute-start | bytes 294920 | tf_op jit(solution)/shard_map/ppermute | solution.py:350
  83.7 9.0 %collective-permute-start.19 = (bf16[256,512]{1,0:T(8,128)(2,1)S(1)}, bf16[256,512]{1,0:T(8,128)(2,1)S(1)}, u32[]{:S(2)}, u32[]{:S(2)}) collective-permute-start(bf16[256,512]{1,0:T(8,128)(2,1)S(1)} %collective-permute-done.17.r1), channel_id=1, source_target_pairs={{0,4},{4,0},{8,12},{12,8},{1,5},{5,1},{9,13},{13,9},{2,6},{6,2},{1... | collective-permute-start | bytes 786440 | tf_op jit(solution)/shard_map/ppermute | solution.py:353
  96.0 1.9 %collective-permute-start.20 = (bf16[128,256]{1,0:T(8,128)(2,1)S(1)}, bf16[128,256]{1,0:T(8,128)(2,1)S(1)}, u32[]{:S(2)}, u32[]{:S(2)}) collective-permute-start(bf16[128,256]{1,0:T(8,128)(2,1)S(1)} %get-tuple-element.66), channel_id=1, source_target_pairs={{0,1},{1,0},{2,3},{3,2},{4,5},{5,4},{6,7},{7,6},{8,9},{9,8},{10,11... | collective-permute-start | bytes 196616 | tf_op jit(solution)/shard_map/ppermute | solution.py:350
  96.3 4.4 %collective-permute-start.21 = (bf16[128,256]{1,0:T(8,128)(2,1)S(1)}, bf16[128,256]{1,0:T(8,128)(2,1)S(1)}, u32[]{:S(2)}, u32[]{:S(2)}) collective-permute-start(bf16[128,256]{1,0:T(8,128)(2,1)S(1)} %get-tuple-element.67), channel_id=1, source_target_pairs={{0,2},{1,3},{2,0},{3,1},{4,6},{5,7},{6,4},{7,5},{8,10},{9,11},{10,... | collective-permute-start | bytes 196616 | tf_op jit(solution)/shard_map/ppermute | solution.py:350
  97.5 4.2 %collective-permute-start.22 = (bf16[128,256]{1,0:T(8,128)(2,1)S(1)}, bf16[128,256]{1,0:T(8,128)(2,1)S(1)}, u32[]{:S(2)}, u32[]{:S(2)}) collective-permute-start(bf16[128,256]{1,0:T(8,128)(2,1)S(1)} %get-tuple-element.68), channel_id=1, source_target_pairs={{0,3},{1,2},{2,1},{3,0},{4,7},{5,6},{6,5},{7,4},{8,11},{9,10},{10,... | collective-permute-start | bytes 196616 | tf_op jit(solution)/shard_map/ppermute | solution.py:350
  100.8 1.0 copy-start.4

commit v4 on v3

--- a/solution.py
+++ b/solution.py
@@ -1,3 +1,4 @@
+import functools
 import math
 
 import jax
@@ -317,6 +318,69 @@
         body([whole, n1, r2, r3], [None] * 4 + [mask[0, z ^ 2] == 1, mask[0, z ^ 3] == 1])
 
 
+def pack_kernel(copies, width, mask, offset, *refs):
+    ins, outs, sems = refs[:3], refs[3:-1], refs[-1]
+    h = lax.axis_index("head")
+    started = []
+    for n, (operand, d, begin, result, at, lanes) in enumerate(copies):
+        source = ins[operand].at[:, pl.ds(pl.multiple_of((h ^ d) * width + begin, HEAD_DIM), lanes)]
+        copy = pltpu.make_async_copy(source, outs[result].at[:, at : at + lanes], sems.at[n])
+        copy.start()
+        started.append(copy)
+    if len(outs) > 1 + max(copy[3] for copy in copies):
+        told = outs[-1]
+        for group in range(told.shape[1] // 128):
+            value = mask[0, group] if group < 4 else offset[0]
+            rows = jnp.full((told.shape[0], 128), value, jnp.int32).astype(jnp.float32)
+            told[:, group * 128 : (group + 1) * 128] = rows.astype(told.dtype)
+    for copy in started:
+        copy.wait()
+
+
+def packed(operands, mask, offset, results, width, told):
+    rows = operands[0].shape[0]
+    copies, shapes = [], []
+    for n, parts in enumerate(results):
+        at = 0
+        for operand, d, begin, lanes in parts:
+            copies.append((operand, d, begin, n, at, lanes))
+            at += lanes
+        shapes.append(jax.ShapeDtypeStruct((rows, at), jnp.bfloat16))
+    if told:
+        shapes.append(jax.ShapeDtypeStruct((INFO_ROWS, told), jnp.bfloat16))
+    return pl.pallas_call(
+        functools.partial(pack_kernel, copies, width),
+        in_specs=[pl.BlockSpec(memory_space=pltpu.SMEM)] * 2 + [pl.BlockSpec(memory_space=pltpu.HBM)] * 3,
+        out_specs=[pl.BlockSpec(memory_space=pltpu.VMEM)] * len(shapes),
+        out_shape=shapes,
+        scratch_shapes=[pltpu.SemaphoreType.DMA((len(copies),))],
+        compiler_params=pltpu.CompilerParams(vmem_limit_bytes=4 * 1024 * 1024),
+    )(mask, offset, *operands)
+
+
+def relayed_kernel(mine, other, out):
+    tile = out.shape[0]
+    offset = jnp.max(mine[tile : tile + INFO_ROWS, 4 * 128 : 5 * 128].astype(jnp.float32))
+    here = offset == (lax.axis_index("head") // 2).astype(jnp.float32)
+
+    @pl.when(here)
+    def _():
+        out[...] = mine[:tile]
+
+    @pl.when(jnp.logical_not(here))
+    def _():
+        out[...] = other[...]
+
+
+def relayed(mine, other):
+    return pl.pallas_call(
+        relayed_kernel,
+        in_specs=[pl.BlockSpec(memory_space=pltpu.VMEM)] * 2,
+        out_specs=pl.BlockSpec(memory_space=pltpu.VMEM),
+        out_shape=jax.ShapeDtypeStruct(other.shape, other.dtype),
+    )(mine, other)
+
+
 def run_kernel(kernel, mask, arrays, outs, chunks, tile, heads):
     return pl.pallas_call(
         kernel,
@@ -324,7 +388,7 @@
         out_specs=[pl.BlockSpec(memory_space=pltpu.VMEM)] * len(outs),
         out_shape=[jax.ShapeDtypeStruct((rows, heads * HEAD_DIM), jnp.bfloat16) for rows in outs],
         scratch_shapes=[pltpu.VMEM((tile, 7 * tile), jnp.float32) for _ in range(chunks)],
-        compiler_params=pltpu.CompilerParams(vmem_limit_bytes=20 * 1024 * 1024),
+        compiler_params=pltpu.CompilerParams(vmem_limit_bytes=(4 + 2 * chunks) * 1024 * 1024),
         cost_estimate=pl.CostEstimate(
             flops=heads * chunks * tile * 7 * tile * HEAD_DIM * 4,
             bytes_accessed=sum(x.size * 2 for x in arrays),
@@ -346,6 +410,9 @@
     def columns(array, d, begin, end):
         return lax.dynamic_slice_in_dim(array, (h ^ d) * width + begin, end - begin, axis=1)
 
+    def beside(*arrays):
+        return jnp.concatenate(arrays, axis=1)
+
     def to_head(array, d):
         return lax.ppermute(array, "head", [(i, i ^ d) for i in range(4)])
 
@@ -355,40 +422,49 @@
     def after(array, earlier):
         return lax.optimization_barrier((array, earlier))[0]
 
-    def beside(*arrays):
-        return jnp.concatenate(arrays, axis=1)
-
     def below(*arrays):
         return jnp.concatenate(arrays, axis=0)
 
-    k = [columns(keys, d, 0, cut) for d in range(4)]
-    v = [columns(values, d, 0, cut) for d in range(4)]
-    k, v = lax.optimization_barrier((k, v))
-    got = to_head(beside(k[1], v[1], k[3], v[3]), 1)
-    told = [pair_mask[0, g] for g in range(4)] + [tile_offset[0]] + [0] * (2 * FIRST - 5)
-    told = beside(*[jnp.broadcast_to(jnp.asarray(t).astype(jnp.bfloat16), (INFO_ROWS, 128)) for t in told])
-    mine = below(beside(k[0], v[0]), got[:, : 2 * cut], told)
-    other = to_head(below(beside(k[2], v[2]), got[:, 2 * cut :]), 2)
+    operands = (queries, keys, values)
+
+    def keys_values(d, begin, end):
+        return [(1, d, begin, end - begin), (2, d, begin, end - begin)]
+
+    first = [[columns(array, d, 0, cut) for array in (keys, values)] for d in range(4)]
+    first = lax.optimization_barrier(first)
+    got = to_head(beside(*first[1], *first[3]), 1)
+    pay, q_own, q_far, own, far, told = packed(
+        operands,
+        pair_mask,
+        tile_offset,
+        [
+            [(0, 1, 0, width), (0, 3, 0, width)] + keys_values(1, cut, width) + keys_values(3, cut, width),
+            [(0, 0, 0, width)],
+            [(0, 2, 0, width)],
+            keys_values(0, cut, width),
+            keys_values(2, cut, width),
+        ],
+        width,
+        2 * cut,
+    )
+    mine = below(beside(*first[0]), got[:, : 2 * cut], told)
+    other = to_head(below(beside(*first[2]), got[:, 2 * cut :]), 2)
     n1_mine = along(mine, OUTER)
     n2_mine = along(mine, INNER)
     n1_other = along(other, OUTER)
     n2_other = along(other, INNER)
-    picked = n1_mine[tile, 4 * 128] == x.astype(jnp.bfloat16)
-    r1 = along(jnp.where(picked, n1_mine[:tile], n1_other), INNER)
+    r1 = along(after(relayed(n1_mine, n1_other), n2_mine), INNER)
     first = [mine, other, n1_mine, n1_other, n2_mine, n2_other, r1]
 
-    q = [columns(queries, d, 0, width) for d in range(4)]
-    k = [columns(keys, d, cut, width) for d in range(4)]
-    v = [columns(values, d, cut, width) for d in range(4)]
-    q, k, v = lax.optimization_barrier((q, k, v))
-    got = to_head(after(beside(q[1], q[3], k[1], v[1], k[3], v[3]), mine), 1)
-    q_mine = below(q[0], got[:, :width])
-    q_other = to_head(after(below(q[2], got[:, width : 2 * width]), other), 2)
+    got = to_head(after(pay, got), 1)
+    q_mine = below(q_own, got[:, :width])
+    q_other = to_head(after(below(q_far, got[:, width : 2 * width]), other), 2)
     split = 2 * width + 2 * (width - cut)
-    mine2 = below(beside(k[0], v[0]), got[:, 2 * width : split])
-    other2 = to_head(after(below(beside(k[2], v[2]), got[:, split:]), q_other), 2)
+    mine2 = below(own, got[:, 2 * width : split])
+    other2 = to_head(after(below(far, got[:, split:]), q_other), 2)
     q_guest = along(below(q_mine[:, :cut], q_other[:, :cut]), OUTER)
     whole = jnp.where(x == tile_offset[0], below(mine2, other2), below(other2, mine2))
+    whole = after(whole, n2_other)
     n1 = along(whole, OUTER)
     n2 = along(whole, INNER)
     r1 = along(n1[:tile], INNER)
@@ -398,7 +474,7 @@
     *own, guest = run_kernel(
         first_kernel, pair_mask, [q_mine, q_other, q_guest, *first], [rows] * 4 + [2 * tile], 4, tile, FIRST
     )
-    back = along(guest, OUTWARD)
+    back = along(after(guest, n2), OUTWARD)
     end_frame = (z == 0) | (z == 3)
     out = [jnp.where(end_frame, back[d * rows : (d + 1) * rows], own[d]) for d in range(4)]
     out = [out[0]] + [to_head(out[d], d) for d in (1, 2, 3)]

time: 103 us -> 98.7 us (0.958)
  local copies, waits for them, and re-layouts: 14.2 us -> 9.13 us
  Pallas kernels: 5.42 us -> 8.36 us
  waiting for transfers between devices: 45.4 us -> 42.6 us
  starting transfers between devices: 32.6 us -> 34.6 us
    unnamed x27 -> x20, local copies, waits for them, and re-layouts: 8.22 us -> 2.36 us
    ppermute x12, waiting for transfers between devices: 26.5 us -> 23.4 us  [along(): return lax.ppermute(array, 'frame', pairs)]
    pallas_call x0 -> x2, Pallas kernels: none -> 2.85 us  [the longest x1 2.03 us: relayed(): pl.pallas_call(relayed_kernel, in_specs=[pl.BlockSpec(memory_space=pltpu....]
    ppermute x11, starting transfers between devices: 7.96 us -> 9.94 us  [to_head(): return lax.ppermute(array, 'head', [(i, i ^ d) for i in range(4)])]
    dynamic_update_slice x3, local copies, waits for them, and re-layouts: 0.06 us -> 1.95 us  [four_frames(): lax.dynamic_update_slice_in_dim(result, out[d], (h ^ d) * width, axis=1)]
    dynamic_update_slice x4, local copies, waits for them, and re-layouts: 0.66 us -> 2.54 us  [four_frames(): lax.dynamic_update_slice_in_dim(result, late[d], (h ^ d) * width + cut, a...]
    dynamic_slice x3 -> x1, local copies, waits for them, and re-layouts: 3.17 us -> 1.4 us  [columns(): lax.dynamic_slice_in_dim(array, (h ^ d) * width + begin, end - begin, axi...]
    slice x5 -> x3, local copies, waits for them, and re-layouts: 1.31 us -> 0.07 us  [the longest x1 0.03 us: four_frames(): q_other = to_head(after(below(q_far, got[:, width:2 * width]), other), 2)]
  transfers between devices with their start and end apart: 23 -> 23, of which waited for: 10 -> 9; matrix products, arithmetic and copies ran while one was open for 13% -> 7% of each run, Pallas kernels for 2% -> 5%
where the time goes in v4:
time: 98.7 us; the launch traced here: 97.9 us
  waiting for transfers between devices  42.6 us (43%)
  starting transfers between devices  34.6 us (35%)
  local copies, waits for them, and re-layouts  9.13 us (9%)
  Pallas kernels  8.36 us (8%)
  other arithmetic  2.31 us (2%)
    ppermute x12, starting transfers between devices, along(): return lax.ppermute(array, 'frame', pairs)  24.7 us
    ppermute x12, waiting for transfers between devices, along(): return lax.ppermute(array, 'frame', pairs)  23.4 us
    ppermute x11, waiting for transfers between devices, to_head(): return lax.ppermute(array, 'head', [(i, i ^ d) for i in range(4)])  19.2 us
    ppermute x11, starting transfers between devices, to_head(): return lax.ppermute(array, 'head', [(i, i ^ d) for i in range(4)])  9.94 us
    pallas_call x2, Pallas kernels, run_kernel(): pl.pallas_call(kernel, in_specs=[pl.BlockSpec(memory_space=pltpu.SMEM)] +...  5.51 us
    dynamic_update_slice x4, local copies, waits for them, and re-layouts, four_frames(): lax.dynamic_update_slice_in_dim(result, late[d], (h ^ d) * width + cut, a...  2.54 us
    unnamed x20, local copies, waits for them, and re-layouts  2.36 us
    pallas_call x1, Pallas kernels, relayed(): pl.pallas_call(relayed_kernel, in_specs=[pl.BlockSpec(memory_space=pltpu....  2.03 us
  transfers between devices with their start and end apart: 23, of which 9 were waited for; matrix products, arithmetic and copies ran while one was open for 7% of the time, Pallas kernels for 5%

profile of v4, /device:TPU:0, one launch (start us, length us, event | category | flops | bytes accessed | tf_op | source)
XLA Modules:
  0.0 97.9 jit_solution(11873753320621466181)
XLA Ops:
  0.0 1.4 %constant_dynamic-slice_fusion = (bf16[128,384]{1,0:T(8,128)(2,1)S(1)}, bf16[128,384]{1,0:T(8,128)(2,1)S(1)}, bf16[128,384]{1,0:T(8,128)(2,1)S(1)}, bf16[128,384...) fusion(bf16[128,2560]{1,0:T(8,128)(2,1)} %refs_2_.1, ...), kind=kLoop, calls=%fused_computation.23 | loop fusion | bytes 1572880 | tf_op jit(solution)/shard_map/dynamic_slice | solution.py:411
  1.5 0.5 collective-permute-start
  2.7 0.8 shard_map.55
  3.5 0.4 collective-permute-start.1
  4.0 2.7 %collective-permute-start.2 = (bf16[256,768]{1,0:T(8,128)(2,1)S(1)}, bf16[256,768]{1,0:T(8,128)(2,1)}, u32[]{:S(2)}, u32[]{:S(2)}) collective-permute-start(bf16[256,768]{1,0:T(8,128)(2,1)S(1)} %pad_maximum_fusion.2), channel_id=1, source_target_pairs={{0,2},{1,3},{2,0},{3,1},{4,6},{5,7},{6,4},{7,5},{8,10},{9,11},{10,... | collective-permute-start | bytes 1179656 | tf_op jit(solution)/shard_map/ppermute | solution.py:417
  6.8 1.6 %collective-permute-start.5 = (bf16[272,768]{1,0:T(8,128)(2,1)S(1)}, bf16[272,768]{1,0:T(8,128)(2,1)S(1)}, u32[]{:S(2)}, u32[]{:S(2)}) collective-permute-start(bf16[272,768]{1,0:T(8,128)(2,1)S(1)} %pad_maximum_fusion.mine), channel_id=1, source_target_pairs={{0,4},{4,0},{8,12},{12,8},{1,5},{5,1},{9,13},{13,9},{2,6},{6,2},{1... | collective-permute-start | bytes 1253384 | tf_op jit(solution)/shard_map/ppermute | solution.py:420
  8.4 1.4 %collective-permute-start.7 = (bf16[272,768]{1,0:T(8,128)(2,1)S(1)}, bf16[272,768]{1,0:T(8,128)(2,1)}, u32[]{:S(2)}, u32[]{:S(2)}) collective-permute-start(bf16[272,768]{1,0:T(8,128)(2,1)S(1)} %pad_maximum_fusion.mine), channel_id=1, source_target_pairs={{0,0},{4,8},{8,4},{12,12},{1,1},{5,9},{9,5},{13,13},{2,2},{6,10},{... | collective-permute-start | bytes 1253384 | tf_op jit(solution)/shard_map/ppermute | solution.py:420
  9.8 6.6 %collective-permute-done.2.other = bf16[256,768]{1,0:T(8,128)(2,1)} collective-permute-done((bf16[256,768]{1,0:T(8,128)(2,1)S(1)}, bf16[256,768]{1,0:T(8,128)(2,1)}, u32[]{:S(2)}, u32[]{:S(2)}) %collective-permute-start.2) | collective-permute-done | bytes 393248 | tf_op jit(solution)/shard_map/ppermute | solution.py:417
  16.4 4.5 %collective-permute-start.8 = (bf16[256,768]{1,0:T(8,128)(2,1)}, bf16[256,768]{1,0:T(8,128)(2,1)}, u32[]{:S(2)}, u32[]{:S(2)}) collective-permute-start(bf16[256,768]{1,0:T(8,128)(2,1)} %collective-permute-done.2.other), channel_id=1, source_target_pairs={{0,0},{4,8},{8,4},{12,12},{1,1},{5,9},{9,5},{13,13},{2,2},{6,10},{... | collective-permute-start | bytes 1179656 | tf_op jit(solution)/shard_map/ppermute | solution.py:420
  20.9 0.9 collective-permute-start.6
  21.9 1.6 %collective-permute-start.3 = (bf16[256,640]{1,0:T(8,128)(2,1)S(1)}, bf16[256,640]{1,0:T(8,128)(2,1)S(1)}, u32[]{:S(2)}, u32[]{:S(2)}) collective-permute-start(bf16[256,640]{1,0:T(8,128)(2,1)S(1)} %pad_maximum_fusion.5), channel_id=1, source_target_pairs={{0,2},{1,3},{2,0},{3,1},{4,6},{5,7},{6,4},{7,5},{8,10},{9,11},{10,... | collective-permute-start | bytes 983048 | tf_op jit(solution)/shard_map/ppermute | solution.py:417
  23.5 7.0 %collective-permute-done.3.q_other = bf16[256,640]{1,0:T(8,128)(2,1)S(1)} collective-permute-done((bf16[256,640]{1,0:T(8,128)(2,1)S(1)}, bf16[256,640]{1,0:T(8,128)(2,1)S(1)}, u32[]{:S(2)}, u32[]{:S(2)}) %collective-permute-start.3) | collective-permute-done | bytes 327712 | tf_op jit(solution)/shard_map/ppermute | solution.py:417
  30.5 1.5 %collective-permute-start.10 = (bf16[256,512]{1,0:T(8,128)(2,1)S(1)}, bf16[256,512]{1,0:T(8,128)(2,1)}, u32[]{:S(2)}, u32[]{:S(2)}) collective-permute-start(bf16[256,512]{1,0:T(8,128)(2,1)S(1)} %pad_maximum_fusion.6), channel_id=1, source_target_pairs={{0,2},{1,3},{2,0},{3,1},{4,6},{5,7},{6,4},{7,5},{8,10},{9,11},{10,... | collective-permute-start | bytes 786440 | tf_op jit(solution)/shard_map/ppermute | solution.py:417
  32.1 0.7 copy-done.3
  32.8 0.7 copy-done.5
  33.5 2.0 %shard_map.56 = bf16[256,768]{1,0:T(8,128)(2,1)} custom-call(bf16[272,768]{1,0:T(8,128)(2,1)} %copy-done.3, bf16[256,768]{1,0:T(8,128)(2,1)} %copy-done.5), custom_call_target="tpu_custom_call" | custom-call | tf_op jit(solution)/shard_map/pallas_call | solution.py:376
  35.6 4.5 %collective-permute-start.9 = (bf16[256,768]{1,0:T(8,128)(2,1)}, bf16[256,768]{1,0:T(8,128)(2,1)}, u32[]{:S(2)}, u32[]{:S(2)}) collective-permute-start(bf16[256,768]{1,0:T(8,128)(2,1)} %shard_map.56), channel_id=1, source_target_pairs={{0,0},{4,8},{8,4},{12,12},{1,1},{5,9},{9,5},{13,13},{2,2},{6,10},{... | collective-permute-start | bytes 1179656 | tf_op jit(solution)/shard_map/ppermute | solution.py:420
  40.1 1.9 %collective-permute-start.4 = (bf16[512,384]{1,0:T(8,128)(2,1)S(1)}, bf16[512,384]{1,0:T(8,128)(2,1)}, u32[]{:S(2)}, u32[]{:S(2)}) collective-permute-start(bf16[512,384]{1,0:T(8,128)(2,1)S(1)} %pad_maximum_fusion.3), channel_id=1, source_target_pairs={{0,4},{4,0},{8,12},{12,8},{1,5},{5,1},{9,13},{13,9},{2,6},{6,2},{1... | collective-permute-start | bytes 1179656 | tf_op jit(solution)/shard_map/ppermute | solution.py:420
  42.0 1.2 %maximum_select_fusion.whole = bf16[512,512]{1,0:T(8,128)(2,1)S(1)} fusion(bf16[256,512]{1,0:T(8,128)(2,1)} %collective-permute-done.10, bf16[128,512]{1,0:T(8,128)(2,1)S(1)} %get-tuple-element.71, bf16[128,512]{1,0:T(8,128)(2,1)S(1)} %get-tuple-element.50, pred[]{:T(512)S(6)} %eq.11), kind=kLoop, calls=%fused_computation | loop fusion | flops 3407872 | bytes 1048577 | tf_op jit(solution)/shard_map/jit(_where)/select_n | solution.py:466
  43.3 0.8 collective-permute-start.11
  44.1 4.1 %collective-permute-start.16 = (bf16[512,512]{1,0:T(8,128)(2,1)S(1)}, bf16[512,512]{1,0:T(8,128)(2,1)S(1)}, u32[]{:S(2)}, u32[]{:S(2)}) collective-permute-start(bf16[512,512]{1,0:T(8,128)(2,1)S(1)} %maximum_select_fusion.whole), channel_id=1, source_target_pairs={{0,4},{4,0},{8,12},{12,8},{1,5},{5,1},{9,13},{13,9},{2,6},{6,2},{1... | collective-permute-start | bytes 1572872 | tf_op jit(solution)/shard_map/ppermute | solution.py:420
  48.3 3.6 %collective-permute-done.4.q_guest = bf16[512,384]{1,0:T(8,128)(2,1)} collective-permute-done((bf16[512,384]{1,0:T(8,128)(2,1)S(1)}, bf16[512,384]{1,0:T(8,128)(2,1)}, u32[]{:S(2)}, u32[]{:S(2)}) %collective-permute-start.4) | collective-permute-done | bytes 393248 | tf_op jit(solution)/shard_map/ppermute | solution.py:420
  51.9 2.3 %shard_map.57 = (bf16[128,384]{1,0:T(8,128)(2,1)S(1)}, bf16[128,384]{1,0:T(8,128)(2,1)S(1)}, bf16[128,384]{1,0:T(8,128)(2,1)S(1)}, bf16[128,384]{1,0:T(8,128)(2,1)S(1)}, bf16[512,384]{1,0:T(8,128)(2,1)}) custom-call(s32[1,4]{1,0:T(1,128)S(1)} %copy-done.7, bf16[256,640]{1,0:T(8,128)(2,1)S(1)} %pad_maximum_fusion.4.q_mine, ...), custom_call_target="tpu_custom_call" | custom-call | flops 2818572288 | bytes 3874816 | tf_op jit(solution)/shard_map/pallas_call | solution.py:385
  54.1 1.3 %collective-permute-start.12 = (bf16[512,384]{1,0:T(8,128)(2,1)}, bf16[512,384]{1,0:T(8,128)(2,1)S(1)}, u32[]{:S(2)}, u32[]{:S(2)}) collective-permute-start(bf16[512,384]{1,0:T(8,128)(2,1)} %get-tuple-element.54), channel_id=1, source_target_pairs={{4,0},{8,12},{5,1},{9,13},{6,2},{10,14},{7,3},{11,15},{20,16},{24,... | collective-permute-start | bytes 1179656 | tf_op jit(solution)/shard_map/ppermute | solution.py:420
  55.4 5.2 %collective-permute-done.16.n1 = bf16[512,512]{1,0:T(8,128)(2,1)S(1)} collective-permute-done((bf16[512,512]{1,0:T(8,128)(2,1)S(1)}, bf16[512,512]{1,0:T(8,128)(2,1)S(1)}, u32[]{:S(2)}, u32[]{:S(2)}) %collective-permute-start.16) | collective-permute-done | bytes 524320 | tf_op jit(solution)/shard_map/ppermute | solution.py:420
  60.6 0.7 slice.69
  61.3 1.6 %collective-permute-start.17 = (bf16[256,512]{1,0:T(8,128)(2,1)}, bf16[256,512]{1,0:T(8,128)(2,1)S(1)}, u32[]{:S(2)}, u32[]{:S(2)}) collective-permute-start(bf16[256,512]{1,0:T(8,128)(2,1)} %slice.69), channel_id=1, source_target_pairs={{0,0},{4,8},{8,4},{12,12},{1,1},{5,9},{9,5},{13,13},{2,2},{6,10},{... | collective-permute-start | bytes 786440 | tf_op jit(solution)/shard_map/ppermute | solution.py:420
  62.9 9.3 %collective-permute-done.12 = bf16[512,384]{1,0:T(8,128)(2,1)S(1)} collective-permute-done((bf16[512,384]{1,0:T(8,128)(2,1)}, bf16[512,384]{1,0:T(8,128)(2,1)S(1)}, u32[]{:S(2)}, u32[]{:S(2)}) %collective-permute-start.12) | collective-permute-done | bytes 393248 | tf_op jit(solution)/shard_map/ppermute | solution.py:420
  72.3 0.8 slice_select_fusion
  73.1 0.8 copy-done.8
  74.0 2.0 %collective-permute-start.19 = (bf16[256,512]{1,0:T(8,128)(2,1)S(1)}, bf16[256,512]{1,0:T(8,128)(2,1)S(1)}, u32[]{:S(2)}, u32[]{:S(2)}) collective-permute-start(bf16[256,512]{1,0:T(8,128)(2,1)S(1)} %collective-permute-done.17.r1), channel_id=1, source_target_pairs={{0,4},{4,0},{8,12},{12,8},{1,5},{5,1},{9,13},{13,9},{2,6},{6,2},{1... | collective-permute-start | bytes 786440 | tf_op jit(solution)/shard_map/ppermute | solution.py:420
  76.0 0.3 collective-permute-start.14
  76.4 1.0 %collective-permute-start.15 = (bf16[128,384]{1,0:T(8,128)(2,1)S(1)}, bf16[128,384]{1,0:T(8,128)(2,1)S(1)}, u32[]{:S(2)}, u32[]{:S(2)}) collective-permute-start(bf16[128,384]{1,0:T(8,128)(2,1)S(1)} %get-tuple-element.75), channel_id=1, source_target_pairs={{0,3},{1,2},{2,1},{3,0},{4,7},{5,6},{6,5},{7,4},{8,11},{9,10},{10,... | collective-permute-start | bytes 294920 | tf_op jit(solution)/shard_map/ppermute | solution.py:417
  77.4 0.7 constant_dynamic-update-slice_fusion.6
  78.0 3.7 %collective-permute-done.14 = bf16[128,384]{1,0:T(8,128)(2,1)S(1)} collective-permute-done((bf16[128,384]{1,0:T(8,128)(2,1)S(1)}, bf16[128,384]{1,0:T(8,128)(2,1)S(1)}, u32[]{:S(2)}, u32[]{:S(2)}) %collective-permute-start.14) | collective-permute-done | bytes 98336 | tf_op jit(solution)/shard_map/ppermute | solution.py:417
  81.7 0.7 constant_dynamic-update-slice_fusion.5
  82.4 0.7 constant_dynamic-update-slice_fusion.4
  83.0 0.1 collective-permute-done.18.r2
  83.1 5.2 %collective-permute-done.19.r3 = bf16[256,512]{1,0:T(8,128)(2,1)S(1)} collective-permute-done((bf16[256,512]{1,0:T(8,128)(2,1)S(1)}, bf16[256,512]{1,0:T(8,128)(2,1)S(1)}, u32[]{:S(2)}, u32[]{:S(2)}) %collective-permute-start.19) | collective-permute-done | bytes 262176 | tf_op jit(solution)/shard_map/ppermute | solution.py:420
  88.4 3.3 %shard_map.58 = (bf16[128,256]{1,0:T(8,128)(2,1)S(1)}, bf16[128,256]{1,0:T(8,128)(2,1)S(1)}, bf16[128,256]{1,0:T(8,128)(2,1)S(1)}, bf16[128,256]{1,0:T(8,128)(2,1)S(1)}) custom-call(s32[1,4]{1,0:T(1,128)S(1)} %copy-done.7, bf16[256,640]{1,0:T(8,128)(2,1)S(1)} %pad_maximum_fusion.4.q_mine, bf16[256,640]{1,0:T(8,128)(2,1)S(1)} %collective-permute-done.3.q_other, ...), custom_call_target="tpu_custom_call" | custom-call | flops 939524096 | bytes 3014656 | tf_op jit(solution)/shard_map/pallas_call | solution.py:385
  91.6 0.1 collective-permute-start.20
  91.7 0.4 collective-permute-start.21
  92.1 1.5 %collective-permute-start.22 = (bf16[128,256]{1,0:T(8,128)(2,1)S(1)}, bf16[128,256]{1,0:T(8,128)(2,1)S(1)}, u32[]{:S(2)}, u32[]{:S(2)}) collective-permute-start(bf16[128,256]{1,0:T(8,128)(2,1)S(1)} %get-tuple-element.62), channel_id=1, source_target_pairs={{0,3},{1,2},{2,1},{3,0},{4,7},{5,6},{6,5},{7,4},{8,11},{9,10},{10,... | collective-permute-start | bytes 196616 | tf_op jit(solution)/shard_map/ppermute | solution.py:417
  93.6 0.6 constant_dynamic-update-slice_fusion.3
  94.2 0.6 constant_dynamic-update-slice_fusion.2
  94.8 1.8 %collective-permute-done.21 = bf16[128,256]{1,0:T(8,128)(2,1)S(1)} collective-permute-done((bf16[128,256]{1,0:T(8,128)(2,1)S(1)}, bf16[128,256]{1,0:T(8,128)(2,1)S(1)}, u32[]{:S(2)}, u32[]{:S(2)}) %collective-permute-start.21) | collective-permute-done | bytes 65568 | tf_op jit(solution)/shard_map/ppermute | solution.py:417
  96.7 0.6 constant_dynamic-update-slice_fusion.1
  97.3 0.6 constant_dynamic-update-slice_fusion
  (47 shorter events, 0.6 us)
Async XLA Ops:
  0.0 2.6 %copy-start.1 = (bf16[128,2560]{1,0:T(8,128)(2,1)S(1)}, bf16[128,2560]{1,0:T(8,128)(2,1)}, u32[]{:S(2)}) copy-start(bf16[128,2560]{1,0:T(8,128)(2,1)} %refs_2_.1) | copy-start | bytes 1966084
  0.0 2.7 %copy-start.2 = (bf16[128,2560]{1,0:T(8,128)(2,1)S(1)}, bf16[128,2560]{1,0:T(8,128)(2,1)}, u32[]{:S(2)}) copy-start(bf16[128,2560]{1,0:T(8,128)(2,1)} %refs_0_.1) | copy-start | bytes 1966084
  1.4 1.3 %copy-start = (bf16[128,2560]{1,0:T(8,128)(2,1)S(1)}, bf16[128,2560]{1,0:T(8,128)(2,1)}, u32[]{:S(2)}) copy-start(bf16[128,2560]{1,0:T(8,128)(2,1)} %refs_1_.1) | copy-start | bytes 1966084
  1.5 1.2 %copy-start.7 = (s32[1,4]{1,0:T(1,128)S(1)}, s32[1,4]{1,0:T(1,128)}, u32[]{:S(2)}) copy-start(s32[1,4]{1,0:T(1,128)} %mask.5) | copy-start | bytes 52
  1.5 2.0 %collective-permute-start = (bf16[128,1536]{1,0:T(8,128)(2,1)S(1)}, bf16[128,1536]{1,0:T(8,128)(2,1)S(1)}, u32[]{:S(2)}, u32[]{:S(2)}) collective-permute-start(bf16[128,1536]{1,0:T(8,128)(2,1)S(1)} %pad_maximum_fusion.1), channel_id=1, source_target_pairs={{0,1},{1,0},{2,3},{3,2},{4,5},{5,4},{6,7},{7,6},{8,9},{9,8},{10,11... | collective-permute-start | bytes 1179656 | tf_op jit(solution)/shard_map/ppermute | solution.py:417
  3.5 18.3 %collective-permute-start.1 = (bf16[128,2304]{1,0:T(8,128)(2,1)S(1)}, bf16[128,2304]{1,0:T(8,128)(2,1)S(1)}, u32[]{:S(2)}, u32[]{:S(2)}) collective-permute-start(bf16[128,2304]{1,0:T(8,128)(2,1)S(1)} %get-tuple-element.40), channel_id=1, source_target_pairs={{0,1},{1,0},{2,3},{3,2},{4,5},{5,4},{6,7},{7,6},{8,9},{9,8},{10,11... | collective-permute-start | bytes 1769480 | tf_op jit(solution)/shard_map/ppermute | solution.py:417
  4.0 12.4 %collective-permute-start.2 = (bf16[256,768]{1,0:T(8,128)(2,1)S(1)}, bf16[256,768]{1,0:T(8,128)(2,1)}, u32[]{:S(2)}, u32[]{:S(2)}) collective-permute-start(bf16[256,768]{1,0:T(8,128)(2,1)S(1)} %pad_maximum_fusion.2), channel_id=1, source_target_pairs={{0,2},{1,3},{2,0},{3,1},{4,6},{5,7},{6,4},{7,5},{8,10},{9,11},{10,... | collective-permute-start | bytes 1179656 | tf_op jit(solution)/shard_map/ppermute | solution.py:417
  6.8 25.3 %collective-permute-start.5 = (bf16[272,768]{1,0:T(8,128)(2,1)S(1)}, bf16[272,768]{1,0:T(8,128)(2,1)S(1)}, u32[]{:S(2)}, u32[]{:S(2)}) collective-permute-start(bf16[272,768]{1,0:T(8,128)(2,1)S(1)} %pad_maximum_fusion.mine), channel_id=1, source_target_pairs={{0,4},{4,0},{8,12},{12,8},{1,5},{5,1},{9,13},{13,9},{2,6},{6,2},{1... | collective-permute-start | bytes 1253384 | tf_op jit(solution)/shard_map/ppermute | solution.py:420
  8.4 27.2 %collective-permute-start.7 = (bf16[272,768]{1,0:T(8,128)(2,1)S(1)}, bf16[272,768]{1,0:T(8,128)(2,1)}, u32[]{:S(2)}, u32[]{:S(2)}) collective-permute-start(bf16[272,768]{1,0:T(8,128)(2,1)S(1)} %pad_maximum_fusion.mine), channel_id=1, source_target_pairs={{0,0},{4,8},{8,4},{12,12},{1,1},{5,9},{9,5},{13,13},{2,2},{6,10},{... | collective-permute-start | bytes 1253384 | tf_op jit(solution)/shard_map/ppermute | solution.py:420
  16.4 26.8 %collective-permute-start.8 = (bf16[256,768]{1,0:T(8,128)(2,1)}, bf16[256,768]{1,0:T(8,128)(2,1)}, u32[]{:S(2)}, u32[]{:S(2)}) collective-permute-start(bf16[256,768]{1,0:T(8,128)(2,1)} %collective-permute-done.2.other), channel_id=1, source_target_pairs={{0,0},{4,8},{8,4},{12,12},{1,1},{5,9},{9,5},{13,13},{2,2},{6,10},{... | collective-permute-start | bytes 1179656 | tf_op jit(solution)/shard_map/ppermute | solution.py:420
  20.9 11.1 %collective-permute-start.6 = (bf16[256,768]{1,0:T(8,128)(2,1)}, bf16[256,768]{1,0:T(8,128)(2,1)S(1)}, u32[]{:S(2)}, u32[]{:S(2)}) collective-permute-start(bf16[256,768]{1,0:T(8,128)(2,1)} %collective-permute-done.2.other), channel_id=1, source_target_pairs={{0,4},{4,0},{8,12},{12,8},{1,5},{5,1},{9,13},{13,9},{2,6},{6,2},{1... | collective-permute-start | bytes 1179656 | tf_op jit(solution)/shard_map/ppermute | solution.py:420
  21.9 8.6 %collective-permute-start.3 = (bf16[256,640]{1,0:T(8,128)(2,1)S(1)}, bf16[256,640]{1,0:T(8,128)(2,1)S(1)}, u32[]{:S(2)}, u32[]{:S(2)}) collective-permute-start(bf16[256,640]{1,0:T(8,128)(2,1)S(1)} %pad_maximum_fusion.5), channel_id=1, source_target_pairs={{0,2},{1,3},{2,0},{3,1},{4,6},{5,7},{6,4},{7,5},{8,10},{9,11},{10,... | collective-permute-start | bytes 983048 | tf_op jit(solution)/shard_map/ppermute | solution.py:417
  30.5 11.5 %collective-permute-start.10 = (bf16[256,512]{1,0:T(8,128)(2,1)S(1)}, bf16[256,512]{1,0:T(8,128)(2,1)}, u32[]{:S(2)}, u32[]{:S(2)}) collective-permute-start(bf16[256,512]{1,0:T(8,128)(2,1)S(1)} %pad_maximum_fusion.6), channel_id=1, source_target_pairs={{0,2},{1,3},{2,0},{3,1},{4,6},{5,7},{6,4},{7,5},{8,10},{9,11},{10,... | collective-permute-start | bytes 786440 | tf_op jit(solution)/shard_map/ppermute | solution.py:417
  32.0 0.8 copy-start.3
  32.8 0.8 copy-start.5
  35.6 12.7 %collective-permute-start.9 = (bf16[256,768]{1,0:T(8,128)(2,1)}, bf16[256,768]{1,0:T(8,128)(2,1)}, u32[]{:S(2)}, u32[]{:S(2)}) collective-permute-start(bf16[256,768]{1,0:T(8,128)(2,1)} %shard_map.56), channel_id=1, source_target_pairs={{0,0},{4,8},{8,4},{12,12},{1,1},{5,9},{9,5},{13,13},{2,2},{6,10},{... | collective-permute-start | bytes 1179656 | tf_op jit(solution)/shard_map/ppermute | solution.py:420
  40.1 11.8 %collective-permute-start.4 = (bf16[512,384]{1,0:T(8,128)(2,1)S(1)}, bf16[512,384]{1,0:T(8,128)(2,1)}, u32[]{:S(2)}, u32[]{:S(2)}) collective-permute-start(bf16[512,384]{1,0:T(8,128)(2,1)S(1)} %pad_maximum_fusion.3), channel_id=1, source_target_pairs={{0,4},{4,0},{8,12},{12,8},{1,5},{5,1},{9,13},{13,9},{2,6},{6,2},{1... | collective-permute-start | bytes 1179656 | tf_op jit(solution)/shard_map/ppermute | solution.py:420
  42.0 9.9 %copy-start.6 = (bf16[256,768]{1,0:T(8,128)(2,1)S(1)}, bf16[256,768]{1,0:T(8,128)(2,1)}, u32[]{:S(2)}) copy-start(bf16[256,768]{1,0:T(8,128)(2,1)} %copy-done.5) | copy-start | bytes 1179652
  43.2 8.6 %copy-start.4 = (bf16[272,768]{1,0:T(8,128)(2,1)S(1)}, bf16[272,768]{1,0:T(8,128)(2,1)}, u32[]{:S(2)}) copy-start(bf16[272,768]{1,0:T(8,128)(2,1)} %copy-done.3) | copy-start | bytes 1253380
  43.3 10.9 %collective-permute-start.11 = (bf16[512,512]{1,0:T(8,128)(2,1)S(1)}, bf16[512,512]{1,0:T(8,128)(2,1)S(1)}, u32[]{:S(2)}, u32[]{:S(2)}) collective-permute-start(bf16[512,512]{1,0:T(8,128)(2,1)S(1)} %maximum_select_fusion.whole), channel_id=1, source_target_pairs={{0,0},{4,8},{8,4},{12,12},{1,1},{5,9},{9,5},{13,13},{2,2},{6,10},{... | collective-permute-start | bytes 1572872 | tf_op jit(solution)/shard_map/ppermute | solution.py:420
  44.1 16.5 %collective-permute-start.16 = (bf16[512,512]{1,0:T(8,128)(2,1)S(1)}, bf16[512,512]{1,0:T(8,128)(2,1)S(1)}, u32[]{:S(2)}, u32[]{:S(2)}) collective-permute-start(bf16[512,512]{1,0:T(8,128)(2,1)S(1)} %maximum_select_fusion.whole), channel_id=1, source_target_pairs={{0,4},{4,0},{8,12},{12,8},{1,5},{5,1},{9,13},{13,9},{2,6},{6,2},{1... | collective-permute-start | bytes 1572872 | tf_op jit(solution)/shard_map/ppermute | solution.py:420
  54.1 18.1 %collective-permute-start.12 = (bf16[512,384]{1,0:T(8,128)(2,1)}, bf16[512,384]{1,0:T(8,128)(2,1)S(1)}, u32[]{:S(2)}, u32[]{:S(2)}) collective-permute-start(bf16[512,384]{1,0:T(8,128)(2,1)} %get-tuple-element.54), channel_id=1, source_target_pairs={{4,0},{8,12},{5,1},{9,13},{6,2},{10,14},{7,3},{11,15},{20,16},{24,... | collective-permute-start | bytes 1179656 | tf_op jit(solution)/shard_map/ppermute | solution.py:420
  61.3 12.7 %collective-permute-start.17 = (bf16[256,512]{1,0:T(8,128)(2,1)}, bf16[256,512]{1,0:T(8,128)(2,1)S(1)}, u32[]{:S(2)}, u32[]{:S(2)}) collective-permute-start(bf16[256,512]{1,0:T(8,128)(2,1)} %slice.69), channel_id=1, source_target_pairs={{0,0},{4,8},{8,4},{12,12},{1,1},{5,9},{9,5},{13,13},{2,2},{6,10},{... | collective-permute-start | bytes 786440 | tf_op jit(solution)/shard_map/ppermute | solution.py:420
  73.1 0.8 copy-start.8
  73.9 3.4 %collective-permute-start.13 = (bf16[128,384]{1,0:T(8,128)(2,1)}, bf16[128,384]{1,0:T(8,128)(2,1)S(1)}, u32[]{:S(2)}, u32[]{:S(2)}) collective-permute-start(bf16[128,384]{1,0:T(8,128)(2,1)} %get-tuple-element.77), channel_id=1, source_target_pairs={{0,1},{1,0},{2,3},{3,2},{4,5},{5,4},{6,7},{7,6},{8,9},{9,8},{10,11... | collective-permute-start | bytes 294920 | tf_op jit(solution)/shard_map/ppermute | solution.py:417
  73.9 2.1 %copy-start.9 = (bf16[128,384]{1,0:T(8,128)(2,1)S(1)}, bf16[128,384]{1,0:T(8,128)(2,1)}, u32[]{:S(2)}) copy-start(bf16[128,384]{1,0:T(8,128)(2,1)} %get-tuple-element.76) | copy-start | bytes 294916
  73.9 9.2 %collective-permute-start.18 = (bf16[256,512]{1,0:T(8,128)(2,1)S(1)}, bf16[256,512]{1,0:T(8,128)(2,1)S(1)}, u32[]{:S(2)}, u32[]{:S(2)}) collective-permute-start(bf16[256,512]{1,0:T(8,128)(2,1)S(1)} %slice.70), channel_id=1, source_target_pairs={{0,4},{4,0},{8,12},{12,8},{1,5},{5,1},{9,13},{13,9},{2,6},{6,2},{1... | collective-permute-start | bytes 786440 | tf_op jit(solution)/shard_map/ppermute | solution.py:420
  74.0 14.3 %collective-permute-start.19 = (bf16[256,512]{1,0:T(8,128)(2,1)S(1)}, bf16[256,512]{1,0:T(8,128)(2,1)S(1)}, u32[]{:S(2)}, u32[]{:S(2)}) collective-permute-start(bf16[256,512]{1,0:T(8,128)(2,1)S(1)} %collective-permute-done.17.r1), channel_id=1, source_target_pairs={{0,4},{4,0},{8,12},{12,8},{1,5},{5,1},{9,13},{13,9},{2,6},{6,2},{1... | collective-permute-start | bytes 786440 | tf_op jit(solution)/shard_map/ppermute | solution.py:420
  76.0 5.7 %collective-permute-start.14 = (bf16[128,384]{1,0:T(8,128)(2,1)S(1)}, bf16[128,384]{1,0:T(8,128)(2,1)S(1)}, u32[]{:S(2)}, u32[]{:S(2)}) collective-permute-start(bf16[128,384]{1,0:T(8,128)(2,1)S(1)} %copy-done.9), channel_id=1, source_target_pairs={{0,2},{1,3},{2,0},{3,1},{4,6},{5,7},{6,4},{7,5},{8,10},{9,11},{10,... | collective-permute-start | bytes 294920 | tf_op jit(solution)/shard_map/ppermute | solution.py:417
  76.4 6.0 %collective-permute-start.15 = (bf16[128,384]{1,0:T(8,128)(2,1)S(1)}, bf16[128,384]{1,0:T(8,128)(2,1)S(1)}, u32[]{:S(2)}, u32[]{:S(2)}) collective-permute-start(bf16[128,384]{1,0:T(8,128)(2,1)S(1)} %get-tuple-element.75), channel_id=1, source_target_pairs={{0,3},{1,2},{2,1},{3,0},{4,7},{5,6},{6,5},{7,4},{8,11},{9,10},{10,... | collective-permute-start | bytes 294920 | tf_op jit(solution)/shard_map/ppermute | solution.py:417
  91.6 2.6 %collective-permute-start.20 = (bf16[128,256]{1,0:T(8,128)(2,1)S(1)}, bf16[128,256]{1,0:T(8,128)(2,1)S(1)}, u32[]{:S(2)}, u32[]{:S(2)}) collective-permute-start(bf16[128,256]{1,0:T(8,128)(2,1)S(1)} %get-tuple-element.60), channel_id=1, source_target_pairs={{0,1},{1,0},{2,3},{3,2},{4,5},{5,4},{6,7},{7,6},{8,9},{9,8},{10,11... | collective-permute-start | bytes 196616 | tf_op jit(solution)/shard_map/ppermute | solution.py:417
  91.7 5.0 %collective-permute-start.21 = (bf16[128,256]{1,0:T(8,128)(2,1)S(1)}, bf16[128,256]{1,0:T(8,128)(2,1)S(1)}, u32[]{:S(2)}, u32[]{:S(2)}) collective-permute-start(bf16[128,256]{1,0:T(8,128)(2,1)S(1)} %get-tuple-element.61), channel_id=1, source_target_pairs={{0,2},{1,3},{2,0},{3,1},{4,6},{5,7},{6,4},{7,5},{8,10},{9,11},{10,... | collective-permute-start | bytes 196616 | tf_op jit(solution)/shard_map/ppermute | solution.py:417
  92.1 5.2 %collective-permute-start.22 = (bf16[128,256]{1,0:T(8,128)(2,1)S(1)}, bf16[128,256]{1,0:T(8,128)(2,1)S(1)}, u32[]{:S(2)}, u32[]{:S(2)}) collective-permute-start(bf16[128,256]{1,0:T(8,128)(2,1)S(1)} %get-tuple-element.62), channel_id=1, source_target_pairs={{0,3},{1,2},{2,1},{3,0},{4,7},{5,6},{6,5},{7,4},{8,11},{9,10},{10,... | collective-permute-start | bytes 196616 | tf_op jit(solution)/shard_map/ppermute | solution.py:417

commit v5 on v0

--- a/solution.py
+++ b/solution.py
@@ -1,9 +1,16 @@
+import functools
+import math
+
 import jax
 import jax.numpy as jnp
 from jax import lax
+from jax.experimental import pallas as pl
+from jax.experimental.pallas import tpu as pltpu
 from jax.sharding import PartitionSpec as P
 
 HEAD_DIM = 128
+SCALE = 1.0 / HEAD_DIM**0.5
+LOG2E = math.log2(math.e)
 
 
 def padded(x, sides, width):
@@ -19,14 +26,6 @@
     return x
 
 
-def shortened(x):
-
-    def short(part):
-        return part.astype(jnp.bfloat16) if part.dtype == jnp.float32 else part
-
-    return jax.tree.map(short, x)
-
-
 def from_partner(x, axis, bit):
     return lax.ppermute(x, axis, [(i, i ^ 1 << bit) for i in range(lax.axis_size(axis))])
 
@@ -45,11 +44,10 @@
     q_three = query_rows.reshape(count, heads, HEAD_DIM).transpose(1, 0, 2)
     k_three = key_rows.reshape(-1, heads, HEAD_DIM).transpose(1, 0, 2)
     v_three = value_rows.reshape(-1, heads, HEAD_DIM).transpose(1, 0, 2)
-    scale = 1.0 / HEAD_DIM**0.5
 
     def one_head(operands):
         q_head, k_head, v_head = operands
-        scores = jnp.dot(q_head, k_head.T, preferred_element_type=jnp.float32) * scale
+        scores = jnp.dot(q_head, k_head.T, preferred_element_type=jnp.float32) * SCALE
         scores = jnp.where(valid[None, :] > 0, scores, -1e30)
         top = jnp.max(scores, axis=1, keepdims=True)
         weights = jnp.exp(scores - top) * valid[None, :]
@@ -65,7 +63,7 @@
     return jnp.where(upper == 1, jnp.concatenate([theirs, mine]), jnp.concatenate([mine, theirs]))
 
 
-def per_device(queries, keys, values, pair_mask, tile_offset):
+def general(queries, keys, values, pair_mask, tile_offset):
     frames_n = lax.axis_size("frame")
     current = lax.axis_index("frame")
     q_rows, k_rows, v_rows = (
@@ -122,10 +120,7 @@
         active = [level for level in swap_levels if level >= bit]
         k_pack = jnp.concatenate([growing[level][0].reshape(-1, width) for level in active])
         v_pack = jnp.concatenate([growing[level][1].reshape(-1, width) for level in active])
-        k_in, v_in = (
-            from_partner(shortened(k_pack), "frame", bit).astype(k_pack.dtype),
-            from_partner(shortened(v_pack), "frame", bit).astype(v_pack.dtype),
-        )
+        k_in, v_in = (from_partner(k_pack, "frame", bit), from_partner(v_pack, "frame", bit))
         upper = current // 2**bit % 2
         position = 0
         for level in active:
@@ -160,7 +155,280 @@
     return lax.all_to_all(result, "head", split_axis=0, concat_axis=1, tiled=True)
 
 
+INFO_ROWS = 16
+OUTER = [(0, 1), (1, 0), (2, 3), (3, 2)]
+INNER = [(1, 2), (2, 1)]
+OUTWARD = [(1, 0), (2, 3)]
+
+
+def fold(x):
+    parts = [x[:, at : at + 128] for at in range(0, x.shape[1], 128)]
+    best = parts[0]
+    for part in parts[1:]:
+        best = jnp.maximum(best, part)
+    return best
+
+
+def scores_of(q, slots, held):
+    free, top = None, None
+    for at, (k, valid) in enumerate(slots):
+        s = lax.dot_general(q, k[...], (((1,), (1,)), ((), ())), preferred_element_type=jnp.float32)
+        held[:, at * s.shape[1] : (at + 1) * s.shape[1]] = s
+        best = fold(s)
+        if valid is None:
+            free = best if free is None else jnp.maximum(free, best)
+        else:
+            best = jnp.where(valid, jnp.max(best, axis=1, keepdims=True), -1e30)
+            top = best if top is None else jnp.maximum(top, best)
+    free = jnp.max(free, axis=1, keepdims=True)
+    return free if top is None else jnp.maximum(free, top)
+
+
+def weights_of(top, slots, held, out):
+    factor = SCALE * LOG2E
+    total = None
+    for at, (k, valid) in enumerate(slots):
+        tile = k.shape[0]
+        level = top if valid is None else jnp.where(valid, top, 1e30)
+        w = jnp.exp2((held[:, at * tile : (at + 1) * tile] - level) * factor)
+        out[:, at * tile : (at + 1) * tile] = w.astype(jnp.bfloat16)
+        for begin in range(0, tile, 128):
+            part = w[:, begin : begin + 128]
+            total = part if total is None else total + part
+    return jnp.sum(total, axis=1, keepdims=True)
+
+
+def inner_frame():
+    z = lax.axis_index("frame")
+    return (z == 1) | (z == 2)
+
+
+def weights_kernel(mask, q_mine, q_other, mine, other, n1m, n1o, n2m, n2o, r1, r2, r3, weights, totals, held0, held1):
+    z = lax.axis_index("frame")
+    tile = r1.shape[0]
+    near = mask[0, z ^ 2] == 1
+    always = [(mine, None), (other, None), (n1m, None), (n1o, None)]
+
+    def body(slots):
+        rooms = (held0, held1)
+        tops = [scores_of(q[...], slots, held) for q, held in zip((q_mine, q_other), rooms)]
+        for half, (top, held) in enumerate(zip(tops, rooms)):
+            rows = slice(half * tile, (half + 1) * tile)
+            total = weights_of(top, slots, held, weights.at[rows])
+            totals[rows] = jnp.broadcast_to(total, (tile, totals.shape[1]))
+
+    @pl.when(inner_frame())
+    def _():
+        body(always + [(n2m, None), (n2o, None), (r1, near)])
+
+    @pl.when(jnp.logical_not(inner_frame()))
+    def _():
+        body(always + [(r2, near), (r3, mask[0, z ^ 3] == 1)])
+
+
+def values_kernel(weights, totals, mine, other, n1m, n1o, n2m, n2o, r1, r2, r3, *outs):
+    tile = r1.shape[0]
+    rows = outs[0].shape[0]
+    always = [mine, other, n1m, n1o]
+
+    def body(slots):
+        for d, out in enumerate(outs):
+            span = slice(d * rows, (d + 1) * rows)
+            mixed = None
+            for at, v in enumerate(slots):
+                w = weights[span, at * tile : (at + 1) * tile]
+                mix = jnp.dot(w, v[...], preferred_element_type=jnp.float32)
+                mixed = mix if mixed is None else mixed + mix
+            out[...] = (mixed / totals[span]).astype(jnp.bfloat16)
+
+    @pl.when(inner_frame())
+    def _():
+        body(always + [n2m, n2o, r1])
+
+    @pl.when(jnp.logical_not(inner_frame()))
+    def _():
+        body(always + [r2, r3])
+
+
+def by_head(x, rows, first=0):
+    return x, pl.BlockSpec((rows, HEAD_DIM), lambda i: (0, first + i))
+
+
+def find_weights(mask, q_mine, q_other, keys, heads):
+    tile = q_mine.shape[0]
+    blocks = [by_head(q_mine, tile), by_head(q_other, tile)] + [by_head(k, tile) for k in keys]
+    shapes = [(2 * tile, 7 * tile, jnp.bfloat16), (2 * tile, HEAD_DIM, jnp.float32)]
+    return pl.pallas_call(
+        weights_kernel,
+        grid=(heads,),
+        in_specs=[pl.BlockSpec(memory_space=pltpu.SMEM)] + [spec for _, spec in blocks],
+        out_specs=[pl.BlockSpec((rows, lanes), lambda i: (i, 0)) for rows, lanes, _ in shapes],
+        out_shape=[jax.ShapeDtypeStruct((heads * rows, lanes), dtype) for rows, lanes, dtype in shapes],
+        scratch_shapes=[pltpu.VMEM((tile, 7 * tile), jnp.float32)] * 2,
+        compiler_params=pltpu.CompilerParams(vmem_limit_bytes=16 * 1024 * 1024),
+        cost_estimate=pl.CostEstimate(
+            flops=heads * 28 * tile * tile * HEAD_DIM,
+            bytes_accessed=heads * 28 * tile * tile,
+            transcendentals=heads * 14 * tile * tile,
+        ),
+    )(mask, *[x for x, _ in blocks])
+
+
+def mix_values(weights, totals, values, heads):
+    rows, lanes = weights.shape[0] // heads, weights.shape[1]
+    tile = lanes // 7
+    blocks = [by_head(v, tile, first) for v, first in values]
+    return pl.pallas_call(
+        values_kernel,
+        grid=(heads,),
+        in_specs=[pl.BlockSpec((rows, lanes), lambda i: (i, 0)), pl.BlockSpec((rows, HEAD_DIM), lambda i: (i, 0))]
+        + [spec for _, spec in blocks],
+        out_specs=[pl.BlockSpec((rows // 4, HEAD_DIM), lambda i: (0, i))] * 4,
+        out_shape=[jax.ShapeDtypeStruct((rows // 4, heads * HEAD_DIM), jnp.bfloat16)] * 4,
+        compiler_params=pltpu.CompilerParams(vmem_limit_bytes=16 * 1024 * 1024),
+        cost_estimate=pl.CostEstimate(
+            flops=heads * 2 * rows * lanes * HEAD_DIM, bytes_accessed=heads * 2 * rows * lanes, transcendentals=0
+        ),
+    )(weights, totals, *[x for x, _ in blocks])
+
+
+def pack_kernel(copies, width, mask, offset, *refs):
+    ins, outs, sems = refs[:3], refs[3:-1], refs[-1]
+    h = lax.axis_index("head")
+    started = []
+    for n, (operand, d, begin, result, at, lanes) in enumerate(copies):
+        source = ins[operand].at[:, pl.ds(pl.multiple_of((h ^ d) * width + begin, HEAD_DIM), lanes)]
+        copy = pltpu.make_async_copy(source, outs[result].at[:, at : at + lanes], sems.at[n])
+        copy.start()
+        started.append(copy)
+    if len(outs) > 1 + max(copy[3] for copy in copies):
+        told = outs[-1]
+        for group in range(told.shape[1] // 128):
+            value = mask[0, group] if group < 4 else offset[0]
+            rows = jnp.full((told.shape[0], 128), value, jnp.int32).astype(jnp.float32)
+            told[:, group * 128 : (group + 1) * 128] = rows.astype(told.dtype)
+    for copy in started:
+        copy.wait()
+
+
+def packed(operands, mask, offset, results, width, told):
+    rows = operands[0].shape[0]
+    copies, shapes = [], []
+    for n, parts in enumerate(results):
+        at = 0
+        for operand, d, begin, lanes in parts:
+            copies.append((operand, d, begin, n, at, lanes))
+            at += lanes
+        shapes.append(jax.ShapeDtypeStruct((rows, at), jnp.bfloat16))
+    if told:
+        shapes.append(jax.ShapeDtypeStruct((INFO_ROWS, told), jnp.bfloat16))
+    return pl.pallas_call(
+        functools.partial(pack_kernel, copies, width),
+        in_specs=[pl.BlockSpec(memory_space=pltpu.SMEM)] * 2 + [pl.BlockSpec(memory_space=pltpu.HBM)] * 3,
+        out_specs=[pl.BlockSpec(memory_space=pltpu.VMEM)] * len(shapes),
+        out_shape=shapes,
+        scratch_shapes=[pltpu.SemaphoreType.DMA((len(copies),))],
+        compiler_params=pltpu.CompilerParams(vmem_limit_bytes=4 * 1024 * 1024),
+    )(mask, offset, *operands)
+
+
+def relayed_kernel(mine, other, k_out, v_out):
+    tile, width = k_out.shape
+    offset = jnp.max(mine[tile : tile + INFO_ROWS, 4 * 128 : 5 * 128].astype(jnp.float32))
+    here = offset == (lax.axis_index("head") // 2).astype(jnp.float32)
+
+    def take(ref):
+        k_out[...] = ref[:tile, :width]
+        v_out[...] = ref[:tile, width:]
+
+    @pl.when(here)
+    def _():
+        take(mine)
+
+    @pl.when(jnp.logical_not(here))
+    def _():
+        take(other)
+
+
+def relayed(mine, other):
+    tile, lanes = other.shape
+    return pl.pallas_call(
+        relayed_kernel,
+        in_specs=[pl.BlockSpec(memory_space=pltpu.VMEM)] * 2,
+        out_specs=[pl.BlockSpec(memory_space=pltpu.VMEM)] * 2,
+        out_shape=[jax.ShapeDtypeStruct((tile, lanes // 2), other.dtype)] * 2,
+        compiler_params=pltpu.CompilerParams(vmem_limit_bytes=4 * 1024 * 1024),
+    )(mine, other)
+
+
+def four_frames(queries, keys, values, pair_mask, tile_offset):
+    h = lax.axis_index("head")
+    rows, features = queries.shape
+    width = features // 4
+    heads = width // HEAD_DIM
+
+    def columns(array, d):
+        return lax.dynamic_slice_in_dim(array, (h ^ d) * width, width, axis=1)
+
+    def beside(*arrays):
+        return jnp.concatenate(arrays, axis=1)
+
+    def below(*arrays):
+        return jnp.concatenate(arrays, axis=0)
+
+    def to_head(array, d):
+        return lax.ppermute(array, "head", [(i, i ^ d) for i in range(4)])
+
+    def along(array, pairs):
+        return lax.ppermute(array, "frame", pairs)
+
+    def after(array, earlier):
+        return lax.optimization_barrier((array, earlier))[0]
+
+    kv = [[columns(array, d) for array in (keys, values)] for d in range(4)]
+    kv = lax.optimization_barrier(kv)
+    got = to_head(beside(*kv[1], *kv[3]), 1)
+    pay, q_own, q_far, told = packed(
+        (queries, keys, values),
+        pair_mask,
+        tile_offset,
+        [[(0, 1, 0, width), (0, 3, 0, width)], [(0, 0, 0, width)], [(0, 2, 0, width)]],
+        width,
+        2 * width,
+    )
+    mine = below(beside(*kv[0]), got[:, : 2 * width], told)
+    other = to_head(below(beside(*kv[2]), got[:, 2 * width :]), 2)
+    n1m = along(mine, OUTER)
+    n2m = along(mine, INNER)
+    n1o = along(other, OUTER)
+    n2o = along(other, INNER)
+
+    got = to_head(after(pay, got), 1)
+    q_mine = below(q_own, got[:, :width])
+    q_other = to_head(after(below(q_far, got[:, width:]), other), 2)
+
+    r1k, r1v = after(relayed(n1m, n1o), n2m)
+    r1k = along(r1k, INNER)
+    r1v = along(r1v, INNER)
+    r2k, r2v = relayed(n2m, n2o)
+    r2k = along(r2k, OUTWARD)
+    r3k = along(r1k, OUTWARD)
+    r2v = along(after(r2v, r1k), OUTWARD)
+    r3v = along(r1v, OUTWARD)
+
+    near = [mine, other, n1m, n1o, n2m, n2o]
+    weights, totals = find_weights(pair_mask, q_mine, q_other, [*near, r1k, r2k, r3k], heads)
+    out = mix_values(weights, totals, [(x, heads) for x in near] + [(x, 0) for x in (r1v, r2v, r3v)], heads)
+    out = [out[0]] + [to_head(out[d], d) for d in (1, 2, 3)]
+    result = jnp.zeros((rows, features), jnp.bfloat16)
+    for d in range(4):
+        result = lax.dynamic_update_slice_in_dim(result, out[d], (h ^ d) * width, axis=1)
+    return result
+
+
 def solution(mesh):
+    sizes = dict(mesh.shape)
+    per_device = four_frames if sizes["frame"] == 4 and sizes["head"] == 4 else general
     return jax.shard_map(
         per_device,
         mesh=mesh,

time: 172 us -> 91.5 us (0.53)
  local copies, waits for them, and re-layouts: 31 us -> 2.42 us
  blocking collectives: 25.3 us -> 0 us
  matrix products: 18.7 us -> 0 us
  other arithmetic: 14.5 us -> 0.21 us
  between operations: 14.2 us -> 0.95 us
  Pallas kernels: 0 us -> 11.4 us
  waiting for transfers between devices: 53.3 us -> 59 us
  starting transfers between devices: 14.2 us -> 17.2 us
    all_to_all x2 -> x0, blocking collectives: 25.3 us -> none  [the longest x1 12.7 us: per_device(): lax.all_to_all(values, 'head', split_axis=1, concat_axis=0, tiled=True)]
    ppermute x2 -> x17, waiting for transfers between devices: 33.8 us -> 59 us  [the longest x10 35.6 us: along(): return lax.ppermute(array, 'frame', pairs)]
    all_to_all x2 -> x0, waiting for transfers between devices: 19.5 us -> none  [the longest x1 9.93 us: per_device(): lax.all_to_all(queries, 'head', split_axis=1, concat_axis=0, tiled=True)]
    dot_general x10 -> x0, matrix products: 18.7 us -> none  [the longest x5 14.2 us: one_head(): jnp.dot(weights.astype(jnp.bfloat16), v_head, preferred_element_type=jnp....]
    pallas_call x0 -> x5, Pallas kernels: none -> 11.4 us  [the longest x1 6.42 us: find_weights(): pl.pallas_call(weights_kernel, grid=(heads,), in_specs=[pl.BlockSpec(memo...]
    ppermute x2 -> x17, starting transfers between devices: 6.51 us -> 17.2 us  [the longest x10 11.4 us: along(): return lax.ppermute(array, 'frame', pairs)]
    unnamed x17 -> x10, local copies, waits for them, and re-layouts: 9.13 us -> 0.03 us
    slice x3 -> x2, local copies, waits for them, and re-layouts: 8.96 us -> 0.07 us  [the longest x1 0.04 us: four_frames(): mine = below(beside(*kv[0]), got[:, :2 * width], told)]
  transfers between devices with their start and end apart: 6 -> 17, of which waited for: 4 -> 11; matrix products, arithmetic and copies ran while one was open for 11% -> 0% of each run, Pallas kernels for 0% -> 8%
where the time goes in v5:
time: 91.5 us; the launch traced here: 91.2 us
  waiting for transfers between devices  59 us (64%)
  starting transfers between devices  17.2 us (19%)
  Pallas kernels  11.4 us (12%)
  local copies, waits for them, and re-layouts  2.42 us (3%)
  between operations  0.95 us (1%)
    ppermute x10, waiting for transfers between devices, along(): return lax.ppermute(array, 'frame', pairs)  35.6 us
    ppermute x7, waiting for transfers between devices, to_head(): return lax.ppermute(array, 'head', [(i, i ^ d) for i in range(4)])  23.4 us
    ppermute x10, starting transfers between devices, along(): return lax.ppermute(array, 'frame', pairs)  11.4 us
    pallas_call x1, Pallas kernels, find_weights(): pl.pallas_call(weights_kernel, grid=(heads,), in_specs=[pl.BlockSpec(memo...  6.42 us
    ppermute x7, starting transfers between devices, to_head(): return lax.ppermute(array, 'head', [(i, i ^ d) for i in range(4)])  5.81 us
    pallas_call x1, Pallas kernels, mix_values(): pl.pallas_call(values_kernel, grid=(heads,), in_specs=[pl.BlockSpec((rows...  3.94 us
  transfers between devices with their start and end apart: 17, of which 11 were waited for; matrix products, arithmetic and copies ran while one was open for 0% of the time, Pallas kernels for 8%

profile of v5, /device:TPU:0, one launch (start us, length us, event | category | flops | bytes accessed | tf_op | source)
XLA Modules:
  0.0 91.2 jit_solution(10730510292905861141)
XLA Ops:
  0.0 1.5 %constant_dynamic-slice_fusion = (bf16[128,640]{1,0:T(8,128)(2,1)S(1)}, bf16[128,640]{1,0:T(8,128)(2,1)S(1)}, bf16[128,640]{1,0:T(8,128)(2,1)S(1)}, bf16[128,640...) fusion(bf16[128,2560]{1,0:T(8,128)(2,1)} %refs_2_.1, ...), kind=kLoop, calls=%fused_computation.9 | loop fusion | bytes 2621456 | tf_op jit(solution)/shard_map/dynamic_slice | solution.py:371
  1.5 0.1 pad_maximum_fusion.1
  1.6 0.0 copy-start
  1.6 0.0 copy-start.1
  1.6 0.0 copy-start.2
  1.6 0.0 copy-start.3
  1.6 0.5 collective-permute-start
  2.1 1.7 %collective-permute-done = bf16[128,2560]{1,0:T(8,128)(2,1)S(1)} collective-permute-done((bf16[128,2560]{1,0:T(8,128)(2,1)S(1)}, bf16[128,2560]{1,0:T(8,128)(2,1)S(1)}, u32[]{:S(2)}, u32[]{:S(2)}) %collective-permute-start) | collective-permute-done | bytes 655392 | tf_op jit(solution)/shard_map/ppermute | solution.py:380
  4.0 2.9 %collective-permute-start.2 = (bf16[256,1280]{1,0:T(8,128)(2,1)S(1)}, bf16[256,1280]{1,0:T(8,128)(2,1)S(1)}, u32[]{:S(2)}, u32[]{:S(2)}) collective-permute-start(bf16[256,1280]{1,0:T(8,128)(2,1)S(1)} %pad_maximum_fusion.2), channel_id=1, source_target_pairs={{0,2},{1,3},{2,0},{3,1},{4,6},{5,7},{6,4},{7,5},{8,10},{9,11},{10,... | collective-permute-start | bytes 1966088 | tf_op jit(solution)/shard_map/ppermute | solution.py:380
  7.6 0.7 shard_map.55
  8.3 0.1 pad_maximum_fusion.mine
  8.3 1.6 %collective-permute-start.4 = (bf16[272,1280]{1,0:T(8,128)(2,1)S(1)}, bf16[272,1280]{1,0:T(8,128)(2,1)S(1)}, u32[]{:S(2)}, u32[]{:S(2)}) collective-permute-start(bf16[272,1280]{1,0:T(8,128)(2,1)S(1)} %pad_maximum_fusion.mine), channel_id=1, source_target_pairs={{0,4},{4,0},{8,12},{12,8},{1,5},{5,1},{9,13},{13,9},{2,6},{6,2},{1... | collective-permute-start | bytes 2088968 | tf_op jit(solution)/shard_map/ppermute | solution.py:383
  10.0 0.7 collective-permute-start.6
  10.7 11.3 %collective-permute-done.2.other = bf16[256,1280]{1,0:T(8,128)(2,1)S(1)} collective-permute-done((bf16[256,1280]{1,0:T(8,128)(2,1)S(1)}, bf16[256,1280]{1,0:T(8,128)(2,1)S(1)}, u32[]{:S(2)}, u32[]{:S(2)}) %collective-permute-start.2) | collective-permute-done | bytes 655392 | tf_op jit(solution)/shard_map/ppermute | solution.py:380
  21.9 1.8 %collective-permute-start.5 = (bf16[256,1280]{1,0:T(8,128)(2,1)S(1)}, bf16[256,1280]{1,0:T(8,128)(2,1)S(1)}, u32[]{:S(2)}, u32[]{:S(2)}) collective-permute-start(bf16[256,1280]{1,0:T(8,128)(2,1)S(1)} %collective-permute-done.2.other), channel_id=1, source_target_pairs={{0,4},{4,0},{8,12},{12,8},{1,5},{5,1},{9,13},{13,9},{2,6},{6,2},{1... | collective-permute-start | bytes 1966088 | tf_op jit(solution)/shard_map/ppermute | solution.py:383
  23.7 0.0 collective-permute-start.1
  23.8 0.7 collective-permute-start.7
  24.5 2.4 %collective-permute-done.4.mine.n1m = bf16[272,1280]{1,0:T(8,128)(2,1)S(1)} collective-permute-done((bf16[272,1280]{1,0:T(8,128)(2,1)S(1)}, bf16[272,1280]{1,0:T(8,128)(2,1)S(1)}, u32[]{:S(2)}, u32[]{:S(2)}) %collective-permute-start.4) | collective-permute-done | bytes 696352 | tf_op jit(solution)/shard_map/ppermute | solution.py:383
  26.9 12.9 %collective-permute-done.5.other.n1o = bf16[256,1280]{1,0:T(8,128)(2,1)S(1)} collective-permute-done((bf16[256,1280]{1,0:T(8,128)(2,1)S(1)}, bf16[256,1280]{1,0:T(8,128)(2,1)S(1)}, u32[]{:S(2)}, u32[]{:S(2)}) %collective-permute-start.5) | collective-permute-done | bytes 655392 | tf_op jit(solution)/shard_map/ppermute | solution.py:383
  39.8 0.2 shard_map.56
  40.0 0.0 collective-permute-done.6.mine.n2m
  40.0 0.7 collective-permute-start.8
  40.7 0.7 collective-permute-start.11
  41.4 0.0 collective-permute-done.1
  41.5 0.4 collective-permute-start.3
  41.9 0.0 collective-permute-done.7.other.n2o
  41.9 0.2 shard_map.57
  42.1 1.3 %collective-permute-start.9 = (bf16[256,640]{1,0:T(8,128)(2,1)S(1)}, bf16[256,640]{1,0:T(8,128)(2,1)S(1)}, u32[]{:S(2)}, u32[]{:S(2)}) collective-permute-start(bf16[256,640]{1,0:T(8,128)(2,1)S(1)} %get-tuple-element.49), channel_id=1, source_target_pairs={{4,0},{8,12},{5,1},{9,13},{6,2},{10,14},{7,3},{11,15},{20,16},{24,... | collective-permute-start | bytes 983048 | tf_op jit(solution)/shard_map/ppermute | solution.py:383
  43.4 0.0 collective-permute-done.8.r1
  43.4 1.3 %collective-permute-start.10 = (bf16[256,640]{1,0:T(8,128)(2,1)S(1)}, bf16[256,640]{1,0:T(8,128)(2,1)S(1)}, u32[]{:S(2)}, u32[]{:S(2)}) collective-permute-start(bf16[256,640]{1,0:T(8,128)(2,1)S(1)} %collective-permute-done.8.r1), channel_id=1, source_target_pairs={{4,0},{8,12},{5,1},{9,13},{6,2},{10,14},{7,3},{11,15},{20,16},{24,... | collective-permute-start | bytes 983048 | tf_op jit(solution)/shard_map/ppermute | solution.py:383
  44.7 1.3 %collective-permute-start.12 = (bf16[256,640]{1,0:T(8,128)(2,1)S(1)}, bf16[256,640]{1,0:T(8,128)(2,1)S(1)}, u32[]{:S(2)}, u32[]{:S(2)}) collective-permute-start(bf16[256,640]{1,0:T(8,128)(2,1)S(1)} %get-tuple-element.54), channel_id=1, source_target_pairs={{4,0},{8,12},{5,1},{9,13},{6,2},{10,14},{7,3},{11,15},{20,16},{24,... | collective-permute-start | bytes 983048 | tf_op jit(solution)/shard_map/ppermute | solution.py:383
  46.0 0.0 collective-permute-done.11.r1
  46.0 1.3 %collective-permute-start.13 = (bf16[256,640]{1,0:T(8,128)(2,1)S(1)}, bf16[256,640]{1,0:T(8,128)(2,1)S(1)}, u32[]{:S(2)}, u32[]{:S(2)}) collective-permute-start(bf16[256,640]{1,0:T(8,128)(2,1)S(1)} %collective-permute-done.11.r1), channel_id=1, source_target_pairs={{4,0},{8,12},{5,1},{9,13},{6,2},{10,14},{7,3},{11,15},{20,16},{24,... | collective-permute-start | bytes 983048 | tf_op jit(solution)/shard_map/ppermute | solution.py:383
  47.3 2.8 %collective-permute-done.3.q_other = bf16[256,640]{1,0:T(8,128)(2,1)S(1)} collective-permute-done((bf16[256,640]{1,0:T(8,128)(2,1)S(1)}, bf16[256,640]{1,0:T(8,128)(2,1)S(1)}, u32[]{:S(2)}, u32[]{:S(2)}) %collective-permute-start.3) | collective-permute-done | bytes 327712 | tf_op jit(solution)/shard_map/ppermute | solution.py:380
  50.1 8.1 %collective-permute-done.9.r2 = bf16[256,640]{1,0:T(8,128)(2,1)S(1)} collective-permute-done((bf16[256,640]{1,0:T(8,128)(2,1)S(1)}, bf16[256,640]{1,0:T(8,128)(2,1)S(1)}, u32[]{:S(2)}, u32[]{:S(2)}) %collective-permute-start.9) | collective-permute-done | bytes 327712 | tf_op jit(solution)/shard_map/ppermute | solution.py:383
  58.2 7.0 %collective-permute-done.10.r3 = bf16[256,640]{1,0:T(8,128)(2,1)S(1)} collective-permute-done((bf16[256,640]{1,0:T(8,128)(2,1)S(1)}, bf16[256,640]{1,0:T(8,128)(2,1)S(1)}, u32[]{:S(2)}, u32[]{:S(2)}) %collective-permute-start.10) | collective-permute-done | bytes 327712 | tf_op jit(solution)/shard_map/ppermute | solution.py:383
  65.2 6.4 %shard_map.58 = (bf16[2560,1792]{1,0:T(8,128)(2,1)S(1)}, f32[2560,128]{1,0:T(8,128)S(1)}) custom-call(s32[1,4]{1,0:T(1,128)S(1)} %copy-done.3, bf16[256,640]{1,0:T(8,128)(2,1)S(1)} %pad_maximum_fusion.3.q_mine, bf16[256,640]{1,0:T(8,128)(2,1)S(1)} %collective-permute-done.3.q_other, bf16[272,1280]{1,0:T(8,128)(2,1)S(1)} %pad_maximum_fusion.mine, ...), custom_call_target="tpu_custom_call" | custom-call | flops 1174405120 | bytes 9175040 | tf_op jit(solution)/shard_map/pallas_call | solution.py:261
  71.6 0.6 collective-permute-done.12.r2
  72.3 4.5 %collective-permute-done.13.r3 = bf16[256,640]{1,0:T(8,128)(2,1)S(1)} collective-permute-done((bf16[256,640]{1,0:T(8,128)(2,1)S(1)}, bf16[256,640]{1,0:T(8,128)(2,1)S(1)}, u32[]{:S(2)}, u32[]{:S(2)}) %collective-permute-start.13) | collective-permute-done | bytes 327712 | tf_op jit(solution)/shard_map/ppermute | solution.py:383
  76.8 3.9 %shard_map.59 = (bf16[128,640]{1,0:T(8,128)(2,1)S(1)}, bf16[128,640]{1,0:T(8,128)(2,1)S(1)}, bf16[128,640]{1,0:T(8,128)(2,1)S(1)}, bf16[128,640]{1,0:T(8,128)(2,1)S(1)}) custom-call(bf16[2560,1792]{1,0:T(8,128)(2,1)S(1)} %get-tuple-element.50.weights, f32[2560,128]{1,0:T(8,128)S(1)} %get-tuple-element.51.totals, bf16[272,1280]{1,0:T(8,128)(2,1)S(1)} %pad_maximum_fusion.mine, ...), custom_call_target="tpu_custom_call" | custom-call | flops 1174405120 | bytes 9175040 | tf_op jit(solution)/shard_map/pallas_call | solution.py:281
  80.8 0.1 collective-permute-start.14
  80.8 1.4 %collective-permute-start.15 = (bf16[128,640]{1,0:T(8,128)(2,1)S(1)}, bf16[128,640]{1,0:T(8,128)(2,1)S(1)}, u32[]{:S(2)}, u32[]{:S(2)}) collective-permute-start(bf16[128,640]{1,0:T(8,128)(2,1)S(1)} %get-tuple-element.57), channel_id=1, source_target_pairs={{0,2},{1,3},{2,0},{3,1},{4,6},{5,7},{6,4},{7,5},{8,10},{9,11},{10,... | collective-permute-start | bytes 491528 | tf_op jit(solution)/shard_map/ppermute | solution.py:380
  82.3 0.4 collective-permute-start.16
  82.8 0.0 collective-permute-done.14
  82.8 5.1 %collective-permute-done.15 = bf16[128,640]{1,0:T(8,128)(2,1)S(1)} collective-permute-done((bf16[128,640]{1,0:T(8,128)(2,1)S(1)}, bf16[128,640]{1,0:T(8,128)(2,1)S(1)}, u32[]{:S(2)}, u32[]{:S(2)}) %collective-permute-start.15) | collective-permute-done | bytes 163872 | tf_op jit(solution)/shard_map/ppermute | solution.py:380
  87.9 0.0 copy-start.4
  87.9 2.6 %collective-permute-done.16 = bf16[128,640]{1,0:T(8,128)(2,1)S(1)} collective-permute-done((bf16[128,640]{1,0:T(8,128)(2,1)S(1)}, bf16[128,640]{1,0:T(8,128)(2,1)S(1)}, u32[]{:S(2)}, u32[]{:S(2)}) %collective-permute-start.16) | collective-permute-done | bytes 163872 | tf_op jit(solution)/shard_map/ppermute | solution.py:380
  90.5 0.7 constant_dynamic-update-slice_fusion
  (14 shorter events, 0.3 us)
Async XLA Ops:
  1.6 6.0 %copy-start = (bf16[128,2560]{1,0:T(8,128)(2,1)S(1)}, bf16[128,2560]{1,0:T(8,128)(2,1)}, u32[]{:S(2)}) copy-start(bf16[128,2560]{1,0:T(8,128)(2,1)} %refs_1_.1) | copy-start | bytes 1966084
  1.6 6.0 %copy-start.1 = (bf16[128,2560]{1,0:T(8,128)(2,1)S(1)}, bf16[128,2560]{1,0:T(8,128)(2,1)}, u32[]{:S(2)}) copy-start(bf16[128,2560]{1,0:T(8,128)(2,1)} %refs_2_.1) | copy-start | bytes 1966084
  1.6 6.0 %copy-start.2 = (bf16[128,2560]{1,0:T(8,128)(2,1)S(1)}, bf16[128,2560]{1,0:T(8,128)(2,1)}, u32[]{:S(2)}) copy-start(bf16[128,2560]{1,0:T(8,128)(2,1)} %refs_0_.1) | copy-start | bytes 1966084
  1.6 6.0 %copy-start.3 = (s32[1,4]{1,0:T(1,128)S(1)}, s32[1,4]{1,0:T(1,128)}, u32[]{:S(2)}) copy-start(s32[1,4]{1,0:T(1,128)} %mask.3) | copy-start | bytes 52
  1.6 2.2 %collective-permute-start = (bf16[128,2560]{1,0:T(8,128)(2,1)S(1)}, bf16[128,2560]{1,0:T(8,128)(2,1)S(1)}, u32[]{:S(2)}, u32[]{:S(2)}) collective-permute-start(bf16[128,2560]{1,0:T(8,128)(2,1)S(1)} %pad_maximum_fusion.1), channel_id=1, source_target_pairs={{0,1},{1,0},{2,3},{3,2},{4,5},{5,4},{6,7},{7,6},{8,9},{9,8},{10,11... | collective-permute-start | bytes 1966088 | tf_op jit(solution)/shard_map/ppermute | solution.py:380
  4.0 18.0 %collective-permute-start.2 = (bf16[256,1280]{1,0:T(8,128)(2,1)S(1)}, bf16[256,1280]{1,0:T(8,128)(2,1)S(1)}, u32[]{:S(2)}, u32[]{:S(2)}) collective-permute-start(bf16[256,1280]{1,0:T(8,128)(2,1)S(1)} %pad_maximum_fusion.2), channel_id=1, source_target_pairs={{0,2},{1,3},{2,0},{3,1},{4,6},{5,7},{6,4},{7,5},{8,10},{9,11},{10,... | collective-permute-start | bytes 1966088 | tf_op jit(solution)/shard_map/ppermute | solution.py:380
  8.3 18.6 %collective-permute-start.4 = (bf16[272,1280]{1,0:T(8,128)(2,1)S(1)}, bf16[272,1280]{1,0:T(8,128)(2,1)S(1)}, u32[]{:S(2)}, u32[]{:S(2)}) collective-permute-start(bf16[272,1280]{1,0:T(8,128)(2,1)S(1)} %pad_maximum_fusion.mine), channel_id=1, source_target_pairs={{0,4},{4,0},{8,12},{12,8},{1,5},{5,1},{9,13},{13,9},{2,6},{6,2},{1... | collective-permute-start | bytes 2088968 | tf_op jit(solution)/shard_map/ppermute | solution.py:383
  10.0 30.0 %collective-permute-start.6 = (bf16[272,1280]{1,0:T(8,128)(2,1)S(1)}, bf16[272,1280]{1,0:T(8,128)(2,1)S(1)}, u32[]{:S(2)}, u32[]{:S(2)}) collective-permute-start(bf16[272,1280]{1,0:T(8,128)(2,1)S(1)} %pad_maximum_fusion.mine), channel_id=1, source_target_pairs={{4,8},{8,4},{5,9},{9,5},{6,10},{10,6},{7,11},{11,7},{20,24},{24,20... | collective-permute-start | bytes 2088968 | tf_op jit(solution)/shard_map/ppermute | solution.py:383
  21.9 17.9 %collective-permute-start.5 = (bf16[256,1280]{1,0:T(8,128)(2,1)S(1)}, bf16[256,1280]{1,0:T(8,128)(2,1)S(1)}, u32[]{:S(2)}, u32[]{:S(2)}) collective-permute-start(bf16[256,1280]{1,0:T(8,128)(2,1)S(1)} %collective-permute-done.2.other), channel_id=1, source_target_pairs={{0,4},{4,0},{8,12},{12,8},{1,5},{5,1},{9,13},{13,9},{2,6},{6,2},{1... | collective-permute-start | bytes 1966088 | tf_op jit(solution)/shard_map/ppermute | solution.py:383
  23.7 17.6 %collective-permute-start.1 = (bf16[128,1280]{1,0:T(8,128)(2,1)S(1)}, bf16[128,1280]{1,0:T(8,128)(2,1)S(1)}, u32[]{:S(2)}, u32[]{:S(2)}) collective-permute-start(bf16[128,1280]{1,0:T(8,128)(2,1)S(1)} %get-tuple-element.38), channel_id=1, source_target_pairs={{0,1},{1,0},{2,3},{3,2},{4,5},{5,4},{6,7},{7,6},{8,9},{9,8},{10,11... | collective-permute-start | bytes 983048 | tf_op jit(solution)/shard_map/ppermute | solution.py:380
  23.8 18.2 %collective-permute-start.7 = (bf16[256,1280]{1,0:T(8,128)(2,1)S(1)}, bf16[256,1280]{1,0:T(8,128)(2,1)S(1)}, u32[]{:S(2)}, u32[]{:S(2)}) collective-permute-start(bf16[256,1280]{1,0:T(8,128)(2,1)S(1)} %collective-permute-done.2.other), channel_id=1, source_target_pairs={{4,8},{8,4},{5,9},{9,5},{6,10},{10,6},{7,11},{11,7},{20,24},{24,20... | collective-permute-start | bytes 1966088 | tf_op jit(solution)/shard_map/ppermute | solution.py:383
  40.0 3.4 %collective-permute-start.8 = (bf16[256,640]{1,0:T(8,128)(2,1)S(1)}, bf16[256,640]{1,0:T(8,128)(2,1)S(1)}, u32[]{:S(2)}, u32[]{:S(2)}) collective-permute-start(bf16[256,640]{1,0:T(8,128)(2,1)S(1)} %get-tuple-element.48), channel_id=1, source_target_pairs={{4,8},{8,4},{5,9},{9,5},{6,10},{10,6},{7,11},{11,7},{20,24},{24,20... | collective-permute-start | bytes 983048 | tf_op jit(solution)/shard_map/ppermute | solution.py:383
  40.7 5.3 %collective-permute-start.11 = (bf16[256,640]{1,0:T(8,128)(2,1)S(1)}, bf16[256,640]{1,0:T(8,128)(2,1)S(1)}, u32[]{:S(2)}, u32[]{:S(2)}) collective-permute-start(bf16[256,640]{1,0:T(8,128)(2,1)S(1)} %get-tuple-element.52), channel_id=1, source_target_pairs={{4,8},{8,4},{5,9},{9,5},{6,10},{10,6},{7,11},{11,7},{20,24},{24,20... | collective-permute-start | bytes 983048 | tf_op jit(solution)/shard_map/ppermute | solution.py:383
  41.5 8.7 %collective-permute-start.3 = (bf16[256,640]{1,0:T(8,128)(2,1)S(1)}, bf16[256,640]{1,0:T(8,128)(2,1)S(1)}, u32[]{:S(2)}, u32[]{:S(2)}) collective-permute-start(bf16[256,640]{1,0:T(8,128)(2,1)S(1)} %pad_maximum_fusion.4), channel_id=1, source_target_pairs={{0,2},{1,3},{2,0},{3,1},{4,6},{5,7},{6,4},{7,5},{8,10},{9,11},{10,... | collective-permute-start | bytes 983048 | tf_op jit(solution)/shard_map/ppermute | solution.py:380
  42.1 16.1 %collective-permute-start.9 = (bf16[256,640]{1,0:T(8,128)(2,1)S(1)}, bf16[256,640]{1,0:T(8,128)(2,1)S(1)}, u32[]{:S(2)}, u32[]{:S(2)}) collective-permute-start(bf16[256,640]{1,0:T(8,128)(2,1)S(1)} %get-tuple-element.49), channel_id=1, source_target_pairs={{4,0},{8,12},{5,1},{9,13},{6,2},{10,14},{7,3},{11,15},{20,16},{24,... | collective-permute-start | bytes 983048 | tf_op jit(solution)/shard_map/ppermute | solution.py:383
  43.4 21.8 %collective-permute-start.10 = (bf16[256,640]{1,0:T(8,128)(2,1)S(1)}, bf16[256,640]{1,0:T(8,128)(2,1)S(1)}, u32[]{:S(2)}, u32[]{:S(2)}) collective-permute-start(bf16[256,640]{1,0:T(8,128)(2,1)S(1)} %collective-permute-done.8.r1), channel_id=1, source_target_pairs={{4,0},{8,12},{5,1},{9,13},{6,2},{10,14},{7,3},{11,15},{20,16},{24,... | collective-permute-start | bytes 983048 | tf_op jit(solution)/shard_map/ppermute | solution.py:383
  44.7 27.6 %collective-permute-start.12 = (bf16[256,640]{1,0:T(8,128)(2,1)S(1)}, bf16[256,640]{1,0:T(8,128)(2,1)S(1)}, u32[]{:S(2)}, u32[]{:S(2)}) collective-permute-start(bf16[256,640]{1,0:T(8,128)(2,1)S(1)} %get-tuple-element.54), channel_id=1, source_target_pairs={{4,0},{8,12},{5,1},{9,13},{6,2},{10,14},{7,3},{11,15},{20,16},{24,... | collective-permute-start | bytes 983048 | tf_op jit(solution)/shard_map/ppermute | solution.py:383
  46.0 30.8 %collective-permute-start.13 = (bf16[256,640]{1,0:T(8,128)(2,1)S(1)}, bf16[256,640]{1,0:T(8,128)(2,1)S(1)}, u32[]{:S(2)}, u32[]{:S(2)}) collective-permute-start(bf16[256,640]{1,0:T(8,128)(2,1)S(1)} %collective-permute-done.11.r1), channel_id=1, source_target_pairs={{4,0},{8,12},{5,1},{9,13},{6,2},{10,14},{7,3},{11,15},{20,16},{24,... | collective-permute-start | bytes 983048 | tf_op jit(solution)/shard_map/ppermute | solution.py:383
  80.8 2.0 %collective-permute-start.14 = (bf16[128,640]{1,0:T(8,128)(2,1)S(1)}, bf16[128,640]{1,0:T(8,128)(2,1)S(1)}, u32[]{:S(2)}, u32[]{:S(2)}) collective-permute-start(bf16[128,640]{1,0:T(8,128)(2,1)S(1)} %get-tuple-element.56), channel_id=1, source_target_pairs={{0,1},{1,0},{2,3},{3,2},{4,5},{5,4},{6,7},{7,6},{8,9},{9,8},{10,11... | collective-permute-start | bytes 491528 | tf_op jit(solution)/shard_map/ppermute | solution.py:380
  80.8 7.1 %collective-permute-start.15 = (bf16[128,640]{1,0:T(8,128)(2,1)S(1)}, bf16[128,640]{1,0:T(8,128)(2,1)S(1)}, u32[]{:S(2)}, u32[]{:S(2)}) collective-permute-start(bf16[128,640]{1,0:T(8,128)(2,1)S(1)} %get-tuple-element.57), channel_id=1, source_target_pairs={{0,2},{1,3},{2,0},{3,1},{4,6},{5,7},{6,4},{7,5},{8,10},{9,11},{10,... | collective-permute-start | bytes 491528 | tf_op jit(solution)/shard_map/ppermute | solution.py:380
  82.3 8.2 %collective-permute-start.16 = (bf16[128,640]{1,0:T(8,128)(2,1)S(1)}, bf16[128,640]{1,0:T(8,128)(2,1)S(1)}, u32[]{:S(2)}, u32[]{:S(2)}) collective-permute-start(bf16[128,640]{1,0:T(8,128)(2,1)S(1)} %get-tuple-element.58), channel_id=1, source_target_pairs={{0,3},{1,2},{2,1},{3,0},{4,7},{5,6},{6,5},{7,4},{8,11},{9,10},{10,... | collective-permute-start | bytes 491528 | tf_op jit(solution)/shard_map/ppermute | solution.py:380
  87.9 2.6 %copy-start.4 = (bf16[128,2560]{1,0:T(8,128)(2,1)}, bf16[128,2560]{1,0:T(8,128)(2,1)S(1)}, u32[]{:S(2)}) copy-start(bf16[128,2560]{1,0:T(8,128)(2,1)S(1)} %constant_dynamic-update-slice_fusion.1) | copy-start | bytes 1966084

commit v6 on v5

--- a/solution.py
+++ b/solution.py
@@ -274,14 +274,17 @@
     )(mask, *[x for x, _ in blocks])
 
 
-def mix_values(weights, totals, values, heads):
-    rows, lanes = weights.shape[0] // heads, weights.shape[1]
-    tile = lanes // 7
+def mix_values(weights, totals, values, skip, heads):
+    tile = weights.shape[1] // 7
+    rows, lanes = 2 * tile, weights.shape[1]
     blocks = [by_head(v, tile, first) for v, first in values]
     return pl.pallas_call(
         values_kernel,
         grid=(heads,),
-        in_specs=[pl.BlockSpec((rows, lanes), lambda i: (i, 0)), pl.BlockSpec((rows, HEAD_DIM), lambda i: (i, 0))]
+        in_specs=[
+            pl.BlockSpec((rows, lanes), lambda i: (skip + i, 0)),
+            pl.BlockSpec((rows, HEAD_DIM), lambda i: (skip + i, 0)),
+        ]
         + [spec for _, spec in blocks],
         out_specs=[pl.BlockSpec((rows // 4, HEAD_DIM), lambda i: (0, i))] * 4,
         out_shape=[jax.ShapeDtypeStruct((rows // 4, heads * HEAD_DIM), jnp.bfloat16)] * 4,
@@ -332,31 +335,26 @@
     )(mask, offset, *operands)
 
 
-def relayed_kernel(mine, other, k_out, v_out):
-    tile, width = k_out.shape
+def relayed_kernel(at, mine, other, out):
+    tile, width = out.shape
     offset = jnp.max(mine[tile : tile + INFO_ROWS, 4 * 128 : 5 * 128].astype(jnp.float32))
     here = offset == (lax.axis_index("head") // 2).astype(jnp.float32)
 
-    def take(ref):
-        k_out[...] = ref[:tile, :width]
-        v_out[...] = ref[:tile, width:]
-
     @pl.when(here)
     def _():
-        take(mine)
+        out[...] = mine[:tile, at : at + width]
 
     @pl.when(jnp.logical_not(here))
     def _():
-        take(other)
-
-
-def relayed(mine, other):
-    tile, lanes = other.shape
+        out[...] = other[...]
+
+
+def relayed(mine, other, at):
     return pl.pallas_call(
-        relayed_kernel,
+        functools.partial(relayed_kernel, at),
         in_specs=[pl.BlockSpec(memory_space=pltpu.VMEM)] * 2,
-        out_specs=[pl.BlockSpec(memory_space=pltpu.VMEM)] * 2,
-        out_shape=[jax.ShapeDtypeStruct((tile, lanes // 2), other.dtype)] * 2,
+        out_specs=pl.BlockSpec(memory_space=pltpu.VMEM),
+        out_shape=jax.ShapeDtypeStruct(other.shape, other.dtype),
         compiler_params=pltpu.CompilerParams(vmem_limit_bytes=4 * 1024 * 1024),
     )(mine, other)
 
@@ -397,32 +395,39 @@
         2 * width,
     )
     mine = below(beside(*kv[0]), got[:, : 2 * width], told)
-    other = to_head(below(beside(*kv[2]), got[:, 2 * width :]), 2)
+    other_k = to_head(below(kv[2][0], got[:, 2 * width : 3 * width]), 2)
+    other_v = to_head(below(kv[2][1], got[:, 3 * width :]), 2)
     n1m = along(mine, OUTER)
     n2m = along(mine, INNER)
-    n1o = along(other, OUTER)
-    n2o = along(other, INNER)
+    n1k = along(other_k, OUTER)
+    n2k = along(other_k, INNER)
+    n1v = along(other_v, OUTER)
+    n2v = along(other_v, INNER)
 
     got = to_head(after(pay, got), 1)
     q_mine = below(q_own, got[:, :width])
-    q_other = to_head(after(below(q_far, got[:, width:]), other), 2)
-
-    r1k, r1v = after(relayed(n1m, n1o), n2m)
-    r1k = along(r1k, INNER)
-    r1v = along(r1v, INNER)
-    r2k, r2v = relayed(n2m, n2o)
-    r2k = along(r2k, OUTWARD)
+    q_other = to_head(after(below(q_far, got[:, width:]), other_v), 2)
+
+    r1k = along(after(relayed(n1m, n1k, 0), (n2m, n2k)), INNER)
+    r1v = along(after(relayed(n1m, n1v, width), n2v), INNER)
+    r2k = along(relayed(n2m, n2k, 0), OUTWARD)
     r3k = along(r1k, OUTWARD)
-    r2v = along(after(r2v, r1k), OUTWARD)
-    r3v = along(r1v, OUTWARD)
-
-    near = [mine, other, n1m, n1o, n2m, n2o]
-    weights, totals = find_weights(pair_mask, q_mine, q_other, [*near, r1k, r2k, r3k], heads)
-    out = mix_values(weights, totals, [(x, heads) for x in near] + [(x, 0) for x in (r1v, r2v, r3v)], heads)
-    out = [out[0]] + [to_head(out[d], d) for d in (1, 2, 3)]
+    r2v = along(after(relayed(n2m, n2v, width), r1k), OUTWARD)
+
+    weights, totals = find_weights(
+        pair_mask, q_mine, q_other, [mine, other_k, n1m, n1k, n2m, n2k, r1k, r2k, r3k], heads
+    )
     result = jnp.zeros((rows, features), jnp.bfloat16)
-    for d in range(4):
-        result = lax.dynamic_update_slice_in_dim(result, out[d], (h ^ d) * width, axis=1)
+    cut = (heads + 1) // 2
+    for begin, end in ((0, cut), (cut, heads)):
+        r3v = along(r1v[:, begin * HEAD_DIM : end * HEAD_DIM], OUTWARD)
+        whole = [(x, heads + begin) for x in (mine, n1m, n2m)]
+        part = [(x, begin) for x in (other_v, n1v, n2v, r1v, r2v)]
+        slots = [whole[0], part[0], whole[1], part[1], whole[2], part[2], part[3], part[4], (r3v, 0)]
+        out = mix_values(weights, totals, slots, begin, end - begin)
+        out = [out[0]] + [to_head(out[d], d) for d in (1, 2, 3)]
+        for d in range(4):
+            result = lax.dynamic_update_slice_in_dim(result, out[d], (h ^ d) * width + begin * HEAD_DIM, axis=1)
     return result
 
 

time: 91.5 us -> 94.3 us (1.031)
  waiting for transfers between devices: 59 us -> 39.9 us
  starting transfers between devices: 17.2 us -> 27.8 us
  local copies, waits for them, and re-layouts: 2.42 us -> 7.45 us
  Pallas kernels: 11.4 us -> 15.5 us
  other arithmetic: 0.21 us -> 1.95 us
    ppermute x7 -> x11, waiting for transfers between devices: 23.4 us -> 12.9 us  [to_head(): return lax.ppermute(array, 'head', [(i, i ^ d) for i in range(4)])]
    ppermute x10 -> x13, waiting for transfers between devices: 35.6 us -> 27.1 us  [along(): return lax.ppermute(array, 'frame', pairs)]
    ppermute x10 -> x13, starting transfers between devices: 11.4 us -> 19.4 us  [along(): return lax.ppermute(array, 'frame', pairs)]
    unnamed x10 -> x24, local copies, waits for them, and re-layouts: 0.03 us -> 4.23 us
    ppermute x7 -> x11, starting transfers between devices: 5.81 us -> 8.43 us  [to_head(): return lax.ppermute(array, 'head', [(i, i ^ d) for i in range(4)])]
    pallas_call x2 -> x4, Pallas kernels: 0.35 us -> 2.79 us  [relayed(): pl.pallas_call(functools.partial(relayed_kernel, at), in_specs=[pl.BlockS...]
    concatenate x4 -> x5, other arithmetic: 0.16 us -> 1.89 us  [below(): return jnp.concatenate(arrays, axis=0)]
    pallas_call x1 -> x2, Pallas kernels: 3.94 us -> 5.45 us  [mix_values(): pl.pallas_call(values_kernel, grid=(heads,), in_specs=[pl.BlockSpec((rows...]
  transfers between devices with their start and end apart: 17 -> 24, of which waited for: 11 -> 9; matrix products, arithmetic and copies ran while one was open for 0% -> 3% of each run, Pallas kernels for 8% -> 17%
where the time goes in v6:
time: 94.3 us; the launch traced here: 93.7 us
  waiting for transfers between devices  39.9 us (42%)
  starting transfers between devices  27.8 us (29%)
  Pallas kernels  15.5 us (16%)
  local copies, waits for them, and re-layouts  7.45 us (8%)
  other arithmetic  1.95 us (2%)
  between operations  1.04 us (1%)
    ppermute x13, waiting for transfers between devices, along(): return lax.ppermute(array, 'frame', pairs)  27.1 us
    ppermute x13, starting transfers between devices, along(): return lax.ppermute(array, 'frame', pairs)  19.4 us
    ppermute x11, waiting for transfers between devices, to_head(): return lax.ppermute(array, 'head', [(i, i ^ d) for i in range(4)])  12.9 us
    ppermute x11, starting transfers between devices, to_head(): return lax.ppermute(array, 'head', [(i, i ^ d) for i in range(4)])  8.43 us
    pallas_call x1, Pallas kernels, find_weights(): pl.pallas_call(weights_kernel, grid=(heads,), in_specs=[pl.BlockSpec(memo...  6.56 us
    pallas_call x2, Pallas kernels, mix_values(): pl.pallas_call(values_kernel, grid=(heads,), in_specs=[pl.BlockSpec((rows...  5.45 us
    unnamed x24, local copies, waits for them, and re-layouts  4.23 us
    pallas_call x4, Pallas kernels, relayed(): pl.pallas_call(functools.partial(relayed_kernel, at), in_specs=[pl.BlockS...  2.79 us
  transfers between devices with their start and end apart: 24, of which 9 were waited for; matrix products, arithmetic and copies ran while one was open for 3% of the time, Pallas kernels for 17%

profile of v6, /device:TPU:0, one launch (start us, length us, event | category | flops | bytes accessed | tf_op | source)
XLA Modules:
  0.0 93.7 jit_solution(17020326148069803828)
XLA Ops:
  0.0 1.6 %constant_dynamic-slice_fusion = (bf16[128,640]{1,0:T(8,128)(2,1)S(1)}, bf16[128,640]{1,0:T(8,128)(2,1)S(1)}, bf16[128,640]{1,0:T(8,128)(2,1)S(1)}, bf16[128,640...) fusion(bf16[128,2560]{1,0:T(8,128)(2,1)} %refs_2_.1, ...), kind=kLoop, calls=%fused_computation.14 | loop fusion | bytes 2621456 | tf_op jit(solution)/shard_map/dynamic_slice | solution.py:369
  1.7 0.5 collective-permute-start
  2.9 0.7 shard_map.55
  3.6 0.7 copy-done.7
  4.4 2.7 %collective-permute-start.5 = (bf16[272,1280]{1,0:T(8,128)(2,1)S(1)}, bf16[272,1280]{1,0:T(8,128)(2,1)S(1)}, u32[]{:S(2)}, u32[]{:S(2)}) collective-permute-start(bf16[272,1280]{1,0:T(8,128)(2,1)S(1)} %pad_maximum_fusion.mine), channel_id=1, source_target_pairs={{0,4},{4,0},{8,12},{12,8},{1,5},{5,1},{9,13},{13,9},{2,6},{6,2},{1... | collective-permute-start | bytes 2088968 | tf_op jit(solution)/shard_map/ppermute | solution.py:381
  7.1 0.7 collective-permute-start.7
  7.8 1.6 %collective-permute-start.4 = (bf16[256,640]{1,0:T(8,128)(2,1)S(1)}, bf16[256,640]{1,0:T(8,128)(2,1)S(1)}, u32[]{:S(2)}, u32[]{:S(2)}) collective-permute-start(bf16[256,640]{1,0:T(8,128)(2,1)S(1)} %pad_maximum_fusion.5), channel_id=1, source_target_pairs={{0,2},{1,3},{2,0},{3,1},{4,6},{5,7},{6,4},{7,5},{8,10},{9,11},{10,... | collective-permute-start | bytes 983048 | tf_op jit(solution)/shard_map/ppermute | solution.py:378
  9.4 0.6 collective-permute-start.2
  10.0 8.4 %collective-permute-done.4.other = bf16[256,640]{1,0:T(8,128)(2,1)S(1)} collective-permute-done((bf16[256,640]{1,0:T(8,128)(2,1)S(1)}, bf16[256,640]{1,0:T(8,128)(2,1)S(1)}, u32[]{:S(2)}, u32[]{:S(2)}) %collective-permute-start.4) | collective-permute-done | bytes 327712 | tf_op jit(solution)/shard_map/ppermute | solution.py:378
  18.5 4.4 %collective-permute-start.6 = (bf16[256,640]{1,0:T(8,128)(2,1)S(1)}, bf16[256,640]{1,0:T(8,128)(2,1)S(1)}, u32[]{:S(2)}, u32[]{:S(2)}) collective-permute-start(bf16[256,640]{1,0:T(8,128)(2,1)S(1)} %collective-permute-done.4.other), channel_id=1, source_target_pairs={{0,4},{4,0},{8,12},{12,8},{1,5},{5,1},{9,13},{13,9},{2,6},{6,2},{1... | collective-permute-start | bytes 983048 | tf_op jit(solution)/shard_map/ppermute | solution.py:381
  22.9 0.7 collective-permute-start.8
  23.5 1.2 %collective-permute-done.2.other = bf16[256,640]{1,0:T(8,128)(2,1)S(1)} collective-permute-done((bf16[256,640]{1,0:T(8,128)(2,1)S(1)}, bf16[256,640]{1,0:T(8,128)(2,1)S(1)}, u32[]{:S(2)}, u32[]{:S(2)}) %collective-permute-start.2) | collective-permute-done | bytes 327712 | tf_op jit(solution)/shard_map/ppermute | solution.py:378
  24.7 5.6 %collective-permute-done.6.other.n1o = bf16[256,640]{1,0:T(8,128)(2,1)S(1)} collective-permute-done((bf16[256,640]{1,0:T(8,128)(2,1)S(1)}, bf16[256,640]{1,0:T(8,128)(2,1)S(1)}, u32[]{:S(2)}, u32[]{:S(2)}) %collective-permute-start.6) | collective-permute-done | bytes 327712 | tf_op jit(solution)/shard_map/ppermute | solution.py:381
  30.3 1.7 %collective-permute-start.12 = (bf16[256,640]{1,0:T(8,128)(2,1)S(1)}, bf16[256,640]{1,0:T(8,128)(2,1)S(1)}, u32[]{:S(2)}, u32[]{:S(2)}) collective-permute-start(bf16[256,640]{1,0:T(8,128)(2,1)S(1)} %collective-permute-done.2.other), channel_id=1, source_target_pairs={{0,4},{4,0},{8,12},{12,8},{1,5},{5,1},{9,13},{13,9},{2,6},{6,2},{1... | collective-permute-start | bytes 983048 | tf_op jit(solution)/shard_map/ppermute | solution.py:381
  32.1 0.7 collective-permute-start.13
  32.9 1.4 %collective-permute-start.9 = (bf16[256,640]{1,0:T(8,128)(2,1)S(1)}, bf16[256,640]{1,0:T(8,128)(2,1)}, u32[]{:S(2)}, u32[]{:S(2)}) collective-permute-start(bf16[256,640]{1,0:T(8,128)(2,1)S(1)} %shard_map.56), channel_id=1, source_target_pairs={{4,8},{8,4},{5,9},{9,5},{6,10},{10,6},{7,11},{11,7},{20,24},{24,20... | collective-permute-start | bytes 983048 | tf_op jit(solution)/shard_map/ppermute | solution.py:381
  34.3 0.7 fusion.1
  35.0 3.8 %collective-permute-done.12.other.n1o = bf16[256,640]{1,0:T(8,128)(2,1)S(1)} collective-permute-done((bf16[256,640]{1,0:T(8,128)(2,1)S(1)}, bf16[256,640]{1,0:T(8,128)(2,1)S(1)}, u32[]{:S(2)}, u32[]{:S(2)}) %collective-permute-start.12) | collective-permute-done | bytes 327712 | tf_op jit(solution)/shard_map/ppermute | solution.py:381
  38.9 0.9 shard_map.59
  39.8 0.7 collective-permute-start.14
  40.5 0.8 pad_maximum_fusion.3
  41.2 1.8 %collective-permute-start.3 = (bf16[256,640]{1,0:T(8,128)(2,1)}, bf16[256,640]{1,0:T(8,128)(2,1)}, u32[]{:S(2)}, u32[]{:S(2)}) collective-permute-start(bf16[256,640]{1,0:T(8,128)(2,1)} %pad_maximum_fusion.3), channel_id=1, source_target_pairs={{0,2},{1,3},{2,0},{3,1},{4,6},{5,7},{6,4},{7,5},{8,10},{9,11},{10,... | collective-permute-start | bytes 983048 | tf_op jit(solution)/shard_map/ppermute | solution.py:378
  43.0 0.9 shard_map.57
  43.9 1.3 %collective-permute-start.10 = (bf16[256,640]{1,0:T(8,128)(2,1)}, bf16[256,640]{1,0:T(8,128)(2,1)}, u32[]{:S(2)}, u32[]{:S(2)}) collective-permute-start(bf16[256,640]{1,0:T(8,128)(2,1)} %shard_map.57), channel_id=1, source_target_pairs={{4,0},{8,12},{5,1},{9,13},{6,2},{10,14},{7,3},{11,15},{20,16},{24,... | collective-permute-start | bytes 983048 | tf_op jit(solution)/shard_map/ppermute | solution.py:381
  45.2 1.3 %collective-permute-start.11 = (bf16[256,640]{1,0:T(8,128)(2,1)}, bf16[256,640]{1,0:T(8,128)(2,1)}, u32[]{:S(2)}, u32[]{:S(2)}) collective-permute-start(bf16[256,640]{1,0:T(8,128)(2,1)} %collective-permute-done.9.r1), channel_id=1, source_target_pairs={{4,0},{8,12},{5,1},{9,13},{6,2},{10,14},{7,3},{11,15},{20,16},{24,... | collective-permute-start | bytes 983048 | tf_op jit(solution)/shard_map/ppermute | solution.py:381
  46.5 0.9 shard_map.60
  47.4 1.3 %collective-permute-start.15 = (bf16[256,640]{1,0:T(8,128)(2,1)}, bf16[256,640]{1,0:T(8,128)(2,1)}, u32[]{:S(2)}, u32[]{:S(2)}) collective-permute-start(bf16[256,640]{1,0:T(8,128)(2,1)} %shard_map.60), channel_id=1, source_target_pairs={{4,0},{8,12},{5,1},{9,13},{6,2},{10,14},{7,3},{11,15},{20,16},{24,... | collective-permute-start | bytes 983048 | tf_op jit(solution)/shard_map/ppermute | solution.py:381
  48.8 1.3 %collective-permute-start.16 = (bf16[256,384]{1,0:T(8,128)(2,1)S(1)}, bf16[256,384]{1,0:T(8,128)(2,1)S(1)}, u32[]{:S(2)}, u32[]{:S(2)}) collective-permute-start(bf16[256,384]{1,0:T(8,128)(2,1)S(1)} %slice.33), channel_id=1, source_target_pairs={{4,0},{8,12},{5,1},{9,13},{6,2},{10,14},{7,3},{11,15},{20,16},{24,... | collective-permute-start | bytes 589832 | tf_op jit(solution)/shard_map/ppermute | solution.py:381
  50.1 1.0 %pad_maximum_fusion.2.q_mine = bf16[256,640]{1,0:T(8,128)(2,1)S(1)} fusion(bf16[128,640]{1,0:T(8,128)(2,1)} %get-tuple-element.70, bf16[128,640]{1,0:T(8,128)(2,1)} %copy-done.7), kind=kLoop, calls=%fused_computation.2 | loop fusion | flops 655360 | bytes 655360 | tf_op jit(solution)/shard_map/concatenate | solution.py:375
  51.1 1.3 %collective-permute-start.20 = (bf16[256,256]{1,0:T(8,128)(2,1)S(1)}, bf16[256,256]{1,0:T(8,128)(2,1)S(1)}, u32[]{:S(2)}, u32[]{:S(2)}) collective-permute-start(bf16[256,256]{1,0:T(8,128)(2,1)S(1)} %slice.34), channel_id=1, source_target_pairs={{4,0},{8,12},{5,1},{9,13},{6,2},{10,14},{7,3},{11,15},{20,16},{24,... | collective-permute-start | bytes 393224 | tf_op jit(solution)/shard_map/ppermute | solution.py:381
  52.4 10.6 %collective-permute-done.10.r2 = bf16[256,640]{1,0:T(8,128)(2,1)} collective-permute-done((bf16[256,640]{1,0:T(8,128)(2,1)}, bf16[256,640]{1,0:T(8,128)(2,1)}, u32[]{:S(2)}, u32[]{:S(2)}) %collective-permute-start.10) | collective-permute-done | bytes 327712 | tf_op jit(solution)/shard_map/ppermute | solution.py:381
  63.0 7.0 %collective-permute-done.11.r3 = bf16[256,640]{1,0:T(8,128)(2,1)} collective-permute-done((bf16[256,640]{1,0:T(8,128)(2,1)}, bf16[256,640]{1,0:T(8,128)(2,1)}, u32[]{:S(2)}, u32[]{:S(2)}) %collective-permute-start.11) | collective-permute-done | bytes 327712 | tf_op jit(solution)/shard_map/ppermute | solution.py:381
  70.0 1.0 %copy-done.4 = bf16[256,640]{1,0:T(8,128)(2,1)S(1)} copy-done((bf16[256,640]{1,0:T(8,128)(2,1)S(1)}, bf16[256,640]{1,0:T(8,128)(2,1)}, u32[]{:S(2)}) %copy-start.4) | copy-done | bytes 327704
  71.0 1.0 %copy-done.6 = bf16[256,640]{1,0:T(8,128)(2,1)S(1)} copy-done((bf16[256,640]{1,0:T(8,128)(2,1)S(1)}, bf16[256,640]{1,0:T(8,128)(2,1)}, u32[]{:S(2)}) %copy-start.6) | copy-done | bytes 327704
  72.0 1.0 %copy-done.10 = bf16[256,640]{1,0:T(8,128)(2,1)S(1)} copy-done((bf16[256,640]{1,0:T(8,128)(2,1)S(1)}, bf16[256,640]{1,0:T(8,128)(2,1)}, u32[]{:S(2)}) %copy-start.10) | copy-done | bytes 327704
  72.9 6.6 %shard_map.58 = (bf16[2560,1792]{1,0:T(8,128)(2,1)S(1)}, f32[2560,128]{1,0:T(8,128)S(1)}) custom-call(s32[1,4]{1,0:T(1,128)S(1)} %copy-done.8, bf16[256,640]{1,0:T(8,128)(2,1)S(1)} %pad_maximum_fusion.2.q_mine, bf16[256,640]{1,0:T(8,128)(2,1)} %collective-permute-done.3.q_other, bf16[272,1280]{1,0:T(8,128)(2,1)S(1)} %pad_maximum_fusion.mine, ...), custom_call_target="tpu_custom_call" | custom-call | flops 1174405120 | bytes 9175040 | tf_op jit(solution)/shard_map/pallas_call | solution.py:261
  79.5 3.2 %shard_map.61 = (bf16[128,384]{1,0:T(8,128)(2,1)S(1)}, bf16[128,384]{1,0:T(8,128)(2,1)S(1)}, bf16[128,384]{1,0:T(8,128)(2,1)S(1)}, bf16[128,384]{1,0:T(8,128)(2,1)S(1)}) custom-call(bf16[2560,1792]{1,0:T(8,128)(2,1)S(1)} %get-tuple-element.47.weights, f32[2560,128]{1,0:T(8,128)S(1)} %get-tuple-element.48.totals, bf16[272,1280]{1,0:T(8,128)(2,1)S(1)} %pad_maximum_fusion.mine, ...), custom_call_target="tpu_custom_call" | custom-call | flops 704643072 | bytes 5505024 | tf_op jit(solution)/shard_map/pallas_call | solution.py:281
  82.8 0.6 collective-permute-start.18
  83.4 1.3 %collective-permute-start.19 = (bf16[128,384]{1,0:T(8,128)(2,1)S(1)}, bf16[128,384]{1,0:T(8,128)(2,1)S(1)}, u32[]{:S(2)}, u32[]{:S(2)}) collective-permute-start(bf16[128,384]{1,0:T(8,128)(2,1)S(1)} %get-tuple-element.54), channel_id=1, source_target_pairs={{0,3},{1,2},{2,1},{3,0},{4,7},{5,6},{6,5},{7,4},{8,11},{9,10},{10,... | collective-permute-start | bytes 294920 | tf_op jit(solution)/shard_map/ppermute | solution.py:378
  84.7 2.2 %shard_map.62 = (bf16[128,256]{1,0:T(8,128)(2,1)S(1)}, bf16[128,256]{1,0:T(8,128)(2,1)S(1)}, bf16[128,256]{1,0:T(8,128)(2,1)S(1)}, bf16[128,256]{1,0:T(8,128)(2,1)S(1)}) custom-call(bf16[2560,1792]{1,0:T(8,128)(2,1)S(1)} %get-tuple-element.47.weights, f32[2560,128]{1,0:T(8,128)S(1)} %get-tuple-element.48.totals, bf16[272,1280]{1,0:T(8,128)(2,1)S(1)} %pad_maximum_fusion.mine, ...), custom_call_target="tpu_custom_call" | custom-call | flops 469762048 | bytes 3670016 | tf_op jit(solution)/shard_map/pallas_call | solution.py:281
  86.9 0.4 collective-permute-start.21
  87.3 0.5 collective-permute-start.22
  88.0 1.0 %collective-permute-start.23 = (bf16[128,256]{1,0:T(8,128)(2,1)S(1)}, bf16[128,256]{1,0:T(8,128)(2,1)S(1)}, u32[]{:S(2)}, u32[]{:S(2)}) collective-permute-start(bf16[128,256]{1,0:T(8,128)(2,1)S(1)} %get-tuple-element.58), channel_id=1, source_target_pairs={{0,3},{1,2},{2,1},{3,0},{4,7},{5,6},{6,5},{7,4},{8,11},{9,10},{10,... | collective-permute-start | bytes 196616 | tf_op jit(solution)/shard_map/ppermute | solution.py:378
  89.1 0.6 collective-permute-done.19
  89.7 2.5 %collective-permute-done.22 = bf16[128,256]{1,0:T(8,128)(2,1)S(1)} collective-permute-done((bf16[128,256]{1,0:T(8,128)(2,1)S(1)}, bf16[128,256]{1,0:T(8,128)(2,1)S(1)}, u32[]{:S(2)}, u32[]{:S(2)}) %collective-permute-start.22) | collective-permute-done | bytes 65568 | tf_op jit(solution)/shard_map/ppermute | solution.py:378
  92.2 0.2 collective-permute-done.23
  92.4 0.6 copy-done.11
  93.0 0.6 constant_dynamic-update-slice_fusion
  (53 shorter events, 0.7 us)
Async XLA Ops:
  0.0 2.9 %copy-start = (bf16[128,2560]{1,0:T(8,128)(2,1)S(1)}, bf16[128,2560]{1,0:T(8,128)(2,1)}, u32[]{:S(2)}) copy-start(bf16[128,2560]{1,0:T(8,128)(2,1)} %refs_1_.1) | copy-start | bytes 1966084
  0.0 2.9 %copy-start.1 = (bf16[128,2560]{1,0:T(8,128)(2,1)S(1)}, bf16[128,2560]{1,0:T(8,128)(2,1)}, u32[]{:S(2)}) copy-start(bf16[128,2560]{1,0:T(8,128)(2,1)} %refs_2_.1) | copy-start | bytes 1966084
  0.0 2.9 %copy-start.2 = (bf16[128,2560]{1,0:T(8,128)(2,1)S(1)}, bf16[128,2560]{1,0:T(8,128)(2,1)}, u32[]{:S(2)}) copy-start(bf16[128,2560]{1,0:T(8,128)(2,1)} %refs_0_.1) | copy-start | bytes 1966084
  0.0 2.9 %copy-start.8 = (s32[1,4]{1,0:T(1,128)S(1)}, s32[1,4]{1,0:T(1,128)}, u32[]{:S(2)}) copy-start(s32[1,4]{1,0:T(1,128)} %mask.3) | copy-start | bytes 52
  1.7 2.6 %collective-permute-start = (bf16[128,2560]{1,0:T(8,128)(2,1)S(1)}, bf16[128,2560]{1,0:T(8,128)(2,1)S(1)}, u32[]{:S(2)}, u32[]{:S(2)}) collective-permute-start(bf16[128,2560]{1,0:T(8,128)(2,1)S(1)} %pad_maximum_fusion.1), channel_id=1, source_target_pairs={{0,1},{1,0},{2,3},{3,2},{4,5},{5,4},{6,7},{7,6},{8,9},{9,8},{10,11... | collective-permute-start | bytes 1966088 | tf_op jit(solution)/shard_map/ppermute | solution.py:378
  3.6 0.7 copy-start.7
  4.4 27.7 %collective-permute-start.5 = (bf16[272,1280]{1,0:T(8,128)(2,1)S(1)}, bf16[272,1280]{1,0:T(8,128)(2,1)S(1)}, u32[]{:S(2)}, u32[]{:S(2)}) collective-permute-start(bf16[272,1280]{1,0:T(8,128)(2,1)S(1)} %pad_maximum_fusion.mine), channel_id=1, source_target_pairs={{0,4},{4,0},{8,12},{12,8},{1,5},{5,1},{9,13},{13,9},{2,6},{6,2},{1... | collective-permute-start | bytes 2088968 | tf_op jit(solution)/shard_map/ppermute | solution.py:381
  7.1 25.9 %collective-permute-start.7 = (bf16[272,1280]{1,0:T(8,128)(2,1)S(1)}, bf16[272,1280]{1,0:T(8,128)(2,1)S(1)}, u32[]{:S(2)}, u32[]{:S(2)}) collective-permute-start(bf16[272,1280]{1,0:T(8,128)(2,1)S(1)} %pad_maximum_fusion.mine), channel_id=1, source_target_pairs={{4,8},{8,4},{5,9},{9,5},{6,10},{10,6},{7,11},{11,7},{20,24},{24,20... | collective-permute-start | bytes 2088968 | tf_op jit(solution)/shard_map/ppermute | solution.py:381
  7.8 10.6 %collective-permute-start.4 = (bf16[256,640]{1,0:T(8,128)(2,1)S(1)}, bf16[256,640]{1,0:T(8,128)(2,1)S(1)}, u32[]{:S(2)}, u32[]{:S(2)}) collective-permute-start(bf16[256,640]{1,0:T(8,128)(2,1)S(1)} %pad_maximum_fusion.5), channel_id=1, source_target_pairs={{0,2},{1,3},{2,0},{3,1},{4,6},{5,7},{6,4},{7,5},{8,10},{9,11},{10,... | collective-permute-start | bytes 983048 | tf_op jit(solution)/shard_map/ppermute | solution.py:378
  9.4 15.3 %collective-permute-start.2 = (bf16[256,640]{1,0:T(8,128)(2,1)S(1)}, bf16[256,640]{1,0:T(8,128)(2,1)S(1)}, u32[]{:S(2)}, u32[]{:S(2)}) collective-permute-start(bf16[256,640]{1,0:T(8,128)(2,1)S(1)} %pad_maximum_fusion.4), channel_id=1, source_target_pairs={{0,2},{1,3},{2,0},{3,1},{4,6},{5,7},{6,4},{7,5},{8,10},{9,11},{10,... | collective-permute-start | bytes 983048 | tf_op jit(solution)/shard_map/ppermute | solution.py:378
  18.5 21.3 %copy-start.9 = (bf16[256,640]{1,0:T(8,128)(2,1)}, bf16[256,640]{1,0:T(8,128)(2,1)S(1)}, u32[]{:S(2)}) copy-start(bf16[256,640]{1,0:T(8,128)(2,1)S(1)} %collective-permute-done.4.other) | copy-start | bytes 983044
  18.5 11.9 %collective-permute-start.6 = (bf16[256,640]{1,0:T(8,128)(2,1)S(1)}, bf16[256,640]{1,0:T(8,128)(2,1)S(1)}, u32[]{:S(2)}, u32[]{:S(2)}) collective-permute-start(bf16[256,640]{1,0:T(8,128)(2,1)S(1)} %collective-permute-done.4.other), channel_id=1, source_target_pairs={{0,4},{4,0},{8,12},{12,8},{1,5},{5,1},{9,13},{13,9},{2,6},{6,2},{1... | collective-permute-start | bytes 983048 | tf_op jit(solution)/shard_map/ppermute | solution.py:381
  22.9 10.0 %collective-permute-start.8 = (bf16[256,640]{1,0:T(8,128)(2,1)S(1)}, bf16[256,640]{1,0:T(8,128)(2,1)S(1)}, u32[]{:S(2)}, u32[]{:S(2)}) collective-permute-start(bf16[256,640]{1,0:T(8,128)(2,1)S(1)} %collective-permute-done.4.other), channel_id=1, source_target_pairs={{4,8},{8,4},{5,9},{9,5},{6,10},{10,6},{7,11},{11,7},{20,24},{24,20... | collective-permute-start | bytes 983048 | tf_op jit(solution)/shard_map/ppermute | solution.py:381
  24.7 9.6 %collective-permute-start.1 = (bf16[128,1280]{1,0:T(8,128)(2,1)S(1)}, bf16[128,1280]{1,0:T(8,128)(2,1)S(1)}, u32[]{:S(2)}, u32[]{:S(2)}) collective-permute-start(bf16[128,1280]{1,0:T(8,128)(2,1)S(1)} %get-tuple-element.38), channel_id=1, source_target_pairs={{0,1},{1,0},{2,3},{3,2},{4,5},{5,4},{6,7},{7,6},{8,9},{9,8},{10,11... | collective-permute-start | bytes 983048 | tf_op jit(solution)/shard_map/ppermute | solution.py:378
  30.3 9.4 %copy-start.3 = (bf16[256,640]{1,0:T(8,128)(2,1)}, bf16[256,640]{1,0:T(8,128)(2,1)S(1)}, u32[]{:S(2)}) copy-start(bf16[256,640]{1,0:T(8,128)(2,1)S(1)} %collective-permute-done.6.other.n1o) | copy-start | bytes 983044
  30.3 8.6 %collective-permute-start.12 = (bf16[256,640]{1,0:T(8,128)(2,1)S(1)}, bf16[256,640]{1,0:T(8,128)(2,1)S(1)}, u32[]{:S(2)}, u32[]{:S(2)}) collective-permute-start(bf16[256,640]{1,0:T(8,128)(2,1)S(1)} %collective-permute-done.2.other), channel_id=1, source_target_pairs={{0,4},{4,0},{8,12},{12,8},{1,5},{5,1},{9,13},{13,9},{2,6},{6,2},{1... | collective-permute-start | bytes 983048 | tf_op jit(solution)/shard_map/ppermute | solution.py:381
  32.1 7.7 %collective-permute-start.13 = (bf16[256,640]{1,0:T(8,128)(2,1)S(1)}, bf16[256,640]{1,0:T(8,128)(2,1)S(1)}, u32[]{:S(2)}, u32[]{:S(2)}) collective-permute-start(bf16[256,640]{1,0:T(8,128)(2,1)S(1)} %collective-permute-done.2.other), channel_id=1, source_target_pairs={{4,8},{8,4},{5,9},{9,5},{6,10},{10,6},{7,11},{11,7},{20,24},{24,20... | collective-permute-start | bytes 983048 | tf_op jit(solution)/shard_map/ppermute | solution.py:381
  32.9 11.0 %copy-start.5 = (bf16[256,640]{1,0:T(8,128)(2,1)}, bf16[256,640]{1,0:T(8,128)(2,1)S(1)}, u32[]{:S(2)}) copy-start(bf16[256,640]{1,0:T(8,128)(2,1)S(1)} %collective-permute-done.8.other.n2o) | copy-start | bytes 983044
  32.9 12.3 %collective-permute-start.9 = (bf16[256,640]{1,0:T(8,128)(2,1)S(1)}, bf16[256,640]{1,0:T(8,128)(2,1)}, u32[]{:S(2)}, u32[]{:S(2)}) collective-permute-start(bf16[256,640]{1,0:T(8,128)(2,1)S(1)} %shard_map.56), channel_id=1, source_target_pairs={{4,8},{8,4},{5,9},{9,5},{6,10},{10,6},{7,11},{11,7},{20,24},{24,20... | collective-permute-start | bytes 983048 | tf_op jit(solution)/shard_map/ppermute | solution.py:381
  39.8 8.9 %collective-permute-start.14 = (bf16[256,640]{1,0:T(8,128)(2,1)}, bf16[256,640]{1,0:T(8,128)(2,1)S(1)}, u32[]{:S(2)}, u32[]{:S(2)}) collective-permute-start(bf16[256,640]{1,0:T(8,128)(2,1)} %shard_map.59), channel_id=1, source_target_pairs={{4,8},{8,4},{5,9},{9,5},{6,10},{10,6},{7,11},{11,7},{20,24},{24,20... | collective-permute-start | bytes 983048 | tf_op jit(solution)/shard_map/ppermute | solution.py:381
  41.2 9.9 %collective-permute-start.3 = (bf16[256,640]{1,0:T(8,128)(2,1)}, bf16[256,640]{1,0:T(8,128)(2,1)}, u32[]{:S(2)}, u32[]{:S(2)}) collective-permute-start(bf16[256,640]{1,0:T(8,128)(2,1)} %pad_maximum_fusion.3), channel_id=1, source_target_pairs={{0,2},{1,3},{2,0},{3,1},{4,6},{5,7},{6,4},{7,5},{8,10},{9,11},{10,... | collective-permute-start | bytes 983048 | tf_op jit(solution)/shard_map/ppermute | solution.py:378
  43.9 19.1 %collective-permute-start.10 = (bf16[256,640]{1,0:T(8,128)(2,1)}, bf16[256,640]{1,0:T(8,128)(2,1)}, u32[]{:S(2)}, u32[]{:S(2)}) collective-permute-start(bf16[256,640]{1,0:T(8,128)(2,1)} %shard_map.57), channel_id=1, source_target_pairs={{4,0},{8,12},{5,1},{9,13},{6,2},{10,14},{7,3},{11,15},{20,16},{24,... | collective-permute-start | bytes 983048 | tf_op jit(solution)/shard_map/ppermute | solution.py:381
  45.2 24.8 %collective-permute-start.11 = (bf16[256,640]{1,0:T(8,128)(2,1)}, bf16[256,640]{1,0:T(8,128)(2,1)}, u32[]{:S(2)}, u32[]{:S(2)}) collective-permute-start(bf16[256,640]{1,0:T(8,128)(2,1)} %collective-permute-done.9.r1), channel_id=1, source_target_pairs={{4,0},{8,12},{5,1},{9,13},{6,2},{10,14},{7,3},{11,15},{20,16},{24,... | collective-permute-start | bytes 983048 | tf_op jit(solution)/shard_map/ppermute | solution.py:381
  47.4 32.1 %collective-permute-start.15 = (bf16[256,640]{1,0:T(8,128)(2,1)}, bf16[256,640]{1,0:T(8,128)(2,1)}, u32[]{:S(2)}, u32[]{:S(2)}) collective-permute-start(bf16[256,640]{1,0:T(8,128)(2,1)} %shard_map.60), channel_id=1, source_target_pairs={{4,0},{8,12},{5,1},{9,13},{6,2},{10,14},{7,3},{11,15},{20,16},{24,... | collective-permute-start | bytes 983048 | tf_op jit(solution)/shard_map/ppermute | solution.py:381
  48.8 30.7 %collective-permute-start.16 = (bf16[256,384]{1,0:T(8,128)(2,1)S(1)}, bf16[256,384]{1,0:T(8,128)(2,1)S(1)}, u32[]{:S(2)}, u32[]{:S(2)}) collective-permute-start(bf16[256,384]{1,0:T(8,128)(2,1)S(1)} %slice.33), channel_id=1, source_target_pairs={{4,0},{8,12},{5,1},{9,13},{6,2},{10,14},{7,3},{11,15},{20,16},{24,... | collective-permute-start | bytes 589832 | tf_op jit(solution)/shard_map/ppermute | solution.py:381
  51.1 33.5 %collective-permute-start.20 = (bf16[256,256]{1,0:T(8,128)(2,1)S(1)}, bf16[256,256]{1,0:T(8,128)(2,1)S(1)}, u32[]{:S(2)}, u32[]{:S(2)}) collective-permute-start(bf16[256,256]{1,0:T(8,128)(2,1)S(1)} %slice.34), channel_id=1, source_target_pairs={{4,0},{8,12},{5,1},{9,13},{6,2},{10,14},{7,3},{11,15},{20,16},{24,... | collective-permute-start | bytes 393224 | tf_op jit(solution)/shard_map/ppermute | solution.py:381
  70.0 1.0 %copy-start.4 = (bf16[256,640]{1,0:T(8,128)(2,1)S(1)}, bf16[256,640]{1,0:T(8,128)(2,1)}, u32[]{:S(2)}) copy-start(bf16[256,640]{1,0:T(8,128)(2,1)} %copy-done.3) | copy-start | bytes 983044
  71.0 1.0 %copy-start.6 = (bf16[256,640]{1,0:T(8,128)(2,1)S(1)}, bf16[256,640]{1,0:T(8,128)(2,1)}, u32[]{:S(2)}) copy-start(bf16[256,640]{1,0:T(8,128)(2,1)} %copy-done.5) | copy-start | bytes 983044
  72.0 1.0 %copy-start.10 = (bf16[256,640]{1,0:T(8,128)(2,1)S(1)}, bf16[256,640]{1,0:T(8,128)(2,1)}, u32[]{:S(2)}) copy-start(bf16[256,640]{1,0:T(8,128)(2,1)} %copy-done.9) | copy-start | bytes 983044
  82.7 5.2 %collective-permute-start.17 = (bf16[128,384]{1,0:T(8,128)(2,1)S(1)}, bf16[128,384]{1,0:T(8,128)(2,1)S(1)}, u32[]{:S(2)}, u32[]{:S(2)}) collective-permute-start(bf16[128,384]{1,0:T(8,128)(2,1)S(1)} %get-tuple-element.52), channel_id=1, source_target_pairs={{0,1},{1,0},{2,3},{3,2},{4,5},{5,4},{6,7},{7,6},{8,9},{9,8},{10,11... | collective-permute-start | bytes 294920 | tf_op jit(solution)/shard_map/ppermute | solution.py:378
  82.8 6.2 %collective-permute-start.18 = (bf16[128,384]{1,0:T(8,128)(2,1)S(1)}, bf16[128,384]{1,0:T(8,128)(2,1)S(1)}, u32[]{:S(2)}, u32[]{:S(2)}) collective-permute-start(bf16[128,384]{1,0:T(8,128)(2,1)S(1)} %get-tuple-element.53), channel_id=1, source_target_pairs={{0,2},{1,3},{2,0},{3,1},{4,6},{5,7},{6,4},{7,5},{8,10},{9,11},{10,... | collective-permute-start | bytes 294920 | tf_op jit(solution)/shard_map/ppermute | solution.py:378
  83.4 6.3 %collective-permute-start.19 = (bf16[128,384]{1,0:T(8,128)(2,1)S(1)}, bf16[128,384]{1,0:T(8,128)(2,1)S(1)}, u32[]{:S(2)}, u32[]{:S(2)}) collective-permute-start(bf16[128,384]{1,0:T(8,128)(2,1)S(1)} %get-tuple-element.54), channel_id=1, source_target_pairs={{0,3},{1,2},{2,1},{3,0},{4,7},{5,6},{6,5},{7,4},{8,11},{9,10},{10,... | collective-permute-start | bytes 294920 | tf_op jit(solution)/shard_map/ppermute | solution.py:378
  86.9 2.8 %collective-permute-start.21 = (bf16[128,256]{1,0:T(8,128)(2,1)S(1)}, bf16[128,256]{1,0:T(8,128)(2,1)S(1)}, u32[]{:S(2)}, u32[]{:S(2)}) collective-permute-start(bf16[128,256]{1,0:T(8,128)(2,1)S(1)} %get-tuple-element.56), channel_id=1, source_target_pairs={{0,1},{1,0},{2,3},{3,2},{4,5},{5,4},{6,7},{7,6},{8,9},{9,8},{10,11... | collective-permute-start | bytes 196616 | tf_op jit(solution)/shard_map/ppermute | solution.py:378
  87.3 4.9 %collective-permute-start.22 = (bf16[128,256]{1,0:T(8,128)(2,1)S(1)}, bf16[128,256]{1,0:T(8,128)(2,1)S(1)}, u32[]{:S(2)}, u32[]{:S(2)}) collective-permute-start(bf16[128,256]{1,0:T(8,128)(2,1)S(1)} %get-tuple-element.57), channel_id=1, source_target_pairs={{0,2},{1,3},{2,0},{3,1},{4,6},{5,7},{6,4},{7,5},{8,10},{9,11},{10,... | collective-permute-start | bytes 196616 | tf_op jit(solution)/shard_map/ppermute | solution.py:378
  88.0 4.5 %collective-permute-start.23 = (bf16[128,256]{1,0:T(8,128)(2,1)S(1)}, bf16[128,256]{1,0:T(8,128)(2,1)S(1)}, u32[]{:S(2)}, u32[]{:S(2)}) collective-permute-start(bf16[128,256]{1,0:T(8,128)(2,1)S(1)} %get-tuple-element.58), channel_id=1, source_target_pairs={{0,3},{1,2},{2,1},{3,0},{4,7},{5,6},{6,5},{7,4},{8,11},{9,10},{10,... | collective-permute-start | bytes 196616 | tf_op jit(solution)/shard_map/ppermute | solution.py:378
  92.2 0.8 copy-start.11

commit v7 on v5

--- a/solution.py
+++ b/solution.py
@@ -157,8 +157,6 @@
 
 INFO_ROWS = 16
 OUTER = [(0, 1), (1, 0), (2, 3), (3, 2)]
-INNER = [(1, 2), (2, 1)]
-OUTWARD = [(1, 0), (2, 3)]
 
 
 def fold(x):
@@ -226,28 +224,47 @@
         body(always + [(r2, near), (r3, mask[0, z ^ 3] == 1)])
 
 
-def values_kernel(weights, totals, mine, other, n1m, n1o, n2m, n2o, r1, r2, r3, *outs):
+def mixed_tiles(weights, at, values):
+    mixed = None
+    for n, v in enumerate(values):
+        tile = v.shape[0]
+        mix = jnp.dot(weights[:, (at + n) * tile : (at + n + 1) * tile], v[...], preferred_element_type=jnp.float32)
+        mixed = mix if mixed is None else mixed + mix
+    return mixed
+
+
+def values_kernel(weights, mine, other, n1m, n1o, n2m, n2o, r2, out):
+    tile = r2.shape[0]
+    always = [mine, other, n1m, n1o]
+    for half in range(2):
+        rows = slice(half * tile, (half + 1) * tile)
+
+        @pl.when(inner_frame())
+        def _():
+            out[rows] = mixed_tiles(weights.at[rows], 0, always + [n2m, n2o])
+
+        @pl.when(jnp.logical_not(inner_frame()))
+        def _():
+            out[rows] = mixed_tiles(weights.at[rows], 0, always + [r2])
+
+
+def last_kernel(weights, totals, partial, r1, r3, *outs):
+    rows = outs[0].shape[0]
     tile = r1.shape[0]
-    rows = outs[0].shape[0]
-    always = [mine, other, n1m, n1o]
-
-    def body(slots):
+
+    def body(at, value):
         for d, out in enumerate(outs):
             span = slice(d * rows, (d + 1) * rows)
-            mixed = None
-            for at, v in enumerate(slots):
-                w = weights[span, at * tile : (at + 1) * tile]
-                mix = jnp.dot(w, v[...], preferred_element_type=jnp.float32)
-                mixed = mix if mixed is None else mixed + mix
-            out[...] = (mixed / totals[span]).astype(jnp.bfloat16)
+            mix = jnp.dot(weights[span, at * tile : (at + 1) * tile], value[...], preferred_element_type=jnp.float32)
+            out[...] = ((partial[span] + mix) / totals[span]).astype(jnp.bfloat16)
 
     @pl.when(inner_frame())
     def _():
-        body(always + [n2m, n2o, r1])
+        body(6, r1)
 
     @pl.when(jnp.logical_not(inner_frame()))
     def _():
-        body(always + [r2, r3])
+        body(5, r3)
 
 
 def by_head(x, rows, first=0):
@@ -274,22 +291,35 @@
     )(mask, *[x for x, _ in blocks])
 
 
-def mix_values(weights, totals, values, heads):
+def mix_values(weights, totals, near, r1, r2, r3, heads):
     rows, lanes = weights.shape[0] // heads, weights.shape[1]
     tile = lanes // 7
-    blocks = [by_head(v, tile, first) for v, first in values]
-    return pl.pallas_call(
+    whole = weights, pl.BlockSpec((rows, lanes), lambda i: (i, 0))
+    blocks = [whole] + [by_head(v, tile, heads) for v in near] + [by_head(r2, tile)]
+    partial = pl.pallas_call(
         values_kernel,
         grid=(heads,),
-        in_specs=[pl.BlockSpec((rows, lanes), lambda i: (i, 0)), pl.BlockSpec((rows, HEAD_DIM), lambda i: (i, 0))]
-        + [spec for _, spec in blocks],
-        out_specs=[pl.BlockSpec((rows // 4, HEAD_DIM), lambda i: (0, i))] * 4,
-        out_shape=[jax.ShapeDtypeStruct((rows // 4, heads * HEAD_DIM), jnp.bfloat16)] * 4,
-        compiler_params=pltpu.CompilerParams(vmem_limit_bytes=16 * 1024 * 1024),
+        in_specs=[spec for _, spec in blocks],
+        out_specs=pl.BlockSpec((rows, HEAD_DIM), lambda i: (i, 0)),
+        out_shape=jax.ShapeDtypeStruct((heads * rows, HEAD_DIM), jnp.float32),
+        compiler_params=pltpu.CompilerParams(vmem_limit_bytes=12 * 1024 * 1024),
         cost_estimate=pl.CostEstimate(
             flops=heads * 2 * rows * lanes * HEAD_DIM, bytes_accessed=heads * 2 * rows * lanes, transcendentals=0
         ),
-    )(weights, totals, *[x for x, _ in blocks])
+    )(*[x for x, _ in blocks])
+    sums = [(x, pl.BlockSpec((rows, HEAD_DIM), lambda i: (i, 0))) for x in (totals, partial)]
+    blocks = [whole] + sums + [by_head(r1, tile), by_head(r3, tile)]
+    return pl.pallas_call(
+        last_kernel,
+        grid=(heads,),
+        in_specs=[spec for _, spec in blocks],
+        out_specs=[pl.BlockSpec((rows // 4, HEAD_DIM), lambda i: (0, i))] * 4,
+        out_shape=[jax.ShapeDtypeStruct((rows // 4, heads * HEAD_DIM), jnp.bfloat16)] * 4,
+        compiler_params=pltpu.CompilerParams(vmem_limit_bytes=12 * 1024 * 1024),
+        cost_estimate=pl.CostEstimate(
+            flops=heads * 2 * rows * tile * HEAD_DIM, bytes_accessed=heads * 2 * rows * lanes, transcendentals=0
+        ),
+    )(*[x for x, _ in blocks])
 
 
 def pack_kernel(copies, width, mask, offset, *refs):
@@ -382,6 +412,10 @@
     def along(array, pairs):
         return lax.ppermute(array, "frame", pairs)
 
+    def across(array):
+        pairs = [(4 * z + j, 4 * (3 - z) + j if z in (1, 2) else 4 * z + (j ^ 1)) for z in range(4) for j in range(4)]
+        return lax.ppermute(array, ("frame", "head"), pairs)
+
     def after(array, earlier):
         return lax.optimization_barrier((array, earlier))[0]
 
@@ -399,26 +433,26 @@
     mine = below(beside(*kv[0]), got[:, : 2 * width], told)
     other = to_head(below(beside(*kv[2]), got[:, 2 * width :]), 2)
     n1m = along(mine, OUTER)
-    n2m = along(mine, INNER)
+    n2m = across(mine)
     n1o = along(other, OUTER)
-    n2o = along(other, INNER)
+    n2o = across(other)
 
     got = to_head(after(pay, got), 1)
     q_mine = below(q_own, got[:, :width])
     q_other = to_head(after(below(q_far, got[:, width:]), other), 2)
 
     r1k, r1v = after(relayed(n1m, n1o), n2m)
-    r1k = along(r1k, INNER)
-    r1v = along(r1v, INNER)
+    r1k = across(r1k)
+    r1v = across(r1v)
     r2k, r2v = relayed(n2m, n2o)
-    r2k = along(r2k, OUTWARD)
-    r3k = along(r1k, OUTWARD)
-    r2v = along(after(r2v, r1k), OUTWARD)
-    r3v = along(r1v, OUTWARD)
+    r2k = along(r2k, OUTER)
+    r3k = along(r1k, OUTER)
+    r2v = along(after(r2v, r1k), OUTER)
+    r3v = along(r1v, OUTER)
 
     near = [mine, other, n1m, n1o, n2m, n2o]
     weights, totals = find_weights(pair_mask, q_mine, q_other, [*near, r1k, r2k, r3k], heads)
-    out = mix_values(weights, totals, [(x, heads) for x in near] + [(x, 0) for x in (r1v, r2v, r3v)], heads)
+    out = mix_values(weights, totals, near, r1v, r2v, r3v, heads)
     out = [out[0]] + [to_head(out[d], d) for d in (1, 2, 3)]
     result = jnp.zeros((rows, features), jnp.bfloat16)
     for d in range(4):

time: 91.5 us -> 84 us (0.918)
  waiting for transfers between devices: 59 us -> 41.9 us
  starting transfers between devices: 17.2 us -> 26.3 us
    ppermute x10 -> x6, waiting for transfers between devices: 35.6 us -> 20.6 us  [along(): return lax.ppermute(array, 'frame', pairs)]
    ppermute x10 -> x6, starting transfers between devices: 11.4 us -> 19.4 us  [along(): return lax.ppermute(array, 'frame', pairs)]
    ppermute x7, waiting for transfers between devices: 23.4 us -> 21.3 us  [to_head(): return lax.ppermute(array, 'head', [(i, i ^ d) for i in range(4)])]
    ppermute x0 -> x4, starting transfers between devices: none -> 1.13 us  [across(): return lax.ppermute(array, ('frame', 'head'), pairs)]
    pallas_call x1 -> x2, Pallas kernels: 3.94 us -> 4.65 us  [the longest x1 3.12 us: mix_values(): pl.pallas_call(values_kernel, grid=(heads,), in_specs=[spec for _, spec i...]
  transfers between devices with their start and end apart: 17 -> 17, of which waited for: 11 -> 9; matrix products, arithmetic and copies ran while one was open for 0% -> 0% of each run, Pallas kernels for 8% -> 13%
where the time goes in v7:
time: 84 us; the launch traced here: 83.9 us
  waiting for transfers between devices  41.9 us (50%)
  starting transfers between devices  26.3 us (31%)
  Pallas kernels  12.1 us (14%)
  local copies, waits for them, and re-layouts  2.42 us (3%)
  between operations  0.9 us (1%)
    ppermute x7, waiting for transfers between devices, to_head(): return lax.ppermute(array, 'head', [(i, i ^ d) for i in range(4)])  21.3 us
    ppermute x6, waiting for transfers between devices, along(): return lax.ppermute(array, 'frame', pairs)  20.6 us
    ppermute x6, starting transfers between devices, along(): return lax.ppermute(array, 'frame', pairs)  19.4 us
    pallas_call x1, Pallas kernels, find_weights(): pl.pallas_call(weights_kernel, grid=(heads,), in_specs=[pl.BlockSpec(memo...  6.41 us
    ppermute x7, starting transfers between devices, to_head(): return lax.ppermute(array, 'head', [(i, i ^ d) for i in range(4)])  5.81 us
    pallas_call x1, Pallas kernels, mix_values(): pl.pallas_call(values_kernel, grid=(heads,), in_specs=[spec for _, spec i...  3.12 us
  transfers between devices with their start and end apart: 17, of which 9 were waited for; matrix products, arithmetic and copies ran while one was open for 0% of the time, Pallas kernels for 13%

profile of v7, /device:TPU:0, one launch (start us, length us, event | category | flops | bytes accessed | tf_op | source)
XLA Modules:
  0.0 83.9 jit_solution(7237037851987892557)
XLA Ops:
  0.0 1.5 %constant_dynamic-slice_fusion = (bf16[128,640]{1,0:T(8,128)(2,1)S(1)}, bf16[128,640]{1,0:T(8,128)(2,1)S(1)}, bf16[128,640]{1,0:T(8,128)(2,1)S(1)}, bf16[128,640...) fusion(bf16[128,2560]{1,0:T(8,128)(2,1)} %refs_2_.1, ...), kind=kLoop, calls=%fused_computation.9 | loop fusion | bytes 2621456 | tf_op jit(solution)/shard_map/dynamic_slice | solution.py:401
  1.5 0.1 pad_maximum_fusion.1
  1.6 0.0 copy-start
  1.6 0.0 copy-start.1
  1.6 0.0 copy-start.2
  1.6 0.0 copy-start.3
  1.6 0.5 collective-permute-start
  2.1 1.7 %collective-permute-done = bf16[128,2560]{1,0:T(8,128)(2,1)S(1)} collective-permute-done((bf16[128,2560]{1,0:T(8,128)(2,1)S(1)}, bf16[128,2560]{1,0:T(8,128)(2,1)S(1)}, u32[]{:S(2)}, u32[]{:S(2)}) %collective-permute-start) | collective-permute-done | bytes 655392 | tf_op jit(solution)/shard_map/ppermute | solution.py:410
  4.0 2.9 %collective-permute-start.2 = (bf16[256,1280]{1,0:T(8,128)(2,1)S(1)}, bf16[256,1280]{1,0:T(8,128)(2,1)S(1)}, u32[]{:S(2)}, u32[]{:S(2)}) collective-permute-start(bf16[256,1280]{1,0:T(8,128)(2,1)S(1)} %pad_maximum_fusion.2), channel_id=1, source_target_pairs={{0,2},{1,3},{2,0},{3,1},{4,6},{5,7},{6,4},{7,5},{8,10},{9,11},{10,... | collective-permute-start | bytes 1966088 | tf_op jit(solution)/shard_map/ppermute | solution.py:410
  7.6 0.7 shard_map.55
  8.3 0.1 pad_maximum_fusion.mine
  8.3 1.6 %collective-permute-start.4 = (bf16[272,1280]{1,0:T(8,128)(2,1)S(1)}, bf16[272,1280]{1,0:T(8,128)(2,1)S(1)}, u32[]{:S(2)}, u32[]{:S(2)}) collective-permute-start(bf16[272,1280]{1,0:T(8,128)(2,1)S(1)} %pad_maximum_fusion.mine), channel_id=1, source_target_pairs={{0,4},{4,0},{8,12},{12,8},{1,5},{5,1},{9,13},{13,9},{2,6},{6,2},{1... | collective-permute-start | bytes 2088968 | tf_op jit(solution)/shard_map/ppermute | solution.py:413
  10.0 0.0 collective-permute-start.6
  10.0 12.0 %collective-permute-done.2.other = bf16[256,1280]{1,0:T(8,128)(2,1)S(1)} collective-permute-done((bf16[256,1280]{1,0:T(8,128)(2,1)S(1)}, bf16[256,1280]{1,0:T(8,128)(2,1)S(1)}, u32[]{:S(2)}, u32[]{:S(2)}) %collective-permute-start.2) | collective-permute-done | bytes 655392 | tf_op jit(solution)/shard_map/ppermute | solution.py:410
  21.9 1.8 %collective-permute-start.5 = (bf16[256,1280]{1,0:T(8,128)(2,1)S(1)}, bf16[256,1280]{1,0:T(8,128)(2,1)S(1)}, u32[]{:S(2)}, u32[]{:S(2)}) collective-permute-start(bf16[256,1280]{1,0:T(8,128)(2,1)S(1)} %collective-permute-done.2.other), channel_id=1, source_target_pairs={{0,4},{4,0},{8,12},{12,8},{1,5},{5,1},{9,13},{13,9},{2,6},{6,2},{1... | collective-permute-start | bytes 1966088 | tf_op jit(solution)/shard_map/ppermute | solution.py:413
  23.8 0.0 collective-permute-start.1
  23.8 0.5 collective-permute-start.7
  24.3 2.6 %collective-permute-done.4.mine.n1m = bf16[272,1280]{1,0:T(8,128)(2,1)S(1)} collective-permute-done((bf16[272,1280]{1,0:T(8,128)(2,1)S(1)}, bf16[272,1280]{1,0:T(8,128)(2,1)S(1)}, u32[]{:S(2)}, u32[]{:S(2)}) %collective-permute-start.4) | collective-permute-done | bytes 696352 | tf_op jit(solution)/shard_map/ppermute | solution.py:413
  26.9 12.9 %collective-permute-done.5.other.n1o = bf16[256,1280]{1,0:T(8,128)(2,1)S(1)} collective-permute-done((bf16[256,1280]{1,0:T(8,128)(2,1)S(1)}, bf16[256,1280]{1,0:T(8,128)(2,1)S(1)}, u32[]{:S(2)}, u32[]{:S(2)}) %collective-permute-start.5) | collective-permute-done | bytes 655392 | tf_op jit(solution)/shard_map/ppermute | solution.py:413
  39.8 0.2 shard_map.56
  40.0 0.0 collective-permute-done.6.mine.n2m
  40.0 0.1 collective-permute-start.8
  40.1 0.0 collective-permute-done.1
  40.1 0.5 collective-permute-start.12
  40.7 0.4 collective-permute-start.3
  41.2 0.0 collective-permute-done.7.other.n2o
  41.2 0.2 shard_map.57
  41.3 3.3 %collective-permute-start.9 = (bf16[256,640]{1,0:T(8,128)(2,1)S(1)}, bf16[256,640]{1,0:T(8,128)(2,1)S(1)}, u32[]{:S(2)}, u32[]{:S(2)}) collective-permute-start(bf16[256,640]{1,0:T(8,128)(2,1)S(1)} %get-tuple-element.49), channel_id=1, source_target_pairs={{0,4},{4,0},{8,12},{12,8},{1,5},{5,1},{9,13},{13,9},{2,6},{6,2},{1... | collective-permute-start | bytes 983048 | tf_op jit(solution)/shard_map/ppermute | solution.py:413
  44.7 7.7 %collective-permute-start.10 = (bf16[256,640]{1,0:T(8,128)(2,1)S(1)}, bf16[256,640]{1,0:T(8,128)(2,1)S(1)}, u32[]{:S(2)}, u32[]{:S(2)}) collective-permute-start(bf16[256,640]{1,0:T(8,128)(2,1)S(1)} %collective-permute-done.8.r1), channel_id=1, source_target_pairs={{0,4},{4,0},{8,12},{12,8},{1,5},{5,1},{9,13},{13,9},{2,6},{6,2},{1... | collective-permute-start | bytes 983048 | tf_op jit(solution)/shard_map/ppermute | solution.py:413
  52.3 0.0 collective-permute-start.11
  52.3 0.0 collective-permute-done.12.r1
  52.4 4.9 %collective-permute-start.13 = (bf16[256,640]{1,0:T(8,128)(2,1)S(1)}, bf16[256,640]{1,0:T(8,128)(2,1)S(1)}, u32[]{:S(2)}, u32[]{:S(2)}) collective-permute-start(bf16[256,640]{1,0:T(8,128)(2,1)S(1)} %collective-permute-done.12.r1), channel_id=1, source_target_pairs={{0,4},{4,0},{8,12},{12,8},{1,5},{5,1},{9,13},{13,9},{2,6},{6,2},{1... | collective-permute-start | bytes 983048 | tf_op jit(solution)/shard_map/ppermute | solution.py:413
  57.3 0.0 collective-permute-done.3.q_other
  57.3 0.0 collective-permute-done.9.r2
  57.3 3.6 %collective-permute-done.10.r3 = bf16[256,640]{1,0:T(8,128)(2,1)S(1)} collective-permute-done((bf16[256,640]{1,0:T(8,128)(2,1)S(1)}, bf16[256,640]{1,0:T(8,128)(2,1)S(1)}, u32[]{:S(2)}, u32[]{:S(2)}) %collective-permute-start.10) | collective-permute-done | bytes 327712 | tf_op jit(solution)/shard_map/ppermute | solution.py:413
  60.9 6.4 %shard_map.58 = (bf16[2560,1792]{1,0:T(8,128)(2,1)S(1)}, f32[2560,128]{1,0:T(8,128)S(1)}) custom-call(s32[1,4]{1,0:T(1,128)S(1)} %copy-done.3, bf16[256,640]{1,0:T(8,128)(2,1)S(1)} %pad_maximum_fusion.3.q_mine, bf16[256,640]{1,0:T(8,128)(2,1)S(1)} %collective-permute-done.3.q_other, bf16[272,1280]{1,0:T(8,128)(2,1)S(1)} %pad_maximum_fusion.mine, ...), custom_call_target="tpu_custom_call" | custom-call | flops 1174405120 | bytes 9175040 | tf_op jit(solution)/shard_map/pallas_call | solution.py:278
  67.4 0.6 collective-permute-done.11.r2
  68.0 3.1 %shard_map.59.partial = f32[2560,128]{1,0:T(8,128)S(1)} custom-call(bf16[2560,1792]{1,0:T(8,128)(2,1)S(1)} %get-tuple-element.50.weights, bf16[272,1280]{1,0:T(8,128)(2,1)S(1)} %pad_maximum_fusion.mine, bf16[256,1280]{1,0:T(8,128)(2,1)S(1)} %collective-permute-done.2.other, bf16[272,1280]{1,0:T(8,128)(2,1)S(1)} %collective-permute-done.4.mine.n1m, ...), custom_call_target="tpu_custom_call" | custom-call | flops 1174405120 | bytes 9175040 | tf_op jit(solution)/shard_map/pallas_call | solution.py:299
  71.1 0.8 collective-permute-done.13.r3
  71.9 1.5 %shard_map.60 = (bf16[128,640]{1,0:T(8,128)(2,1)S(1)}, bf16[128,640]{1,0:T(8,128)(2,1)S(1)}, bf16[128,640]{1,0:T(8,128)(2,1)S(1)}, bf16[128,640]{1,0:T(8,128)(2,1)S(1)}) custom-call(bf16[2560,1792]{1,0:T(8,128)(2,1)S(1)} %get-tuple-element.50.weights, f32[2560,128]{1,0:T(8,128)S(1)} %get-tuple-element.51.totals, f32[2560,128]{1,0:T(8,128)S(1)} %shard_map.59.partial, ...), custom_call_target="tpu_custom_call" | custom-call | flops 167772160 | bytes 9175040 | tf_op jit(solution)/shard_map/pallas_call | solution.py:312
  73.4 0.1 collective-permute-start.14
  73.5 1.7 %collective-permute-start.15 = (bf16[128,640]{1,0:T(8,128)(2,1)S(1)}, bf16[128,640]{1,0:T(8,128)(2,1)S(1)}, u32[]{:S(2)}, u32[]{:S(2)}) collective-permute-start(bf16[128,640]{1,0:T(8,128)(2,1)S(1)} %get-tuple-element.57), channel_id=1, source_target_pairs={{0,2},{1,3},{2,0},{3,1},{4,6},{5,7},{6,4},{7,5},{8,10},{9,11},{10,... | collective-permute-start | bytes 491528 | tf_op jit(solution)/shard_map/ppermute | solution.py:410
  75.2 0.2 collective-permute-start.16
  75.4 0.0 collective-permute-done.14
  75.5 5.1 %collective-permute-done.15 = bf16[128,640]{1,0:T(8,128)(2,1)S(1)} collective-permute-done((bf16[128,640]{1,0:T(8,128)(2,1)S(1)}, bf16[128,640]{1,0:T(8,128)(2,1)S(1)}, u32[]{:S(2)}, u32[]{:S(2)}) %collective-permute-start.15) | collective-permute-done | bytes 163872 | tf_op jit(solution)/shard_map/ppermute | solution.py:410
  80.6 0.0 copy-start.4
  80.6 2.6 %collective-permute-done.16 = bf16[128,640]{1,0:T(8,128)(2,1)S(1)} collective-permute-done((bf16[128,640]{1,0:T(8,128)(2,1)S(1)}, bf16[128,640]{1,0:T(8,128)(2,1)S(1)}, u32[]{:S(2)}, u32[]{:S(2)}) %collective-permute-start.16) | collective-permute-done | bytes 163872 | tf_op jit(solution)/shard_map/ppermute | solution.py:410
  83.2 0.7 constant_dynamic-update-slice_fusion
  (15 shorter events, 0.3 us)
Async XLA Ops:
  1.6 6.0 %copy-start = (bf16[128,2560]{1,0:T(8,128)(2,1)S(1)}, bf16[128,2560]{1,0:T(8,128)(2,1)}, u32[]{:S(2)}) copy-start(bf16[128,2560]{1,0:T(8,128)(2,1)} %refs_1_.1) | copy-start | bytes 1966084
  1.6 6.0 %copy-start.1 = (bf16[128,2560]{1,0:T(8,128)(2,1)S(1)}, bf16[128,2560]{1,0:T(8,128)(2,1)}, u32[]{:S(2)}) copy-start(bf16[128,2560]{1,0:T(8,128)(2,1)} %refs_2_.1) | copy-start | bytes 1966084
  1.6 6.0 %copy-start.2 = (bf16[128,2560]{1,0:T(8,128)(2,1)S(1)}, bf16[128,2560]{1,0:T(8,128)(2,1)}, u32[]{:S(2)}) copy-start(bf16[128,2560]{1,0:T(8,128)(2,1)} %refs_0_.1) | copy-start | bytes 1966084
  1.6 6.0 %copy-start.3 = (s32[1,4]{1,0:T(1,128)S(1)}, s32[1,4]{1,0:T(1,128)}, u32[]{:S(2)}) copy-start(s32[1,4]{1,0:T(1,128)} %mask.3) | copy-start | bytes 52
  1.6 2.2 %collective-permute-start = (bf16[128,2560]{1,0:T(8,128)(2,1)S(1)}, bf16[128,2560]{1,0:T(8,128)(2,1)S(1)}, u32[]{:S(2)}, u32[]{:S(2)}) collective-permute-start(bf16[128,2560]{1,0:T(8,128)(2,1)S(1)} %pad_maximum_fusion.1), channel_id=1, source_target_pairs={{0,1},{1,0},{2,3},{3,2},{4,5},{5,4},{6,7},{7,6},{8,9},{9,8},{10,11... | collective-permute-start | bytes 1966088 | tf_op jit(solution)/shard_map/ppermute | solution.py:410
  4.0 18.0 %collective-permute-start.2 = (bf16[256,1280]{1,0:T(8,128)(2,1)S(1)}, bf16[256,1280]{1,0:T(8,128)(2,1)S(1)}, u32[]{:S(2)}, u32[]{:S(2)}) collective-permute-start(bf16[256,1280]{1,0:T(8,128)(2,1)S(1)} %pad_maximum_fusion.2), channel_id=1, source_target_pairs={{0,2},{1,3},{2,0},{3,1},{4,6},{5,7},{6,4},{7,5},{8,10},{9,11},{10,... | collective-permute-start | bytes 1966088 | tf_op jit(solution)/shard_map/ppermute | solution.py:410
  8.3 18.6 %collective-permute-start.4 = (bf16[272,1280]{1,0:T(8,128)(2,1)S(1)}, bf16[272,1280]{1,0:T(8,128)(2,1)S(1)}, u32[]{:S(2)}, u32[]{:S(2)}) collective-permute-start(bf16[272,1280]{1,0:T(8,128)(2,1)S(1)} %pad_maximum_fusion.mine), channel_id=1, source_target_pairs={{0,4},{4,0},{8,12},{12,8},{1,5},{5,1},{9,13},{13,9},{2,6},{6,2},{1... | collective-permute-start | bytes 2088968 | tf_op jit(solution)/shard_map/ppermute | solution.py:413
  10.0 30.0 %collective-permute-start.6 = (bf16[272,1280]{1,0:T(8,128)(2,1)S(1)}, bf16[272,1280]{1,0:T(8,128)(2,1)S(1)}, u32[]{:S(2)}, u32[]{:S(2)}) collective-permute-start(bf16[272,1280]{1,0:T(8,128)(2,1)S(1)} %pad_maximum_fusion.mine), channel_id=1, source_target_pairs={{0,1},{1,0},{2,3},{3,2},{4,8},{5,9},{6,10},{7,11},{8,4},{9,5},{10,... | collective-permute-start | bytes 2088968 | tf_op jit(solution)/shard_map/ppermute | solution.py:417
  21.9 17.9 %collective-permute-start.5 = (bf16[256,1280]{1,0:T(8,128)(2,1)S(1)}, bf16[256,1280]{1,0:T(8,128)(2,1)S(1)}, u32[]{:S(2)}, u32[]{:S(2)}) collective-permute-start(bf16[256,1280]{1,0:T(8,128)(2,1)S(1)} %collective-permute-done.2.other), channel_id=1, source_target_pairs={{0,4},{4,0},{8,12},{12,8},{1,5},{5,1},{9,13},{13,9},{2,6},{6,2},{1... | collective-permute-start | bytes 1966088 | tf_op jit(solution)/shard_map/ppermute | solution.py:413
  23.8 16.3 %collective-permute-start.1 = (bf16[128,1280]{1,0:T(8,128)(2,1)S(1)}, bf16[128,1280]{1,0:T(8,128)(2,1)S(1)}, u32[]{:S(2)}, u32[]{:S(2)}) collective-permute-start(bf16[128,1280]{1,0:T(8,128)(2,1)S(1)} %get-tuple-element.38), channel_id=1, source_target_pairs={{0,1},{1,0},{2,3},{3,2},{4,5},{5,4},{6,7},{7,6},{8,9},{9,8},{10,11... | collective-permute-start | bytes 983048 | tf_op jit(solution)/shard_map/ppermute | solution.py:410
  23.8 17.4 %collective-permute-start.7 = (bf16[256,1280]{1,0:T(8,128)(2,1)S(1)}, bf16[256,1280]{1,0:T(8,128)(2,1)S(1)}, u32[]{:S(2)}, u32[]{:S(2)}) collective-permute-start(bf16[256,1280]{1,0:T(8,128)(2,1)S(1)} %collective-permute-done.2.other), channel_id=1, source_target_pairs={{0,1},{1,0},{2,3},{3,2},{4,8},{5,9},{6,10},{7,11},{8,4},{9,5},{10,... | collective-permute-start | bytes 1966088 | tf_op jit(solution)/shard_map/ppermute | solution.py:417
  40.0 4.7 %collective-permute-start.8 = (bf16[256,640]{1,0:T(8,128)(2,1)S(1)}, bf16[256,640]{1,0:T(8,128)(2,1)S(1)}, u32[]{:S(2)}, u32[]{:S(2)}) collective-permute-start(bf16[256,640]{1,0:T(8,128)(2,1)S(1)} %get-tuple-element.48), channel_id=1, source_target_pairs={{0,1},{1,0},{2,3},{3,2},{4,8},{5,9},{6,10},{7,11},{8,4},{9,5},{10,... | collective-permute-start | bytes 983048 | tf_op jit(solution)/shard_map/ppermute | solution.py:417
  40.1 12.2 %collective-permute-start.12 = (bf16[256,640]{1,0:T(8,128)(2,1)S(1)}, bf16[256,640]{1,0:T(8,128)(2,1)S(1)}, u32[]{:S(2)}, u32[]{:S(2)}) collective-permute-start(bf16[256,640]{1,0:T(8,128)(2,1)S(1)} %get-tuple-element.54), channel_id=1, source_target_pairs={{0,1},{1,0},{2,3},{3,2},{4,8},{5,9},{6,10},{7,11},{8,4},{9,5},{10,... | collective-permute-start | bytes 983048 | tf_op jit(solution)/shard_map/ppermute | solution.py:417
  40.7 16.6 %collective-permute-start.3 = (bf16[256,640]{1,0:T(8,128)(2,1)S(1)}, bf16[256,640]{1,0:T(8,128)(2,1)S(1)}, u32[]{:S(2)}, u32[]{:S(2)}) collective-permute-start(bf16[256,640]{1,0:T(8,128)(2,1)S(1)} %pad_maximum_fusion.4), channel_id=1, source_target_pairs={{0,2},{1,3},{2,0},{3,1},{4,6},{5,7},{6,4},{7,5},{8,10},{9,11},{10,... | collective-permute-start | bytes 983048 | tf_op jit(solution)/shard_map/ppermute | solution.py:410
  41.3 16.0 %collective-permute-start.9 = (bf16[256,640]{1,0:T(8,128)(2,1)S(1)}, bf16[256,640]{1,0:T(8,128)(2,1)S(1)}, u32[]{:S(2)}, u32[]{:S(2)}) collective-permute-start(bf16[256,640]{1,0:T(8,128)(2,1)S(1)} %get-tuple-element.49), channel_id=1, source_target_pairs={{0,4},{4,0},{8,12},{12,8},{1,5},{5,1},{9,13},{13,9},{2,6},{6,2},{1... | collective-permute-start | bytes 983048 | tf_op jit(solution)/shard_map/ppermute | solution.py:413
  44.7 16.3 %collective-permute-start.10 = (bf16[256,640]{1,0:T(8,128)(2,1)S(1)}, bf16[256,640]{1,0:T(8,128)(2,1)S(1)}, u32[]{:S(2)}, u32[]{:S(2)}) collective-permute-start(bf16[256,640]{1,0:T(8,128)(2,1)S(1)} %collective-permute-done.8.r1), channel_id=1, source_target_pairs={{0,4},{4,0},{8,12},{12,8},{1,5},{5,1},{9,13},{13,9},{2,6},{6,2},{1... | collective-permute-start | bytes 983048 | tf_op jit(solution)/shard_map/ppermute | solution.py:413
  52.3 15.6 %collective-permute-start.11 = (bf16[256,640]{1,0:T(8,128)(2,1)S(1)}, bf16[256,640]{1,0:T(8,128)(2,1)S(1)}, u32[]{:S(2)}, u32[]{:S(2)}) collective-permute-start(bf16[256,640]{1,0:T(8,128)(2,1)S(1)} %get-tuple-element.53), channel_id=1, source_target_pairs={{0,4},{4,0},{8,12},{12,8},{1,5},{5,1},{9,13},{13,9},{2,6},{6,2},{1... | collective-permute-start | bytes 983048 | tf_op jit(solution)/shard_map/ppermute | solution.py:413
  52.4 19.5 %collective-permute-start.13 = (bf16[256,640]{1,0:T(8,128)(2,1)S(1)}, bf16[256,640]{1,0:T(8,128)(2,1)S(1)}, u32[]{:S(2)}, u32[]{:S(2)}) collective-permute-start(bf16[256,640]{1,0:T(8,128)(2,1)S(1)} %collective-permute-done.12.r1), channel_id=1, source_target_pairs={{0,4},{4,0},{8,12},{12,8},{1,5},{5,1},{9,13},{13,9},{2,6},{6,2},{1... | collective-permute-start | bytes 983048 | tf_op jit(solution)/shard_map/ppermute | solution.py:413
  73.4 2.0 %collective-permute-start.14 = (bf16[128,640]{1,0:T(8,128)(2,1)S(1)}, bf16[128,640]{1,0:T(8,128)(2,1)S(1)}, u32[]{:S(2)}, u32[]{:S(2)}) collective-permute-start(bf16[128,640]{1,0:T(8,128)(2,1)S(1)} %get-tuple-element.56), channel_id=1, source_target_pairs={{0,1},{1,0},{2,3},{3,2},{4,5},{5,4},{6,7},{7,6},{8,9},{9,8},{10,11... | collective-permute-start | bytes 491528 | tf_op jit(solution)/shard_map/ppermute | solution.py:410
  73.5 7.1 %collective-permute-start.15 = (bf16[128,640]{1,0:T(8,128)(2,1)S(1)}, bf16[128,640]{1,0:T(8,128)(2,1)S(1)}, u32[]{:S(2)}, u32[]{:S(2)}) collective-permute-start(bf16[128,640]{1,0:T(8,128)(2,1)S(1)} %get-tuple-element.57), channel_id=1, source_target_pairs={{0,2},{1,3},{2,0},{3,1},{4,6},{5,7},{6,4},{7,5},{8,10},{9,11},{10,... | collective-permute-start | bytes 491528 | tf_op jit(solution)/shard_map/ppermute | solution.py:410
  75.2 8.0 %collective-permute-start.16 = (bf16[128,640]{1,0:T(8,128)(2,1)S(1)}, bf16[128,640]{1,0:T(8,128)(2,1)S(1)}, u32[]{:S(2)}, u32[]{:S(2)}) collective-permute-start(bf16[128,640]{1,0:T(8,128)(2,1)S(1)} %get-tuple-element.58), channel_id=1, source_target_pairs={{0,3},{1,2},{2,1},{3,0},{4,7},{5,6},{6,5},{7,4},{8,11},{9,10},{10,... | collective-permute-start | bytes 491528 | tf_op jit(solution)/shard_map/ppermute | solution.py:410
  80.6 2.6 %copy-start.4 = (bf16[128,2560]{1,0:T(8,128)(2,1)}, bf16[128,2560]{1,0:T(8,128)(2,1)S(1)}, u32[]{:S(2)}) copy-start(bf16[128,2560]{1,0:T(8,128)(2,1)S(1)} %constant_dynamic-update-slice_fusion.1) | copy-start | bytes 1966084

commit v8 on v7

--- a/solution.py
+++ b/solution.py
@@ -233,38 +233,37 @@
     return mixed
 
 
-def values_kernel(weights, mine, other, n1m, n1o, n2m, n2o, r2, out):
-    tile = r2.shape[0]
-    always = [mine, other, n1m, n1o]
+def near_kernel(weights, mine, other, n1m, n1o, n2m, n2o, out):
+    tile = n1o.shape[0]
+    near = [mine, other, n1m, n1o]
     for half in range(2):
         rows = slice(half * tile, (half + 1) * tile)
 
         @pl.when(inner_frame())
         def _():
-            out[rows] = mixed_tiles(weights.at[rows], 0, always + [n2m, n2o])
+            out[rows] = mixed_tiles(weights.at[rows], 0, near + [n2m, n2o])
 
         @pl.when(jnp.logical_not(inner_frame()))
         def _():
-            out[rows] = mixed_tiles(weights.at[rows], 0, always + [r2])
-
-
-def last_kernel(weights, totals, partial, r1, r3, *outs):
+            out[rows] = mixed_tiles(weights.at[rows], 0, near)
+
+
+def far_kernel(weights, totals, near, r1, r2, r3, *outs):
     rows = outs[0].shape[0]
-    tile = r1.shape[0]
-
-    def body(at, value):
+
+    def body(at, values):
         for d, out in enumerate(outs):
             span = slice(d * rows, (d + 1) * rows)
-            mix = jnp.dot(weights[span, at * tile : (at + 1) * tile], value[...], preferred_element_type=jnp.float32)
-            out[...] = ((partial[span] + mix) / totals[span]).astype(jnp.bfloat16)
+            mixed = near[span] + mixed_tiles(weights.at[span], at, values)
+            out[...] = (mixed / totals[span]).astype(jnp.bfloat16)
 
     @pl.when(inner_frame())
     def _():
-        body(6, r1)
+        body(6, [r1])
 
     @pl.when(jnp.logical_not(inner_frame()))
     def _():
-        body(5, r3)
+        body(4, [r2, r3])
 
 
 def by_head(x, rows, first=0):
@@ -291,13 +290,11 @@
     )(mask, *[x for x, _ in blocks])
 
 
-def mix_values(weights, totals, near, r1, r2, r3, heads):
+def mix_near(weights, near, heads):
     rows, lanes = weights.shape[0] // heads, weights.shape[1]
-    tile = lanes // 7
-    whole = weights, pl.BlockSpec((rows, lanes), lambda i: (i, 0))
-    blocks = [whole] + [by_head(v, tile, heads) for v in near] + [by_head(r2, tile)]
-    partial = pl.pallas_call(
-        values_kernel,
+    blocks = [(weights, pl.BlockSpec((rows, lanes), lambda i: (i, 0)))] + [by_head(v, rows // 2, heads) for v in near]
+    return pl.pallas_call(
+        near_kernel,
         grid=(heads,),
         in_specs=[spec for _, spec in blocks],
         out_specs=pl.BlockSpec((rows, HEAD_DIM), lambda i: (i, 0)),
@@ -307,17 +304,27 @@
             flops=heads * 2 * rows * lanes * HEAD_DIM, bytes_accessed=heads * 2 * rows * lanes, transcendentals=0
         ),
     )(*[x for x, _ in blocks])
-    sums = [(x, pl.BlockSpec((rows, HEAD_DIM), lambda i: (i, 0))) for x in (totals, partial)]
-    blocks = [whole] + sums + [by_head(r1, tile), by_head(r3, tile)]
+
+
+def add_far(weights, totals, mixed, r1, r2, r3, begin, end):
+    lanes = weights.shape[1]
+    tile = r1.shape[0]
+    rows = 2 * tile
+    heads = end - begin
+    blocks = [
+        (x, pl.BlockSpec((rows, width), lambda i: (begin + i, 0)))
+        for x, width in ((weights, lanes), (totals, HEAD_DIM), (mixed, HEAD_DIM))
+    ]
+    blocks += [by_head(r1, tile, begin), by_head(r2, tile), by_head(r3, tile)]
     return pl.pallas_call(
-        last_kernel,
+        far_kernel,
         grid=(heads,),
         in_specs=[spec for _, spec in blocks],
         out_specs=[pl.BlockSpec((rows // 4, HEAD_DIM), lambda i: (0, i))] * 4,
         out_shape=[jax.ShapeDtypeStruct((rows // 4, heads * HEAD_DIM), jnp.bfloat16)] * 4,
         compiler_params=pltpu.CompilerParams(vmem_limit_bytes=12 * 1024 * 1024),
         cost_estimate=pl.CostEstimate(
-            flops=heads * 2 * rows * tile * HEAD_DIM, bytes_accessed=heads * 2 * rows * lanes, transcendentals=0
+            flops=heads * 4 * rows * tile * HEAD_DIM, bytes_accessed=heads * 2 * rows * lanes, transcendentals=0
         ),
     )(*[x for x, _ in blocks])
 
@@ -443,20 +450,30 @@
 
     r1k, r1v = after(relayed(n1m, n1o), n2m)
     r1k = across(r1k)
-    r1v = across(r1v)
+    r1v = across(after(r1v, n2o))
     r2k, r2v = relayed(n2m, n2o)
     r2k = along(r2k, OUTER)
-    r3k = along(r1k, OUTER)
-    r2v = along(after(r2v, r1k), OUTER)
-    r3v = along(r1v, OUTER)
-
+    r3k = along(after(r1k, r2k), OUTER)
+
+    cut = (heads + 1) // 2
+    groups = [slice(0, cut * HEAD_DIM), slice(cut * HEAD_DIM, width)]
+    far2 = along(r2v[:, groups[0]], OUTER)
+    far3 = along(r1v[:, groups[0]], OUTER)
     near = [mine, other, n1m, n1o, n2m, n2o]
-    weights, totals = find_weights(pair_mask, q_mine, q_other, [*near, r1k, r2k, r3k], heads)
-    out = mix_values(weights, totals, near, r1v, r2v, r3v, heads)
-    out = [out[0]] + [to_head(out[d], d) for d in (1, 2, 3)]
+    weights, totals = find_weights(
+        pair_mask, q_mine, q_other, [*near, r1k, r2k, after(r3k, far2)], heads
+    )
+    both = along(after(below(r2v[:, groups[1]], r1v[:, groups[1]]), totals), OUTER)
+    mixed = mix_near(after(weights, far3), near, heads)
     result = jnp.zeros((rows, features), jnp.bfloat16)
-    for d in range(4):
-        result = lax.dynamic_update_slice_in_dim(result, out[d], (h ^ d) * width, axis=1)
+    pieces = []
+    for begin, end, tiles in ((0, cut, (far2, far3)), (cut, heads, (both[: 2 * rows], both[2 * rows :]))):
+        out = add_far(weights, totals, mixed, r1v, *tiles, begin, end)
+        moved = [out[0]] + [to_head(out[d], d) for d in (1, 2, 3)]
+        pieces = [(after(piece, moved[1]) if d else piece, d, at) for piece, d, at in pieces]
+        pieces += [(piece, d, begin) for d, piece in enumerate(moved)]
+    for piece, d, begin in pieces:
+        result = lax.dynamic_update_slice_in_dim(result, piece, (h ^ d) * width + begin * HEAD_DIM, axis=1)
     return result
 
 

time: 84 us -> 99.9 us (1.19)
  local copies, waits for them, and re-layouts: 2.42 us -> 16.8 us
  waiting for transfers between devices: 41.9 us -> 43.1 us
  starting transfers between devices: 26.3 us -> 25.3 us
    unnamed x10 -> x32, local copies, waits for them, and re-layouts: 0.03 us -> 12.7 us
    ppermute x6 -> x7, waiting for transfers between devices: 20.6 us -> 25.6 us  [along(): return lax.ppermute(array, 'frame', pairs)]
    ppermute x7 -> x10, waiting for transfers between devices: 21.3 us -> 17.5 us  [to_head(): return lax.ppermute(array, 'head', [(i, i ^ d) for i in range(4)])]
    ppermute x6 -> x7, starting transfers between devices: 19.4 us -> 16.7 us  [along(): return lax.ppermute(array, 'frame', pairs)]
    ppermute x7 -> x10, starting transfers between devices: 5.81 us -> 8.08 us  [to_head(): return lax.ppermute(array, 'head', [(i, i ^ d) for i in range(4)])]
    slice x0 -> x5, local copies, waits for them, and re-layouts: none -> 1.72 us  [the longest x1 0.99 us: four_frames(): both[2 * rows:]]
    pallas_call x2 -> x3, Pallas kernels: 4.65 us -> 4.74 us  [the longest x1 2.68 us: mix_near(): pl.pallas_call(near_kernel, grid=(heads,), in_specs=[spec for _, spec in...]
  transfers between devices with their start and end apart: 17 -> 21, of which waited for: 9 -> 10; matrix products, arithmetic and copies ran while one was open for 0% -> 3% of each run, Pallas kernels for 13% -> 12%
where the time goes in v8:
time: 99.9 us; the launch traced here: 99.5 us
  waiting for transfers between devices  43.1 us (43%)
  starting transfers between devices  25.3 us (25%)
  local copies, waits for them, and re-layouts  16.8 us (17%)
  Pallas kernels  12.2 us (12%)
  between operations  1 us (1%)
    ppermute x7, waiting for transfers between devices, along(): return lax.ppermute(array, 'frame', pairs)  25.6 us
    ppermute x10, waiting for transfers between devices, to_head(): return lax.ppermute(array, 'head', [(i, i ^ d) for i in range(4)])  17.5 us
    ppermute x7, starting transfers between devices, along(): return lax.ppermute(array, 'frame', pairs)  16.7 us
    unnamed x32, local copies, waits for them, and re-layouts  12.7 us
    ppermute x10, starting transfers between devices, to_head(): return lax.ppermute(array, 'head', [(i, i ^ d) for i in range(4)])  8.08 us
    pallas_call x1, Pallas kernels, find_weights(): pl.pallas_call(weights_kernel, grid=(heads,), in_specs=[pl.BlockSpec(memo...  6.44 us
    pallas_call x1, Pallas kernels, mix_near(): pl.pallas_call(near_kernel, grid=(heads,), in_specs=[spec for _, spec in...  2.68 us
    pallas_call x2, Pallas kernels, add_far(): pl.pallas_call(far_kernel, grid=(heads,), in_specs=[spec for _, spec in b...  2.06 us
  transfers between devices with their start and end apart: 21, of which 10 were waited for; matrix products, arithmetic and copies ran while one was open for 3% of the time, Pallas kernels for 12%

profile of v8, /device:TPU:0, one launch (start us, length us, event | category | flops | bytes accessed | tf_op | source)
XLA Modules:
  0.0 99.5 jit_solution(754572511812767056)
XLA Ops:
  0.0 1.5 %constant_dynamic-slice_fusion = (bf16[128,640]{1,0:T(8,128)(2,1)S(1)}, bf16[128,640]{1,0:T(8,128)(2,1)S(1)}, bf16[128,640]{1,0:T(8,128)(2,1)S(1)}, bf16[128,640...) fusion(bf16[128,2560]{1,0:T(8,128)(2,1)} %refs_2_.1, ...), kind=kLoop, calls=%fused_computation.14 | loop fusion | bytes 2621456 | tf_op jit(solution)/shard_map/dynamic_slice | solution.py:408
  1.6 0.5 collective-permute-start
  2.1 1.7 %collective-permute-done = bf16[128,2560]{1,0:T(8,128)(2,1)S(1)} collective-permute-done((bf16[128,2560]{1,0:T(8,128)(2,1)S(1)}, bf16[128,2560]{1,0:T(8,128)(2,1)S(1)}, u32[]{:S(2)}, u32[]{:S(2)}) %collective-permute-start) | collective-permute-done | bytes 655392 | tf_op jit(solution)/shard_map/ppermute | solution.py:417
  4.0 2.9 %collective-permute-start.2 = (bf16[256,1280]{1,0:T(8,128)(2,1)S(1)}, bf16[256,1280]{1,0:T(8,128)(2,1)S(1)}, u32[]{:S(2)}, u32[]{:S(2)}) collective-permute-start(bf16[256,1280]{1,0:T(8,128)(2,1)S(1)} %pad_maximum_fusion.2), channel_id=1, source_target_pairs={{0,2},{1,3},{2,0},{3,1},{4,6},{5,7},{6,4},{7,5},{8,10},{9,11},{10,... | collective-permute-start | bytes 1966088 | tf_op jit(solution)/shard_map/ppermute | solution.py:417
  7.6 0.7 shard_map.55
  8.3 1.6 %collective-permute-start.4 = (bf16[272,1280]{1,0:T(8,128)(2,1)S(1)}, bf16[272,1280]{1,0:T(8,128)(2,1)S(1)}, u32[]{:S(2)}, u32[]{:S(2)}) collective-permute-start(bf16[272,1280]{1,0:T(8,128)(2,1)S(1)} %pad_maximum_fusion.mine), channel_id=1, source_target_pairs={{0,4},{4,0},{8,12},{12,8},{1,5},{5,1},{9,13},{13,9},{2,6},{6,2},{1... | collective-permute-start | bytes 2088968 | tf_op jit(solution)/shard_map/ppermute | solution.py:420
  10.0 12.0 %collective-permute-done.2.other = bf16[256,1280]{1,0:T(8,128)(2,1)S(1)} collective-permute-done((bf16[256,1280]{1,0:T(8,128)(2,1)S(1)}, bf16[256,1280]{1,0:T(8,128)(2,1)S(1)}, u32[]{:S(2)}, u32[]{:S(2)}) %collective-permute-start.2) | collective-permute-done | bytes 655392 | tf_op jit(solution)/shard_map/ppermute | solution.py:417
  21.9 1.8 %collective-permute-start.5 = (bf16[256,1280]{1,0:T(8,128)(2,1)S(1)}, bf16[256,1280]{1,0:T(8,128)(2,1)S(1)}, u32[]{:S(2)}, u32[]{:S(2)}) collective-permute-start(bf16[256,1280]{1,0:T(8,128)(2,1)S(1)} %collective-permute-done.2.other), channel_id=1, source_target_pairs={{0,4},{4,0},{8,12},{12,8},{1,5},{5,1},{9,13},{13,9},{2,6},{6,2},{1... | collective-permute-start | bytes 1966088 | tf_op jit(solution)/shard_map/ppermute | solution.py:420
  23.8 0.5 collective-permute-start.1
  24.3 2.6 %collective-permute-done.4.mine.n1m = bf16[272,1280]{1,0:T(8,128)(2,1)S(1)} collective-permute-done((bf16[272,1280]{1,0:T(8,128)(2,1)S(1)}, bf16[272,1280]{1,0:T(8,128)(2,1)S(1)}, u32[]{:S(2)}, u32[]{:S(2)}) %collective-permute-start.4) | collective-permute-done | bytes 696352 | tf_op jit(solution)/shard_map/ppermute | solution.py:420
  26.9 12.9 %collective-permute-done.5.other.n1o = bf16[256,1280]{1,0:T(8,128)(2,1)S(1)} collective-permute-done((bf16[256,1280]{1,0:T(8,128)(2,1)S(1)}, bf16[256,1280]{1,0:T(8,128)(2,1)S(1)}, u32[]{:S(2)}, u32[]{:S(2)}) %collective-permute-start.5) | collective-permute-done | bytes 655392 | tf_op jit(solution)/shard_map/ppermute | solution.py:420
  39.8 0.2 shard_map.56
  40.0 0.2 shard_map.57
  40.2 2.5 %collective-permute-start.9 = (bf16[256,640]{1,0:T(8,128)(2,1)S(1)}, bf16[256,640]{1,0:T(8,128)(2,1)S(1)}, u32[]{:S(2)}, u32[]{:S(2)}) collective-permute-start(bf16[256,640]{1,0:T(8,128)(2,1)S(1)} %get-tuple-element.60), channel_id=1, source_target_pairs={{0,4},{4,0},{8,12},{12,8},{1,5},{5,1},{9,13},{13,9},{2,6},{6,2},{1... | collective-permute-start | bytes 983048 | tf_op jit(solution)/shard_map/ppermute | solution.py:420
  42.8 0.6 collective-permute-start.12
  43.4 6.2 %collective-permute-done.9.r2 = bf16[256,640]{1,0:T(8,128)(2,1)S(1)} collective-permute-done((bf16[256,640]{1,0:T(8,128)(2,1)S(1)}, bf16[256,640]{1,0:T(8,128)(2,1)S(1)}, u32[]{:S(2)}, u32[]{:S(2)}) %collective-permute-start.9) | collective-permute-done | bytes 327712 | tf_op jit(solution)/shard_map/ppermute | solution.py:420
  49.6 4.0 %collective-permute-start.10 = (bf16[256,640]{1,0:T(8,128)(2,1)S(1)}, bf16[256,640]{1,0:T(8,128)(2,1)S(1)}, u32[]{:S(2)}, u32[]{:S(2)}) collective-permute-start(bf16[256,640]{1,0:T(8,128)(2,1)S(1)} %collective-permute-done.8.r1), channel_id=1, source_target_pairs={{0,4},{4,0},{8,12},{12,8},{1,5},{5,1},{9,13},{13,9},{2,6},{6,2},{1... | collective-permute-start | bytes 983048 | tf_op jit(solution)/shard_map/ppermute | solution.py:420
  53.6 0.5 collective-permute-start.3
  54.2 0.1 collective-permute-start.11
  54.3 0.7 slice.44
  55.0 4.3 %collective-permute-start.13 = (bf16[256,384]{1,0:T(8,128)(2,1)}, bf16[256,384]{1,0:T(8,128)(2,1)S(1)}, u32[]{:S(2)}, u32[]{:S(2)}) collective-permute-start(bf16[256,384]{1,0:T(8,128)(2,1)} %slice.44), channel_id=1, source_target_pairs={{0,4},{4,0},{8,12},{12,8},{1,5},{5,1},{9,13},{13,9},{2,6},{6,2},{1... | collective-permute-start | bytes 589832 | tf_op jit(solution)/shard_map/ppermute | solution.py:420
  59.3 0.7 pad_maximum_fusion.5
  60.0 3.9 %collective-permute-done.11.r2 = bf16[256,384]{1,0:T(8,128)(2,1)S(1)} collective-permute-done((bf16[256,384]{1,0:T(8,128)(2,1)S(1)}, bf16[256,384]{1,0:T(8,128)(2,1)S(1)}, u32[]{:S(2)}, u32[]{:S(2)}) %collective-permute-start.11) | collective-permute-done | bytes 196640 | tf_op jit(solution)/shard_map/ppermute | solution.py:420
  64.0 6.4 %shard_map.58 = (bf16[2560,1792]{1,0:T(8,128)(2,1)S(1)}, f32[2560,128]{1,0:T(8,128)S(1)}) custom-call(s32[1,4]{1,0:T(1,128)S(1)} %copy-done.14, bf16[256,640]{1,0:T(8,128)(2,1)S(1)} %pad_maximum_fusion.3.q_mine, bf16[256,640]{1,0:T(8,128)(2,1)S(1)} %collective-permute-done.3.q_other, bf16[272,1280]{1,0:T(8,128)(2,1)S(1)} %pad_maximum_fusion.mine, ...), custom_call_target="tpu_custom_call" | custom-call | flops 1174405120 | bytes 9175040 | tf_op jit(solution)/shard_map/pallas_call | solution.py:277
  70.4 3.6 %copy-done = bf16[2560,1792]{1,0:T(8,128)(2,1)} copy-done((bf16[2560,1792]{1,0:T(8,128)(2,1)}, bf16[2560,1792]{1,0:T(8,128)(2,1)S(1)}, u32[]{:S(2)}) %copy-start) | copy-done | bytes 9175064
  74.0 2.3 %collective-permute-start.15 = (bf16[512,256]{1,0:T(8,128)(2,1)}, bf16[512,256]{1,0:T(8,128)(2,1)}, u32[]{:S(2)}, u32[]{:S(2)}) collective-permute-start(bf16[512,256]{1,0:T(8,128)(2,1)} %pad_maximum_fusion.5), channel_id=1, source_target_pairs={{0,4},{4,0},{8,12},{12,8},{1,5},{5,1},{9,13},{13,9},{2,6},{6,2},{1... | collective-permute-start | bytes 786440 | tf_op jit(solution)/shard_map/ppermute | solution.py:420
  76.3 3.6 %copy-done.1 = bf16[2560,1792]{1,0:T(8,128)(2,1)S(1)} copy-done((bf16[2560,1792]{1,0:T(8,128)(2,1)S(1)}, bf16[2560,1792]{1,0:T(8,128)(2,1)}, u32[]{:S(2)}) %copy-start.1) | copy-done | bytes 9175064
  79.9 1.1 %copy-done.4 = bf16[272,1280]{1,0:T(8,128)(2,1)S(1)} copy-done((bf16[272,1280]{1,0:T(8,128)(2,1)S(1)}, bf16[272,1280]{1,0:T(8,128)(2,1)}, u32[]{:S(2)}) %copy-start.4) | copy-done | bytes 696344
  81.0 1.1 %copy-done.8 = bf16[256,1280]{1,0:T(8,128)(2,1)S(1)} copy-done((bf16[256,1280]{1,0:T(8,128)(2,1)S(1)}, bf16[256,1280]{1,0:T(8,128)(2,1)}, u32[]{:S(2)}) %copy-start.8) | copy-done | bytes 655384
  82.1 1.1 %copy-done.10 = bf16[256,1280]{1,0:T(8,128)(2,1)S(1)} copy-done((bf16[256,1280]{1,0:T(8,128)(2,1)S(1)}, bf16[256,1280]{1,0:T(8,128)(2,1)}, u32[]{:S(2)}) %copy-start.10) | copy-done | bytes 655384
  83.2 1.1 %copy-done.13 = bf16[256,1280]{1,0:T(8,128)(2,1)S(1)} copy-done((bf16[256,1280]{1,0:T(8,128)(2,1)S(1)}, bf16[256,1280]{1,0:T(8,128)(2,1)}, u32[]{:S(2)}) %copy-start.13) | copy-done | bytes 655384
  84.3 2.7 %shard_map.59.near = f32[2560,128]{1,0:T(8,128)S(1)} custom-call(bf16[2560,1792]{1,0:T(8,128)(2,1)S(1)} %copy-done.1, bf16[272,1280]{1,0:T(8,128)(2,1)S(1)} %pad_maximum_fusion.mine, bf16[256,1280]{1,0:T(8,128)(2,1)S(1)} %copy-done.13, bf16[272,1280]{1,0:T(8,128)(2,1)S(1)} %collective-permute-done.4.mine.n1m, bf16[256,1280]{1,0:T(8,128)(2,1)S(1)} %copy-done.8, ...), custom_call_target="tpu_custom_call" | custom-call | flops 1174405120 | bytes 9175040 | tf_op jit(solution)/shard_map/pallas_call | solution.py:296
  87.0 0.9 copy-done.2
  87.9 1.2 %shard_map.60 = (bf16[128,384]{1,0:T(8,128)(2,1)S(1)}, bf16[128,384]{1,0:T(8,128)(2,1)S(1)}, bf16[128,384]{1,0:T(8,128)(2,1)S(1)}, bf16[128,384]{1,0:T(8,128)(2,1)S(1)}) custom-call(bf16[2560,1792]{1,0:T(8,128)(2,1)S(1)} %copy-done.2, f32[2560,128]{1,0:T(8,128)S(1)} %get-tuple-element.65.totals, f32[2560,128]{1,0:T(8,128)S(1)} %shard_map.59.near, ...), custom_call_target="tpu_custom_call" | custom-call | flops 201326592 | bytes 5505024 | tf_op jit(solution)/shard_map/pallas_call | solution.py:319
  89.1 0.1 collective-permute-start.18
  89.2 0.9 collective-permute-start.17
  90.0 1.0 collective-permute-start.14
  91.0 1.0 fusion.2
  92.0 0.8 shard_map.61
  92.9 0.1 collective-permute-start.16
  93.0 0.9 collective-permute-start.19
  93.9 0.3 collective-permute-done.18
  94.2 0.7 collective-permute-start.20
  95.0 0.2 collective-permute-done.17
  95.2 2.7 %collective-permute-done.19 = bf16[128,256]{1,0:T(8,128)(2,1)S(1)} collective-permute-done((bf16[128,256]{1,0:T(8,128)(2,1)S(1)}, bf16[128,256]{1,0:T(8,128)(2,1)S(1)}, u32[]{:S(2)}, u32[]{:S(2)}) %collective-permute-start.19) | collective-permute-done | bytes 65568 | tf_op jit(solution)/shard_map/ppermute | solution.py:417
  98.0 0.6 collective-permute-done.20
  98.6 0.2 copy-done.15
  98.8 0.6 constant_dynamic-update-slice_fusion
  (56 shorter events, 0.6 us)
Async XLA Ops:
  1.6 6.0 %copy-start.5 = (bf16[128,2560]{1,0:T(8,128)(2,1)S(1)}, bf16[128,2560]{1,0:T(8,128)(2,1)}, u32[]{:S(2)}) copy-start(bf16[128,2560]{1,0:T(8,128)(2,1)} %refs_1_.1) | copy-start | bytes 1966084
  1.6 6.0 %copy-start.6 = (bf16[128,2560]{1,0:T(8,128)(2,1)S(1)}, bf16[128,2560]{1,0:T(8,128)(2,1)}, u32[]{:S(2)}) copy-start(bf16[128,2560]{1,0:T(8,128)(2,1)} %refs_2_.1) | copy-start | bytes 1966084
  1.6 6.0 %copy-start.11 = (bf16[128,2560]{1,0:T(8,128)(2,1)S(1)}, bf16[128,2560]{1,0:T(8,128)(2,1)}, u32[]{:S(2)}) copy-start(bf16[128,2560]{1,0:T(8,128)(2,1)} %refs_0_.1) | copy-start | bytes 1966084
  1.6 6.0 %copy-start.14 = (s32[1,4]{1,0:T(1,128)S(1)}, s32[1,4]{1,0:T(1,128)}, u32[]{:S(2)}) copy-start(s32[1,4]{1,0:T(1,128)} %mask.3) | copy-start | bytes 52
  1.6 2.2 %collective-permute-start = (bf16[128,2560]{1,0:T(8,128)(2,1)S(1)}, bf16[128,2560]{1,0:T(8,128)(2,1)S(1)}, u32[]{:S(2)}, u32[]{:S(2)}) collective-permute-start(bf16[128,2560]{1,0:T(8,128)(2,1)S(1)} %pad_maximum_fusion.1), channel_id=1, source_target_pairs={{0,1},{1,0},{2,3},{3,2},{4,5},{5,4},{6,7},{7,6},{8,9},{9,8},{10,11... | collective-permute-start | bytes 1966088 | tf_op jit(solution)/shard_map/ppermute | solution.py:417
  4.0 18.0 %collective-permute-start.2 = (bf16[256,1280]{1,0:T(8,128)(2,1)S(1)}, bf16[256,1280]{1,0:T(8,128)(2,1)S(1)}, u32[]{:S(2)}, u32[]{:S(2)}) collective-permute-start(bf16[256,1280]{1,0:T(8,128)(2,1)S(1)} %pad_maximum_fusion.2), channel_id=1, source_target_pairs={{0,2},{1,3},{2,0},{3,1},{4,6},{5,7},{6,4},{7,5},{8,10},{9,11},{10,... | collective-permute-start | bytes 1966088 | tf_op jit(solution)/shard_map/ppermute | solution.py:417
  8.3 18.6 %collective-permute-start.4 = (bf16[272,1280]{1,0:T(8,128)(2,1)S(1)}, bf16[272,1280]{1,0:T(8,128)(2,1)S(1)}, u32[]{:S(2)}, u32[]{:S(2)}) collective-permute-start(bf16[272,1280]{1,0:T(8,128)(2,1)S(1)} %pad_maximum_fusion.mine), channel_id=1, source_target_pairs={{0,4},{4,0},{8,12},{12,8},{1,5},{5,1},{9,13},{13,9},{2,6},{6,2},{1... | collective-permute-start | bytes 2088968 | tf_op jit(solution)/shard_map/ppermute | solution.py:420
  10.0 30.0 %collective-permute-start.6 = (bf16[272,1280]{1,0:T(8,128)(2,1)S(1)}, bf16[272,1280]{1,0:T(8,128)(2,1)S(1)}, u32[]{:S(2)}, u32[]{:S(2)}) collective-permute-start(bf16[272,1280]{1,0:T(8,128)(2,1)S(1)} %pad_maximum_fusion.mine), channel_id=1, source_target_pairs={{0,1},{1,0},{2,3},{3,2},{4,8},{5,9},{6,10},{7,11},{8,4},{9,5},{10,... | collective-permute-start | bytes 2088968 | tf_op jit(solution)/shard_map/ppermute | solution.py:424
  21.9 42.0 %copy-start.12 = (bf16[256,1280]{1,0:T(8,128)(2,1)}, bf16[256,1280]{1,0:T(8,128)(2,1)S(1)}, u32[]{:S(2)}) copy-start(bf16[256,1280]{1,0:T(8,128)(2,1)S(1)} %collective-permute-done.2.other) | copy-start | bytes 1966084
  21.9 17.9 %collective-permute-start.5 = (bf16[256,1280]{1,0:T(8,128)(2,1)S(1)}, bf16[256,1280]{1,0:T(8,128)(2,1)S(1)}, u32[]{:S(2)}, u32[]{:S(2)}) collective-permute-start(bf16[256,1280]{1,0:T(8,128)(2,1)S(1)} %collective-permute-done.2.other), channel_id=1, source_target_pairs={{0,4},{4,0},{8,12},{12,8},{1,5},{5,1},{9,13},{13,9},{2,6},{6,2},{1... | collective-permute-start | bytes 1966088 | tf_op jit(solution)/shard_map/ppermute | solution.py:420
  23.8 16.3 %collective-permute-start.7 = (bf16[256,1280]{1,0:T(8,128)(2,1)S(1)}, bf16[256,1280]{1,0:T(8,128)(2,1)S(1)}, u32[]{:S(2)}, u32[]{:S(2)}) collective-permute-start(bf16[256,1280]{1,0:T(8,128)(2,1)S(1)} %collective-permute-done.2.other), channel_id=1, source_target_pairs={{0,1},{1,0},{2,3},{3,2},{4,8},{5,9},{6,10},{7,11},{8,4},{9,5},{10,... | collective-permute-start | bytes 1966088 | tf_op jit(solution)/shard_map/ppermute | solution.py:424
  23.8 19.0 %collective-permute-start.1 = (bf16[128,1280]{1,0:T(8,128)(2,1)S(1)}, bf16[128,1280]{1,0:T(8,128)(2,1)S(1)}, u32[]{:S(2)}, u32[]{:S(2)}) collective-permute-start(bf16[128,1280]{1,0:T(8,128)(2,1)S(1)} %get-tuple-element.49), channel_id=1, source_target_pairs={{0,1},{1,0},{2,3},{3,2},{4,5},{5,4},{6,7},{7,6},{8,9},{9,8},{10,11... | collective-permute-start | bytes 983048 | tf_op jit(solution)/shard_map/ppermute | solution.py:417
  39.8 24.1 %copy-start.7 = (bf16[256,1280]{1,0:T(8,128)(2,1)}, bf16[256,1280]{1,0:T(8,128)(2,1)S(1)}, u32[]{:S(2)}) copy-start(bf16[256,1280]{1,0:T(8,128)(2,1)S(1)} %collective-permute-done.5.other.n1o) | copy-start | bytes 1966084
  40.0 23.9 %copy-start.3 = (bf16[272,1280]{1,0:T(8,128)(2,1)}, bf16[272,1280]{1,0:T(8,128)(2,1)S(1)}, u32[]{:S(2)}) copy-start(bf16[272,1280]{1,0:T(8,128)(2,1)S(1)} %collective-permute-done.6.mine.n2m) | copy-start | bytes 2088964
  40.0 23.9 %copy-start.9 = (bf16[256,1280]{1,0:T(8,128)(2,1)}, bf16[256,1280]{1,0:T(8,128)(2,1)S(1)}, u32[]{:S(2)}) copy-start(bf16[256,1280]{1,0:T(8,128)(2,1)S(1)} %collective-permute-done.7.other.n2o) | copy-start | bytes 1966084
  40.2 9.4 %collective-permute-start.9 = (bf16[256,640]{1,0:T(8,128)(2,1)S(1)}, bf16[256,640]{1,0:T(8,128)(2,1)S(1)}, u32[]{:S(2)}, u32[]{:S(2)}) collective-permute-start(bf16[256,640]{1,0:T(8,128)(2,1)S(1)} %get-tuple-element.60), channel_id=1, source_target_pairs={{0,4},{4,0},{8,12},{12,8},{1,5},{5,1},{9,13},{13,9},{2,6},{6,2},{1... | collective-permute-start | bytes 983048 | tf_op jit(solution)/shard_map/ppermute | solution.py:420
  42.8 6.9 %collective-permute-start.8 = (bf16[256,640]{1,0:T(8,128)(2,1)S(1)}, bf16[256,640]{1,0:T(8,128)(2,1)S(1)}, u32[]{:S(2)}, u32[]{:S(2)}) collective-permute-start(bf16[256,640]{1,0:T(8,128)(2,1)S(1)} %get-tuple-element.59), channel_id=1, source_target_pairs={{0,1},{1,0},{2,3},{3,2},{4,8},{5,9},{6,10},{7,11},{8,4},{9,5},{10,... | collective-permute-start | bytes 983048 | tf_op jit(solution)/shard_map/ppermute | solution.py:424
  42.8 11.5 %collective-permute-start.12 = (bf16[256,640]{1,0:T(8,128)(2,1)S(1)}, bf16[256,640]{1,0:T(8,128)(2,1)S(1)}, u32[]{:S(2)}, u32[]{:S(2)}) collective-permute-start(bf16[256,640]{1,0:T(8,128)(2,1)S(1)} %get-tuple-element.67), channel_id=1, source_target_pairs={{0,1},{1,0},{2,3},{3,2},{4,8},{5,9},{6,10},{7,11},{8,4},{9,5},{10,... | collective-permute-start | bytes 983048 | tf_op jit(solution)/shard_map/ppermute | solution.py:424
  49.6 14.3 %collective-permute-start.10 = (bf16[256,640]{1,0:T(8,128)(2,1)S(1)}, bf16[256,640]{1,0:T(8,128)(2,1)S(1)}, u32[]{:S(2)}, u32[]{:S(2)}) collective-permute-start(bf16[256,640]{1,0:T(8,128)(2,1)S(1)} %collective-permute-done.8.r1), channel_id=1, source_target_pairs={{0,4},{4,0},{8,12},{12,8},{1,5},{5,1},{9,13},{13,9},{2,6},{6,2},{1... | collective-permute-start | bytes 983048 | tf_op jit(solution)/shard_map/ppermute | solution.py:420
  53.6 10.3 %collective-permute-start.3 = (bf16[256,640]{1,0:T(8,128)(2,1)S(1)}, bf16[256,640]{1,0:T(8,128)(2,1)S(1)}, u32[]{:S(2)}, u32[]{:S(2)}) collective-permute-start(bf16[256,640]{1,0:T(8,128)(2,1)S(1)} %pad_maximum_fusion.4), channel_id=1, source_target_pairs={{0,2},{1,3},{2,0},{3,1},{4,6},{5,7},{6,4},{7,5},{8,10},{9,11},{10,... | collective-permute-start | bytes 983048 | tf_op jit(solution)/shard_map/ppermute | solution.py:417
  54.2 9.7 %collective-permute-start.11 = (bf16[256,384]{1,0:T(8,128)(2,1)S(1)}, bf16[256,384]{1,0:T(8,128)(2,1)S(1)}, u32[]{:S(2)}, u32[]{:S(2)}) collective-permute-start(bf16[256,384]{1,0:T(8,128)(2,1)S(1)} %slice.34), channel_id=1, source_target_pairs={{0,4},{4,0},{8,12},{12,8},{1,5},{5,1},{9,13},{13,9},{2,6},{6,2},{1... | collective-permute-start | bytes 589832 | tf_op jit(solution)/shard_map/ppermute | solution.py:420
  55.0 21.3 %collective-permute-start.13 = (bf16[256,384]{1,0:T(8,128)(2,1)}, bf16[256,384]{1,0:T(8,128)(2,1)S(1)}, u32[]{:S(2)}, u32[]{:S(2)}) collective-permute-start(bf16[256,384]{1,0:T(8,128)(2,1)} %slice.44), channel_id=1, source_target_pairs={{0,4},{4,0},{8,12},{12,8},{1,5},{5,1},{9,13},{13,9},{2,6},{6,2},{1... | collective-permute-start | bytes 589832 | tf_op jit(solution)/shard_map/ppermute | solution.py:420
  70.4 3.6 %copy-start = (bf16[2560,1792]{1,0:T(8,128)(2,1)}, bf16[2560,1792]{1,0:T(8,128)(2,1)S(1)}, u32[]{:S(2)}) copy-start(bf16[2560,1792]{1,0:T(8,128)(2,1)S(1)} %get-tuple-element.68.weights) | copy-start | bytes 27525124
  74.0 17.1 %collective-permute-start.15 = (bf16[512,256]{1,0:T(8,128)(2,1)}, bf16[512,256]{1,0:T(8,128)(2,1)}, u32[]{:S(2)}, u32[]{:S(2)}) collective-permute-start(bf16[512,256]{1,0:T(8,128)(2,1)} %pad_maximum_fusion.5), channel_id=1, source_target_pairs={{0,4},{4,0},{8,12},{12,8},{1,5},{5,1},{9,13},{13,9},{2,6},{6,2},{1... | collective-permute-start | bytes 786440 | tf_op jit(solution)/shard_map/ppermute | solution.py:420
  76.3 3.6 %copy-start.1 = (bf16[2560,1792]{1,0:T(8,128)(2,1)S(1)}, bf16[2560,1792]{1,0:T(8,128)(2,1)}, u32[]{:S(2)}) copy-start(bf16[2560,1792]{1,0:T(8,128)(2,1)} %copy-done) | copy-start | bytes 27525124
  79.9 1.1 %copy-start.4 = (bf16[272,1280]{1,0:T(8,128)(2,1)S(1)}, bf16[272,1280]{1,0:T(8,128)(2,1)}, u32[]{:S(2)}) copy-start(bf16[272,1280]{1,0:T(8,128)(2,1)} %copy-done.3) | copy-start | bytes 2088964
  81.0 1.1 %copy-start.8 = (bf16[256,1280]{1,0:T(8,128)(2,1)S(1)}, bf16[256,1280]{1,0:T(8,128)(2,1)}, u32[]{:S(2)}) copy-start(bf16[256,1280]{1,0:T(8,128)(2,1)} %copy-done.7) | copy-start | bytes 1966084
  82.1 1.1 %copy-start.10 = (bf16[256,1280]{1,0:T(8,128)(2,1)S(1)}, bf16[256,1280]{1,0:T(8,128)(2,1)}, u32[]{:S(2)}) copy-start(bf16[256,1280]{1,0:T(8,128)(2,1)} %copy-done.9) | copy-start | bytes 1966084
  83.2 1.1 %copy-start.13 = (bf16[256,1280]{1,0:T(8,128)(2,1)S(1)}, bf16[256,1280]{1,0:T(8,128)(2,1)}, u32[]{:S(2)}) copy-start(bf16[256,1280]{1,0:T(8,128)(2,1)} %copy-done.12) | copy-start | bytes 1966084
  84.3 3.6 %copy-start.2 = (bf16[2560,1792]{1,0:T(8,128)(2,1)S(1)}, bf16[2560,1792]{1,0:T(8,128)(2,1)}, u32[]{:S(2)}) copy-start(bf16[2560,1792]{1,0:T(8,128)(2,1)} %copy-done) | copy-start | bytes 27525124
  89.1 5.1 %collective-permute-start.18 = (bf16[128,384]{1,0:T(8,128)(2,1)S(1)}, bf16[128,384]{1,0:T(8,128)(2,1)S(1)}, u32[]{:S(2)}, u32[]{:S(2)}) collective-permute-start(bf16[128,384]{1,0:T(8,128)(2,1)S(1)} %get-tuple-element.76), channel_id=1, source_target_pairs={{0,3},{1,2},{2,1},{3,0},{4,7},{5,6},{6,5},{7,4},{8,11},{9,10},{10,... | collective-permute-start | bytes 294920 | tf_op jit(solution)/shard_map/ppermute | solution.py:417
  89.2 5.9 %collective-permute-start.17 = (bf16[128,384]{1,0:T(8,128)(2,1)S(1)}, bf16[128,384]{1,0:T(8,128)(2,1)S(1)}, u32[]{:S(2)}, u32[]{:S(2)}) collective-permute-start(bf16[128,384]{1,0:T(8,128)(2,1)S(1)} %get-tuple-element.74), channel_id=1, source_target_pairs={{0,2},{1,3},{2,0},{3,1},{4,6},{5,7},{6,4},{7,5},{8,10},{9,11},{10,... | collective-permute-start | bytes 294920 | tf_op jit(solution)/shard_map/ppermute | solution.py:417
  90.0 5.1 %collective-permute-start.14 = (bf16[128,384]{1,0:T(8,128)(2,1)S(1)}, bf16[128,384]{1,0:T(8,128)(2,1)S(1)}, u32[]{:S(2)}, u32[]{:S(2)}) collective-permute-start(bf16[128,384]{1,0:T(8,128)(2,1)S(1)} %get-tuple-element.70), channel_id=1, source_target_pairs={{0,1},{1,0},{2,3},{3,2},{4,5},{5,4},{6,7},{7,6},{8,9},{9,8},{10,11... | collective-permute-start | bytes 294920 | tf_op jit(solution)/shard_map/ppermute | solution.py:417
  92.9 2.1 %collective-permute-start.16 = (bf16[128,256]{1,0:T(8,128)(2,1)S(1)}, bf16[128,256]{1,0:T(8,128)(2,1)S(1)}, u32[]{:S(2)}, u32[]{:S(2)}) collective-permute-start(bf16[128,256]{1,0:T(8,128)(2,1)S(1)} %get-tuple-element.72), channel_id=1, source_target_pairs={{0,1},{1,0},{2,3},{3,2},{4,5},{5,4},{6,7},{7,6},{8,9},{9,8},{10,11... | collective-permute-start | bytes 196616 | tf_op jit(solution)/shard_map/ppermute | solution.py:417
  93.0 5.0 %collective-permute-start.19 = (bf16[128,256]{1,0:T(8,128)(2,1)S(1)}, bf16[128,256]{1,0:T(8,128)(2,1)S(1)}, u32[]{:S(2)}, u32[]{:S(2)}) collective-permute-start(bf16[128,256]{1,0:T(8,128)(2,1)S(1)} %get-tuple-element.79), channel_id=1, source_target_pairs={{0,2},{1,3},{2,0},{3,1},{4,6},{5,7},{6,4},{7,5},{8,10},{9,11},{10,... | collective-permute-start | bytes 196616 | tf_op jit(solution)/shard_map/ppermute | solution.py:417
  94.2 4.4 %collective-permute-start.20 = (bf16[128,256]{1,0:T(8,128)(2,1)S(1)}, bf16[128,256]{1,0:T(8,128)(2,1)S(1)}, u32[]{:S(2)}, u32[]{:S(2)}) collective-permute-start(bf16[128,256]{1,0:T(8,128)(2,1)S(1)} %get-tuple-element.80), channel_id=1, source_target_pairs={{0,3},{1,2},{2,1},{3,0},{4,7},{5,6},{6,5},{7,4},{8,11},{9,10},{10,... | collective-permute-start | bytes 196616 | tf_op jit(solution)/shard_map/ppermute | solution.py:417
  98.0 0.8 copy-start.15

commit v9 on v6

--- a/solution.py
+++ b/solution.py
@@ -157,8 +157,6 @@
 
 INFO_ROWS = 16
 OUTER = [(0, 1), (1, 0), (2, 3), (3, 2)]
-INNER = [(1, 2), (2, 1)]
-OUTWARD = [(1, 0), (2, 3)]
 
 
 def fold(x):
@@ -184,115 +182,116 @@
     return free if top is None else jnp.maximum(free, top)
 
 
-def weights_of(top, slots, held, out):
+def attention_kernel(mask, q_mine, q_other, km, ko, n1km, n1ko, n2km, n2ko, r1, r2, r3, v, n1v, n2v, *rest):
+    mixed_out, totals, far_weights, held0, held1 = rest
     factor = SCALE * LOG2E
-    total = None
-    for at, (k, valid) in enumerate(slots):
-        tile = k.shape[0]
-        level = top if valid is None else jnp.where(valid, top, 1e30)
-        w = jnp.exp2((held[:, at * tile : (at + 1) * tile] - level) * factor)
-        out[:, at * tile : (at + 1) * tile] = w.astype(jnp.bfloat16)
-        for begin in range(0, tile, 128):
-            part = w[:, begin : begin + 128]
-            total = part if total is None else total + part
-    return jnp.sum(total, axis=1, keepdims=True)
-
-
-def inner_frame():
-    z = lax.axis_index("frame")
-    return (z == 1) | (z == 2)
-
-
-def weights_kernel(mask, q_mine, q_other, mine, other, n1m, n1o, n2m, n2o, r1, r2, r3, weights, totals, held0, held1):
     z = lax.axis_index("frame")
     tile = r1.shape[0]
-    near = mask[0, z ^ 2] == 1
-    always = [(mine, None), (other, None), (n1m, None), (n1o, None)]
-
-    def body(slots):
+    near2 = mask[0, z ^ 2] == 1
+
+    def body(near, values, far):
         rooms = (held0, held1)
+        slots = [(k, None) for k in near] + far
         tops = [scores_of(q[...], slots, held) for q, held in zip((q_mine, q_other), rooms)]
         for half, (top, held) in enumerate(zip(tops, rooms)):
             rows = slice(half * tile, (half + 1) * tile)
-            total = weights_of(top, slots, held, weights.at[rows])
-            totals[rows] = jnp.broadcast_to(total, (tile, totals.shape[1]))
-
-    @pl.when(inner_frame())
-    def _():
-        body(always + [(n2m, None), (n2o, None), (r1, near)])
-
-    @pl.when(jnp.logical_not(inner_frame()))
-    def _():
-        body(always + [(r2, near), (r3, mask[0, z ^ 3] == 1)])
-
-
-def values_kernel(weights, totals, mine, other, n1m, n1o, n2m, n2o, r1, r2, r3, *outs):
-    tile = r1.shape[0]
-    rows = outs[0].shape[0]
-    always = [mine, other, n1m, n1o]
-
-    def body(slots):
+            total, mixed = None, None
+            for at, (_, valid) in enumerate(slots):
+                level = top if valid is None else jnp.where(valid, top, 1e30)
+                w = jnp.exp2((held[:, at * tile : (at + 1) * tile] - level) * factor)
+                rounded = w.astype(jnp.bfloat16)
+                if at < len(near):
+                    value = values[at // 2][(at % 2) * tile : (at % 2 + 1) * tile]
+                    mix = jnp.dot(rounded, value, preferred_element_type=jnp.float32)
+                    mixed = mix if mixed is None else mixed + mix
+                else:
+                    begin = (at - len(near)) * tile
+                    far_weights[rows, begin : begin + tile] = rounded
+                for begin in range(0, tile, 128):
+                    part = w[:, begin : begin + 128]
+                    total = part if total is None else total + part
+            mixed_out[rows] = mixed
+            totals[rows] = jnp.broadcast_to(jnp.sum(total, axis=1, keepdims=True), (tile, totals.shape[1]))
+
+    inner = (z == 1) | (z == 2)
+
+    @pl.when(inner)
+    def _():
+        body([km, ko, n1km, n1ko, n2km, n2ko], [v, n1v, n2v], [(r1, near2)])
+
+    @pl.when(jnp.logical_not(inner))
+    def _():
+        body([km, ko, n1km, n1ko], [v, n1v], [(r2, near2), (r3, mask[0, z ^ 3] == 1)])
+
+
+def far_kernel(mixed, totals, far_weights, r1, r2, r3, *outs):
+    rows, tile = outs[0].shape[0], r1.shape[0]
+
+    def body(values):
         for d, out in enumerate(outs):
             span = slice(d * rows, (d + 1) * rows)
-            mixed = None
-            for at, v in enumerate(slots):
-                w = weights[span, at * tile : (at + 1) * tile]
-                mix = jnp.dot(w, v[...], preferred_element_type=jnp.float32)
-                mixed = mix if mixed is None else mixed + mix
-            out[...] = (mixed / totals[span]).astype(jnp.bfloat16)
-
-    @pl.when(inner_frame())
-    def _():
-        body(always + [n2m, n2o, r1])
-
-    @pl.when(jnp.logical_not(inner_frame()))
-    def _():
-        body(always + [r2, r3])
+            total = mixed[span]
+            for at, value in enumerate(values):
+                w = far_weights[span, at * tile : (at + 1) * tile]
+                total = total + jnp.dot(w, value[...], preferred_element_type=jnp.float32)
+            out[...] = (total / totals[span]).astype(jnp.bfloat16)
+
+    z = lax.axis_index("frame")
+    inner = (z == 1) | (z == 2)
+
+    @pl.when(inner)
+    def _():
+        body([r1])
+
+    @pl.when(jnp.logical_not(inner))
+    def _():
+        body([r2, r3])
 
 
 def by_head(x, rows, first=0):
     return x, pl.BlockSpec((rows, HEAD_DIM), lambda i: (0, first + i))
 
 
-def find_weights(mask, q_mine, q_other, keys, heads):
-    tile = q_mine.shape[0]
-    blocks = [by_head(q_mine, tile), by_head(q_other, tile)] + [by_head(k, tile) for k in keys]
-    shapes = [(2 * tile, 7 * tile, jnp.bfloat16), (2 * tile, HEAD_DIM, jnp.float32)]
+def by_rows(rows, lanes, first=0):
+    return pl.BlockSpec((rows, lanes), lambda i: (first + i, 0))
+
+
+def attend_near(mask, q, keys, values, heads):
+    tile = q[0].shape[0]
+    blocks = [by_head(x, tile) for x in [*q, *keys]] + [by_head(x, 2 * tile) for x in values]
+    shapes = [(HEAD_DIM, jnp.float32), (HEAD_DIM, jnp.float32), (2 * tile, jnp.bfloat16)]
     return pl.pallas_call(
-        weights_kernel,
+        attention_kernel,
         grid=(heads,),
         in_specs=[pl.BlockSpec(memory_space=pltpu.SMEM)] + [spec for _, spec in blocks],
-        out_specs=[pl.BlockSpec((rows, lanes), lambda i: (i, 0)) for rows, lanes, _ in shapes],
-        out_shape=[jax.ShapeDtypeStruct((heads * rows, lanes), dtype) for rows, lanes, dtype in shapes],
+        out_specs=[by_rows(2 * tile, lanes) for lanes, _ in shapes],
+        out_shape=[jax.ShapeDtypeStruct((heads * 2 * tile, lanes), dtype) for lanes, dtype in shapes],
         scratch_shapes=[pltpu.VMEM((tile, 7 * tile), jnp.float32)] * 2,
         compiler_params=pltpu.CompilerParams(vmem_limit_bytes=16 * 1024 * 1024),
         cost_estimate=pl.CostEstimate(
-            flops=heads * 28 * tile * tile * HEAD_DIM,
-            bytes_accessed=heads * 28 * tile * tile,
+            flops=heads * 56 * tile * tile * HEAD_DIM,
+            bytes_accessed=heads * 20 * tile * tile,
             transcendentals=heads * 14 * tile * tile,
         ),
     )(mask, *[x for x, _ in blocks])
 
 
-def mix_values(weights, totals, values, skip, heads):
-    tile = weights.shape[1] // 7
-    rows, lanes = 2 * tile, weights.shape[1]
-    blocks = [by_head(v, tile, first) for v, first in values]
+def add_far(mixed, totals, far_weights, r1, r2, r3, begin, end):
+    tile = r1.shape[0]
+    rows, heads = 2 * tile, end - begin
+    blocks = [(x, by_rows(rows, x.shape[1], begin)) for x in (mixed, totals, far_weights)]
+    blocks += [by_head(r1, tile, begin), by_head(r2, tile, begin), by_head(r3, tile)]
     return pl.pallas_call(
-        values_kernel,
+        far_kernel,
         grid=(heads,),
-        in_specs=[
-            pl.BlockSpec((rows, lanes), lambda i: (skip + i, 0)),
-            pl.BlockSpec((rows, HEAD_DIM), lambda i: (skip + i, 0)),
-        ]
-        + [spec for _, spec in blocks],
+        in_specs=[spec for _, spec in blocks],
         out_specs=[pl.BlockSpec((rows // 4, HEAD_DIM), lambda i: (0, i))] * 4,
         out_shape=[jax.ShapeDtypeStruct((rows // 4, heads * HEAD_DIM), jnp.bfloat16)] * 4,
-        compiler_params=pltpu.CompilerParams(vmem_limit_bytes=16 * 1024 * 1024),
+        compiler_params=pltpu.CompilerParams(vmem_limit_bytes=8 * 1024 * 1024),
         cost_estimate=pl.CostEstimate(
-            flops=heads * 2 * rows * lanes * HEAD_DIM, bytes_accessed=heads * 2 * rows * lanes, transcendentals=0
+            flops=heads * 4 * rows * tile * HEAD_DIM, bytes_accessed=heads * 12 * rows * tile, transcendentals=0
         ),
-    )(weights, totals, *[x for x, _ in blocks])
+    )(*[x for x, _ in blocks])
 
 
 def pack_kernel(copies, width, mask, offset, *refs):
@@ -335,28 +334,30 @@
     )(mask, offset, *operands)
 
 
-def relayed_kernel(at, mine, other, out):
-    tile, width = out.shape
-    offset = jnp.max(mine[tile : tile + INFO_ROWS, 4 * 128 : 5 * 128].astype(jnp.float32))
-    here = offset == (lax.axis_index("head") // 2).astype(jnp.float32)
+def relayed_kernel(told, *refs):
+    out = refs[-1]
+    tile = out.shape[0]
+    group = told[told.shape[0] - INFO_ROWS :, 4 * 128 : 5 * 128]
+    here = jnp.max(group.astype(jnp.float32)) == (lax.axis_index("head") // 2).astype(jnp.float32)
+    whole = refs[0].shape[0] == 2 * tile
 
     @pl.when(here)
     def _():
-        out[...] = mine[:tile, at : at + width]
+        out[...] = refs[0][:tile] if whole else told[:tile]
 
     @pl.when(jnp.logical_not(here))
     def _():
-        out[...] = other[...]
-
-
-def relayed(mine, other, at):
+        out[...] = refs[0][tile:] if whole else refs[0][...]
+
+
+def relayed(told, array, tile):
     return pl.pallas_call(
-        functools.partial(relayed_kernel, at),
+        relayed_kernel,
         in_specs=[pl.BlockSpec(memory_space=pltpu.VMEM)] * 2,
         out_specs=pl.BlockSpec(memory_space=pltpu.VMEM),
-        out_shape=jax.ShapeDtypeStruct(other.shape, other.dtype),
+        out_shape=jax.ShapeDtypeStruct((tile, array.shape[1]), array.dtype),
         compiler_params=pltpu.CompilerParams(vmem_limit_bytes=4 * 1024 * 1024),
-    )(mine, other)
+    )(told, array)
 
 
 def four_frames(queries, keys, values, pair_mask, tile_offset):
@@ -380,51 +381,57 @@
     def along(array, pairs):
         return lax.ppermute(array, "frame", pairs)
 
+    def across(array):
+        pairs = [(4 * z + j, 4 * (3 - z) + j if z in (1, 2) else 4 * z + (j ^ 1)) for z in range(4) for j in range(4)]
+        return lax.ppermute(array, ("frame", "head"), pairs)
+
     def after(array, earlier):
         return lax.optimization_barrier((array, earlier))[0]
 
+    tile = 2 * rows
     kv = [[columns(array, d) for array in (keys, values)] for d in range(4)]
     kv = lax.optimization_barrier(kv)
     got = to_head(beside(*kv[1], *kv[3]), 1)
+    got = [got[:, n * width : (n + 1) * width] for n in range(4)]
+    ko = to_head(below(kv[2][0], got[2]), 2)
     pay, q_own, q_far, told = packed(
         (queries, keys, values),
-        pair_mask,
+        after(pair_mask, got[0]),
         tile_offset,
         [[(0, 1, 0, width), (0, 3, 0, width)], [(0, 0, 0, width)], [(0, 2, 0, width)]],
         width,
-        2 * width,
-    )
-    mine = below(beside(*kv[0]), got[:, : 2 * width], told)
-    other_k = to_head(below(kv[2][0], got[:, 2 * width : 3 * width]), 2)
-    other_v = to_head(below(kv[2][1], got[:, 3 * width :]), 2)
-    n1m = along(mine, OUTER)
-    n2m = along(mine, INNER)
-    n1k = along(other_k, OUTER)
-    n2k = along(other_k, INNER)
-    n1v = along(other_v, OUTER)
-    n2v = along(other_v, INNER)
-
-    got = to_head(after(pay, got), 1)
+        width,
+    )
+
+    km = below(kv[0][0], got[0], told)
+    n1km = along(km, OUTER)
+    n2km = across(km)
+    vo = to_head(after(below(kv[2][1], got[3]), (n1km, n2km)), 2)
+    n1ko = along(ko, OUTER)
+    n2ko = across(ko)
+    v = below(kv[0][1], got[1], vo)
+    n1v = along(v, OUTER)
+    n2v = across(v)
+
+    got = to_head(pay, 1)
     q_mine = below(q_own, got[:, :width])
-    q_other = to_head(after(below(q_far, got[:, width:]), other_v), 2)
-
-    r1k = along(after(relayed(n1m, n1k, 0), (n2m, n2k)), INNER)
-    r1v = along(after(relayed(n1m, n1v, width), n2v), INNER)
-    r2k = along(relayed(n2m, n2k, 0), OUTWARD)
-    r3k = along(r1k, OUTWARD)
-    r2v = along(after(relayed(n2m, n2v, width), r1k), OUTWARD)
-
-    weights, totals = find_weights(
-        pair_mask, q_mine, q_other, [mine, other_k, n1m, n1k, n2m, n2k, r1k, r2k, r3k], heads
+    q_other = to_head(after(below(q_far, got[:, width:]), vo), 2)
+
+    r1k = across(after(relayed(n1km, n1ko, tile), (n2km, n2ko)))
+    r2k = along(relayed(n2km, n2ko, tile), OUTER)
+    r3k = along(after(r1k, r2k), OUTER)
+    r1v = across(relayed(n1km, n1v, tile))
+    r2v = along(relayed(n2km, n2v, tile), OUTER)
+    mixed, totals, far_weights = attend_near(
+        pair_mask, [q_mine, q_other], [km, ko, n1km, n1ko, n2km, n2ko, r1k, r2k, r3k], [v, n1v, n2v], heads
     )
     result = jnp.zeros((rows, features), jnp.bfloat16)
     cut = (heads + 1) // 2
     for begin, end in ((0, cut), (cut, heads)):
-        r3v = along(r1v[:, begin * HEAD_DIM : end * HEAD_DIM], OUTWARD)
-        whole = [(x, heads + begin) for x in (mine, n1m, n2m)]
-        part = [(x, begin) for x in (other_v, n1v, n2v, r1v, r2v)]
-        slots = [whole[0], part[0], whole[1], part[1], whole[2], part[2], part[3], part[4], (r3v, 0)]
-        out = mix_values(weights, totals, slots, begin, end - begin)
+        r3v = r1v[:, begin * HEAD_DIM : end * HEAD_DIM]
+        r3v = along(r3v if begin == 0 else after(r3v, totals), OUTER)
+        r3v = r3v if begin == 0 else after(r3v, out[1])
+        out = add_far(mixed, totals, far_weights, r1v, r2v, r3v, begin, end)
         out = [out[0]] + [to_head(out[d], d) for d in (1, 2, 3)]
         for d in range(4):
             result = lax.dynamic_update_slice_in_dim(result, out[d], (h ^ d) * width + begin * HEAD_DIM, axis=1)

time: 94.3 us -> 86.4 us (0.916)
  Pallas kernels: 15.5 us -> 11.8 us
  local copies, waits for them, and re-layouts: 7.45 us -> 4.21 us
  waiting for transfers between devices: 39.9 us -> 37.1 us
  starting transfers between devices: 27.8 us -> 30.1 us
    ppermute x11, waiting for transfers between devices: 12.9 us -> 9.06 us  [to_head(): return lax.ppermute(array, 'head', [(i, i ^ d) for i in range(4)])]
    pallas_call x7, Pallas kernels: 14.8 us -> 11.1 us  [the longest x1 7.79 us: attend_near(): pl.pallas_call(attention_kernel, grid=(heads,), in_specs=[pl.BlockSpec(me...]
    unnamed x24 -> x26, local copies, waits for them, and re-layouts: 4.23 us -> 1.13 us
    ppermute x13 -> x8, starting transfers between devices: 19.4 us -> 21.5 us  [along(): return lax.ppermute(array, 'frame', pairs)]
    ppermute x13 -> x8, waiting for transfers between devices: 27.1 us -> 28 us  [along(): return lax.ppermute(array, 'frame', pairs)]
    concatenate x5 -> x6, other arithmetic: 1.89 us -> 1.85 us  [below(): return jnp.concatenate(arrays, axis=0)]
  transfers between devices with their start and end apart: 24 -> 24, of which waited for: 9 -> 11; matrix products, arithmetic and copies ran while one was open for 3% -> 3% of each run, Pallas kernels for 17% -> 13%
where the time goes in v9:
time: 86.4 us; the launch traced here: 86.1 us
  waiting for transfers between devices  37.1 us (43%)
  starting transfers between devices  30.1 us (35%)
  Pallas kernels  11.8 us (14%)
  local copies, waits for them, and re-layouts  4.21 us (5%)
  other arithmetic  1.9 us (2%)
  between operations  0.99 us (1%)
    ppermute x8, waiting for transfers between devices, along(): return lax.ppermute(array, 'frame', pairs)  28 us
    ppermute x8, starting transfers between devices, along(): return lax.ppermute(array, 'frame', pairs)  21.5 us
    ppermute x11, waiting for transfers between devices, to_head(): return lax.ppermute(array, 'head', [(i, i ^ d) for i in range(4)])  9.06 us
    ppermute x11, starting transfers between devices, to_head(): return lax.ppermute(array, 'head', [(i, i ^ d) for i in range(4)])  8.15 us
    pallas_call x1, Pallas kernels, attend_near(): pl.pallas_call(attention_kernel, grid=(heads,), in_specs=[pl.BlockSpec(me...  7.79 us
    pallas_call x2, Pallas kernels, add_far(): pl.pallas_call(far_kernel, grid=(heads,), in_specs=[spec for _, spec in b...  2.03 us
    concatenate x6, other arithmetic, below(): return jnp.concatenate(arrays, axis=0)  1.85 us
  transfers between devices with their start and end apart: 24, of which 11 were waited for; matrix products, arithmetic and copies ran while one was open for 3% of the time, Pallas kernels for 13%

profile of v9, /device:TPU:0, one launch (start us, length us, event | category | flops | bytes accessed | tf_op | source)
XLA Modules:
  0.0 86.1 jit_solution(17978555558022154470)
XLA Ops:
  0.0 1.5 %constant_dynamic-slice_fusion = (bf16[128,640]{1,0:T(8,128)(2,1)S(1)}, bf16[128,640]{1,0:T(8,128)(2,1)S(1)}, bf16[128,640]{1,0:T(8,128)(2,1)S(1)}, bf16[128,640...) fusion(bf16[128,2560]{1,0:T(8,128)(2,1)} %refs_2_.1, ...), kind=kLoop, calls=%fused_computation.15 | loop fusion | bytes 2621456 | tf_op jit(solution)/shard_map/dynamic_slice | solution.py:370
  1.6 0.5 collective-permute-start
  2.8 1.1 %collective-permute-done = bf16[128,2560]{1,0:T(8,128)(2,1)S(1)} collective-permute-done((bf16[128,2560]{1,0:T(8,128)(2,1)S(1)}, bf16[128,2560]{1,0:T(8,128)(2,1)S(1)}, u32[]{:S(2)}, u32[]{:S(2)}) %collective-permute-start) | collective-permute-done | bytes 655392 | tf_op jit(solution)/shard_map/ppermute | solution.py:379
  3.9 0.1 fusion
  4.0 0.7 shard_map.55
  4.7 3.0 %collective-permute-start.2 = (bf16[272,640]{1,0:T(8,128)(2,1)S(1)}, bf16[272,640]{1,0:T(8,128)(2,1)S(1)}, u32[]{:S(2)}, u32[]{:S(2)}) collective-permute-start(bf16[272,640]{1,0:T(8,128)(2,1)S(1)} %pad_maximum_fusion.2.km), channel_id=1, source_target_pairs={{0,4},{4,0},{8,12},{12,8},{1,5},{5,1},{9,13},{13,9},{2,6},{6,2},{1... | collective-permute-start | bytes 1044488 | tf_op jit(solution)/shard_map/ppermute | solution.py:382
  7.7 1.6 %collective-permute-start.6 = (bf16[256,640]{1,0:T(8,128)(2,1)S(1)}, bf16[256,640]{1,0:T(8,128)(2,1)S(1)}, u32[]{:S(2)}, u32[]{:S(2)}) collective-permute-start(bf16[256,640]{1,0:T(8,128)(2,1)S(1)} %pad_maximum_fusion.6), channel_id=1, source_target_pairs={{0,2},{1,3},{2,0},{3,1},{4,6},{5,7},{6,4},{7,5},{8,10},{9,11},{10,... | collective-permute-start | bytes 983048 | tf_op jit(solution)/shard_map/ppermute | solution.py:379
  9.3 6.8 %collective-permute-done.2.told.n1km = bf16[272,640]{1,0:T(8,128)(2,1)S(1)} collective-permute-done((bf16[272,640]{1,0:T(8,128)(2,1)S(1)}, bf16[272,640]{1,0:T(8,128)(2,1)S(1)}, u32[]{:S(2)}, u32[]{:S(2)}) %collective-permute-start.2) | collective-permute-done | bytes 348192 | tf_op jit(solution)/shard_map/ppermute | solution.py:382
  16.2 1.7 %collective-permute-start.4 = (bf16[256,640]{1,0:T(8,128)(2,1)S(1)}, bf16[256,640]{1,0:T(8,128)(2,1)S(1)}, u32[]{:S(2)}, u32[]{:S(2)}) collective-permute-start(bf16[256,640]{1,0:T(8,128)(2,1)S(1)} %pad_maximum_fusion.5), channel_id=1, source_target_pairs={{0,2},{1,3},{2,0},{3,1},{4,6},{5,7},{6,4},{7,5},{8,10},{9,11},{10,... | collective-permute-start | bytes 983048 | tf_op jit(solution)/shard_map/ppermute | solution.py:379
  17.8 0.1 collective-permute-done.6.ko
  17.9 0.4 collective-permute-start.8
  18.3 4.0 %collective-permute-start.7 = (bf16[256,640]{1,0:T(8,128)(2,1)S(1)}, bf16[256,640]{1,0:T(8,128)(2,1)S(1)}, u32[]{:S(2)}, u32[]{:S(2)}) collective-permute-start(bf16[256,640]{1,0:T(8,128)(2,1)S(1)} %collective-permute-done.6.ko), channel_id=1, source_target_pairs={{0,4},{4,0},{8,12},{12,8},{1,5},{5,1},{9,13},{13,9},{2,6},{6,2},{1... | collective-permute-start | bytes 983048 | tf_op jit(solution)/shard_map/ppermute | solution.py:382
  22.3 3.1 %collective-permute-done.4 = bf16[256,640]{1,0:T(8,128)(2,1)S(1)} collective-permute-done((bf16[256,640]{1,0:T(8,128)(2,1)S(1)}, bf16[256,640]{1,0:T(8,128)(2,1)S(1)}, u32[]{:S(2)}, u32[]{:S(2)}) %collective-permute-start.4) | collective-permute-done | bytes 327712 | tf_op jit(solution)/shard_map/ppermute | solution.py:379
  25.4 0.1 pad_maximum_fusion.1.v
  25.5 2.6 %collective-permute-start.12 = (bf16[512,640]{1,0:T(8,128)(2,1)S(1)}, bf16[512,640]{1,0:T(8,128)(2,1)S(1)}, u32[]{:S(2)}, u32[]{:S(2)}) collective-permute-start(bf16[512,640]{1,0:T(8,128)(2,1)S(1)} %pad_maximum_fusion.1.v), channel_id=1, source_target_pairs={{0,4},{4,0},{8,12},{12,8},{1,5},{5,1},{9,13},{13,9},{2,6},{6,2},{1... | collective-permute-start | bytes 1966088 | tf_op jit(solution)/shard_map/ppermute | solution.py:382
  28.1 0.1 shard_map.57
  28.2 3.1 %collective-permute-start.10 = (bf16[256,640]{1,0:T(8,128)(2,1)S(1)}, bf16[256,640]{1,0:T(8,128)(2,1)S(1)}, u32[]{:S(2)}, u32[]{:S(2)}) collective-permute-start(bf16[256,640]{1,0:T(8,128)(2,1)S(1)} %shard_map.57), channel_id=1, source_target_pairs={{0,4},{4,0},{8,12},{12,8},{1,5},{5,1},{9,13},{13,9},{2,6},{6,2},{1... | collective-permute-start | bytes 983048 | tf_op jit(solution)/shard_map/ppermute | solution.py:382
  31.3 0.1 shard_map.56
  31.5 0.1 collective-permute-start.9
  31.6 0.7 fusion.1
  32.3 0.8 pad_maximum_fusion.4
  33.0 0.6 collective-permute-start.5
  33.6 11.3 %collective-permute-done.12.n1v.refs_0_ = bf16[512,640]{1,0:T(8,128)(2,1)S(1)} collective-permute-done((bf16[512,640]{1,0:T(8,128)(2,1)S(1)}, bf16[512,640]{1,0:T(8,128)(2,1)S(1)}, u32[]{:S(2)}, u32[]{:S(2)}) %collective-permute-start.12) | collective-permute-done | bytes 655392 | tf_op jit(solution)/shard_map/ppermute | solution.py:382
  44.9 0.9 %shard_map.59 = bf16[256,640]{1,0:T(8,128)(2,1)} custom-call(bf16[272,640]{1,0:T(8,128)(2,1)S(1)} %collective-permute-done.2.told.n1km, bf16[512,640]{1,0:T(8,128)(2,1)S(1)} %collective-permute-done.12.n1v.refs_0_), custom_call_target="tpu_custom_call" | custom-call | tf_op jit(solution)/shard_map/pallas_call | solution.py:354
  45.8 5.7 %collective-permute-done.10.r2 = bf16[256,640]{1,0:T(8,128)(2,1)S(1)} collective-permute-done((bf16[256,640]{1,0:T(8,128)(2,1)S(1)}, bf16[256,640]{1,0:T(8,128)(2,1)S(1)}, u32[]{:S(2)}, u32[]{:S(2)}) %collective-permute-start.10) | collective-permute-done | bytes 327712 | tf_op jit(solution)/shard_map/ppermute | solution.py:382
  51.4 0.7 copy-done.10
  52.2 1.7 %collective-permute-start.11 = (bf16[256,640]{1,0:T(8,128)(2,1)}, bf16[256,640]{1,0:T(8,128)(2,1)}, u32[]{:S(2)}, u32[]{:S(2)}) collective-permute-start(bf16[256,640]{1,0:T(8,128)(2,1)} %collective-permute-done.9.r1), channel_id=1, source_target_pairs={{0,4},{4,0},{8,12},{12,8},{1,5},{5,1},{9,13},{13,9},{2,6},{6,2},{1... | collective-permute-start | bytes 983048 | tf_op jit(solution)/shard_map/ppermute | solution.py:382
  53.9 0.1 shard_map.60
  54.1 0.3 collective-permute-start.15
  54.4 0.9 %pad_maximum_fusion.3.q_mine = bf16[256,640]{1,0:T(8,128)(2,1)S(1)} fusion(bf16[128,640]{1,0:T(8,128)(2,1)} %get-tuple-element.78, bf16[128,640]{1,0:T(8,128)(2,1)S(1)} %get-tuple-element.40), kind=kLoop, calls=%fused_computation.3 | loop fusion | flops 655360 | bytes 655360 | tf_op jit(solution)/shard_map/concatenate | solution.py:376
  55.4 3.4 %collective-permute-start.16 = (bf16[256,384]{1,0:T(8,128)(2,1)S(1)}, bf16[256,384]{1,0:T(8,128)(2,1)S(1)}, u32[]{:S(2)}, u32[]{:S(2)}) collective-permute-start(bf16[256,384]{1,0:T(8,128)(2,1)S(1)} %slice.38), channel_id=1, source_target_pairs={{0,4},{4,0},{8,12},{12,8},{1,5},{5,1},{9,13},{13,9},{2,6},{6,2},{1... | collective-permute-start | bytes 589832 | tf_op jit(solution)/shard_map/ppermute | solution.py:382
  58.8 4.3 %collective-permute-done.11.r3 = bf16[256,640]{1,0:T(8,128)(2,1)} collective-permute-done((bf16[256,640]{1,0:T(8,128)(2,1)}, bf16[256,640]{1,0:T(8,128)(2,1)}, u32[]{:S(2)}, u32[]{:S(2)}) %collective-permute-start.11) | collective-permute-done | bytes 327712 | tf_op jit(solution)/shard_map/ppermute | solution.py:382
  63.1 7.8 %shard_map.58 = (f32[2560,128]{1,0:T(8,128)S(1)}, f32[2560,128]{1,0:T(8,128)S(1)}, bf16[2560,512]{1,0:T(8,128)(2,1)S(1)}) custom-call(s32[1,4]{1,0:T(1,128)S(1)} %copy-done.7, bf16[256,640]{1,0:T(8,128)(2,1)S(1)} %pad_maximum_fusion.3.q_mine, bf16[256,640]{1,0:T(8,128)(2,1)} %collective-permute-done.5.q_other, bf16[272,640]{1,0:T(8,128)(2,1)S(1)} %pad_maximum_fusion.2.km, ...), custom_call_target="tpu_custom_call" | custom-call | flops 2348810240 | bytes 6553600 | tf_op jit(solution)/shard_map/pallas_call | solution.py:263
  70.9 3.3 %collective-permute-start.20 = (bf16[256,256]{1,0:T(8,128)(2,1)S(1)}, bf16[256,256]{1,0:T(8,128)(2,1)S(1)}, u32[]{:S(2)}, u32[]{:S(2)}) collective-permute-start(bf16[256,256]{1,0:T(8,128)(2,1)S(1)} %slice.39), channel_id=1, source_target_pairs={{0,4},{4,0},{8,12},{12,8},{1,5},{5,1},{9,13},{13,9},{2,6},{6,2},{1... | collective-permute-start | bytes 393224 | tf_op jit(solution)/shard_map/ppermute | solution.py:382
  74.2 1.2 %shard_map.61 = (bf16[128,384]{1,0:T(8,128)(2,1)S(1)}, bf16[128,384]{1,0:T(8,128)(2,1)S(1)}, bf16[128,384]{1,0:T(8,128)(2,1)S(1)}, bf16[128,384]{1,0:T(8,128)(2,1)S(1)}) custom-call(f32[2560,128]{1,0:T(8,128)S(1)} %get-tuple-element.52.mixed, f32[2560,128]{1,0:T(8,128)S(1)} %get-tuple-element.53.totals, bf16[2560,512]{1,0:T(8,128)(2,1)S(1)} %get-tuple-element.54.far_weights, ...), custom_call_target="tpu_custom_call" | custom-call | flops 201326592 | bytes 4718592 | tf_op jit(solution)/shard_map/pallas_call | solution.py:284
  75.4 0.1 collective-permute-start.17
  75.5 0.6 collective-permute-start.18
  76.1 1.3 %collective-permute-start.19 = (bf16[128,384]{1,0:T(8,128)(2,1)S(1)}, bf16[128,384]{1,0:T(8,128)(2,1)S(1)}, u32[]{:S(2)}, u32[]{:S(2)}) collective-permute-start(bf16[128,384]{1,0:T(8,128)(2,1)S(1)} %get-tuple-element.58), channel_id=1, source_target_pairs={{0,3},{1,2},{2,1},{3,0},{4,7},{5,6},{6,5},{7,4},{8,11},{9,10},{10,... | collective-permute-start | bytes 294920 | tf_op jit(solution)/shard_map/ppermute | solution.py:379
  77.4 0.8 shard_map.62
  78.3 0.4 collective-permute-start.21
  78.7 0.5 collective-permute-start.22
  79.2 1.0 %collective-permute-start.23 = (bf16[128,256]{1,0:T(8,128)(2,1)S(1)}, bf16[128,256]{1,0:T(8,128)(2,1)S(1)}, u32[]{:S(2)}, u32[]{:S(2)}) collective-permute-start(bf16[128,256]{1,0:T(8,128)(2,1)S(1)} %get-tuple-element.64), channel_id=1, source_target_pairs={{0,3},{1,2},{2,1},{3,0},{4,7},{5,6},{6,5},{7,4},{8,11},{9,10},{10,... | collective-permute-start | bytes 196616 | tf_op jit(solution)/shard_map/ppermute | solution.py:379
  80.2 0.9 %collective-permute-done.18 = bf16[128,384]{1,0:T(8,128)(2,1)S(1)} collective-permute-done((bf16[128,384]{1,0:T(8,128)(2,1)S(1)}, bf16[128,384]{1,0:T(8,128)(2,1)S(1)}, u32[]{:S(2)}, u32[]{:S(2)}) %collective-permute-start.18) | collective-permute-done | bytes 98336 | tf_op jit(solution)/shard_map/ppermute | solution.py:379
  81.2 1.2 %collective-permute-done.19 = bf16[128,384]{1,0:T(8,128)(2,1)S(1)} collective-permute-done((bf16[128,384]{1,0:T(8,128)(2,1)S(1)}, bf16[128,384]{1,0:T(8,128)(2,1)S(1)}, u32[]{:S(2)}, u32[]{:S(2)}) %collective-permute-start.19) | collective-permute-done | bytes 98336 | tf_op jit(solution)/shard_map/ppermute | solution.py:379
  82.4 2.2 %collective-permute-done.22 = bf16[128,256]{1,0:T(8,128)(2,1)S(1)} collective-permute-done((bf16[128,256]{1,0:T(8,128)(2,1)S(1)}, bf16[128,256]{1,0:T(8,128)(2,1)S(1)}, u32[]{:S(2)}, u32[]{:S(2)}) %collective-permute-start.22) | collective-permute-done | bytes 65568 | tf_op jit(solution)/shard_map/ppermute | solution.py:379
  84.7 0.5 collective-permute-done.23
  85.2 0.4 copy-done.12
  85.5 0.6 constant_dynamic-update-slice_fusion
  (55 shorter events, 0.4 us)
Async XLA Ops:
  1.5 2.4 %copy-start = (bf16[128,2560]{1,0:T(8,128)(2,1)S(1)}, bf16[128,2560]{1,0:T(8,128)(2,1)}, u32[]{:S(2)}) copy-start(bf16[128,2560]{1,0:T(8,128)(2,1)} %refs_1_.1) | copy-start | bytes 1966084
  1.5 2.4 %copy-start.1 = (bf16[128,2560]{1,0:T(8,128)(2,1)S(1)}, bf16[128,2560]{1,0:T(8,128)(2,1)}, u32[]{:S(2)}) copy-start(bf16[128,2560]{1,0:T(8,128)(2,1)} %refs_2_.1) | copy-start | bytes 1966084
  1.5 2.4 %copy-start.2 = (bf16[128,2560]{1,0:T(8,128)(2,1)S(1)}, bf16[128,2560]{1,0:T(8,128)(2,1)}, u32[]{:S(2)}) copy-start(bf16[128,2560]{1,0:T(8,128)(2,1)} %refs_0_.1) | copy-start | bytes 1966084
  1.6 2.4 %copy-start.7 = (s32[1,4]{1,0:T(1,128)S(1)}, s32[1,4]{1,0:T(1,128)}, u32[]{:S(2)}) copy-start(s32[1,4]{1,0:T(1,128)} %mask.2) | copy-start | bytes 52
  1.6 2.2 %collective-permute-start = (bf16[128,2560]{1,0:T(8,128)(2,1)S(1)}, bf16[128,2560]{1,0:T(8,128)(2,1)S(1)}, u32[]{:S(2)}, u32[]{:S(2)}) collective-permute-start(bf16[128,2560]{1,0:T(8,128)(2,1)S(1)} %pad_maximum_fusion), channel_id=1, source_target_pairs={{0,1},{1,0},{2,3},{3,2},{4,5},{5,4},{6,7},{7,6},{8,9},{9,8},{10,11... | collective-permute-start | bytes 1966088 | tf_op jit(solution)/shard_map/ppermute | solution.py:379
  4.7 11.5 %collective-permute-start.2 = (bf16[272,640]{1,0:T(8,128)(2,1)S(1)}, bf16[272,640]{1,0:T(8,128)(2,1)S(1)}, u32[]{:S(2)}, u32[]{:S(2)}) collective-permute-start(bf16[272,640]{1,0:T(8,128)(2,1)S(1)} %pad_maximum_fusion.2.km), channel_id=1, source_target_pairs={{0,4},{4,0},{8,12},{12,8},{1,5},{5,1},{9,13},{13,9},{2,6},{6,2},{1... | collective-permute-start | bytes 1044488 | tf_op jit(solution)/shard_map/ppermute | solution.py:382
  7.7 8.5 %collective-permute-start.3 = (bf16[272,640]{1,0:T(8,128)(2,1)S(1)}, bf16[272,640]{1,0:T(8,128)(2,1)S(1)}, u32[]{:S(2)}, u32[]{:S(2)}) collective-permute-start(bf16[272,640]{1,0:T(8,128)(2,1)S(1)} %pad_maximum_fusion.2.km), channel_id=1, source_target_pairs={{0,1},{1,0},{2,3},{3,2},{4,8},{5,9},{6,10},{7,11},{8,4},{9,5},{10,... | collective-permute-start | bytes 1044488 | tf_op jit(solution)/shard_map/ppermute | solution.py:386
  7.7 10.2 %collective-permute-start.6 = (bf16[256,640]{1,0:T(8,128)(2,1)S(1)}, bf16[256,640]{1,0:T(8,128)(2,1)S(1)}, u32[]{:S(2)}, u32[]{:S(2)}) collective-permute-start(bf16[256,640]{1,0:T(8,128)(2,1)S(1)} %pad_maximum_fusion.6), channel_id=1, source_target_pairs={{0,2},{1,3},{2,0},{3,1},{4,6},{5,7},{6,4},{7,5},{8,10},{9,11},{10,... | collective-permute-start | bytes 983048 | tf_op jit(solution)/shard_map/ppermute | solution.py:379
  16.2 9.2 %collective-permute-start.4 = (bf16[256,640]{1,0:T(8,128)(2,1)S(1)}, bf16[256,640]{1,0:T(8,128)(2,1)S(1)}, u32[]{:S(2)}, u32[]{:S(2)}) collective-permute-start(bf16[256,640]{1,0:T(8,128)(2,1)S(1)} %pad_maximum_fusion.5), channel_id=1, source_target_pairs={{0,2},{1,3},{2,0},{3,1},{4,6},{5,7},{6,4},{7,5},{8,10},{9,11},{10,... | collective-permute-start | bytes 983048 | tf_op jit(solution)/shard_map/ppermute | solution.py:379
  17.8 13.8 %collective-permute-start.1 = (bf16[128,1280]{1,0:T(8,128)(2,1)S(1)}, bf16[128,1280]{1,0:T(8,128)(2,1)S(1)}, u32[]{:S(2)}, u32[]{:S(2)}) collective-permute-start(bf16[128,1280]{1,0:T(8,128)(2,1)S(1)} %get-tuple-element.41), channel_id=1, source_target_pairs={{0,1},{1,0},{2,3},{3,2},{4,5},{5,4},{6,7},{7,6},{8,9},{9,8},{10,11... | collective-permute-start | bytes 983048 | tf_op jit(solution)/shard_map/ppermute | solution.py:379
  17.9 13.6 %copy-start.8 = (bf16[256,640]{1,0:T(8,128)(2,1)}, bf16[256,640]{1,0:T(8,128)(2,1)S(1)}, u32[]{:S(2)}) copy-start(bf16[256,640]{1,0:T(8,128)(2,1)S(1)} %collective-permute-done.6.ko) | copy-start | bytes 983044
  17.9 10.2 %collective-permute-start.8 = (bf16[256,640]{1,0:T(8,128)(2,1)S(1)}, bf16[256,640]{1,0:T(8,128)(2,1)S(1)}, u32[]{:S(2)}, u32[]{:S(2)}) collective-permute-start(bf16[256,640]{1,0:T(8,128)(2,1)S(1)} %collective-permute-done.6.ko), channel_id=1, source_target_pairs={{0,1},{1,0},{2,3},{3,2},{4,8},{5,9},{6,10},{7,11},{8,4},{9,5},{10,... | collective-permute-start | bytes 983048 | tf_op jit(solution)/shard_map/ppermute | solution.py:386
  18.3 13.0 %collective-permute-start.7 = (bf16[256,640]{1,0:T(8,128)(2,1)S(1)}, bf16[256,640]{1,0:T(8,128)(2,1)S(1)}, u32[]{:S(2)}, u32[]{:S(2)}) collective-permute-start(bf16[256,640]{1,0:T(8,128)(2,1)S(1)} %collective-permute-done.6.ko), channel_id=1, source_target_pairs={{0,4},{4,0},{8,12},{12,8},{1,5},{5,1},{9,13},{13,9},{2,6},{6,2},{1... | collective-permute-start | bytes 983048 | tf_op jit(solution)/shard_map/ppermute | solution.py:382
  25.5 19.4 %collective-permute-start.12 = (bf16[512,640]{1,0:T(8,128)(2,1)S(1)}, bf16[512,640]{1,0:T(8,128)(2,1)S(1)}, u32[]{:S(2)}, u32[]{:S(2)}) collective-permute-start(bf16[512,640]{1,0:T(8,128)(2,1)S(1)} %pad_maximum_fusion.1.v), channel_id=1, source_target_pairs={{0,4},{4,0},{8,12},{12,8},{1,5},{5,1},{9,13},{13,9},{2,6},{6,2},{1... | collective-permute-start | bytes 1966088 | tf_op jit(solution)/shard_map/ppermute | solution.py:382
  28.1 25.8 %collective-permute-start.13 = (bf16[512,640]{1,0:T(8,128)(2,1)S(1)}, bf16[512,640]{1,0:T(8,128)(2,1)S(1)}, u32[]{:S(2)}, u32[]{:S(2)}) collective-permute-start(bf16[512,640]{1,0:T(8,128)(2,1)S(1)} %pad_maximum_fusion.1.v), channel_id=1, source_target_pairs={{0,1},{1,0},{2,3},{3,2},{4,8},{5,9},{6,10},{7,11},{8,4},{9,5},{10,... | collective-permute-start | bytes 1966088 | tf_op jit(solution)/shard_map/ppermute | solution.py:386
  28.1 4.2 %copy-start.3 = (bf16[256,640]{1,0:T(8,128)(2,1)}, bf16[256,640]{1,0:T(8,128)(2,1)S(1)}, u32[]{:S(2)}) copy-start(bf16[256,640]{1,0:T(8,128)(2,1)S(1)} %collective-permute-done.8.refs_0_.n2ko) | copy-start | bytes 983044
  28.2 23.2 %collective-permute-start.10 = (bf16[256,640]{1,0:T(8,128)(2,1)S(1)}, bf16[256,640]{1,0:T(8,128)(2,1)S(1)}, u32[]{:S(2)}, u32[]{:S(2)}) collective-permute-start(bf16[256,640]{1,0:T(8,128)(2,1)S(1)} %shard_map.57), channel_id=1, source_target_pairs={{0,4},{4,0},{8,12},{12,8},{1,5},{5,1},{9,13},{13,9},{2,6},{6,2},{1... | collective-permute-start | bytes 983048 | tf_op jit(solution)/shard_map/ppermute | solution.py:382
  31.3 14.4 %copy-start.5 = (bf16[256,640]{1,0:T(8,128)(2,1)}, bf16[256,640]{1,0:T(8,128)(2,1)S(1)}, u32[]{:S(2)}) copy-start(bf16[256,640]{1,0:T(8,128)(2,1)S(1)} %collective-permute-done.7.refs_0_.n1ko) | copy-start | bytes 983044
  31.5 20.7 %collective-permute-start.9 = (bf16[256,640]{1,0:T(8,128)(2,1)S(1)}, bf16[256,640]{1,0:T(8,128)(2,1)}, u32[]{:S(2)}, u32[]{:S(2)}) collective-permute-start(bf16[256,640]{1,0:T(8,128)(2,1)S(1)} %shard_map.56), channel_id=1, source_target_pairs={{0,1},{1,0},{2,3},{3,2},{4,8},{5,9},{6,10},{7,11},{8,4},{9,5},{10,... | collective-permute-start | bytes 983048 | tf_op jit(solution)/shard_map/ppermute | solution.py:386
  33.0 25.8 %collective-permute-start.5 = (bf16[256,640]{1,0:T(8,128)(2,1)}, bf16[256,640]{1,0:T(8,128)(2,1)}, u32[]{:S(2)}, u32[]{:S(2)}) collective-permute-start(bf16[256,640]{1,0:T(8,128)(2,1)} %pad_maximum_fusion.4), channel_id=1, source_target_pairs={{0,2},{1,3},{2,0},{3,1},{4,6},{5,7},{6,4},{7,5},{8,10},{9,11},{10,... | collective-permute-start | bytes 983048 | tf_op jit(solution)/shard_map/ppermute | solution.py:379
  45.8 9.6 %collective-permute-start.14 = (bf16[256,640]{1,0:T(8,128)(2,1)}, bf16[256,640]{1,0:T(8,128)(2,1)S(1)}, u32[]{:S(2)}, u32[]{:S(2)}) collective-permute-start(bf16[256,640]{1,0:T(8,128)(2,1)} %shard_map.59), channel_id=1, source_target_pairs={{0,1},{1,0},{2,3},{3,2},{4,8},{5,9},{6,10},{7,11},{8,4},{9,5},{10,... | collective-permute-start | bytes 983048 | tf_op jit(solution)/shard_map/ppermute | solution.py:386
  51.4 0.7 copy-start.10
  52.2 10.9 %collective-permute-start.11 = (bf16[256,640]{1,0:T(8,128)(2,1)}, bf16[256,640]{1,0:T(8,128)(2,1)}, u32[]{:S(2)}, u32[]{:S(2)}) collective-permute-start(bf16[256,640]{1,0:T(8,128)(2,1)} %collective-permute-done.9.r1), channel_id=1, source_target_pairs={{0,4},{4,0},{8,12},{12,8},{1,5},{5,1},{9,13},{13,9},{2,6},{6,2},{1... | collective-permute-start | bytes 983048 | tf_op jit(solution)/shard_map/ppermute | solution.py:382
  53.9 9.2 %copy-start.4 = (bf16[256,640]{1,0:T(8,128)(2,1)S(1)}, bf16[256,640]{1,0:T(8,128)(2,1)}, u32[]{:S(2)}) copy-start(bf16[256,640]{1,0:T(8,128)(2,1)} %copy-done.3) | copy-start | bytes 983044
  53.9 9.2 %copy-start.6 = (bf16[256,640]{1,0:T(8,128)(2,1)S(1)}, bf16[256,640]{1,0:T(8,128)(2,1)}, u32[]{:S(2)}) copy-start(bf16[256,640]{1,0:T(8,128)(2,1)} %copy-done.5) | copy-start | bytes 983044
  53.9 9.2 %copy-start.9 = (bf16[256,640]{1,0:T(8,128)(2,1)S(1)}, bf16[256,640]{1,0:T(8,128)(2,1)}, u32[]{:S(2)}) copy-start(bf16[256,640]{1,0:T(8,128)(2,1)} %copy-done.8) | copy-start | bytes 983044
  53.9 9.2 %copy-start.11 = (bf16[256,640]{1,0:T(8,128)(2,1)S(1)}, bf16[256,640]{1,0:T(8,128)(2,1)}, u32[]{:S(2)}) copy-start(bf16[256,640]{1,0:T(8,128)(2,1)} %copy-done.10) | copy-start | bytes 983044
  54.1 20.1 %collective-permute-start.15 = (bf16[256,640]{1,0:T(8,128)(2,1)S(1)}, bf16[256,640]{1,0:T(8,128)(2,1)S(1)}, u32[]{:S(2)}, u32[]{:S(2)}) collective-permute-start(bf16[256,640]{1,0:T(8,128)(2,1)S(1)} %shard_map.60), channel_id=1, source_target_pairs={{0,4},{4,0},{8,12},{12,8},{1,5},{5,1},{9,13},{13,9},{2,6},{6,2},{1... | collective-permute-start | bytes 983048 | tf_op jit(solution)/shard_map/ppermute | solution.py:382
  55.4 18.8 %collective-permute-start.16 = (bf16[256,384]{1,0:T(8,128)(2,1)S(1)}, bf16[256,384]{1,0:T(8,128)(2,1)S(1)}, u32[]{:S(2)}, u32[]{:S(2)}) collective-permute-start(bf16[256,384]{1,0:T(8,128)(2,1)S(1)} %slice.38), channel_id=1, source_target_pairs={{0,4},{4,0},{8,12},{12,8},{1,5},{5,1},{9,13},{13,9},{2,6},{6,2},{1... | collective-permute-start | bytes 589832 | tf_op jit(solution)/shard_map/ppermute | solution.py:382
  70.9 6.5 %collective-permute-start.20 = (bf16[256,256]{1,0:T(8,128)(2,1)S(1)}, bf16[256,256]{1,0:T(8,128)(2,1)S(1)}, u32[]{:S(2)}, u32[]{:S(2)}) collective-permute-start(bf16[256,256]{1,0:T(8,128)(2,1)S(1)} %slice.39), channel_id=1, source_target_pairs={{0,4},{4,0},{8,12},{12,8},{1,5},{5,1},{9,13},{13,9},{2,6},{6,2},{1... | collective-permute-start | bytes 393224 | tf_op jit(solution)/shard_map/ppermute | solution.py:382
  75.4 2.0 %collective-permute-start.17 = (bf16[128,384]{1,0:T(8,128)(2,1)S(1)}, bf16[128,384]{1,0:T(8,128)(2,1)S(1)}, u32[]{:S(2)}, u32[]{:S(2)}) collective-permute-start(bf16[128,384]{1,0:T(8,128)(2,1)S(1)} %get-tuple-element.56), channel_id=1, source_target_pairs={{0,1},{1,0},{2,3},{3,2},{4,5},{5,4},{6,7},{7,6},{8,9},{9,8},{10,11... | collective-permute-start | bytes 294920 | tf_op jit(solution)/shard_map/ppermute | solution.py:379
  75.5 5.7 %collective-permute-start.18 = (bf16[128,384]{1,0:T(8,128)(2,1)S(1)}, bf16[128,384]{1,0:T(8,128)(2,1)S(1)}, u32[]{:S(2)}, u32[]{:S(2)}) collective-permute-start(bf16[128,384]{1,0:T(8,128)(2,1)S(1)} %get-tuple-element.57), channel_id=1, source_target_pairs={{0,2},{1,3},{2,0},{3,1},{4,6},{5,7},{6,4},{7,5},{8,10},{9,11},{10,... | collective-permute-start | bytes 294920 | tf_op jit(solution)/shard_map/ppermute | solution.py:379
  76.1 6.3 %collective-permute-start.19 = (bf16[128,384]{1,0:T(8,128)(2,1)S(1)}, bf16[128,384]{1,0:T(8,128)(2,1)S(1)}, u32[]{:S(2)}, u32[]{:S(2)}) collective-permute-start(bf16[128,384]{1,0:T(8,128)(2,1)S(1)} %get-tuple-element.58), channel_id=1, source_target_pairs={{0,3},{1,2},{2,1},{3,0},{4,7},{5,6},{6,5},{7,4},{8,11},{9,10},{10,... | collective-permute-start | bytes 294920 | tf_op jit(solution)/shard_map/ppermute | solution.py:379
  78.3 4.1 %collective-permute-start.21 = (bf16[128,256]{1,0:T(8,128)(2,1)S(1)}, bf16[128,256]{1,0:T(8,128)(2,1)S(1)}, u32[]{:S(2)}, u32[]{:S(2)}) collective-permute-start(bf16[128,256]{1,0:T(8,128)(2,1)S(1)} %get-tuple-element.62), channel_id=1, source_target_pairs={{0,1},{1,0},{2,3},{3,2},{4,5},{5,4},{6,7},{7,6},{8,9},{9,8},{10,11... | collective-permute-start | bytes 196616 | tf_op jit(solution)/shard_map/ppermute | solution.py:379
  78.7 6.0 %collective-permute-start.22 = (bf16[128,256]{1,0:T(8,128)(2,1)S(1)}, bf16[128,256]{1,0:T(8,128)(2,1)S(1)}, u32[]{:S(2)}, u32[]{:S(2)}) collective-permute-start(bf16[128,256]{1,0:T(8,128)(2,1)S(1)} %get-tuple-element.63), channel_id=1, source_target_pairs={{0,2},{1,3},{2,0},{3,1},{4,6},{5,7},{6,4},{7,5},{8,10},{9,11},{10,... | collective-permute-start | bytes 196616 | tf_op jit(solution)/shard_map/ppermute | solution.py:379
  79.2 5.9 %collective-permute-start.23 = (bf16[128,256]{1,0:T(8,128)(2,1)S(1)}, bf16[128,256]{1,0:T(8,128)(2,1)S(1)}, u32[]{:S(2)}, u32[]{:S(2)}) collective-permute-start(bf16[128,256]{1,0:T(8,128)(2,1)S(1)} %get-tuple-element.64), channel_id=1, source_target_pairs={{0,3},{1,2},{2,1},{3,0},{4,7},{5,6},{6,5},{7,4},{8,11},{9,10},{10,... | collective-permute-start | bytes 196616 | tf_op jit(solution)/shard_map/ppermute | solution.py:379
  84.7 0.8 copy-start.12

commit v10 on v9

--- a/solution.py
+++ b/solution.py
@@ -182,8 +182,9 @@
     return free if top is None else jnp.maximum(free, top)
 
 
-def attention_kernel(mask, q_mine, q_other, km, ko, n1km, n1ko, n2km, n2ko, r1, r2, r3, v, n1v, n2v, *rest):
-    mixed_out, totals, far_weights, held0, held1 = rest
+def attention_kernel(mask, q_mine, q_other, *rest):
+    keys, (r1, r2, r3), values = rest[:6], rest[6:9], rest[9:15]
+    mixed_out, totals, far_weights, held0, held1 = rest[15:]
     factor = SCALE * LOG2E
     z = lax.axis_index("frame")
     tile = r1.shape[0]
@@ -201,8 +202,7 @@
                 w = jnp.exp2((held[:, at * tile : (at + 1) * tile] - level) * factor)
                 rounded = w.astype(jnp.bfloat16)
                 if at < len(near):
-                    value = values[at // 2][(at % 2) * tile : (at % 2 + 1) * tile]
-                    mix = jnp.dot(rounded, value, preferred_element_type=jnp.float32)
+                    mix = jnp.dot(rounded, values[at][...], preferred_element_type=jnp.float32)
                     mixed = mix if mixed is None else mixed + mix
                 else:
                     begin = (at - len(near)) * tile
@@ -217,11 +217,11 @@
 
     @pl.when(inner)
     def _():
-        body([km, ko, n1km, n1ko, n2km, n2ko], [v, n1v, n2v], [(r1, near2)])
+        body(keys, values, [(r1, near2)])
 
     @pl.when(jnp.logical_not(inner))
     def _():
-        body([km, ko, n1km, n1ko], [v, n1v], [(r2, near2), (r3, mask[0, z ^ 3] == 1)])
+        body(keys[:4], values[:4], [(r2, near2), (r3, mask[0, z ^ 3] == 1)])
 
 
 def far_kernel(mixed, totals, far_weights, r1, r2, r3, *outs):
@@ -256,22 +256,23 @@
     return pl.BlockSpec((rows, lanes), lambda i: (first + i, 0))
 
 
-def attend_near(mask, q, keys, values, heads):
+def attend_near(mask, q, near, far, begin, end, heads):
     tile = q[0].shape[0]
-    blocks = [by_head(x, tile) for x in [*q, *keys]] + [by_head(x, 2 * tile) for x in values]
+    count = end - begin
+    blocks = [by_head(x, tile, begin) for x in [*q, *near, *far]] + [by_head(x, tile, heads + begin) for x in near]
     shapes = [(HEAD_DIM, jnp.float32), (HEAD_DIM, jnp.float32), (2 * tile, jnp.bfloat16)]
     return pl.pallas_call(
         attention_kernel,
-        grid=(heads,),
+        grid=(count,),
         in_specs=[pl.BlockSpec(memory_space=pltpu.SMEM)] + [spec for _, spec in blocks],
         out_specs=[by_rows(2 * tile, lanes) for lanes, _ in shapes],
-        out_shape=[jax.ShapeDtypeStruct((heads * 2 * tile, lanes), dtype) for lanes, dtype in shapes],
+        out_shape=[jax.ShapeDtypeStruct((count * 2 * tile, lanes), dtype) for lanes, dtype in shapes],
         scratch_shapes=[pltpu.VMEM((tile, 7 * tile), jnp.float32)] * 2,
         compiler_params=pltpu.CompilerParams(vmem_limit_bytes=16 * 1024 * 1024),
         cost_estimate=pl.CostEstimate(
-            flops=heads * 56 * tile * tile * HEAD_DIM,
-            bytes_accessed=heads * 20 * tile * tile,
-            transcendentals=heads * 14 * tile * tile,
+            flops=count * 56 * tile * tile * HEAD_DIM,
+            bytes_accessed=count * 20 * tile * tile,
+            transcendentals=count * 14 * tile * tile,
         ),
     )(mask, *[x for x, _ in blocks])
 
@@ -279,8 +280,8 @@
 def add_far(mixed, totals, far_weights, r1, r2, r3, begin, end):
     tile = r1.shape[0]
     rows, heads = 2 * tile, end - begin
-    blocks = [(x, by_rows(rows, x.shape[1], begin)) for x in (mixed, totals, far_weights)]
-    blocks += [by_head(r1, tile, begin), by_head(r2, tile, begin), by_head(r3, tile)]
+    blocks = [(x, by_rows(rows, x.shape[1])) for x in (mixed, totals, far_weights)]
+    blocks += [by_head(r1, tile, begin), by_head(r2, tile), by_head(r3, tile)]
     return pl.pallas_call(
         far_kernel,
         grid=(heads,),
@@ -334,30 +335,33 @@
     )(mask, offset, *operands)
 
 
-def relayed_kernel(told, *refs):
-    out = refs[-1]
-    tile = out.shape[0]
-    group = told[told.shape[0] - INFO_ROWS :, 4 * 128 : 5 * 128]
-    here = jnp.max(group.astype(jnp.float32)) == (lax.axis_index("head") // 2).astype(jnp.float32)
-    whole = refs[0].shape[0] == 2 * tile
+def relayed_kernel(mine, other, k_out, v_out):
+    tile, width = k_out.shape
+    offset = jnp.max(mine[tile : tile + INFO_ROWS, 4 * 128 : 5 * 128].astype(jnp.float32))
+    here = offset == (lax.axis_index("head") // 2).astype(jnp.float32)
+
+    def take(ref):
+        k_out[...] = ref[:tile, :width]
+        v_out[...] = ref[:tile, width:]
 
     @pl.when(here)
     def _():
-        out[...] = refs[0][:tile] if whole else told[:tile]
+        take(mine)
 
     @pl.when(jnp.logical_not(here))
     def _():
-        out[...] = refs[0][tile:] if whole else refs[0][...]
-
-
-def relayed(told, array, tile):
+        take(other)
+
+
+def relayed(mine, other):
+    tile, lanes = other.shape
     return pl.pallas_call(
         relayed_kernel,
         in_specs=[pl.BlockSpec(memory_space=pltpu.VMEM)] * 2,
-        out_specs=pl.BlockSpec(memory_space=pltpu.VMEM),
-        out_shape=jax.ShapeDtypeStruct((tile, array.shape[1]), array.dtype),
+        out_specs=[pl.BlockSpec(memory_space=pltpu.VMEM)] * 2,
+        out_shape=[jax.ShapeDtypeStruct((tile, lanes // 2), other.dtype)] * 2,
         compiler_params=pltpu.CompilerParams(vmem_limit_bytes=4 * 1024 * 1024),
-    )(told, array)
+    )(mine, other)
 
 
 def four_frames(queries, keys, values, pair_mask, tile_offset):
@@ -388,53 +392,52 @@
     def after(array, earlier):
         return lax.optimization_barrier((array, earlier))[0]
 
-    tile = 2 * rows
     kv = [[columns(array, d) for array in (keys, values)] for d in range(4)]
     kv = lax.optimization_barrier(kv)
     got = to_head(beside(*kv[1], *kv[3]), 1)
-    got = [got[:, n * width : (n + 1) * width] for n in range(4)]
-    ko = to_head(below(kv[2][0], got[2]), 2)
     pay, q_own, q_far, told = packed(
         (queries, keys, values),
-        after(pair_mask, got[0]),
+        pair_mask,
         tile_offset,
         [[(0, 1, 0, width), (0, 3, 0, width)], [(0, 0, 0, width)], [(0, 2, 0, width)]],
         width,
-        width,
+        2 * width,
     )
-
-    km = below(kv[0][0], got[0], told)
-    n1km = along(km, OUTER)
-    n2km = across(km)
-    vo = to_head(after(below(kv[2][1], got[3]), (n1km, n2km)), 2)
-    n1ko = along(ko, OUTER)
-    n2ko = across(ko)
-    v = below(kv[0][1], got[1], vo)
-    n1v = along(v, OUTER)
-    n2v = across(v)
-
-    got = to_head(pay, 1)
+    mine = below(beside(*kv[0]), got[:, : 2 * width], told)
+    other = to_head(below(beside(*kv[2]), got[:, 2 * width :]), 2)
+    n1m = along(mine, OUTER)
+    n2m = across(mine)
+    n1o = along(other, OUTER)
+    n2o = across(other)
+
+    got = to_head(after(pay, got), 1)
     q_mine = below(q_own, got[:, :width])
-    q_other = to_head(after(below(q_far, got[:, width:]), vo), 2)
-
-    r1k = across(after(relayed(n1km, n1ko, tile), (n2km, n2ko)))
-    r2k = along(relayed(n2km, n2ko, tile), OUTER)
-    r3k = along(after(r1k, r2k), OUTER)
-    r1v = across(relayed(n1km, n1v, tile))
-    r2v = along(relayed(n2km, n2v, tile), OUTER)
-    mixed, totals, far_weights = attend_near(
-        pair_mask, [q_mine, q_other], [km, ko, n1km, n1ko, n2km, n2ko, r1k, r2k, r3k], [v, n1v, n2v], heads
-    )
+    q_other = to_head(after(below(q_far, got[:, width:]), other), 2)
+
+    cut = (heads + 1) // 2
+    first, second = slice(0, cut * HEAD_DIM), slice(cut * HEAD_DIM, width)
+    r1k, r1v = after(relayed(n1m, n1o), n2m)
+    r1k = across(r1k)
+    r2k, r2v = relayed(n2m, n2o)
+    r1v = across(after(r1v, r2v))
+    r2k = along(r2k, OUTER)
+    r3k = along(after(r1k, (r2k, q_other)), OUTER)
+    first_r2v = along(after(r2v[:, first], r3k), OUTER)
+    first_r3v = along(after(r1v[:, first], r3k), OUTER)
+    far = [r1k, r2k, r3k]
+    near = [mine, other, n1m, n1o, n2m, n2o]
+    q = [q_mine, q_other]
+    first_parts = attend_near(pair_mask, q, near, far, 0, cut, heads)
+    both = along(after(below(r2v[:, second], r1v[:, second]), first_parts[1]), OUTER)
+    second_parts = attend_near(pair_mask, q, near, far, cut, heads, heads)
+    out = add_far(*first_parts, r1v, first_r2v, first_r3v, 0, cut)
+    pieces = [(to_head(out[d], d) if d else out[0], d, 0) for d in range(4)]
+    both = after(both, out[1])
+    out = add_far(*second_parts, r1v, both[: 2 * rows], both[2 * rows :], cut, heads)
+    pieces += [(to_head(out[d], d) if d else out[0], d, cut) for d in range(4)]
     result = jnp.zeros((rows, features), jnp.bfloat16)
-    cut = (heads + 1) // 2
-    for begin, end in ((0, cut), (cut, heads)):
-        r3v = r1v[:, begin * HEAD_DIM : end * HEAD_DIM]
-        r3v = along(r3v if begin == 0 else after(r3v, totals), OUTER)
-        r3v = r3v if begin == 0 else after(r3v, out[1])
-        out = add_far(mixed, totals, far_weights, r1v, r2v, r3v, begin, end)
-        out = [out[0]] + [to_head(out[d], d) for d in (1, 2, 3)]
-        for d in range(4):
-            result = lax.dynamic_update_slice_in_dim(result, out[d], (h ^ d) * width + begin * HEAD_DIM, axis=1)
+    for piece, d, begin in pieces:
+        result = lax.dynamic_update_slice_in_dim(result, piece, (h ^ d) * width + begin * HEAD_DIM, axis=1)
     return result
 
 

time: 86.4 us -> 94.5 us (1.094)
  local copies, waits for them, and re-layouts: 4.21 us -> 14.8 us
  starting transfers between devices: 30.1 us -> 24.9 us
  waiting for transfers between devices: 37.1 us -> 39.8 us
  other arithmetic: 1.9 us -> 0.95 us
    unnamed x26 -> x50, local copies, waits for them, and re-layouts: 1.13 us -> 9.95 us
    ppermute x11 -> x10, waiting for transfers between devices: 9.06 us -> 17 us  [to_head(): return lax.ppermute(array, 'head', [(i, i ^ d) for i in range(4)])]
    ppermute x8 -> x7, starting transfers between devices: 21.5 us -> 15 us  [along(): return lax.ppermute(array, 'frame', pairs)]
    ppermute x8 -> x7, waiting for transfers between devices: 28 us -> 22.8 us  [along(): return lax.ppermute(array, 'frame', pairs)]
    slice x4 -> x7, local copies, waits for them, and re-layouts: 0.78 us -> 2.56 us  [the longest x1 0.99 us: four_frames(): both[2 * rows:]]
    pallas_call x2, Pallas kernels: 2.03 us -> 3.31 us  [add_far(): pl.pallas_call(far_kernel, grid=(heads,), in_specs=[spec for _, spec in b...]
    ppermute x11 -> x10, starting transfers between devices: 8.15 us -> 9.37 us  [to_head(): return lax.ppermute(array, 'head', [(i, i ^ d) for i in range(4)])]
    pallas_call x4 -> x2, Pallas kernels: 1.33 us -> 0.35 us  [relayed(): pl.pallas_call(relayed_kernel, in_specs=[pl.BlockSpec(memory_space=pltpu....]
  transfers between devices with their start and end apart: 24 -> 21, of which waited for: 11 -> 9; matrix products, arithmetic and copies ran while one was open for 3% -> 4% of each run, Pallas kernels for 13% -> 13%
where the time goes in v10:
time: 94.5 us; the launch traced here: 94 us
  waiting for transfers between devices  39.8 us (42%)
  starting transfers between devices  24.9 us (26%)
  local copies, waits for them, and re-layouts  14.8 us (16%)
  Pallas kernels  12.4 us (13%)
  between operations  1.07 us (1%)
  other arithmetic  0.95 us (1%)
    ppermute x7, waiting for transfers between devices, along(): return lax.ppermute(array, 'frame', pairs)  22.8 us
    ppermute x10, waiting for transfers between devices, to_head(): return lax.ppermute(array, 'head', [(i, i ^ d) for i in range(4)])  17 us
    ppermute x7, starting transfers between devices, along(): return lax.ppermute(array, 'frame', pairs)  15 us
    unnamed x50, local copies, waits for them, and re-layouts  9.95 us
    ppermute x10, starting transfers between devices, to_head(): return lax.ppermute(array, 'head', [(i, i ^ d) for i in range(4)])  9.37 us
    pallas_call x2, Pallas kernels, attend_near(): pl.pallas_call(attention_kernel, grid=(count,), in_specs=[pl.BlockSpec(me...  8.1 us
    pallas_call x2, Pallas kernels, add_far(): pl.pallas_call(far_kernel, grid=(heads,), in_specs=[spec for _, spec in b...  3.31 us
  transfers between devices with their start and end apart: 21, of which 9 were waited for; matrix products, arithmetic and copies ran while one was open for 4% of the time, Pallas kernels for 13%

profile of v10, /device:TPU:0, one launch (start us, length us, event | category | flops | bytes accessed | tf_op | source)
XLA Modules:
  0.0 94.0 jit_solution(6944809577328649493)
XLA Ops:
  0.0 1.5 %constant_dynamic-slice_fusion = (bf16[128,640]{1,0:T(8,128)(2,1)S(1)}, bf16[128,640]{1,0:T(8,128)(2,1)S(1)}, bf16[128,640]{1,0:T(8,128)(2,1)S(1)}, bf16[128,640...) fusion(bf16[128,2560]{1,0:T(8,128)(2,1)} %refs_2_.1, ...), kind=kLoop, calls=%fused_computation.14 | loop fusion | bytes 2621456 | tf_op jit(solution)/shard_map/dynamic_slice | solution.py:374
  1.6 0.5 collective-permute-start
  2.1 1.7 %collective-permute-done = bf16[128,2560]{1,0:T(8,128)(2,1)S(1)} collective-permute-done((bf16[128,2560]{1,0:T(8,128)(2,1)S(1)}, bf16[128,2560]{1,0:T(8,128)(2,1)S(1)}, u32[]{:S(2)}, u32[]{:S(2)}) %collective-permute-start) | collective-permute-done | bytes 655392 | tf_op jit(solution)/shard_map/ppermute | solution.py:383
  4.0 2.9 %collective-permute-start.2 = (bf16[256,1280]{1,0:T(8,128)(2,1)S(1)}, bf16[256,1280]{1,0:T(8,128)(2,1)S(1)}, u32[]{:S(2)}, u32[]{:S(2)}) collective-permute-start(bf16[256,1280]{1,0:T(8,128)(2,1)S(1)} %pad_maximum_fusion.2), channel_id=1, source_target_pairs={{0,2},{1,3},{2,0},{3,1},{4,6},{5,7},{6,4},{7,5},{8,10},{9,11},{10,... | collective-permute-start | bytes 1966088 | tf_op jit(solution)/shard_map/ppermute | solution.py:383
  7.6 0.7 shard_map.55
  8.3 1.6 %collective-permute-start.4 = (bf16[272,1280]{1,0:T(8,128)(2,1)S(1)}, bf16[272,1280]{1,0:T(8,128)(2,1)S(1)}, u32[]{:S(2)}, u32[]{:S(2)}) collective-permute-start(bf16[272,1280]{1,0:T(8,128)(2,1)S(1)} %pad_maximum_fusion.rest_0_.rest_9_), channel_id=1, source_target_pairs={{0,4},{4,0},{8,12},{12,8},{1,5},{5,1},{9,13},{13,9},{2,6},{6,2},{1... | collective-permute-start | bytes 2088968 | tf_op jit(solution)/shard_map/ppermute | solution.py:386
  10.0 0.5 collective-permute-start.1
  10.5 11.4 %collective-permute-done.2.rest_1_.rest_10_ = bf16[256,1280]{1,0:T(8,128)(2,1)S(1)} collective-permute-done((bf16[256,1280]{1,0:T(8,128)(2,1)S(1)}, bf16[256,1280]{1,0:T(8,128)(2,1)S(1)}, u32[]{:S(2)}, u32[]{:S(2)}) %collective-permute-start.2) | collective-permute-done | bytes 655392 | tf_op jit(solution)/shard_map/ppermute | solution.py:383
  21.9 1.8 %collective-permute-start.5 = (bf16[256,1280]{1,0:T(8,128)(2,1)S(1)}, bf16[256,1280]{1,0:T(8,128)(2,1)S(1)}, u32[]{:S(2)}, u32[]{:S(2)}) collective-permute-start(bf16[256,1280]{1,0:T(8,128)(2,1)S(1)} %collective-permute-done.2.rest_1_.rest_10_), channel_id=1, source_target_pairs={{0,4},{4,0},{8,12},{12,8},{1,5},{5,1},{9,13},{13,9},{2,6},{6,2},{1... | collective-permute-start | bytes 1966088 | tf_op jit(solution)/shard_map/ppermute | solution.py:386
  23.8 1.6 %collective-permute-start.3 = (bf16[256,640]{1,0:T(8,128)(2,1)S(1)}, bf16[256,640]{1,0:T(8,128)(2,1)S(1)}, u32[]{:S(2)}, u32[]{:S(2)}) collective-permute-start(bf16[256,640]{1,0:T(8,128)(2,1)S(1)} %pad_maximum_fusion.4), channel_id=1, source_target_pairs={{0,2},{1,3},{2,0},{3,1},{4,6},{5,7},{6,4},{7,5},{8,10},{9,11},{10,... | collective-permute-start | bytes 983048 | tf_op jit(solution)/shard_map/ppermute | solution.py:383
  25.4 1.5 %collective-permute-done.4.mine.rest_2_.rest_11_ = bf16[272,1280]{1,0:T(8,128)(2,1)S(1)} collective-permute-done((bf16[272,1280]{1,0:T(8,128)(2,1)S(1)}, bf16[272,1280]{1,0:T(8,128)(2,1)S(1)}, u32[]{:S(2)}, u32[]{:S(2)}) %collective-permute-start.4) | collective-permute-done | bytes 696352 | tf_op jit(solution)/shard_map/ppermute | solution.py:386
  26.9 12.9 %collective-permute-done.5.other.rest_3_.rest_12_ = bf16[256,1280]{1,0:T(8,128)(2,1)S(1)} collective-permute-done((bf16[256,1280]{1,0:T(8,128)(2,1)S(1)}, bf16[256,1280]{1,0:T(8,128)(2,1)S(1)}, u32[]{:S(2)}, u32[]{:S(2)}) %collective-permute-start.5) | collective-permute-done | bytes 655392 | tf_op jit(solution)/shard_map/ppermute | solution.py:386
  40.0 0.2 shard_map.57
  40.2 2.6 %collective-permute-start.9 = (bf16[256,640]{1,0:T(8,128)(2,1)S(1)}, bf16[256,640]{1,0:T(8,128)(2,1)S(1)}, u32[]{:S(2)}, u32[]{:S(2)}) collective-permute-start(bf16[256,640]{1,0:T(8,128)(2,1)S(1)} %get-tuple-element.62), channel_id=1, source_target_pairs={{0,4},{4,0},{8,12},{12,8},{1,5},{5,1},{9,13},{13,9},{2,6},{6,2},{1... | collective-permute-start | bytes 983048 | tf_op jit(solution)/shard_map/ppermute | solution.py:386
  42.8 0.5 collective-permute-start.11
  43.3 6.3 %collective-permute-done.9.rest_7_ = bf16[256,640]{1,0:T(8,128)(2,1)S(1)} collective-permute-done((bf16[256,640]{1,0:T(8,128)(2,1)S(1)}, bf16[256,640]{1,0:T(8,128)(2,1)S(1)}, u32[]{:S(2)}, u32[]{:S(2)}) %collective-permute-start.9) | collective-permute-done | bytes 327712 | tf_op jit(solution)/shard_map/ppermute | solution.py:386
  49.6 4.0 %collective-permute-start.10 = (bf16[256,640]{1,0:T(8,128)(2,1)S(1)}, bf16[256,640]{1,0:T(8,128)(2,1)S(1)}, u32[]{:S(2)}, u32[]{:S(2)}) collective-permute-start(bf16[256,640]{1,0:T(8,128)(2,1)S(1)} %collective-permute-done.8.rest_6_), channel_id=1, source_target_pairs={{0,4},{4,0},{8,12},{12,8},{1,5},{5,1},{9,13},{13,9},{2,6},{6,2},{1... | collective-permute-start | bytes 983048 | tf_op jit(solution)/shard_map/ppermute | solution.py:386
  53.7 0.8 slice.34
  54.5 0.7 slice.44
  55.2 0.7 copy-done.4
  55.9 0.7 pad_maximum_fusion.5
  56.6 2.0 %collective-permute-done.10.rest_8_ = bf16[256,640]{1,0:T(8,128)(2,1)S(1)} collective-permute-done((bf16[256,640]{1,0:T(8,128)(2,1)S(1)}, bf16[256,640]{1,0:T(8,128)(2,1)S(1)}, u32[]{:S(2)}, u32[]{:S(2)}) %collective-permute-start.10) | collective-permute-done | bytes 327712 | tf_op jit(solution)/shard_map/ppermute | solution.py:386
  58.7 2.1 %collective-permute-start.13 = (bf16[256,384]{1,0:T(8,128)(2,1)}, bf16[256,384]{1,0:T(8,128)(2,1)}, u32[]{:S(2)}, u32[]{:S(2)}) collective-permute-start(bf16[256,384]{1,0:T(8,128)(2,1)} %slice.44), channel_id=1, source_target_pairs={{0,4},{4,0},{8,12},{12,8},{1,5},{5,1},{9,13},{13,9},{2,6},{6,2},{1... | collective-permute-start | bytes 589832 | tf_op jit(solution)/shard_map/ppermute | solution.py:386
  60.8 4.8 %shard_map.58 = (f32[1536,128]{1,0:T(8,128)S(1)}, f32[1536,128]{1,0:T(8,128)S(1)}, bf16[1536,512]{1,0:T(8,128)(2,1)S(1)}) custom-call(s32[1,4]{1,0:T(1,128)S(1)} %copy-done.23, bf16[256,640]{1,0:T(8,128)(2,1)S(1)} %pad_maximum_fusion.3.q_mine, bf16[256,640]{1,0:T(8,128)(2,1)S(1)} %collective-permute-done.3.q_other, ...), custom_call_target="tpu_custom_call" | custom-call | flops 1409286144 | bytes 3932160 | tf_op jit(solution)/shard_map/pallas_call | solution.py:264
  65.7 1.2 %copy-done.8 = bf16[1536,512]{1,0:T(8,128)(2,1)} copy-done((bf16[1536,512]{1,0:T(8,128)(2,1)}, bf16[1536,512]{1,0:T(8,128)(2,1)S(1)}, u32[]{:S(2)}) %copy-start.8) | copy-done | bytes 1572888
  66.9 0.9 copy-done.18
  67.7 0.9 copy-done.20
  68.6 2.8 %collective-permute-start.17 = (bf16[512,256]{1,0:T(8,128)(2,1)}, bf16[512,256]{1,0:T(8,128)(2,1)}, u32[]{:S(2)}, u32[]{:S(2)}) collective-permute-start(bf16[512,256]{1,0:T(8,128)(2,1)} %pad_maximum_fusion.5), channel_id=1, source_target_pairs={{0,4},{4,0},{8,12},{12,8},{1,5},{5,1},{9,13},{13,9},{2,6},{6,2},{1... | collective-permute-start | bytes 786440 | tf_op jit(solution)/shard_map/ppermute | solution.py:386
  71.5 1.1 %copy-done.1 = bf16[256,1280]{1,0:T(8,128)(2,1)S(1)} copy-done((bf16[256,1280]{1,0:T(8,128)(2,1)S(1)}, bf16[256,1280]{1,0:T(8,128)(2,1)}, u32[]{:S(2)}) %copy-start.1) | copy-done | bytes 655384
  72.5 1.0 %copy-done.3 = bf16[256,640]{1,0:T(8,128)(2,1)S(1)} copy-done((bf16[256,640]{1,0:T(8,128)(2,1)S(1)}, bf16[256,640]{1,0:T(8,128)(2,1)}, u32[]{:S(2)}) %copy-start.3) | copy-done | bytes 327704
  73.5 1.0 %copy-done.11 = bf16[256,640]{1,0:T(8,128)(2,1)S(1)} copy-done((bf16[256,640]{1,0:T(8,128)(2,1)S(1)}, bf16[256,640]{1,0:T(8,128)(2,1)}, u32[]{:S(2)}) %copy-start.11) | copy-done | bytes 327704
  74.5 1.0 %copy-done.13 = bf16[256,640]{1,0:T(8,128)(2,1)S(1)} copy-done((bf16[256,640]{1,0:T(8,128)(2,1)S(1)}, bf16[256,640]{1,0:T(8,128)(2,1)}, u32[]{:S(2)}) %copy-start.13) | copy-done | bytes 327704
  75.5 1.0 %copy-done.15 = bf16[256,640]{1,0:T(8,128)(2,1)S(1)} copy-done((bf16[256,640]{1,0:T(8,128)(2,1)S(1)}, bf16[256,640]{1,0:T(8,128)(2,1)}, u32[]{:S(2)}) %copy-start.15) | copy-done | bytes 327704
  76.4 1.0 %copy-done.17 = bf16[256,640]{1,0:T(8,128)(2,1)S(1)} copy-done((bf16[256,640]{1,0:T(8,128)(2,1)S(1)}, bf16[256,640]{1,0:T(8,128)(2,1)}, u32[]{:S(2)}) %copy-start.17) | copy-done | bytes 327704
  77.4 3.3 %shard_map.60 = (f32[1024,128]{1,0:T(8,128)S(1)}, f32[1024,128]{1,0:T(8,128)S(1)}, bf16[1024,512]{1,0:T(8,128)(2,1)S(1)}) custom-call(s32[1,4]{1,0:T(1,128)S(1)} %copy-done.23, bf16[256,640]{1,0:T(8,128)(2,1)S(1)} %copy-done.3, bf16[256,640]{1,0:T(8,128)(2,1)S(1)} %copy-done.11, bf16[272,1280]{1,0:T(8,128)(2,1)S(1)} %pad_maximum_fusion.rest_0_.rest_9_, ...), custom_call_target="tpu_custom_call" | custom-call | flops 939524096 | bytes 2621440 | tf_op jit(solution)/shard_map/pallas_call | solution.py:264
  80.8 2.5 %shard_map.59 = (bf16[128,384]{1,0:T(8,128)(2,1)S(1)}, bf16[128,384]{1,0:T(8,128)(2,1)S(1)}, bf16[128,384]{1,0:T(8,128)(2,1)S(1)}, bf16[128,384]{1,0:T(8,128)(2,1)S(1)}) custom-call(f32[1536,128]{1,0:T(8,128)S(1)} %copy-done.19, f32[1536,128]{1,0:T(8,128)S(1)} %copy-done.21, bf16[1536,512]{1,0:T(8,128)(2,1)S(1)} %copy-done.9, ...), custom_call_target="tpu_custom_call" | custom-call | flops 201326592 | bytes 4718592 | tf_op jit(solution)/shard_map/pallas_call | solution.py:285
  83.4 0.7 collective-permute-start.15
  84.1 1.1 %collective-permute-start.16 = (bf16[128,384]{1,0:T(8,128)(2,1)S(1)}, bf16[128,384]{1,0:T(8,128)(2,1)S(1)}, u32[]{:S(2)}, u32[]{:S(2)}) collective-permute-start(bf16[128,384]{1,0:T(8,128)(2,1)S(1)} %get-tuple-element.75), channel_id=1, source_target_pairs={{0,3},{1,2},{2,1},{3,0},{4,7},{5,6},{6,5},{7,4},{8,11},{9,10},{10,... | collective-permute-start | bytes 294920 | tf_op jit(solution)/shard_map/ppermute | solution.py:383
  85.3 1.0 %fusion.2 = (bf16[256,256]{1,0:T(8,128)(2,1)S(1)}, bf16[256,256]{1,0:T(8,128)(2,1)S(1)}) fusion(bf16[512,256]{1,0:T(8,128)(2,1)} %collective-permute-done.17), kind=kLoop, calls=%fused_computation.24 | loop fusion | bytes 524288 | tf_op jit(solution)/shard_map/slice | solution.py:436
  86.3 0.8 shard_map.61
  87.2 0.4 collective-permute-start.18
  87.6 0.7 collective-permute-start.19
  88.2 0.9 collective-permute-start.20
  89.2 1.1 %collective-permute-done.16 = bf16[128,384]{1,0:T(8,128)(2,1)S(1)} collective-permute-done((bf16[128,384]{1,0:T(8,128)(2,1)S(1)}, bf16[128,384]{1,0:T(8,128)(2,1)S(1)}, u32[]{:S(2)}, u32[]{:S(2)}) %collective-permute-start.16) | collective-permute-done | bytes 98336 | tf_op jit(solution)/shard_map/ppermute | solution.py:383
  90.3 2.2 %collective-permute-done.19 = bf16[128,256]{1,0:T(8,128)(2,1)S(1)} collective-permute-done((bf16[128,256]{1,0:T(8,128)(2,1)S(1)}, bf16[128,256]{1,0:T(8,128)(2,1)S(1)}, u32[]{:S(2)}, u32[]{:S(2)}) %collective-permute-start.19) | collective-permute-done | bytes 65568 | tf_op jit(solution)/shard_map/ppermute | solution.py:383
  92.5 0.5 collective-permute-done.20
  93.1 0.3 copy-done.24
  93.4 0.6 constant_dynamic-update-slice_fusion
  (74 shorter events, 0.9 us)
Async XLA Ops:
  1.6 6.0 %copy-start.6 = (bf16[128,2560]{1,0:T(8,128)(2,1)S(1)}, bf16[128,2560]{1,0:T(8,128)(2,1)}, u32[]{:S(2)}) copy-start(bf16[128,2560]{1,0:T(8,128)(2,1)} %refs_1_.1) | copy-start | bytes 1966084
  1.6 6.0 %copy-start.7 = (bf16[128,2560]{1,0:T(8,128)(2,1)S(1)}, bf16[128,2560]{1,0:T(8,128)(2,1)}, u32[]{:S(2)}) copy-start(bf16[128,2560]{1,0:T(8,128)(2,1)} %refs_2_.1) | copy-start | bytes 1966084
  1.6 6.0 %copy-start.22 = (bf16[128,2560]{1,0:T(8,128)(2,1)S(1)}, bf16[128,2560]{1,0:T(8,128)(2,1)}, u32[]{:S(2)}) copy-start(bf16[128,2560]{1,0:T(8,128)(2,1)} %refs_0_.1) | copy-start | bytes 1966084
  1.6 6.0 %copy-start.23 = (s32[1,4]{1,0:T(1,128)S(1)}, s32[1,4]{1,0:T(1,128)}, u32[]{:S(2)}) copy-start(s32[1,4]{1,0:T(1,128)} %mask.5) | copy-start | bytes 52
  1.6 2.2 %collective-permute-start = (bf16[128,2560]{1,0:T(8,128)(2,1)S(1)}, bf16[128,2560]{1,0:T(8,128)(2,1)S(1)}, u32[]{:S(2)}, u32[]{:S(2)}) collective-permute-start(bf16[128,2560]{1,0:T(8,128)(2,1)S(1)} %pad_maximum_fusion.1), channel_id=1, source_target_pairs={{0,1},{1,0},{2,3},{3,2},{4,5},{5,4},{6,7},{7,6},{8,9},{9,8},{10,11... | collective-permute-start | bytes 1966088 | tf_op jit(solution)/shard_map/ppermute | solution.py:383
  4.0 18.0 %collective-permute-start.2 = (bf16[256,1280]{1,0:T(8,128)(2,1)S(1)}, bf16[256,1280]{1,0:T(8,128)(2,1)S(1)}, u32[]{:S(2)}, u32[]{:S(2)}) collective-permute-start(bf16[256,1280]{1,0:T(8,128)(2,1)S(1)} %pad_maximum_fusion.2), channel_id=1, source_target_pairs={{0,2},{1,3},{2,0},{3,1},{4,6},{5,7},{6,4},{7,5},{8,10},{9,11},{10,... | collective-permute-start | bytes 1966088 | tf_op jit(solution)/shard_map/ppermute | solution.py:383
  8.3 18.6 %collective-permute-start.4 = (bf16[272,1280]{1,0:T(8,128)(2,1)S(1)}, bf16[272,1280]{1,0:T(8,128)(2,1)S(1)}, u32[]{:S(2)}, u32[]{:S(2)}) collective-permute-start(bf16[272,1280]{1,0:T(8,128)(2,1)S(1)} %pad_maximum_fusion.rest_0_.rest_9_), channel_id=1, source_target_pairs={{0,4},{4,0},{8,12},{12,8},{1,5},{5,1},{9,13},{13,9},{2,6},{6,2},{1... | collective-permute-start | bytes 2088968 | tf_op jit(solution)/shard_map/ppermute | solution.py:386
  10.0 30.0 %collective-permute-start.6 = (bf16[272,1280]{1,0:T(8,128)(2,1)S(1)}, bf16[272,1280]{1,0:T(8,128)(2,1)S(1)}, u32[]{:S(2)}, u32[]{:S(2)}) collective-permute-start(bf16[272,1280]{1,0:T(8,128)(2,1)S(1)} %pad_maximum_fusion.rest_0_.rest_9_), channel_id=1, source_target_pairs={{0,1},{1,0},{2,3},{3,2},{4,8},{5,9},{6,10},{7,11},{8,4},{9,5},{10,... | collective-permute-start | bytes 2088968 | tf_op jit(solution)/shard_map/ppermute | solution.py:390
  10.0 13.8 %collective-permute-start.1 = (bf16[128,1280]{1,0:T(8,128)(2,1)S(1)}, bf16[128,1280]{1,0:T(8,128)(2,1)S(1)}, u32[]{:S(2)}, u32[]{:S(2)}) collective-permute-start(bf16[128,1280]{1,0:T(8,128)(2,1)S(1)} %get-tuple-element.51), channel_id=1, source_target_pairs={{0,1},{1,0},{2,3},{3,2},{4,5},{5,4},{6,7},{7,6},{8,9},{9,8},{10,11... | collective-permute-start | bytes 983048 | tf_op jit(solution)/shard_map/ppermute | solution.py:383
  21.9 38.9 %copy-start = (bf16[256,1280]{1,0:T(8,128)(2,1)}, bf16[256,1280]{1,0:T(8,128)(2,1)S(1)}, u32[]{:S(2)}) copy-start(bf16[256,1280]{1,0:T(8,128)(2,1)S(1)} %collective-permute-done.2.rest_1_.rest_10_) | copy-start | bytes 1966084
  21.9 17.9 %collective-permute-start.5 = (bf16[256,1280]{1,0:T(8,128)(2,1)S(1)}, bf16[256,1280]{1,0:T(8,128)(2,1)S(1)}, u32[]{:S(2)}, u32[]{:S(2)}) collective-permute-start(bf16[256,1280]{1,0:T(8,128)(2,1)S(1)} %collective-permute-done.2.rest_1_.rest_10_), channel_id=1, source_target_pairs={{0,4},{4,0},{8,12},{12,8},{1,5},{5,1},{9,13},{13,9},{2,6},{6,2},{1... | collective-permute-start | bytes 1966088 | tf_op jit(solution)/shard_map/ppermute | solution.py:386
  23.8 16.3 %collective-permute-start.7 = (bf16[256,1280]{1,0:T(8,128)(2,1)S(1)}, bf16[256,1280]{1,0:T(8,128)(2,1)S(1)}, u32[]{:S(2)}, u32[]{:S(2)}) collective-permute-start(bf16[256,1280]{1,0:T(8,128)(2,1)S(1)} %collective-permute-done.2.rest_1_.rest_10_), channel_id=1, source_target_pairs={{0,1},{1,0},{2,3},{3,2},{4,8},{5,9},{6,10},{7,11},{8,4},{9,5},{10,... | collective-permute-start | bytes 1966088 | tf_op jit(solution)/shard_map/ppermute | solution.py:390
  23.8 19.4 %collective-permute-start.3 = (bf16[256,640]{1,0:T(8,128)(2,1)S(1)}, bf16[256,640]{1,0:T(8,128)(2,1)S(1)}, u32[]{:S(2)}, u32[]{:S(2)}) collective-permute-start(bf16[256,640]{1,0:T(8,128)(2,1)S(1)} %pad_maximum_fusion.4), channel_id=1, source_target_pairs={{0,2},{1,3},{2,0},{3,1},{4,6},{5,7},{6,4},{7,5},{8,10},{9,11},{10,... | collective-permute-start | bytes 983048 | tf_op jit(solution)/shard_map/ppermute | solution.py:383
  40.2 9.4 %collective-permute-start.9 = (bf16[256,640]{1,0:T(8,128)(2,1)S(1)}, bf16[256,640]{1,0:T(8,128)(2,1)S(1)}, u32[]{:S(2)}, u32[]{:S(2)}) collective-permute-start(bf16[256,640]{1,0:T(8,128)(2,1)S(1)} %get-tuple-element.62), channel_id=1, source_target_pairs={{0,4},{4,0},{8,12},{12,8},{1,5},{5,1},{9,13},{13,9},{2,6},{6,2},{1... | collective-permute-start | bytes 983048 | tf_op jit(solution)/shard_map/ppermute | solution.py:386
  42.8 6.9 %collective-permute-start.8 = (bf16[256,640]{1,0:T(8,128)(2,1)S(1)}, bf16[256,640]{1,0:T(8,128)(2,1)S(1)}, u32[]{:S(2)}, u32[]{:S(2)}) collective-permute-start(bf16[256,640]{1,0:T(8,128)(2,1)S(1)} %get-tuple-element.61), channel_id=1, source_target_pairs={{0,1},{1,0},{2,3},{3,2},{4,8},{5,9},{6,10},{7,11},{8,4},{9,5},{10,... | collective-permute-start | bytes 983048 | tf_op jit(solution)/shard_map/ppermute | solution.py:390
  42.8 11.7 %collective-permute-start.11 = (bf16[256,640]{1,0:T(8,128)(2,1)S(1)}, bf16[256,640]{1,0:T(8,128)(2,1)S(1)}, u32[]{:S(2)}, u32[]{:S(2)}) collective-permute-start(bf16[256,640]{1,0:T(8,128)(2,1)S(1)} %get-tuple-element.69), channel_id=1, source_target_pairs={{0,1},{1,0},{2,3},{3,2},{4,8},{5,9},{6,10},{7,11},{8,4},{9,5},{10,... | collective-permute-start | bytes 983048 | tf_op jit(solution)/shard_map/ppermute | solution.py:390
  43.3 22.3 %copy-start.10 = (bf16[256,640]{1,0:T(8,128)(2,1)}, bf16[256,640]{1,0:T(8,128)(2,1)S(1)}, u32[]{:S(2)}) copy-start(bf16[256,640]{1,0:T(8,128)(2,1)S(1)} %collective-permute-done.3.q_other) | copy-start | bytes 983044
  49.6 16.0 %copy-start.12 = (bf16[256,640]{1,0:T(8,128)(2,1)}, bf16[256,640]{1,0:T(8,128)(2,1)S(1)}, u32[]{:S(2)}) copy-start(bf16[256,640]{1,0:T(8,128)(2,1)S(1)} %collective-permute-done.9.rest_7_) | copy-start | bytes 983044
  49.6 16.0 %copy-start.14 = (bf16[256,640]{1,0:T(8,128)(2,1)}, bf16[256,640]{1,0:T(8,128)(2,1)S(1)}, u32[]{:S(2)}) copy-start(bf16[256,640]{1,0:T(8,128)(2,1)S(1)} %collective-permute-done.8.rest_6_) | copy-start | bytes 983044
  49.6 9.0 %collective-permute-start.10 = (bf16[256,640]{1,0:T(8,128)(2,1)S(1)}, bf16[256,640]{1,0:T(8,128)(2,1)S(1)}, u32[]{:S(2)}, u32[]{:S(2)}) collective-permute-start(bf16[256,640]{1,0:T(8,128)(2,1)S(1)} %collective-permute-done.8.rest_6_), channel_id=1, source_target_pairs={{0,4},{4,0},{8,12},{12,8},{1,5},{5,1},{9,13},{13,9},{2,6},{6,2},{1... | collective-permute-start | bytes 983048 | tf_op jit(solution)/shard_map/ppermute | solution.py:386
  53.7 12.0 %copy-start.2 = (bf16[256,640]{1,0:T(8,128)(2,1)}, bf16[256,640]{1,0:T(8,128)(2,1)S(1)}, u32[]{:S(2)}) copy-start(bf16[256,640]{1,0:T(8,128)(2,1)S(1)} %pad_maximum_fusion.3.q_mine) | copy-start | bytes 983044
  55.2 0.7 copy-start.4
  58.7 7.0 %copy-start.16 = (bf16[256,640]{1,0:T(8,128)(2,1)}, bf16[256,640]{1,0:T(8,128)(2,1)S(1)}, u32[]{:S(2)}) copy-start(bf16[256,640]{1,0:T(8,128)(2,1)S(1)} %collective-permute-done.10.rest_8_) | copy-start | bytes 983044
  58.7 22.1 %collective-permute-start.13 = (bf16[256,384]{1,0:T(8,128)(2,1)}, bf16[256,384]{1,0:T(8,128)(2,1)}, u32[]{:S(2)}, u32[]{:S(2)}) collective-permute-start(bf16[256,384]{1,0:T(8,128)(2,1)} %slice.44), channel_id=1, source_target_pairs={{0,4},{4,0},{8,12},{12,8},{1,5},{5,1},{9,13},{13,9},{2,6},{6,2},{1... | collective-permute-start | bytes 589832 | tf_op jit(solution)/shard_map/ppermute | solution.py:386
  60.8 20.0 %collective-permute-start.12 = (bf16[256,384]{1,0:T(8,128)(2,1)}, bf16[256,384]{1,0:T(8,128)(2,1)}, u32[]{:S(2)}, u32[]{:S(2)}) collective-permute-start(bf16[256,384]{1,0:T(8,128)(2,1)} %slice.34), channel_id=1, source_target_pairs={{0,4},{4,0},{8,12},{12,8},{1,5},{5,1},{9,13},{13,9},{2,6},{6,2},{1... | collective-permute-start | bytes 589832 | tf_op jit(solution)/shard_map/ppermute | solution.py:386
  65.7 1.2 %copy-start.8 = (bf16[1536,512]{1,0:T(8,128)(2,1)}, bf16[1536,512]{1,0:T(8,128)(2,1)S(1)}, u32[]{:S(2)}) copy-start(bf16[1536,512]{1,0:T(8,128)(2,1)S(1)} %get-tuple-element.66.far_weights) | copy-start | bytes 4718596
  66.9 0.9 copy-start.18
  67.7 0.9 copy-start.20
  68.6 16.7 %collective-permute-start.17 = (bf16[512,256]{1,0:T(8,128)(2,1)}, bf16[512,256]{1,0:T(8,128)(2,1)}, u32[]{:S(2)}, u32[]{:S(2)}) collective-permute-start(bf16[512,256]{1,0:T(8,128)(2,1)} %pad_maximum_fusion.5), channel_id=1, source_target_pairs={{0,4},{4,0},{8,12},{12,8},{1,5},{5,1},{9,13},{13,9},{2,6},{6,2},{1... | collective-permute-start | bytes 786440 | tf_op jit(solution)/shard_map/ppermute | solution.py:386
  71.5 1.1 %copy-start.1 = (bf16[256,1280]{1,0:T(8,128)(2,1)S(1)}, bf16[256,1280]{1,0:T(8,128)(2,1)}, u32[]{:S(2)}) copy-start(bf16[256,1280]{1,0:T(8,128)(2,1)} %copy-done) | copy-start | bytes 1966084
  72.5 1.0 %copy-start.3 = (bf16[256,640]{1,0:T(8,128)(2,1)S(1)}, bf16[256,640]{1,0:T(8,128)(2,1)}, u32[]{:S(2)}) copy-start(bf16[256,640]{1,0:T(8,128)(2,1)} %copy-done.2) | copy-start | bytes 983044
  73.5 1.0 %copy-start.11 = (bf16[256,640]{1,0:T(8,128)(2,1)S(1)}, bf16[256,640]{1,0:T(8,128)(2,1)}, u32[]{:S(2)}) copy-start(bf16[256,640]{1,0:T(8,128)(2,1)} %copy-done.10) | copy-start | bytes 983044
  74.5 1.0 %copy-start.13 = (bf16[256,640]{1,0:T(8,128)(2,1)S(1)}, bf16[256,640]{1,0:T(8,128)(2,1)}, u32[]{:S(2)}) copy-start(bf16[256,640]{1,0:T(8,128)(2,1)} %copy-done.12) | copy-start | bytes 983044
  75.5 1.0 %copy-start.15 = (bf16[256,640]{1,0:T(8,128)(2,1)S(1)}, bf16[256,640]{1,0:T(8,128)(2,1)}, u32[]{:S(2)}) copy-start(bf16[256,640]{1,0:T(8,128)(2,1)} %copy-done.14) | copy-start | bytes 983044
  76.4 1.0 %copy-start.17 = (bf16[256,640]{1,0:T(8,128)(2,1)S(1)}, bf16[256,640]{1,0:T(8,128)(2,1)}, u32[]{:S(2)}) copy-start(bf16[256,640]{1,0:T(8,128)(2,1)} %copy-done.16) | copy-start | bytes 983044
  77.4 3.4 %copy-start.5 = (bf16[256,640]{1,0:T(8,128)(2,1)S(1)}, bf16[256,640]{1,0:T(8,128)(2,1)}, u32[]{:S(2)}) copy-start(bf16[256,640]{1,0:T(8,128)(2,1)} %copy-done.4) | copy-start | bytes 983044
  77.4 3.4 %copy-start.9 = (bf16[1536,512]{1,0:T(8,128)(2,1)S(1)}, bf16[1536,512]{1,0:T(8,128)(2,1)}, u32[]{:S(2)}) copy-start(bf16[1536,512]{1,0:T(8,128)(2,1)} %copy-done.8) | copy-start | bytes 4718596
  77.4 3.4 %copy-start.19 = (f32[1536,128]{1,0:T(8,128)S(1)}, f32[1536,128]{1,0:T(8,128)}, u32[]{:S(2)}) copy-start(f32[1536,128]{1,0:T(8,128)} %copy-done.18) | copy-start | bytes 2359300
  77.4 3.4 %copy-start.21 = (f32[1536,128]{1,0:T(8,128)S(1)}, f32[1536,128]{1,0:T(8,128)}, u32[]{:S(2)}) copy-start(f32[1536,128]{1,0:T(8,128)} %copy-done.20) | copy-start | bytes 2359300
  83.3 4.9 %collective-permute-start.14 = (bf16[128,384]{1,0:T(8,128)(2,1)S(1)}, bf16[128,384]{1,0:T(8,128)(2,1)S(1)}, u32[]{:S(2)}, u32[]{:S(2)}) collective-permute-start(bf16[128,384]{1,0:T(8,128)(2,1)S(1)} %get-tuple-element.73), channel_id=1, source_target_pairs={{0,1},{1,0},{2,3},{3,2},{4,5},{5,4},{6,7},{7,6},{8,9},{9,8},{10,11... | collective-permute-start | bytes 294920 | tf_op jit(solution)/shard_map/ppermute | solution.py:383
  83.4 5.7 %collective-permute-start.15 = (bf16[128,384]{1,0:T(8,128)(2,1)S(1)}, bf16[128,384]{1,0:T(8,128)(2,1)S(1)}, u32[]{:S(2)}, u32[]{:S(2)}) collective-permute-start(bf16[128,384]{1,0:T(8,128)(2,1)S(1)} %get-tuple-element.74), channel_id=1, source_target_pairs={{0,2},{1,3},{2,0},{3,1},{4,6},{5,7},{6,4},{7,5},{8,10},{9,11},{10,... | collective-permute-start | bytes 294920 | tf_op jit(solution)/shard_map/ppermute | solution.py:383
  84.1 6.1 %collective-permute-start.16 = (bf16[128,384]{1,0:T(8,128)(2,1)S(1)}, bf16[128,384]{1,0:T(8,128)(2,1)S(1)}, u32[]{:S(2)}, u32[]{:S(2)}) collective-permute-start(bf16[128,384]{1,0:T(8,128)(2,1)S(1)} %get-tuple-element.75), channel_id=1, source_target_pairs={{0,3},{1,2},{2,1},{3,0},{4,7},{5,6},{6,5},{7,4},{8,11},{9,10},{10,... | collective-permute-start | bytes 294920 | tf_op jit(solution)/shard_map/ppermute | solution.py:383
  87.2 3.1 %collective-permute-start.18 = (bf16[128,256]{1,0:T(8,128)(2,1)S(1)}, bf16[128,256]{1,0:T(8,128)(2,1)S(1)}, u32[]{:S(2)}, u32[]{:S(2)}) collective-permute-start(bf16[128,256]{1,0:T(8,128)(2,1)S(1)} %get-tuple-element.82), channel_id=1, source_target_pairs={{0,1},{1,0},{2,3},{3,2},{4,5},{5,4},{6,7},{7,6},{8,9},{9,8},{10,11... | collective-permute-start | bytes 196616 | tf_op jit(solution)/shard_map/ppermute | solution.py:383
  87.6 4.9 %collective-permute-start.19 = (bf16[128,256]{1,0:T(8,128)(2,1)S(1)}, bf16[128,256]{1,0:T(8,128)(2,1)S(1)}, u32[]{:S(2)}, u32[]{:S(2)}) collective-permute-start(bf16[128,256]{1,0:T(8,128)(2,1)S(1)} %get-tuple-element.83), channel_id=1, source_target_pairs={{0,2},{1,3},{2,0},{3,1},{4,6},{5,7},{6,4},{7,5},{8,10},{9,11},{10,... | collective-permute-start | bytes 196616 | tf_op jit(solution)/shard_map/ppermute | solution.py:383
  88.2 4.8 %collective-permute-start.20 = (bf16[128,256]{1,0:T(8,128)(2,1)S(1)}, bf16[128,256]{1,0:T(8,128)(2,1)S(1)}, u32[]{:S(2)}, u32[]{:S(2)}) collective-permute-start(bf16[128,256]{1,0:T(8,128)(2,1)S(1)} %get-tuple-element.84), channel_id=1, source_target_pairs={{0,3},{1,2},{2,1},{3,0},{4,7},{5,6},{6,5},{7,4},{8,11},{9,10},{10,... | collective-permute-start | bytes 196616 | tf_op jit(solution)/shard_map/ppermute | solution.py:383
  92.5 0.8 copy-start.24

commit v11 on v5

--- a/solution.py
+++ b/solution.py
@@ -155,47 +155,10 @@
     return lax.all_to_all(result, "head", split_axis=0, concat_axis=1, tiled=True)
 
 
+HOME = 3
 INFO_ROWS = 16
 OUTER = [(0, 1), (1, 0), (2, 3), (3, 2)]
-INNER = [(1, 2), (2, 1)]
-OUTWARD = [(1, 0), (2, 3)]
-
-
-def fold(x):
-    parts = [x[:, at : at + 128] for at in range(0, x.shape[1], 128)]
-    best = parts[0]
-    for part in parts[1:]:
-        best = jnp.maximum(best, part)
-    return best
-
-
-def scores_of(q, slots, held):
-    free, top = None, None
-    for at, (k, valid) in enumerate(slots):
-        s = lax.dot_general(q, k[...], (((1,), (1,)), ((), ())), preferred_element_type=jnp.float32)
-        held[:, at * s.shape[1] : (at + 1) * s.shape[1]] = s
-        best = fold(s)
-        if valid is None:
-            free = best if free is None else jnp.maximum(free, best)
-        else:
-            best = jnp.where(valid, jnp.max(best, axis=1, keepdims=True), -1e30)
-            top = best if top is None else jnp.maximum(top, best)
-    free = jnp.max(free, axis=1, keepdims=True)
-    return free if top is None else jnp.maximum(free, top)
-
-
-def weights_of(top, slots, held, out):
-    factor = SCALE * LOG2E
-    total = None
-    for at, (k, valid) in enumerate(slots):
-        tile = k.shape[0]
-        level = top if valid is None else jnp.where(valid, top, 1e30)
-        w = jnp.exp2((held[:, at * tile : (at + 1) * tile] - level) * factor)
-        out[:, at * tile : (at + 1) * tile] = w.astype(jnp.bfloat16)
-        for begin in range(0, tile, 128):
-            part = w[:, begin : begin + 128]
-            total = part if total is None else total + part
-    return jnp.sum(total, axis=1, keepdims=True)
+FACTOR = SCALE * LOG2E
 
 
 def inner_frame():
@@ -203,93 +166,197 @@
     return (z == 1) | (z == 2)
 
 
-def weights_kernel(mask, q_mine, q_other, mine, other, n1m, n1o, n2m, n2o, r1, r2, r3, weights, totals, held0, held1):
+def head_lanes(first, i):
+    return pl.ds(pl.multiple_of((first + i) * HEAD_DIM, HEAD_DIM), HEAD_DIM)
+
+
+def keys_of(ref, first, i, rows):
+    return ref[:rows, head_lanes(first, i)]
+
+
+def values_of(ref, first, i, rows):
+    return ref[:rows, head_lanes(ref.shape[1] // (2 * HEAD_DIM) + first, i)]
+
+
+def dot_keys(q, k):
+    return lax.dot_general(q, k, (((1,), (1,)), ((), ())), preferred_element_type=jnp.float32)
+
+
+def fold(x, op):
+    result = x[:, :128]
+    for at in range(128, x.shape[1], 128):
+        result = op(result, x[:, at : at + 128])
+    return result
+
+
+def near_kernel(first, skip, counts, q_mine, q_other, *refs):
+    tiles, (mixed_out, tops, totals, done), rooms = refs[:-6], refs[-6:-2], refs[-2:]
+    done[...] = jnp.zeros_like(done)
+    rows = q_mine.shape[0]
+
+    def one_head(used, i):
+        found = []
+        for q, held in zip((q_mine, q_other), rooms):
+            best = None
+            for at, ref in enumerate(used):
+                s = dot_keys(q[:, head_lanes(skip, i)], keys_of(ref, first, i, rows))
+                held[:, at * rows : (at + 1) * rows] = s
+                part = fold(s, jnp.maximum)
+                best = part if best is None else jnp.maximum(best, part)
+            found.append(jnp.max(best, axis=1, keepdims=True))
+        for half, (top, held) in enumerate(zip(found, rooms)):
+            total, mixed = None, None
+            for at, ref in enumerate(used):
+                w = jnp.exp2((held[:, at * rows : (at + 1) * rows] - top) * FACTOR)
+                mix = jnp.dot(w.astype(jnp.bfloat16), values_of(ref, first, i, rows), preferred_element_type=jnp.float32)
+                part = fold(w, jnp.add)
+                mixed = mix if mixed is None else mixed + mix
+                total = part if total is None else total + part
+            span = pl.ds(pl.multiple_of((2 * i + half) * rows, rows), rows)
+            mixed_out[span] = mixed
+            tops[span] = jnp.broadcast_to(top, (rows, HEAD_DIM))
+            totals[span] = jnp.broadcast_to(jnp.sum(total, axis=1, keepdims=True), (rows, HEAD_DIM))
+
+    for wanted, (n_tiles, n_heads) in zip((True, False), counts):
+        if n_heads:
+
+            @pl.when(inner_frame() == wanted)
+            def _():
+                def step(i, carry):
+                    one_head(tiles[:n_tiles], i)
+                    return carry
+
+                lax.fori_loop(0, n_heads, step, 0)
+
+
+def add_far(q, state, slots, i, row, held):
+    rows = q.shape[0]
+    span = pl.ds(pl.multiple_of(row, rows), rows)
+    near_top = state[1][span][:, :1]
+    top = near_top
+    for at, (ref, first, valid) in enumerate(slots):
+        s = dot_keys(q, keys_of(ref, first, i, rows))
+        held[:, at * rows : (at + 1) * rows] = s
+        best = jnp.max(fold(s, jnp.maximum), axis=1, keepdims=True)
+        top = jnp.maximum(top, best if valid is None else jnp.where(valid, best, -1e30))
+    shrink = jnp.exp2((near_top - top) * FACTOR)
+    mixed = state[0][span] * shrink
+    total = None
+    for at, (ref, first, valid) in enumerate(slots):
+        level = top if valid is None else jnp.where(valid, top, 1e30)
+        w = jnp.exp2((held[:, at * rows : (at + 1) * rows] - level) * FACTOR)
+        mixed += jnp.dot(w.astype(jnp.bfloat16), values_of(ref, first, i, rows), preferred_element_type=jnp.float32)
+        part = fold(w, jnp.add)
+        total = part if total is None else total + part
+    total = jnp.sum(total, axis=1, keepdims=True) + state[2][span][:, :1] * shrink
+    return (mixed * (1.0 / total)).astype(jnp.bfloat16)
+
+
+def write_pieces(outs, half, lanes, value):
+    rows = outs[0].shape[0]
+    outs[2 * half][:, lanes] = value[:rows]
+    outs[2 * half + 1][:, lanes] = value[rows:]
+
+
+def home_kernel(mask, q_mine, q_other, mixed, tops, totals, r1, r2, r3, *rest):
+    outs, rooms = rest[:4], rest[4:]
     z = lax.axis_index("frame")
-    tile = r1.shape[0]
-    near = mask[0, z ^ 2] == 1
-    always = [(mine, None), (other, None), (n1m, None), (n1o, None)]
+    near2 = mask[0, z ^ 2] == 1
+    rows = q_mine.shape[0]
 
     def body(slots):
-        rooms = (held0, held1)
-        tops = [scores_of(q[...], slots, held) for q, held in zip((q_mine, q_other), rooms)]
-        for half, (top, held) in enumerate(zip(tops, rooms)):
-            rows = slice(half * tile, (half + 1) * tile)
-            total = weights_of(top, slots, held, weights.at[rows])
-            totals[rows] = jnp.broadcast_to(total, (tile, totals.shape[1]))
+        def step(i, carry):
+            for half, (q, held) in enumerate(zip((q_mine, q_other), rooms)):
+                value = add_far(q[:, head_lanes(0, i)], (mixed, tops, totals), slots, i, (2 * i + half) * rows, held)
+                write_pieces(outs, half, head_lanes(0, i), value)
+            return carry
+
+        lax.fori_loop(0, outs[0].shape[1] // HEAD_DIM, step, 0)
 
     @pl.when(inner_frame())
     def _():
-        body(always + [(n2m, None), (n2o, None), (r1, near)])
+        body([(r1, 0, near2)])
 
     @pl.when(jnp.logical_not(inner_frame()))
     def _():
-        body(always + [(r2, near), (r3, mask[0, z ^ 3] == 1)])
-
-
-def values_kernel(weights, totals, mine, other, n1m, n1o, n2m, n2o, r1, r2, r3, *outs):
-    tile = r1.shape[0]
-    rows = outs[0].shape[0]
-    always = [mine, other, n1m, n1o]
-
-    def body(slots):
+        body([(r2, 0, near2), (r3, 0, mask[0, z ^ 3] == 1)])
+
+
+def guest_kernel(first, q, mixed, tops, totals, n1m, n2m, n2o, r1, out, *rooms):
+    rows = r1.shape[0]
+    z = lax.axis_index("frame")
+
+    def told(ref, group):
+        return ref[rows : rows + 1, group * 128 : (group + 1) * 128][:, :1].astype(jnp.float32)
+
+    @pl.when(inner_frame())
+    def _():
+        near2 = jnp.where(z == 1, told(n1m, 2), told(n1m, 1)) > 0.5
+        near1 = jnp.where(z == 1, told(n1m, 3), told(n1m, 0)) > 0.5
+        picked = told(n2m, 4) == (lax.axis_index("head") // 2).astype(jnp.float32)
+        slots = [(n2m, first, near2 & picked), (n2o, first, near2 & jnp.logical_not(picked)), (r1, 0, near1)]
+
+        def step(i, carry):
+            for half, held in enumerate(rooms):
+                span = slice(half * rows, (half + 1) * rows)
+                value = add_far(q[span, head_lanes(0, i)], (mixed, tops, totals), slots, i, (2 * i + half) * rows, held)
+                out[span, head_lanes(0, i)] = value
+            return carry
+
+        lax.fori_loop(0, out.shape[1] // HEAD_DIM, step, 0)
+
+
+def rest_kernel(first, mask, q_mine, q_other, mixed, tops, totals, r1, back, *rest):
+    outs, rooms = rest[:4], rest[4:]
+    z = lax.axis_index("frame")
+    rows = q_mine.shape[0]
+
+    @pl.when(inner_frame())
+    def _():
+        def step(i, carry):
+            for half, (q, held) in enumerate(zip((q_mine, q_other), rooms)):
+                slots = [(r1, 0, mask[0, z ^ 2] == 1)]
+                row = (2 * i + half) * rows
+                value = add_far(q[:, head_lanes(first, i)], (mixed, tops, totals), slots, i, row, held)
+                write_pieces(outs, half, head_lanes(0, i), value)
+            return carry
+
+        lax.fori_loop(0, outs[0].shape[1] // HEAD_DIM, step, 0)
+
+    @pl.when(jnp.logical_not(inner_frame()))
+    def _():
         for d, out in enumerate(outs):
-            span = slice(d * rows, (d + 1) * rows)
-            mixed = None
-            for at, v in enumerate(slots):
-                w = weights[span, at * tile : (at + 1) * tile]
-                mix = jnp.dot(w, v[...], preferred_element_type=jnp.float32)
-                mixed = mix if mixed is None else mixed + mix
-            out[...] = (mixed / totals[span]).astype(jnp.bfloat16)
-
-    @pl.when(inner_frame())
-    def _():
-        body(always + [n2m, n2o, r1])
-
-    @pl.when(jnp.logical_not(inner_frame()))
-    def _():
-        body(always + [r2, r3])
-
-
-def by_head(x, rows, first=0):
-    return x, pl.BlockSpec((rows, HEAD_DIM), lambda i: (0, first + i))
-
-
-def find_weights(mask, q_mine, q_other, keys, heads):
-    tile = q_mine.shape[0]
-    blocks = [by_head(q_mine, tile), by_head(q_other, tile)] + [by_head(k, tile) for k in keys]
-    shapes = [(2 * tile, 7 * tile, jnp.bfloat16), (2 * tile, HEAD_DIM, jnp.float32)]
+            out[...] = back[d * out.shape[0] : (d + 1) * out.shape[0]]
+
+
+def pass_kernel(done, x, out):
+    out[...] = x[...]
+
+
+def passed(x, done):
     return pl.pallas_call(
-        weights_kernel,
-        grid=(heads,),
-        in_specs=[pl.BlockSpec(memory_space=pltpu.SMEM)] + [spec for _, spec in blocks],
-        out_specs=[pl.BlockSpec((rows, lanes), lambda i: (i, 0)) for rows, lanes, _ in shapes],
-        out_shape=[jax.ShapeDtypeStruct((heads * rows, lanes), dtype) for rows, lanes, dtype in shapes],
-        scratch_shapes=[pltpu.VMEM((tile, 7 * tile), jnp.float32)] * 2,
-        compiler_params=pltpu.CompilerParams(vmem_limit_bytes=16 * 1024 * 1024),
+        pass_kernel,
+        in_specs=[pl.BlockSpec(memory_space=pltpu.VMEM)] * 2,
+        out_specs=pl.BlockSpec(memory_space=pltpu.VMEM),
+        out_shape=jax.ShapeDtypeStruct(x.shape, x.dtype),
+        compiler_params=pltpu.CompilerParams(vmem_limit_bytes=4 * 1024 * 1024),
+    )(done, x)
+
+
+def run_kernel(kernel, mask, arrays, outs, rooms, flops):
+    scalars = [] if mask is None else [mask]
+    return pl.pallas_call(
+        kernel,
+        in_specs=[pl.BlockSpec(memory_space=pltpu.SMEM)] * len(scalars)
+        + [pl.BlockSpec(memory_space=pltpu.VMEM)] * len(arrays),
+        out_specs=[pl.BlockSpec(memory_space=pltpu.VMEM)] * len(outs),
+        out_shape=[jax.ShapeDtypeStruct(shape, dtype) for shape, dtype in outs],
+        scratch_shapes=[pltpu.VMEM(rooms, jnp.float32)] * 2,
+        compiler_params=pltpu.CompilerParams(vmem_limit_bytes=12 * 1024 * 1024),
         cost_estimate=pl.CostEstimate(
-            flops=heads * 28 * tile * tile * HEAD_DIM,
-            bytes_accessed=heads * 28 * tile * tile,
-            transcendentals=heads * 14 * tile * tile,
+            flops=flops, bytes_accessed=sum(x.size * 2 for x in arrays), transcendentals=flops // (4 * HEAD_DIM)
         ),
-    )(mask, *[x for x, _ in blocks])
-
-
-def mix_values(weights, totals, values, heads):
-    rows, lanes = weights.shape[0] // heads, weights.shape[1]
-    tile = lanes // 7
-    blocks = [by_head(v, tile, first) for v, first in values]
-    return pl.pallas_call(
-        values_kernel,
-        grid=(heads,),
-        in_specs=[pl.BlockSpec((rows, lanes), lambda i: (i, 0)), pl.BlockSpec((rows, HEAD_DIM), lambda i: (i, 0))]
-        + [spec for _, spec in blocks],
-        out_specs=[pl.BlockSpec((rows // 4, HEAD_DIM), lambda i: (0, i))] * 4,
-        out_shape=[jax.ShapeDtypeStruct((rows // 4, heads * HEAD_DIM), jnp.bfloat16)] * 4,
-        compiler_params=pltpu.CompilerParams(vmem_limit_bytes=16 * 1024 * 1024),
-        cost_estimate=pl.CostEstimate(
-            flops=heads * 2 * rows * lanes * HEAD_DIM, bytes_accessed=heads * 2 * rows * lanes, transcendentals=0
-        ),
-    )(weights, totals, *[x for x, _ in blocks])
+    )(*scalars, *arrays)
 
 
 def pack_kernel(copies, width, mask, offset, *refs):
@@ -332,14 +399,16 @@
     )(mask, offset, *operands)
 
 
-def relayed_kernel(mine, other, k_out, v_out):
-    tile, width = k_out.shape
+def relayed_kernel(parts, mine, other, *outs):
+    tile = other.shape[0]
+    half = other.shape[1] // 2
     offset = jnp.max(mine[tile : tile + INFO_ROWS, 4 * 128 : 5 * 128].astype(jnp.float32))
     here = offset == (lax.axis_index("head") // 2).astype(jnp.float32)
 
     def take(ref):
-        k_out[...] = ref[:tile, :width]
-        v_out[...] = ref[:tile, width:]
+        for (begin, end), out in zip(parts, outs):
+            out[:, : end - begin] = ref[:tile, begin:end]
+            out[:, end - begin :] = ref[:tile, half + begin : half + end]
 
     @pl.when(here)
     def _():
@@ -350,13 +419,12 @@
         take(other)
 
 
-def relayed(mine, other):
-    tile, lanes = other.shape
+def relayed(mine, other, parts):
     return pl.pallas_call(
-        relayed_kernel,
+        functools.partial(relayed_kernel, parts),
         in_specs=[pl.BlockSpec(memory_space=pltpu.VMEM)] * 2,
-        out_specs=[pl.BlockSpec(memory_space=pltpu.VMEM)] * 2,
-        out_shape=[jax.ShapeDtypeStruct((tile, lanes // 2), other.dtype)] * 2,
+        out_specs=[pl.BlockSpec(memory_space=pltpu.VMEM)] * len(parts),
+        out_shape=[jax.ShapeDtypeStruct((other.shape[0], 2 * (end - begin)), other.dtype) for begin, end in parts],
         compiler_params=pltpu.CompilerParams(vmem_limit_bytes=4 * 1024 * 1024),
     )(mine, other)
 
@@ -381,6 +449,10 @@
 
     def along(array, pairs):
         return lax.ppermute(array, "frame", pairs)
+
+    def across(array):
+        pairs = [(4 * z + j, 4 * (3 - z) + j if z in (1, 2) else 4 * z + (j ^ 1)) for z in range(4) for j in range(4)]
+        return lax.ppermute(array, ("frame", "head"), pairs)
 
     def after(array, earlier):
         return lax.optimization_barrier((array, earlier))[0]
@@ -399,30 +471,84 @@
     mine = below(beside(*kv[0]), got[:, : 2 * width], told)
     other = to_head(below(beside(*kv[2]), got[:, 2 * width :]), 2)
     n1m = along(mine, OUTER)
-    n2m = along(mine, INNER)
+    n2m = across(mine)
     n1o = along(other, OUTER)
-    n2o = along(other, INNER)
+    n2o = across(other)
 
     got = to_head(after(pay, got), 1)
     q_mine = below(q_own, got[:, :width])
     q_other = to_head(after(below(q_far, got[:, width:]), other), 2)
 
-    r1k, r1v = after(relayed(n1m, n1o), n2m)
-    r1k = along(r1k, INNER)
-    r1v = along(r1v, INNER)
-    r2k, r2v = relayed(n2m, n2o)
-    r2k = along(r2k, OUTWARD)
-    r3k = along(r1k, OUTWARD)
-    r2v = along(after(r2v, r1k), OUTWARD)
-    r3v = along(r1v, OUTWARD)
-
-    near = [mine, other, n1m, n1o, n2m, n2o]
-    weights, totals = find_weights(pair_mask, q_mine, q_other, [*near, r1k, r2k, r3k], heads)
-    out = mix_values(weights, totals, [(x, heads) for x in near] + [(x, 0) for x in (r1v, r2v, r3v)], heads)
-    out = [out[0]] + [to_head(out[d], d) for d in (1, 2, 3)]
+    tile = 2 * rows
+    cut = HOME * HEAD_DIM
+    guests = heads - HOME
+    q_guest = along(below(q_mine[:, cut:], q_other[:, cut:]), OUTER)
+    r1_home, r1_rest = after(relayed(n1m, n1o, [(0, cut), (cut, width)]), n2m)
+    r1_home = across(r1_home)
+    (r2,) = relayed(n2m, n2o, [(0, cut)])
+    r1_rest = across(after(r1_rest, r2))
+    r2 = along(r2, OUTER)
+
+    def state(count):
+        return [((count * 2 * tile, HEAD_DIM), jnp.float32)] * 3 + [((8, 128), jnp.float32)]
+
+    def flops(chunks, tiles):
+        return 4 * chunks * tiles * tile * tile * HEAD_DIM
+
+    bf16 = jnp.bfloat16
+    q = [q_mine, q_other]
+    around = [mine, other, n1m, n1o, n2m, n2o]
+    *near, done = run_kernel(
+        functools.partial(near_kernel, 0, 0, ((6, HOME), (4, HOME))),
+        None,
+        [*q, *around],
+        state(HOME),
+        (tile, 6 * tile),
+        flops(2 * HOME, 6),
+    )
+    r3 = along(after(passed(r1_home, done), r2), OUTER)
+    q_halves = [q_guest[:tile], q_guest[tile:]]
+    *guest_near, _ = run_kernel(
+        functools.partial(near_kernel, HOME, 0, ((4, guests), (0, 0))),
+        None,
+        [*q_halves, mine, other, n1m, n1o],
+        state(guests),
+        (tile, 4 * tile),
+        flops(2 * guests, 4),
+    )
+    (back,) = run_kernel(
+        functools.partial(guest_kernel, HOME),
+        None,
+        [q_guest, *guest_near, n1m, n2m, n2o, r1_rest],
+        [((2 * tile, width - cut), bf16)],
+        (tile, 3 * tile),
+        flops(2 * guests, 3),
+    )
+    back = along(back, OUTER)
+    out = run_kernel(
+        home_kernel, pair_mask, [*q, *near, r1_home, r2, r3], [((rows, cut), bf16)] * 4, (tile, 2 * tile), flops(2 * HOME, 2)
+    )
+    pieces = [(to_head(out[d], d) if d else out[0], d, 0) for d in range(4)]
+    *rest_near, _ = run_kernel(
+        functools.partial(near_kernel, HOME, HOME, ((6, guests), (0, 0))),
+        None,
+        [*q, *around],
+        state(guests),
+        (tile, 6 * tile),
+        flops(2 * guests, 6),
+    )
+    out = run_kernel(
+        functools.partial(rest_kernel, HOME),
+        pair_mask,
+        [*q, *rest_near, r1_rest, after(back, out[1])],
+        [((rows, width - cut), bf16)] * 4,
+        (tile, tile),
+        flops(2 * guests, 1),
+    )
+    pieces += [(to_head(out[d], d) if d else out[0], d, cut) for d in range(4)]
     result = jnp.zeros((rows, features), jnp.bfloat16)
-    for d in range(4):
-        result = lax.dynamic_update_slice_in_dim(result, out[d], (h ^ d) * width, axis=1)
+    for piece, d, begin in pieces:
+        result = lax.dynamic_update_slice_in_dim(result, piece, (h ^ d) * width + begin, axis=1)
     return result
 
 

time: 91.5 us -> 87.5 us (0.956)
  waiting for transfers between devices: 59 us -> 40.1 us
  local copies, waits for them, and re-layouts: 2.42 us -> 9.68 us
  starting transfers between devices: 17.2 us -> 24.3 us
    ppermute x10 -> x6, waiting for transfers between devices: 35.6 us -> 22.1 us  [along(): return lax.ppermute(array, 'frame', pairs)]
    unnamed x10 -> x48, local copies, waits for them, and re-layouts: 0.03 us -> 7.29 us
    ppermute x7 -> x10, waiting for transfers between devices: 23.4 us -> 18 us  [to_head(): return lax.ppermute(array, 'head', [(i, i ^ d) for i in range(4)])]
    ppermute x10 -> x6, starting transfers between devices: 11.4 us -> 15 us  [along(): return lax.ppermute(array, 'frame', pairs)]
    ppermute x7 -> x10, starting transfers between devices: 5.81 us -> 8.99 us  [to_head(): return lax.ppermute(array, 'head', [(i, i ^ d) for i in range(4)])]
    pallas_call x4 -> x9, Pallas kernels: 10.7 us -> 11.1 us  [the longest x6 9.96 us: run_kernel(): pl.pallas_call(kernel, in_specs=[pl.BlockSpec(memory_space=pltpu.SMEM)] *...]
  transfers between devices with their start and end apart: 17 -> 20, of which waited for: 11 -> 10; matrix products, arithmetic and copies ran while one was open for 0% -> 0% of each run, Pallas kernels for 8% -> 14%
where the time goes in v11:
time: 87.5 us; the launch traced here: 87.2 us
  waiting for transfers between devices  40.1 us (46%)
  starting transfers between devices  24.3 us (28%)
  Pallas kernels  11.8 us (13%)
  local copies, waits for them, and re-layouts  9.68 us (11%)
  between operations  1.05 us (1%)
    ppermute x6, waiting for transfers between devices, along(): return lax.ppermute(array, 'frame', pairs)  22.1 us
    ppermute x10, waiting for transfers between devices, to_head(): return lax.ppermute(array, 'head', [(i, i ^ d) for i in range(4)])  18 us
    ppermute x6, starting transfers between devices, along(): return lax.ppermute(array, 'frame', pairs)  15 us
    pallas_call x6, Pallas kernels, run_kernel(): pl.pallas_call(kernel, in_specs=[pl.BlockSpec(memory_space=pltpu.SMEM)] *...  9.96 us
    ppermute x10, starting transfers between devices, to_head(): return lax.ppermute(array, 'head', [(i, i ^ d) for i in range(4)])  8.99 us
    unnamed x48, local copies, waits for them, and re-layouts  7.29 us
  transfers between devices with their start and end apart: 20, of which 10 were waited for; matrix products, arithmetic and copies ran while one was open for 0% of the time, Pallas kernels for 14%

profile of v11, /device:TPU:0, one launch (start us, length us, event | category | flops | bytes accessed | tf_op | source)
XLA Modules:
  0.0 87.2 jit_solution(7138151080172874720)
XLA Ops:
  0.0 1.5 %constant_dynamic-slice_fusion = (bf16[128,640]{1,0:T(8,128)(2,1)S(1)}, bf16[128,640]{1,0:T(8,128)(2,1)S(1)}, bf16[128,640]{1,0:T(8,128)(2,1)S(1)}, bf16[128,640...) fusion(bf16[128,2560]{1,0:T(8,128)(2,1)} %refs_2_.1, ...), kind=kLoop, calls=%fused_computation.17 | loop fusion | bytes 2621456 | tf_op jit(solution)/shard_map/dynamic_slice | solution.py:439
  1.6 0.5 collective-permute-start
  2.1 1.7 %collective-permute-done = bf16[128,2560]{1,0:T(8,128)(2,1)S(1)} collective-permute-done((bf16[128,2560]{1,0:T(8,128)(2,1)S(1)}, bf16[128,2560]{1,0:T(8,128)(2,1)S(1)}, u32[]{:S(2)}, u32[]{:S(2)}) %collective-permute-start) | collective-permute-done | bytes 655392 | tf_op jit(solution)/shard_map/ppermute | solution.py:448
  4.0 2.9 %collective-permute-start.2 = (bf16[256,1280]{1,0:T(8,128)(2,1)S(1)}, bf16[256,1280]{1,0:T(8,128)(2,1)S(1)}, u32[]{:S(2)}, u32[]{:S(2)}) collective-permute-start(bf16[256,1280]{1,0:T(8,128)(2,1)S(1)} %pad_maximum_fusion.2), channel_id=1, source_target_pairs={{0,2},{1,3},{2,0},{3,1},{4,6},{5,7},{6,4},{7,5},{8,10},{9,11},{10,... | collective-permute-start | bytes 1966088 | tf_op jit(solution)/shard_map/ppermute | solution.py:448
  7.6 0.7 shard_map.55
  8.4 1.6 %collective-permute-start.4 = (bf16[272,1280]{1,0:T(8,128)(2,1)S(1)}, bf16[272,1280]{1,0:T(8,128)(2,1)S(1)}, u32[]{:S(2)}, u32[]{:S(2)}) collective-permute-start(bf16[272,1280]{1,0:T(8,128)(2,1)S(1)} %pad_maximum_fusion.refs_0_), channel_id=1, source_target_pairs={{0,4},{4,0},{8,12},{12,8},{1,5},{5,1},{9,13},{13,9},{2,6},{6,2},{1... | collective-permute-start | bytes 2088968 | tf_op jit(solution)/shard_map/ppermute | solution.py:451
  10.0 0.2 collective-permute-start.6
  10.3 11.7 %collective-permute-done.2.refs_1_ = bf16[256,1280]{1,0:T(8,128)(2,1)S(1)} collective-permute-done((bf16[256,1280]{1,0:T(8,128)(2,1)S(1)}, bf16[256,1280]{1,0:T(8,128)(2,1)S(1)}, u32[]{:S(2)}, u32[]{:S(2)}) %collective-permute-start.2) | collective-permute-done | bytes 655392 | tf_op jit(solution)/shard_map/ppermute | solution.py:448
  21.9 1.8 %collective-permute-start.5 = (bf16[256,1280]{1,0:T(8,128)(2,1)S(1)}, bf16[256,1280]{1,0:T(8,128)(2,1)S(1)}, u32[]{:S(2)}, u32[]{:S(2)}) collective-permute-start(bf16[256,1280]{1,0:T(8,128)(2,1)S(1)} %collective-permute-done.2.refs_1_), channel_id=1, source_target_pairs={{0,4},{4,0},{8,12},{12,8},{1,5},{5,1},{9,13},{13,9},{2,6},{6,2},{1... | collective-permute-start | bytes 1966088 | tf_op jit(solution)/shard_map/ppermute | solution.py:451
  23.8 1.6 %collective-permute-start.3 = (bf16[256,640]{1,0:T(8,128)(2,1)S(1)}, bf16[256,640]{1,0:T(8,128)(2,1)S(1)}, u32[]{:S(2)}, u32[]{:S(2)}) collective-permute-start(bf16[256,640]{1,0:T(8,128)(2,1)S(1)} %pad_maximum_fusion.4), channel_id=1, source_target_pairs={{0,2},{1,3},{2,0},{3,1},{4,6},{5,7},{6,4},{7,5},{8,10},{9,11},{10,... | collective-permute-start | bytes 983048 | tf_op jit(solution)/shard_map/ppermute | solution.py:448
  25.4 1.5 %collective-permute-done.4.refs_2_.mine.n1m = bf16[272,1280]{1,0:T(8,128)(2,1)S(1)} collective-permute-done((bf16[272,1280]{1,0:T(8,128)(2,1)S(1)}, bf16[272,1280]{1,0:T(8,128)(2,1)S(1)}, u32[]{:S(2)}, u32[]{:S(2)}) %collective-permute-start.4) | collective-permute-done | bytes 696352 | tf_op jit(solution)/shard_map/ppermute | solution.py:451
  26.9 13.6 %collective-permute-done.5.refs_3_.other = bf16[256,1280]{1,0:T(8,128)(2,1)S(1)} collective-permute-done((bf16[256,1280]{1,0:T(8,128)(2,1)S(1)}, bf16[256,1280]{1,0:T(8,128)(2,1)S(1)}, u32[]{:S(2)}, u32[]{:S(2)}) %collective-permute-start.5) | collective-permute-done | bytes 655392 | tf_op jit(solution)/shard_map/ppermute | solution.py:451
  40.5 0.2 shard_map.57
  40.8 0.2 shard_map.58
  41.0 3.2 %collective-permute-start.9 = (bf16[256,768]{1,0:T(8,128)(2,1)S(1)}, bf16[256,768]{1,0:T(8,128)(2,1)S(1)}, u32[]{:S(2)}, u32[]{:S(2)}) collective-permute-start(bf16[256,768]{1,0:T(8,128)(2,1)S(1)} %shard_map.58), channel_id=1, source_target_pairs={{0,4},{4,0},{8,12},{12,8},{1,5},{5,1},{9,13},{13,9},{2,6},{6,2},{1... | collective-permute-start | bytes 1179656 | tf_op jit(solution)/shard_map/ppermute | solution.py:451
  44.4 2.9 %shard_map.56 = (f32[1536,128]{1,0:T(8,128)S(1)}, f32[1536,128]{1,0:T(8,128)S(1)}, f32[1536,128]{1,0:T(8,128)S(1)}, f32[8,128]{1,0:T(8,128)S(1)}) custom-call(bf16[256,640]{1,0:T(8,128)(2,1)S(1)} %pad_maximum_fusion.3.q_mine, bf16[256,640]{1,0:T(8,128)(2,1)S(1)} %collective-permute-done.3.q_other, bf16[272,1280]{1,0:T(8,128)(2,1)S(1)} %pad_maximum_fusion.refs_0_, ...), custom_call_target="tpu_custom_call" | custom-call | flops 1207959552 | bytes 4710400 | tf_op jit(solution)/shard_map/pallas_call | solution.py:348
  47.4 0.9 %copy-done.15 = f32[1536,128]{1,0:T(8,128)} copy-done((f32[1536,128]{1,0:T(8,128)}, f32[1536,128]{1,0:T(8,128)S(1)}, u32[]{:S(2)}) %copy-start.15) | copy-done | bytes 786456
  48.3 0.9 %copy-done.17 = f32[1536,128]{1,0:T(8,128)} copy-done((f32[1536,128]{1,0:T(8,128)}, f32[1536,128]{1,0:T(8,128)S(1)}, u32[]{:S(2)}) %copy-start.17) | copy-done | bytes 786456
  49.2 0.8 shard_map.59
  50.0 4.1 %collective-permute-done.9.r2 = bf16[256,768]{1,0:T(8,128)(2,1)S(1)} collective-permute-done((bf16[256,768]{1,0:T(8,128)(2,1)S(1)}, bf16[256,768]{1,0:T(8,128)(2,1)S(1)}, u32[]{:S(2)}, u32[]{:S(2)}) %collective-permute-start.9) | collective-permute-done | bytes 393248 | tf_op jit(solution)/shard_map/ppermute | solution.py:451
  54.2 0.7 copy-done.20
  54.9 2.1 %collective-permute-start.10 = (bf16[256,768]{1,0:T(8,128)(2,1)}, bf16[256,768]{1,0:T(8,128)(2,1)}, u32[]{:S(2)}, u32[]{:S(2)}) collective-permute-start(bf16[256,768]{1,0:T(8,128)(2,1)} %shard_map.59), channel_id=1, source_target_pairs={{0,4},{4,0},{8,12},{12,8},{1,5},{5,1},{9,13},{13,9},{2,6},{6,2},{1... | collective-permute-start | bytes 1179656 | tf_op jit(solution)/shard_map/ppermute | solution.py:451
  56.9 2.8 %collective-permute-done.15.q = bf16[512,256]{1,0:T(8,128)(2,1)S(1)} collective-permute-done((bf16[512,256]{1,0:T(8,128)(2,1)S(1)}, bf16[512,256]{1,0:T(8,128)(2,1)S(1)}, u32[]{:S(2)}, u32[]{:S(2)}) %collective-permute-start.15) | collective-permute-done | bytes 262176 | tf_op jit(solution)/shard_map/ppermute | solution.py:451
  59.8 0.6 shard_map.62
  60.4 0.8 shard_map.63
  61.3 6.2 %collective-permute-start.16 = (bf16[512,256]{1,0:T(8,128)(2,1)}, bf16[512,256]{1,0:T(8,128)(2,1)}, u32[]{:S(2)}, u32[]{:S(2)}) collective-permute-start(bf16[512,256]{1,0:T(8,128)(2,1)} %shard_map.63), channel_id=1, source_target_pairs={{0,4},{4,0},{8,12},{12,8},{1,5},{5,1},{9,13},{13,9},{2,6},{6,2},{1... | collective-permute-start | bytes 786440 | tf_op jit(solution)/shard_map/ppermute | solution.py:451
  67.4 1.0 %copy-done.1 = bf16[256,640]{1,0:T(8,128)(2,1)S(1)} copy-done((bf16[256,640]{1,0:T(8,128)(2,1)S(1)}, bf16[256,640]{1,0:T(8,128)(2,1)}, u32[]{:S(2)}) %copy-start.1) | copy-done | bytes 327704
  68.4 1.0 %copy-done.4 = bf16[256,640]{1,0:T(8,128)(2,1)S(1)} copy-done((bf16[256,640]{1,0:T(8,128)(2,1)S(1)}, bf16[256,640]{1,0:T(8,128)(2,1)}, u32[]{:S(2)}) %copy-start.4) | copy-done | bytes 327704
  69.4 1.1 %copy-done.6 = bf16[256,1280]{1,0:T(8,128)(2,1)S(1)} copy-done((bf16[256,1280]{1,0:T(8,128)(2,1)S(1)}, bf16[256,1280]{1,0:T(8,128)(2,1)}, u32[]{:S(2)}) %copy-start.6) | copy-done | bytes 655384
  70.5 0.6 shard_map.61
  71.1 0.3 copy-done.2
  71.4 0.1 copy-done.10
  71.6 0.3 copy-done.14
  71.8 0.2 copy-done.16
  72.1 0.2 copy-done.18
  72.4 4.0 %shard_map.60 = (bf16[128,384]{1,0:T(8,128)(2,1)S(1)}, bf16[128,384]{1,0:T(8,128)(2,1)S(1)}, bf16[128,384]{1,0:T(8,128)(2,1)S(1)}, bf16[128,384]{1,0:T(8,128)(2,1)S(1)}) custom-call(s32[1,4]{1,0:T(1,128)S(1)} %copy-done.22, bf16[256,640]{1,0:T(8,128)(2,1)S(1)} %copy-done.2, bf16[256,640]{1,0:T(8,128)(2,1)S(1)} %copy-done.4, f32[1536,128]{1,0:T(8,128)S(1)} %copy-done.14, ...), custom_call_target="tpu_custom_call" | custom-call | flops 402653184 | bytes 3014656 | tf_op jit(solution)/shard_map/pallas_call | solution.py:348
  76.5 0.7 collective-permute-start.12
  77.2 1.2 %collective-permute-start.13 = (bf16[128,384]{1,0:T(8,128)(2,1)S(1)}, bf16[128,384]{1,0:T(8,128)(2,1)S(1)}, u32[]{:S(2)}, u32[]{:S(2)}) collective-permute-start(bf16[128,384]{1,0:T(8,128)(2,1)S(1)} %get-tuple-element.69), channel_id=1, source_target_pairs={{0,3},{1,2},{2,1},{3,0},{4,7},{5,6},{6,5},{7,4},{8,11},{9,10},{10,... | collective-permute-start | bytes 294920 | tf_op jit(solution)/shard_map/ppermute | solution.py:448
  78.4 1.0 %shard_map.64 = (bf16[128,256]{1,0:T(8,128)(2,1)S(1)}, bf16[128,256]{1,0:T(8,128)(2,1)S(1)}, bf16[128,256]{1,0:T(8,128)(2,1)S(1)}, bf16[128,256]{1,0:T(8,128)(2,1)S(1)}) custom-call(s32[1,4]{1,0:T(1,128)S(1)} %copy-done.22, bf16[256,640]{1,0:T(8,128)(2,1)S(1)} %copy-done.2, bf16[256,640]{1,0:T(8,128)(2,1)S(1)} %copy-done.4, ...), custom_call_target="tpu_custom_call" | custom-call | flops 134217728 | bytes 1966080 | tf_op jit(solution)/shard_map/pallas_call | solution.py:348
  79.4 0.4 collective-permute-start.17
  79.8 0.6 collective-permute-start.18
  80.5 1.0 %collective-permute-start.19 = (bf16[128,256]{1,0:T(8,128)(2,1)S(1)}, bf16[128,256]{1,0:T(8,128)(2,1)S(1)}, u32[]{:S(2)}, u32[]{:S(2)}) collective-permute-start(bf16[128,256]{1,0:T(8,128)(2,1)S(1)} %get-tuple-element.82), channel_id=1, source_target_pairs={{0,3},{1,2},{2,1},{3,0},{4,7},{5,6},{6,5},{7,4},{8,11},{9,10},{10,... | collective-permute-start | bytes 196616 | tf_op jit(solution)/shard_map/ppermute | solution.py:448
  81.5 0.7 collective-permute-done.12
  82.2 1.2 %collective-permute-done.13 = bf16[128,384]{1,0:T(8,128)(2,1)S(1)} collective-permute-done((bf16[128,384]{1,0:T(8,128)(2,1)S(1)}, bf16[128,384]{1,0:T(8,128)(2,1)S(1)}, u32[]{:S(2)}, u32[]{:S(2)}) %collective-permute-start.13) | collective-permute-done | bytes 98336 | tf_op jit(solution)/shard_map/ppermute | solution.py:448
  83.4 2.3 %collective-permute-done.18 = bf16[128,256]{1,0:T(8,128)(2,1)S(1)} collective-permute-done((bf16[128,256]{1,0:T(8,128)(2,1)S(1)}, bf16[128,256]{1,0:T(8,128)(2,1)S(1)}, u32[]{:S(2)}, u32[]{:S(2)}) %collective-permute-start.18) | collective-permute-done | bytes 65568 | tf_op jit(solution)/shard_map/ppermute | solution.py:448
  85.7 0.5 collective-permute-done.19
  86.2 0.4 copy-done.23
  86.5 0.6 constant_dynamic-update-slice_fusion
  (71 shorter events, 1.1 us)
Async XLA Ops:
  1.6 2.2 %collective-permute-start = (bf16[128,2560]{1,0:T(8,128)(2,1)S(1)}, bf16[128,2560]{1,0:T(8,128)(2,1)S(1)}, u32[]{:S(2)}, u32[]{:S(2)}) collective-permute-start(bf16[128,2560]{1,0:T(8,128)(2,1)S(1)} %pad_maximum_fusion.1), channel_id=1, source_target_pairs={{0,1},{1,0},{2,3},{3,2},{4,5},{5,4},{6,7},{7,6},{8,9},{9,8},{10,11... | collective-permute-start | bytes 1966088 | tf_op jit(solution)/shard_map/ppermute | solution.py:448
  3.8 3.7 %copy-start.19 = (bf16[128,2560]{1,0:T(8,128)(2,1)S(1)}, bf16[128,2560]{1,0:T(8,128)(2,1)}, u32[]{:S(2)}) copy-start(bf16[128,2560]{1,0:T(8,128)(2,1)} %refs_0_.1) | copy-start | bytes 1966084
  3.9 3.7 %copy-start.7 = (bf16[128,2560]{1,0:T(8,128)(2,1)S(1)}, bf16[128,2560]{1,0:T(8,128)(2,1)}, u32[]{:S(2)}) copy-start(bf16[128,2560]{1,0:T(8,128)(2,1)} %refs_1_.1) | copy-start | bytes 1966084
  3.9 3.7 %copy-start.8 = (bf16[128,2560]{1,0:T(8,128)(2,1)S(1)}, bf16[128,2560]{1,0:T(8,128)(2,1)}, u32[]{:S(2)}) copy-start(bf16[128,2560]{1,0:T(8,128)(2,1)} %refs_2_.1) | copy-start | bytes 1966084
  3.9 3.7 %copy-start.22 = (s32[1,4]{1,0:T(1,128)S(1)}, s32[1,4]{1,0:T(1,128)}, u32[]{:S(2)}) copy-start(s32[1,4]{1,0:T(1,128)} %mask.5) | copy-start | bytes 52
  4.0 18.0 %collective-permute-start.2 = (bf16[256,1280]{1,0:T(8,128)(2,1)S(1)}, bf16[256,1280]{1,0:T(8,128)(2,1)S(1)}, u32[]{:S(2)}, u32[]{:S(2)}) collective-permute-start(bf16[256,1280]{1,0:T(8,128)(2,1)S(1)} %pad_maximum_fusion.2), channel_id=1, source_target_pairs={{0,2},{1,3},{2,0},{3,1},{4,6},{5,7},{6,4},{7,5},{8,10},{9,11},{10,... | collective-permute-start | bytes 1966088 | tf_op jit(solution)/shard_map/ppermute | solution.py:448
  8.3 15.5 %collective-permute-start.1 = (bf16[128,1280]{1,0:T(8,128)(2,1)S(1)}, bf16[128,1280]{1,0:T(8,128)(2,1)S(1)}, u32[]{:S(2)}, u32[]{:S(2)}) collective-permute-start(bf16[128,1280]{1,0:T(8,128)(2,1)S(1)} %get-tuple-element.50), channel_id=1, source_target_pairs={{0,1},{1,0},{2,3},{3,2},{4,5},{5,4},{6,7},{7,6},{8,9},{9,8},{10,11... | collective-permute-start | bytes 983048 | tf_op jit(solution)/shard_map/ppermute | solution.py:448
  8.4 18.5 %collective-permute-start.4 = (bf16[272,1280]{1,0:T(8,128)(2,1)S(1)}, bf16[272,1280]{1,0:T(8,128)(2,1)S(1)}, u32[]{:S(2)}, u32[]{:S(2)}) collective-permute-start(bf16[272,1280]{1,0:T(8,128)(2,1)S(1)} %pad_maximum_fusion.refs_0_), channel_id=1, source_target_pairs={{0,4},{4,0},{8,12},{12,8},{1,5},{5,1},{9,13},{13,9},{2,6},{6,2},{1... | collective-permute-start | bytes 2088968 | tf_op jit(solution)/shard_map/ppermute | solution.py:451
  10.0 30.7 %collective-permute-start.6 = (bf16[272,1280]{1,0:T(8,128)(2,1)S(1)}, bf16[272,1280]{1,0:T(8,128)(2,1)S(1)}, u32[]{:S(2)}, u32[]{:S(2)}) collective-permute-start(bf16[272,1280]{1,0:T(8,128)(2,1)S(1)} %pad_maximum_fusion.refs_0_), channel_id=1, source_target_pairs={{0,1},{1,0},{2,3},{3,2},{4,8},{5,9},{6,10},{7,11},{8,4},{9,5},{10,... | collective-permute-start | bytes 2088968 | tf_op jit(solution)/shard_map/ppermute | solution.py:455
  21.9 37.9 %copy-start.5 = (bf16[256,1280]{1,0:T(8,128)(2,1)}, bf16[256,1280]{1,0:T(8,128)(2,1)S(1)}, u32[]{:S(2)}) copy-start(bf16[256,1280]{1,0:T(8,128)(2,1)S(1)} %collective-permute-done.2.refs_1_) | copy-start | bytes 1966084
  21.9 18.6 %collective-permute-start.5 = (bf16[256,1280]{1,0:T(8,128)(2,1)S(1)}, bf16[256,1280]{1,0:T(8,128)(2,1)S(1)}, u32[]{:S(2)}, u32[]{:S(2)}) collective-permute-start(bf16[256,1280]{1,0:T(8,128)(2,1)S(1)} %collective-permute-done.2.refs_1_), channel_id=1, source_target_pairs={{0,4},{4,0},{8,12},{12,8},{1,5},{5,1},{9,13},{13,9},{2,6},{6,2},{1... | collective-permute-start | bytes 1966088 | tf_op jit(solution)/shard_map/ppermute | solution.py:451
  23.7 17.0 %collective-permute-start.7 = (bf16[256,1280]{1,0:T(8,128)(2,1)S(1)}, bf16[256,1280]{1,0:T(8,128)(2,1)S(1)}, u32[]{:S(2)}, u32[]{:S(2)}) collective-permute-start(bf16[256,1280]{1,0:T(8,128)(2,1)S(1)} %collective-permute-done.2.refs_1_), channel_id=1, source_target_pairs={{0,1},{1,0},{2,3},{3,2},{4,8},{5,9},{6,10},{7,11},{8,4},{9,5},{10,... | collective-permute-start | bytes 1966088 | tf_op jit(solution)/shard_map/ppermute | solution.py:455
  23.8 20.4 %collective-permute-start.3 = (bf16[256,640]{1,0:T(8,128)(2,1)S(1)}, bf16[256,640]{1,0:T(8,128)(2,1)S(1)}, u32[]{:S(2)}, u32[]{:S(2)}) collective-permute-start(bf16[256,640]{1,0:T(8,128)(2,1)S(1)} %pad_maximum_fusion.4), channel_id=1, source_target_pairs={{0,2},{1,3},{2,0},{3,1},{4,6},{5,7},{6,4},{7,5},{8,10},{9,11},{10,... | collective-permute-start | bytes 983048 | tf_op jit(solution)/shard_map/ppermute | solution.py:448
  40.7 8.5 %collective-permute-start.8 = (bf16[256,768]{1,0:T(8,128)(2,1)S(1)}, bf16[256,768]{1,0:T(8,128)(2,1)S(1)}, u32[]{:S(2)}, u32[]{:S(2)}) collective-permute-start(bf16[256,768]{1,0:T(8,128)(2,1)S(1)} %get-tuple-element.63), channel_id=1, source_target_pairs={{0,1},{1,0},{2,3},{3,2},{4,8},{5,9},{6,10},{7,11},{8,4},{9,5},{10,... | collective-permute-start | bytes 1179656 | tf_op jit(solution)/shard_map/ppermute | solution.py:455
  41.0 13.2 %collective-permute-start.9 = (bf16[256,768]{1,0:T(8,128)(2,1)S(1)}, bf16[256,768]{1,0:T(8,128)(2,1)S(1)}, u32[]{:S(2)}, u32[]{:S(2)}) collective-permute-start(bf16[256,768]{1,0:T(8,128)(2,1)S(1)} %shard_map.58), channel_id=1, source_target_pairs={{0,4},{4,0},{8,12},{12,8},{1,5},{5,1},{9,13},{13,9},{2,6},{6,2},{1... | collective-permute-start | bytes 1179656 | tf_op jit(solution)/shard_map/ppermute | solution.py:451
  44.2 3.2 %copy-start.3 = (bf16[256,640]{1,0:T(8,128)(2,1)}, bf16[256,640]{1,0:T(8,128)(2,1)S(1)}, u32[]{:S(2)}) copy-start(bf16[256,640]{1,0:T(8,128)(2,1)S(1)} %collective-permute-done.3.q_other) | copy-start | bytes 983044
  44.2 15.5 %collective-permute-start.15 = (bf16[512,256]{1,0:T(8,128)(2,1)S(1)}, bf16[512,256]{1,0:T(8,128)(2,1)S(1)}, u32[]{:S(2)}, u32[]{:S(2)}) collective-permute-start(bf16[512,256]{1,0:T(8,128)(2,1)S(1)} %pad_maximum_fusion.5), channel_id=1, source_target_pairs={{0,4},{4,0},{8,12},{12,8},{1,5},{5,1},{9,13},{13,9},{2,6},{6,2},{1... | collective-permute-start | bytes 786440 | tf_op jit(solution)/shard_map/ppermute | solution.py:451
  44.4 3.0 %copy-start = (bf16[256,640]{1,0:T(8,128)(2,1)}, bf16[256,640]{1,0:T(8,128)(2,1)S(1)}, u32[]{:S(2)}) copy-start(bf16[256,640]{1,0:T(8,128)(2,1)S(1)} %pad_maximum_fusion.3.q_mine) | copy-start | bytes 983044
  44.4 16.1 %collective-permute-start.14 = (bf16[256,512]{1,0:T(8,128)(2,1)S(1)}, bf16[256,512]{1,0:T(8,128)(2,1)S(1)}, u32[]{:S(2)}, u32[]{:S(2)}) collective-permute-start(bf16[256,512]{1,0:T(8,128)(2,1)S(1)} %get-tuple-element.74), channel_id=1, source_target_pairs={{0,1},{1,0},{2,3},{3,2},{4,8},{5,9},{6,10},{7,11},{8,4},{9,5},{10,... | collective-permute-start | bytes 786440 | tf_op jit(solution)/shard_map/ppermute | solution.py:455
  47.4 0.9 %copy-start.15 = (f32[1536,128]{1,0:T(8,128)}, f32[1536,128]{1,0:T(8,128)S(1)}, u32[]{:S(2)}) copy-start(f32[1536,128]{1,0:T(8,128)S(1)} %get-tuple-element.59.tops) | copy-start | bytes 2359300
  48.3 0.9 %copy-start.17 = (f32[1536,128]{1,0:T(8,128)}, f32[1536,128]{1,0:T(8,128)S(1)}, u32[]{:S(2)}) copy-start(f32[1536,128]{1,0:T(8,128)S(1)} %get-tuple-element.60.totals) | copy-start | bytes 2359300
  49.2 11.2 %copy-start.13 = (f32[1536,128]{1,0:T(8,128)}, f32[1536,128]{1,0:T(8,128)S(1)}, u32[]{:S(2)}) copy-start(f32[1536,128]{1,0:T(8,128)S(1)} %get-tuple-element.58.mixed) | copy-start | bytes 2359300
  49.2 11.2 %copy-start.9 = (bf16[256,768]{1,0:T(8,128)(2,1)}, bf16[256,768]{1,0:T(8,128)(2,1)S(1)}, u32[]{:S(2)}) copy-start(bf16[256,768]{1,0:T(8,128)(2,1)S(1)} %collective-permute-done.8.x.r1) | copy-start | bytes 1179652
  54.2 0.7 copy-start.20
  54.9 16.2 %collective-permute-start.10 = (bf16[256,768]{1,0:T(8,128)(2,1)}, bf16[256,768]{1,0:T(8,128)(2,1)}, u32[]{:S(2)}, u32[]{:S(2)}) collective-permute-start(bf16[256,768]{1,0:T(8,128)(2,1)} %shard_map.59), channel_id=1, source_target_pairs={{0,4},{4,0},{8,12},{12,8},{1,5},{5,1},{9,13},{13,9},{2,6},{6,2},{1... | collective-permute-start | bytes 1179656 | tf_op jit(solution)/shard_map/ppermute | solution.py:451
  60.4 0.8 copy-start.11
  61.3 15.3 %collective-permute-start.16 = (bf16[512,256]{1,0:T(8,128)(2,1)}, bf16[512,256]{1,0:T(8,128)(2,1)}, u32[]{:S(2)}, u32[]{:S(2)}) collective-permute-start(bf16[512,256]{1,0:T(8,128)(2,1)} %shard_map.63), channel_id=1, source_target_pairs={{0,4},{4,0},{8,12},{12,8},{1,5},{5,1},{9,13},{13,9},{2,6},{6,2},{1... | collective-permute-start | bytes 786440 | tf_op jit(solution)/shard_map/ppermute | solution.py:451
  67.4 1.0 %copy-start.1 = (bf16[256,640]{1,0:T(8,128)(2,1)S(1)}, bf16[256,640]{1,0:T(8,128)(2,1)}, u32[]{:S(2)}) copy-start(bf16[256,640]{1,0:T(8,128)(2,1)} %copy-done) | copy-start | bytes 983044
  68.4 1.0 %copy-start.4 = (bf16[256,640]{1,0:T(8,128)(2,1)S(1)}, bf16[256,640]{1,0:T(8,128)(2,1)}, u32[]{:S(2)}) copy-start(bf16[256,640]{1,0:T(8,128)(2,1)} %copy-done.3) | copy-start | bytes 983044
  69.4 1.1 %copy-start.6 = (bf16[256,1280]{1,0:T(8,128)(2,1)S(1)}, bf16[256,1280]{1,0:T(8,128)(2,1)}, u32[]{:S(2)}) copy-start(bf16[256,1280]{1,0:T(8,128)(2,1)} %copy-done.5) | copy-start | bytes 1966084
  70.5 1.0 %copy-start.2 = (bf16[256,640]{1,0:T(8,128)(2,1)S(1)}, bf16[256,640]{1,0:T(8,128)(2,1)}, u32[]{:S(2)}) copy-start(bf16[256,640]{1,0:T(8,128)(2,1)} %copy-done) | copy-start | bytes 983044
  70.5 1.1 %copy-start.10 = (bf16[256,768]{1,0:T(8,128)(2,1)S(1)}, bf16[256,768]{1,0:T(8,128)(2,1)}, u32[]{:S(2)}) copy-start(bf16[256,768]{1,0:T(8,128)(2,1)} %copy-done.9) | copy-start | bytes 1179652
  70.5 1.4 %copy-start.14 = (f32[1536,128]{1,0:T(8,128)S(1)}, f32[1536,128]{1,0:T(8,128)}, u32[]{:S(2)}) copy-start(f32[1536,128]{1,0:T(8,128)} %copy-done.13) | copy-start | bytes 2359300
  70.5 1.6 %copy-start.16 = (f32[1536,128]{1,0:T(8,128)S(1)}, f32[1536,128]{1,0:T(8,128)}, u32[]{:S(2)}) copy-start(f32[1536,128]{1,0:T(8,128)} %copy-done.15) | copy-start | bytes 2359300
  70.5 1.8 %copy-start.18 = (f32[1536,128]{1,0:T(8,128)S(1)}, f32[1536,128]{1,0:T(8,128)}, u32[]{:S(2)}) copy-start(f32[1536,128]{1,0:T(8,128)} %copy-done.17) | copy-start | bytes 2359300
  70.5 1.9 %copy-start.21 = (bf16[256,768]{1,0:T(8,128)(2,1)S(1)}, bf16[256,768]{1,0:T(8,128)(2,1)}, u32[]{:S(2)}) copy-start(bf16[256,768]{1,0:T(8,128)(2,1)} %copy-done.20) | copy-start | bytes 1179652
  72.4 6.0 %copy-start.12 = (bf16[256,512]{1,0:T(8,128)(2,1)S(1)}, bf16[256,512]{1,0:T(8,128)(2,1)}, u32[]{:S(2)}) copy-start(bf16[256,512]{1,0:T(8,128)(2,1)} %copy-done.11) | copy-start | bytes 786436
  76.4 4.1 %collective-permute-start.11 = (bf16[128,384]{1,0:T(8,128)(2,1)S(1)}, bf16[128,384]{1,0:T(8,128)(2,1)S(1)}, u32[]{:S(2)}, u32[]{:S(2)}) collective-permute-start(bf16[128,384]{1,0:T(8,128)(2,1)S(1)} %get-tuple-element.67), channel_id=1, source_target_pairs={{0,1},{1,0},{2,3},{3,2},{4,5},{5,4},{6,7},{7,6},{8,9},{9,8},{10,11... | collective-permute-start | bytes 294920 | tf_op jit(solution)/shard_map/ppermute | solution.py:448
  76.5 5.7 %collective-permute-start.12 = (bf16[128,384]{1,0:T(8,128)(2,1)S(1)}, bf16[128,384]{1,0:T(8,128)(2,1)S(1)}, u32[]{:S(2)}, u32[]{:S(2)}) collective-permute-start(bf16[128,384]{1,0:T(8,128)(2,1)S(1)} %get-tuple-element.68), channel_id=1, source_target_pairs={{0,2},{1,3},{2,0},{3,1},{4,6},{5,7},{6,4},{7,5},{8,10},{9,11},{10,... | collective-permute-start | bytes 294920 | tf_op jit(solution)/shard_map/ppermute | solution.py:448
  77.2 6.2 %collective-permute-start.13 = (bf16[128,384]{1,0:T(8,128)(2,1)S(1)}, bf16[128,384]{1,0:T(8,128)(2,1)S(1)}, u32[]{:S(2)}, u32[]{:S(2)}) collective-permute-start(bf16[128,384]{1,0:T(8,128)(2,1)S(1)} %get-tuple-element.69), channel_id=1, source_target_pairs={{0,3},{1,2},{2,1},{3,0},{4,7},{5,6},{6,5},{7,4},{8,11},{9,10},{10,... | collective-permute-start | bytes 294920 | tf_op jit(solution)/shard_map/ppermute | solution.py:448
  79.4 4.0 %collective-permute-start.17 = (bf16[128,256]{1,0:T(8,128)(2,1)S(1)}, bf16[128,256]{1,0:T(8,128)(2,1)S(1)}, u32[]{:S(2)}, u32[]{:S(2)}) collective-permute-start(bf16[128,256]{1,0:T(8,128)(2,1)S(1)} %get-tuple-element.80), channel_id=1, source_target_pairs={{0,1},{1,0},{2,3},{3,2},{4,5},{5,4},{6,7},{7,6},{8,9},{9,8},{10,11... | collective-permute-start | bytes 196616 | tf_op jit(solution)/shard_map/ppermute | solution.py:448
  79.8 5.9 %collective-permute-start.18 = (bf16[128,256]{1,0:T(8,128)(2,1)S(1)}, bf16[128,256]{1,0:T(8,128)(2,1)S(1)}, u32[]{:S(2)}, u32[]{:S(2)}) collective-permute-start(bf16[128,256]{1,0:T(8,128)(2,1)S(1)} %get-tuple-element.81), channel_id=1, source_target_pairs={{0,2},{1,3},{2,0},{3,1},{4,6},{5,7},{6,4},{7,5},{8,10},{9,11},{10,... | collective-permute-start | bytes 196616 | tf_op jit(solution)/shard_map/ppermute | solution.py:448
  80.5 5.7 %collective-permute-start.19 = (bf16[128,256]{1,0:T(8,128)(2,1)S(1)}, bf16[128,256]{1,0:T(8,128)(2,1)S(1)}, u32[]{:S(2)}, u32[]{:S(2)}) collective-permute-start(bf16[128,256]{1,0:T(8,128)(2,1)S(1)} %get-tuple-element.82), channel_id=1, source_target_pairs={{0,3},{1,2},{2,1},{3,0},{4,7},{5,6},{6,5},{7,4},{8,11},{9,10},{10,... | collective-permute-start | bytes 196616 | tf_op jit(solution)/shard_map/ppermute | solution.py:448
  85.7 0.8 copy-start.23

commit v12 on v11

--- a/solution.py
+++ b/solution.py
@@ -189,17 +189,18 @@
     return result
 
 
-def near_kernel(first, skip, counts, q_mine, q_other, *refs):
-    tiles, (mixed_out, tops, totals, done), rooms = refs[:-6], refs[-6:-2], refs[-2:]
+def near_kernel(first, counts, queries_of, n_queries, *refs):
+    queries, tiles, (mixed_out, stats, done), rooms = refs[:n_queries], refs[n_queries:-5], refs[-5:-2], refs[-2:]
+    rows = rooms[0].shape[0]
     done[...] = jnp.zeros_like(done)
-    rows = q_mine.shape[0]
 
     def one_head(used, i):
         found = []
-        for q, held in zip((q_mine, q_other), rooms):
+        for half, held in enumerate(rooms):
+            q = queries_of(queries, half, i)
             best = None
             for at, ref in enumerate(used):
-                s = dot_keys(q[:, head_lanes(skip, i)], keys_of(ref, first, i, rows))
+                s = dot_keys(q, keys_of(ref, first, i, rows))
                 held[:, at * rows : (at + 1) * rows] = s
                 part = fold(s, jnp.maximum)
                 best = part if best is None else jnp.maximum(best, part)
@@ -214,8 +215,9 @@
                 total = part if total is None else total + part
             span = pl.ds(pl.multiple_of((2 * i + half) * rows, rows), rows)
             mixed_out[span] = mixed
-            tops[span] = jnp.broadcast_to(top, (rows, HEAD_DIM))
-            totals[span] = jnp.broadcast_to(jnp.sum(total, axis=1, keepdims=True), (rows, HEAD_DIM))
+            half_lanes = (rows, HEAD_DIM // 2)
+            stats[span, : HEAD_DIM // 2] = jnp.broadcast_to(top, half_lanes)
+            stats[span, HEAD_DIM // 2 :] = jnp.broadcast_to(jnp.sum(total, axis=1, keepdims=True), half_lanes)
 
     for wanted, (n_tiles, n_heads) in zip((True, False), counts):
         if n_heads:
@@ -229,10 +231,18 @@
                 lax.fori_loop(0, n_heads, step, 0)
 
 
-def add_far(q, state, slots, i, row, held):
+def own_queries(refs, half, i):
+    return refs[half][:, head_lanes(0, i)]
+
+
+def guest_queries(refs, half, i):
+    return refs[0][:, head_lanes(half * HOME, i)]
+
+
+def add_far(q, state, slots, i, begin, held):
     rows = q.shape[0]
-    span = pl.ds(pl.multiple_of(row, rows), rows)
-    near_top = state[1][span][:, :1]
+    span = slice(begin, begin + rows)
+    near_top = state[1][span, :1]
     top = near_top
     for at, (ref, first, valid) in enumerate(slots):
         s = dot_keys(q, keys_of(ref, first, i, rows))
@@ -248,41 +258,40 @@
         mixed += jnp.dot(w.astype(jnp.bfloat16), values_of(ref, first, i, rows), preferred_element_type=jnp.float32)
         part = fold(w, jnp.add)
         total = part if total is None else total + part
-    total = jnp.sum(total, axis=1, keepdims=True) + state[2][span][:, :1] * shrink
+    total = jnp.sum(total, axis=1, keepdims=True) + state[1][span, HEAD_DIM // 2 : HEAD_DIM // 2 + 1] * shrink
     return (mixed * (1.0 / total)).astype(jnp.bfloat16)
 
 
-def write_pieces(outs, half, lanes, value):
-    rows = outs[0].shape[0]
-    outs[2 * half][:, lanes] = value[:rows]
-    outs[2 * half + 1][:, lanes] = value[rows:]
-
-
-def home_kernel(mask, q_mine, q_other, mixed, tops, totals, r1, r2, r3, *rest):
+def lanes_of(i):
+    return slice(i * HEAD_DIM, (i + 1) * HEAD_DIM)
+
+
+def finish_own(first, queries, state, slots, outs, rooms):
+    rows, piece = queries[0].shape[0], outs[0].shape[0]
+    for i in range(outs[0].shape[1] // HEAD_DIM):
+        for half, q in enumerate(queries):
+            begin = (2 * (first + i) + half) * rows
+            value = add_far(q[:, lanes_of(first + i)], state, slots, i, begin, rooms[2 * i + half])
+            outs[2 * half][:, lanes_of(i)] = value[:piece]
+            outs[2 * half + 1][:, lanes_of(i)] = value[piece:]
+
+
+def home_kernel(mask, q_mine, q_other, mixed, stats, r1, r2, r3, *rest):
     outs, rooms = rest[:4], rest[4:]
     z = lax.axis_index("frame")
     near2 = mask[0, z ^ 2] == 1
-    rows = q_mine.shape[0]
-
-    def body(slots):
-        def step(i, carry):
-            for half, (q, held) in enumerate(zip((q_mine, q_other), rooms)):
-                value = add_far(q[:, head_lanes(0, i)], (mixed, tops, totals), slots, i, (2 * i + half) * rows, held)
-                write_pieces(outs, half, head_lanes(0, i), value)
-            return carry
-
-        lax.fori_loop(0, outs[0].shape[1] // HEAD_DIM, step, 0)
 
     @pl.when(inner_frame())
     def _():
-        body([(r1, 0, near2)])
+        finish_own(0, (q_mine, q_other), (mixed, stats), [(r1, 0, near2)], outs, rooms)
 
     @pl.when(jnp.logical_not(inner_frame()))
     def _():
-        body([(r2, 0, near2), (r3, 0, mask[0, z ^ 3] == 1)])
-
-
-def guest_kernel(first, q, mixed, tops, totals, n1m, n2m, n2o, r1, out, *rooms):
+        slots = [(r2, 0, near2), (r3, 0, mask[0, z ^ 3] == 1)]
+        finish_own(0, (q_mine, q_other), (mixed, stats), slots, outs, rooms)
+
+
+def guest_kernel(q, mixed, stats, n1m, n2m, n2o, r1, out, *rooms):
     rows = r1.shape[0]
     z = lax.axis_index("frame")
 
@@ -294,34 +303,21 @@
         near2 = jnp.where(z == 1, told(n1m, 2), told(n1m, 1)) > 0.5
         near1 = jnp.where(z == 1, told(n1m, 3), told(n1m, 0)) > 0.5
         picked = told(n2m, 4) == (lax.axis_index("head") // 2).astype(jnp.float32)
-        slots = [(n2m, first, near2 & picked), (n2o, first, near2 & jnp.logical_not(picked)), (r1, 0, near1)]
-
-        def step(i, carry):
-            for half, held in enumerate(rooms):
-                span = slice(half * rows, (half + 1) * rows)
-                value = add_far(q[span, head_lanes(0, i)], (mixed, tops, totals), slots, i, (2 * i + half) * rows, held)
-                out[span, head_lanes(0, i)] = value
-            return carry
-
-        lax.fori_loop(0, out.shape[1] // HEAD_DIM, step, 0)
-
-
-def rest_kernel(first, mask, q_mine, q_other, mixed, tops, totals, r1, back, *rest):
+        slots = [(n2m, HOME, near2 & picked), (n2o, HOME, near2 & jnp.logical_not(picked)), (r1, 0, near1)]
+        for i in range(out.shape[1] // HEAD_DIM):
+            for half in range(2):
+                begin = (2 * i + half) * rows
+                value = add_far(guest_queries((q,), half, i), (mixed, stats), slots, i, begin, rooms[2 * i + half])
+                out[half * rows : (half + 1) * rows, lanes_of(i)] = value
+
+
+def rest_kernel(mask, q_mine, q_other, mixed, stats, r1, back, *rest):
     outs, rooms = rest[:4], rest[4:]
     z = lax.axis_index("frame")
-    rows = q_mine.shape[0]
 
     @pl.when(inner_frame())
     def _():
-        def step(i, carry):
-            for half, (q, held) in enumerate(zip((q_mine, q_other), rooms)):
-                slots = [(r1, 0, mask[0, z ^ 2] == 1)]
-                row = (2 * i + half) * rows
-                value = add_far(q[:, head_lanes(first, i)], (mixed, tops, totals), slots, i, row, held)
-                write_pieces(outs, half, head_lanes(0, i), value)
-            return carry
-
-        lax.fori_loop(0, outs[0].shape[1] // HEAD_DIM, step, 0)
+        finish_own(HOME, (q_mine, q_other), (mixed, stats), [(r1, 0, mask[0, z ^ 2] == 1)], outs, rooms)
 
     @pl.when(jnp.logical_not(inner_frame()))
     def _():
@@ -351,8 +347,8 @@
         + [pl.BlockSpec(memory_space=pltpu.VMEM)] * len(arrays),
         out_specs=[pl.BlockSpec(memory_space=pltpu.VMEM)] * len(outs),
         out_shape=[jax.ShapeDtypeStruct(shape, dtype) for shape, dtype in outs],
-        scratch_shapes=[pltpu.VMEM(rooms, jnp.float32)] * 2,
-        compiler_params=pltpu.CompilerParams(vmem_limit_bytes=12 * 1024 * 1024),
+        scratch_shapes=[pltpu.VMEM(rooms[1], jnp.float32)] * rooms[0],
+        compiler_params=pltpu.CompilerParams(vmem_limit_bytes=10 * 1024 * 1024),
         cost_estimate=pl.CostEstimate(
             flops=flops, bytes_accessed=sum(x.size * 2 for x in arrays), transcendentals=flops // (4 * HEAD_DIM)
         ),
@@ -429,6 +425,31 @@
     )(mine, other)
 
 
+def swap_kernel(mine, other, q_mine, q_other, out):
+    cut = HOME * HEAD_DIM
+
+    @pl.when(inner_frame())
+    def _():
+        relayed_kernel([(0, cut)], mine, other, out)
+
+    @pl.when(jnp.logical_not(inner_frame()))
+    def _():
+        count = q_mine.shape[1] - cut
+        out[...] = jnp.zeros_like(out)
+        out[:, :count] = q_mine[:, cut:]
+        out[:, cut : cut + count] = q_other[:, cut:]
+
+
+def swapped(mine, other, q_mine, q_other):
+    return pl.pallas_call(
+        swap_kernel,
+        in_specs=[pl.BlockSpec(memory_space=pltpu.VMEM)] * 4,
+        out_specs=pl.BlockSpec(memory_space=pltpu.VMEM),
+        out_shape=jax.ShapeDtypeStruct((other.shape[0], 2 * HOME * HEAD_DIM), other.dtype),
+        compiler_params=pltpu.CompilerParams(vmem_limit_bytes=4 * 1024 * 1024),
+    )(mine, other, q_mine, q_other)
+
+
 def four_frames(queries, keys, values, pair_mask, tile_offset):
     h = lax.axis_index("head")
     rows, features = queries.shape
@@ -482,67 +503,60 @@
     tile = 2 * rows
     cut = HOME * HEAD_DIM
     guests = heads - HOME
-    q_guest = along(below(q_mine[:, cut:], q_other[:, cut:]), OUTER)
     r1_home, r1_rest = after(relayed(n1m, n1o, [(0, cut), (cut, width)]), n2m)
     r1_home = across(r1_home)
-    (r2,) = relayed(n2m, n2o, [(0, cut)])
-    r1_rest = across(after(r1_rest, r2))
-    r2 = along(r2, OUTER)
+    swap = along(swapped(n2m, n2o, q_mine, q_other), OUTER)
+    r1_rest = across(after(r1_rest, n2o))
 
     def state(count):
-        return [((count * 2 * tile, HEAD_DIM), jnp.float32)] * 3 + [((8, 128), jnp.float32)]
+        return [((count * 2 * tile, HEAD_DIM), jnp.float32)] * 2 + [((8, 128), jnp.float32)]
 
     def flops(chunks, tiles):
         return 4 * chunks * tiles * tile * tile * HEAD_DIM
 
     bf16 = jnp.bfloat16
     q = [q_mine, q_other]
-    around = [mine, other, n1m, n1o, n2m, n2o]
     *near, done = run_kernel(
-        functools.partial(near_kernel, 0, 0, ((6, HOME), (4, HOME))),
+        functools.partial(near_kernel, 0, ((6, heads), (4, HOME)), own_queries, 2),
         None,
-        [*q, *around],
-        state(HOME),
-        (tile, 6 * tile),
-        flops(2 * HOME, 6),
-    )
-    r3 = along(after(passed(r1_home, done), r2), OUTER)
-    q_halves = [q_guest[:tile], q_guest[tile:]]
+        [*q, mine, other, n1m, n1o, n2m, n2o],
+        state(heads),
+        (2, (tile, 6 * tile)),
+        flops(2 * heads, 6),
+    )
+    r3 = along(after(passed(r1_home, done), swap), OUTER)
     *guest_near, _ = run_kernel(
-        functools.partial(near_kernel, HOME, 0, ((4, guests), (0, 0))),
+        functools.partial(near_kernel, HOME, ((4, guests), (0, 0)), guest_queries, 1),
         None,
-        [*q_halves, mine, other, n1m, n1o],
+        [swap, mine, other, n1m, n1o],
         state(guests),
-        (tile, 4 * tile),
+        (2, (tile, 4 * tile)),
         flops(2 * guests, 4),
     )
     (back,) = run_kernel(
-        functools.partial(guest_kernel, HOME),
+        guest_kernel,
         None,
-        [q_guest, *guest_near, n1m, n2m, n2o, r1_rest],
+        [swap, *guest_near, n1m, n2m, n2o, r1_rest],
         [((2 * tile, width - cut), bf16)],
-        (tile, 3 * tile),
+        (2 * guests, (tile, 3 * tile)),
         flops(2 * guests, 3),
     )
     back = along(back, OUTER)
     out = run_kernel(
-        home_kernel, pair_mask, [*q, *near, r1_home, r2, r3], [((rows, cut), bf16)] * 4, (tile, 2 * tile), flops(2 * HOME, 2)
+        home_kernel,
+        pair_mask,
+        [*q, *near, r1_home, swap, r3],
+        [((rows, cut), bf16)] * 4,
+        (2 * HOME, (tile, 2 * tile)),
+        flops(2 * HOME, 2),
     )
     pieces = [(to_head(out[d], d) if d else out[0], d, 0) for d in range(4)]
-    *rest_near, _ = run_kernel(
-        functools.partial(near_kernel, HOME, HOME, ((6, guests), (0, 0))),
-        None,
-        [*q, *around],
-        state(guests),
-        (tile, 6 * tile),
-        flops(2 * guests, 6),
-    )
     out = run_kernel(
-        functools.partial(rest_kernel, HOME),
+        rest_kernel,
         pair_mask,
-        [*q, *rest_near, r1_rest, after(back, out[1])],
+        [*q, *near, r1_rest, after(back, out[1])],
         [((rows, width - cut), bf16)] * 4,
-        (tile, tile),
+        (2 * guests, (tile, tile)),
         flops(2 * guests, 1),
     )
     pieces += [(to_head(out[d], d) if d else out[0], d, cut) for d in range(4)]

time: 87.5 us -> 82.9 us (0.947); the launches traced: 87.2 us -> 81.4 us
  local copies, waits for them, and re-layouts: 9.68 us -> 4.8 us
    unnamed x48 -> x24, local copies, waits for them, and re-layouts: 7.29 us -> 2.43 us
    pallas_call x6 -> x5, Pallas kernels: 9.96 us -> 9.28 us  [run_kernel(): pl.pallas_call(kernel, in_specs=[pl.BlockSpec(memory_space=pltpu.SMEM)] *...]
    ppermute x6 -> x5, starting transfers between devices: 15 us -> 15.6 us  [along(): return lax.ppermute(array, 'frame', pairs)]
    ppermute x6 -> x5, waiting for transfers between devices: 22.1 us -> 21.5 us  [along(): return lax.ppermute(array, 'frame', pairs)]
  transfers between devices with their start and end apart: 20 -> 19, of which waited for: 10 -> 9; matrix products, arithmetic and copies ran while one was open for 0% -> 0% of each run, Pallas kernels for 14% -> 14%
where the time goes in v12:
time: 82.9 us; the launch traced here: 81.4 us
  waiting for transfers between devices  39.5 us (48%)
  starting transfers between devices  24.9 us (30%)
  Pallas kernels  11 us (13%)
  local copies, waits for them, and re-layouts  4.8 us (6%)
  between operations  0.98 us (1%)
    ppermute x5, waiting for transfers between devices, along(): return lax.ppermute(array, 'frame', pairs)  21.5 us
    ppermute x10, waiting for transfers between devices, to_head(): return lax.ppermute(array, 'head', [(i, i ^ d) for i in range(4)])  18 us
    ppermute x5, starting transfers between devices, along(): return lax.ppermute(array, 'frame', pairs)  15.6 us
    pallas_call x5, Pallas kernels, run_kernel(): pl.pallas_call(kernel, in_specs=[pl.BlockSpec(memory_space=pltpu.SMEM)] *...  9.28 us
    ppermute x10, starting transfers between devices, to_head(): return lax.ppermute(array, 'head', [(i, i ^ d) for i in range(4)])  8.99 us
    unnamed x24, local copies, waits for them, and re-layouts  2.43 us
  transfers between devices with their start and end apart: 19, of which 9 were waited for; matrix products, arithmetic and copies ran while one was open for 0% of the time, Pallas kernels for 14%

profile of v12, /device:TPU:0, one launch (start us, length us, event | category | flops | bytes accessed | tf_op | source)
XLA Modules:
  0.0 81.4 jit_solution(16799027886832561861)
XLA Ops:
  0.0 1.5 %constant_dynamic-slice_fusion = (bf16[128,640]{1,0:T(8,128)(2,1)S(1)}, bf16[128,640]{1,0:T(8,128)(2,1)S(1)}, bf16[128,640]{1,0:T(8,128)(2,1)S(1)}, bf16[128,640...) fusion(bf16[128,2560]{1,0:T(8,128)(2,1)} %refs_2_.1, ...), kind=kLoop, calls=%fused_computation.13 | loop fusion | bytes 2621456 | tf_op jit(solution)/shard_map/dynamic_slice | solution.py:460
  1.5 0.1 pad_maximum_fusion.1
  1.6 0.0 copy-start.3
  1.6 0.0 copy-start.4
  1.6 0.0 copy-start.9
  1.6 0.0 copy-start.10
  1.6 0.5 collective-permute-start
  2.1 1.7 %collective-permute-done = bf16[128,2560]{1,0:T(8,128)(2,1)S(1)} collective-permute-done((bf16[128,2560]{1,0:T(8,128)(2,1)S(1)}, bf16[128,2560]{1,0:T(8,128)(2,1)S(1)}, u32[]{:S(2)}, u32[]{:S(2)}) %collective-permute-start) | collective-permute-done | bytes 655392 | tf_op jit(solution)/shard_map/ppermute | solution.py:469
  4.0 2.9 %collective-permute-start.2 = (bf16[256,1280]{1,0:T(8,128)(2,1)S(1)}, bf16[256,1280]{1,0:T(8,128)(2,1)S(1)}, u32[]{:S(2)}, u32[]{:S(2)}) collective-permute-start(bf16[256,1280]{1,0:T(8,128)(2,1)S(1)} %pad_maximum_fusion.2), channel_id=1, source_target_pairs={{0,2},{1,3},{2,0},{3,1},{4,6},{5,7},{6,4},{7,5},{8,10},{9,11},{10,... | collective-permute-start | bytes 1966088 | tf_op jit(solution)/shard_map/ppermute | solution.py:469
  7.6 0.7 shard_map.55
  8.3 0.1 collective-permute-start.1
  8.3 0.1 pad_maximum_fusion.refs_2_.refs_1_
  8.4 1.6 %collective-permute-start.4 = (bf16[272,1280]{1,0:T(8,128)(2,1)S(1)}, bf16[272,1280]{1,0:T(8,128)(2,1)S(1)}, u32[]{:S(2)}, u32[]{:S(2)}) collective-permute-start(bf16[272,1280]{1,0:T(8,128)(2,1)S(1)} %pad_maximum_fusion.refs_2_.refs_1_), channel_id=1, source_target_pairs={{0,4},{4,0},{8,12},{12,8},{1,5},{5,1},{9,13},{13,9},{2,6},{6,2},{1... | collective-permute-start | bytes 2088968 | tf_op jit(solution)/shard_map/ppermute | solution.py:472
  10.0 0.2 collective-permute-start.6
  10.3 11.7 %collective-permute-done.2.refs_3_.refs_2_ = bf16[256,1280]{1,0:T(8,128)(2,1)S(1)} collective-permute-done((bf16[256,1280]{1,0:T(8,128)(2,1)S(1)}, bf16[256,1280]{1,0:T(8,128)(2,1)S(1)}, u32[]{:S(2)}, u32[]{:S(2)}) %collective-permute-start.2) | collective-permute-done | bytes 655392 | tf_op jit(solution)/shard_map/ppermute | solution.py:469
  21.9 3.4 %collective-permute-start.5 = (bf16[256,1280]{1,0:T(8,128)(2,1)S(1)}, bf16[256,1280]{1,0:T(8,128)(2,1)S(1)}, u32[]{:S(2)}, u32[]{:S(2)}) collective-permute-start(bf16[256,1280]{1,0:T(8,128)(2,1)S(1)} %collective-permute-done.2.refs_3_.refs_2_), channel_id=1, source_target_pairs={{0,4},{4,0},{8,12},{12,8},{1,5},{5,1},{9,13},{13,9},{2,6},{6,2},{1... | collective-permute-start | bytes 1966088 | tf_op jit(solution)/shard_map/ppermute | solution.py:472
  25.4 1.6 %collective-permute-start.3 = (bf16[256,640]{1,0:T(8,128)(2,1)S(1)}, bf16[256,640]{1,0:T(8,128)(2,1)S(1)}, u32[]{:S(2)}, u32[]{:S(2)}) collective-permute-start(bf16[256,640]{1,0:T(8,128)(2,1)S(1)} %pad_maximum_fusion.4), channel_id=1, source_target_pairs={{0,2},{1,3},{2,0},{3,1},{4,6},{5,7},{6,4},{7,5},{8,10},{9,11},{10,... | collective-permute-start | bytes 983048 | tf_op jit(solution)/shard_map/ppermute | solution.py:469
  27.0 13.5 %collective-permute-done.5.refs_5_.other.refs_4_ = bf16[256,1280]{1,0:T(8,128)(2,1)S(1)} collective-permute-done((bf16[256,1280]{1,0:T(8,128)(2,1)S(1)}, bf16[256,1280]{1,0:T(8,128)(2,1)S(1)}, u32[]{:S(2)}, u32[]{:S(2)}) %collective-permute-start.5) | collective-permute-done | bytes 655392 | tf_op jit(solution)/shard_map/ppermute | solution.py:472
  40.5 0.2 shard_map.57
  40.7 0.1 collective-permute-start.8
  40.8 0.1 shard_map.58
  40.9 3.3 %collective-permute-start.9 = (bf16[256,768]{1,0:T(8,128)(2,1)S(1)}, bf16[256,768]{1,0:T(8,128)(2,1)S(1)}, u32[]{:S(2)}, u32[]{:S(2)}) collective-permute-start(bf16[256,768]{1,0:T(8,128)(2,1)S(1)} %shard_map.58), channel_id=1, source_target_pairs={{0,4},{4,0},{8,12},{12,8},{1,5},{5,1},{9,13},{13,9},{2,6},{6,2},{1... | collective-permute-start | bytes 1179656 | tf_op jit(solution)/shard_map/ppermute | solution.py:472
  44.2 2.9 %shard_map.56 = (f32[2560,128]{1,0:T(8,128)S(1)}, f32[2560,128]{1,0:T(8,128)S(1)}, f32[8,128]{1,0:T(8,128)S(1)}) custom-call(bf16[256,640]{1,0:T(8,128)(2,1)S(1)} %pad_maximum_fusion.3.refs_0_.q_mine, bf16[256,640]{1,0:T(8,128)(2,1)S(1)} %collective-permute-done.3.refs_1_.q_other, bf16[272,1280]{1,0:T(8,128)(2,1)S(1)} %pad_maximum_fusion.refs_2_.refs_1_, ...), custom_call_target="tpu_custom_call" | custom-call | flops 2013265920 | bytes 4710400 | tf_op jit(solution)/shard_map/pallas_call | solution.py:344
  47.1 0.0 copy-start.5
  47.1 0.8 %shard_map.59 = bf16[256,768]{1,0:T(8,128)(2,1)} custom-call(f32[8,128]{1,0:T(8,128)S(1)} %get-tuple-element.58.done, bf16[256,768]{1,0:T(8,128)(2,1)S(1)} %collective-permute-done.8.x.r1), custom_call_target="tpu_custom_call" | custom-call | tf_op jit(solution)/shard_map/pallas_call | solution.py:333
  48.0 4.9 %collective-permute-done.9.r2.refs_0_.q = bf16[256,768]{1,0:T(8,128)(2,1)S(1)} collective-permute-done((bf16[256,768]{1,0:T(8,128)(2,1)S(1)}, bf16[256,768]{1,0:T(8,128)(2,1)S(1)}, u32[]{:S(2)}, u32[]{:S(2)}) %collective-permute-start.9) | collective-permute-done | bytes 393248 | tf_op jit(solution)/shard_map/ppermute | solution.py:472
  52.9 2.3 %collective-permute-start.10 = (bf16[256,768]{1,0:T(8,128)(2,1)}, bf16[256,768]{1,0:T(8,128)(2,1)}, u32[]{:S(2)}, u32[]{:S(2)}) collective-permute-start(bf16[256,768]{1,0:T(8,128)(2,1)} %shard_map.59), channel_id=1, source_target_pairs={{0,4},{4,0},{8,12},{12,8},{1,5},{5,1},{9,13},{13,9},{2,6},{6,2},{1... | collective-permute-start | bytes 1179656 | tf_op jit(solution)/shard_map/ppermute | solution.py:472
  55.2 0.6 shard_map.61
  55.8 0.8 shard_map.62
  56.6 0.0 copy-done.7
  56.6 5.0 %collective-permute-start.15 = (bf16[512,256]{1,0:T(8,128)(2,1)}, bf16[512,256]{1,0:T(8,128)(2,1)}, u32[]{:S(2)}, u32[]{:S(2)}) collective-permute-start(bf16[512,256]{1,0:T(8,128)(2,1)} %shard_map.62), channel_id=1, source_target_pairs={{0,4},{4,0},{8,12},{12,8},{1,5},{5,1},{9,13},{13,9},{2,6},{6,2},{1... | collective-permute-start | bytes 786440 | tf_op jit(solution)/shard_map/ppermute | solution.py:472
  61.6 3.1 %collective-permute-done.10.r3 = bf16[256,768]{1,0:T(8,128)(2,1)} collective-permute-done((bf16[256,768]{1,0:T(8,128)(2,1)}, bf16[256,768]{1,0:T(8,128)(2,1)}, u32[]{:S(2)}, u32[]{:S(2)}) %collective-permute-start.10) | collective-permute-done | bytes 393248 | tf_op jit(solution)/shard_map/ppermute | solution.py:472
  64.7 1.0 %copy-done.1 = bf16[256,640]{1,0:T(8,128)(2,1)S(1)} copy-done((bf16[256,640]{1,0:T(8,128)(2,1)S(1)}, bf16[256,640]{1,0:T(8,128)(2,1)}, u32[]{:S(2)}) %copy-start.1) | copy-done | bytes 327704
  65.6 1.0 %copy-done.6 = bf16[256,768]{1,0:T(8,128)(2,1)S(1)} copy-done((bf16[256,768]{1,0:T(8,128)(2,1)S(1)}, bf16[256,768]{1,0:T(8,128)(2,1)}, u32[]{:S(2)}) %copy-start.6) | copy-done | bytes 393240
  66.6 4.0 %shard_map.60 = (bf16[128,384]{1,0:T(8,128)(2,1)S(1)}, bf16[128,384]{1,0:T(8,128)(2,1)S(1)}, bf16[128,384]{1,0:T(8,128)(2,1)S(1)}, bf16[128,384]{1,0:T(8,128)(2,1)S(1)}) custom-call(s32[1,4]{1,0:T(1,128)S(1)} %copy-done.10, bf16[256,640]{1,0:T(8,128)(2,1)S(1)} %pad_maximum_fusion.3.refs_0_.q_mine, bf16[256,640]{1,0:T(8,128)(2,1)S(1)} %copy-done.1, ...), custom_call_target="tpu_custom_call" | custom-call | flops 402653184 | bytes 3145728 | tf_op jit(solution)/shard_map/pallas_call | solution.py:344
  70.7 0.1 collective-permute-start.11
  70.8 0.7 collective-permute-start.12
  71.5 1.1 %collective-permute-start.13 = (bf16[128,384]{1,0:T(8,128)(2,1)S(1)}, bf16[128,384]{1,0:T(8,128)(2,1)S(1)}, u32[]{:S(2)}, u32[]{:S(2)}) collective-permute-start(bf16[128,384]{1,0:T(8,128)(2,1)S(1)} %get-tuple-element.63), channel_id=1, source_target_pairs={{0,3},{1,2},{2,1},{3,0},{4,7},{5,6},{6,5},{7,4},{8,11},{9,10},{10,... | collective-permute-start | bytes 294920 | tf_op jit(solution)/shard_map/ppermute | solution.py:469
  72.6 1.0 %shard_map.63 = (bf16[128,256]{1,0:T(8,128)(2,1)S(1)}, bf16[128,256]{1,0:T(8,128)(2,1)S(1)}, bf16[128,256]{1,0:T(8,128)(2,1)S(1)}, bf16[128,256]{1,0:T(8,128)(2,1)S(1)}) custom-call(s32[1,4]{1,0:T(1,128)S(1)} %copy-done.10, bf16[256,640]{1,0:T(8,128)(2,1)S(1)} %pad_maximum_fusion.3.refs_0_.q_mine, bf16[256,640]{1,0:T(8,128)(2,1)S(1)} %copy-done.2, ...), custom_call_target="tpu_custom_call" | custom-call | flops 134217728 | bytes 2490368 | tf_op jit(solution)/shard_map/pallas_call | solution.py:344
  73.6 0.4 collective-permute-start.16
  74.0 0.7 collective-permute-start.17
  74.8 0.9 %collective-permute-start.18 = (bf16[128,256]{1,0:T(8,128)(2,1)S(1)}, bf16[128,256]{1,0:T(8,128)(2,1)S(1)}, u32[]{:S(2)}, u32[]{:S(2)}) collective-permute-start(bf16[128,256]{1,0:T(8,128)(2,1)S(1)} %get-tuple-element.72), channel_id=1, source_target_pairs={{0,3},{1,2},{2,1},{3,0},{4,7},{5,6},{6,5},{7,4},{8,11},{9,10},{10,... | collective-permute-start | bytes 196616 | tf_op jit(solution)/shard_map/ppermute | solution.py:469
  75.7 0.7 collective-permute-done.12
  76.5 1.2 %collective-permute-done.13 = bf16[128,384]{1,0:T(8,128)(2,1)S(1)} collective-permute-done((bf16[128,384]{1,0:T(8,128)(2,1)S(1)}, bf16[128,384]{1,0:T(8,128)(2,1)S(1)}, u32[]{:S(2)}, u32[]{:S(2)}) %collective-permute-start.13) | collective-permute-done | bytes 98336 | tf_op jit(solution)/shard_map/ppermute | solution.py:469
  77.7 2.3 %collective-permute-done.17 = bf16[128,256]{1,0:T(8,128)(2,1)S(1)} collective-permute-done((bf16[128,256]{1,0:T(8,128)(2,1)S(1)}, bf16[128,256]{1,0:T(8,128)(2,1)S(1)}, u32[]{:S(2)}, u32[]{:S(2)}) %collective-permute-start.17) | collective-permute-done | bytes 65568 | tf_op jit(solution)/shard_map/ppermute | solution.py:469
  80.0 0.5 collective-permute-done.18
  80.4 0.4 copy-done.11
  80.8 0.6 constant_dynamic-update-slice_fusion
  (40 shorter events, 0.4 us)
Async XLA Ops:
  1.6 6.0 %copy-start.3 = (bf16[128,2560]{1,0:T(8,128)(2,1)S(1)}, bf16[128,2560]{1,0:T(8,128)(2,1)}, u32[]{:S(2)}) copy-start(bf16[128,2560]{1,0:T(8,128)(2,1)} %refs_1_.1) | copy-start | bytes 1966084
  1.6 6.0 %copy-start.4 = (bf16[128,2560]{1,0:T(8,128)(2,1)S(1)}, bf16[128,2560]{1,0:T(8,128)(2,1)}, u32[]{:S(2)}) copy-start(bf16[128,2560]{1,0:T(8,128)(2,1)} %refs_2_.1) | copy-start | bytes 1966084
  1.6 6.0 %copy-start.9 = (bf16[128,2560]{1,0:T(8,128)(2,1)S(1)}, bf16[128,2560]{1,0:T(8,128)(2,1)}, u32[]{:S(2)}) copy-start(bf16[128,2560]{1,0:T(8,128)(2,1)} %refs_0_.1) | copy-start | bytes 1966084
  1.6 6.0 %copy-start.10 = (s32[1,4]{1,0:T(1,128)S(1)}, s32[1,4]{1,0:T(1,128)}, u32[]{:S(2)}) copy-start(s32[1,4]{1,0:T(1,128)} %mask.5) | copy-start | bytes 52
  1.6 2.2 %collective-permute-start = (bf16[128,2560]{1,0:T(8,128)(2,1)S(1)}, bf16[128,2560]{1,0:T(8,128)(2,1)S(1)}, u32[]{:S(2)}, u32[]{:S(2)}) collective-permute-start(bf16[128,2560]{1,0:T(8,128)(2,1)S(1)} %pad_maximum_fusion.1), channel_id=1, source_target_pairs={{0,1},{1,0},{2,3},{3,2},{4,5},{5,4},{6,7},{7,6},{8,9},{9,8},{10,11... | collective-permute-start | bytes 1966088 | tf_op jit(solution)/shard_map/ppermute | solution.py:469
  4.0 18.0 %collective-permute-start.2 = (bf16[256,1280]{1,0:T(8,128)(2,1)S(1)}, bf16[256,1280]{1,0:T(8,128)(2,1)S(1)}, u32[]{:S(2)}, u32[]{:S(2)}) collective-permute-start(bf16[256,1280]{1,0:T(8,128)(2,1)S(1)} %pad_maximum_fusion.2), channel_id=1, source_target_pairs={{0,2},{1,3},{2,0},{3,1},{4,6},{5,7},{6,4},{7,5},{8,10},{9,11},{10,... | collective-permute-start | bytes 1966088 | tf_op jit(solution)/shard_map/ppermute | solution.py:469
  8.3 17.1 %collective-permute-start.1 = (bf16[128,1280]{1,0:T(8,128)(2,1)S(1)}, bf16[128,1280]{1,0:T(8,128)(2,1)S(1)}, u32[]{:S(2)}, u32[]{:S(2)}) collective-permute-start(bf16[128,1280]{1,0:T(8,128)(2,1)S(1)} %get-tuple-element.45), channel_id=1, source_target_pairs={{0,1},{1,0},{2,3},{3,2},{4,5},{5,4},{6,7},{7,6},{8,9},{9,8},{10,11... | collective-permute-start | bytes 983048 | tf_op jit(solution)/shard_map/ppermute | solution.py:469
  8.4 18.6 %collective-permute-start.4 = (bf16[272,1280]{1,0:T(8,128)(2,1)S(1)}, bf16[272,1280]{1,0:T(8,128)(2,1)S(1)}, u32[]{:S(2)}, u32[]{:S(2)}) collective-permute-start(bf16[272,1280]{1,0:T(8,128)(2,1)S(1)} %pad_maximum_fusion.refs_2_.refs_1_), channel_id=1, source_target_pairs={{0,4},{4,0},{8,12},{12,8},{1,5},{5,1},{9,13},{13,9},{2,6},{6,2},{1... | collective-permute-start | bytes 2088968 | tf_op jit(solution)/shard_map/ppermute | solution.py:472
  10.0 30.7 %collective-permute-start.6 = (bf16[272,1280]{1,0:T(8,128)(2,1)S(1)}, bf16[272,1280]{1,0:T(8,128)(2,1)S(1)}, u32[]{:S(2)}, u32[]{:S(2)}) collective-permute-start(bf16[272,1280]{1,0:T(8,128)(2,1)S(1)} %pad_maximum_fusion.refs_2_.refs_1_), channel_id=1, source_target_pairs={{0,1},{1,0},{2,3},{3,2},{4,8},{5,9},{6,10},{7,11},{8,4},{9,5},{10,... | collective-permute-start | bytes 2088968 | tf_op jit(solution)/shard_map/ppermute | solution.py:476
  21.9 18.9 %collective-permute-start.7 = (bf16[256,1280]{1,0:T(8,128)(2,1)S(1)}, bf16[256,1280]{1,0:T(8,128)(2,1)S(1)}, u32[]{:S(2)}, u32[]{:S(2)}) collective-permute-start(bf16[256,1280]{1,0:T(8,128)(2,1)S(1)} %collective-permute-done.2.refs_3_.refs_2_), channel_id=1, source_target_pairs={{0,1},{1,0},{2,3},{3,2},{4,8},{5,9},{6,10},{7,11},{8,4},{9,5},{10,... | collective-permute-start | bytes 1966088 | tf_op jit(solution)/shard_map/ppermute | solution.py:476
  21.9 18.6 %collective-permute-start.5 = (bf16[256,1280]{1,0:T(8,128)(2,1)S(1)}, bf16[256,1280]{1,0:T(8,128)(2,1)S(1)}, u32[]{:S(2)}, u32[]{:S(2)}) collective-permute-start(bf16[256,1280]{1,0:T(8,128)(2,1)S(1)} %collective-permute-done.2.refs_3_.refs_2_), channel_id=1, source_target_pairs={{0,4},{4,0},{8,12},{12,8},{1,5},{5,1},{9,13},{13,9},{2,6},{6,2},{1... | collective-permute-start | bytes 1966088 | tf_op jit(solution)/shard_map/ppermute | solution.py:472
  25.4 15.4 %collective-permute-start.3 = (bf16[256,640]{1,0:T(8,128)(2,1)S(1)}, bf16[256,640]{1,0:T(8,128)(2,1)S(1)}, u32[]{:S(2)}, u32[]{:S(2)}) collective-permute-start(bf16[256,640]{1,0:T(8,128)(2,1)S(1)} %pad_maximum_fusion.4), channel_id=1, source_target_pairs={{0,2},{1,3},{2,0},{3,1},{4,6},{5,7},{6,4},{7,5},{8,10},{9,11},{10,... | collective-permute-start | bytes 983048 | tf_op jit(solution)/shard_map/ppermute | solution.py:469
  40.7 6.4 %collective-permute-start.8 = (bf16[256,768]{1,0:T(8,128)(2,1)S(1)}, bf16[256,768]{1,0:T(8,128)(2,1)S(1)}, u32[]{:S(2)}, u32[]{:S(2)}) collective-permute-start(bf16[256,768]{1,0:T(8,128)(2,1)S(1)} %get-tuple-element.57), channel_id=1, source_target_pairs={{0,1},{1,0},{2,3},{3,2},{4,8},{5,9},{6,10},{7,11},{8,4},{9,5},{10,... | collective-permute-start | bytes 1179656 | tf_op jit(solution)/shard_map/ppermute | solution.py:476
  40.8 6.3 %copy-start = (bf16[256,640]{1,0:T(8,128)(2,1)}, bf16[256,640]{1,0:T(8,128)(2,1)S(1)}, u32[]{:S(2)}) copy-start(bf16[256,640]{1,0:T(8,128)(2,1)S(1)} %collective-permute-done.3.refs_1_.q_other) | copy-start | bytes 983044
  40.9 12.0 %collective-permute-start.9 = (bf16[256,768]{1,0:T(8,128)(2,1)S(1)}, bf16[256,768]{1,0:T(8,128)(2,1)S(1)}, u32[]{:S(2)}, u32[]{:S(2)}) collective-permute-start(bf16[256,768]{1,0:T(8,128)(2,1)S(1)} %shard_map.58), channel_id=1, source_target_pairs={{0,4},{4,0},{8,12},{12,8},{1,5},{5,1},{9,13},{13,9},{2,6},{6,2},{1... | collective-permute-start | bytes 1179656 | tf_op jit(solution)/shard_map/ppermute | solution.py:472
  44.2 11.6 %collective-permute-start.14 = (bf16[256,512]{1,0:T(8,128)(2,1)S(1)}, bf16[256,512]{1,0:T(8,128)(2,1)S(1)}, u32[]{:S(2)}, u32[]{:S(2)}) collective-permute-start(bf16[256,512]{1,0:T(8,128)(2,1)S(1)} %get-tuple-element.65), channel_id=1, source_target_pairs={{0,1},{1,0},{2,3},{3,2},{4,8},{5,9},{6,10},{7,11},{8,4},{9,5},{10,... | collective-permute-start | bytes 786440 | tf_op jit(solution)/shard_map/ppermute | solution.py:476
  47.1 8.7 %copy-start.5 = (bf16[256,768]{1,0:T(8,128)(2,1)}, bf16[256,768]{1,0:T(8,128)(2,1)S(1)}, u32[]{:S(2)}) copy-start(bf16[256,768]{1,0:T(8,128)(2,1)S(1)} %collective-permute-done.8.x.r1) | copy-start | bytes 1179652
  52.9 11.8 %collective-permute-start.10 = (bf16[256,768]{1,0:T(8,128)(2,1)}, bf16[256,768]{1,0:T(8,128)(2,1)}, u32[]{:S(2)}, u32[]{:S(2)}) collective-permute-start(bf16[256,768]{1,0:T(8,128)(2,1)} %shard_map.59), channel_id=1, source_target_pairs={{0,4},{4,0},{8,12},{12,8},{1,5},{5,1},{9,13},{13,9},{2,6},{6,2},{1... | collective-permute-start | bytes 1179656 | tf_op jit(solution)/shard_map/ppermute | solution.py:472
  55.8 0.8 copy-start.7
  56.6 14.1 %collective-permute-start.15 = (bf16[512,256]{1,0:T(8,128)(2,1)}, bf16[512,256]{1,0:T(8,128)(2,1)}, u32[]{:S(2)}, u32[]{:S(2)}) collective-permute-start(bf16[512,256]{1,0:T(8,128)(2,1)} %shard_map.62), channel_id=1, source_target_pairs={{0,4},{4,0},{8,12},{12,8},{1,5},{5,1},{9,13},{13,9},{2,6},{6,2},{1... | collective-permute-start | bytes 786440 | tf_op jit(solution)/shard_map/ppermute | solution.py:472
  64.7 1.0 %copy-start.1 = (bf16[256,640]{1,0:T(8,128)(2,1)S(1)}, bf16[256,640]{1,0:T(8,128)(2,1)}, u32[]{:S(2)}) copy-start(bf16[256,640]{1,0:T(8,128)(2,1)} %copy-done) | copy-start | bytes 983044
  65.6 1.0 %copy-start.6 = (bf16[256,768]{1,0:T(8,128)(2,1)S(1)}, bf16[256,768]{1,0:T(8,128)(2,1)}, u32[]{:S(2)}) copy-start(bf16[256,768]{1,0:T(8,128)(2,1)} %copy-done.5) | copy-start | bytes 1179652
  66.6 6.0 %copy-start.2 = (bf16[256,640]{1,0:T(8,128)(2,1)S(1)}, bf16[256,640]{1,0:T(8,128)(2,1)}, u32[]{:S(2)}) copy-start(bf16[256,640]{1,0:T(8,128)(2,1)} %copy-done) | copy-start | bytes 983044
  66.6 6.0 %copy-start.8 = (bf16[256,512]{1,0:T(8,128)(2,1)S(1)}, bf16[256,512]{1,0:T(8,128)(2,1)}, u32[]{:S(2)}) copy-start(bf16[256,512]{1,0:T(8,128)(2,1)} %copy-done.7) | copy-start | bytes 786436
  70.7 4.1 %collective-permute-start.11 = (bf16[128,384]{1,0:T(8,128)(2,1)S(1)}, bf16[128,384]{1,0:T(8,128)(2,1)S(1)}, u32[]{:S(2)}, u32[]{:S(2)}) collective-permute-start(bf16[128,384]{1,0:T(8,128)(2,1)S(1)} %get-tuple-element.61), channel_id=1, source_target_pairs={{0,1},{1,0},{2,3},{3,2},{4,5},{5,4},{6,7},{7,6},{8,9},{9,8},{10,11... | collective-permute-start | bytes 294920 | tf_op jit(solution)/shard_map/ppermute | solution.py:469
  70.8 5.7 %collective-permute-start.12 = (bf16[128,384]{1,0:T(8,128)(2,1)S(1)}, bf16[128,384]{1,0:T(8,128)(2,1)S(1)}, u32[]{:S(2)}, u32[]{:S(2)}) collective-permute-start(bf16[128,384]{1,0:T(8,128)(2,1)S(1)} %get-tuple-element.62), channel_id=1, source_target_pairs={{0,2},{1,3},{2,0},{3,1},{4,6},{5,7},{6,4},{7,5},{8,10},{9,11},{10,... | collective-permute-start | bytes 294920 | tf_op jit(solution)/shard_map/ppermute | solution.py:469
  71.5 6.1 %collective-permute-start.13 = (bf16[128,384]{1,0:T(8,128)(2,1)S(1)}, bf16[128,384]{1,0:T(8,128)(2,1)S(1)}, u32[]{:S(2)}, u32[]{:S(2)}) collective-permute-start(bf16[128,384]{1,0:T(8,128)(2,1)S(1)} %get-tuple-element.63), channel_id=1, source_target_pairs={{0,3},{1,2},{2,1},{3,0},{4,7},{5,6},{6,5},{7,4},{8,11},{9,10},{10,... | collective-permute-start | bytes 294920 | tf_op jit(solution)/shard_map/ppermute | solution.py:469
  73.6 4.0 %collective-permute-start.16 = (bf16[128,256]{1,0:T(8,128)(2,1)S(1)}, bf16[128,256]{1,0:T(8,128)(2,1)S(1)}, u32[]{:S(2)}, u32[]{:S(2)}) collective-permute-start(bf16[128,256]{1,0:T(8,128)(2,1)S(1)} %get-tuple-element.70), channel_id=1, source_target_pairs={{0,1},{1,0},{2,3},{3,2},{4,5},{5,4},{6,7},{7,6},{8,9},{9,8},{10,11... | collective-permute-start | bytes 196616 | tf_op jit(solution)/shard_map/ppermute | solution.py:469
  74.0 5.9 %collective-permute-start.17 = (bf16[128,256]{1,0:T(8,128)(2,1)S(1)}, bf16[128,256]{1,0:T(8,128)(2,1)S(1)}, u32[]{:S(2)}, u32[]{:S(2)}) collective-permute-start(bf16[128,256]{1,0:T(8,128)(2,1)S(1)} %get-tuple-element.71), channel_id=1, source_target_pairs={{0,2},{1,3},{2,0},{3,1},{4,6},{5,7},{6,4},{7,5},{8,10},{9,11},{10,... | collective-permute-start | bytes 196616 | tf_op jit(solution)/shard_map/ppermute | solution.py:469
  74.8 5.6 %collective-permute-start.18 = (bf16[128,256]{1,0:T(8,128)(2,1)S(1)}, bf16[128,256]{1,0:T(8,128)(2,1)S(1)}, u32[]{:S(2)}, u32[]{:S(2)}) collective-permute-start(bf16[128,256]{1,0:T(8,128)(2,1)S(1)} %get-tuple-element.72), channel_id=1, source_target_pairs={{0,3},{1,2},{2,1},{3,0},{4,7},{5,6},{6,5},{7,4},{8,11},{9,10},{10,... | collective-permute-start | bytes 196616 | tf_op jit(solution)/shard_map/ppermute | solution.py:469
  80.0 0.8 %copy-start.11 = (bf16[128,2560]{1,0:T(8,128)(2,1)}, bf16[128,2560]{1,0:T(8,128)(2,1)S(1)}, u32[]{:S(2)}) copy-start(bf16[128,2560]{1,0:T(8,128)(2,1)S(1)} %constant_dynamic-update-slice_fusion.1) | copy-start | bytes 1966084

commit v13 on v12

--- a/solution.py
+++ b/solution.py
@@ -232,7 +232,8 @@
 
 
 def own_queries(refs, half, i):
-    return refs[half][:, head_lanes(0, i)]
+    rows = refs[0].shape[0] // 2
+    return refs[0][half * rows : (half + 1) * rows, head_lanes(0, i)]
 
 
 def guest_queries(refs, half, i):
@@ -241,8 +242,9 @@
 
 def add_far(q, state, slots, i, begin, held):
     rows = q.shape[0]
-    span = slice(begin, begin + rows)
-    near_top = state[1][span, :1]
+    span = pl.ds(pl.multiple_of(begin, rows), rows)
+    stats = state[1][span]
+    near_top = stats[:, :1]
     top = near_top
     for at, (ref, first, valid) in enumerate(slots):
         s = dot_keys(q, keys_of(ref, first, i, rows))
@@ -258,40 +260,51 @@
         mixed += jnp.dot(w.astype(jnp.bfloat16), values_of(ref, first, i, rows), preferred_element_type=jnp.float32)
         part = fold(w, jnp.add)
         total = part if total is None else total + part
-    total = jnp.sum(total, axis=1, keepdims=True) + state[1][span, HEAD_DIM // 2 : HEAD_DIM // 2 + 1] * shrink
+    total = jnp.sum(total, axis=1, keepdims=True) + stats[:, HEAD_DIM // 2 : HEAD_DIM // 2 + 1] * shrink
     return (mixed * (1.0 / total)).astype(jnp.bfloat16)
 
 
-def lanes_of(i):
-    return slice(i * HEAD_DIM, (i + 1) * HEAD_DIM)
-
-
-def finish_own(first, queries, state, slots, outs, rooms):
-    rows, piece = queries[0].shape[0], outs[0].shape[0]
-    for i in range(outs[0].shape[1] // HEAD_DIM):
-        for half, q in enumerate(queries):
-            begin = (2 * (first + i) + half) * rows
-            value = add_far(q[:, lanes_of(first + i)], state, slots, i, begin, rooms[2 * i + half])
-            outs[2 * half][:, lanes_of(i)] = value[:piece]
-            outs[2 * half + 1][:, lanes_of(i)] = value[piece:]
-
-
-def home_kernel(mask, q_mine, q_other, mixed, stats, r1, r2, r3, *rest):
-    outs, rooms = rest[:4], rest[4:]
+def each_half(heads, body):
+    def step(n, carry):
+        body(lax.shift_right_logical(n, 1), lax.bitwise_and(n, 1))
+        return carry
+
+    lax.fori_loop(0, 2 * heads, step, 0)
+
+
+def finish_own(first, queries, state, slots, outs, held):
+    piece = outs[0].shape[0]
+    rows = 2 * piece
+
+    def body(i, half):
+        q = queries[pl.ds(pl.multiple_of(half * rows, rows), rows), head_lanes(first, i)]
+        value = add_far(q, state, slots, i, (2 * (first + i) + half) * rows, held)
+        for wanted in range(2):
+
+            @pl.when(half == wanted)
+            def _():
+                outs[2 * wanted][:, head_lanes(0, i)] = value[:piece]
+                outs[2 * wanted + 1][:, head_lanes(0, i)] = value[piece:]
+
+    each_half(outs[0].shape[1] // HEAD_DIM, body)
+
+
+def home_kernel(mask, q, mixed, stats, r1, r2, r3, *rest):
+    outs, held = rest[:4], rest[4]
     z = lax.axis_index("frame")
     near2 = mask[0, z ^ 2] == 1
 
     @pl.when(inner_frame())
     def _():
-        finish_own(0, (q_mine, q_other), (mixed, stats), [(r1, 0, near2)], outs, rooms)
+        finish_own(0, q, (mixed, stats), [(r1, 0, near2)], outs, held)
 
     @pl.when(jnp.logical_not(inner_frame()))
     def _():
         slots = [(r2, 0, near2), (r3, 0, mask[0, z ^ 3] == 1)]
-        finish_own(0, (q_mine, q_other), (mixed, stats), slots, outs, rooms)
-
-
-def guest_kernel(q, mixed, stats, n1m, n2m, n2o, r1, out, *rooms):
+        finish_own(0, q, (mixed, stats), slots, outs, held)
+
+
+def guest_kernel(q, mixed, stats, n1m, n2m, n2o, r1, out, held):
     rows = r1.shape[0]
     z = lax.axis_index("frame")
 
@@ -304,20 +317,21 @@
         near1 = jnp.where(z == 1, told(n1m, 3), told(n1m, 0)) > 0.5
         picked = told(n2m, 4) == (lax.axis_index("head") // 2).astype(jnp.float32)
         slots = [(n2m, HOME, near2 & picked), (n2o, HOME, near2 & jnp.logical_not(picked)), (r1, 0, near1)]
-        for i in range(out.shape[1] // HEAD_DIM):
-            for half in range(2):
-                begin = (2 * i + half) * rows
-                value = add_far(guest_queries((q,), half, i), (mixed, stats), slots, i, begin, rooms[2 * i + half])
-                out[half * rows : (half + 1) * rows, lanes_of(i)] = value
-
-
-def rest_kernel(mask, q_mine, q_other, mixed, stats, r1, back, *rest):
-    outs, rooms = rest[:4], rest[4:]
+
+        def body(i, half):
+            value = add_far(guest_queries((q,), half, i), (mixed, stats), slots, i, (2 * i + half) * rows, held)
+            out[pl.ds(pl.multiple_of(half * rows, rows), rows), head_lanes(0, i)] = value
+
+        each_half(out.shape[1] // HEAD_DIM, body)
+
+
+def rest_kernel(mask, q, mixed, stats, r1, back, *rest):
+    outs, held = rest[:4], rest[4]
     z = lax.axis_index("frame")
 
     @pl.when(inner_frame())
     def _():
-        finish_own(HOME, (q_mine, q_other), (mixed, stats), [(r1, 0, mask[0, z ^ 2] == 1)], outs, rooms)
+        finish_own(HOME, q, (mixed, stats), [(r1, 0, mask[0, z ^ 2] == 1)], outs, held)
 
     @pl.when(jnp.logical_not(inner_frame()))
     def _():
@@ -425,7 +439,7 @@
     )(mine, other)
 
 
-def swap_kernel(mine, other, q_mine, q_other, out):
+def swap_kernel(mine, other, q, out):
     cut = HOME * HEAD_DIM
 
     @pl.when(inner_frame())
@@ -434,20 +448,20 @@
 
     @pl.when(jnp.logical_not(inner_frame()))
     def _():
-        count = q_mine.shape[1] - cut
+        rows, count = out.shape[0], q.shape[1] - cut
         out[...] = jnp.zeros_like(out)
-        out[:, :count] = q_mine[:, cut:]
-        out[:, cut : cut + count] = q_other[:, cut:]
-
-
-def swapped(mine, other, q_mine, q_other):
+        out[:, :count] = q[:rows, cut:]
+        out[:, cut : cut + count] = q[rows:, cut:]
+
+
+def swapped(mine, other, q):
     return pl.pallas_call(
         swap_kernel,
-        in_specs=[pl.BlockSpec(memory_space=pltpu.VMEM)] * 4,
+        in_specs=[pl.BlockSpec(memory_space=pltpu.VMEM)] * 3,
         out_specs=pl.BlockSpec(memory_space=pltpu.VMEM),
         out_shape=jax.ShapeDtypeStruct((other.shape[0], 2 * HOME * HEAD_DIM), other.dtype),
         compiler_params=pltpu.CompilerParams(vmem_limit_bytes=4 * 1024 * 1024),
-    )(mine, other, q_mine, q_other)
+    )(mine, other, q)
 
 
 def four_frames(queries, keys, values, pair_mask, tile_offset):
@@ -497,15 +511,14 @@
     n2o = across(other)
 
     got = to_head(after(pay, got), 1)
-    q_mine = below(q_own, got[:, :width])
-    q_other = to_head(after(below(q_far, got[:, width:]), other), 2)
+    q = below(q_own, got[:, :width], to_head(after(below(q_far, got[:, width:]), other), 2))
 
     tile = 2 * rows
     cut = HOME * HEAD_DIM
     guests = heads - HOME
     r1_home, r1_rest = after(relayed(n1m, n1o, [(0, cut), (cut, width)]), n2m)
     r1_home = across(r1_home)
-    swap = along(swapped(n2m, n2o, q_mine, q_other), OUTER)
+    swap = along(swapped(n2m, n2o, q), OUTER)
     r1_rest = across(after(r1_rest, n2o))
 
     def state(count):
@@ -515,11 +528,10 @@
         return 4 * chunks * tiles * tile * tile * HEAD_DIM
 
     bf16 = jnp.bfloat16
-    q = [q_mine, q_other]
     *near, done = run_kernel(
-        functools.partial(near_kernel, 0, ((6, heads), (4, HOME)), own_queries, 2),
+        functools.partial(near_kernel, 0, ((6, heads), (4, HOME)), own_queries, 1),
         None,
-        [*q, mine, other, n1m, n1o, n2m, n2o],
+        [q, mine, other, n1m, n1o, n2m, n2o],
         state(heads),
         (2, (tile, 6 * tile)),
         flops(2 * heads, 6),
@@ -538,25 +550,25 @@
         None,
         [swap, *guest_near, n1m, n2m, n2o, r1_rest],
         [((2 * tile, width - cut), bf16)],
-        (2 * guests, (tile, 3 * tile)),
+        (1, (tile, 3 * tile)),
         flops(2 * guests, 3),
     )
     back = along(back, OUTER)
     out = run_kernel(
         home_kernel,
         pair_mask,
-        [*q, *near, r1_home, swap, r3],
+        [q, *near, r1_home, swap, r3],
         [((rows, cut), bf16)] * 4,
-        (2 * HOME, (tile, 2 * tile)),
+        (1, (tile, 2 * tile)),
         flops(2 * HOME, 2),
     )
     pieces = [(to_head(out[d], d) if d else out[0], d, 0) for d in range(4)]
     out = run_kernel(
         rest_kernel,
         pair_mask,
-        [*q, *near, r1_rest, after(back, out[1])],
+        [q, *near, r1_rest, after(back, out[1])],
         [((rows, width - cut), bf16)] * 4,
-        (2 * guests, (tile, tile)),
+        (1, (tile, tile)),
         flops(2 * guests, 1),
     )
     pieces += [(to_head(out[d], d) if d else out[0], d, cut) for d in range(4)]

time: 82.9 us -> 83.4 us (level); the launches traced: 81.4 us -> 83.1 us
  starting transfers between devices: 24.9 us -> 26.6 us
  Pallas kernels: 11 us -> 11.9 us
    ppermute x5, waiting for transfers between devices: 21.5 us -> 15.2 us  [along(): return lax.ppermute(array, 'frame', pairs)]
    ppermute x10, waiting for transfers between devices: 18 us -> 23.5 us  [to_head(): return lax.ppermute(array, 'head', [(i, i ^ d) for i in range(4)])]
    ppermute x5, starting transfers between devices: 15.6 us -> 16.9 us  [along(): return lax.ppermute(array, 'frame', pairs)]
    pallas_call x5, Pallas kernels: 9.28 us -> 10.1 us  [run_kernel(): pl.pallas_call(kernel, in_specs=[pl.BlockSpec(memory_space=pltpu.SMEM)] *...]
    unnamed x24 -> x18, local copies, waits for them, and re-layouts: 2.43 us -> 2.4 us
  transfers between devices with their start and end apart: 19 -> 19, of which waited for: 9 -> 10; matrix products, arithmetic and copies ran while one was open for 0% -> 0% of each run, Pallas kernels for 14% -> 14%
where the time goes in v13:
time: 83.4 us; the launch traced here: 83.1 us
  waiting for transfers between devices  38.7 us (46%)
  starting transfers between devices  26.6 us (32%)
  Pallas kernels  11.9 us (14%)
  local copies, waits for them, and re-layouts  4.78 us (6%)
  between operations  0.96 us (1%)
    ppermute x10, waiting for transfers between devices, to_head(): return lax.ppermute(array, 'head', [(i, i ^ d) for i in range(4)])  23.5 us
    ppermute x5, starting transfers between devices, along(): return lax.ppermute(array, 'frame', pairs)  16.9 us
    ppermute x5, waiting for transfers between devices, along(): return lax.ppermute(array, 'frame', pairs)  15.2 us
    pallas_call x5, Pallas kernels, run_kernel(): pl.pallas_call(kernel, in_specs=[pl.BlockSpec(memory_space=pltpu.SMEM)] *...  10.1 us
    ppermute x10, starting transfers between devices, to_head(): return lax.ppermute(array, 'head', [(i, i ^ d) for i in range(4)])  8.99 us
    unnamed x18, local copies, waits for them, and re-layouts  2.4 us
  transfers between devices with their start and end apart: 19, of which 10 were waited for; matrix products, arithmetic and copies ran while one was open for 0% of the time, Pallas kernels for 14%

profile of v13, /device:TPU:0, one launch (start us, length us, event | category | flops | bytes accessed | tf_op | source)
XLA Modules:
  0.0 83.1 jit_solution(2056702110068043186)
XLA Ops:
  0.0 1.5 %constant_dynamic-slice_fusion = (bf16[128,640]{1,0:T(8,128)(2,1)S(1)}, bf16[128,640]{1,0:T(8,128)(2,1)S(1)}, bf16[128,640]{1,0:T(8,128)(2,1)S(1)}, bf16[128,640...) fusion(bf16[128,2560]{1,0:T(8,128)(2,1)} %refs_2_.1, ...), kind=kLoop, calls=%fused_computation.13 | loop fusion | bytes 2621456 | tf_op jit(solution)/shard_map/dynamic_slice | solution.py:474
  1.5 0.1 pad_maximum_fusion.1
  1.6 0.0 copy-start.2
  1.6 0.0 copy-start.3
  1.6 0.0 copy-start.7
  1.6 0.5 collective-permute-start
  2.1 1.7 %collective-permute-done = bf16[128,2560]{1,0:T(8,128)(2,1)S(1)} collective-permute-done((bf16[128,2560]{1,0:T(8,128)(2,1)S(1)}, bf16[128,2560]{1,0:T(8,128)(2,1)S(1)}, u32[]{:S(2)}, u32[]{:S(2)}) %collective-permute-start) | collective-permute-done | bytes 655392 | tf_op jit(solution)/shard_map/ppermute | solution.py:483
  4.0 2.9 %collective-permute-start.2 = (bf16[256,1280]{1,0:T(8,128)(2,1)S(1)}, bf16[256,1280]{1,0:T(8,128)(2,1)S(1)}, u32[]{:S(2)}, u32[]{:S(2)}) collective-permute-start(bf16[256,1280]{1,0:T(8,128)(2,1)S(1)} %pad_maximum_fusion.2), channel_id=1, source_target_pairs={{0,2},{1,3},{2,0},{3,1},{4,6},{5,7},{6,4},{7,5},{8,10},{9,11},{10,... | collective-permute-start | bytes 1966088 | tf_op jit(solution)/shard_map/ppermute | solution.py:483
  7.6 0.7 shard_map.55
  8.3 0.1 collective-permute-start.1
  8.4 0.1 pad_maximum_fusion.refs_1_
  8.4 0.6 collective-permute-start.6
  9.0 2.7 %collective-permute-start.4 = (bf16[272,1280]{1,0:T(8,128)(2,1)S(1)}, bf16[272,1280]{1,0:T(8,128)(2,1)S(1)}, u32[]{:S(2)}, u32[]{:S(2)}) collective-permute-start(bf16[272,1280]{1,0:T(8,128)(2,1)S(1)} %pad_maximum_fusion.refs_1_), channel_id=1, source_target_pairs={{0,4},{4,0},{8,12},{12,8},{1,5},{5,1},{9,13},{13,9},{2,6},{6,2},{1... | collective-permute-start | bytes 2088968 | tf_op jit(solution)/shard_map/ppermute | solution.py:486
  11.6 10.3 %collective-permute-done.2.refs_2_ = bf16[256,1280]{1,0:T(8,128)(2,1)S(1)} collective-permute-done((bf16[256,1280]{1,0:T(8,128)(2,1)S(1)}, bf16[256,1280]{1,0:T(8,128)(2,1)S(1)}, u32[]{:S(2)}, u32[]{:S(2)}) %collective-permute-start.2) | collective-permute-done | bytes 655392 | tf_op jit(solution)/shard_map/ppermute | solution.py:483
  21.9 3.4 %collective-permute-start.5 = (bf16[256,1280]{1,0:T(8,128)(2,1)S(1)}, bf16[256,1280]{1,0:T(8,128)(2,1)S(1)}, u32[]{:S(2)}, u32[]{:S(2)}) collective-permute-start(bf16[256,1280]{1,0:T(8,128)(2,1)S(1)} %collective-permute-done.2.refs_2_), channel_id=1, source_target_pairs={{0,4},{4,0},{8,12},{12,8},{1,5},{5,1},{9,13},{13,9},{2,6},{6,2},{1... | collective-permute-start | bytes 1966088 | tf_op jit(solution)/shard_map/ppermute | solution.py:486
  25.4 1.6 %collective-permute-start.3 = (bf16[256,640]{1,0:T(8,128)(2,1)S(1)}, bf16[256,640]{1,0:T(8,128)(2,1)S(1)}, u32[]{:S(2)}, u32[]{:S(2)}) collective-permute-start(bf16[256,640]{1,0:T(8,128)(2,1)S(1)} %pad_maximum_fusion.4), channel_id=1, source_target_pairs={{0,2},{1,3},{2,0},{3,1},{4,6},{5,7},{6,4},{7,5},{8,10},{9,11},{10,... | collective-permute-start | bytes 983048 | tf_op jit(solution)/shard_map/ppermute | solution.py:483
  27.0 6.9 %collective-permute-done.3 = bf16[256,640]{1,0:T(8,128)(2,1)S(1)} collective-permute-done((bf16[256,640]{1,0:T(8,128)(2,1)S(1)}, bf16[256,640]{1,0:T(8,128)(2,1)S(1)}, u32[]{:S(2)}, u32[]{:S(2)}) %collective-permute-start.3) | collective-permute-done | bytes 327712 | tf_op jit(solution)/shard_map/ppermute | solution.py:483
  33.8 0.1 pad_maximum_fusion.3.refs_0_.q
  33.9 7.8 %collective-permute-done.5.refs_4_.other = bf16[256,1280]{1,0:T(8,128)(2,1)S(1)} collective-permute-done((bf16[256,1280]{1,0:T(8,128)(2,1)S(1)}, bf16[256,1280]{1,0:T(8,128)(2,1)S(1)}, u32[]{:S(2)}, u32[]{:S(2)}) %collective-permute-start.5) | collective-permute-done | bytes 655392 | tf_op jit(solution)/shard_map/ppermute | solution.py:486
  41.7 0.2 shard_map.57
  41.9 0.1 collective-permute-start.8
  41.9 0.1 shard_map.58
  42.0 2.3 %collective-permute-start.9 = (bf16[256,768]{1,0:T(8,128)(2,1)S(1)}, bf16[256,768]{1,0:T(8,128)(2,1)S(1)}, u32[]{:S(2)}, u32[]{:S(2)}) collective-permute-start(bf16[256,768]{1,0:T(8,128)(2,1)S(1)} %shard_map.58), channel_id=1, source_target_pairs={{0,4},{4,0},{8,12},{12,8},{1,5},{5,1},{9,13},{13,9},{2,6},{6,2},{1... | collective-permute-start | bytes 1179656 | tf_op jit(solution)/shard_map/ppermute | solution.py:486
  44.4 2.9 %shard_map.56 = (f32[2560,128]{1,0:T(8,128)S(1)}, f32[2560,128]{1,0:T(8,128)S(1)}, f32[8,128]{1,0:T(8,128)S(1)}) custom-call(bf16[512,640]{1,0:T(8,128)(2,1)S(1)} %pad_maximum_fusion.3.refs_0_.q, bf16[272,1280]{1,0:T(8,128)(2,1)S(1)} %pad_maximum_fusion.refs_1_, bf16[256,1280]{1,0:T(8,128)(2,1)S(1)} %collective-permute-done.2.refs_2_, ...), custom_call_target="tpu_custom_call" | custom-call | flops 2013265920 | bytes 4710400 | tf_op jit(solution)/shard_map/pallas_call | solution.py:358
  47.3 0.0 copy-start.4
  47.3 0.8 %shard_map.59 = bf16[256,768]{1,0:T(8,128)(2,1)} custom-call(f32[8,128]{1,0:T(8,128)S(1)} %get-tuple-element.58.done, bf16[256,768]{1,0:T(8,128)(2,1)S(1)} %collective-permute-done.8.x.r1), custom_call_target="tpu_custom_call" | custom-call | tf_op jit(solution)/shard_map/pallas_call | solution.py:347
  48.1 5.4 %collective-permute-done.9.r2.refs_0_.q = bf16[256,768]{1,0:T(8,128)(2,1)S(1)} collective-permute-done((bf16[256,768]{1,0:T(8,128)(2,1)S(1)}, bf16[256,768]{1,0:T(8,128)(2,1)S(1)}, u32[]{:S(2)}, u32[]{:S(2)}) %collective-permute-start.9) | collective-permute-done | bytes 393248 | tf_op jit(solution)/shard_map/ppermute | solution.py:486
  53.6 3.0 %collective-permute-start.10 = (bf16[256,768]{1,0:T(8,128)(2,1)}, bf16[256,768]{1,0:T(8,128)(2,1)}, u32[]{:S(2)}, u32[]{:S(2)}) collective-permute-start(bf16[256,768]{1,0:T(8,128)(2,1)} %shard_map.59), channel_id=1, source_target_pairs={{0,4},{4,0},{8,12},{12,8},{1,5},{5,1},{9,13},{13,9},{2,6},{6,2},{1... | collective-permute-start | bytes 1179656 | tf_op jit(solution)/shard_map/ppermute | solution.py:486
  56.5 0.6 shard_map.61
  57.1 0.7 shard_map.62
  57.9 5.6 %collective-permute-start.15 = (bf16[512,256]{1,0:T(8,128)(2,1)}, bf16[512,256]{1,0:T(8,128)(2,1)}, u32[]{:S(2)}, u32[]{:S(2)}) collective-permute-start(bf16[512,256]{1,0:T(8,128)(2,1)} %shard_map.62), channel_id=1, source_target_pairs={{0,4},{4,0},{8,12},{12,8},{1,5},{5,1},{9,13},{13,9},{2,6},{6,2},{1... | collective-permute-start | bytes 786440 | tf_op jit(solution)/shard_map/ppermute | solution.py:486
  63.4 2.0 %collective-permute-done.10.r3 = bf16[256,768]{1,0:T(8,128)(2,1)} collective-permute-done((bf16[256,768]{1,0:T(8,128)(2,1)}, bf16[256,768]{1,0:T(8,128)(2,1)}, u32[]{:S(2)}, u32[]{:S(2)}) %collective-permute-start.10) | collective-permute-done | bytes 393248 | tf_op jit(solution)/shard_map/ppermute | solution.py:486
  65.4 1.0 %copy-done.1 = bf16[256,768]{1,0:T(8,128)(2,1)S(1)} copy-done((bf16[256,768]{1,0:T(8,128)(2,1)S(1)}, bf16[256,768]{1,0:T(8,128)(2,1)}, u32[]{:S(2)}) %copy-start.1) | copy-done | bytes 393240
  66.4 1.0 %copy-done.5 = bf16[256,768]{1,0:T(8,128)(2,1)S(1)} copy-done((bf16[256,768]{1,0:T(8,128)(2,1)S(1)}, bf16[256,768]{1,0:T(8,128)(2,1)}, u32[]{:S(2)}) %copy-start.5) | copy-done | bytes 393240
  67.4 4.9 %shard_map.60 = (bf16[128,384]{1,0:T(8,128)(2,1)S(1)}, bf16[128,384]{1,0:T(8,128)(2,1)S(1)}, bf16[128,384]{1,0:T(8,128)(2,1)S(1)}, bf16[128,384]{1,0:T(8,128)(2,1)S(1)}) custom-call(s32[1,4]{1,0:T(1,128)S(1)} %copy-done.7, bf16[512,640]{1,0:T(8,128)(2,1)S(1)} %pad_maximum_fusion.3.refs_0_.q, f32[2560,128]{1,0:T(8,128)S(1)} %get-tuple-element.53.mixed, ...), custom_call_target="tpu_custom_call" | custom-call | flops 402653184 | bytes 3145728 | tf_op jit(solution)/shard_map/pallas_call | solution.py:358
  72.4 0.1 collective-permute-start.11
  72.5 0.6 collective-permute-start.12
  73.1 1.2 %collective-permute-start.13 = (bf16[128,384]{1,0:T(8,128)(2,1)S(1)}, bf16[128,384]{1,0:T(8,128)(2,1)S(1)}, u32[]{:S(2)}, u32[]{:S(2)}) collective-permute-start(bf16[128,384]{1,0:T(8,128)(2,1)S(1)} %get-tuple-element.63), channel_id=1, source_target_pairs={{0,3},{1,2},{2,1},{3,0},{4,7},{5,6},{6,5},{7,4},{8,11},{9,10},{10,... | collective-permute-start | bytes 294920 | tf_op jit(solution)/shard_map/ppermute | solution.py:483
  74.3 1.0 %shard_map.63 = (bf16[128,256]{1,0:T(8,128)(2,1)S(1)}, bf16[128,256]{1,0:T(8,128)(2,1)S(1)}, bf16[128,256]{1,0:T(8,128)(2,1)S(1)}, bf16[128,256]{1,0:T(8,128)(2,1)S(1)}) custom-call(s32[1,4]{1,0:T(1,128)S(1)} %copy-done.7, bf16[512,640]{1,0:T(8,128)(2,1)S(1)} %pad_maximum_fusion.3.refs_0_.q, f32[2560,128]{1,0:T(8,128)S(1)} %get-tuple-element.53.mixed, ...), custom_call_target="tpu_custom_call" | custom-call | flops 134217728 | bytes 2490368 | tf_op jit(solution)/shard_map/pallas_call | solution.py:358
  75.3 0.4 collective-permute-start.16
  75.7 0.6 collective-permute-start.17
  76.4 1.0 %collective-permute-start.18 = (bf16[128,256]{1,0:T(8,128)(2,1)S(1)}, bf16[128,256]{1,0:T(8,128)(2,1)S(1)}, u32[]{:S(2)}, u32[]{:S(2)}) collective-permute-start(bf16[128,256]{1,0:T(8,128)(2,1)S(1)} %get-tuple-element.72), channel_id=1, source_target_pairs={{0,3},{1,2},{2,1},{3,0},{4,7},{5,6},{6,5},{7,4},{8,11},{9,10},{10,... | collective-permute-start | bytes 196616 | tf_op jit(solution)/shard_map/ppermute | solution.py:483
  77.4 0.7 collective-permute-done.12
  78.1 1.2 %collective-permute-done.13 = bf16[128,384]{1,0:T(8,128)(2,1)S(1)} collective-permute-done((bf16[128,384]{1,0:T(8,128)(2,1)S(1)}, bf16[128,384]{1,0:T(8,128)(2,1)S(1)}, u32[]{:S(2)}, u32[]{:S(2)}) %collective-permute-start.13) | collective-permute-done | bytes 98336 | tf_op jit(solution)/shard_map/ppermute | solution.py:483
  79.4 2.3 %collective-permute-done.17 = bf16[128,256]{1,0:T(8,128)(2,1)S(1)} collective-permute-done((bf16[128,256]{1,0:T(8,128)(2,1)S(1)}, bf16[128,256]{1,0:T(8,128)(2,1)S(1)}, u32[]{:S(2)}, u32[]{:S(2)}) %collective-permute-start.17) | collective-permute-done | bytes 65568 | tf_op jit(solution)/shard_map/ppermute | solution.py:483
  81.7 0.5 collective-permute-done.18
  82.1 0.4 copy-done.8
  82.5 0.6 constant_dynamic-update-slice_fusion
  (34 shorter events, 0.4 us)
Async XLA Ops:
  1.6 6.0 %copy-start.2 = (bf16[128,2560]{1,0:T(8,128)(2,1)S(1)}, bf16[128,2560]{1,0:T(8,128)(2,1)}, u32[]{:S(2)}) copy-start(bf16[128,2560]{1,0:T(8,128)(2,1)} %refs_1_.1) | copy-start | bytes 1966084
  1.6 6.0 %copy-start.3 = (bf16[128,2560]{1,0:T(8,128)(2,1)S(1)}, bf16[128,2560]{1,0:T(8,128)(2,1)}, u32[]{:S(2)}) copy-start(bf16[128,2560]{1,0:T(8,128)(2,1)} %refs_2_.1) | copy-start | bytes 1966084
  1.6 6.0 %copy-start.6 = (bf16[128,2560]{1,0:T(8,128)(2,1)S(1)}, bf16[128,2560]{1,0:T(8,128)(2,1)}, u32[]{:S(2)}) copy-start(bf16[128,2560]{1,0:T(8,128)(2,1)} %refs_0_.1) | copy-start | bytes 1966084
  1.6 6.0 %copy-start.7 = (s32[1,4]{1,0:T(1,128)S(1)}, s32[1,4]{1,0:T(1,128)}, u32[]{:S(2)}) copy-start(s32[1,4]{1,0:T(1,128)} %mask.5) | copy-start | bytes 52
  1.6 2.2 %collective-permute-start = (bf16[128,2560]{1,0:T(8,128)(2,1)S(1)}, bf16[128,2560]{1,0:T(8,128)(2,1)S(1)}, u32[]{:S(2)}, u32[]{:S(2)}) collective-permute-start(bf16[128,2560]{1,0:T(8,128)(2,1)S(1)} %pad_maximum_fusion.1), channel_id=1, source_target_pairs={{0,1},{1,0},{2,3},{3,2},{4,5},{5,4},{6,7},{7,6},{8,9},{9,8},{10,11... | collective-permute-start | bytes 1966088 | tf_op jit(solution)/shard_map/ppermute | solution.py:483
  4.0 18.0 %collective-permute-start.2 = (bf16[256,1280]{1,0:T(8,128)(2,1)S(1)}, bf16[256,1280]{1,0:T(8,128)(2,1)S(1)}, u32[]{:S(2)}, u32[]{:S(2)}) collective-permute-start(bf16[256,1280]{1,0:T(8,128)(2,1)S(1)} %pad_maximum_fusion.2), channel_id=1, source_target_pairs={{0,2},{1,3},{2,0},{3,1},{4,6},{5,7},{6,4},{7,5},{8,10},{9,11},{10,... | collective-permute-start | bytes 1966088 | tf_op jit(solution)/shard_map/ppermute | solution.py:483
  8.3 17.1 %collective-permute-start.1 = (bf16[128,1280]{1,0:T(8,128)(2,1)S(1)}, bf16[128,1280]{1,0:T(8,128)(2,1)S(1)}, u32[]{:S(2)}, u32[]{:S(2)}) collective-permute-start(bf16[128,1280]{1,0:T(8,128)(2,1)S(1)} %get-tuple-element.45), channel_id=1, source_target_pairs={{0,1},{1,0},{2,3},{3,2},{4,5},{5,4},{6,7},{7,6},{8,9},{9,8},{10,11... | collective-permute-start | bytes 983048 | tf_op jit(solution)/shard_map/ppermute | solution.py:483
  8.4 33.4 %collective-permute-start.6 = (bf16[272,1280]{1,0:T(8,128)(2,1)S(1)}, bf16[272,1280]{1,0:T(8,128)(2,1)S(1)}, u32[]{:S(2)}, u32[]{:S(2)}) collective-permute-start(bf16[272,1280]{1,0:T(8,128)(2,1)S(1)} %pad_maximum_fusion.refs_1_), channel_id=1, source_target_pairs={{0,1},{1,0},{2,3},{3,2},{4,8},{5,9},{6,10},{7,11},{8,4},{9,5},{10,... | collective-permute-start | bytes 2088968 | tf_op jit(solution)/shard_map/ppermute | solution.py:490
  9.0 24.9 %collective-permute-start.4 = (bf16[272,1280]{1,0:T(8,128)(2,1)S(1)}, bf16[272,1280]{1,0:T(8,128)(2,1)S(1)}, u32[]{:S(2)}, u32[]{:S(2)}) collective-permute-start(bf16[272,1280]{1,0:T(8,128)(2,1)S(1)} %pad_maximum_fusion.refs_1_), channel_id=1, source_target_pairs={{0,4},{4,0},{8,12},{12,8},{1,5},{5,1},{9,13},{13,9},{2,6},{6,2},{1... | collective-permute-start | bytes 2088968 | tf_op jit(solution)/shard_map/ppermute | solution.py:486
  21.9 20.0 %collective-permute-start.7 = (bf16[256,1280]{1,0:T(8,128)(2,1)S(1)}, bf16[256,1280]{1,0:T(8,128)(2,1)S(1)}, u32[]{:S(2)}, u32[]{:S(2)}) collective-permute-start(bf16[256,1280]{1,0:T(8,128)(2,1)S(1)} %collective-permute-done.2.refs_2_), channel_id=1, source_target_pairs={{0,1},{1,0},{2,3},{3,2},{4,8},{5,9},{6,10},{7,11},{8,4},{9,5},{10,... | collective-permute-start | bytes 1966088 | tf_op jit(solution)/shard_map/ppermute | solution.py:490
  21.9 19.7 %collective-permute-start.5 = (bf16[256,1280]{1,0:T(8,128)(2,1)S(1)}, bf16[256,1280]{1,0:T(8,128)(2,1)S(1)}, u32[]{:S(2)}, u32[]{:S(2)}) collective-permute-start(bf16[256,1280]{1,0:T(8,128)(2,1)S(1)} %collective-permute-done.2.refs_2_), channel_id=1, source_target_pairs={{0,4},{4,0},{8,12},{12,8},{1,5},{5,1},{9,13},{13,9},{2,6},{6,2},{1... | collective-permute-start | bytes 1966088 | tf_op jit(solution)/shard_map/ppermute | solution.py:486
  25.4 8.4 %collective-permute-start.3 = (bf16[256,640]{1,0:T(8,128)(2,1)S(1)}, bf16[256,640]{1,0:T(8,128)(2,1)S(1)}, u32[]{:S(2)}, u32[]{:S(2)}) collective-permute-start(bf16[256,640]{1,0:T(8,128)(2,1)S(1)} %pad_maximum_fusion.4), channel_id=1, source_target_pairs={{0,2},{1,3},{2,0},{3,1},{4,6},{5,7},{6,4},{7,5},{8,10},{9,11},{10,... | collective-permute-start | bytes 983048 | tf_op jit(solution)/shard_map/ppermute | solution.py:483
  41.9 5.4 %collective-permute-start.8 = (bf16[256,768]{1,0:T(8,128)(2,1)S(1)}, bf16[256,768]{1,0:T(8,128)(2,1)S(1)}, u32[]{:S(2)}, u32[]{:S(2)}) collective-permute-start(bf16[256,768]{1,0:T(8,128)(2,1)S(1)} %get-tuple-element.57), channel_id=1, source_target_pairs={{0,1},{1,0},{2,3},{3,2},{4,8},{5,9},{6,10},{7,11},{8,4},{9,5},{10,... | collective-permute-start | bytes 1179656 | tf_op jit(solution)/shard_map/ppermute | solution.py:490
  42.0 11.6 %collective-permute-start.9 = (bf16[256,768]{1,0:T(8,128)(2,1)S(1)}, bf16[256,768]{1,0:T(8,128)(2,1)S(1)}, u32[]{:S(2)}, u32[]{:S(2)}) collective-permute-start(bf16[256,768]{1,0:T(8,128)(2,1)S(1)} %shard_map.58), channel_id=1, source_target_pairs={{0,4},{4,0},{8,12},{12,8},{1,5},{5,1},{9,13},{13,9},{2,6},{6,2},{1... | collective-permute-start | bytes 1179656 | tf_op jit(solution)/shard_map/ppermute | solution.py:486
  44.4 12.8 %collective-permute-start.14 = (bf16[256,512]{1,0:T(8,128)(2,1)S(1)}, bf16[256,512]{1,0:T(8,128)(2,1)S(1)}, u32[]{:S(2)}, u32[]{:S(2)}) collective-permute-start(bf16[256,512]{1,0:T(8,128)(2,1)S(1)} %get-tuple-element.65), channel_id=1, source_target_pairs={{0,1},{1,0},{2,3},{3,2},{4,8},{5,9},{6,10},{7,11},{8,4},{9,5},{10,... | collective-permute-start | bytes 786440 | tf_op jit(solution)/shard_map/ppermute | solution.py:490
  47.3 9.8 %copy-start.4 = (bf16[256,768]{1,0:T(8,128)(2,1)}, bf16[256,768]{1,0:T(8,128)(2,1)S(1)}, u32[]{:S(2)}) copy-start(bf16[256,768]{1,0:T(8,128)(2,1)S(1)} %collective-permute-done.8.x.r1) | copy-start | bytes 1179652
  53.6 3.6 %copy-start = (bf16[256,768]{1,0:T(8,128)(2,1)}, bf16[256,768]{1,0:T(8,128)(2,1)S(1)}, u32[]{:S(2)}) copy-start(bf16[256,768]{1,0:T(8,128)(2,1)S(1)} %collective-permute-done.9.r2.refs_0_.q) | copy-start | bytes 1179652
  53.6 11.9 %collective-permute-start.10 = (bf16[256,768]{1,0:T(8,128)(2,1)}, bf16[256,768]{1,0:T(8,128)(2,1)}, u32[]{:S(2)}, u32[]{:S(2)}) collective-permute-start(bf16[256,768]{1,0:T(8,128)(2,1)} %shard_map.59), channel_id=1, source_target_pairs={{0,4},{4,0},{8,12},{12,8},{1,5},{5,1},{9,13},{13,9},{2,6},{6,2},{1... | collective-permute-start | bytes 1179656 | tf_op jit(solution)/shard_map/ppermute | solution.py:486
  57.9 14.6 %collective-permute-start.15 = (bf16[512,256]{1,0:T(8,128)(2,1)}, bf16[512,256]{1,0:T(8,128)(2,1)}, u32[]{:S(2)}, u32[]{:S(2)}) collective-permute-start(bf16[512,256]{1,0:T(8,128)(2,1)} %shard_map.62), channel_id=1, source_target_pairs={{0,4},{4,0},{8,12},{12,8},{1,5},{5,1},{9,13},{13,9},{2,6},{6,2},{1... | collective-permute-start | bytes 786440 | tf_op jit(solution)/shard_map/ppermute | solution.py:486
  65.4 1.0 %copy-start.1 = (bf16[256,768]{1,0:T(8,128)(2,1)S(1)}, bf16[256,768]{1,0:T(8,128)(2,1)}, u32[]{:S(2)}) copy-start(bf16[256,768]{1,0:T(8,128)(2,1)} %copy-done) | copy-start | bytes 1179652
  66.4 1.0 %copy-start.5 = (bf16[256,768]{1,0:T(8,128)(2,1)S(1)}, bf16[256,768]{1,0:T(8,128)(2,1)}, u32[]{:S(2)}) copy-start(bf16[256,768]{1,0:T(8,128)(2,1)} %copy-done.4) | copy-start | bytes 1179652
  72.4 4.0 %collective-permute-start.11 = (bf16[128,384]{1,0:T(8,128)(2,1)S(1)}, bf16[128,384]{1,0:T(8,128)(2,1)S(1)}, u32[]{:S(2)}, u32[]{:S(2)}) collective-permute-start(bf16[128,384]{1,0:T(8,128)(2,1)S(1)} %get-tuple-element.61), channel_id=1, source_target_pairs={{0,1},{1,0},{2,3},{3,2},{4,5},{5,4},{6,7},{7,6},{8,9},{9,8},{10,11... | collective-permute-start | bytes 294920 | tf_op jit(solution)/shard_map/ppermute | solution.py:483
  72.5 5.7 %collective-permute-start.12 = (bf16[128,384]{1,0:T(8,128)(2,1)S(1)}, bf16[128,384]{1,0:T(8,128)(2,1)S(1)}, u32[]{:S(2)}, u32[]{:S(2)}) collective-permute-start(bf16[128,384]{1,0:T(8,128)(2,1)S(1)} %get-tuple-element.62), channel_id=1, source_target_pairs={{0,2},{1,3},{2,0},{3,1},{4,6},{5,7},{6,4},{7,5},{8,10},{9,11},{10,... | collective-permute-start | bytes 294920 | tf_op jit(solution)/shard_map/ppermute | solution.py:483
  73.1 6.2 %collective-permute-start.13 = (bf16[128,384]{1,0:T(8,128)(2,1)S(1)}, bf16[128,384]{1,0:T(8,128)(2,1)S(1)}, u32[]{:S(2)}, u32[]{:S(2)}) collective-permute-start(bf16[128,384]{1,0:T(8,128)(2,1)S(1)} %get-tuple-element.63), channel_id=1, source_target_pairs={{0,3},{1,2},{2,1},{3,0},{4,7},{5,6},{6,5},{7,4},{8,11},{9,10},{10,... | collective-permute-start | bytes 294920 | tf_op jit(solution)/shard_map/ppermute | solution.py:483
  75.3 4.0 %collective-permute-start.16 = (bf16[128,256]{1,0:T(8,128)(2,1)S(1)}, bf16[128,256]{1,0:T(8,128)(2,1)S(1)}, u32[]{:S(2)}, u32[]{:S(2)}) collective-permute-start(bf16[128,256]{1,0:T(8,128)(2,1)S(1)} %get-tuple-element.70), channel_id=1, source_target_pairs={{0,1},{1,0},{2,3},{3,2},{4,5},{5,4},{6,7},{7,6},{8,9},{9,8},{10,11... | collective-permute-start | bytes 196616 | tf_op jit(solution)/shard_map/ppermute | solution.py:483
  75.7 5.9 %collective-permute-start.17 = (bf16[128,256]{1,0:T(8,128)(2,1)S(1)}, bf16[128,256]{1,0:T(8,128)(2,1)S(1)}, u32[]{:S(2)}, u32[]{:S(2)}) collective-permute-start(bf16[128,256]{1,0:T(8,128)(2,1)S(1)} %get-tuple-element.71), channel_id=1, source_target_pairs={{0,2},{1,3},{2,0},{3,1},{4,6},{5,7},{6,4},{7,5},{8,10},{9,11},{10,... | collective-permute-start | bytes 196616 | tf_op jit(solution)/shard_map/ppermute | solution.py:483
  76.4 5.7 %collective-permute-start.18 = (bf16[128,256]{1,0:T(8,128)(2,1)S(1)}, bf16[128,256]{1,0:T(8,128)(2,1)S(1)}, u32[]{:S(2)}, u32[]{:S(2)}) collective-permute-start(bf16[128,256]{1,0:T(8,128)(2,1)S(1)} %get-tuple-element.72), channel_id=1, source_target_pairs={{0,3},{1,2},{2,1},{3,0},{4,7},{5,6},{6,5},{7,4},{8,11},{9,10},{10,... | collective-permute-start | bytes 196616 | tf_op jit(solution)/shard_map/ppermute | solution.py:483
  81.6 0.8 %copy-start.8 = (bf16[128,2560]{1,0:T(8,128)(2,1)}, bf16[128,2560]{1,0:T(8,128)(2,1)S(1)}, u32[]{:S(2)}) copy-start(bf16[128,2560]{1,0:T(8,128)(2,1)S(1)} %constant_dynamic-update-slice_fusion.1) | copy-start | bytes 1966084

commit v14 on v13

--- a/solution.py
+++ b/solution.py
@@ -189,10 +189,15 @@
     return result
 
 
-def near_kernel(first, counts, queries_of, n_queries, *refs):
-    queries, tiles, (mixed_out, stats, done), rooms = refs[:n_queries], refs[n_queries:-5], refs[-5:-2], refs[-2:]
+def near_kernel(first, counts, queries_of, carries, *refs):
+    n_outs = 5 if carries else 4
+    ins, outs, rooms = refs[: -2 - n_outs], refs[-2 - n_outs : -2], refs[-2:]
+    queries, tiles = ins[0], ins[1:]
+    mixed_out, tops, totals, done = outs[:4]
     rows = rooms[0].shape[0]
     done[...] = jnp.zeros_like(done)
+    if carries:
+        outs[4][...] = ins[-1][...]
 
     def one_head(used, i):
         found = []
@@ -215,9 +220,8 @@
                 total = part if total is None else total + part
             span = pl.ds(pl.multiple_of((2 * i + half) * rows, rows), rows)
             mixed_out[span] = mixed
-            half_lanes = (rows, HEAD_DIM // 2)
-            stats[span, : HEAD_DIM // 2] = jnp.broadcast_to(top, half_lanes)
-            stats[span, HEAD_DIM // 2 :] = jnp.broadcast_to(jnp.sum(total, axis=1, keepdims=True), half_lanes)
+            tops[span] = jnp.broadcast_to(top, (rows, HEAD_DIM))
+            totals[span] = jnp.broadcast_to(jnp.sum(total, axis=1, keepdims=True), (rows, HEAD_DIM))
 
     for wanted, (n_tiles, n_heads) in zip((True, False), counts):
         if n_heads:
@@ -231,85 +235,92 @@
                 lax.fori_loop(0, n_heads, step, 0)
 
 
-def own_queries(refs, half, i):
-    rows = refs[0].shape[0] // 2
-    return refs[0][half * rows : (half + 1) * rows, head_lanes(0, i)]
-
-
-def guest_queries(refs, half, i):
-    return refs[0][:, head_lanes(half * HOME, i)]
+def own_queries(ref, half, i):
+    rows = ref.shape[0] // 2
+    return ref[half * rows : (half + 1) * rows, head_lanes(0, i)]
+
+
+def guest_queries(ref, half, i):
+    return ref[:, head_lanes(half * HOME, i)]
 
 
 def add_far(q, state, slots, i, begin, held):
     rows = q.shape[0]
     span = pl.ds(pl.multiple_of(begin, rows), rows)
-    stats = state[1][span]
-    near_top = stats[:, :1]
+    near_top = state[1][span]
     top = near_top
     for at, (ref, first, valid) in enumerate(slots):
         s = dot_keys(q, keys_of(ref, first, i, rows))
         held[:, at * rows : (at + 1) * rows] = s
-        best = jnp.max(fold(s, jnp.maximum), axis=1, keepdims=True)
-        top = jnp.maximum(top, best if valid is None else jnp.where(valid, best, -1e30))
+        best = jnp.broadcast_to(jnp.max(fold(s, jnp.maximum), axis=1, keepdims=True), near_top.shape)
+        top = jnp.maximum(top, jnp.where(valid, best, -1e30))
     shrink = jnp.exp2((near_top - top) * FACTOR)
     mixed = state[0][span] * shrink
     total = None
     for at, (ref, first, valid) in enumerate(slots):
-        level = top if valid is None else jnp.where(valid, top, 1e30)
-        w = jnp.exp2((held[:, at * rows : (at + 1) * rows] - level) * FACTOR)
-        mixed += jnp.dot(w.astype(jnp.bfloat16), values_of(ref, first, i, rows), preferred_element_type=jnp.float32)
-        part = fold(w, jnp.add)
-        total = part if total is None else total + part
-    total = jnp.sum(total, axis=1, keepdims=True) + stats[:, HEAD_DIM // 2 : HEAD_DIM // 2 + 1] * shrink
+        level = jnp.where(valid, top, 1e30)
+        parts = []
+        for lane in range(at * rows, (at + 1) * rows, HEAD_DIM):
+            part = jnp.exp2((held[:, lane : lane + HEAD_DIM] - level) * FACTOR)
+            total = part if total is None else total + part
+            parts.append(part.astype(jnp.bfloat16))
+        w = jnp.concatenate(parts, axis=1)
+        mixed += jnp.dot(w, values_of(ref, first, i, rows), preferred_element_type=jnp.float32)
+    total = jnp.broadcast_to(jnp.sum(total, axis=1, keepdims=True), near_top.shape) + state[2][span] * shrink
     return (mixed * (1.0 / total)).astype(jnp.bfloat16)
 
 
-def each_half(heads, body):
-    def step(n, carry):
-        body(lax.shift_right_logical(n, 1), lax.bitwise_and(n, 1))
+def each_head(heads, body):
+    def step(i, carry):
+        body(i)
         return carry
 
-    lax.fori_loop(0, 2 * heads, step, 0)
-
-
-def finish_own(first, queries, state, slots, outs, held):
+    lax.fori_loop(0, heads, step, 0)
+
+
+def finish_own(first, queries, state, slots, outs, rooms):
     piece = outs[0].shape[0]
     rows = 2 * piece
 
-    def body(i, half):
-        q = queries[pl.ds(pl.multiple_of(half * rows, rows), rows), head_lanes(first, i)]
-        value = add_far(q, state, slots, i, (2 * (first + i) + half) * rows, held)
-        for wanted in range(2):
-
-            @pl.when(half == wanted)
-            def _():
-                outs[2 * wanted][:, head_lanes(0, i)] = value[:piece]
-                outs[2 * wanted + 1][:, head_lanes(0, i)] = value[piece:]
-
-    each_half(outs[0].shape[1] // HEAD_DIM, body)
-
-
-def home_kernel(mask, q, mixed, stats, r1, r2, r3, *rest):
-    outs, held = rest[:4], rest[4]
+    def body(i):
+        for half, held in enumerate(rooms):
+            q = queries[half * rows : (half + 1) * rows, head_lanes(first, i)]
+            value = add_far(q, state, slots, i, (2 * (first + i) + half) * rows, held)
+            outs[2 * half][:, head_lanes(0, i)] = value[:piece]
+            outs[2 * half + 1][:, head_lanes(0, i)] = value[piece:]
+
+    each_head(outs[0].shape[1] // HEAD_DIM, body)
+
+
+def home_kernel(mask, q, mixed, tops, totals, r1, r2, r3, *rest):
+    outs, rooms, got, sems = rest[:4], rest[4:6], rest[6:8], rest[8]
     z = lax.axis_index("frame")
     near2 = mask[0, z ^ 2] == 1
 
+    def body(far, valid):
+        copies = [pltpu.make_async_copy(ref, room, sems.at[n]) for n, (ref, room) in enumerate(zip(far, got))]
+        for copy in copies:
+            copy.start()
+        for copy in copies:
+            copy.wait()
+        slots = [(room, 0, ok) for room, ok in zip(got, valid)]
+        finish_own(0, q, (mixed, tops, totals), slots, outs, rooms)
+
     @pl.when(inner_frame())
     def _():
-        finish_own(0, q, (mixed, stats), [(r1, 0, near2)], outs, held)
+        body([r1], [near2])
 
     @pl.when(jnp.logical_not(inner_frame()))
     def _():
-        slots = [(r2, 0, near2), (r3, 0, mask[0, z ^ 3] == 1)]
-        finish_own(0, q, (mixed, stats), slots, outs, held)
-
-
-def guest_kernel(q, mixed, stats, n1m, n2m, n2o, r1, out, held):
+        body([r2, r3], [near2, mask[0, z ^ 3] == 1])
+
+
+def guest_kernel(q, mixed, tops, totals, n1m, n2m, n2o, r1, out, *rooms):
     rows = r1.shape[0]
     z = lax.axis_index("frame")
 
     def told(ref, group):
-        return ref[rows : rows + 1, group * 128 : (group + 1) * 128][:, :1].astype(jnp.float32)
+        return ref[rows : rows + 1, group * 128 : (group + 1) * 128].astype(jnp.float32)
 
     @pl.when(inner_frame())
     def _():
@@ -318,20 +329,21 @@
         picked = told(n2m, 4) == (lax.axis_index("head") // 2).astype(jnp.float32)
         slots = [(n2m, HOME, near2 & picked), (n2o, HOME, near2 & jnp.logical_not(picked)), (r1, 0, near1)]
 
-        def body(i, half):
-            value = add_far(guest_queries((q,), half, i), (mixed, stats), slots, i, (2 * i + half) * rows, held)
-            out[pl.ds(pl.multiple_of(half * rows, rows), rows), head_lanes(0, i)] = value
-
-        each_half(out.shape[1] // HEAD_DIM, body)
-
-
-def rest_kernel(mask, q, mixed, stats, r1, back, *rest):
-    outs, held = rest[:4], rest[4]
+        def body(i):
+            for half, held in enumerate(rooms):
+                value = add_far(guest_queries(q, half, i), (mixed, tops, totals), slots, i, (2 * i + half) * rows, held)
+                out[half * rows : (half + 1) * rows, head_lanes(0, i)] = value
+
+        each_head(out.shape[1] // HEAD_DIM, body)
+
+
+def rest_kernel(mask, q, mixed, tops, totals, r1, back, *rest):
+    outs, rooms = rest[:4], rest[4:]
     z = lax.axis_index("frame")
 
     @pl.when(inner_frame())
     def _():
-        finish_own(HOME, q, (mixed, stats), [(r1, 0, mask[0, z ^ 2] == 1)], outs, held)
+        finish_own(HOME, q, (mixed, tops, totals), [(r1, 0, mask[0, z ^ 2] == 1)], outs, rooms)
 
     @pl.when(jnp.logical_not(inner_frame()))
     def _():
@@ -353,20 +365,24 @@
     )(done, x)
 
 
-def run_kernel(kernel, mask, arrays, outs, rooms, flops):
+def run_kernel(kernel, mask, arrays, outs, room, flops, loose=()):
     scalars = [] if mask is None else [mask]
+    scratch = [pltpu.VMEM(room, jnp.float32)] * 2
+    if loose:
+        scratch += [pltpu.VMEM(loose[0].shape, loose[0].dtype)] * 2 + [pltpu.SemaphoreType.DMA((2,))]
     return pl.pallas_call(
         kernel,
         in_specs=[pl.BlockSpec(memory_space=pltpu.SMEM)] * len(scalars)
-        + [pl.BlockSpec(memory_space=pltpu.VMEM)] * len(arrays),
+        + [pl.BlockSpec(memory_space=pltpu.VMEM)] * len(arrays)
+        + [pl.BlockSpec(memory_space=pl.ANY)] * len(loose),
         out_specs=[pl.BlockSpec(memory_space=pltpu.VMEM)] * len(outs),
         out_shape=[jax.ShapeDtypeStruct(shape, dtype) for shape, dtype in outs],
-        scratch_shapes=[pltpu.VMEM(rooms[1], jnp.float32)] * rooms[0],
+        scratch_shapes=scratch,
         compiler_params=pltpu.CompilerParams(vmem_limit_bytes=10 * 1024 * 1024),
         cost_estimate=pl.CostEstimate(
             flops=flops, bytes_accessed=sum(x.size * 2 for x in arrays), transcendentals=flops // (4 * HEAD_DIM)
         ),
-    )(*scalars, *arrays)
+    )(*scalars, *arrays, *loose)
 
 
 def pack_kernel(copies, width, mask, offset, *refs):
@@ -519,30 +535,30 @@
     r1_home, r1_rest = after(relayed(n1m, n1o, [(0, cut), (cut, width)]), n2m)
     r1_home = across(r1_home)
     swap = along(swapped(n2m, n2o, q), OUTER)
-    r1_rest = across(after(r1_rest, n2o))
 
     def state(count):
-        return [((count * 2 * tile, HEAD_DIM), jnp.float32)] * 2 + [((8, 128), jnp.float32)]
+        return [((count * 2 * tile, HEAD_DIM), jnp.float32)] * 3 + [((8, 128), jnp.float32)]
 
     def flops(chunks, tiles):
         return 4 * chunks * tiles * tile * tile * HEAD_DIM
 
     bf16 = jnp.bfloat16
-    *near, done = run_kernel(
-        functools.partial(near_kernel, 0, ((6, heads), (4, HOME)), own_queries, 1),
+    *near, done, r1_rest = run_kernel(
+        functools.partial(near_kernel, 0, ((6, heads), (4, HOME)), own_queries, True),
         None,
-        [q, mine, other, n1m, n1o, n2m, n2o],
-        state(heads),
-        (2, (tile, 6 * tile)),
+        [q, mine, other, n1m, n1o, n2m, n2o, r1_rest],
+        state(heads) + [(r1_rest.shape, bf16)],
+        (tile, 6 * tile),
         flops(2 * heads, 6),
     )
+    r1_rest = across(r1_rest)
     r3 = along(after(passed(r1_home, done), swap), OUTER)
     *guest_near, _ = run_kernel(
-        functools.partial(near_kernel, HOME, ((4, guests), (0, 0)), guest_queries, 1),
+        functools.partial(near_kernel, HOME, ((4, guests), (0, 0)), guest_queries, False),
         None,
         [swap, mine, other, n1m, n1o],
         state(guests),
-        (2, (tile, 4 * tile)),
+        (tile, 4 * tile),
         flops(2 * guests, 4),
     )
     (back,) = run_kernel(
@@ -550,17 +566,18 @@
         None,
         [swap, *guest_near, n1m, n2m, n2o, r1_rest],
         [((2 * tile, width - cut), bf16)],
-        (1, (tile, 3 * tile)),
+        (tile, 3 * tile),
         flops(2 * guests, 3),
     )
     back = along(back, OUTER)
     out = run_kernel(
         home_kernel,
         pair_mask,
-        [q, *near, r1_home, swap, r3],
+        [q, *near],
         [((rows, cut), bf16)] * 4,
-        (1, (tile, 2 * tile)),
+        (tile, 2 * tile),
         flops(2 * HOME, 2),
+        loose=(r1_home, swap, r3),
     )
     pieces = [(to_head(out[d], d) if d else out[0], d, 0) for d in range(4)]
     out = run_kernel(
@@ -568,7 +585,7 @@
         pair_mask,
         [q, *near, r1_rest, after(back, out[1])],
         [((rows, width - cut), bf16)] * 4,
-        (1, (tile, tile)),
+        (tile, tile),
         flops(2 * guests, 1),
     )
     pieces += [(to_head(out[d], d) if d else out[0], d, cut) for d in range(4)]

time: 83.4 us -> 83.8 us (level)
  local copies, waits for them, and re-layouts: 4.78 us -> 6.09 us
    unnamed x18 -> x22, local copies, waits for them, and re-layouts: 2.4 us -> 3.72 us
where the time goes in v14:
time: 83.8 us; the launch traced here: 83.4 us
  waiting for transfers between devices  39.1 us (47%)
  starting transfers between devices  25.8 us (31%)
  Pallas kernels  11.3 us (13%)
  local copies, waits for them, and re-layouts  6.09 us (7%)
  between operations  0.99 us (1%)
    ppermute x10, waiting for transfers between devices, to_head(): return lax.ppermute(array, 'head', [(i, i ^ d) for i in range(4)])  23.5 us
    ppermute x5, starting transfers between devices, along(): return lax.ppermute(array, 'frame', pairs)  16.1 us
    ppermute x5, waiting for transfers between devices, along(): return lax.ppermute(array, 'frame', pairs)  15.6 us
    pallas_call x5, Pallas kernels, run_kernel(): pl.pallas_call(kernel, in_specs=[pl.BlockSpec(memory_space=pltpu.SMEM)] *...  9.44 us
    ppermute x10, starting transfers between devices, to_head(): return lax.ppermute(array, 'head', [(i, i ^ d) for i in range(4)])  8.99 us
    unnamed x22, local copies, waits for them, and re-layouts  3.72 us
  transfers between devices with their start and end apart: 19, of which 10 were waited for; matrix products, arithmetic and copies ran while one was open for 0% of the time, Pallas kernels for 14%

profile of v14, /device:TPU:0, one launch (start us, length us, event | category | flops | bytes accessed | tf_op | source)
XLA Modules:
  0.0 83.4 jit_solution(13873138005396051210)
XLA Ops:
  0.0 1.5 %constant_dynamic-slice_fusion = (bf16[128,640]{1,0:T(8,128)(2,1)S(1)}, bf16[128,640]{1,0:T(8,128)(2,1)S(1)}, bf16[128,640]{1,0:T(8,128)(2,1)S(1)}, bf16[128,640...) fusion(bf16[128,2560]{1,0:T(8,128)(2,1)} %refs_2_.1, ...), kind=kLoop, calls=%fused_computation.13 | loop fusion | bytes 2621456 | tf_op jit(solution)/shard_map/dynamic_slice | solution.py:490
  1.5 0.1 pad_maximum_fusion.1
  1.6 0.0 copy-start.8
  1.6 0.0 copy-start.9
  1.6 0.5 collective-permute-start
  2.1 1.7 %collective-permute-done = bf16[128,2560]{1,0:T(8,128)(2,1)S(1)} collective-permute-done((bf16[128,2560]{1,0:T(8,128)(2,1)S(1)}, bf16[128,2560]{1,0:T(8,128)(2,1)S(1)}, u32[]{:S(2)}, u32[]{:S(2)}) %collective-permute-start) | collective-permute-done | bytes 655392 | tf_op jit(solution)/shard_map/ppermute | solution.py:499
  4.0 2.9 %collective-permute-start.2 = (bf16[256,1280]{1,0:T(8,128)(2,1)S(1)}, bf16[256,1280]{1,0:T(8,128)(2,1)S(1)}, u32[]{:S(2)}, u32[]{:S(2)}) collective-permute-start(bf16[256,1280]{1,0:T(8,128)(2,1)S(1)} %pad_maximum_fusion.2), channel_id=1, source_target_pairs={{0,2},{1,3},{2,0},{3,1},{4,6},{5,7},{6,4},{7,5},{8,10},{9,11},{10,... | collective-permute-start | bytes 1966088 | tf_op jit(solution)/shard_map/ppermute | solution.py:499
  7.6 0.7 shard_map.55
  8.3 0.1 collective-permute-start.1
  8.4 0.1 pad_maximum_fusion.refs_1_
  8.4 0.6 collective-permute-start.6
  9.0 2.7 %collective-permute-start.4 = (bf16[272,1280]{1,0:T(8,128)(2,1)S(1)}, bf16[272,1280]{1,0:T(8,128)(2,1)S(1)}, u32[]{:S(2)}, u32[]{:S(2)}) collective-permute-start(bf16[272,1280]{1,0:T(8,128)(2,1)S(1)} %pad_maximum_fusion.refs_1_), channel_id=1, source_target_pairs={{0,4},{4,0},{8,12},{12,8},{1,5},{5,1},{9,13},{13,9},{2,6},{6,2},{1... | collective-permute-start | bytes 2088968 | tf_op jit(solution)/shard_map/ppermute | solution.py:502
  11.6 10.3 %collective-permute-done.2.refs_2_ = bf16[256,1280]{1,0:T(8,128)(2,1)S(1)} collective-permute-done((bf16[256,1280]{1,0:T(8,128)(2,1)S(1)}, bf16[256,1280]{1,0:T(8,128)(2,1)S(1)}, u32[]{:S(2)}, u32[]{:S(2)}) %collective-permute-start.2) | collective-permute-done | bytes 655392 | tf_op jit(solution)/shard_map/ppermute | solution.py:499
  21.9 3.4 %collective-permute-start.5 = (bf16[256,1280]{1,0:T(8,128)(2,1)S(1)}, bf16[256,1280]{1,0:T(8,128)(2,1)S(1)}, u32[]{:S(2)}, u32[]{:S(2)}) collective-permute-start(bf16[256,1280]{1,0:T(8,128)(2,1)S(1)} %collective-permute-done.2.refs_2_), channel_id=1, source_target_pairs={{0,4},{4,0},{8,12},{12,8},{1,5},{5,1},{9,13},{13,9},{2,6},{6,2},{1... | collective-permute-start | bytes 1966088 | tf_op jit(solution)/shard_map/ppermute | solution.py:502
  25.4 1.6 %collective-permute-start.3 = (bf16[256,640]{1,0:T(8,128)(2,1)S(1)}, bf16[256,640]{1,0:T(8,128)(2,1)S(1)}, u32[]{:S(2)}, u32[]{:S(2)}) collective-permute-start(bf16[256,640]{1,0:T(8,128)(2,1)S(1)} %pad_maximum_fusion.4), channel_id=1, source_target_pairs={{0,2},{1,3},{2,0},{3,1},{4,6},{5,7},{6,4},{7,5},{8,10},{9,11},{10,... | collective-permute-start | bytes 983048 | tf_op jit(solution)/shard_map/ppermute | solution.py:499
  27.0 6.9 %collective-permute-done.3 = bf16[256,640]{1,0:T(8,128)(2,1)S(1)} collective-permute-done((bf16[256,640]{1,0:T(8,128)(2,1)S(1)}, bf16[256,640]{1,0:T(8,128)(2,1)S(1)}, u32[]{:S(2)}, u32[]{:S(2)}) %collective-permute-start.3) | collective-permute-done | bytes 327712 | tf_op jit(solution)/shard_map/ppermute | solution.py:499
  33.8 0.1 pad_maximum_fusion.3.refs_0_.q
  33.9 7.7 %collective-permute-done.5.other.refs_4_ = bf16[256,1280]{1,0:T(8,128)(2,1)S(1)} collective-permute-done((bf16[256,1280]{1,0:T(8,128)(2,1)S(1)}, bf16[256,1280]{1,0:T(8,128)(2,1)S(1)}, u32[]{:S(2)}, u32[]{:S(2)}) %collective-permute-start.5) | collective-permute-done | bytes 655392 | tf_op jit(solution)/shard_map/ppermute | solution.py:502
  41.7 0.2 shard_map.56
  41.9 0.1 collective-permute-start.8
  41.9 0.1 shard_map.58
  42.0 2.3 %collective-permute-start.9 = (bf16[256,768]{1,0:T(8,128)(2,1)S(1)}, bf16[256,768]{1,0:T(8,128)(2,1)S(1)}, u32[]{:S(2)}, u32[]{:S(2)}) collective-permute-start(bf16[256,768]{1,0:T(8,128)(2,1)S(1)} %shard_map.58), channel_id=1, source_target_pairs={{0,4},{4,0},{8,12},{12,8},{1,5},{5,1},{9,13},{13,9},{2,6},{6,2},{1... | collective-permute-start | bytes 1179656 | tf_op jit(solution)/shard_map/ppermute | solution.py:502
  44.3 2.9 %shard_map.57 = (f32[2560,128]{1,0:T(8,128)S(1)}, f32[2560,128]{1,0:T(8,128)S(1)}, f32[2560,128]{1,0:T(8,128)S(1)}, f32[8,128]{1,0:T(8,128)S(1)}, bf16[256,512]{1,0:T(8,128)(2,1)S(1)}) custom-call(bf16[512,640]{1,0:T(8,128)(2,1)S(1)} %pad_maximum_fusion.3.refs_0_.q, bf16[272,1280]{1,0:T(8,128)(2,1)S(1)} %pad_maximum_fusion.refs_1_, ...), custom_call_target="tpu_custom_call" | custom-call | flops 2013265920 | bytes 4972544 | tf_op jit(solution)/shard_map/pallas_call | solution.py:373
  47.3 0.1 collective-permute-start.14
  47.4 0.9 %shard_map.59 = bf16[256,768]{1,0:T(8,128)(2,1)} custom-call(f32[8,128]{1,0:T(8,128)S(1)} %get-tuple-element.62.done, bf16[256,768]{1,0:T(8,128)(2,1)S(1)} %collective-permute-done.8.x.r1), custom_call_target="tpu_custom_call" | custom-call | tf_op jit(solution)/shard_map/pallas_call | solution.py:359
  48.3 5.2 %collective-permute-done.9.r2.refs_0_.q = bf16[256,768]{1,0:T(8,128)(2,1)S(1)} collective-permute-done((bf16[256,768]{1,0:T(8,128)(2,1)S(1)}, bf16[256,768]{1,0:T(8,128)(2,1)S(1)}, u32[]{:S(2)}, u32[]{:S(2)}) %collective-permute-start.9) | collective-permute-done | bytes 393248 | tf_op jit(solution)/shard_map/ppermute | solution.py:502
  53.6 1.8 %collective-permute-start.10 = (bf16[256,768]{1,0:T(8,128)(2,1)}, bf16[256,768]{1,0:T(8,128)(2,1)}, u32[]{:S(2)}, u32[]{:S(2)}) collective-permute-start(bf16[256,768]{1,0:T(8,128)(2,1)} %shard_map.59), channel_id=1, source_target_pairs={{0,4},{4,0},{8,12},{12,8},{1,5},{5,1},{9,13},{13,9},{2,6},{6,2},{1... | collective-permute-start | bytes 1179656 | tf_op jit(solution)/shard_map/ppermute | solution.py:502
  55.4 0.6 shard_map.61
  56.0 0.7 shard_map.62
  56.7 5.9 %collective-permute-start.15 = (bf16[512,256]{1,0:T(8,128)(2,1)}, bf16[512,256]{1,0:T(8,128)(2,1)}, u32[]{:S(2)}, u32[]{:S(2)}) collective-permute-start(bf16[512,256]{1,0:T(8,128)(2,1)} %shard_map.62), channel_id=1, source_target_pairs={{0,4},{4,0},{8,12},{12,8},{1,5},{5,1},{9,13},{13,9},{2,6},{6,2},{1... | collective-permute-start | bytes 786440 | tf_op jit(solution)/shard_map/ppermute | solution.py:502
  62.6 2.6 %collective-permute-done.10.r3 = bf16[256,768]{1,0:T(8,128)(2,1)} collective-permute-done((bf16[256,768]{1,0:T(8,128)(2,1)}, bf16[256,768]{1,0:T(8,128)(2,1)}, u32[]{:S(2)}, u32[]{:S(2)}) %collective-permute-start.10) | collective-permute-done | bytes 393248 | tf_op jit(solution)/shard_map/ppermute | solution.py:502
  65.2 1.3 %copy-done.1 = f32[2560,128]{1,0:T(8,128)S(1)} copy-done((f32[2560,128]{1,0:T(8,128)S(1)}, f32[2560,128]{1,0:T(8,128)}, u32[]{:S(2)}) %copy-start.1) | copy-done | bytes 1310744
  66.5 1.0 %copy-done.3 = bf16[256,768]{1,0:T(8,128)(2,1)S(1)} copy-done((bf16[256,768]{1,0:T(8,128)(2,1)S(1)}, bf16[256,768]{1,0:T(8,128)(2,1)}, u32[]{:S(2)}) %copy-start.3) | copy-done | bytes 393240
  67.5 1.0 %copy-done.7 = bf16[256,768]{1,0:T(8,128)(2,1)S(1)} copy-done((bf16[256,768]{1,0:T(8,128)(2,1)S(1)}, bf16[256,768]{1,0:T(8,128)(2,1)}, u32[]{:S(2)}) %copy-start.7) | copy-done | bytes 393240
  68.5 4.2 %shard_map.60 = (bf16[128,384]{1,0:T(8,128)(2,1)S(1)}, bf16[128,384]{1,0:T(8,128)(2,1)S(1)}, bf16[128,384]{1,0:T(8,128)(2,1)S(1)}, bf16[128,384]{1,0:T(8,128)(2,1)S(1)}) custom-call(s32[1,4]{1,0:T(1,128)S(1)} %copy-done.9, bf16[512,640]{1,0:T(8,128)(2,1)S(1)} %pad_maximum_fusion.3.refs_0_.q, f32[2560,128]{1,0:T(8,128)S(1)} %get-tuple-element.58.mixed, ...), custom_call_target="tpu_custom_call" | custom-call | flops 402653184 | bytes 2621440 | tf_op jit(solution)/shard_map/pallas_call | solution.py:373
  72.7 0.1 collective-permute-start.11
  72.8 0.6 collective-permute-start.12
  73.4 1.2 %collective-permute-start.13 = (bf16[128,384]{1,0:T(8,128)(2,1)S(1)}, bf16[128,384]{1,0:T(8,128)(2,1)S(1)}, u32[]{:S(2)}, u32[]{:S(2)}) collective-permute-start(bf16[128,384]{1,0:T(8,128)(2,1)S(1)} %get-tuple-element.67), channel_id=1, source_target_pairs={{0,3},{1,2},{2,1},{3,0},{4,7},{5,6},{6,5},{7,4},{8,11},{9,10},{10,... | collective-permute-start | bytes 294920 | tf_op jit(solution)/shard_map/ppermute | solution.py:499
  74.6 1.0 %shard_map.63 = (bf16[128,256]{1,0:T(8,128)(2,1)S(1)}, bf16[128,256]{1,0:T(8,128)(2,1)S(1)}, bf16[128,256]{1,0:T(8,128)(2,1)S(1)}, bf16[128,256]{1,0:T(8,128)(2,1)S(1)}) custom-call(s32[1,4]{1,0:T(1,128)S(1)} %copy-done.9, bf16[512,640]{1,0:T(8,128)(2,1)S(1)} %pad_maximum_fusion.3.refs_0_.q, f32[2560,128]{1,0:T(8,128)S(1)} %get-tuple-element.58.mixed, ...), custom_call_target="tpu_custom_call" | custom-call | flops 134217728 | bytes 3145728 | tf_op jit(solution)/shard_map/pallas_call | solution.py:373
  75.6 0.4 collective-permute-start.16
  76.1 0.5 collective-permute-start.17
  76.7 1.0 %collective-permute-start.18 = (bf16[128,256]{1,0:T(8,128)(2,1)S(1)}, bf16[128,256]{1,0:T(8,128)(2,1)S(1)}, u32[]{:S(2)}, u32[]{:S(2)}) collective-permute-start(bf16[128,256]{1,0:T(8,128)(2,1)S(1)} %get-tuple-element.76), channel_id=1, source_target_pairs={{0,3},{1,2},{2,1},{3,0},{4,7},{5,6},{6,5},{7,4},{8,11},{9,10},{10,... | collective-permute-start | bytes 196616 | tf_op jit(solution)/shard_map/ppermute | solution.py:499
  77.7 0.7 collective-permute-done.12
  78.5 1.2 %collective-permute-done.13 = bf16[128,384]{1,0:T(8,128)(2,1)S(1)} collective-permute-done((bf16[128,384]{1,0:T(8,128)(2,1)S(1)}, bf16[128,384]{1,0:T(8,128)(2,1)S(1)}, u32[]{:S(2)}, u32[]{:S(2)}) %collective-permute-start.13) | collective-permute-done | bytes 98336 | tf_op jit(solution)/shard_map/ppermute | solution.py:499
  79.7 2.3 %collective-permute-done.17 = bf16[128,256]{1,0:T(8,128)(2,1)S(1)} collective-permute-done((bf16[128,256]{1,0:T(8,128)(2,1)S(1)}, bf16[128,256]{1,0:T(8,128)(2,1)S(1)}, u32[]{:S(2)}, u32[]{:S(2)}) %collective-permute-start.17) | collective-permute-done | bytes 65568 | tf_op jit(solution)/shard_map/ppermute | solution.py:499
  82.0 0.5 collective-permute-done.18
  82.4 0.4 copy-done.10
  82.8 0.6 constant_dynamic-update-slice_fusion
  (38 shorter events, 0.4 us)
Async XLA Ops:
  1.6 6.0 %copy-start.4 = (bf16[128,2560]{1,0:T(8,128)(2,1)S(1)}, bf16[128,2560]{1,0:T(8,128)(2,1)}, u32[]{:S(2)}) copy-start(bf16[128,2560]{1,0:T(8,128)(2,1)} %refs_1_.1) | copy-start | bytes 1966084
  1.6 6.0 %copy-start.5 = (bf16[128,2560]{1,0:T(8,128)(2,1)S(1)}, bf16[128,2560]{1,0:T(8,128)(2,1)}, u32[]{:S(2)}) copy-start(bf16[128,2560]{1,0:T(8,128)(2,1)} %refs_2_.1) | copy-start | bytes 1966084
  1.6 6.0 %copy-start.8 = (bf16[128,2560]{1,0:T(8,128)(2,1)S(1)}, bf16[128,2560]{1,0:T(8,128)(2,1)}, u32[]{:S(2)}) copy-start(bf16[128,2560]{1,0:T(8,128)(2,1)} %refs_0_.1) | copy-start | bytes 1966084
  1.6 6.0 %copy-start.9 = (s32[1,4]{1,0:T(1,128)S(1)}, s32[1,4]{1,0:T(1,128)}, u32[]{:S(2)}) copy-start(s32[1,4]{1,0:T(1,128)} %mask.5) | copy-start | bytes 52
  1.6 2.2 %collective-permute-start = (bf16[128,2560]{1,0:T(8,128)(2,1)S(1)}, bf16[128,2560]{1,0:T(8,128)(2,1)S(1)}, u32[]{:S(2)}, u32[]{:S(2)}) collective-permute-start(bf16[128,2560]{1,0:T(8,128)(2,1)S(1)} %pad_maximum_fusion.1), channel_id=1, source_target_pairs={{0,1},{1,0},{2,3},{3,2},{4,5},{5,4},{6,7},{7,6},{8,9},{9,8},{10,11... | collective-permute-start | bytes 1966088 | tf_op jit(solution)/shard_map/ppermute | solution.py:499
  4.0 18.0 %collective-permute-start.2 = (bf16[256,1280]{1,0:T(8,128)(2,1)S(1)}, bf16[256,1280]{1,0:T(8,128)(2,1)S(1)}, u32[]{:S(2)}, u32[]{:S(2)}) collective-permute-start(bf16[256,1280]{1,0:T(8,128)(2,1)S(1)} %pad_maximum_fusion.2), channel_id=1, source_target_pairs={{0,2},{1,3},{2,0},{3,1},{4,6},{5,7},{6,4},{7,5},{8,10},{9,11},{10,... | collective-permute-start | bytes 1966088 | tf_op jit(solution)/shard_map/ppermute | solution.py:499
  8.3 17.1 %collective-permute-start.1 = (bf16[128,1280]{1,0:T(8,128)(2,1)S(1)}, bf16[128,1280]{1,0:T(8,128)(2,1)S(1)}, u32[]{:S(2)}, u32[]{:S(2)}) collective-permute-start(bf16[128,1280]{1,0:T(8,128)(2,1)S(1)} %get-tuple-element.47), channel_id=1, source_target_pairs={{0,1},{1,0},{2,3},{3,2},{4,5},{5,4},{6,7},{7,6},{8,9},{9,8},{10,11... | collective-permute-start | bytes 983048 | tf_op jit(solution)/shard_map/ppermute | solution.py:499
  8.4 33.4 %collective-permute-start.6 = (bf16[272,1280]{1,0:T(8,128)(2,1)S(1)}, bf16[272,1280]{1,0:T(8,128)(2,1)S(1)}, u32[]{:S(2)}, u32[]{:S(2)}) collective-permute-start(bf16[272,1280]{1,0:T(8,128)(2,1)S(1)} %pad_maximum_fusion.refs_1_), channel_id=1, source_target_pairs={{0,1},{1,0},{2,3},{3,2},{4,8},{5,9},{6,10},{7,11},{8,4},{9,5},{10,... | collective-permute-start | bytes 2088968 | tf_op jit(solution)/shard_map/ppermute | solution.py:506
  9.0 24.9 %collective-permute-start.4 = (bf16[272,1280]{1,0:T(8,128)(2,1)S(1)}, bf16[272,1280]{1,0:T(8,128)(2,1)S(1)}, u32[]{:S(2)}, u32[]{:S(2)}) collective-permute-start(bf16[272,1280]{1,0:T(8,128)(2,1)S(1)} %pad_maximum_fusion.refs_1_), channel_id=1, source_target_pairs={{0,4},{4,0},{8,12},{12,8},{1,5},{5,1},{9,13},{13,9},{2,6},{6,2},{1... | collective-permute-start | bytes 2088968 | tf_op jit(solution)/shard_map/ppermute | solution.py:502
  21.9 20.0 %collective-permute-start.7 = (bf16[256,1280]{1,0:T(8,128)(2,1)S(1)}, bf16[256,1280]{1,0:T(8,128)(2,1)S(1)}, u32[]{:S(2)}, u32[]{:S(2)}) collective-permute-start(bf16[256,1280]{1,0:T(8,128)(2,1)S(1)} %collective-permute-done.2.refs_2_), channel_id=1, source_target_pairs={{0,1},{1,0},{2,3},{3,2},{4,8},{5,9},{6,10},{7,11},{8,4},{9,5},{10,... | collective-permute-start | bytes 1966088 | tf_op jit(solution)/shard_map/ppermute | solution.py:506
  21.9 19.7 %collective-permute-start.5 = (bf16[256,1280]{1,0:T(8,128)(2,1)S(1)}, bf16[256,1280]{1,0:T(8,128)(2,1)S(1)}, u32[]{:S(2)}, u32[]{:S(2)}) collective-permute-start(bf16[256,1280]{1,0:T(8,128)(2,1)S(1)} %collective-permute-done.2.refs_2_), channel_id=1, source_target_pairs={{0,4},{4,0},{8,12},{12,8},{1,5},{5,1},{9,13},{13,9},{2,6},{6,2},{1... | collective-permute-start | bytes 1966088 | tf_op jit(solution)/shard_map/ppermute | solution.py:502
  25.4 8.4 %collective-permute-start.3 = (bf16[256,640]{1,0:T(8,128)(2,1)S(1)}, bf16[256,640]{1,0:T(8,128)(2,1)S(1)}, u32[]{:S(2)}, u32[]{:S(2)}) collective-permute-start(bf16[256,640]{1,0:T(8,128)(2,1)S(1)} %pad_maximum_fusion.4), channel_id=1, source_target_pairs={{0,2},{1,3},{2,0},{3,1},{4,6},{5,7},{6,4},{7,5},{8,10},{9,11},{10,... | collective-permute-start | bytes 983048 | tf_op jit(solution)/shard_map/ppermute | solution.py:499
  41.9 5.5 %collective-permute-start.8 = (bf16[256,768]{1,0:T(8,128)(2,1)S(1)}, bf16[256,768]{1,0:T(8,128)(2,1)S(1)}, u32[]{:S(2)}, u32[]{:S(2)}) collective-permute-start(bf16[256,768]{1,0:T(8,128)(2,1)S(1)} %get-tuple-element.61), channel_id=1, source_target_pairs={{0,1},{1,0},{2,3},{3,2},{4,8},{5,9},{6,10},{7,11},{8,4},{9,5},{10,... | collective-permute-start | bytes 1179656 | tf_op jit(solution)/shard_map/ppermute | solution.py:506
  42.0 11.6 %collective-permute-start.9 = (bf16[256,768]{1,0:T(8,128)(2,1)S(1)}, bf16[256,768]{1,0:T(8,128)(2,1)S(1)}, u32[]{:S(2)}, u32[]{:S(2)}) collective-permute-start(bf16[256,768]{1,0:T(8,128)(2,1)S(1)} %shard_map.58), channel_id=1, source_target_pairs={{0,4},{4,0},{8,12},{12,8},{1,5},{5,1},{9,13},{13,9},{2,6},{6,2},{1... | collective-permute-start | bytes 1179656 | tf_op jit(solution)/shard_map/ppermute | solution.py:502
  47.3 8.7 %copy-start = (f32[2560,128]{1,0:T(8,128)}, f32[2560,128]{1,0:T(8,128)S(1)}, u32[]{:S(2)}) copy-start(f32[2560,128]{1,0:T(8,128)S(1)} %get-tuple-element.60.totals) | copy-start | bytes 3932164
  47.3 8.7 %collective-permute-start.14 = (bf16[256,512]{1,0:T(8,128)(2,1)S(1)}, bf16[256,512]{1,0:T(8,128)(2,1)S(1)}, u32[]{:S(2)}, u32[]{:S(2)}) collective-permute-start(bf16[256,512]{1,0:T(8,128)(2,1)S(1)} %get-tuple-element.68), channel_id=1, source_target_pairs={{0,1},{1,0},{2,3},{3,2},{4,8},{5,9},{6,10},{7,11},{8,4},{9,5},{10,... | collective-permute-start | bytes 786440 | tf_op jit(solution)/shard_map/ppermute | solution.py:506
  47.4 8.6 %copy-start.6 = (bf16[256,768]{1,0:T(8,128)(2,1)}, bf16[256,768]{1,0:T(8,128)(2,1)S(1)}, u32[]{:S(2)}) copy-start(bf16[256,768]{1,0:T(8,128)(2,1)S(1)} %collective-permute-done.8.x.r1) | copy-start | bytes 1179652
  53.6 2.4 %copy-start.2 = (bf16[256,768]{1,0:T(8,128)(2,1)}, bf16[256,768]{1,0:T(8,128)(2,1)S(1)}, u32[]{:S(2)}) copy-start(bf16[256,768]{1,0:T(8,128)(2,1)S(1)} %collective-permute-done.9.r2.refs_0_.q) | copy-start | bytes 1179652
  53.6 11.6 %collective-permute-start.10 = (bf16[256,768]{1,0:T(8,128)(2,1)}, bf16[256,768]{1,0:T(8,128)(2,1)}, u32[]{:S(2)}, u32[]{:S(2)}) collective-permute-start(bf16[256,768]{1,0:T(8,128)(2,1)} %shard_map.59), channel_id=1, source_target_pairs={{0,4},{4,0},{8,12},{12,8},{1,5},{5,1},{9,13},{13,9},{2,6},{6,2},{1... | collective-permute-start | bytes 1179656 | tf_op jit(solution)/shard_map/ppermute | solution.py:502
  56.7 16.1 %collective-permute-start.15 = (bf16[512,256]{1,0:T(8,128)(2,1)}, bf16[512,256]{1,0:T(8,128)(2,1)}, u32[]{:S(2)}, u32[]{:S(2)}) collective-permute-start(bf16[512,256]{1,0:T(8,128)(2,1)} %shard_map.62), channel_id=1, source_target_pairs={{0,4},{4,0},{8,12},{12,8},{1,5},{5,1},{9,13},{13,9},{2,6},{6,2},{1... | collective-permute-start | bytes 786440 | tf_op jit(solution)/shard_map/ppermute | solution.py:502
  65.2 1.3 %copy-start.1 = (f32[2560,128]{1,0:T(8,128)S(1)}, f32[2560,128]{1,0:T(8,128)}, u32[]{:S(2)}) copy-start(f32[2560,128]{1,0:T(8,128)} %copy-done) | copy-start | bytes 3932164
  66.5 1.0 %copy-start.3 = (bf16[256,768]{1,0:T(8,128)(2,1)S(1)}, bf16[256,768]{1,0:T(8,128)(2,1)}, u32[]{:S(2)}) copy-start(bf16[256,768]{1,0:T(8,128)(2,1)} %copy-done.2) | copy-start | bytes 1179652
  67.5 1.0 %copy-start.7 = (bf16[256,768]{1,0:T(8,128)(2,1)S(1)}, bf16[256,768]{1,0:T(8,128)(2,1)}, u32[]{:S(2)}) copy-start(bf16[256,768]{1,0:T(8,128)(2,1)} %copy-done.6) | copy-start | bytes 1179652
  72.7 4.0 %collective-permute-start.11 = (bf16[128,384]{1,0:T(8,128)(2,1)S(1)}, bf16[128,384]{1,0:T(8,128)(2,1)S(1)}, u32[]{:S(2)}, u32[]{:S(2)}) collective-permute-start(bf16[128,384]{1,0:T(8,128)(2,1)S(1)} %get-tuple-element.65), channel_id=1, source_target_pairs={{0,1},{1,0},{2,3},{3,2},{4,5},{5,4},{6,7},{7,6},{8,9},{9,8},{10,11... | collective-permute-start | bytes 294920 | tf_op jit(solution)/shard_map/ppermute | solution.py:499
  72.8 5.7 %collective-permute-start.12 = (bf16[128,384]{1,0:T(8,128)(2,1)S(1)}, bf16[128,384]{1,0:T(8,128)(2,1)S(1)}, u32[]{:S(2)}, u32[]{:S(2)}) collective-permute-start(bf16[128,384]{1,0:T(8,128)(2,1)S(1)} %get-tuple-element.66), channel_id=1, source_target_pairs={{0,2},{1,3},{2,0},{3,1},{4,6},{5,7},{6,4},{7,5},{8,10},{9,11},{10,... | collective-permute-start | bytes 294920 | tf_op jit(solution)/shard_map/ppermute | solution.py:499
  73.4 6.2 %collective-permute-start.13 = (bf16[128,384]{1,0:T(8,128)(2,1)S(1)}, bf16[128,384]{1,0:T(8,128)(2,1)S(1)}, u32[]{:S(2)}, u32[]{:S(2)}) collective-permute-start(bf16[128,384]{1,0:T(8,128)(2,1)S(1)} %get-tuple-element.67), channel_id=1, source_target_pairs={{0,3},{1,2},{2,1},{3,0},{4,7},{5,6},{6,5},{7,4},{8,11},{9,10},{10,... | collective-permute-start | bytes 294920 | tf_op jit(solution)/shard_map/ppermute | solution.py:499
  75.6 4.0 %collective-permute-start.16 = (bf16[128,256]{1,0:T(8,128)(2,1)S(1)}, bf16[128,256]{1,0:T(8,128)(2,1)S(1)}, u32[]{:S(2)}, u32[]{:S(2)}) collective-permute-start(bf16[128,256]{1,0:T(8,128)(2,1)S(1)} %get-tuple-element.74), channel_id=1, source_target_pairs={{0,1},{1,0},{2,3},{3,2},{4,5},{5,4},{6,7},{7,6},{8,9},{9,8},{10,11... | collective-permute-start | bytes 196616 | tf_op jit(solution)/shard_map/ppermute | solution.py:499
  76.1 5.9 %collective-permute-start.17 = (bf16[128,256]{1,0:T(8,128)(2,1)S(1)}, bf16[128,256]{1,0:T(8,128)(2,1)S(1)}, u32[]{:S(2)}, u32[]{:S(2)}) collective-permute-start(bf16[128,256]{1,0:T(8,128)(2,1)S(1)} %get-tuple-element.75), channel_id=1, source_target_pairs={{0,2},{1,3},{2,0},{3,1},{4,6},{5,7},{6,4},{7,5},{8,10},{9,11},{10,... | collective-permute-start | bytes 196616 | tf_op jit(solution)/shard_map/ppermute | solution.py:499
  76.7 5.7 %collective-permute-start.18 = (bf16[128,256]{1,0:T(8,128)(2,1)S(1)}, bf16[128,256]{1,0:T(8,128)(2,1)S(1)}, u32[]{:S(2)}, u32[]{:S(2)}) collective-permute-start(bf16[128,256]{1,0:T(8,128)(2,1)S(1)} %get-tuple-element.76), channel_id=1, source_target_pairs={{0,3},{1,2},{2,1},{3,0},{4,7},{5,6},{6,5},{7,4},{8,11},{9,10},{10,... | collective-permute-start | bytes 196616 | tf_op jit(solution)/shard_map/ppermute | solution.py:499
  82.0 0.8 %copy-start.10 = (bf16[128,2560]{1,0:T(8,128)(2,1)}, bf16[128,2560]{1,0:T(8,128)(2,1)S(1)}, u32[]{:S(2)}) copy-start(bf16[128,2560]{1,0:T(8,128)(2,1)S(1)} %constant_dynamic-update-slice_fusion.1) | copy-start | bytes 1966084

commit v15 on v14

--- a/solution.py
+++ b/solution.py
@@ -190,14 +190,14 @@
 
 
 def near_kernel(first, counts, queries_of, carries, *refs):
-    n_outs = 5 if carries else 4
+    n_outs = 4 if carries else 3
     ins, outs, rooms = refs[: -2 - n_outs], refs[-2 - n_outs : -2], refs[-2:]
     queries, tiles = ins[0], ins[1:]
-    mixed_out, tops, totals, done = outs[:4]
+    mixed_out, levels, done = outs[:3]
     rows = rooms[0].shape[0]
     done[...] = jnp.zeros_like(done)
     if carries:
-        outs[4][...] = ins[-1][...]
+        outs[3][...] = ins[-1][...]
 
     def one_head(used, i):
         found = []
@@ -219,9 +219,9 @@
                 mixed = mix if mixed is None else mixed + mix
                 total = part if total is None else total + part
             span = pl.ds(pl.multiple_of((2 * i + half) * rows, rows), rows)
-            mixed_out[span] = mixed
-            tops[span] = jnp.broadcast_to(top, (rows, HEAD_DIM))
-            totals[span] = jnp.broadcast_to(jnp.sum(total, axis=1, keepdims=True), (rows, HEAD_DIM))
+            total = jnp.broadcast_to(jnp.sum(total, axis=1, keepdims=True), (rows, HEAD_DIM))
+            mixed_out[span] = mixed * (1.0 / total)
+            levels[span] = jnp.broadcast_to(top, (rows, HEAD_DIM)) * FACTOR + jnp.log2(total)
 
     for wanted, (n_tiles, n_heads) in zip((True, False), counts):
         if n_heads:
@@ -244,29 +244,36 @@
     return ref[:, head_lanes(half * HOME, i)]
 
 
+def far_tile(ref, first, valid):
+    return functools.partial(keys_of, ref, first), functools.partial(values_of, ref, first), valid
+
+
+def far_pair(keys, values, valid):
+    return functools.partial(keys_of, keys, 0), functools.partial(keys_of, values, 0), valid
+
+
 def add_far(q, state, slots, i, begin, held):
     rows = q.shape[0]
     span = pl.ds(pl.multiple_of(begin, rows), rows)
-    near_top = state[1][span]
-    top = near_top
-    for at, (ref, first, valid) in enumerate(slots):
-        s = dot_keys(q, keys_of(ref, first, i, rows))
+    near_level = state[1][span]
+    level = near_level
+    for at, (keys, _, valid) in enumerate(slots):
+        s = dot_keys(q, keys(i, rows)) * FACTOR
         held[:, at * rows : (at + 1) * rows] = s
-        best = jnp.broadcast_to(jnp.max(fold(s, jnp.maximum), axis=1, keepdims=True), near_top.shape)
-        top = jnp.maximum(top, jnp.where(valid, best, -1e30))
-    shrink = jnp.exp2((near_top - top) * FACTOR)
+        best = jnp.broadcast_to(jnp.max(fold(s, jnp.maximum), axis=1, keepdims=True), near_level.shape)
+        level = jnp.maximum(level, jnp.where(valid, best, -1e30))
+    shrink = jnp.exp2(near_level - level)
     mixed = state[0][span] * shrink
     total = None
-    for at, (ref, first, valid) in enumerate(slots):
-        level = jnp.where(valid, top, 1e30)
+    for at, (_, values, valid) in enumerate(slots):
+        used = jnp.where(valid, level, 1e30)
         parts = []
         for lane in range(at * rows, (at + 1) * rows, HEAD_DIM):
-            part = jnp.exp2((held[:, lane : lane + HEAD_DIM] - level) * FACTOR)
+            part = jnp.exp2(held[:, lane : lane + HEAD_DIM] - used)
             total = part if total is None else total + part
             parts.append(part.astype(jnp.bfloat16))
-        w = jnp.concatenate(parts, axis=1)
-        mixed += jnp.dot(w, values_of(ref, first, i, rows), preferred_element_type=jnp.float32)
-    total = jnp.broadcast_to(jnp.sum(total, axis=1, keepdims=True), near_top.shape) + state[2][span] * shrink
+        mixed += jnp.dot(jnp.concatenate(parts, axis=1), values(i, rows), preferred_element_type=jnp.float32)
+    total = jnp.broadcast_to(jnp.sum(total, axis=1, keepdims=True), near_level.shape) + shrink
     return (mixed * (1.0 / total)).astype(jnp.bfloat16)
 
 
@@ -292,30 +299,22 @@
     each_head(outs[0].shape[1] // HEAD_DIM, body)
 
 
-def home_kernel(mask, q, mixed, tops, totals, r1, r2, r3, *rest):
-    outs, rooms, got, sems = rest[:4], rest[4:6], rest[6:8], rest[8]
+def home_kernel(mask, q, mixed, levels, r1k, r1v, r2, r3k, r3v, *rest):
+    outs, rooms = rest[:4], rest[4:]
     z = lax.axis_index("frame")
     near2 = mask[0, z ^ 2] == 1
 
-    def body(far, valid):
-        copies = [pltpu.make_async_copy(ref, room, sems.at[n]) for n, (ref, room) in enumerate(zip(far, got))]
-        for copy in copies:
-            copy.start()
-        for copy in copies:
-            copy.wait()
-        slots = [(room, 0, ok) for room, ok in zip(got, valid)]
-        finish_own(0, q, (mixed, tops, totals), slots, outs, rooms)
-
     @pl.when(inner_frame())
     def _():
-        body([r1], [near2])
+        finish_own(0, q, (mixed, levels), [far_pair(r1k, r1v, near2)], outs, rooms)
 
     @pl.when(jnp.logical_not(inner_frame()))
     def _():
-        body([r2, r3], [near2, mask[0, z ^ 3] == 1])
-
-
-def guest_kernel(q, mixed, tops, totals, n1m, n2m, n2o, r1, out, *rooms):
+        slots = [far_tile(r2, 0, near2), far_pair(r3k, r3v, mask[0, z ^ 3] == 1)]
+        finish_own(0, q, (mixed, levels), slots, outs, rooms)
+
+
+def guest_kernel(q, mixed, levels, n1m, n2m, n2o, r1, out, *rooms):
     rows = r1.shape[0]
     z = lax.axis_index("frame")
 
@@ -327,23 +326,27 @@
         near2 = jnp.where(z == 1, told(n1m, 2), told(n1m, 1)) > 0.5
         near1 = jnp.where(z == 1, told(n1m, 3), told(n1m, 0)) > 0.5
         picked = told(n2m, 4) == (lax.axis_index("head") // 2).astype(jnp.float32)
-        slots = [(n2m, HOME, near2 & picked), (n2o, HOME, near2 & jnp.logical_not(picked)), (r1, 0, near1)]
+        slots = [
+            far_tile(n2m, HOME, near2 & picked),
+            far_tile(n2o, HOME, near2 & jnp.logical_not(picked)),
+            far_tile(r1, 0, near1),
+        ]
 
         def body(i):
             for half, held in enumerate(rooms):
-                value = add_far(guest_queries(q, half, i), (mixed, tops, totals), slots, i, (2 * i + half) * rows, held)
+                value = add_far(guest_queries(q, half, i), (mixed, levels), slots, i, (2 * i + half) * rows, held)
                 out[half * rows : (half + 1) * rows, head_lanes(0, i)] = value
 
         each_head(out.shape[1] // HEAD_DIM, body)
 
 
-def rest_kernel(mask, q, mixed, tops, totals, r1, back, *rest):
+def rest_kernel(mask, q, mixed, levels, r1, back, *rest):
     outs, rooms = rest[:4], rest[4:]
     z = lax.axis_index("frame")
 
     @pl.when(inner_frame())
     def _():
-        finish_own(HOME, q, (mixed, tops, totals), [(r1, 0, mask[0, z ^ 2] == 1)], outs, rooms)
+        finish_own(HOME, q, (mixed, levels), [far_tile(r1, 0, mask[0, z ^ 2] == 1)], outs, rooms)
 
     @pl.when(jnp.logical_not(inner_frame()))
     def _():
@@ -351,38 +354,36 @@
             out[...] = back[d * out.shape[0] : (d + 1) * out.shape[0]]
 
 
-def pass_kernel(done, x, out):
-    out[...] = x[...]
-
-
-def passed(x, done):
+def pass_kernel(done, *refs):
+    half = len(refs) // 2
+    for x, out in zip(refs[:half], refs[half:]):
+        out[...] = x[...]
+
+
+def passed(done, *arrays):
     return pl.pallas_call(
         pass_kernel,
-        in_specs=[pl.BlockSpec(memory_space=pltpu.VMEM)] * 2,
-        out_specs=pl.BlockSpec(memory_space=pltpu.VMEM),
-        out_shape=jax.ShapeDtypeStruct(x.shape, x.dtype),
+        in_specs=[pl.BlockSpec(memory_space=pltpu.VMEM)] * (1 + len(arrays)),
+        out_specs=[pl.BlockSpec(memory_space=pltpu.VMEM)] * len(arrays),
+        out_shape=[jax.ShapeDtypeStruct(x.shape, x.dtype) for x in arrays],
         compiler_params=pltpu.CompilerParams(vmem_limit_bytes=4 * 1024 * 1024),
-    )(done, x)
-
-
-def run_kernel(kernel, mask, arrays, outs, room, flops, loose=()):
+    )(done, *arrays)
+
+
+def run_kernel(kernel, mask, arrays, outs, room, flops, grant):
     scalars = [] if mask is None else [mask]
-    scratch = [pltpu.VMEM(room, jnp.float32)] * 2
-    if loose:
-        scratch += [pltpu.VMEM(loose[0].shape, loose[0].dtype)] * 2 + [pltpu.SemaphoreType.DMA((2,))]
     return pl.pallas_call(
         kernel,
         in_specs=[pl.BlockSpec(memory_space=pltpu.SMEM)] * len(scalars)
-        + [pl.BlockSpec(memory_space=pltpu.VMEM)] * len(arrays)
-        + [pl.BlockSpec(memory_space=pl.ANY)] * len(loose),
+        + [pl.BlockSpec(memory_space=pltpu.VMEM)] * len(arrays),
         out_specs=[pl.BlockSpec(memory_space=pltpu.VMEM)] * len(outs),
         out_shape=[jax.ShapeDtypeStruct(shape, dtype) for shape, dtype in outs],
-        scratch_shapes=scratch,
-        compiler_params=pltpu.CompilerParams(vmem_limit_bytes=10 * 1024 * 1024),
+        scratch_shapes=[pltpu.VMEM(room, jnp.float32)] * 2,
+        compiler_params=pltpu.CompilerParams(vmem_limit_bytes=grant * 1024 * 1024),
         cost_estimate=pl.CostEstimate(
             flops=flops, bytes_accessed=sum(x.size * 2 for x in arrays), transcendentals=flops // (4 * HEAD_DIM)
         ),
-    )(*scalars, *arrays, *loose)
+    )(*scalars, *arrays)
 
 
 def pack_kernel(copies, width, mask, offset, *refs):
@@ -427,14 +428,15 @@
 
 def relayed_kernel(parts, mine, other, *outs):
     tile = other.shape[0]
-    half = other.shape[1] // 2
     offset = jnp.max(mine[tile : tile + INFO_ROWS, 4 * 128 : 5 * 128].astype(jnp.float32))
     here = offset == (lax.axis_index("head") // 2).astype(jnp.float32)
 
     def take(ref):
-        for (begin, end), out in zip(parts, outs):
-            out[:, : end - begin] = ref[:tile, begin:end]
-            out[:, end - begin :] = ref[:tile, half + begin : half + end]
+        for spans, out in zip(parts, outs):
+            at = 0
+            for begin, end in spans:
+                out[:, at : at + end - begin] = ref[:tile, begin:end]
+                at += end - begin
 
     @pl.when(here)
     def _():
@@ -446,11 +448,12 @@
 
 
 def relayed(mine, other, parts):
+    widths = [sum(end - begin for begin, end in spans) for spans in parts]
     return pl.pallas_call(
         functools.partial(relayed_kernel, parts),
         in_specs=[pl.BlockSpec(memory_space=pltpu.VMEM)] * 2,
         out_specs=[pl.BlockSpec(memory_space=pltpu.VMEM)] * len(parts),
-        out_shape=[jax.ShapeDtypeStruct((other.shape[0], 2 * (end - begin)), other.dtype) for begin, end in parts],
+        out_shape=[jax.ShapeDtypeStruct((other.shape[0], width), other.dtype) for width in widths],
         compiler_params=pltpu.CompilerParams(vmem_limit_bytes=4 * 1024 * 1024),
     )(mine, other)
 
@@ -460,7 +463,8 @@
 
     @pl.when(inner_frame())
     def _():
-        relayed_kernel([(0, cut)], mine, other, out)
+        half = other.shape[1] // 2
+        relayed_kernel([[(0, cut), (half, half + cut)]], mine, other, out)
 
     @pl.when(jnp.logical_not(inner_frame()))
     def _():
@@ -532,27 +536,33 @@
     tile = 2 * rows
     cut = HOME * HEAD_DIM
     guests = heads - HOME
-    r1_home, r1_rest = after(relayed(n1m, n1o, [(0, cut), (cut, width)]), n2m)
-    r1_home = across(r1_home)
+    r1k, r1v, r1_rest = after(
+        relayed(n1m, n1o, [[(0, cut)], [(width, width + cut)], [(cut, width), (width + cut, 2 * width)]]), n2m
+    )
+    r1k = across(r1k)
     swap = along(swapped(n2m, n2o, q), OUTER)
+    r1v = across(after(r1v, n2o))
 
     def state(count):
-        return [((count * 2 * tile, HEAD_DIM), jnp.float32)] * 3 + [((8, 128), jnp.float32)]
+        return [((count * 2 * tile, HEAD_DIM), jnp.float32)] * 2 + [((8, 128), jnp.float32)]
 
     def flops(chunks, tiles):
         return 4 * chunks * tiles * tile * tile * HEAD_DIM
 
     bf16 = jnp.bfloat16
-    *near, done, r1_rest = run_kernel(
-        functools.partial(near_kernel, 0, ((6, heads), (4, HOME)), own_queries, True),
+    *near, done = run_kernel(
+        functools.partial(near_kernel, 0, ((6, heads), (4, HOME)), own_queries, False),
         None,
-        [q, mine, other, n1m, n1o, n2m, n2o, r1_rest],
-        state(heads) + [(r1_rest.shape, bf16)],
+        [q, mine, other, n1m, n1o, n2m, n2o],
+        state(heads),
         (tile, 6 * tile),
         flops(2 * heads, 6),
-    )
+        8,
+    )
+    r3k, r1_rest = passed(done, r1k, r1_rest)
+    r3k = along(r3k, OUTER)
     r1_rest = across(r1_rest)
-    r3 = along(after(passed(r1_home, done), swap), OUTER)
+    r3v = along(after(r1v, swap), OUTER)
     *guest_near, _ = run_kernel(
         functools.partial(near_kernel, HOME, ((4, guests), (0, 0)), guest_queries, False),
         None,
@@ -560,6 +570,7 @@
         state(guests),
         (tile, 4 * tile),
         flops(2 * guests, 4),
+        6,
     )
     (back,) = run_kernel(
         guest_kernel,
@@ -568,16 +579,17 @@
         [((2 * tile, width - cut), bf16)],
         (tile, 3 * tile),
         flops(2 * guests, 3),
+        6,
     )
     back = along(back, OUTER)
     out = run_kernel(
         home_kernel,
         pair_mask,
-        [q, *near],
+        [q, *near, r1k, r1v, swap, r3k, r3v],
         [((rows, cut), bf16)] * 4,
         (tile, 2 * tile),
         flops(2 * HOME, 2),
-        loose=(r1_home, swap, r3),
+        6,
     )
     pieces = [(to_head(out[d], d) if d else out[0], d, 0) for d in range(4)]
     out = run_kernel(
@@ -587,6 +599,7 @@
         [((rows, width - cut), bf16)] * 4,
         (tile, tile),
         flops(2 * guests, 1),
+        6,
     )
     pieces += [(to_head(out[d], d) if d else out[0], d, cut) for d in range(4)]
     result = jnp.zeros((rows, features), jnp.bfloat16)

time: 83.8 us -> 83.3 us (level)
  waiting for transfers between devices: 39.1 us -> 27.1 us
  starting transfers between devices: 25.8 us -> 36.9 us
  local copies, waits for them, and re-layouts: 6.09 us -> 8.33 us
  Pallas kernels: 11.3 us -> 9.39 us
    ppermute x5 -> x6, waiting for transfers between devices: 15.6 us -> 0.02 us  [along(): return lax.ppermute(array, 'frame', pairs)]
    ppermute x5 -> x6, starting transfers between devices: 16.1 us -> 26.8 us  [along(): return lax.ppermute(array, 'frame', pairs)]
    ppermute x10, waiting for transfers between devices: 23.5 us -> 27.1 us  [to_head(): return lax.ppermute(array, 'head', [(i, i ^ d) for i in range(4)])]
    unnamed x22 -> x34, local copies, waits for them, and re-layouts: 3.72 us -> 5.96 us
    pallas_call x5, Pallas kernels: 9.44 us -> 7.64 us  [run_kernel(): pl.pallas_call(kernel, in_specs=[pl.BlockSpec(memory_space=pltpu.SMEM)] *...]
  transfers between devices with their start and end apart: 19 -> 21, of which waited for: 10 -> 6; matrix products, arithmetic and copies ran while one was open for 0% -> 0% of each run, Pallas kernels for 14% -> 11%
where the time goes in v15:
time: 83.3 us; the launch traced here: 83 us
  starting transfers between devices  36.9 us (44%)
  waiting for transfers between devices  27.1 us (33%)
  Pallas kernels  9.39 us (11%)
  local copies, waits for them, and re-layouts  8.33 us (10%)
  between operations  1 us (1%)
    ppermute x10, waiting for transfers between devices, to_head(): return lax.ppermute(array, 'head', [(i, i ^ d) for i in range(4)])  27.1 us
    ppermute x6, starting transfers between devices, along(): return lax.ppermute(array, 'frame', pairs)  26.8 us
    ppermute x10, starting transfers between devices, to_head(): return lax.ppermute(array, 'head', [(i, i ^ d) for i in range(4)])  8.93 us
    pallas_call x5, Pallas kernels, run_kernel(): pl.pallas_call(kernel, in_specs=[pl.BlockSpec(memory_space=pltpu.SMEM)] *...  7.64 us
    unnamed x34, local copies, waits for them, and re-layouts  5.96 us
  transfers between devices with their start and end apart: 21, of which 6 were waited for; matrix products, arithmetic and copies ran while one was open for 0% of the time, Pallas kernels for 11%

profile of v15, /device:TPU:0, one launch (start us, length us, event | category | flops | bytes accessed | tf_op | source)
XLA Modules:
  0.0 83.0 jit_solution(12645431754241547111)
XLA Ops:
  0.0 1.5 %constant_dynamic-slice_fusion = (bf16[128,640]{1,0:T(8,128)(2,1)S(1)}, bf16[128,640]{1,0:T(8,128)(2,1)S(1)}, bf16[128,640]{1,0:T(8,128)(2,1)S(1)}, bf16[128,640...) fusion(bf16[128,2560]{1,0:T(8,128)(2,1)} %refs_2_.1, ...), kind=kLoop, calls=%fused_computation.13 | loop fusion | bytes 2621456 | tf_op jit(solution)/shard_map/dynamic_slice | solution.py:494
  1.5 0.1 pad_maximum_fusion.1
  1.6 0.0 copy-start.12
  1.6 0.0 copy-start.15
  1.6 0.5 collective-permute-start
  2.1 1.7 %collective-permute-done = bf16[128,2560]{1,0:T(8,128)(2,1)S(1)} collective-permute-done((bf16[128,2560]{1,0:T(8,128)(2,1)S(1)}, bf16[128,2560]{1,0:T(8,128)(2,1)S(1)}, u32[]{:S(2)}, u32[]{:S(2)}) %collective-permute-start) | collective-permute-done | bytes 655392 | tf_op jit(solution)/shard_map/ppermute | solution.py:503
  4.0 2.9 %collective-permute-start.2 = (bf16[256,1280]{1,0:T(8,128)(2,1)S(1)}, bf16[256,1280]{1,0:T(8,128)(2,1)S(1)}, u32[]{:S(2)}, u32[]{:S(2)}) collective-permute-start(bf16[256,1280]{1,0:T(8,128)(2,1)S(1)} %pad_maximum_fusion.2), channel_id=1, source_target_pairs={{0,2},{1,3},{2,0},{3,1},{4,6},{5,7},{6,4},{7,5},{8,10},{9,11},{10,... | collective-permute-start | bytes 1966088 | tf_op jit(solution)/shard_map/ppermute | solution.py:503
  7.6 0.7 shard_map.55
  8.3 0.1 collective-permute-start.1
  8.3 0.1 pad_maximum_fusion.refs_1_
  8.4 0.6 collective-permute-start.6
  9.0 2.7 %collective-permute-start.4 = (bf16[272,1280]{1,0:T(8,128)(2,1)S(1)}, bf16[272,1280]{1,0:T(8,128)(2,1)S(1)}, u32[]{:S(2)}, u32[]{:S(2)}) collective-permute-start(bf16[272,1280]{1,0:T(8,128)(2,1)S(1)} %pad_maximum_fusion.refs_1_), channel_id=1, source_target_pairs={{0,4},{4,0},{8,12},{12,8},{1,5},{5,1},{9,13},{13,9},{2,6},{6,2},{1... | collective-permute-start | bytes 2088968 | tf_op jit(solution)/shard_map/ppermute | solution.py:506
  11.6 10.3 %collective-permute-done.2.refs_2_ = bf16[256,1280]{1,0:T(8,128)(2,1)S(1)} collective-permute-done((bf16[256,1280]{1,0:T(8,128)(2,1)S(1)}, bf16[256,1280]{1,0:T(8,128)(2,1)S(1)}, u32[]{:S(2)}, u32[]{:S(2)}) %collective-permute-start.2) | collective-permute-done | bytes 655392 | tf_op jit(solution)/shard_map/ppermute | solution.py:503
  22.0 3.5 %collective-permute-start.5 = (bf16[256,1280]{1,0:T(8,128)(2,1)S(1)}, bf16[256,1280]{1,0:T(8,128)(2,1)S(1)}, u32[]{:S(2)}, u32[]{:S(2)}) collective-permute-start(bf16[256,1280]{1,0:T(8,128)(2,1)S(1)} %collective-permute-done.2.refs_2_), channel_id=1, source_target_pairs={{0,4},{4,0},{8,12},{12,8},{1,5},{5,1},{9,13},{13,9},{2,6},{6,2},{1... | collective-permute-start | bytes 1966088 | tf_op jit(solution)/shard_map/ppermute | solution.py:506
  25.5 1.6 %collective-permute-start.3 = (bf16[256,640]{1,0:T(8,128)(2,1)S(1)}, bf16[256,640]{1,0:T(8,128)(2,1)S(1)}, u32[]{:S(2)}, u32[]{:S(2)}) collective-permute-start(bf16[256,640]{1,0:T(8,128)(2,1)S(1)} %pad_maximum_fusion.4), channel_id=1, source_target_pairs={{0,2},{1,3},{2,0},{3,1},{4,6},{5,7},{6,4},{7,5},{8,10},{9,11},{10,... | collective-permute-start | bytes 983048 | tf_op jit(solution)/shard_map/ppermute | solution.py:503
  27.0 6.9 %collective-permute-done.3 = bf16[256,640]{1,0:T(8,128)(2,1)S(1)} collective-permute-done((bf16[256,640]{1,0:T(8,128)(2,1)S(1)}, bf16[256,640]{1,0:T(8,128)(2,1)S(1)}, u32[]{:S(2)}, u32[]{:S(2)}) %collective-permute-start.3) | collective-permute-done | bytes 327712 | tf_op jit(solution)/shard_map/ppermute | solution.py:503
  33.9 0.1 pad_maximum_fusion.3.refs_0_.q
  34.0 0.1 shard_map.58
  34.1 8.3 %collective-permute-start.10 = (bf16[256,768]{1,0:T(8,128)(2,1)S(1)}, bf16[256,768]{1,0:T(8,128)(2,1)S(1)}, u32[]{:S(2)}, u32[]{:S(2)}) collective-permute-start(bf16[256,768]{1,0:T(8,128)(2,1)S(1)} %shard_map.58), channel_id=1, source_target_pairs={{0,4},{4,0},{8,12},{12,8},{1,5},{5,1},{9,13},{13,9},{2,6},{6,2},{1... | collective-permute-start | bytes 1179656 | tf_op jit(solution)/shard_map/ppermute | solution.py:506
  42.4 0.2 shard_map.57
  42.5 0.1 collective-permute-start.8
  42.6 0.5 collective-permute-start.9
  43.1 2.9 %shard_map.56 = (f32[2560,128]{1,0:T(8,128)S(1)}, f32[2560,128]{1,0:T(8,128)S(1)}, f32[8,128]{1,0:T(8,128)S(1)}) custom-call(bf16[512,640]{1,0:T(8,128)(2,1)S(1)} %pad_maximum_fusion.3.refs_0_.q, bf16[272,1280]{1,0:T(8,128)(2,1)S(1)} %pad_maximum_fusion.refs_1_, bf16[256,1280]{1,0:T(8,128)(2,1)S(1)} %collective-permute-done.2.refs_2_, ...), custom_call_target="tpu_custom_call" | custom-call | flops 2013265920 | bytes 4710400 | tf_op jit(solution)/shard_map/pallas_call | solution.py:375
  46.1 1.1 %copy-done = f32[2560,128]{1,0:T(8,128)} copy-done((f32[2560,128]{1,0:T(8,128)}, f32[2560,128]{1,0:T(8,128)S(1)}, u32[]{:S(2)}) %copy-start) | copy-done | bytes 1310744
  47.2 0.8 %shard_map.59 = (bf16[256,384]{1,0:T(8,128)(2,1)}, bf16[256,512]{1,0:T(8,128)(2,1)}) custom-call(f32[8,128]{1,0:T(8,128)S(1)} %get-tuple-element.65.done, bf16[256,384]{1,0:T(8,128)(2,1)S(1)} %collective-permute-done.8.refs_0_.r1k, bf16[256,512]{1,0:T(8,128)(2,1)S(1)} %get-tuple-element.66.refs_1_), custom_call_target="tpu_custom_call" | custom-call | tf_op jit(solution)/shard_map/pallas_call | solution.py:364
  48.1 0.1 collective-permute-start.16
  48.1 6.9 %collective-permute-start.11 = (bf16[256,384]{1,0:T(8,128)(2,1)}, bf16[256,384]{1,0:T(8,128)(2,1)}, u32[]{:S(2)}, u32[]{:S(2)}) collective-permute-start(bf16[256,384]{1,0:T(8,128)(2,1)} %get-tuple-element.67), channel_id=1, source_target_pairs={{0,4},{4,0},{8,12},{12,8},{1,5},{5,1},{9,13},{13,9},{2,6},{6,2},{1... | collective-permute-start | bytes 589832 | tf_op jit(solution)/shard_map/ppermute | solution.py:506
  55.0 0.1 collective-permute-start.12
  55.1 1.1 %copy-done.3 = bf16[272,1280]{1,0:T(8,128)(2,1)S(1)} copy-done((bf16[272,1280]{1,0:T(8,128)(2,1)S(1)}, bf16[272,1280]{1,0:T(8,128)(2,1)}, u32[]{:S(2)}) %copy-start.3) | copy-done | bytes 696344
  56.2 1.1 %copy-done.9 = bf16[256,1280]{1,0:T(8,128)(2,1)S(1)} copy-done((bf16[256,1280]{1,0:T(8,128)(2,1)S(1)}, bf16[256,1280]{1,0:T(8,128)(2,1)}, u32[]{:S(2)}) %copy-start.9) | copy-done | bytes 655384
  57.3 1.1 %copy-done.14 = bf16[256,1280]{1,0:T(8,128)(2,1)S(1)} copy-done((bf16[256,1280]{1,0:T(8,128)(2,1)S(1)}, bf16[256,1280]{1,0:T(8,128)(2,1)}, u32[]{:S(2)}) %copy-start.14) | copy-done | bytes 655384
  58.4 0.6 shard_map.61
  59.0 0.5 copy-done.5
  59.5 0.2 copy-done.11
  59.7 5.4 %collective-permute-start.17 = (bf16[512,256]{1,0:T(8,128)(2,1)S(1)}, bf16[512,256]{1,0:T(8,128)(2,1)S(1)}, u32[]{:S(2)}, u32[]{:S(2)}) collective-permute-start(bf16[512,256]{1,0:T(8,128)(2,1)S(1)} %shard_map.62), channel_id=1, source_target_pairs={{0,4},{4,0},{8,12},{12,8},{1,5},{5,1},{9,13},{13,9},{2,6},{6,2},{1... | collective-permute-start | bytes 786440 | tf_op jit(solution)/shard_map/ppermute | solution.py:506
  65.1 3.5 %shard_map.60 = (bf16[128,384]{1,0:T(8,128)(2,1)S(1)}, bf16[128,384]{1,0:T(8,128)(2,1)S(1)}, bf16[128,384]{1,0:T(8,128)(2,1)S(1)}, bf16[128,384]{1,0:T(8,128)(2,1)S(1)}) custom-call(s32[1,4]{1,0:T(1,128)S(1)} %copy-done.15, bf16[512,640]{1,0:T(8,128)(2,1)S(1)} %pad_maximum_fusion.3.refs_0_.q, f32[2560,128]{1,0:T(8,128)S(1)} %get-tuple-element.57.mixed, ...), custom_call_target="tpu_custom_call" | custom-call | flops 402653184 | bytes 3145728 | tf_op jit(solution)/shard_map/pallas_call | solution.py:375
  68.7 0.1 collective-permute-start.13
  68.8 0.6 collective-permute-start.14
  69.3 1.3 %collective-permute-start.15 = (bf16[128,384]{1,0:T(8,128)(2,1)S(1)}, bf16[128,384]{1,0:T(8,128)(2,1)S(1)}, u32[]{:S(2)}, u32[]{:S(2)}) collective-permute-start(bf16[128,384]{1,0:T(8,128)(2,1)S(1)} %get-tuple-element.72), channel_id=1, source_target_pairs={{0,3},{1,2},{2,1},{3,0},{4,7},{5,6},{6,5},{7,4},{8,11},{9,10},{10,... | collective-permute-start | bytes 294920 | tf_op jit(solution)/shard_map/ppermute | solution.py:503
  70.7 3.7 %collective-permute-done.14 = bf16[128,384]{1,0:T(8,128)(2,1)S(1)} collective-permute-done((bf16[128,384]{1,0:T(8,128)(2,1)S(1)}, bf16[128,384]{1,0:T(8,128)(2,1)S(1)}, u32[]{:S(2)}, u32[]{:S(2)}) %collective-permute-start.14) | collective-permute-done | bytes 98336 | tf_op jit(solution)/shard_map/ppermute | solution.py:503
  74.4 1.2 %collective-permute-done.15 = bf16[128,384]{1,0:T(8,128)(2,1)S(1)} collective-permute-done((bf16[128,384]{1,0:T(8,128)(2,1)S(1)}, bf16[128,384]{1,0:T(8,128)(2,1)S(1)}, u32[]{:S(2)}, u32[]{:S(2)}) %collective-permute-start.15) | collective-permute-done | bytes 98336 | tf_op jit(solution)/shard_map/ppermute | solution.py:503
  75.6 0.6 shard_map.63
  76.2 0.3 collective-permute-start.18
  76.6 0.5 collective-permute-start.19
  77.1 1.1 %collective-permute-start.20 = (bf16[128,256]{1,0:T(8,128)(2,1)S(1)}, bf16[128,256]{1,0:T(8,128)(2,1)S(1)}, u32[]{:S(2)}, u32[]{:S(2)}) collective-permute-start(bf16[128,256]{1,0:T(8,128)(2,1)S(1)} %get-tuple-element.80), channel_id=1, source_target_pairs={{0,3},{1,2},{2,1},{3,0},{4,7},{5,6},{6,5},{7,4},{8,11},{9,10},{10,... | collective-permute-start | bytes 196616 | tf_op jit(solution)/shard_map/ppermute | solution.py:503
  78.2 3.3 %collective-permute-done.19 = bf16[128,256]{1,0:T(8,128)(2,1)S(1)} collective-permute-done((bf16[128,256]{1,0:T(8,128)(2,1)S(1)}, bf16[128,256]{1,0:T(8,128)(2,1)S(1)}, u32[]{:S(2)}, u32[]{:S(2)}) %collective-permute-start.19) | collective-permute-done | bytes 65568 | tf_op jit(solution)/shard_map/ppermute | solution.py:503
  81.5 0.8 copy-done.16
  82.4 0.6 constant_dynamic-update-slice_fusion
  (54 shorter events, 0.4 us)
Async XLA Ops:
  1.6 6.0 %copy-start.6 = (bf16[128,2560]{1,0:T(8,128)(2,1)S(1)}, bf16[128,2560]{1,0:T(8,128)(2,1)}, u32[]{:S(2)}) copy-start(bf16[128,2560]{1,0:T(8,128)(2,1)} %refs_1_.1) | copy-start | bytes 1966084
  1.6 6.0 %copy-start.7 = (bf16[128,2560]{1,0:T(8,128)(2,1)S(1)}, bf16[128,2560]{1,0:T(8,128)(2,1)}, u32[]{:S(2)}) copy-start(bf16[128,2560]{1,0:T(8,128)(2,1)} %refs_2_.1) | copy-start | bytes 1966084
  1.6 6.0 %copy-start.12 = (bf16[128,2560]{1,0:T(8,128)(2,1)S(1)}, bf16[128,2560]{1,0:T(8,128)(2,1)}, u32[]{:S(2)}) copy-start(bf16[128,2560]{1,0:T(8,128)(2,1)} %refs_0_.1) | copy-start | bytes 1966084
  1.6 6.0 %copy-start.15 = (s32[1,4]{1,0:T(1,128)S(1)}, s32[1,4]{1,0:T(1,128)}, u32[]{:S(2)}) copy-start(s32[1,4]{1,0:T(1,128)} %mask.5) | copy-start | bytes 52
  1.6 2.2 %collective-permute-start = (bf16[128,2560]{1,0:T(8,128)(2,1)S(1)}, bf16[128,2560]{1,0:T(8,128)(2,1)S(1)}, u32[]{:S(2)}, u32[]{:S(2)}) collective-permute-start(bf16[128,2560]{1,0:T(8,128)(2,1)S(1)} %pad_maximum_fusion.1), channel_id=1, source_target_pairs={{0,1},{1,0},{2,3},{3,2},{4,5},{5,4},{6,7},{7,6},{8,9},{9,8},{10,11... | collective-permute-start | bytes 1966088 | tf_op jit(solution)/shard_map/ppermute | solution.py:503
  4.0 18.0 %collective-permute-start.2 = (bf16[256,1280]{1,0:T(8,128)(2,1)S(1)}, bf16[256,1280]{1,0:T(8,128)(2,1)S(1)}, u32[]{:S(2)}, u32[]{:S(2)}) collective-permute-start(bf16[256,1280]{1,0:T(8,128)(2,1)S(1)} %pad_maximum_fusion.2), channel_id=1, source_target_pairs={{0,2},{1,3},{2,0},{3,1},{4,6},{5,7},{6,4},{7,5},{8,10},{9,11},{10,... | collective-permute-start | bytes 1966088 | tf_op jit(solution)/shard_map/ppermute | solution.py:503
  8.3 13.7 %collective-permute-start.1 = (bf16[128,1280]{1,0:T(8,128)(2,1)S(1)}, bf16[128,1280]{1,0:T(8,128)(2,1)S(1)}, u32[]{:S(2)}, u32[]{:S(2)}) collective-permute-start(bf16[128,1280]{1,0:T(8,128)(2,1)S(1)} %get-tuple-element.49), channel_id=1, source_target_pairs={{0,1},{1,0},{2,3},{3,2},{4,5},{5,4},{6,7},{7,6},{8,9},{9,8},{10,11... | collective-permute-start | bytes 983048 | tf_op jit(solution)/shard_map/ppermute | solution.py:503
  8.4 34.7 %copy-start.2 = (bf16[272,1280]{1,0:T(8,128)(2,1)}, bf16[272,1280]{1,0:T(8,128)(2,1)S(1)}, u32[]{:S(2)}) copy-start(bf16[272,1280]{1,0:T(8,128)(2,1)S(1)} %pad_maximum_fusion.refs_1_) | copy-start | bytes 2088964
  8.4 25.5 %collective-permute-start.6 = (bf16[272,1280]{1,0:T(8,128)(2,1)S(1)}, bf16[272,1280]{1,0:T(8,128)(2,1)S(1)}, u32[]{:S(2)}, u32[]{:S(2)}) collective-permute-start(bf16[272,1280]{1,0:T(8,128)(2,1)S(1)} %pad_maximum_fusion.refs_1_), channel_id=1, source_target_pairs={{0,1},{1,0},{2,3},{3,2},{4,8},{5,9},{6,10},{7,11},{8,4},{9,5},{10,... | collective-permute-start | bytes 2088968 | tf_op jit(solution)/shard_map/ppermute | solution.py:510
  9.0 33.4 %collective-permute-start.4 = (bf16[272,1280]{1,0:T(8,128)(2,1)S(1)}, bf16[272,1280]{1,0:T(8,128)(2,1)S(1)}, u32[]{:S(2)}, u32[]{:S(2)}) collective-permute-start(bf16[272,1280]{1,0:T(8,128)(2,1)S(1)} %pad_maximum_fusion.refs_1_), channel_id=1, source_target_pairs={{0,4},{4,0},{8,12},{12,8},{1,5},{5,1},{9,13},{13,9},{2,6},{6,2},{1... | collective-permute-start | bytes 2088968 | tf_op jit(solution)/shard_map/ppermute | solution.py:506
  21.9 21.2 %copy-start.13 = (bf16[256,1280]{1,0:T(8,128)(2,1)}, bf16[256,1280]{1,0:T(8,128)(2,1)S(1)}, u32[]{:S(2)}) copy-start(bf16[256,1280]{1,0:T(8,128)(2,1)S(1)} %collective-permute-done.2.refs_2_) | copy-start | bytes 1966084
  21.9 12.1 %collective-permute-start.7 = (bf16[256,1280]{1,0:T(8,128)(2,1)S(1)}, bf16[256,1280]{1,0:T(8,128)(2,1)S(1)}, u32[]{:S(2)}, u32[]{:S(2)}) collective-permute-start(bf16[256,1280]{1,0:T(8,128)(2,1)S(1)} %collective-permute-done.2.refs_2_), channel_id=1, source_target_pairs={{0,1},{1,0},{2,3},{3,2},{4,8},{5,9},{6,10},{7,11},{8,4},{9,5},{10,... | collective-permute-start | bytes 1966088 | tf_op jit(solution)/shard_map/ppermute | solution.py:510
  22.0 20.4 %collective-permute-start.5 = (bf16[256,1280]{1,0:T(8,128)(2,1)S(1)}, bf16[256,1280]{1,0:T(8,128)(2,1)S(1)}, u32[]{:S(2)}, u32[]{:S(2)}) collective-permute-start(bf16[256,1280]{1,0:T(8,128)(2,1)S(1)} %collective-permute-done.2.refs_2_), channel_id=1, source_target_pairs={{0,4},{4,0},{8,12},{12,8},{1,5},{5,1},{9,13},{13,9},{2,6},{6,2},{1... | collective-permute-start | bytes 1966088 | tf_op jit(solution)/shard_map/ppermute | solution.py:506
  25.5 8.4 %collective-permute-start.3 = (bf16[256,640]{1,0:T(8,128)(2,1)S(1)}, bf16[256,640]{1,0:T(8,128)(2,1)S(1)}, u32[]{:S(2)}, u32[]{:S(2)}) collective-permute-start(bf16[256,640]{1,0:T(8,128)(2,1)S(1)} %pad_maximum_fusion.4), channel_id=1, source_target_pairs={{0,2},{1,3},{2,0},{3,1},{4,6},{5,7},{6,4},{7,5},{8,10},{9,11},{10,... | collective-permute-start | bytes 983048 | tf_op jit(solution)/shard_map/ppermute | solution.py:503
  34.0 9.2 %copy-start.4 = (bf16[272,1280]{1,0:T(8,128)(2,1)}, bf16[272,1280]{1,0:T(8,128)(2,1)S(1)}, u32[]{:S(2)}) copy-start(bf16[272,1280]{1,0:T(8,128)(2,1)S(1)} %collective-permute-done.6.refs_5_.mine.n2m) | copy-start | bytes 2088964
  34.0 9.1 %copy-start.10 = (bf16[256,1280]{1,0:T(8,128)(2,1)}, bf16[256,1280]{1,0:T(8,128)(2,1)S(1)}, u32[]{:S(2)}) copy-start(bf16[256,1280]{1,0:T(8,128)(2,1)S(1)} %collective-permute-done.7.refs_6_.other.n2o) | copy-start | bytes 1966084
  34.1 21.0 %collective-permute-start.10 = (bf16[256,768]{1,0:T(8,128)(2,1)S(1)}, bf16[256,768]{1,0:T(8,128)(2,1)S(1)}, u32[]{:S(2)}, u32[]{:S(2)}) collective-permute-start(bf16[256,768]{1,0:T(8,128)(2,1)S(1)} %shard_map.58), channel_id=1, source_target_pairs={{0,4},{4,0},{8,12},{12,8},{1,5},{5,1},{9,13},{13,9},{2,6},{6,2},{1... | collective-permute-start | bytes 1179656 | tf_op jit(solution)/shard_map/ppermute | solution.py:506
  42.4 3.7 %copy-start.8 = (bf16[256,1280]{1,0:T(8,128)(2,1)}, bf16[256,1280]{1,0:T(8,128)(2,1)S(1)}, u32[]{:S(2)}) copy-start(bf16[256,1280]{1,0:T(8,128)(2,1)S(1)} %collective-permute-done.5.refs_4_.other) | copy-start | bytes 1966084
  42.5 4.7 %collective-permute-start.8 = (bf16[256,384]{1,0:T(8,128)(2,1)S(1)}, bf16[256,384]{1,0:T(8,128)(2,1)S(1)}, u32[]{:S(2)}, u32[]{:S(2)}) collective-permute-start(bf16[256,384]{1,0:T(8,128)(2,1)S(1)} %get-tuple-element.62), channel_id=1, source_target_pairs={{0,1},{1,0},{2,3},{3,2},{4,8},{5,9},{6,10},{7,11},{8,4},{9,5},{10,... | collective-permute-start | bytes 589832 | tf_op jit(solution)/shard_map/ppermute | solution.py:510
  42.6 12.4 %collective-permute-start.9 = (bf16[256,384]{1,0:T(8,128)(2,1)S(1)}, bf16[256,384]{1,0:T(8,128)(2,1)}, u32[]{:S(2)}, u32[]{:S(2)}) collective-permute-start(bf16[256,384]{1,0:T(8,128)(2,1)S(1)} %get-tuple-element.64), channel_id=1, source_target_pairs={{0,1},{1,0},{2,3},{3,2},{4,8},{5,9},{6,10},{7,11},{8,4},{9,5},{10,... | collective-permute-start | bytes 589832 | tf_op jit(solution)/shard_map/ppermute | solution.py:510
  46.1 1.1 %copy-start = (f32[2560,128]{1,0:T(8,128)}, f32[2560,128]{1,0:T(8,128)S(1)}, u32[]{:S(2)}) copy-start(f32[2560,128]{1,0:T(8,128)S(1)} %get-tuple-element.58.levels) | copy-start | bytes 3932164
  48.1 10.9 %collective-permute-start.16 = (bf16[256,512]{1,0:T(8,128)(2,1)}, bf16[256,512]{1,0:T(8,128)(2,1)S(1)}, u32[]{:S(2)}, u32[]{:S(2)}) collective-permute-start(bf16[256,512]{1,0:T(8,128)(2,1)} %get-tuple-element.73), channel_id=1, source_target_pairs={{0,1},{1,0},{2,3},{3,2},{4,8},{5,9},{6,10},{7,11},{8,4},{9,5},{10,... | collective-permute-start | bytes 786440 | tf_op jit(solution)/shard_map/ppermute | solution.py:510
  48.1 17.0 %collective-permute-start.11 = (bf16[256,384]{1,0:T(8,128)(2,1)}, bf16[256,384]{1,0:T(8,128)(2,1)}, u32[]{:S(2)}, u32[]{:S(2)}) collective-permute-start(bf16[256,384]{1,0:T(8,128)(2,1)} %get-tuple-element.67), channel_id=1, source_target_pairs={{0,4},{4,0},{8,12},{12,8},{1,5},{5,1},{9,13},{13,9},{2,6},{6,2},{1... | collective-permute-start | bytes 589832 | tf_op jit(solution)/shard_map/ppermute | solution.py:506
  55.0 10.1 %collective-permute-start.12 = (bf16[256,384]{1,0:T(8,128)(2,1)}, bf16[256,384]{1,0:T(8,128)(2,1)}, u32[]{:S(2)}, u32[]{:S(2)}) collective-permute-start(bf16[256,384]{1,0:T(8,128)(2,1)} %collective-permute-done.9.r1v), channel_id=1, source_target_pairs={{0,4},{4,0},{8,12},{12,8},{1,5},{5,1},{9,13},{13,9},{2,6},{6,2},{1... | collective-permute-start | bytes 589832 | tf_op jit(solution)/shard_map/ppermute | solution.py:506
  55.1 1.1 %copy-start.3 = (bf16[272,1280]{1,0:T(8,128)(2,1)S(1)}, bf16[272,1280]{1,0:T(8,128)(2,1)}, u32[]{:S(2)}) copy-start(bf16[272,1280]{1,0:T(8,128)(2,1)} %copy-done.2) | copy-start | bytes 2088964
  56.2 1.1 %copy-start.9 = (bf16[256,1280]{1,0:T(8,128)(2,1)S(1)}, bf16[256,1280]{1,0:T(8,128)(2,1)}, u32[]{:S(2)}) copy-start(bf16[256,1280]{1,0:T(8,128)(2,1)} %copy-done.8) | copy-start | bytes 1966084
  57.3 1.1 %copy-start.14 = (bf16[256,1280]{1,0:T(8,128)(2,1)S(1)}, bf16[256,1280]{1,0:T(8,128)(2,1)}, u32[]{:S(2)}) copy-start(bf16[256,1280]{1,0:T(8,128)(2,1)} %copy-done.13) | copy-start | bytes 1966084
  58.4 1.1 %copy-start.5 = (bf16[272,1280]{1,0:T(8,128)(2,1)S(1)}, bf16[272,1280]{1,0:T(8,128)(2,1)}, u32[]{:S(2)}) copy-start(bf16[272,1280]{1,0:T(8,128)(2,1)} %copy-done.4) | copy-start | bytes 2088964
  58.4 1.3 %copy-start.11 = (bf16[256,1280]{1,0:T(8,128)(2,1)S(1)}, bf16[256,1280]{1,0:T(8,128)(2,1)}, u32[]{:S(2)}) copy-start(bf16[256,1280]{1,0:T(8,128)(2,1)} %copy-done.10) | copy-start | bytes 1966084
  59.7 5.5 %copy-start.1 = (f32[2560,128]{1,0:T(8,128)S(1)}, f32[2560,128]{1,0:T(8,128)}, u32[]{:S(2)}) copy-start(f32[2560,128]{1,0:T(8,128)} %copy-done) | copy-start | bytes 3932164
  59.7 16.0 %collective-permute-start.17 = (bf16[512,256]{1,0:T(8,128)(2,1)S(1)}, bf16[512,256]{1,0:T(8,128)(2,1)S(1)}, u32[]{:S(2)}, u32[]{:S(2)}) collective-permute-start(bf16[512,256]{1,0:T(8,128)(2,1)S(1)} %shard_map.62), channel_id=1, source_target_pairs={{0,4},{4,0},{8,12},{12,8},{1,5},{5,1},{9,13},{13,9},{2,6},{6,2},{1... | collective-permute-start | bytes 786440 | tf_op jit(solution)/shard_map/ppermute | solution.py:506
  68.7 2.0 %collective-permute-start.13 = (bf16[128,384]{1,0:T(8,128)(2,1)S(1)}, bf16[128,384]{1,0:T(8,128)(2,1)S(1)}, u32[]{:S(2)}, u32[]{:S(2)}) collective-permute-start(bf16[128,384]{1,0:T(8,128)(2,1)S(1)} %get-tuple-element.70), channel_id=1, source_target_pairs={{0,1},{1,0},{2,3},{3,2},{4,5},{5,4},{6,7},{7,6},{8,9},{9,8},{10,11... | collective-permute-start | bytes 294920 | tf_op jit(solution)/shard_map/ppermute | solution.py:503
  68.8 5.7 %collective-permute-start.14 = (bf16[128,384]{1,0:T(8,128)(2,1)S(1)}, bf16[128,384]{1,0:T(8,128)(2,1)S(1)}, u32[]{:S(2)}, u32[]{:S(2)}) collective-permute-start(bf16[128,384]{1,0:T(8,128)(2,1)S(1)} %get-tuple-element.71), channel_id=1, source_target_pairs={{0,2},{1,3},{2,0},{3,1},{4,6},{5,7},{6,4},{7,5},{8,10},{9,11},{10,... | collective-permute-start | bytes 294920 | tf_op jit(solution)/shard_map/ppermute | solution.py:503
  69.3 6.3 %collective-permute-start.15 = (bf16[128,384]{1,0:T(8,128)(2,1)S(1)}, bf16[128,384]{1,0:T(8,128)(2,1)S(1)}, u32[]{:S(2)}, u32[]{:S(2)}) collective-permute-start(bf16[128,384]{1,0:T(8,128)(2,1)S(1)} %get-tuple-element.72), channel_id=1, source_target_pairs={{0,3},{1,2},{2,1},{3,0},{4,7},{5,6},{6,5},{7,4},{8,11},{9,10},{10,... | collective-permute-start | bytes 294920 | tf_op jit(solution)/shard_map/ppermute | solution.py:503
  76.2 1.9 %collective-permute-start.18 = (bf16[128,256]{1,0:T(8,128)(2,1)S(1)}, bf16[128,256]{1,0:T(8,128)(2,1)S(1)}, u32[]{:S(2)}, u32[]{:S(2)}) collective-permute-start(bf16[128,256]{1,0:T(8,128)(2,1)S(1)} %get-tuple-element.78), channel_id=1, source_target_pairs={{0,1},{1,0},{2,3},{3,2},{4,5},{5,4},{6,7},{7,6},{8,9},{9,8},{10,11... | collective-permute-start | bytes 196616 | tf_op jit(solution)/shard_map/ppermute | solution.py:503
  76.6 4.9 %collective-permute-start.19 = (bf16[128,256]{1,0:T(8,128)(2,1)S(1)}, bf16[128,256]{1,0:T(8,128)(2,1)S(1)}, u32[]{:S(2)}, u32[]{:S(2)}) collective-permute-start(bf16[128,256]{1,0:T(8,128)(2,1)S(1)} %get-tuple-element.79), channel_id=1, source_target_pairs={{0,2},{1,3},{2,0},{3,1},{4,6},{5,7},{6,4},{7,5},{8,10},{9,11},{10,... | collective-permute-start | bytes 196616 | tf_op jit(solution)/shard_map/ppermute | solution.py:503
  77.1 4.4 %collective-permute-start.20 = (bf16[128,256]{1,0:T(8,128)(2,1)S(1)}, bf16[128,256]{1,0:T(8,128)(2,1)S(1)}, u32[]{:S(2)}, u32[]{:S(2)}) collective-permute-start(bf16[128,256]{1,0:T(8,128)(2,1)S(1)} %get-tuple-element.80), channel_id=1, source_target_pairs={{0,3},{1,2},{2,1},{3,0},{4,7},{5,6},{6,5},{7,4},{8,11},{9,10},{10,... | collective-permute-start | bytes 196616 | tf_op jit(solution)/shard_map/ppermute | solution.py:503
  81.5 0.8 %copy-start.16 = (bf16[128,2560]{1,0:T(8,128)(2,1)}, bf16[128,2560]{1,0:T(8,128)(2,1)S(1)}, u32[]{:S(2)}) copy-start(bf16[128,2560]{1,0:T(8,128)(2,1)S(1)} %constant_dynamic-update-slice_fusion.1) | copy-start | bytes 1966084

commit v16 on v15

--- a/solution.py
+++ b/solution.py
@@ -557,7 +557,7 @@
         state(heads),
         (tile, 6 * tile),
         flops(2 * heads, 6),
-        8,
+        10,
     )
     r3k, r1_rest = passed(done, r1k, r1_rest)
     r3k = along(r3k, OUTER)
@@ -570,7 +570,7 @@
         state(guests),
         (tile, 4 * tile),
         flops(2 * guests, 4),
-        6,
+        10,
     )
     (back,) = run_kernel(
         guest_kernel,
@@ -579,7 +579,7 @@
         [((2 * tile, width - cut), bf16)],
         (tile, 3 * tile),
         flops(2 * guests, 3),
-        6,
+        10,
     )
     back = along(back, OUTER)
     out = run_kernel(
@@ -589,7 +589,7 @@
         [((rows, cut), bf16)] * 4,
         (tile, 2 * tile),
         flops(2 * HOME, 2),
-        6,
+        10,
     )
     pieces = [(to_head(out[d], d) if d else out[0], d, 0) for d in range(4)]
     out = run_kernel(
@@ -599,9 +599,11 @@
         [((rows, width - cut), bf16)] * 4,
         (tile, tile),
         flops(2 * guests, 1),
-        6,
-    )
-    pieces += [(to_head(out[d], d) if d else out[0], d, cut) for d in range(4)]
+        10,
+    )
+    moved = [out[0]] + [to_head(out[d], d) for d in (1, 2, 3)]
+    pieces = [(after(piece, moved[1] if d == 3 else out[1]) if d > 1 else piece, d, at) for piece, d, at in pieces]
+    pieces += [(piece, d, cut) for d, piece in enumerate(moved)]
     result = jnp.zeros((rows, features), jnp.bfloat16)
     for piece, d, begin in pieces:
         result = lax.dynamic_update_slice_in_dim(result, piece, (h ^ d) * width + begin, axis=1)

time: 83.3 us -> 81.8 us (0.982)
  waiting for transfers between devices: 27.1 us -> 25.9 us
    ppermute x10, waiting for transfers between devices: 27.1 us -> 25.8 us  [to_head(): return lax.ppermute(array, 'head', [(i, i ^ d) for i in range(4)])]
  transfers between devices with their start and end apart: 21 -> 21, of which waited for: 6 -> 7; matrix products, arithmetic and copies ran while one was open for 0% -> 0% of each run, Pallas kernels for 11% -> 12%
where the time goes in v16:
time: 81.8 us; the launch traced here: 81.5 us
  starting transfers between devices  37.5 us (46%)
  waiting for transfers between devices  25.9 us (32%)
  Pallas kernels  9.4 us (11%)
  local copies, waits for them, and re-layouts  7.52 us (9%)
  between operations  1 us (1%)
    ppermute x6, starting transfers between devices, along(): return lax.ppermute(array, 'frame', pairs)  26.8 us
    ppermute x10, waiting for transfers between devices, to_head(): return lax.ppermute(array, 'head', [(i, i ^ d) for i in range(4)])  25.8 us
    ppermute x10, starting transfers between devices, to_head(): return lax.ppermute(array, 'head', [(i, i ^ d) for i in range(4)])  9.46 us
    pallas_call x5, Pallas kernels, run_kernel(): pl.pallas_call(kernel, in_specs=[pl.BlockSpec(memory_space=pltpu.SMEM)] *...  7.66 us
    unnamed x34, local copies, waits for them, and re-layouts  5.14 us
  transfers between devices with their start and end apart: 21, of which 7 were waited for; matrix products, arithmetic and copies ran while one was open for 0% of the time, Pallas kernels for 12%

profile of v16, /device:TPU:0, one launch (start us, length us, event | category | flops | bytes accessed | tf_op | source)
XLA Modules:
  0.0 81.5 jit_solution(402531697120115189)
XLA Ops:
  0.0 1.5 %constant_dynamic-slice_fusion = (bf16[128,640]{1,0:T(8,128)(2,1)S(1)}, bf16[128,640]{1,0:T(8,128)(2,1)S(1)}, bf16[128,640]{1,0:T(8,128)(2,1)S(1)}, bf16[128,640...) fusion(bf16[128,2560]{1,0:T(8,128)(2,1)} %refs_2_.1, ...), kind=kLoop, calls=%fused_computation.13 | loop fusion | bytes 2621456 | tf_op jit(solution)/shard_map/dynamic_slice | solution.py:494
  1.5 0.1 pad_maximum_fusion.1
  1.6 0.0 copy-start.6
  1.6 0.0 copy-start.7
  1.6 0.0 copy-start.12
  1.6 0.5 collective-permute-start
  2.1 1.7 %collective-permute-done = bf16[128,2560]{1,0:T(8,128)(2,1)S(1)} collective-permute-done((bf16[128,2560]{1,0:T(8,128)(2,1)S(1)}, bf16[128,2560]{1,0:T(8,128)(2,1)S(1)}, u32[]{:S(2)}, u32[]{:S(2)}) %collective-permute-start) | collective-permute-done | bytes 655392 | tf_op jit(solution)/shard_map/ppermute | solution.py:503
  4.0 2.9 %collective-permute-start.2 = (bf16[256,1280]{1,0:T(8,128)(2,1)S(1)}, bf16[256,1280]{1,0:T(8,128)(2,1)S(1)}, u32[]{:S(2)}, u32[]{:S(2)}) collective-permute-start(bf16[256,1280]{1,0:T(8,128)(2,1)S(1)} %pad_maximum_fusion.2), channel_id=1, source_target_pairs={{0,2},{1,3},{2,0},{3,1},{4,6},{5,7},{6,4},{7,5},{8,10},{9,11},{10,... | collective-permute-start | bytes 1966088 | tf_op jit(solution)/shard_map/ppermute | solution.py:503
  7.6 0.7 shard_map.55
  8.3 0.1 collective-permute-start.1
  8.3 0.1 pad_maximum_fusion.refs_1_
  8.4 0.6 collective-permute-start.6
  9.0 2.7 %collective-permute-start.4 = (bf16[272,1280]{1,0:T(8,128)(2,1)S(1)}, bf16[272,1280]{1,0:T(8,128)(2,1)S(1)}, u32[]{:S(2)}, u32[]{:S(2)}) collective-permute-start(bf16[272,1280]{1,0:T(8,128)(2,1)S(1)} %pad_maximum_fusion.refs_1_), channel_id=1, source_target_pairs={{0,4},{4,0},{8,12},{12,8},{1,5},{5,1},{9,13},{13,9},{2,6},{6,2},{1... | collective-permute-start | bytes 2088968 | tf_op jit(solution)/shard_map/ppermute | solution.py:506
  11.6 10.3 %collective-permute-done.2.refs_2_ = bf16[256,1280]{1,0:T(8,128)(2,1)S(1)} collective-permute-done((bf16[256,1280]{1,0:T(8,128)(2,1)S(1)}, bf16[256,1280]{1,0:T(8,128)(2,1)S(1)}, u32[]{:S(2)}, u32[]{:S(2)}) %collective-permute-start.2) | collective-permute-done | bytes 655392 | tf_op jit(solution)/shard_map/ppermute | solution.py:503
  22.0 3.5 %collective-permute-start.5 = (bf16[256,1280]{1,0:T(8,128)(2,1)S(1)}, bf16[256,1280]{1,0:T(8,128)(2,1)S(1)}, u32[]{:S(2)}, u32[]{:S(2)}) collective-permute-start(bf16[256,1280]{1,0:T(8,128)(2,1)S(1)} %collective-permute-done.2.refs_2_), channel_id=1, source_target_pairs={{0,4},{4,0},{8,12},{12,8},{1,5},{5,1},{9,13},{13,9},{2,6},{6,2},{1... | collective-permute-start | bytes 1966088 | tf_op jit(solution)/shard_map/ppermute | solution.py:506
  25.5 1.6 %collective-permute-start.3 = (bf16[256,640]{1,0:T(8,128)(2,1)S(1)}, bf16[256,640]{1,0:T(8,128)(2,1)S(1)}, u32[]{:S(2)}, u32[]{:S(2)}) collective-permute-start(bf16[256,640]{1,0:T(8,128)(2,1)S(1)} %pad_maximum_fusion.4), channel_id=1, source_target_pairs={{0,2},{1,3},{2,0},{3,1},{4,6},{5,7},{6,4},{7,5},{8,10},{9,11},{10,... | collective-permute-start | bytes 983048 | tf_op jit(solution)/shard_map/ppermute | solution.py:503
  27.0 6.9 %collective-permute-done.3 = bf16[256,640]{1,0:T(8,128)(2,1)S(1)} collective-permute-done((bf16[256,640]{1,0:T(8,128)(2,1)S(1)}, bf16[256,640]{1,0:T(8,128)(2,1)S(1)}, u32[]{:S(2)}, u32[]{:S(2)}) %collective-permute-start.3) | collective-permute-done | bytes 327712 | tf_op jit(solution)/shard_map/ppermute | solution.py:503
  33.9 0.1 pad_maximum_fusion.3.refs_0_.q
  34.0 0.1 shard_map.58
  34.1 8.3 %collective-permute-start.10 = (bf16[256,768]{1,0:T(8,128)(2,1)S(1)}, bf16[256,768]{1,0:T(8,128)(2,1)S(1)}, u32[]{:S(2)}, u32[]{:S(2)}) collective-permute-start(bf16[256,768]{1,0:T(8,128)(2,1)S(1)} %shard_map.58), channel_id=1, source_target_pairs={{0,4},{4,0},{8,12},{12,8},{1,5},{5,1},{9,13},{13,9},{2,6},{6,2},{1... | collective-permute-start | bytes 1179656 | tf_op jit(solution)/shard_map/ppermute | solution.py:506
  42.4 0.2 shard_map.57
  42.5 0.1 collective-permute-start.8
  42.6 0.5 collective-permute-start.9
  43.1 2.9 %shard_map.56 = (f32[2560,128]{1,0:T(8,128)S(1)}, f32[2560,128]{1,0:T(8,128)S(1)}, f32[8,128]{1,0:T(8,128)S(1)}) custom-call(bf16[512,640]{1,0:T(8,128)(2,1)S(1)} %pad_maximum_fusion.3.refs_0_.q, bf16[272,1280]{1,0:T(8,128)(2,1)S(1)} %pad_maximum_fusion.refs_1_, bf16[256,1280]{1,0:T(8,128)(2,1)S(1)} %collective-permute-done.2.refs_2_, ...), custom_call_target="tpu_custom_call" | custom-call | flops 2013265920 | bytes 4710400 | tf_op jit(solution)/shard_map/pallas_call | solution.py:375
  46.1 1.1 %copy-done = f32[2560,128]{1,0:T(8,128)} copy-done((f32[2560,128]{1,0:T(8,128)}, f32[2560,128]{1,0:T(8,128)S(1)}, u32[]{:S(2)}) %copy-start) | copy-done | bytes 1310744
  47.2 0.8 %shard_map.59 = (bf16[256,384]{1,0:T(8,128)(2,1)}, bf16[256,512]{1,0:T(8,128)(2,1)}) custom-call(f32[8,128]{1,0:T(8,128)S(1)} %get-tuple-element.67.done, bf16[256,384]{1,0:T(8,128)(2,1)S(1)} %collective-permute-done.8.refs_0_.r1k, bf16[256,512]{1,0:T(8,128)(2,1)S(1)} %get-tuple-element.68.refs_1_), custom_call_target="tpu_custom_call" | custom-call | tf_op jit(solution)/shard_map/pallas_call | solution.py:364
  48.1 0.1 collective-permute-start.15
  48.1 6.9 %collective-permute-start.11 = (bf16[256,384]{1,0:T(8,128)(2,1)}, bf16[256,384]{1,0:T(8,128)(2,1)}, u32[]{:S(2)}, u32[]{:S(2)}) collective-permute-start(bf16[256,384]{1,0:T(8,128)(2,1)} %get-tuple-element.69), channel_id=1, source_target_pairs={{0,4},{4,0},{8,12},{12,8},{1,5},{5,1},{9,13},{13,9},{2,6},{6,2},{1... | collective-permute-start | bytes 589832 | tf_op jit(solution)/shard_map/ppermute | solution.py:506
  55.0 0.1 collective-permute-start.12
  55.1 1.1 %copy-done.3 = bf16[272,1280]{1,0:T(8,128)(2,1)S(1)} copy-done((bf16[272,1280]{1,0:T(8,128)(2,1)S(1)}, bf16[272,1280]{1,0:T(8,128)(2,1)}, u32[]{:S(2)}) %copy-start.3) | copy-done | bytes 696344
  56.2 1.1 %copy-done.9 = bf16[256,1280]{1,0:T(8,128)(2,1)S(1)} copy-done((bf16[256,1280]{1,0:T(8,128)(2,1)S(1)}, bf16[256,1280]{1,0:T(8,128)(2,1)}, u32[]{:S(2)}) %copy-start.9) | copy-done | bytes 655384
  57.3 1.1 %copy-done.14 = bf16[256,1280]{1,0:T(8,128)(2,1)S(1)} copy-done((bf16[256,1280]{1,0:T(8,128)(2,1)S(1)}, bf16[256,1280]{1,0:T(8,128)(2,1)}, u32[]{:S(2)}) %copy-start.14) | copy-done | bytes 655384
  58.4 0.6 shard_map.61
  59.0 0.5 copy-done.5
  59.5 0.2 copy-done.11
  59.7 5.4 %collective-permute-start.16 = (bf16[512,256]{1,0:T(8,128)(2,1)S(1)}, bf16[512,256]{1,0:T(8,128)(2,1)S(1)}, u32[]{:S(2)}, u32[]{:S(2)}) collective-permute-start(bf16[512,256]{1,0:T(8,128)(2,1)S(1)} %shard_map.62), channel_id=1, source_target_pairs={{0,4},{4,0},{8,12},{12,8},{1,5},{5,1},{9,13},{13,9},{2,6},{6,2},{1... | collective-permute-start | bytes 786440 | tf_op jit(solution)/shard_map/ppermute | solution.py:506
  65.1 3.5 %shard_map.60 = (bf16[128,384]{1,0:T(8,128)(2,1)S(1)}, bf16[128,384]{1,0:T(8,128)(2,1)S(1)}, bf16[128,384]{1,0:T(8,128)(2,1)S(1)}, bf16[128,384]{1,0:T(8,128)(2,1)S(1)}) custom-call(s32[1,4]{1,0:T(1,128)S(1)} %copy-done.15, bf16[512,640]{1,0:T(8,128)(2,1)S(1)} %pad_maximum_fusion.3.refs_0_.q, f32[2560,128]{1,0:T(8,128)S(1)} %get-tuple-element.59.mixed, ...), custom_call_target="tpu_custom_call" | custom-call | flops 402653184 | bytes 3145728 | tf_op jit(solution)/shard_map/pallas_call | solution.py:375
  68.7 0.1 collective-permute-start.17
  68.7 0.6 collective-permute-start.14
  69.3 1.2 %collective-permute-start.13 = (bf16[128,384]{1,0:T(8,128)(2,1)S(1)}, bf16[128,384]{1,0:T(8,128)(2,1)S(1)}, u32[]{:S(2)}, u32[]{:S(2)}) collective-permute-start(bf16[128,384]{1,0:T(8,128)(2,1)S(1)} %get-tuple-element.72), channel_id=1, source_target_pairs={{0,1},{1,0},{2,3},{3,2},{4,5},{5,4},{6,7},{7,6},{8,9},{9,8},{10,11... | collective-permute-start | bytes 294920 | tf_op jit(solution)/shard_map/ppermute | solution.py:503
  70.7 0.9 %collective-permute-done.13 = bf16[128,384]{1,0:T(8,128)(2,1)S(1)} collective-permute-done((bf16[128,384]{1,0:T(8,128)(2,1)S(1)}, bf16[128,384]{1,0:T(8,128)(2,1)S(1)}, u32[]{:S(2)}, u32[]{:S(2)}) %collective-permute-start.13) | collective-permute-done | bytes 98336 | tf_op jit(solution)/shard_map/ppermute | solution.py:503
  71.6 0.6 shard_map.63
  72.2 0.4 collective-permute-start.18
  72.6 1.9 %collective-permute-done.14 = bf16[128,384]{1,0:T(8,128)(2,1)S(1)} collective-permute-done((bf16[128,384]{1,0:T(8,128)(2,1)S(1)}, bf16[128,384]{1,0:T(8,128)(2,1)S(1)}, u32[]{:S(2)}, u32[]{:S(2)}) %collective-permute-start.14) | collective-permute-done | bytes 98336 | tf_op jit(solution)/shard_map/ppermute | solution.py:503
  74.4 2.0 %collective-permute-start.19 = (bf16[128,256]{1,0:T(8,128)(2,1)S(1)}, bf16[128,256]{1,0:T(8,128)(2,1)S(1)}, u32[]{:S(2)}, u32[]{:S(2)}) collective-permute-start(bf16[128,256]{1,0:T(8,128)(2,1)S(1)} %get-tuple-element.83), channel_id=1, source_target_pairs={{0,2},{1,3},{2,0},{3,1},{4,6},{5,7},{6,4},{7,5},{8,10},{9,11},{10,... | collective-permute-start | bytes 196616 | tf_op jit(solution)/shard_map/ppermute | solution.py:503
  76.6 2.3 %collective-permute-done.19 = bf16[128,256]{1,0:T(8,128)(2,1)S(1)} collective-permute-done((bf16[128,256]{1,0:T(8,128)(2,1)S(1)}, bf16[128,256]{1,0:T(8,128)(2,1)S(1)}, u32[]{:S(2)}, u32[]{:S(2)}) %collective-permute-start.19) | collective-permute-done | bytes 65568 | tf_op jit(solution)/shard_map/ppermute | solution.py:503
  78.9 2.0 %collective-permute-done.20 = bf16[128,256]{1,0:T(8,128)(2,1)S(1)} collective-permute-done((bf16[128,256]{1,0:T(8,128)(2,1)S(1)}, bf16[128,256]{1,0:T(8,128)(2,1)S(1)}, u32[]{:S(2)}, u32[]{:S(2)}) %collective-permute-start.20) | collective-permute-done | bytes 65568 | tf_op jit(solution)/shard_map/ppermute | solution.py:503
  80.8 0.6 constant_dynamic-update-slice_fusion
  (54 shorter events, 0.4 us)
Async XLA Ops:
  1.6 6.0 %copy-start.6 = (bf16[128,2560]{1,0:T(8,128)(2,1)S(1)}, bf16[128,2560]{1,0:T(8,128)(2,1)}, u32[]{:S(2)}) copy-start(bf16[128,2560]{1,0:T(8,128)(2,1)} %refs_1_.1) | copy-start | bytes 1966084
  1.6 6.0 %copy-start.7 = (bf16[128,2560]{1,0:T(8,128)(2,1)S(1)}, bf16[128,2560]{1,0:T(8,128)(2,1)}, u32[]{:S(2)}) copy-start(bf16[128,2560]{1,0:T(8,128)(2,1)} %refs_2_.1) | copy-start | bytes 1966084
  1.6 6.0 %copy-start.12 = (bf16[128,2560]{1,0:T(8,128)(2,1)S(1)}, bf16[128,2560]{1,0:T(8,128)(2,1)}, u32[]{:S(2)}) copy-start(bf16[128,2560]{1,0:T(8,128)(2,1)} %refs_0_.1) | copy-start | bytes 1966084
  1.6 6.0 %copy-start.15 = (s32[1,4]{1,0:T(1,128)S(1)}, s32[1,4]{1,0:T(1,128)}, u32[]{:S(2)}) copy-start(s32[1,4]{1,0:T(1,128)} %mask.5) | copy-start | bytes 52
  1.6 2.2 %collective-permute-start = (bf16[128,2560]{1,0:T(8,128)(2,1)S(1)}, bf16[128,2560]{1,0:T(8,128)(2,1)S(1)}, u32[]{:S(2)}, u32[]{:S(2)}) collective-permute-start(bf16[128,2560]{1,0:T(8,128)(2,1)S(1)} %pad_maximum_fusion.1), channel_id=1, source_target_pairs={{0,1},{1,0},{2,3},{3,2},{4,5},{5,4},{6,7},{7,6},{8,9},{9,8},{10,11... | collective-permute-start | bytes 1966088 | tf_op jit(solution)/shard_map/ppermute | solution.py:503
  4.0 18.0 %collective-permute-start.2 = (bf16[256,1280]{1,0:T(8,128)(2,1)S(1)}, bf16[256,1280]{1,0:T(8,128)(2,1)S(1)}, u32[]{:S(2)}, u32[]{:S(2)}) collective-permute-start(bf16[256,1280]{1,0:T(8,128)(2,1)S(1)} %pad_maximum_fusion.2), channel_id=1, source_target_pairs={{0,2},{1,3},{2,0},{3,1},{4,6},{5,7},{6,4},{7,5},{8,10},{9,11},{10,... | collective-permute-start | bytes 1966088 | tf_op jit(solution)/shard_map/ppermute | solution.py:503
  8.3 13.7 %collective-permute-start.1 = (bf16[128,1280]{1,0:T(8,128)(2,1)S(1)}, bf16[128,1280]{1,0:T(8,128)(2,1)S(1)}, u32[]{:S(2)}, u32[]{:S(2)}) collective-permute-start(bf16[128,1280]{1,0:T(8,128)(2,1)S(1)} %get-tuple-element.51), channel_id=1, source_target_pairs={{0,1},{1,0},{2,3},{3,2},{4,5},{5,4},{6,7},{7,6},{8,9},{9,8},{10,11... | collective-permute-start | bytes 983048 | tf_op jit(solution)/shard_map/ppermute | solution.py:503
  8.4 34.7 %copy-start.2 = (bf16[272,1280]{1,0:T(8,128)(2,1)}, bf16[272,1280]{1,0:T(8,128)(2,1)S(1)}, u32[]{:S(2)}) copy-start(bf16[272,1280]{1,0:T(8,128)(2,1)S(1)} %pad_maximum_fusion.refs_1_) | copy-start | bytes 2088964
  8.4 25.5 %collective-permute-start.6 = (bf16[272,1280]{1,0:T(8,128)(2,1)S(1)}, bf16[272,1280]{1,0:T(8,128)(2,1)S(1)}, u32[]{:S(2)}, u32[]{:S(2)}) collective-permute-start(bf16[272,1280]{1,0:T(8,128)(2,1)S(1)} %pad_maximum_fusion.refs_1_), channel_id=1, source_target_pairs={{0,1},{1,0},{2,3},{3,2},{4,8},{5,9},{6,10},{7,11},{8,4},{9,5},{10,... | collective-permute-start | bytes 2088968 | tf_op jit(solution)/shard_map/ppermute | solution.py:510
  9.0 33.4 %collective-permute-start.4 = (bf16[272,1280]{1,0:T(8,128)(2,1)S(1)}, bf16[272,1280]{1,0:T(8,128)(2,1)S(1)}, u32[]{:S(2)}, u32[]{:S(2)}) collective-permute-start(bf16[272,1280]{1,0:T(8,128)(2,1)S(1)} %pad_maximum_fusion.refs_1_), channel_id=1, source_target_pairs={{0,4},{4,0},{8,12},{12,8},{1,5},{5,1},{9,13},{13,9},{2,6},{6,2},{1... | collective-permute-start | bytes 2088968 | tf_op jit(solution)/shard_map/ppermute | solution.py:506
  21.9 21.2 %copy-start.13 = (bf16[256,1280]{1,0:T(8,128)(2,1)}, bf16[256,1280]{1,0:T(8,128)(2,1)S(1)}, u32[]{:S(2)}) copy-start(bf16[256,1280]{1,0:T(8,128)(2,1)S(1)} %collective-permute-done.2.refs_2_) | copy-start | bytes 1966084
  21.9 12.1 %collective-permute-start.7 = (bf16[256,1280]{1,0:T(8,128)(2,1)S(1)}, bf16[256,1280]{1,0:T(8,128)(2,1)S(1)}, u32[]{:S(2)}, u32[]{:S(2)}) collective-permute-start(bf16[256,1280]{1,0:T(8,128)(2,1)S(1)} %collective-permute-done.2.refs_2_), channel_id=1, source_target_pairs={{0,1},{1,0},{2,3},{3,2},{4,8},{5,9},{6,10},{7,11},{8,4},{9,5},{10,... | collective-permute-start | bytes 1966088 | tf_op jit(solution)/shard_map/ppermute | solution.py:510
  22.0 20.4 %collective-permute-start.5 = (bf16[256,1280]{1,0:T(8,128)(2,1)S(1)}, bf16[256,1280]{1,0:T(8,128)(2,1)S(1)}, u32[]{:S(2)}, u32[]{:S(2)}) collective-permute-start(bf16[256,1280]{1,0:T(8,128)(2,1)S(1)} %collective-permute-done.2.refs_2_), channel_id=1, source_target_pairs={{0,4},{4,0},{8,12},{12,8},{1,5},{5,1},{9,13},{13,9},{2,6},{6,2},{1... | collective-permute-start | bytes 1966088 | tf_op jit(solution)/shard_map/ppermute | solution.py:506
  25.5 8.4 %collective-permute-start.3 = (bf16[256,640]{1,0:T(8,128)(2,1)S(1)}, bf16[256,640]{1,0:T(8,128)(2,1)S(1)}, u32[]{:S(2)}, u32[]{:S(2)}) collective-permute-start(bf16[256,640]{1,0:T(8,128)(2,1)S(1)} %pad_maximum_fusion.4), channel_id=1, source_target_pairs={{0,2},{1,3},{2,0},{3,1},{4,6},{5,7},{6,4},{7,5},{8,10},{9,11},{10,... | collective-permute-start | bytes 983048 | tf_op jit(solution)/shard_map/ppermute | solution.py:503
  34.0 9.2 %copy-start.4 = (bf16[272,1280]{1,0:T(8,128)(2,1)}, bf16[272,1280]{1,0:T(8,128)(2,1)S(1)}, u32[]{:S(2)}) copy-start(bf16[272,1280]{1,0:T(8,128)(2,1)S(1)} %collective-permute-done.6.refs_5_.mine.n2m) | copy-start | bytes 2088964
  34.0 9.1 %copy-start.10 = (bf16[256,1280]{1,0:T(8,128)(2,1)}, bf16[256,1280]{1,0:T(8,128)(2,1)S(1)}, u32[]{:S(2)}) copy-start(bf16[256,1280]{1,0:T(8,128)(2,1)S(1)} %collective-permute-done.7.refs_6_.other.n2o) | copy-start | bytes 1966084
  34.1 21.0 %collective-permute-start.10 = (bf16[256,768]{1,0:T(8,128)(2,1)S(1)}, bf16[256,768]{1,0:T(8,128)(2,1)S(1)}, u32[]{:S(2)}, u32[]{:S(2)}) collective-permute-start(bf16[256,768]{1,0:T(8,128)(2,1)S(1)} %shard_map.58), channel_id=1, source_target_pairs={{0,4},{4,0},{8,12},{12,8},{1,5},{5,1},{9,13},{13,9},{2,6},{6,2},{1... | collective-permute-start | bytes 1179656 | tf_op jit(solution)/shard_map/ppermute | solution.py:506
  42.4 3.7 %copy-start.8 = (bf16[256,1280]{1,0:T(8,128)(2,1)}, bf16[256,1280]{1,0:T(8,128)(2,1)S(1)}, u32[]{:S(2)}) copy-start(bf16[256,1280]{1,0:T(8,128)(2,1)S(1)} %collective-permute-done.5.refs_4_.other) | copy-start | bytes 1966084
  42.5 4.7 %collective-permute-start.8 = (bf16[256,384]{1,0:T(8,128)(2,1)S(1)}, bf16[256,384]{1,0:T(8,128)(2,1)S(1)}, u32[]{:S(2)}, u32[]{:S(2)}) collective-permute-start(bf16[256,384]{1,0:T(8,128)(2,1)S(1)} %get-tuple-element.64), channel_id=1, source_target_pairs={{0,1},{1,0},{2,3},{3,2},{4,8},{5,9},{6,10},{7,11},{8,4},{9,5},{10,... | collective-permute-start | bytes 589832 | tf_op jit(solution)/shard_map/ppermute | solution.py:510
  42.6 12.4 %collective-permute-start.9 = (bf16[256,384]{1,0:T(8,128)(2,1)S(1)}, bf16[256,384]{1,0:T(8,128)(2,1)}, u32[]{:S(2)}, u32[]{:S(2)}) collective-permute-start(bf16[256,384]{1,0:T(8,128)(2,1)S(1)} %get-tuple-element.66), channel_id=1, source_target_pairs={{0,1},{1,0},{2,3},{3,2},{4,8},{5,9},{6,10},{7,11},{8,4},{9,5},{10,... | collective-permute-start | bytes 589832 | tf_op jit(solution)/shard_map/ppermute | solution.py:510
  46.1 1.1 %copy-start = (f32[2560,128]{1,0:T(8,128)}, f32[2560,128]{1,0:T(8,128)S(1)}, u32[]{:S(2)}) copy-start(f32[2560,128]{1,0:T(8,128)S(1)} %get-tuple-element.60.levels) | copy-start | bytes 3932164
  48.1 10.9 %collective-permute-start.15 = (bf16[256,512]{1,0:T(8,128)(2,1)}, bf16[256,512]{1,0:T(8,128)(2,1)S(1)}, u32[]{:S(2)}, u32[]{:S(2)}) collective-permute-start(bf16[256,512]{1,0:T(8,128)(2,1)} %get-tuple-element.74), channel_id=1, source_target_pairs={{0,1},{1,0},{2,3},{3,2},{4,8},{5,9},{6,10},{7,11},{8,4},{9,5},{10,... | collective-permute-start | bytes 786440 | tf_op jit(solution)/shard_map/ppermute | solution.py:510
  48.1 17.0 %collective-permute-start.11 = (bf16[256,384]{1,0:T(8,128)(2,1)}, bf16[256,384]{1,0:T(8,128)(2,1)}, u32[]{:S(2)}, u32[]{:S(2)}) collective-permute-start(bf16[256,384]{1,0:T(8,128)(2,1)} %get-tuple-element.69), channel_id=1, source_target_pairs={{0,4},{4,0},{8,12},{12,8},{1,5},{5,1},{9,13},{13,9},{2,6},{6,2},{1... | collective-permute-start | bytes 589832 | tf_op jit(solution)/shard_map/ppermute | solution.py:506
  55.0 10.1 %collective-permute-start.12 = (bf16[256,384]{1,0:T(8,128)(2,1)}, bf16[256,384]{1,0:T(8,128)(2,1)}, u32[]{:S(2)}, u32[]{:S(2)}) collective-permute-start(bf16[256,384]{1,0:T(8,128)(2,1)} %collective-permute-done.9.r1v), channel_id=1, source_target_pairs={{0,4},{4,0},{8,12},{12,8},{1,5},{5,1},{9,13},{13,9},{2,6},{6,2},{1... | collective-permute-start | bytes 589832 | tf_op jit(solution)/shard_map/ppermute | solution.py:506
  55.1 1.1 %copy-start.3 = (bf16[272,1280]{1,0:T(8,128)(2,1)S(1)}, bf16[272,1280]{1,0:T(8,128)(2,1)}, u32[]{:S(2)}) copy-start(bf16[272,1280]{1,0:T(8,128)(2,1)} %copy-done.2) | copy-start | bytes 2088964
  56.2 1.1 %copy-start.9 = (bf16[256,1280]{1,0:T(8,128)(2,1)S(1)}, bf16[256,1280]{1,0:T(8,128)(2,1)}, u32[]{:S(2)}) copy-start(bf16[256,1280]{1,0:T(8,128)(2,1)} %copy-done.8) | copy-start | bytes 1966084
  57.3 1.1 %copy-start.14 = (bf16[256,1280]{1,0:T(8,128)(2,1)S(1)}, bf16[256,1280]{1,0:T(8,128)(2,1)}, u32[]{:S(2)}) copy-start(bf16[256,1280]{1,0:T(8,128)(2,1)} %copy-done.13) | copy-start | bytes 1966084
  58.4 1.1 %copy-start.5 = (bf16[272,1280]{1,0:T(8,128)(2,1)S(1)}, bf16[272,1280]{1,0:T(8,128)(2,1)}, u32[]{:S(2)}) copy-start(bf16[272,1280]{1,0:T(8,128)(2,1)} %copy-done.4) | copy-start | bytes 2088964
  58.4 1.3 %copy-start.11 = (bf16[256,1280]{1,0:T(8,128)(2,1)S(1)}, bf16[256,1280]{1,0:T(8,128)(2,1)}, u32[]{:S(2)}) copy-start(bf16[256,1280]{1,0:T(8,128)(2,1)} %copy-done.10) | copy-start | bytes 1966084
  59.7 5.4 %copy-start.1 = (f32[2560,128]{1,0:T(8,128)S(1)}, f32[2560,128]{1,0:T(8,128)}, u32[]{:S(2)}) copy-start(f32[2560,128]{1,0:T(8,128)} %copy-done) | copy-start | bytes 3932164
  59.7 11.9 %collective-permute-start.16 = (bf16[512,256]{1,0:T(8,128)(2,1)S(1)}, bf16[512,256]{1,0:T(8,128)(2,1)S(1)}, u32[]{:S(2)}, u32[]{:S(2)}) collective-permute-start(bf16[512,256]{1,0:T(8,128)(2,1)S(1)} %shard_map.62), channel_id=1, source_target_pairs={{0,4},{4,0},{8,12},{12,8},{1,5},{5,1},{9,13},{13,9},{2,6},{6,2},{1... | collective-permute-start | bytes 786440 | tf_op jit(solution)/shard_map/ppermute | solution.py:506
  68.7 7.8 %collective-permute-start.17 = (bf16[128,384]{1,0:T(8,128)(2,1)S(1)}, bf16[128,384]{1,0:T(8,128)(2,1)S(1)}, u32[]{:S(2)}, u32[]{:S(2)}) collective-permute-start(bf16[128,384]{1,0:T(8,128)(2,1)S(1)} %get-tuple-element.80), channel_id=1, source_target_pairs={{0,3},{1,2},{2,1},{3,0},{4,7},{5,6},{6,5},{7,4},{8,11},{9,10},{10,... | collective-permute-start | bytes 294920 | tf_op jit(solution)/shard_map/ppermute | solution.py:503
  68.7 5.7 %collective-permute-start.14 = (bf16[128,384]{1,0:T(8,128)(2,1)S(1)}, bf16[128,384]{1,0:T(8,128)(2,1)S(1)}, u32[]{:S(2)}, u32[]{:S(2)}) collective-permute-start(bf16[128,384]{1,0:T(8,128)(2,1)S(1)} %get-tuple-element.73), channel_id=1, source_target_pairs={{0,2},{1,3},{2,0},{3,1},{4,6},{5,7},{6,4},{7,5},{8,10},{9,11},{10,... | collective-permute-start | bytes 294920 | tf_op jit(solution)/shard_map/ppermute | solution.py:503
  69.3 2.2 %collective-permute-start.13 = (bf16[128,384]{1,0:T(8,128)(2,1)S(1)}, bf16[128,384]{1,0:T(8,128)(2,1)S(1)}, u32[]{:S(2)}, u32[]{:S(2)}) collective-permute-start(bf16[128,384]{1,0:T(8,128)(2,1)S(1)} %get-tuple-element.72), channel_id=1, source_target_pairs={{0,1},{1,0},{2,3},{3,2},{4,5},{5,4},{6,7},{7,6},{8,9},{9,8},{10,11... | collective-permute-start | bytes 294920 | tf_op jit(solution)/shard_map/ppermute | solution.py:503
  72.2 4.4 %collective-permute-start.18 = (bf16[128,256]{1,0:T(8,128)(2,1)S(1)}, bf16[128,256]{1,0:T(8,128)(2,1)S(1)}, u32[]{:S(2)}, u32[]{:S(2)}) collective-permute-start(bf16[128,256]{1,0:T(8,128)(2,1)S(1)} %get-tuple-element.78), channel_id=1, source_target_pairs={{0,1},{1,0},{2,3},{3,2},{4,5},{5,4},{6,7},{7,6},{8,9},{9,8},{10,11... | collective-permute-start | bytes 196616 | tf_op jit(solution)/shard_map/ppermute | solution.py:503
  74.4 4.4 %collective-permute-start.19 = (bf16[128,256]{1,0:T(8,128)(2,1)S(1)}, bf16[128,256]{1,0:T(8,128)(2,1)S(1)}, u32[]{:S(2)}, u32[]{:S(2)}) collective-permute-start(bf16[128,256]{1,0:T(8,128)(2,1)S(1)} %get-tuple-element.83), channel_id=1, source_target_pairs={{0,2},{1,3},{2,0},{3,1},{4,6},{5,7},{6,4},{7,5},{8,10},{9,11},{10,... | collective-permute-start | bytes 196616 | tf_op jit(solution)/shard_map/ppermute | solution.py:503
  76.5 4.4 %collective-permute-start.20 = (bf16[128,256]{1,0:T(8,128)(2,1)S(1)}, bf16[128,256]{1,0:T(8,128)(2,1)S(1)}, u32[]{:S(2)}, u32[]{:S(2)}) collective-permute-start(bf16[128,256]{1,0:T(8,128)(2,1)S(1)} %get-tuple-element.84), channel_id=1, source_target_pairs={{0,3},{1,2},{2,1},{3,0},{4,7},{5,6},{6,5},{7,4},{8,11},{9,10},{10,... | collective-permute-start | bytes 196616 | tf_op jit(solution)/shard_map/ppermute | solution.py:503
  78.9 2.0 %copy-start.16 = (bf16[128,2560]{1,0:T(8,128)(2,1)}, bf16[128,2560]{1,0:T(8,128)(2,1)S(1)}, u32[]{:S(2)}) copy-start(bf16[128,2560]{1,0:T(8,128)(2,1)S(1)} %constant_dynamic-update-slice_fusion.1) | copy-start | bytes 1966084

commit v17 on v16

--- a/solution.py
+++ b/solution.py
@@ -189,15 +189,24 @@
     return result
 
 
-def near_kernel(first, counts, queries_of, carries, *refs):
-    n_outs = 4 if carries else 3
+def near_kernel(first, counts, queries_of, extra, *refs):
+    n_outs = 3 + extra
     ins, outs, rooms = refs[: -2 - n_outs], refs[-2 - n_outs : -2], refs[-2:]
     queries, tiles = ins[0], ins[1:]
     mixed_out, levels, done = outs[:3]
     rows = rooms[0].shape[0]
     done[...] = jnp.zeros_like(done)
-    if carries:
-        outs[3][...] = ins[-1][...]
+    if extra:
+
+        @pl.when(inner_frame())
+        def _():
+            for ref, out in zip(tiles, outs[3:-1]):
+                half, count = ref.shape[1] // 2, out.shape[1] // 2
+                out[:, :count] = ref[:rows, half - count : half]
+                out[:, count:] = ref[:rows, 2 * half - count :]
+            info = outs[-1]
+            info[:INFO_ROWS] = tiles[2][rows:, : info.shape[1]]
+            info[INFO_ROWS:] = tiles[4][rows:, : info.shape[1]]
 
     def one_head(used, i):
         found = []
@@ -314,21 +323,21 @@
         finish_own(0, q, (mixed, levels), slots, outs, rooms)
 
 
-def guest_kernel(q, mixed, levels, n1m, n2m, n2o, r1, out, *rooms):
+def guest_kernel(q, mixed, levels, info, n2m, n2o, r1, out, *rooms):
     rows = r1.shape[0]
     z = lax.axis_index("frame")
 
-    def told(ref, group):
-        return ref[rows : rows + 1, group * 128 : (group + 1) * 128].astype(jnp.float32)
+    def told(row, group):
+        return info[row : row + 1, group * 128 : (group + 1) * 128].astype(jnp.float32)
 
     @pl.when(inner_frame())
     def _():
-        near2 = jnp.where(z == 1, told(n1m, 2), told(n1m, 1)) > 0.5
-        near1 = jnp.where(z == 1, told(n1m, 3), told(n1m, 0)) > 0.5
-        picked = told(n2m, 4) == (lax.axis_index("head") // 2).astype(jnp.float32)
+        near2 = jnp.where(z == 1, told(0, 2), told(0, 1)) > 0.5
+        near1 = jnp.where(z == 1, told(0, 3), told(0, 0)) > 0.5
+        picked = told(INFO_ROWS, 4) == (lax.axis_index("head") // 2).astype(jnp.float32)
         slots = [
-            far_tile(n2m, HOME, near2 & picked),
-            far_tile(n2o, HOME, near2 & jnp.logical_not(picked)),
+            far_tile(n2m, 0, near2 & picked),
+            far_tile(n2o, 0, near2 & jnp.logical_not(picked)),
             far_tile(r1, 0, near1),
         ]
 
@@ -550,23 +559,24 @@
         return 4 * chunks * tiles * tile * tile * HEAD_DIM
 
     bf16 = jnp.bfloat16
-    *near, done = run_kernel(
-        functools.partial(near_kernel, 0, ((6, heads), (4, HOME)), own_queries, False),
+    near_mixed, near_levels, done, *kept, info = run_kernel(
+        functools.partial(near_kernel, 0, ((6, heads), (4, HOME)), own_queries, 7),
         None,
         [q, mine, other, n1m, n1o, n2m, n2o],
-        state(heads),
+        state(heads) + [((tile, 2 * (width - cut)), bf16)] * 6 + [((2 * INFO_ROWS, 5 * 128), bf16)],
         (tile, 6 * tile),
         flops(2 * heads, 6),
         10,
     )
+    near = [near_mixed, near_levels]
     r3k, r1_rest = passed(done, r1k, r1_rest)
     r3k = along(r3k, OUTER)
     r1_rest = across(r1_rest)
     r3v = along(after(r1v, swap), OUTER)
     *guest_near, _ = run_kernel(
-        functools.partial(near_kernel, HOME, ((4, guests), (0, 0)), guest_queries, False),
+        functools.partial(near_kernel, 0, ((4, guests), (0, 0)), guest_queries, 0),
         None,
-        [swap, mine, other, n1m, n1o],
+        [swap, *kept[:4]],
         state(guests),
         (tile, 4 * tile),
         flops(2 * guests, 4),
@@ -575,7 +585,7 @@
     (back,) = run_kernel(
         guest_kernel,
         None,
-        [swap, *guest_near, n1m, n2m, n2o, r1_rest],
+        [swap, *guest_near, info, *kept[4:], r1_rest],
         [((2 * tile, width - cut), bf16)],
         (tile, 3 * tile),
         flops(2 * guests, 3),

time: 81.8 us -> 87.2 us (1.066)
  local copies, waits for them, and re-layouts: 7.52 us -> 12.6 us
    unnamed x34 -> x48, local copies, waits for them, and re-layouts: 5.14 us -> 10.2 us
  transfers between devices with their start and end apart: 21 -> 21, of which waited for: 7 -> 7; matrix products, arithmetic and copies ran while one was open for 0% -> 0% of each run, Pallas kernels for 12% -> 11%
where the time goes in v17:
time: 87.2 us; the launch traced here: 86.9 us
  starting transfers between devices  37.8 us (43%)
  waiting for transfers between devices  25.9 us (30%)
  local copies, waits for them, and re-layouts  12.6 us (14%)
  Pallas kernels  9.41 us (11%)
  between operations  0.98 us (1%)
    ppermute x6, starting transfers between devices, along(): return lax.ppermute(array, 'frame', pairs)  27.1 us
    ppermute x10, waiting for transfers between devices, to_head(): return lax.ppermute(array, 'head', [(i, i ^ d) for i in range(4)])  25.8 us
    unnamed x48, local copies, waits for them, and re-layouts  10.2 us
    ppermute x10, starting transfers between devices, to_head(): return lax.ppermute(array, 'head', [(i, i ^ d) for i in range(4)])  9.44 us
    pallas_call x5, Pallas kernels, run_kernel(): pl.pallas_call(kernel, in_specs=[pl.BlockSpec(memory_space=pltpu.SMEM)] *...  7.62 us
  transfers between devices with their start and end apart: 21, of which 7 were waited for; matrix products, arithmetic and copies ran while one was open for 0% of the time, Pallas kernels for 11%

profile of v17, /device:TPU:0, one launch (start us, length us, event | category | flops | bytes accessed | tf_op | source)
XLA Modules:
  0.0 86.9 jit_solution(10333923800134341734)
XLA Ops:
  0.0 1.5 %constant_dynamic-slice_fusion = (bf16[128,640]{1,0:T(8,128)(2,1)S(1)}, bf16[128,640]{1,0:T(8,128)(2,1)S(1)}, bf16[128,640]{1,0:T(8,128)(2,1)S(1)}, bf16[128,640...) fusion(bf16[128,2560]{1,0:T(8,128)(2,1)} %refs_2_.1, ...), kind=kLoop, calls=%fused_computation.13 | loop fusion | bytes 2621456 | tf_op jit(solution)/shard_map/dynamic_slice | solution.py:503
  1.6 0.5 collective-permute-start
  2.1 1.7 %collective-permute-done = bf16[128,2560]{1,0:T(8,128)(2,1)S(1)} collective-permute-done((bf16[128,2560]{1,0:T(8,128)(2,1)S(1)}, bf16[128,2560]{1,0:T(8,128)(2,1)S(1)}, u32[]{:S(2)}, u32[]{:S(2)}) %collective-permute-start) | collective-permute-done | bytes 655392 | tf_op jit(solution)/shard_map/ppermute | solution.py:512
  4.0 2.9 %collective-permute-start.2 = (bf16[256,1280]{1,0:T(8,128)(2,1)S(1)}, bf16[256,1280]{1,0:T(8,128)(2,1)S(1)}, u32[]{:S(2)}, u32[]{:S(2)}) collective-permute-start(bf16[256,1280]{1,0:T(8,128)(2,1)S(1)} %pad_maximum_fusion.2), channel_id=1, source_target_pairs={{0,2},{1,3},{2,0},{3,1},{4,6},{5,7},{6,4},{7,5},{8,10},{9,11},{10,... | collective-permute-start | bytes 1966088 | tf_op jit(solution)/shard_map/ppermute | solution.py:512
  7.6 0.7 shard_map.55
  8.4 0.6 collective-permute-start.6
  9.0 2.7 %collective-permute-start.4 = (bf16[272,1280]{1,0:T(8,128)(2,1)S(1)}, bf16[272,1280]{1,0:T(8,128)(2,1)S(1)}, u32[]{:S(2)}, u32[]{:S(2)}) collective-permute-start(bf16[272,1280]{1,0:T(8,128)(2,1)S(1)} %pad_maximum_fusion.refs_1_), channel_id=1, source_target_pairs={{0,4},{4,0},{8,12},{12,8},{1,5},{5,1},{9,13},{13,9},{2,6},{6,2},{1... | collective-permute-start | bytes 2088968 | tf_op jit(solution)/shard_map/ppermute | solution.py:515
  11.6 10.3 %collective-permute-done.2.refs_2_ = bf16[256,1280]{1,0:T(8,128)(2,1)S(1)} collective-permute-done((bf16[256,1280]{1,0:T(8,128)(2,1)S(1)}, bf16[256,1280]{1,0:T(8,128)(2,1)S(1)}, u32[]{:S(2)}, u32[]{:S(2)}) %collective-permute-start.2) | collective-permute-done | bytes 655392 | tf_op jit(solution)/shard_map/ppermute | solution.py:512
  22.0 3.5 %collective-permute-start.5 = (bf16[256,1280]{1,0:T(8,128)(2,1)S(1)}, bf16[256,1280]{1,0:T(8,128)(2,1)S(1)}, u32[]{:S(2)}, u32[]{:S(2)}) collective-permute-start(bf16[256,1280]{1,0:T(8,128)(2,1)S(1)} %collective-permute-done.2.refs_2_), channel_id=1, source_target_pairs={{0,4},{4,0},{8,12},{12,8},{1,5},{5,1},{9,13},{13,9},{2,6},{6,2},{1... | collective-permute-start | bytes 1966088 | tf_op jit(solution)/shard_map/ppermute | solution.py:515
  25.5 1.6 %collective-permute-start.3 = (bf16[256,640]{1,0:T(8,128)(2,1)S(1)}, bf16[256,640]{1,0:T(8,128)(2,1)S(1)}, u32[]{:S(2)}, u32[]{:S(2)}) collective-permute-start(bf16[256,640]{1,0:T(8,128)(2,1)S(1)} %pad_maximum_fusion.4), channel_id=1, source_target_pairs={{0,2},{1,3},{2,0},{3,1},{4,6},{5,7},{6,4},{7,5},{8,10},{9,11},{10,... | collective-permute-start | bytes 983048 | tf_op jit(solution)/shard_map/ppermute | solution.py:512
  27.0 6.9 %collective-permute-done.3 = bf16[256,640]{1,0:T(8,128)(2,1)S(1)} collective-permute-done((bf16[256,640]{1,0:T(8,128)(2,1)S(1)}, bf16[256,640]{1,0:T(8,128)(2,1)S(1)}, u32[]{:S(2)}, u32[]{:S(2)}) %collective-permute-start.3) | collective-permute-done | bytes 327712 | tf_op jit(solution)/shard_map/ppermute | solution.py:512
  34.0 8.3 %collective-permute-start.10 = (bf16[256,768]{1,0:T(8,128)(2,1)S(1)}, bf16[256,768]{1,0:T(8,128)(2,1)S(1)}, u32[]{:S(2)}, u32[]{:S(2)}) collective-permute-start(bf16[256,768]{1,0:T(8,128)(2,1)S(1)} %shard_map.58), channel_id=1, source_target_pairs={{0,4},{4,0},{8,12},{12,8},{1,5},{5,1},{9,13},{13,9},{2,6},{6,2},{1... | collective-permute-start | bytes 1179656 | tf_op jit(solution)/shard_map/ppermute | solution.py:515
  42.3 0.2 shard_map.57
  42.5 0.1 collective-permute-start.8
  42.6 0.5 collective-permute-start.9
  43.1 2.9 %shard_map.56 = (f32[2560,128]{1,0:T(8,128)S(1)}, f32[2560,128]{1,0:T(8,128)S(1)}, f32[8,128]{1,0:T(8,128)S(1)}, bf16[256,512]{1,0:T(8,128)(2,1)S(1)}, bf16[256,...) custom-call(bf16[512,640]{1,0:T(8,128)(2,1)S(1)} %pad_maximum_fusion, ...), custom_call_target="tpu_custom_call" | custom-call | flops 2013265920 | bytes 4710400 | tf_op jit(solution)/shard_map/pallas_call | solution.py:384
  46.1 0.7 copy-done.10
  46.7 0.6 copy-done.12
  47.4 0.7 copy-done.15
  48.1 0.7 copy-done.17
  48.8 0.7 copy-done.19
  49.5 0.7 copy-done.21
  50.2 0.9 %shard_map.59 = (bf16[256,384]{1,0:T(8,128)(2,1)}, bf16[256,512]{1,0:T(8,128)(2,1)}) custom-call(f32[8,128]{1,0:T(8,128)S(1)} %get-tuple-element.74.done, bf16[256,384]{1,0:T(8,128)(2,1)S(1)} %collective-permute-done.8.refs_0_.r1k, bf16[256,512]{1,0:T(8,128)(2,1)S(1)} %get-tuple-element.75.refs_1_), custom_call_target="tpu_custom_call" | custom-call | tf_op jit(solution)/shard_map/pallas_call | solution.py:373
  51.0 0.1 collective-permute-start.15
  51.1 7.0 %collective-permute-start.11 = (bf16[256,384]{1,0:T(8,128)(2,1)}, bf16[256,384]{1,0:T(8,128)(2,1)}, u32[]{:S(2)}, u32[]{:S(2)}) collective-permute-start(bf16[256,384]{1,0:T(8,128)(2,1)} %get-tuple-element.76), channel_id=1, source_target_pairs={{0,4},{4,0},{8,12},{12,8},{1,5},{5,1},{9,13},{13,9},{2,6},{6,2},{1... | collective-permute-start | bytes 589832 | tf_op jit(solution)/shard_map/ppermute | solution.py:515
  58.2 0.7 copy-done.2
  58.9 1.0 %copy-done.3 = bf16[256,768]{1,0:T(8,128)(2,1)S(1)} copy-done((bf16[256,768]{1,0:T(8,128)(2,1)S(1)}, bf16[256,768]{1,0:T(8,128)(2,1)}, u32[]{:S(2)}) %copy-start.3) | copy-done | bytes 393240
  59.9 0.9 %copy-done.16 = bf16[256,512]{1,0:T(8,128)(2,1)S(1)} copy-done((bf16[256,512]{1,0:T(8,128)(2,1)S(1)}, bf16[256,512]{1,0:T(8,128)(2,1)}, u32[]{:S(2)}) %copy-start.16) | copy-done | bytes 262168
  60.9 0.9 %copy-done.18 = bf16[256,512]{1,0:T(8,128)(2,1)S(1)} copy-done((bf16[256,512]{1,0:T(8,128)(2,1)S(1)}, bf16[256,512]{1,0:T(8,128)(2,1)}, u32[]{:S(2)}) %copy-start.18) | copy-done | bytes 262168
  61.8 0.9 %copy-done.20 = bf16[256,512]{1,0:T(8,128)(2,1)S(1)} copy-done((bf16[256,512]{1,0:T(8,128)(2,1)S(1)}, bf16[256,512]{1,0:T(8,128)(2,1)}, u32[]{:S(2)}) %copy-start.20) | copy-done | bytes 262168
  62.8 0.9 %copy-done.22 = bf16[256,512]{1,0:T(8,128)(2,1)S(1)} copy-done((bf16[256,512]{1,0:T(8,128)(2,1)S(1)}, bf16[256,512]{1,0:T(8,128)(2,1)}, u32[]{:S(2)}) %copy-start.22) | copy-done | bytes 262168
  63.7 0.6 shard_map.61
  64.3 0.4 copy-done.4
  64.7 0.1 copy-done.9
  64.8 0.1 copy-done.11
  64.9 5.7 %collective-permute-start.16 = (bf16[512,256]{1,0:T(8,128)(2,1)S(1)}, bf16[512,256]{1,0:T(8,128)(2,1)S(1)}, u32[]{:S(2)}, u32[]{:S(2)}) collective-permute-start(bf16[512,256]{1,0:T(8,128)(2,1)S(1)} %shard_map.62), channel_id=1, source_target_pairs={{0,4},{4,0},{8,12},{12,8},{1,5},{5,1},{9,13},{13,9},{2,6},{6,2},{1... | collective-permute-start | bytes 786440 | tf_op jit(solution)/shard_map/ppermute | solution.py:515
  70.6 3.5 %shard_map.60 = (bf16[128,384]{1,0:T(8,128)(2,1)S(1)}, bf16[128,384]{1,0:T(8,128)(2,1)S(1)}, bf16[128,384]{1,0:T(8,128)(2,1)S(1)}, bf16[128,384]{1,0:T(8,128)(2,1)S(1)}) custom-call(s32[1,4]{1,0:T(1,128)S(1)} %copy-done.14, bf16[512,640]{1,0:T(8,128)(2,1)S(1)} %pad_maximum_fusion.3.refs_0_.q, f32[2560,128]{1,0:T(8,128)S(1)} %get-tuple-element.66.mixed, ...), custom_call_target="tpu_custom_call" | custom-call | flops 402653184 | bytes 3145728 | tf_op jit(solution)/shard_map/pallas_call | solution.py:384
  74.1 0.1 collective-permute-start.17
  74.2 0.6 collective-permute-start.14
  74.8 1.3 %collective-permute-start.13 = (bf16[128,384]{1,0:T(8,128)(2,1)S(1)}, bf16[128,384]{1,0:T(8,128)(2,1)S(1)}, u32[]{:S(2)}, u32[]{:S(2)}) collective-permute-start(bf16[128,384]{1,0:T(8,128)(2,1)S(1)} %get-tuple-element.79), channel_id=1, source_target_pairs={{0,1},{1,0},{2,3},{3,2},{4,5},{5,4},{6,7},{7,6},{8,9},{9,8},{10,11... | collective-permute-start | bytes 294920 | tf_op jit(solution)/shard_map/ppermute | solution.py:512
  76.1 0.9 collective-permute-done.13
  77.0 0.6 shard_map.63
  77.6 0.4 collective-permute-start.18
  78.0 1.9 %collective-permute-done.14 = bf16[128,384]{1,0:T(8,128)(2,1)S(1)} collective-permute-done((bf16[128,384]{1,0:T(8,128)(2,1)S(1)}, bf16[128,384]{1,0:T(8,128)(2,1)S(1)}, u32[]{:S(2)}, u32[]{:S(2)}) %collective-permute-start.14) | collective-permute-done | bytes 98336 | tf_op jit(solution)/shard_map/ppermute | solution.py:512
  79.8 2.0 %collective-permute-start.19 = (bf16[128,256]{1,0:T(8,128)(2,1)S(1)}, bf16[128,256]{1,0:T(8,128)(2,1)S(1)}, u32[]{:S(2)}, u32[]{:S(2)}) collective-permute-start(bf16[128,256]{1,0:T(8,128)(2,1)S(1)} %get-tuple-element.97), channel_id=1, source_target_pairs={{0,2},{1,3},{2,0},{3,1},{4,6},{5,7},{6,4},{7,5},{8,10},{9,11},{10,... | collective-permute-start | bytes 196616 | tf_op jit(solution)/shard_map/ppermute | solution.py:512
  82.0 2.3 %collective-permute-done.19 = bf16[128,256]{1,0:T(8,128)(2,1)S(1)} collective-permute-done((bf16[128,256]{1,0:T(8,128)(2,1)S(1)}, bf16[128,256]{1,0:T(8,128)(2,1)S(1)}, u32[]{:S(2)}, u32[]{:S(2)}) %collective-permute-start.19) | collective-permute-done | bytes 65568 | tf_op jit(solution)/shard_map/ppermute | solution.py:512
  84.3 1.9 %collective-permute-done.20 = bf16[128,256]{1,0:T(8,128)(2,1)S(1)} collective-permute-done((bf16[128,256]{1,0:T(8,128)(2,1)S(1)}, bf16[128,256]{1,0:T(8,128)(2,1)S(1)}, u32[]{:S(2)}, u32[]{:S(2)}) %collective-permute-start.20) | collective-permute-done | bytes 65568 | tf_op jit(solution)/shard_map/ppermute | solution.py:512
  86.2 0.6 constant_dynamic-update-slice_fusion
  (68 shorter events, 0.7 us)
Async XLA Ops:
  1.6 6.0 %copy-start = (bf16[128,2560]{1,0:T(8,128)(2,1)S(1)}, bf16[128,2560]{1,0:T(8,128)(2,1)}, u32[]{:S(2)}) copy-start(bf16[128,2560]{1,0:T(8,128)(2,1)} %refs_1_.1) | copy-start | bytes 1966084
  1.6 6.0 %copy-start.1 = (bf16[128,2560]{1,0:T(8,128)(2,1)S(1)}, bf16[128,2560]{1,0:T(8,128)(2,1)}, u32[]{:S(2)}) copy-start(bf16[128,2560]{1,0:T(8,128)(2,1)} %refs_2_.1) | copy-start | bytes 1966084
  1.6 6.0 %copy-start.7 = (bf16[128,2560]{1,0:T(8,128)(2,1)S(1)}, bf16[128,2560]{1,0:T(8,128)(2,1)}, u32[]{:S(2)}) copy-start(bf16[128,2560]{1,0:T(8,128)(2,1)} %refs_0_.1) | copy-start | bytes 1966084
  1.6 6.0 %copy-start.14 = (s32[1,4]{1,0:T(1,128)S(1)}, s32[1,4]{1,0:T(1,128)}, u32[]{:S(2)}) copy-start(s32[1,4]{1,0:T(1,128)} %mask.5) | copy-start | bytes 52
  1.6 2.2 %collective-permute-start = (bf16[128,2560]{1,0:T(8,128)(2,1)S(1)}, bf16[128,2560]{1,0:T(8,128)(2,1)S(1)}, u32[]{:S(2)}, u32[]{:S(2)}) collective-permute-start(bf16[128,2560]{1,0:T(8,128)(2,1)S(1)} %pad_maximum_fusion.1), channel_id=1, source_target_pairs={{0,1},{1,0},{2,3},{3,2},{4,5},{5,4},{6,7},{7,6},{8,9},{9,8},{10,11... | collective-permute-start | bytes 1966088 | tf_op jit(solution)/shard_map/ppermute | solution.py:512
  4.0 18.0 %collective-permute-start.2 = (bf16[256,1280]{1,0:T(8,128)(2,1)S(1)}, bf16[256,1280]{1,0:T(8,128)(2,1)S(1)}, u32[]{:S(2)}, u32[]{:S(2)}) collective-permute-start(bf16[256,1280]{1,0:T(8,128)(2,1)S(1)} %pad_maximum_fusion.2), channel_id=1, source_target_pairs={{0,2},{1,3},{2,0},{3,1},{4,6},{5,7},{6,4},{7,5},{8,10},{9,11},{10,... | collective-permute-start | bytes 1966088 | tf_op jit(solution)/shard_map/ppermute | solution.py:512
  8.3 13.7 %collective-permute-start.1 = (bf16[128,1280]{1,0:T(8,128)(2,1)S(1)}, bf16[128,1280]{1,0:T(8,128)(2,1)S(1)}, u32[]{:S(2)}, u32[]{:S(2)}) collective-permute-start(bf16[128,1280]{1,0:T(8,128)(2,1)S(1)} %get-tuple-element.58), channel_id=1, source_target_pairs={{0,1},{1,0},{2,3},{3,2},{4,5},{5,4},{6,7},{7,6},{8,9},{9,8},{10,11... | collective-permute-start | bytes 983048 | tf_op jit(solution)/shard_map/ppermute | solution.py:512
  8.4 25.5 %collective-permute-start.6 = (bf16[272,1280]{1,0:T(8,128)(2,1)S(1)}, bf16[272,1280]{1,0:T(8,128)(2,1)S(1)}, u32[]{:S(2)}, u32[]{:S(2)}) collective-permute-start(bf16[272,1280]{1,0:T(8,128)(2,1)S(1)} %pad_maximum_fusion.refs_1_), channel_id=1, source_target_pairs={{0,1},{1,0},{2,3},{3,2},{4,8},{5,9},{6,10},{7,11},{8,4},{9,5},{10,... | collective-permute-start | bytes 2088968 | tf_op jit(solution)/shard_map/ppermute | solution.py:519
  9.0 33.4 %collective-permute-start.4 = (bf16[272,1280]{1,0:T(8,128)(2,1)S(1)}, bf16[272,1280]{1,0:T(8,128)(2,1)S(1)}, u32[]{:S(2)}, u32[]{:S(2)}) collective-permute-start(bf16[272,1280]{1,0:T(8,128)(2,1)S(1)} %pad_maximum_fusion.refs_1_), channel_id=1, source_target_pairs={{0,4},{4,0},{8,12},{12,8},{1,5},{5,1},{9,13},{13,9},{2,6},{6,2},{1... | collective-permute-start | bytes 2088968 | tf_op jit(solution)/shard_map/ppermute | solution.py:515
  21.9 12.0 %collective-permute-start.7 = (bf16[256,1280]{1,0:T(8,128)(2,1)S(1)}, bf16[256,1280]{1,0:T(8,128)(2,1)S(1)}, u32[]{:S(2)}, u32[]{:S(2)}) collective-permute-start(bf16[256,1280]{1,0:T(8,128)(2,1)S(1)} %collective-permute-done.2.refs_2_), channel_id=1, source_target_pairs={{0,1},{1,0},{2,3},{3,2},{4,8},{5,9},{6,10},{7,11},{8,4},{9,5},{10,... | collective-permute-start | bytes 1966088 | tf_op jit(solution)/shard_map/ppermute | solution.py:519
  22.0 20.4 %collective-permute-start.5 = (bf16[256,1280]{1,0:T(8,128)(2,1)S(1)}, bf16[256,1280]{1,0:T(8,128)(2,1)S(1)}, u32[]{:S(2)}, u32[]{:S(2)}) collective-permute-start(bf16[256,1280]{1,0:T(8,128)(2,1)S(1)} %collective-permute-done.2.refs_2_), channel_id=1, source_target_pairs={{0,4},{4,0},{8,12},{12,8},{1,5},{5,1},{9,13},{13,9},{2,6},{6,2},{1... | collective-permute-start | bytes 1966088 | tf_op jit(solution)/shard_map/ppermute | solution.py:515
  25.5 8.4 %collective-permute-start.3 = (bf16[256,640]{1,0:T(8,128)(2,1)S(1)}, bf16[256,640]{1,0:T(8,128)(2,1)S(1)}, u32[]{:S(2)}, u32[]{:S(2)}) collective-permute-start(bf16[256,640]{1,0:T(8,128)(2,1)S(1)} %pad_maximum_fusion.4), channel_id=1, source_target_pairs={{0,2},{1,3},{2,0},{3,1},{4,6},{5,7},{6,4},{7,5},{8,10},{9,11},{10,... | collective-permute-start | bytes 983048 | tf_op jit(solution)/shard_map/ppermute | solution.py:512
  34.0 24.1 %collective-permute-start.10 = (bf16[256,768]{1,0:T(8,128)(2,1)S(1)}, bf16[256,768]{1,0:T(8,128)(2,1)S(1)}, u32[]{:S(2)}, u32[]{:S(2)}) collective-permute-start(bf16[256,768]{1,0:T(8,128)(2,1)S(1)} %shard_map.58), channel_id=1, source_target_pairs={{0,4},{4,0},{8,12},{12,8},{1,5},{5,1},{9,13},{13,9},{2,6},{6,2},{1... | collective-permute-start | bytes 1179656 | tf_op jit(solution)/shard_map/ppermute | solution.py:515
  42.5 7.6 %collective-permute-start.8 = (bf16[256,384]{1,0:T(8,128)(2,1)S(1)}, bf16[256,384]{1,0:T(8,128)(2,1)S(1)}, u32[]{:S(2)}, u32[]{:S(2)}) collective-permute-start(bf16[256,384]{1,0:T(8,128)(2,1)S(1)} %get-tuple-element.71), channel_id=1, source_target_pairs={{0,1},{1,0},{2,3},{3,2},{4,8},{5,9},{6,10},{7,11},{8,4},{9,5},{10,... | collective-permute-start | bytes 589832 | tf_op jit(solution)/shard_map/ppermute | solution.py:519
  42.6 15.5 %collective-permute-start.9 = (bf16[256,384]{1,0:T(8,128)(2,1)S(1)}, bf16[256,384]{1,0:T(8,128)(2,1)}, u32[]{:S(2)}, u32[]{:S(2)}) collective-permute-start(bf16[256,384]{1,0:T(8,128)(2,1)S(1)} %get-tuple-element.73), channel_id=1, source_target_pairs={{0,1},{1,0},{2,3},{3,2},{4,8},{5,9},{6,10},{7,11},{8,4},{9,5},{10,... | collective-permute-start | bytes 589832 | tf_op jit(solution)/shard_map/ppermute | solution.py:519
  46.0 0.7 copy-start.10
  46.7 0.6 copy-start.12
  47.4 0.7 copy-start.15
  48.1 0.7 copy-start.17
  48.8 0.7 copy-start.19
  49.5 0.7 copy-start.21
  50.2 8.0 %copy-start.8 = (bf16[256,512]{1,0:T(8,128)(2,1)}, bf16[256,512]{1,0:T(8,128)(2,1)S(1)}, u32[]{:S(2)}) copy-start(bf16[256,512]{1,0:T(8,128)(2,1)S(1)} %get-tuple-element.89.n2m) | copy-start | bytes 786436
  50.2 8.0 %copy-start.5 = (bf16[256,384]{1,0:T(8,128)(2,1)}, bf16[256,384]{1,0:T(8,128)(2,1)S(1)}, u32[]{:S(2)}) copy-start(bf16[256,384]{1,0:T(8,128)(2,1)S(1)} %collective-permute-done.8.refs_0_.r1k) | copy-start | bytes 589828
  51.0 13.3 %collective-permute-start.15 = (bf16[256,512]{1,0:T(8,128)(2,1)}, bf16[256,512]{1,0:T(8,128)(2,1)S(1)}, u32[]{:S(2)}, u32[]{:S(2)}) collective-permute-start(bf16[256,512]{1,0:T(8,128)(2,1)} %get-tuple-element.81), channel_id=1, source_target_pairs={{0,1},{1,0},{2,3},{3,2},{4,8},{5,9},{6,10},{7,11},{8,4},{9,5},{10,... | collective-permute-start | bytes 786440 | tf_op jit(solution)/shard_map/ppermute | solution.py:519
  51.1 19.4 %collective-permute-start.11 = (bf16[256,384]{1,0:T(8,128)(2,1)}, bf16[256,384]{1,0:T(8,128)(2,1)}, u32[]{:S(2)}, u32[]{:S(2)}) collective-permute-start(bf16[256,384]{1,0:T(8,128)(2,1)} %get-tuple-element.76), channel_id=1, source_target_pairs={{0,4},{4,0},{8,12},{12,8},{1,5},{5,1},{9,13},{13,9},{2,6},{6,2},{1... | collective-permute-start | bytes 589832 | tf_op jit(solution)/shard_map/ppermute | solution.py:515
  58.1 0.7 copy-start.2
  58.9 11.7 %collective-permute-start.12 = (bf16[256,384]{1,0:T(8,128)(2,1)}, bf16[256,384]{1,0:T(8,128)(2,1)}, u32[]{:S(2)}, u32[]{:S(2)}) collective-permute-start(bf16[256,384]{1,0:T(8,128)(2,1)} %collective-permute-done.9.r1v), channel_id=1, source_target_pairs={{0,4},{4,0},{8,12},{12,8},{1,5},{5,1},{9,13},{13,9},{2,6},{6,2},{1... | collective-permute-start | bytes 589832 | tf_op jit(solution)/shard_map/ppermute | solution.py:515
  58.9 1.0 %copy-start.3 = (bf16[256,768]{1,0:T(8,128)(2,1)S(1)}, bf16[256,768]{1,0:T(8,128)(2,1)}, u32[]{:S(2)}) copy-start(bf16[256,768]{1,0:T(8,128)(2,1)} %copy-done.2) | copy-start | bytes 1179652
  59.9 0.9 %copy-start.16 = (bf16[256,512]{1,0:T(8,128)(2,1)S(1)}, bf16[256,512]{1,0:T(8,128)(2,1)}, u32[]{:S(2)}) copy-start(bf16[256,512]{1,0:T(8,128)(2,1)} %copy-done.15) | copy-start | bytes 786436
  60.9 0.9 %copy-start.18 = (bf16[256,512]{1,0:T(8,128)(2,1)S(1)}, bf16[256,512]{1,0:T(8,128)(2,1)}, u32[]{:S(2)}) copy-start(bf16[256,512]{1,0:T(8,128)(2,1)} %copy-done.17) | copy-start | bytes 786436
  61.8 0.9 %copy-start.20 = (bf16[256,512]{1,0:T(8,128)(2,1)S(1)}, bf16[256,512]{1,0:T(8,128)(2,1)}, u32[]{:S(2)}) copy-start(bf16[256,512]{1,0:T(8,128)(2,1)} %copy-done.19) | copy-start | bytes 786436
  62.8 0.9 %copy-start.22 = (bf16[256,512]{1,0:T(8,128)(2,1)S(1)}, bf16[256,512]{1,0:T(8,128)(2,1)}, u32[]{:S(2)}) copy-start(bf16[256,512]{1,0:T(8,128)(2,1)} %copy-done.21) | copy-start | bytes 786436
  63.7 1.0 %copy-start.4 = (bf16[256,768]{1,0:T(8,128)(2,1)S(1)}, bf16[256,768]{1,0:T(8,128)(2,1)}, u32[]{:S(2)}) copy-start(bf16[256,768]{1,0:T(8,128)(2,1)} %copy-done.2) | copy-start | bytes 1179652
  63.7 1.1 %copy-start.9 = (bf16[256,512]{1,0:T(8,128)(2,1)S(1)}, bf16[256,512]{1,0:T(8,128)(2,1)}, u32[]{:S(2)}) copy-start(bf16[256,512]{1,0:T(8,128)(2,1)} %copy-done.8) | copy-start | bytes 786436
  63.7 1.1 %copy-start.11 = (bf16[256,512]{1,0:T(8,128)(2,1)S(1)}, bf16[256,512]{1,0:T(8,128)(2,1)}, u32[]{:S(2)}) copy-start(bf16[256,512]{1,0:T(8,128)(2,1)} %copy-done.10) | copy-start | bytes 786436
  63.7 1.1 %copy-start.13 = (bf16[32,640]{1,0:T(8,128)(2,1)S(1)}, bf16[32,640]{1,0:T(8,128)(2,1)}, u32[]{:S(2)}) copy-start(bf16[32,640]{1,0:T(8,128)(2,1)} %copy-done.12) | copy-start | bytes 122884
  64.3 6.2 %copy-start.6 = (bf16[256,384]{1,0:T(8,128)(2,1)S(1)}, bf16[256,384]{1,0:T(8,128)(2,1)}, u32[]{:S(2)}) copy-start(bf16[256,384]{1,0:T(8,128)(2,1)} %copy-done.5) | copy-start | bytes 589828
  64.9 12.1 %collective-permute-start.16 = (bf16[512,256]{1,0:T(8,128)(2,1)S(1)}, bf16[512,256]{1,0:T(8,128)(2,1)S(1)}, u32[]{:S(2)}, u32[]{:S(2)}) collective-permute-start(bf16[512,256]{1,0:T(8,128)(2,1)S(1)} %shard_map.62), channel_id=1, source_target_pairs={{0,4},{4,0},{8,12},{12,8},{1,5},{5,1},{9,13},{13,9},{2,6},{6,2},{1... | collective-permute-start | bytes 786440 | tf_op jit(solution)/shard_map/ppermute | solution.py:515
  74.1 7.8 %collective-permute-start.17 = (bf16[128,384]{1,0:T(8,128)(2,1)S(1)}, bf16[128,384]{1,0:T(8,128)(2,1)S(1)}, u32[]{:S(2)}, u32[]{:S(2)}) collective-permute-start(bf16[128,384]{1,0:T(8,128)(2,1)S(1)} %get-tuple-element.94), channel_id=1, source_target_pairs={{0,3},{1,2},{2,1},{3,0},{4,7},{5,6},{6,5},{7,4},{8,11},{9,10},{10,... | collective-permute-start | bytes 294920 | tf_op jit(solution)/shard_map/ppermute | solution.py:512
  74.2 5.7 %collective-permute-start.14 = (bf16[128,384]{1,0:T(8,128)(2,1)S(1)}, bf16[128,384]{1,0:T(8,128)(2,1)S(1)}, u32[]{:S(2)}, u32[]{:S(2)}) collective-permute-start(bf16[128,384]{1,0:T(8,128)(2,1)S(1)} %get-tuple-element.80), channel_id=1, source_target_pairs={{0,2},{1,3},{2,0},{3,1},{4,6},{5,7},{6,4},{7,5},{8,10},{9,11},{10,... | collective-permute-start | bytes 294920 | tf_op jit(solution)/shard_map/ppermute | solution.py:512
  74.8 2.2 %collective-permute-start.13 = (bf16[128,384]{1,0:T(8,128)(2,1)S(1)}, bf16[128,384]{1,0:T(8,128)(2,1)S(1)}, u32[]{:S(2)}, u32[]{:S(2)}) collective-permute-start(bf16[128,384]{1,0:T(8,128)(2,1)S(1)} %get-tuple-element.79), channel_id=1, source_target_pairs={{0,1},{1,0},{2,3},{3,2},{4,5},{5,4},{6,7},{7,6},{8,9},{9,8},{10,11... | collective-permute-start | bytes 294920 | tf_op jit(solution)/shard_map/ppermute | solution.py:512
  77.6 4.3 %collective-permute-start.18 = (bf16[128,256]{1,0:T(8,128)(2,1)S(1)}, bf16[128,256]{1,0:T(8,128)(2,1)S(1)}, u32[]{:S(2)}, u32[]{:S(2)}) collective-permute-start(bf16[128,256]{1,0:T(8,128)(2,1)S(1)} %get-tuple-element.92), channel_id=1, source_target_pairs={{0,1},{1,0},{2,3},{3,2},{4,5},{5,4},{6,7},{7,6},{8,9},{9,8},{10,11... | collective-permute-start | bytes 196616 | tf_op jit(solution)/shard_map/ppermute | solution.py:512
  79.8 4.4 %collective-permute-start.19 = (bf16[128,256]{1,0:T(8,128)(2,1)S(1)}, bf16[128,256]{1,0:T(8,128)(2,1)S(1)}, u32[]{:S(2)}, u32[]{:S(2)}) collective-permute-start(bf16[128,256]{1,0:T(8,128)(2,1)S(1)} %get-tuple-element.97), channel_id=1, source_target_pairs={{0,2},{1,3},{2,0},{3,1},{4,6},{5,7},{6,4},{7,5},{8,10},{9,11},{10,... | collective-permute-start | bytes 196616 | tf_op jit(solution)/shard_map/ppermute | solution.py:512
  81.9 4.3 %collective-permute-start.20 = (bf16[128,256]{1,0:T(8,128)(2,1)S(1)}, bf16[128,256]{1,0:T(8,128)(2,1)S(1)}, u32[]{:S(2)}, u32[]{:S(2)}) collective-permute-start(bf16[128,256]{1,0:T(8,128)(2,1)S(1)} %get-tuple-element.98), channel_id=1, source_target_pairs={{0,3},{1,2},{2,1},{3,0},{4,7},{5,6},{6,5},{7,4},{8,11},{9,10},{10,... | collective-permute-start | bytes 196616 | tf_op jit(solution)/shard_map/ppermute | solution.py:512
  84.3 1.9 %copy-start.23 = (bf16[128,2560]{1,0:T(8,128)(2,1)}, bf16[128,2560]{1,0:T(8,128)(2,1)S(1)}, u32[]{:S(2)}) copy-start(bf16[128,2560]{1,0:T(8,128)(2,1)S(1)} %constant_dynamic-update-slice_fusion.1) | copy-start | bytes 1966084

commit v18 on v16

--- a/solution.py
+++ b/solution.py
@@ -557,7 +557,7 @@
         state(heads),
         (tile, 6 * tile),
         flops(2 * heads, 6),
-        10,
+        16,
     )
     r3k, r1_rest = passed(done, r1k, r1_rest)
     r3k = along(r3k, OUTER)
@@ -570,7 +570,7 @@
         state(guests),
         (tile, 4 * tile),
         flops(2 * guests, 4),
-        10,
+        16,
     )
     (back,) = run_kernel(
         guest_kernel,
@@ -579,7 +579,7 @@
         [((2 * tile, width - cut), bf16)],
         (tile, 3 * tile),
         flops(2 * guests, 3),
-        10,
+        16,
     )
     back = along(back, OUTER)
     out = run_kernel(
@@ -589,7 +589,7 @@
         [((rows, cut), bf16)] * 4,
         (tile, 2 * tile),
         flops(2 * HOME, 2),
-        10,
+        16,
     )
     pieces = [(to_head(out[d], d) if d else out[0], d, 0) for d in range(4)]
     out = run_kernel(
@@ -599,7 +599,7 @@
         [((rows, width - cut), bf16)] * 4,
         (tile, tile),
         flops(2 * guests, 1),
-        10,
+        16,
     )
     moved = [out[0]] + [to_head(out[d], d) for d in (1, 2, 3)]
     pieces = [(after(piece, moved[1] if d == 3 else out[1]) if d > 1 else piece, d, at) for piece, d, at in pieces]

time: 81.8 us -> 81.8 us (level)
  no operation moved by 1% of the time
where the time goes in v18:
time: 81.8 us; the launch traced here: 81.5 us
  starting transfers between devices  37.4 us (46%)
  waiting for transfers between devices  25.9 us (32%)
  Pallas kernels  9.4 us (11%)
  local copies, waits for them, and re-layouts  7.52 us (9%)
  between operations  1 us (1%)
    ppermute x6, starting transfers between devices, along(): return lax.ppermute(array, 'frame', pairs)  26.8 us
    ppermute x10, waiting for transfers between devices, to_head(): return lax.ppermute(array, 'head', [(i, i ^ d) for i in range(4)])  25.8 us
    ppermute x10, starting transfers between devices, to_head(): return lax.ppermute(array, 'head', [(i, i ^ d) for i in range(4)])  9.46 us
    pallas_call x5, Pallas kernels, run_kernel(): pl.pallas_call(kernel, in_specs=[pl.BlockSpec(memory_space=pltpu.SMEM)] *...  7.66 us
    unnamed x34, local copies, waits for them, and re-layouts  5.14 us
  transfers between devices with their start and end apart: 21, of which 7 were waited for; matrix products, arithmetic and copies ran while one was open for 0% of the time, Pallas kernels for 12%

profile of v18, /device:TPU:0, one launch (start us, length us, event | category | flops | bytes accessed | tf_op | source)
XLA Modules:
  0.0 81.5 jit_solution(9720473503970080607)
XLA Ops:
  0.0 1.5 %constant_dynamic-slice_fusion = (bf16[128,640]{1,0:T(8,128)(2,1)S(1)}, bf16[128,640]{1,0:T(8,128)(2,1)S(1)}, bf16[128,640]{1,0:T(8,128)(2,1)S(1)}, bf16[128,640...) fusion(bf16[128,2560]{1,0:T(8,128)(2,1)} %refs_2_.1, ...), kind=kLoop, calls=%fused_computation.13 | loop fusion | bytes 2621456 | tf_op jit(solution)/shard_map/dynamic_slice | solution.py:494
  1.5 0.1 pad_maximum_fusion.1
  1.6 0.0 copy-start.6
  1.6 0.0 copy-start.12
  1.6 0.0 copy-start.15
  1.6 0.5 collective-permute-start
  2.1 1.7 %collective-permute-done = bf16[128,2560]{1,0:T(8,128)(2,1)S(1)} collective-permute-done((bf16[128,2560]{1,0:T(8,128)(2,1)S(1)}, bf16[128,2560]{1,0:T(8,128)(2,1)S(1)}, u32[]{:S(2)}, u32[]{:S(2)}) %collective-permute-start) | collective-permute-done | bytes 655392 | tf_op jit(solution)/shard_map/ppermute | solution.py:503
  4.0 2.9 %collective-permute-start.2 = (bf16[256,1280]{1,0:T(8,128)(2,1)S(1)}, bf16[256,1280]{1,0:T(8,128)(2,1)S(1)}, u32[]{:S(2)}, u32[]{:S(2)}) collective-permute-start(bf16[256,1280]{1,0:T(8,128)(2,1)S(1)} %pad_maximum_fusion.2), channel_id=1, source_target_pairs={{0,2},{1,3},{2,0},{3,1},{4,6},{5,7},{6,4},{7,5},{8,10},{9,11},{10,... | collective-permute-start | bytes 1966088 | tf_op jit(solution)/shard_map/ppermute | solution.py:503
  7.6 0.7 shard_map.55
  8.3 0.1 collective-permute-start.1
  8.3 0.1 pad_maximum_fusion.refs_1_
  8.4 0.6 collective-permute-start.6
  9.0 2.7 %collective-permute-start.4 = (bf16[272,1280]{1,0:T(8,128)(2,1)S(1)}, bf16[272,1280]{1,0:T(8,128)(2,1)S(1)}, u32[]{:S(2)}, u32[]{:S(2)}) collective-permute-start(bf16[272,1280]{1,0:T(8,128)(2,1)S(1)} %pad_maximum_fusion.refs_1_), channel_id=1, source_target_pairs={{0,4},{4,0},{8,12},{12,8},{1,5},{5,1},{9,13},{13,9},{2,6},{6,2},{1... | collective-permute-start | bytes 2088968 | tf_op jit(solution)/shard_map/ppermute | solution.py:506
  11.6 10.3 %collective-permute-done.2.refs_2_ = bf16[256,1280]{1,0:T(8,128)(2,1)S(1)} collective-permute-done((bf16[256,1280]{1,0:T(8,128)(2,1)S(1)}, bf16[256,1280]{1,0:T(8,128)(2,1)S(1)}, u32[]{:S(2)}, u32[]{:S(2)}) %collective-permute-start.2) | collective-permute-done | bytes 655392 | tf_op jit(solution)/shard_map/ppermute | solution.py:503
  22.0 3.5 %collective-permute-start.5 = (bf16[256,1280]{1,0:T(8,128)(2,1)S(1)}, bf16[256,1280]{1,0:T(8,128)(2,1)S(1)}, u32[]{:S(2)}, u32[]{:S(2)}) collective-permute-start(bf16[256,1280]{1,0:T(8,128)(2,1)S(1)} %collective-permute-done.2.refs_2_), channel_id=1, source_target_pairs={{0,4},{4,0},{8,12},{12,8},{1,5},{5,1},{9,13},{13,9},{2,6},{6,2},{1... | collective-permute-start | bytes 1966088 | tf_op jit(solution)/shard_map/ppermute | solution.py:506
  25.5 1.6 %collective-permute-start.3 = (bf16[256,640]{1,0:T(8,128)(2,1)S(1)}, bf16[256,640]{1,0:T(8,128)(2,1)S(1)}, u32[]{:S(2)}, u32[]{:S(2)}) collective-permute-start(bf16[256,640]{1,0:T(8,128)(2,1)S(1)} %pad_maximum_fusion.4), channel_id=1, source_target_pairs={{0,2},{1,3},{2,0},{3,1},{4,6},{5,7},{6,4},{7,5},{8,10},{9,11},{10,... | collective-permute-start | bytes 983048 | tf_op jit(solution)/shard_map/ppermute | solution.py:503
  27.0 6.9 %collective-permute-done.3 = bf16[256,640]{1,0:T(8,128)(2,1)S(1)} collective-permute-done((bf16[256,640]{1,0:T(8,128)(2,1)S(1)}, bf16[256,640]{1,0:T(8,128)(2,1)S(1)}, u32[]{:S(2)}, u32[]{:S(2)}) %collective-permute-start.3) | collective-permute-done | bytes 327712 | tf_op jit(solution)/shard_map/ppermute | solution.py:503
  33.9 0.1 pad_maximum_fusion.3.refs_0_.q
  34.0 0.1 shard_map.58
  34.1 8.3 %collective-permute-start.10 = (bf16[256,768]{1,0:T(8,128)(2,1)S(1)}, bf16[256,768]{1,0:T(8,128)(2,1)S(1)}, u32[]{:S(2)}, u32[]{:S(2)}) collective-permute-start(bf16[256,768]{1,0:T(8,128)(2,1)S(1)} %shard_map.58), channel_id=1, source_target_pairs={{0,4},{4,0},{8,12},{12,8},{1,5},{5,1},{9,13},{13,9},{2,6},{6,2},{1... | collective-permute-start | bytes 1179656 | tf_op jit(solution)/shard_map/ppermute | solution.py:506
  42.4 0.2 shard_map.57
  42.5 0.1 collective-permute-start.8
  42.6 0.5 collective-permute-start.9
  43.1 2.9 %shard_map.56 = (f32[2560,128]{1,0:T(8,128)S(1)}, f32[2560,128]{1,0:T(8,128)S(1)}, f32[8,128]{1,0:T(8,128)S(1)}) custom-call(bf16[512,640]{1,0:T(8,128)(2,1)S(1)} %pad_maximum_fusion.3.refs_0_.q, bf16[272,1280]{1,0:T(8,128)(2,1)S(1)} %pad_maximum_fusion.refs_1_, bf16[256,1280]{1,0:T(8,128)(2,1)S(1)} %collective-permute-done.2.refs_2_, ...), custom_call_target="tpu_custom_call" | custom-call | flops 2013265920 | bytes 4710400 | tf_op jit(solution)/shard_map/pallas_call | solution.py:375
  46.1 1.1 %copy-done = f32[2560,128]{1,0:T(8,128)} copy-done((f32[2560,128]{1,0:T(8,128)}, f32[2560,128]{1,0:T(8,128)S(1)}, u32[]{:S(2)}) %copy-start) | copy-done | bytes 1310744
  47.2 0.8 %shard_map.59 = (bf16[256,384]{1,0:T(8,128)(2,1)}, bf16[256,512]{1,0:T(8,128)(2,1)}) custom-call(f32[8,128]{1,0:T(8,128)S(1)} %get-tuple-element.67.done, bf16[256,384]{1,0:T(8,128)(2,1)S(1)} %collective-permute-done.8.refs_0_.r1k, bf16[256,512]{1,0:T(8,128)(2,1)S(1)} %get-tuple-element.68.refs_1_), custom_call_target="tpu_custom_call" | custom-call | tf_op jit(solution)/shard_map/pallas_call | solution.py:364
  48.1 0.1 collective-permute-start.15
  48.1 6.9 %collective-permute-start.11 = (bf16[256,384]{1,0:T(8,128)(2,1)}, bf16[256,384]{1,0:T(8,128)(2,1)}, u32[]{:S(2)}, u32[]{:S(2)}) collective-permute-start(bf16[256,384]{1,0:T(8,128)(2,1)} %get-tuple-element.69), channel_id=1, source_target_pairs={{0,4},{4,0},{8,12},{12,8},{1,5},{5,1},{9,13},{13,9},{2,6},{6,2},{1... | collective-permute-start | bytes 589832 | tf_op jit(solution)/shard_map/ppermute | solution.py:506
  55.0 0.1 collective-permute-start.12
  55.1 1.1 %copy-done.3 = bf16[272,1280]{1,0:T(8,128)(2,1)S(1)} copy-done((bf16[272,1280]{1,0:T(8,128)(2,1)S(1)}, bf16[272,1280]{1,0:T(8,128)(2,1)}, u32[]{:S(2)}) %copy-start.3) | copy-done | bytes 696344
  56.2 1.1 %copy-done.9 = bf16[256,1280]{1,0:T(8,128)(2,1)S(1)} copy-done((bf16[256,1280]{1,0:T(8,128)(2,1)S(1)}, bf16[256,1280]{1,0:T(8,128)(2,1)}, u32[]{:S(2)}) %copy-start.9) | copy-done | bytes 655384
  57.3 1.1 %copy-done.14 = bf16[256,1280]{1,0:T(8,128)(2,1)S(1)} copy-done((bf16[256,1280]{1,0:T(8,128)(2,1)S(1)}, bf16[256,1280]{1,0:T(8,128)(2,1)}, u32[]{:S(2)}) %copy-start.14) | copy-done | bytes 655384
  58.3 0.6 shard_map.61
  58.9 0.5 copy-done.5
  59.5 0.2 copy-done.11
  59.6 5.4 %collective-permute-start.16 = (bf16[512,256]{1,0:T(8,128)(2,1)S(1)}, bf16[512,256]{1,0:T(8,128)(2,1)S(1)}, u32[]{:S(2)}, u32[]{:S(2)}) collective-permute-start(bf16[512,256]{1,0:T(8,128)(2,1)S(1)} %shard_map.62), channel_id=1, source_target_pairs={{0,4},{4,0},{8,12},{12,8},{1,5},{5,1},{9,13},{13,9},{2,6},{6,2},{1... | collective-permute-start | bytes 786440 | tf_op jit(solution)/shard_map/ppermute | solution.py:506
  65.1 3.5 %shard_map.60 = (bf16[128,384]{1,0:T(8,128)(2,1)S(1)}, bf16[128,384]{1,0:T(8,128)(2,1)S(1)}, bf16[128,384]{1,0:T(8,128)(2,1)S(1)}, bf16[128,384]{1,0:T(8,128)(2,1)S(1)}) custom-call(s32[1,4]{1,0:T(1,128)S(1)} %copy-done.15, bf16[512,640]{1,0:T(8,128)(2,1)S(1)} %pad_maximum_fusion.3.refs_0_.q, f32[2560,128]{1,0:T(8,128)S(1)} %get-tuple-element.59.mixed, ...), custom_call_target="tpu_custom_call" | custom-call | flops 402653184 | bytes 3145728 | tf_op jit(solution)/shard_map/pallas_call | solution.py:375
  68.6 0.1 collective-permute-start.17
  68.7 0.6 collective-permute-start.14
  69.3 1.2 %collective-permute-start.13 = (bf16[128,384]{1,0:T(8,128)(2,1)S(1)}, bf16[128,384]{1,0:T(8,128)(2,1)S(1)}, u32[]{:S(2)}, u32[]{:S(2)}) collective-permute-start(bf16[128,384]{1,0:T(8,128)(2,1)S(1)} %get-tuple-element.72), channel_id=1, source_target_pairs={{0,1},{1,0},{2,3},{3,2},{4,5},{5,4},{6,7},{7,6},{8,9},{9,8},{10,11... | collective-permute-start | bytes 294920 | tf_op jit(solution)/shard_map/ppermute | solution.py:503
  70.6 0.9 %collective-permute-done.13 = bf16[128,384]{1,0:T(8,128)(2,1)S(1)} collective-permute-done((bf16[128,384]{1,0:T(8,128)(2,1)S(1)}, bf16[128,384]{1,0:T(8,128)(2,1)S(1)}, u32[]{:S(2)}, u32[]{:S(2)}) %collective-permute-start.13) | collective-permute-done | bytes 98336 | tf_op jit(solution)/shard_map/ppermute | solution.py:503
  71.5 0.6 shard_map.63
  72.1 0.4 collective-permute-start.18
  72.6 1.9 %collective-permute-done.14 = bf16[128,384]{1,0:T(8,128)(2,1)S(1)} collective-permute-done((bf16[128,384]{1,0:T(8,128)(2,1)S(1)}, bf16[128,384]{1,0:T(8,128)(2,1)S(1)}, u32[]{:S(2)}, u32[]{:S(2)}) %collective-permute-start.14) | collective-permute-done | bytes 98336 | tf_op jit(solution)/shard_map/ppermute | solution.py:503
  74.4 2.0 %collective-permute-start.19 = (bf16[128,256]{1,0:T(8,128)(2,1)S(1)}, bf16[128,256]{1,0:T(8,128)(2,1)S(1)}, u32[]{:S(2)}, u32[]{:S(2)}) collective-permute-start(bf16[128,256]{1,0:T(8,128)(2,1)S(1)} %get-tuple-element.83), channel_id=1, source_target_pairs={{0,2},{1,3},{2,0},{3,1},{4,6},{5,7},{6,4},{7,5},{8,10},{9,11},{10,... | collective-permute-start | bytes 196616 | tf_op jit(solution)/shard_map/ppermute | solution.py:503
  76.6 2.3 %collective-permute-done.19 = bf16[128,256]{1,0:T(8,128)(2,1)S(1)} collective-permute-done((bf16[128,256]{1,0:T(8,128)(2,1)S(1)}, bf16[128,256]{1,0:T(8,128)(2,1)S(1)}, u32[]{:S(2)}, u32[]{:S(2)}) %collective-permute-start.19) | collective-permute-done | bytes 65568 | tf_op jit(solution)/shard_map/ppermute | solution.py:503
  78.9 2.0 %collective-permute-done.20 = bf16[128,256]{1,0:T(8,128)(2,1)S(1)} collective-permute-done((bf16[128,256]{1,0:T(8,128)(2,1)S(1)}, bf16[128,256]{1,0:T(8,128)(2,1)S(1)}, u32[]{:S(2)}, u32[]{:S(2)}) %collective-permute-start.20) | collective-permute-done | bytes 65568 | tf_op jit(solution)/shard_map/ppermute | solution.py:503
  80.8 0.6 constant_dynamic-update-slice_fusion
  (54 shorter events, 0.4 us)
Async XLA Ops:
  1.6 6.0 %copy-start.6 = (bf16[128,2560]{1,0:T(8,128)(2,1)S(1)}, bf16[128,2560]{1,0:T(8,128)(2,1)}, u32[]{:S(2)}) copy-start(bf16[128,2560]{1,0:T(8,128)(2,1)} %refs_1_.1) | copy-start | bytes 1966084
  1.6 6.0 %copy-start.7 = (bf16[128,2560]{1,0:T(8,128)(2,1)S(1)}, bf16[128,2560]{1,0:T(8,128)(2,1)}, u32[]{:S(2)}) copy-start(bf16[128,2560]{1,0:T(8,128)(2,1)} %refs_2_.1) | copy-start | bytes 1966084
  1.6 6.0 %copy-start.12 = (bf16[128,2560]{1,0:T(8,128)(2,1)S(1)}, bf16[128,2560]{1,0:T(8,128)(2,1)}, u32[]{:S(2)}) copy-start(bf16[128,2560]{1,0:T(8,128)(2,1)} %refs_0_.1) | copy-start | bytes 1966084
  1.6 6.0 %copy-start.15 = (s32[1,4]{1,0:T(1,128)S(1)}, s32[1,4]{1,0:T(1,128)}, u32[]{:S(2)}) copy-start(s32[1,4]{1,0:T(1,128)} %mask.5) | copy-start | bytes 52
  1.6 2.2 %collective-permute-start = (bf16[128,2560]{1,0:T(8,128)(2,1)S(1)}, bf16[128,2560]{1,0:T(8,128)(2,1)S(1)}, u32[]{:S(2)}, u32[]{:S(2)}) collective-permute-start(bf16[128,2560]{1,0:T(8,128)(2,1)S(1)} %pad_maximum_fusion.1), channel_id=1, source_target_pairs={{0,1},{1,0},{2,3},{3,2},{4,5},{5,4},{6,7},{7,6},{8,9},{9,8},{10,11... | collective-permute-start | bytes 1966088 | tf_op jit(solution)/shard_map/ppermute | solution.py:503
  4.0 18.0 %collective-permute-start.2 = (bf16[256,1280]{1,0:T(8,128)(2,1)S(1)}, bf16[256,1280]{1,0:T(8,128)(2,1)S(1)}, u32[]{:S(2)}, u32[]{:S(2)}) collective-permute-start(bf16[256,1280]{1,0:T(8,128)(2,1)S(1)} %pad_maximum_fusion.2), channel_id=1, source_target_pairs={{0,2},{1,3},{2,0},{3,1},{4,6},{5,7},{6,4},{7,5},{8,10},{9,11},{10,... | collective-permute-start | bytes 1966088 | tf_op jit(solution)/shard_map/ppermute | solution.py:503
  8.3 13.7 %collective-permute-start.1 = (bf16[128,1280]{1,0:T(8,128)(2,1)S(1)}, bf16[128,1280]{1,0:T(8,128)(2,1)S(1)}, u32[]{:S(2)}, u32[]{:S(2)}) collective-permute-start(bf16[128,1280]{1,0:T(8,128)(2,1)S(1)} %get-tuple-element.51), channel_id=1, source_target_pairs={{0,1},{1,0},{2,3},{3,2},{4,5},{5,4},{6,7},{7,6},{8,9},{9,8},{10,11... | collective-permute-start | bytes 983048 | tf_op jit(solution)/shard_map/ppermute | solution.py:503
  8.4 34.7 %copy-start.2 = (bf16[272,1280]{1,0:T(8,128)(2,1)}, bf16[272,1280]{1,0:T(8,128)(2,1)S(1)}, u32[]{:S(2)}) copy-start(bf16[272,1280]{1,0:T(8,128)(2,1)S(1)} %pad_maximum_fusion.refs_1_) | copy-start | bytes 2088964
  8.4 25.5 %collective-permute-start.6 = (bf16[272,1280]{1,0:T(8,128)(2,1)S(1)}, bf16[272,1280]{1,0:T(8,128)(2,1)S(1)}, u32[]{:S(2)}, u32[]{:S(2)}) collective-permute-start(bf16[272,1280]{1,0:T(8,128)(2,1)S(1)} %pad_maximum_fusion.refs_1_), channel_id=1, source_target_pairs={{0,1},{1,0},{2,3},{3,2},{4,8},{5,9},{6,10},{7,11},{8,4},{9,5},{10,... | collective-permute-start | bytes 2088968 | tf_op jit(solution)/shard_map/ppermute | solution.py:510
  9.0 33.4 %collective-permute-start.4 = (bf16[272,1280]{1,0:T(8,128)(2,1)S(1)}, bf16[272,1280]{1,0:T(8,128)(2,1)S(1)}, u32[]{:S(2)}, u32[]{:S(2)}) collective-permute-start(bf16[272,1280]{1,0:T(8,128)(2,1)S(1)} %pad_maximum_fusion.refs_1_), channel_id=1, source_target_pairs={{0,4},{4,0},{8,12},{12,8},{1,5},{5,1},{9,13},{13,9},{2,6},{6,2},{1... | collective-permute-start | bytes 2088968 | tf_op jit(solution)/shard_map/ppermute | solution.py:506
  21.9 21.2 %copy-start.13 = (bf16[256,1280]{1,0:T(8,128)(2,1)}, bf16[256,1280]{1,0:T(8,128)(2,1)S(1)}, u32[]{:S(2)}) copy-start(bf16[256,1280]{1,0:T(8,128)(2,1)S(1)} %collective-permute-done.2.refs_2_) | copy-start | bytes 1966084
  21.9 12.1 %collective-permute-start.7 = (bf16[256,1280]{1,0:T(8,128)(2,1)S(1)}, bf16[256,1280]{1,0:T(8,128)(2,1)S(1)}, u32[]{:S(2)}, u32[]{:S(2)}) collective-permute-start(bf16[256,1280]{1,0:T(8,128)(2,1)S(1)} %collective-permute-done.2.refs_2_), channel_id=1, source_target_pairs={{0,1},{1,0},{2,3},{3,2},{4,8},{5,9},{6,10},{7,11},{8,4},{9,5},{10,... | collective-permute-start | bytes 1966088 | tf_op jit(solution)/shard_map/ppermute | solution.py:510
  22.0 20.4 %collective-permute-start.5 = (bf16[256,1280]{1,0:T(8,128)(2,1)S(1)}, bf16[256,1280]{1,0:T(8,128)(2,1)S(1)}, u32[]{:S(2)}, u32[]{:S(2)}) collective-permute-start(bf16[256,1280]{1,0:T(8,128)(2,1)S(1)} %collective-permute-done.2.refs_2_), channel_id=1, source_target_pairs={{0,4},{4,0},{8,12},{12,8},{1,5},{5,1},{9,13},{13,9},{2,6},{6,2},{1... | collective-permute-start | bytes 1966088 | tf_op jit(solution)/shard_map/ppermute | solution.py:506
  25.5 8.4 %collective-permute-start.3 = (bf16[256,640]{1,0:T(8,128)(2,1)S(1)}, bf16[256,640]{1,0:T(8,128)(2,1)S(1)}, u32[]{:S(2)}, u32[]{:S(2)}) collective-permute-start(bf16[256,640]{1,0:T(8,128)(2,1)S(1)} %pad_maximum_fusion.4), channel_id=1, source_target_pairs={{0,2},{1,3},{2,0},{3,1},{4,6},{5,7},{6,4},{7,5},{8,10},{9,11},{10,... | collective-permute-start | bytes 983048 | tf_op jit(solution)/shard_map/ppermute | solution.py:503
  34.0 9.2 %copy-start.4 = (bf16[272,1280]{1,0:T(8,128)(2,1)}, bf16[272,1280]{1,0:T(8,128)(2,1)S(1)}, u32[]{:S(2)}) copy-start(bf16[272,1280]{1,0:T(8,128)(2,1)S(1)} %collective-permute-done.6.refs_5_.mine.n2m) | copy-start | bytes 2088964
  34.0 9.1 %copy-start.10 = (bf16[256,1280]{1,0:T(8,128)(2,1)}, bf16[256,1280]{1,0:T(8,128)(2,1)S(1)}, u32[]{:S(2)}) copy-start(bf16[256,1280]{1,0:T(8,128)(2,1)S(1)} %collective-permute-done.7.refs_6_.other.n2o) | copy-start | bytes 1966084
  34.1 20.9 %collective-permute-start.10 = (bf16[256,768]{1,0:T(8,128)(2,1)S(1)}, bf16[256,768]{1,0:T(8,128)(2,1)S(1)}, u32[]{:S(2)}, u32[]{:S(2)}) collective-permute-start(bf16[256,768]{1,0:T(8,128)(2,1)S(1)} %shard_map.58), channel_id=1, source_target_pairs={{0,4},{4,0},{8,12},{12,8},{1,5},{5,1},{9,13},{13,9},{2,6},{6,2},{1... | collective-permute-start | bytes 1179656 | tf_op jit(solution)/shard_map/ppermute | solution.py:506
  42.4 3.7 %copy-start.8 = (bf16[256,1280]{1,0:T(8,128)(2,1)}, bf16[256,1280]{1,0:T(8,128)(2,1)S(1)}, u32[]{:S(2)}) copy-start(bf16[256,1280]{1,0:T(8,128)(2,1)S(1)} %collective-permute-done.5.refs_4_.other) | copy-start | bytes 1966084
  42.5 4.7 %collective-permute-start.8 = (bf16[256,384]{1,0:T(8,128)(2,1)S(1)}, bf16[256,384]{1,0:T(8,128)(2,1)S(1)}, u32[]{:S(2)}, u32[]{:S(2)}) collective-permute-start(bf16[256,384]{1,0:T(8,128)(2,1)S(1)} %get-tuple-element.64), channel_id=1, source_target_pairs={{0,1},{1,0},{2,3},{3,2},{4,8},{5,9},{6,10},{7,11},{8,4},{9,5},{10,... | collective-permute-start | bytes 589832 | tf_op jit(solution)/shard_map/ppermute | solution.py:510
  42.6 12.4 %collective-permute-start.9 = (bf16[256,384]{1,0:T(8,128)(2,1)S(1)}, bf16[256,384]{1,0:T(8,128)(2,1)}, u32[]{:S(2)}, u32[]{:S(2)}) collective-permute-start(bf16[256,384]{1,0:T(8,128)(2,1)S(1)} %get-tuple-element.66), channel_id=1, source_target_pairs={{0,1},{1,0},{2,3},{3,2},{4,8},{5,9},{6,10},{7,11},{8,4},{9,5},{10,... | collective-permute-start | bytes 589832 | tf_op jit(solution)/shard_map/ppermute | solution.py:510
  46.1 1.1 %copy-start = (f32[2560,128]{1,0:T(8,128)}, f32[2560,128]{1,0:T(8,128)S(1)}, u32[]{:S(2)}) copy-start(f32[2560,128]{1,0:T(8,128)S(1)} %get-tuple-element.60.levels) | copy-start | bytes 3932164
  48.1 10.9 %collective-permute-start.15 = (bf16[256,512]{1,0:T(8,128)(2,1)}, bf16[256,512]{1,0:T(8,128)(2,1)S(1)}, u32[]{:S(2)}, u32[]{:S(2)}) collective-permute-start(bf16[256,512]{1,0:T(8,128)(2,1)} %get-tuple-element.74), channel_id=1, source_target_pairs={{0,1},{1,0},{2,3},{3,2},{4,8},{5,9},{6,10},{7,11},{8,4},{9,5},{10,... | collective-permute-start | bytes 786440 | tf_op jit(solution)/shard_map/ppermute | solution.py:510
  48.1 17.0 %collective-permute-start.11 = (bf16[256,384]{1,0:T(8,128)(2,1)}, bf16[256,384]{1,0:T(8,128)(2,1)}, u32[]{:S(2)}, u32[]{:S(2)}) collective-permute-start(bf16[256,384]{1,0:T(8,128)(2,1)} %get-tuple-element.69), channel_id=1, source_target_pairs={{0,4},{4,0},{8,12},{12,8},{1,5},{5,1},{9,13},{13,9},{2,6},{6,2},{1... | collective-permute-start | bytes 589832 | tf_op jit(solution)/shard_map/ppermute | solution.py:506
  55.0 10.1 %collective-permute-start.12 = (bf16[256,384]{1,0:T(8,128)(2,1)}, bf16[256,384]{1,0:T(8,128)(2,1)}, u32[]{:S(2)}, u32[]{:S(2)}) collective-permute-start(bf16[256,384]{1,0:T(8,128)(2,1)} %collective-permute-done.9.r1v), channel_id=1, source_target_pairs={{0,4},{4,0},{8,12},{12,8},{1,5},{5,1},{9,13},{13,9},{2,6},{6,2},{1... | collective-permute-start | bytes 589832 | tf_op jit(solution)/shard_map/ppermute | solution.py:506
  55.1 1.1 %copy-start.3 = (bf16[272,1280]{1,0:T(8,128)(2,1)S(1)}, bf16[272,1280]{1,0:T(8,128)(2,1)}, u32[]{:S(2)}) copy-start(bf16[272,1280]{1,0:T(8,128)(2,1)} %copy-done.2) | copy-start | bytes 2088964
  56.2 1.1 %copy-start.9 = (bf16[256,1280]{1,0:T(8,128)(2,1)S(1)}, bf16[256,1280]{1,0:T(8,128)(2,1)}, u32[]{:S(2)}) copy-start(bf16[256,1280]{1,0:T(8,128)(2,1)} %copy-done.8) | copy-start | bytes 1966084
  57.3 1.1 %copy-start.14 = (bf16[256,1280]{1,0:T(8,128)(2,1)S(1)}, bf16[256,1280]{1,0:T(8,128)(2,1)}, u32[]{:S(2)}) copy-start(bf16[256,1280]{1,0:T(8,128)(2,1)} %copy-done.13) | copy-start | bytes 1966084
  58.3 1.1 %copy-start.5 = (bf16[272,1280]{1,0:T(8,128)(2,1)S(1)}, bf16[272,1280]{1,0:T(8,128)(2,1)}, u32[]{:S(2)}) copy-start(bf16[272,1280]{1,0:T(8,128)(2,1)} %copy-done.4) | copy-start | bytes 2088964
  58.3 1.3 %copy-start.11 = (bf16[256,1280]{1,0:T(8,128)(2,1)S(1)}, bf16[256,1280]{1,0:T(8,128)(2,1)}, u32[]{:S(2)}) copy-start(bf16[256,1280]{1,0:T(8,128)(2,1)} %copy-done.10) | copy-start | bytes 1966084
  59.6 5.4 %copy-start.1 = (f32[2560,128]{1,0:T(8,128)S(1)}, f32[2560,128]{1,0:T(8,128)}, u32[]{:S(2)}) copy-start(f32[2560,128]{1,0:T(8,128)} %copy-done) | copy-start | bytes 3932164
  59.6 11.9 %collective-permute-start.16 = (bf16[512,256]{1,0:T(8,128)(2,1)S(1)}, bf16[512,256]{1,0:T(8,128)(2,1)S(1)}, u32[]{:S(2)}, u32[]{:S(2)}) collective-permute-start(bf16[512,256]{1,0:T(8,128)(2,1)S(1)} %shard_map.62), channel_id=1, source_target_pairs={{0,4},{4,0},{8,12},{12,8},{1,5},{5,1},{9,13},{13,9},{2,6},{6,2},{1... | collective-permute-start | bytes 786440 | tf_op jit(solution)/shard_map/ppermute | solution.py:506
  68.6 7.8 %collective-permute-start.17 = (bf16[128,384]{1,0:T(8,128)(2,1)S(1)}, bf16[128,384]{1,0:T(8,128)(2,1)S(1)}, u32[]{:S(2)}, u32[]{:S(2)}) collective-permute-start(bf16[128,384]{1,0:T(8,128)(2,1)S(1)} %get-tuple-element.80), channel_id=1, source_target_pairs={{0,3},{1,2},{2,1},{3,0},{4,7},{5,6},{6,5},{7,4},{8,11},{9,10},{10,... | collective-permute-start | bytes 294920 | tf_op jit(solution)/shard_map/ppermute | solution.py:503
  68.7 5.7 %collective-permute-start.14 = (bf16[128,384]{1,0:T(8,128)(2,1)S(1)}, bf16[128,384]{1,0:T(8,128)(2,1)S(1)}, u32[]{:S(2)}, u32[]{:S(2)}) collective-permute-start(bf16[128,384]{1,0:T(8,128)(2,1)S(1)} %get-tuple-element.73), channel_id=1, source_target_pairs={{0,2},{1,3},{2,0},{3,1},{4,6},{5,7},{6,4},{7,5},{8,10},{9,11},{10,... | collective-permute-start | bytes 294920 | tf_op jit(solution)/shard_map/ppermute | solution.py:503
  69.3 2.2 %collective-permute-start.13 = (bf16[128,384]{1,0:T(8,128)(2,1)S(1)}, bf16[128,384]{1,0:T(8,128)(2,1)S(1)}, u32[]{:S(2)}, u32[]{:S(2)}) collective-permute-start(bf16[128,384]{1,0:T(8,128)(2,1)S(1)} %get-tuple-element.72), channel_id=1, source_target_pairs={{0,1},{1,0},{2,3},{3,2},{4,5},{5,4},{6,7},{7,6},{8,9},{9,8},{10,11... | collective-permute-start | bytes 294920 | tf_op jit(solution)/shard_map/ppermute | solution.py:503
  72.1 4.4 %collective-permute-start.18 = (bf16[128,256]{1,0:T(8,128)(2,1)S(1)}, bf16[128,256]{1,0:T(8,128)(2,1)S(1)}, u32[]{:S(2)}, u32[]{:S(2)}) collective-permute-start(bf16[128,256]{1,0:T(8,128)(2,1)S(1)} %get-tuple-element.78), channel_id=1, source_target_pairs={{0,1},{1,0},{2,3},{3,2},{4,5},{5,4},{6,7},{7,6},{8,9},{9,8},{10,11... | collective-permute-start | bytes 196616 | tf_op jit(solution)/shard_map/ppermute | solution.py:503
  74.4 4.4 %collective-permute-start.19 = (bf16[128,256]{1,0:T(8,128)(2,1)S(1)}, bf16[128,256]{1,0:T(8,128)(2,1)S(1)}, u32[]{:S(2)}, u32[]{:S(2)}) collective-permute-start(bf16[128,256]{1,0:T(8,128)(2,1)S(1)} %get-tuple-element.83), channel_id=1, source_target_pairs={{0,2},{1,3},{2,0},{3,1},{4,6},{5,7},{6,4},{7,5},{8,10},{9,11},{10,... | collective-permute-start | bytes 196616 | tf_op jit(solution)/shard_map/ppermute | solution.py:503
  76.5 4.4 %collective-permute-start.20 = (bf16[128,256]{1,0:T(8,128)(2,1)S(1)}, bf16[128,256]{1,0:T(8,128)(2,1)S(1)}, u32[]{:S(2)}, u32[]{:S(2)}) collective-permute-start(bf16[128,256]{1,0:T(8,128)(2,1)S(1)} %get-tuple-element.84), channel_id=1, source_target_pairs={{0,3},{1,2},{2,1},{3,0},{4,7},{5,6},{6,5},{7,4},{8,11},{9,10},{10,... | collective-permute-start | bytes 196616 | tf_op jit(solution)/shard_map/ppermute | solution.py:503
  78.9 2.0 %copy-start.16 = (bf16[128,2560]{1,0:T(8,128)(2,1)}, bf16[128,2560]{1,0:T(8,128)(2,1)S(1)}, u32[]{:S(2)}) copy-start(bf16[128,2560]{1,0:T(8,128)(2,1)S(1)} %constant_dynamic-update-slice_fusion.1) | copy-start | bytes 1966084

commit v19 on v18

--- a/solution.py
+++ b/solution.py
@@ -155,7 +155,7 @@
     return lax.all_to_all(result, "head", split_axis=0, concat_axis=1, tiled=True)
 
 
-HOME = 3
+HOME = 4
 INFO_ROWS = 16
 OUTER = [(0, 1), (1, 0), (2, 3), (3, 2)]
 FACTOR = SCALE * LOG2E

time: 81.8 us -> 97.1 us (1.19)
  waiting for transfers between devices: 25.9 us -> 40.9 us
  Pallas kernels: 9.4 us -> 10.9 us
  starting transfers between devices: 37.4 us -> 36.3 us
    ppermute x6, waiting for transfers between devices: 0.02 us -> 17.8 us  [along(): return lax.ppermute(array, 'frame', pairs)]
    unnamed x34 -> x14, local copies, waits for them, and re-layouts: 5.14 us -> 1.49 us
    ppermute x10, waiting for transfers between devices: 25.8 us -> 22.4 us  [to_head(): return lax.ppermute(array, 'head', [(i, i ^ d) for i in range(4)])]
    dynamic_update_slice x8, local copies, waits for them, and re-layouts: 0.75 us -> 3.44 us  [four_frames(): lax.dynamic_update_slice_in_dim(result, piece, (h ^ d) * width + begin, a...]
    pallas_call x5, Pallas kernels: 7.66 us -> 9.95 us  [run_kernel(): pl.pallas_call(kernel, in_specs=[pl.BlockSpec(memory_space=pltpu.SMEM)] *...]
  transfers between devices with their start and end apart: 21 -> 21, of which waited for: 7 -> 10; matrix products, arithmetic and copies ran while one was open for 0% -> 3% of each run, Pallas kernels for 12% -> 11%
where the time goes in v19:
time: 97.1 us; the launch traced here: 95.9 us
  waiting for transfers between devices  40.9 us (42%)
  starting transfers between devices  36.3 us (37%)
  Pallas kernels  10.9 us (11%)
  local copies, waits for them, and re-layouts  6.57 us (7%)
    ppermute x6, starting transfers between devices, along(): return lax.ppermute(array, 'frame', pairs)  26.4 us
    ppermute x10, waiting for transfers between devices, to_head(): return lax.ppermute(array, 'head', [(i, i ^ d) for i in range(4)])  22.4 us
    ppermute x6, waiting for transfers between devices, along(): return lax.ppermute(array, 'frame', pairs)  17.8 us
    pallas_call x5, Pallas kernels, run_kernel(): pl.pallas_call(kernel, in_specs=[pl.BlockSpec(memory_space=pltpu.SMEM)] *...  9.95 us
    ppermute x10, starting transfers between devices, to_head(): return lax.ppermute(array, 'head', [(i, i ^ d) for i in range(4)])  8.77 us
    dynamic_update_slice x8, local copies, waits for them, and re-layouts, four_frames(): lax.dynamic_update_slice_in_dim(result, piece, (h ^ d) * width + begin, a...  3.44 us
  transfers between devices with their start and end apart: 21, of which 10 were waited for; matrix products, arithmetic and copies ran while one was open for 3% of the time, Pallas kernels for 11%

profile of v19, /device:TPU:0, one launch (start us, length us, event | category | flops | bytes accessed | tf_op | source)
XLA Modules:
  0.0 95.9 jit_solution(12787693345758853687)
XLA Ops:
  0.0 1.5 %constant_dynamic-slice_fusion = (bf16[128,640]{1,0:T(8,128)(2,1)S(1)}, bf16[128,640]{1,0:T(8,128)(2,1)S(1)}, bf16[128,640]{1,0:T(8,128)(2,1)S(1)}, bf16[128,640...) fusion(bf16[128,2560]{1,0:T(8,128)(2,1)} %refs_2_.1, ...), kind=kLoop, calls=%fused_computation.13 | loop fusion | bytes 2621456 | tf_op jit(solution)/shard_map/dynamic_slice | solution.py:494
  1.5 0.1 pad_maximum_fusion.1
  1.6 0.0 copy-start
  1.6 0.0 copy-start.1
  1.6 0.0 copy-start.2
  1.6 0.5 collective-permute-start
  2.2 1.7 %collective-permute-done = bf16[128,2560]{1,0:T(8,128)(2,1)S(1)} collective-permute-done((bf16[128,2560]{1,0:T(8,128)(2,1)S(1)}, bf16[128,2560]{1,0:T(8,128)(2,1)S(1)}, u32[]{:S(2)}, u32[]{:S(2)}) %collective-permute-start) | collective-permute-done | bytes 655392 | tf_op jit(solution)/shard_map/ppermute | solution.py:503
  4.0 2.9 %collective-permute-start.2 = (bf16[256,1280]{1,0:T(8,128)(2,1)S(1)}, bf16[256,1280]{1,0:T(8,128)(2,1)S(1)}, u32[]{:S(2)}, u32[]{:S(2)}) collective-permute-start(bf16[256,1280]{1,0:T(8,128)(2,1)S(1)} %pad_maximum_fusion.2), channel_id=1, source_target_pairs={{0,2},{1,3},{2,0},{3,1},{4,6},{5,7},{6,4},{7,5},{8,10},{9,11},{10,... | collective-permute-start | bytes 1966088 | tf_op jit(solution)/shard_map/ppermute | solution.py:503
  7.6 0.7 shard_map.55
  8.3 0.1 collective-permute-start.1
  8.4 0.1 pad_maximum_fusion.refs_1_
  8.4 0.6 collective-permute-start.6
  9.0 13.0 %collective-permute-done.2.refs_2_ = bf16[256,1280]{1,0:T(8,128)(2,1)S(1)} collective-permute-done((bf16[256,1280]{1,0:T(8,128)(2,1)S(1)}, bf16[256,1280]{1,0:T(8,128)(2,1)S(1)}, u32[]{:S(2)}, u32[]{:S(2)}) %collective-permute-start.2) | collective-permute-done | bytes 655392 | tf_op jit(solution)/shard_map/ppermute | solution.py:503
  22.0 1.8 %collective-permute-start.3 = (bf16[256,640]{1,0:T(8,128)(2,1)S(1)}, bf16[256,640]{1,0:T(8,128)(2,1)S(1)}, u32[]{:S(2)}, u32[]{:S(2)}) collective-permute-start(bf16[256,640]{1,0:T(8,128)(2,1)S(1)} %pad_maximum_fusion.4), channel_id=1, source_target_pairs={{0,2},{1,3},{2,0},{3,1},{4,6},{5,7},{6,4},{7,5},{8,10},{9,11},{10,... | collective-permute-start | bytes 983048 | tf_op jit(solution)/shard_map/ppermute | solution.py:503
  23.8 3.1 %collective-permute-start.4 = (bf16[272,1280]{1,0:T(8,128)(2,1)S(1)}, bf16[272,1280]{1,0:T(8,128)(2,1)S(1)}, u32[]{:S(2)}, u32[]{:S(2)}) collective-permute-start(bf16[272,1280]{1,0:T(8,128)(2,1)S(1)} %pad_maximum_fusion.refs_1_), channel_id=1, source_target_pairs={{0,4},{4,0},{8,12},{12,8},{1,5},{5,1},{9,13},{13,9},{2,6},{6,2},{1... | collective-permute-start | bytes 2088968 | tf_op jit(solution)/shard_map/ppermute | solution.py:506
  27.0 0.0 collective-permute-start.5
  27.0 5.2 %collective-permute-done.3 = bf16[256,640]{1,0:T(8,128)(2,1)S(1)} collective-permute-done((bf16[256,640]{1,0:T(8,128)(2,1)S(1)}, bf16[256,640]{1,0:T(8,128)(2,1)S(1)}, u32[]{:S(2)}, u32[]{:S(2)}) %collective-permute-start.3) | collective-permute-done | bytes 327712 | tf_op jit(solution)/shard_map/ppermute | solution.py:503
  32.2 0.1 pad_maximum_fusion.3.refs_0_.q
  32.3 0.1 shard_map.58
  32.4 10.0 %collective-permute-start.10 = (bf16[256,1024]{1,0:T(8,128)(2,1)S(1)}, bf16[256,1024]{1,0:T(8,128)(2,1)S(1)}, u32[]{:S(2)}, u32[]{:S(2)}) collective-permute-start(bf16[256,1024]{1,0:T(8,128)(2,1)S(1)} %shard_map.58), channel_id=1, source_target_pairs={{0,4},{4,0},{8,12},{12,8},{1,5},{5,1},{9,13},{13,9},{2,6},{6,2},{1... | collective-permute-start | bytes 1572872 | tf_op jit(solution)/shard_map/ppermute | solution.py:506
  42.3 1.1 %collective-permute-done.4.refs_3_.mine.n1m = bf16[272,1280]{1,0:T(8,128)(2,1)S(1)} collective-permute-done((bf16[272,1280]{1,0:T(8,128)(2,1)S(1)}, bf16[272,1280]{1,0:T(8,128)(2,1)S(1)}, u32[]{:S(2)}, u32[]{:S(2)}) %collective-permute-start.4) | collective-permute-done | bytes 696352 | tf_op jit(solution)/shard_map/ppermute | solution.py:506
  43.5 14.0 %collective-permute-done.5.refs_4_.other = bf16[256,1280]{1,0:T(8,128)(2,1)S(1)} collective-permute-done((bf16[256,1280]{1,0:T(8,128)(2,1)S(1)}, bf16[256,1280]{1,0:T(8,128)(2,1)S(1)}, u32[]{:S(2)}, u32[]{:S(2)}) %collective-permute-start.5) | collective-permute-done | bytes 655392 | tf_op jit(solution)/shard_map/ppermute | solution.py:506
  57.5 0.2 shard_map.57
  57.7 0.1 collective-permute-start.8
  57.8 0.5 collective-permute-start.9
  58.3 3.9 %shard_map.56 = (f32[2560,128]{1,0:T(8,128)S(1)}, f32[2560,128]{1,0:T(8,128)S(1)}, f32[8,128]{1,0:T(8,128)S(1)}) custom-call(bf16[512,640]{1,0:T(8,128)(2,1)S(1)} %pad_maximum_fusion.3.refs_0_.q, bf16[272,1280]{1,0:T(8,128)(2,1)S(1)} %pad_maximum_fusion.refs_1_, bf16[256,1280]{1,0:T(8,128)(2,1)S(1)} %collective-permute-done.2.refs_2_, ...), custom_call_target="tpu_custom_call" | custom-call | flops 2013265920 | bytes 4710400 | tf_op jit(solution)/shard_map/pallas_call | solution.py:375
  62.3 6.5 %collective-permute-start.11 = (bf16[256,512]{1,0:T(8,128)(2,1)S(1)}, bf16[256,512]{1,0:T(8,128)(2,1)S(1)}, u32[]{:S(2)}, u32[]{:S(2)}) collective-permute-start(bf16[256,512]{1,0:T(8,128)(2,1)S(1)} %get-tuple-element.69), channel_id=1, source_target_pairs={{0,4},{4,0},{8,12},{12,8},{1,5},{5,1},{9,13},{13,9},{2,6},{6,2},{1... | collective-permute-start | bytes 786440 | tf_op jit(solution)/shard_map/ppermute | solution.py:506
  68.8 1.4 %collective-permute-start.12 = (bf16[256,512]{1,0:T(8,128)(2,1)S(1)}, bf16[256,512]{1,0:T(8,128)(2,1)S(1)}, u32[]{:S(2)}, u32[]{:S(2)}) collective-permute-start(bf16[256,512]{1,0:T(8,128)(2,1)S(1)} %collective-permute-done.9.r1v), channel_id=1, source_target_pairs={{0,4},{4,0},{8,12},{12,8},{1,5},{5,1},{9,13},{13,9},{2,6},{6,2},{1... | collective-permute-start | bytes 786440 | tf_op jit(solution)/shard_map/ppermute | solution.py:506
  70.1 0.6 shard_map.61
  70.7 0.8 collective-permute-done.15.r1
  71.5 5.5 %collective-permute-start.16 = (bf16[512,128]{1,0:T(8,128)(2,1)S(1)}, bf16[512,128]{1,0:T(8,128)(2,1)}, u32[]{:S(2)}, u32[]{:S(2)}) collective-permute-start(bf16[512,128]{1,0:T(8,128)(2,1)S(1)} %shard_map.62), channel_id=1, source_target_pairs={{0,4},{4,0},{8,12},{12,8},{1,5},{5,1},{9,13},{13,9},{2,6},{6,2},{1... | collective-permute-start | bytes 393224 | tf_op jit(solution)/shard_map/ppermute | solution.py:506
  76.9 2.6 %collective-permute-done.12.r3v = bf16[256,512]{1,0:T(8,128)(2,1)S(1)} collective-permute-done((bf16[256,512]{1,0:T(8,128)(2,1)S(1)}, bf16[256,512]{1,0:T(8,128)(2,1)S(1)}, u32[]{:S(2)}, u32[]{:S(2)}) %collective-permute-start.12) | collective-permute-done | bytes 262176 | tf_op jit(solution)/shard_map/ppermute | solution.py:506
  79.5 4.5 %shard_map.60 = (bf16[128,512]{1,0:T(8,128)(2,1)S(1)}, bf16[128,512]{1,0:T(8,128)(2,1)}, bf16[128,512]{1,0:T(8,128)(2,1)}, bf16[128,512]{1,0:T(8,128)(2,1)}) custom-call(s32[1,4]{1,0:T(1,128)S(1)} %copy-done.5, bf16[512,640]{1,0:T(8,128)(2,1)S(1)} %pad_maximum_fusion.3.refs_0_.q, f32[2560,128]{1,0:T(8,128)S(1)} %get-tuple-element.59.mixed, ...), custom_call_target="tpu_custom_call" | custom-call | flops 536870912 | bytes 3538944 | tf_op jit(solution)/shard_map/pallas_call | solution.py:375
  83.9 0.6 copy-done.3
  84.6 0.5 collective-permute-start.14
  85.1 1.4 %collective-permute-start.13 = (bf16[128,512]{1,0:T(8,128)(2,1)}, bf16[128,512]{1,0:T(8,128)(2,1)}, u32[]{:S(2)}, u32[]{:S(2)}) collective-permute-start(bf16[128,512]{1,0:T(8,128)(2,1)} %get-tuple-element.72), channel_id=1, source_target_pairs={{0,1},{1,0},{2,3},{3,2},{4,5},{5,4},{6,7},{7,6},{8,9},{9,8},{10,11... | collective-permute-start | bytes 393224 | tf_op jit(solution)/shard_map/ppermute | solution.py:503
  86.5 1.0 %shard_map.63 = (bf16[128,128]{1,0:T(8,128)(2,1)S(1)}, bf16[128,128]{1,0:T(8,128)(2,1)S(1)}, bf16[128,128]{1,0:T(8,128)(2,1)S(1)}, bf16[128,128]{1,0:T(8,128)(2,1)S(1)}) custom-call(s32[1,4]{1,0:T(1,128)S(1)} %copy-done.5, bf16[512,640]{1,0:T(8,128)(2,1)S(1)} %pad_maximum_fusion.3.refs_0_.q, f32[2560,128]{1,0:T(8,128)S(1)} %get-tuple-element.59.mixed, ...), custom_call_target="tpu_custom_call" | custom-call | flops 67108864 | bytes 2228224 | tf_op jit(solution)/shard_map/pallas_call | solution.py:375
  87.4 0.1 collective-permute-start.18
  87.5 0.7 collective-permute-start.19
  88.3 0.4 collective-permute-done.18
  88.7 0.8 collective-permute-start.20
  89.5 1.2 %collective-permute-done.17 = bf16[128,512]{1,0:T(8,128)(2,1)} collective-permute-done((bf16[128,512]{1,0:T(8,128)(2,1)}, bf16[128,512]{1,0:T(8,128)(2,1)}, u32[]{:S(2)}, u32[]{:S(2)}) %collective-permute-start.17) | collective-permute-done | bytes 131104 | tf_op jit(solution)/shard_map/ppermute | solution.py:503
  90.7 0.9 collective-permute-done.14
  91.6 0.9 constant_dynamic-update-slice_fusion.6
  92.5 0.9 constant_dynamic-update-slice_fusion.5
  93.4 0.9 constant_dynamic-update-slice_fusion.4
  94.5 0.8 copy-done.6
  95.3 0.6 constant_dynamic-update-slice_fusion
  (34 shorter events, 0.4 us)
Async XLA Ops:
  1.6 6.0 %copy-start = (bf16[128,2560]{1,0:T(8,128)(2,1)S(1)}, bf16[128,2560]{1,0:T(8,128)(2,1)}, u32[]{:S(2)}) copy-start(bf16[128,2560]{1,0:T(8,128)(2,1)} %refs_1_.1) | copy-start | bytes 1966084
  1.6 6.0 %copy-start.1 = (bf16[128,2560]{1,0:T(8,128)(2,1)S(1)}, bf16[128,2560]{1,0:T(8,128)(2,1)}, u32[]{:S(2)}) copy-start(bf16[128,2560]{1,0:T(8,128)(2,1)} %refs_2_.1) | copy-start | bytes 1966084
  1.6 6.0 %copy-start.2 = (bf16[128,2560]{1,0:T(8,128)(2,1)S(1)}, bf16[128,2560]{1,0:T(8,128)(2,1)}, u32[]{:S(2)}) copy-start(bf16[128,2560]{1,0:T(8,128)(2,1)} %refs_0_.1) | copy-start | bytes 1966084
  1.6 6.0 %copy-start.5 = (s32[1,4]{1,0:T(1,128)S(1)}, s32[1,4]{1,0:T(1,128)}, u32[]{:S(2)}) copy-start(s32[1,4]{1,0:T(1,128)} %mask.5) | copy-start | bytes 52
  1.6 2.2 %collective-permute-start = (bf16[128,2560]{1,0:T(8,128)(2,1)S(1)}, bf16[128,2560]{1,0:T(8,128)(2,1)S(1)}, u32[]{:S(2)}, u32[]{:S(2)}) collective-permute-start(bf16[128,2560]{1,0:T(8,128)(2,1)S(1)} %pad_maximum_fusion.1), channel_id=1, source_target_pairs={{0,1},{1,0},{2,3},{3,2},{4,5},{5,4},{6,7},{7,6},{8,9},{9,8},{10,11... | collective-permute-start | bytes 1966088 | tf_op jit(solution)/shard_map/ppermute | solution.py:503
  4.0 18.0 %collective-permute-start.2 = (bf16[256,1280]{1,0:T(8,128)(2,1)S(1)}, bf16[256,1280]{1,0:T(8,128)(2,1)S(1)}, u32[]{:S(2)}, u32[]{:S(2)}) collective-permute-start(bf16[256,1280]{1,0:T(8,128)(2,1)S(1)} %pad_maximum_fusion.2), channel_id=1, source_target_pairs={{0,2},{1,3},{2,0},{3,1},{4,6},{5,7},{6,4},{7,5},{8,10},{9,11},{10,... | collective-permute-start | bytes 1966088 | tf_op jit(solution)/shard_map/ppermute | solution.py:503
  8.3 13.7 %collective-permute-start.1 = (bf16[128,1280]{1,0:T(8,128)(2,1)S(1)}, bf16[128,1280]{1,0:T(8,128)(2,1)S(1)}, u32[]{:S(2)}, u32[]{:S(2)}) collective-permute-start(bf16[128,1280]{1,0:T(8,128)(2,1)S(1)} %get-tuple-element.51), channel_id=1, source_target_pairs={{0,1},{1,0},{2,3},{3,2},{4,5},{5,4},{6,7},{7,6},{8,9},{9,8},{10,11... | collective-permute-start | bytes 983048 | tf_op jit(solution)/shard_map/ppermute | solution.py:503
  8.4 23.8 %collective-permute-start.6 = (bf16[272,1280]{1,0:T(8,128)(2,1)S(1)}, bf16[272,1280]{1,0:T(8,128)(2,1)S(1)}, u32[]{:S(2)}, u32[]{:S(2)}) collective-permute-start(bf16[272,1280]{1,0:T(8,128)(2,1)S(1)} %pad_maximum_fusion.refs_1_), channel_id=1, source_target_pairs={{0,1},{1,0},{2,3},{3,2},{4,8},{5,9},{6,10},{7,11},{8,4},{9,5},{10,... | collective-permute-start | bytes 2088968 | tf_op jit(solution)/shard_map/ppermute | solution.py:510
  21.9 10.3 %collective-permute-start.7 = (bf16[256,1280]{1,0:T(8,128)(2,1)S(1)}, bf16[256,1280]{1,0:T(8,128)(2,1)S(1)}, u32[]{:S(2)}, u32[]{:S(2)}) collective-permute-start(bf16[256,1280]{1,0:T(8,128)(2,1)S(1)} %collective-permute-done.2.refs_2_), channel_id=1, source_target_pairs={{0,1},{1,0},{2,3},{3,2},{4,8},{5,9},{6,10},{7,11},{8,4},{9,5},{10,... | collective-permute-start | bytes 1966088 | tf_op jit(solution)/shard_map/ppermute | solution.py:510
  22.0 10.2 %collective-permute-start.3 = (bf16[256,640]{1,0:T(8,128)(2,1)S(1)}, bf16[256,640]{1,0:T(8,128)(2,1)S(1)}, u32[]{:S(2)}, u32[]{:S(2)}) collective-permute-start(bf16[256,640]{1,0:T(8,128)(2,1)S(1)} %pad_maximum_fusion.4), channel_id=1, source_target_pairs={{0,2},{1,3},{2,0},{3,1},{4,6},{5,7},{6,4},{7,5},{8,10},{9,11},{10,... | collective-permute-start | bytes 983048 | tf_op jit(solution)/shard_map/ppermute | solution.py:503
  23.8 19.7 %collective-permute-start.4 = (bf16[272,1280]{1,0:T(8,128)(2,1)S(1)}, bf16[272,1280]{1,0:T(8,128)(2,1)S(1)}, u32[]{:S(2)}, u32[]{:S(2)}) collective-permute-start(bf16[272,1280]{1,0:T(8,128)(2,1)S(1)} %pad_maximum_fusion.refs_1_), channel_id=1, source_target_pairs={{0,4},{4,0},{8,12},{12,8},{1,5},{5,1},{9,13},{13,9},{2,6},{6,2},{1... | collective-permute-start | bytes 2088968 | tf_op jit(solution)/shard_map/ppermute | solution.py:506
  27.0 30.6 %collective-permute-start.5 = (bf16[256,1280]{1,0:T(8,128)(2,1)S(1)}, bf16[256,1280]{1,0:T(8,128)(2,1)S(1)}, u32[]{:S(2)}, u32[]{:S(2)}) collective-permute-start(bf16[256,1280]{1,0:T(8,128)(2,1)S(1)} %collective-permute-done.2.refs_2_), channel_id=1, source_target_pairs={{0,4},{4,0},{8,12},{12,8},{1,5},{5,1},{9,13},{13,9},{2,6},{6,2},{1... | collective-permute-start | bytes 1966088 | tf_op jit(solution)/shard_map/ppermute | solution.py:506
  32.4 36.4 %collective-permute-start.10 = (bf16[256,1024]{1,0:T(8,128)(2,1)S(1)}, bf16[256,1024]{1,0:T(8,128)(2,1)S(1)}, u32[]{:S(2)}, u32[]{:S(2)}) collective-permute-start(bf16[256,1024]{1,0:T(8,128)(2,1)S(1)} %shard_map.58), channel_id=1, source_target_pairs={{0,4},{4,0},{8,12},{12,8},{1,5},{5,1},{9,13},{13,9},{2,6},{6,2},{1... | collective-permute-start | bytes 1572872 | tf_op jit(solution)/shard_map/ppermute | solution.py:506
  57.7 4.5 %collective-permute-start.8 = (bf16[256,512]{1,0:T(8,128)(2,1)S(1)}, bf16[256,512]{1,0:T(8,128)(2,1)S(1)}, u32[]{:S(2)}, u32[]{:S(2)}) collective-permute-start(bf16[256,512]{1,0:T(8,128)(2,1)S(1)} %get-tuple-element.64), channel_id=1, source_target_pairs={{0,1},{1,0},{2,3},{3,2},{4,8},{5,9},{6,10},{7,11},{8,4},{9,5},{10,... | collective-permute-start | bytes 786440 | tf_op jit(solution)/shard_map/ppermute | solution.py:510
  57.8 10.9 %collective-permute-start.9 = (bf16[256,512]{1,0:T(8,128)(2,1)S(1)}, bf16[256,512]{1,0:T(8,128)(2,1)S(1)}, u32[]{:S(2)}, u32[]{:S(2)}) collective-permute-start(bf16[256,512]{1,0:T(8,128)(2,1)S(1)} %get-tuple-element.66), channel_id=1, source_target_pairs={{0,1},{1,0},{2,3},{3,2},{4,8},{5,9},{6,10},{7,11},{8,4},{9,5},{10,... | collective-permute-start | bytes 786440 | tf_op jit(solution)/shard_map/ppermute | solution.py:510
  62.3 14.6 %collective-permute-start.11 = (bf16[256,512]{1,0:T(8,128)(2,1)S(1)}, bf16[256,512]{1,0:T(8,128)(2,1)S(1)}, u32[]{:S(2)}, u32[]{:S(2)}) collective-permute-start(bf16[256,512]{1,0:T(8,128)(2,1)S(1)} %get-tuple-element.69), channel_id=1, source_target_pairs={{0,4},{4,0},{8,12},{12,8},{1,5},{5,1},{9,13},{13,9},{2,6},{6,2},{1... | collective-permute-start | bytes 786440 | tf_op jit(solution)/shard_map/ppermute | solution.py:506
  68.8 10.7 %collective-permute-start.12 = (bf16[256,512]{1,0:T(8,128)(2,1)S(1)}, bf16[256,512]{1,0:T(8,128)(2,1)S(1)}, u32[]{:S(2)}, u32[]{:S(2)}) collective-permute-start(bf16[256,512]{1,0:T(8,128)(2,1)S(1)} %collective-permute-done.9.r1v), channel_id=1, source_target_pairs={{0,4},{4,0},{8,12},{12,8},{1,5},{5,1},{9,13},{13,9},{2,6},{6,2},{1... | collective-permute-start | bytes 786440 | tf_op jit(solution)/shard_map/ppermute | solution.py:506
  70.1 1.3 %collective-permute-start.15 = (bf16[256,256]{1,0:T(8,128)(2,1)S(1)}, bf16[256,256]{1,0:T(8,128)(2,1)S(1)}, u32[]{:S(2)}, u32[]{:S(2)}) collective-permute-start(bf16[256,256]{1,0:T(8,128)(2,1)S(1)} %get-tuple-element.74), channel_id=1, source_target_pairs={{0,1},{1,0},{2,3},{3,2},{4,8},{5,9},{6,10},{7,11},{8,4},{9,5},{10,... | collective-permute-start | bytes 393224 | tf_op jit(solution)/shard_map/ppermute | solution.py:510
  71.5 15.0 %collective-permute-start.16 = (bf16[512,128]{1,0:T(8,128)(2,1)S(1)}, bf16[512,128]{1,0:T(8,128)(2,1)}, u32[]{:S(2)}, u32[]{:S(2)}) collective-permute-start(bf16[512,128]{1,0:T(8,128)(2,1)S(1)} %shard_map.62), channel_id=1, source_target_pairs={{0,4},{4,0},{8,12},{12,8},{1,5},{5,1},{9,13},{13,9},{2,6},{6,2},{1... | collective-permute-start | bytes 393224 | tf_op jit(solution)/shard_map/ppermute | solution.py:506
  83.9 0.6 copy-start.3
  84.6 6.1 %collective-permute-start.17 = (bf16[128,512]{1,0:T(8,128)(2,1)}, bf16[128,512]{1,0:T(8,128)(2,1)}, u32[]{:S(2)}, u32[]{:S(2)}) collective-permute-start(bf16[128,512]{1,0:T(8,128)(2,1)} %get-tuple-element.80), channel_id=1, source_target_pairs={{0,3},{1,2},{2,1},{3,0},{4,7},{5,6},{6,5},{7,4},{8,11},{9,10},{10,... | collective-permute-start | bytes 393224 | tf_op jit(solution)/shard_map/ppermute | solution.py:503
  84.6 7.0 %collective-permute-start.14 = (bf16[128,512]{1,0:T(8,128)(2,1)}, bf16[128,512]{1,0:T(8,128)(2,1)}, u32[]{:S(2)}, u32[]{:S(2)}) collective-permute-start(bf16[128,512]{1,0:T(8,128)(2,1)} %get-tuple-element.73), channel_id=1, source_target_pairs={{0,2},{1,3},{2,0},{3,1},{4,6},{5,7},{6,4},{7,5},{8,10},{9,11},{10,... | collective-permute-start | bytes 393224 | tf_op jit(solution)/shard_map/ppermute | solution.py:503
  85.1 6.5 %collective-permute-start.13 = (bf16[128,512]{1,0:T(8,128)(2,1)}, bf16[128,512]{1,0:T(8,128)(2,1)}, u32[]{:S(2)}, u32[]{:S(2)}) collective-permute-start(bf16[128,512]{1,0:T(8,128)(2,1)} %get-tuple-element.72), channel_id=1, source_target_pairs={{0,1},{1,0},{2,3},{3,2},{4,5},{5,4},{6,7},{7,6},{8,9},{9,8},{10,11... | collective-permute-start | bytes 393224 | tf_op jit(solution)/shard_map/ppermute | solution.py:503
  86.4 1.8 %copy-start.4 = (bf16[128,512]{1,0:T(8,128)(2,1)S(1)}, bf16[128,512]{1,0:T(8,128)(2,1)}, u32[]{:S(2)}) copy-start(bf16[128,512]{1,0:T(8,128)(2,1)} %copy-done.3) | copy-start | bytes 393220
  87.4 1.3 %collective-permute-start.18 = (bf16[128,128]{1,0:T(8,128)(2,1)S(1)}, bf16[128,128]{1,0:T(8,128)(2,1)S(1)}, u32[]{:S(2)}, u32[]{:S(2)}) collective-permute-start(bf16[128,128]{1,0:T(8,128)(2,1)S(1)} %get-tuple-element.78), channel_id=1, source_target_pairs={{0,1},{1,0},{2,3},{3,2},{4,5},{5,4},{6,7},{7,6},{8,9},{9,8},{10,11... | collective-permute-start | bytes 98312 | tf_op jit(solution)/shard_map/ppermute | solution.py:503
  87.5 6.9 %collective-permute-start.19 = (bf16[128,128]{1,0:T(8,128)(2,1)S(1)}, bf16[128,128]{1,0:T(8,128)(2,1)S(1)}, u32[]{:S(2)}, u32[]{:S(2)}) collective-permute-start(bf16[128,128]{1,0:T(8,128)(2,1)S(1)} %get-tuple-element.83), channel_id=1, source_target_pairs={{0,2},{1,3},{2,0},{3,1},{4,6},{5,7},{6,4},{7,5},{8,10},{9,11},{10,... | collective-permute-start | bytes 98312 | tf_op jit(solution)/shard_map/ppermute | solution.py:503
  88.7 5.8 %collective-permute-start.20 = (bf16[128,128]{1,0:T(8,128)(2,1)S(1)}, bf16[128,128]{1,0:T(8,128)(2,1)S(1)}, u32[]{:S(2)}, u32[]{:S(2)}) collective-permute-start(bf16[128,128]{1,0:T(8,128)(2,1)S(1)} %get-tuple-element.84), channel_id=1, source_target_pairs={{0,3},{1,2},{2,1},{3,0},{4,7},{5,6},{6,5},{7,4},{8,11},{9,10},{10,... | collective-permute-start | bytes 98312 | tf_op jit(solution)/shard_map/ppermute | solution.py:503
  94.4 0.8 copy-start.6
